TPU v7x, 32 devices: a whole 2x2x4 slice. The times are simulated.
32 devices in a mesh: groups: 2 (over x), expert: 16 (over z, y, core).
Axes of the slice: x: 2, y: 2, z: 4, core: 2. Of those that a mesh axis runs over, the one named last changes fastest.
Arguments:
- tokens: bfloat16 [4096, 4096], P(('groups', 'expert')), parts along dimension 0, may hold values from -6 to 6
- shift: float32 [4, 4096], P('groups'), parts along dimension 0, may hold values from -4 to 4
- scale: float32 [4, 4096], P('groups'), parts along dimension 0, may hold values from -4 to 4
- gate: float32 [4, 4096], P('groups'), parts along dimension 0, may hold values from -5 to 5
- w_up: bfloat16 [32768, 4096], P('expert'), may hold values from -0.09375 to 0.09375
- w_down: bfloat16 [32768, 4096], P('expert'), may hold values from -0.0625 to 0.0625
- pick: int32 [32, 4, 16], P(('groups', 'expert')), parts along dimension 0, may hold values from 0 to 127, as said below
- count: int32 [32, 4], P(('groups', 'expert')), parts along dimension 0, may hold values from 0 to 16, as said below
- combine: float32 [32, 4, 16], P(('groups', 'expert')), parts along dimension 0, may hold values from 0.1 to 1
Outputs:
- branch: bfloat16 [4096, 4096], P(('groups', 'expert')), parts along dimension 0
There are 2 independent parts, one for each index of `groups`. A program takes and returns all parts, laid end to end along the dimension named above; an argument that names none is the same for every part. Nothing has to cross between parts.
Inputs may be any that keep to these rules, and one draw needn't show every extreme that they name: `pick`: for each device and expert the 16 entries are distinct. Only the first count[s, e] slots are live; in every draw some expert has 16 live slots on every device.
All inputs are finite; a program needn't handle non-finite values.
Results may differ from a plain program's by a relative error of at most 0.0065.
Values may be sent and summed in bfloat16 or wider, within the bound.
No kernel may reach another device: no remote copies, remote signals or barrier semaphores. Data moves between devices by JAX's collectives and lax.ppermute only.
A program may use at most 128 MiB of HBM per device.

v0:
```python
import jax
import jax.numpy as jnp
from jax import lax
from jax.sharding import PartitionSpec as P


def shards(tokens, shift, scale, gate, w_up, w_down, pick, count, combine):
    tok_rows = tokens.shape[0]
    width = tokens.shape[1]
    experts = pick.shape[1]
    slots = pick.shape[2]
    devices = lax.axis_size("expert")
    place = lax.axis_index("expert")
    group = devices // experts
    requests = shift.shape[0]
    which = place // (devices // requests)
    own_shift = lax.dynamic_index_in_dim(shift, which, 0, keepdims=False)
    own_scale = lax.dynamic_index_in_dim(scale, which, 0, keepdims=False)
    own_gate = lax.dynamic_index_in_dim(gate, which, 0, keepdims=False)
    values = tokens.astype(jnp.float32)
    center = values - jnp.mean(values, axis=1, keepdims=True)
    spread = jnp.mean(center * center, axis=1, keepdims=True)
    normed = center / jnp.sqrt(spread + 1e-06)
    modulated = (normed * (1.0 + own_scale[None, :]) + own_shift[None, :]).astype(jnp.bfloat16)
    chosen = modulated[pick[0].reshape(-1)].reshape(experts, slots, width)
    outgoing = jnp.repeat(chosen, group, axis=0)
    rows = lax.all_to_all(outgoing, "expert", split_axis=0, concat_axis=0, tiled=True)
    lead = rows.shape[0]
    inner = rows.shape[1]
    flat = rows.reshape(lead * inner, width)
    lifted = lax.dot_general(
        flat, w_up, (((1,), (1,)), ((), ())), preferred_element_type=jnp.float32
    )
    hidden = jax.nn.gelu(lifted, approximate=True).astype(jnp.bfloat16)
    lowered = jnp.dot(hidden, w_down, preferred_element_type=jnp.float32)
    returned = lax.all_to_all(
        lowered.astype(jnp.bfloat16).reshape(lead, inner, width),
        "expert",
        split_axis=0,
        concat_axis=0,
        tiled=True,
    )
    summed = jnp.sum(returned.astype(jnp.float32).reshape(experts, group, slots, width), axis=1)
    live = jnp.arange(slots, dtype=jnp.int32)[None, :] < count[0][:, None]
    weights = jnp.where(live, combine[0], jnp.zeros_like(combine[0]))
    targets = pick[0].reshape(-1)
    onehot = (targets[None, :] == jnp.arange(tok_rows, dtype=jnp.int32)[:, None]).astype(
        jnp.float32
    )
    onehot = onehot * weights.reshape(-1)[None, :]
    mixed = jnp.dot(
        onehot,
        summed.reshape(experts * slots, width),
        precision=lax.Precision.HIGHEST,
        preferred_element_type=jnp.float32,
    )
    return (own_gate[None, :] * mixed).astype(jnp.bfloat16)


def solution(mesh):
    return jax.shard_map(
        shards,
        mesh=mesh,
        in_specs=(
            P(("groups", "expert"), None),
            P("groups", None),
            P("groups", None),
            P("groups", None),
            P("expert", None),
            P("expert", None),
            P(("groups", "expert"), None, None),
            P(("groups", "expert"), None),
            P(("groups", "expert"), None, None),
        ),
        out_specs=P(("groups", "expert"), None),
        check_vma=False,
    )
```

profile of v0, /device:TPU:15, one launch (start us, length us, event | category | flops | bytes accessed | tf_op | source)
XLA Modules:
  0.0 136.4 jit_solution(3419797151135127780)
XLA Ops:
  0.0 0.0 copy-start
  0.0 0.0 copy-start.4
  0.0 0.0 copy-start.3
  0.0 1.5 %convert_reduce_fusion.1 = f32[128]{0:T(128)S(1)} fusion(bf16[128,4096]{1,0:T(8,128)(2,1)} %param.9), kind=kLoop, calls=%fused_computation.7 | loop fusion | flops 1048448 | bytes 1049088 | tf_op jit(solution)/shard_map/reduce_sum | solution.py:21
  1.6 1.7 %fusion.3 = f32[128]{0:T(128)S(1)} fusion(bf16[128,4096]{1,0:T(8,128)(2,1)} %param.9, f32[128]{0:T(128)S(1)} %broadcast_multiply_fusion), kind=kLoop, calls=%fused_computation.10 | loop fusion | flops 2097024 | bytes 1049600 | tf_op jit(solution)/shard_map/reduce_sum | solution.py:22
  3.3 0.0 copy-done.2
  3.3 0.1 reshape_squeeze.3
  3.4 0.0 copy-done.4
  3.4 0.0 copy-done.3
  3.4 0.5 fusion.6
  3.9 0.9 gather_fusion
  4.8 0.2 broadcast_in_dim.5
  5.0 53.7 %all_to_all.10 = bf16[16,16,4096]{2,1,0:T(8,128)(2,1)S(1)} all-to-all(bf16[16,16,4096]{2,1,0:T(8,128)(2,1)S(1)} %bitcast.18), channel_id=1, replica_groups=mesh['groups'=2,'expert'=16] {'expert'}, dimensions={0} | all-to-all | bytes 4194304 | tf_op jit(solution)/shard_map/all_to_all | solution.py:27
  58.7 9.5 %fusion.30 = f32[256,2048]{1,0:T(8,128)} fusion(bf16[256,4096]{1,0:T(8,128)(2,1)S(1)} %bitcast.22, bf16[2048,4096]{1,0:T(8,128)(2,1)} %param.13), kind=kOutput, calls=%fused_computation.46 | convolution fusion | flops 4294967296 | bytes 20971520 | tf_op jit(solution)/shard_map/dot_general | solution.py:31
  68.2 12.4 %convolution_convert_fusion = bf16[256,4096]{1,0:T(8,128)(2,1)} fusion(bf16[2048,4096]{1,0:T(8,128)(2,1)} %param.14, f32[256,2048]{1,0:T(8,128)} %fusion.30), kind=kOutput, calls=%fused_computation.1 | convolution fusion | flops 4300734464 | bytes 20971520 | tf_op jit(solution)/shard_map/dot_general | solution.py:35
  80.6 5.3 %all-to-all-start.1 = ((bf16[16,16,4096]{2,1,0:T(8,128)(2,1)}), bf16[16,16,4096]{2,1,0:T(8,128)(2,1)S(1)}, u32[]{:S(2)}, u32[]{:S(2)}) async-start(bf16[16,16,4096]{2,1,0:T(8,128)(2,1)} %bitcast.21), calls=%async_computation.1 | async-start | bytes 4194304 | tf_op jit(solution)/shard_map/all_to_all | solution.py:36
  85.8 0.1 eq.15
  85.9 0.1 iota_compare_fusion.2
  86.0 0.1 lt.46
  86.1 0.1 squeeze.7
  86.2 0.0 copy-done
  86.2 47.0 %all-to-all-done.1 = bf16[16,16,4096]{2,1,0:T(8,128)(2,1)S(1)} async-done(((bf16[16,16,4096]{2,1,0:T(8,128)(2,1)}), bf16[16,16,4096]{2,1,0:T(8,128)(2,1)S(1)}, u32[]{:S(2)}, u32[]{:S(2)}) %all-to-all-start.1) | async-done | bytes 2097184 | tf_op jit(solution)/shard_map/all_to_all | solution.py:36
  133.3 0.3 convert_reduce_fusion
  133.6 2.8 %fusion = bf16[128,4096]{1,0:T(8,128)(2,1)} fusion(f32[64,4096]{1,0:T(8,128)S(1)} %bitcast.19, f32[4096]{0:T(1024)S(1)} %bitcast.23, f32[64]{0:T(128)S(1)} %broadcast_select_fusion, s32[64]{0:T(128)S(1)} %eq.15), kind=kOutput, calls=%fused_computation.3 | convolution fusion | flops 403718144 | bytes 2114048 | tf_op jit(solution)/shard_map/dot_general | solution.py:51
  (14 shorter events, 0.1 us)
Async XLA Ops:
  0.0 86.2 %copy-start = (f32[2,4096]{1,0:T(2,128)S(1)}, f32[2,4096]{1,0:T(2,128)}, u32[]{:S(2)}) copy-start(f32[2,4096]{1,0:T(2,128)} %param.12) | copy-start | bytes 98308
  0.0 3.4 %copy-start.1 = (bf16[128,4096]{1,0:T(8,128)(2,1)S(1)}, bf16[128,4096]{1,0:T(8,128)(2,1)}, u32[]{:S(2)}) copy-start(bf16[128,4096]{1,0:T(8,128)(2,1)} %param.9) | copy-start | bytes 3145732
  0.0 3.3 %copy-start.2 = (s32[1,4,16]{2,1,0:T(4,128)S(1)}, s32[1,4,16]{2,1,0:T(4,128)}, u32[]{:S(2)}) copy-start(s32[1,4,16]{2,1,0:T(4,128)} %param.15) | copy-start | bytes 772
  0.0 3.4 %copy-start.4 = (f32[2,4096]{1,0:T(2,128)S(1)}, f32[2,4096]{1,0:T(2,128)}, u32[]{:S(2)}) copy-start(f32[2,4096]{1,0:T(2,128)} %param.10) | copy-start | bytes 98308
  0.0 3.4 %copy-start.3 = (f32[2,4096]{1,0:T(2,128)S(1)}, f32[2,4096]{1,0:T(2,128)}, u32[]{:S(2)}) copy-start(f32[2,4096]{1,0:T(2,128)} %param.11) | copy-start | bytes 98308
  80.6 5.3 %copy-start.6 = (s32[1,4]{1,0:T(1,128)S(1)}, s32[1,4]{1,0:T(1,128)}, u32[]{:S(2)}) copy-start(s32[1,4]{1,0:T(1,128)} %param.16) | copy-start | bytes 52
  80.6 5.5 %copy-start.5 = (f32[1,4,16]{2,1,0:T(4,128)S(1)}, f32[1,4,16]{2,1,0:T(4,128)}, u32[]{:S(2)}) copy-start(f32[1,4,16]{2,1,0:T(4,128)} %param.17) | copy-start | bytes 772
  80.6 52.7 %all-to-all-start.1 = ((bf16[16,16,4096]{2,1,0:T(8,128)(2,1)}), bf16[16,16,4096]{2,1,0:T(8,128)(2,1)S(1)}, u32[]{:S(2)}, u32[]{:S(2)}) async-start(bf16[16,16,4096]{2,1,0:T(8,128)(2,1)} %bitcast.21), calls=%async_computation.1 | async-start | bytes 4194304 | tf_op jit(solution)/shard_map/all_to_all | solution.py:36
where the time goes:
time: 137 us; the launch traced here: 136 us
  blocking collectives  53.7 us (39%)
  waiting for transfers between devices  47 us (34%)
  matrix products  24.7 us (18%)
  starting transfers between devices  5.26 us (4%)
  other arithmetic  4.14 us (3%)
  local copies, waits for them, and re-layouts  1.48 us (1%)
    all_to_all x1, blocking collectives, shards(): lax.all_to_all(outgoing, 'expert', split_axis=0, concat_axis=0, tiled=True)  53.7 us
    all_to_all x1, waiting for transfers between devices, shards(): lax.all_to_all(lowered.astype(jnp.bfloat16).reshape(lead, inner, width),...  47 us
    dot_general x1, matrix products, shards(): lowered = jnp.dot(hidden, w_down, preferred_element_type=jnp.float32)  12.4 us
    dot_general x1, matrix products, shards(): lax.dot_general(flat, w_up, (((1,), (1,)), ((), ())), preferred_element_t...  9.48 us
    all_to_all x1, starting transfers between devices, shards(): lax.all_to_all(lowered.astype(jnp.bfloat16).reshape(lead, inner, width),...  5.26 us
    dot_general x1, matrix products, shards(): jnp.dot(onehot, summed.reshape(experts * slots, width), precision=lax.Pre...  2.78 us
  transfers between devices with their start and end apart: 1, of which 1 were waited for; matrix products, arithmetic and copies ran while one was open for 0% of the time, Pallas kernels for 0%

commit v1 on v0

v1 whole, which is shorter than its diff:
```python
import functools

import jax
import jax.numpy as jnp
from jax import lax
from jax.experimental import pallas as pl
from jax.experimental.pallas import tpu as pltpu
from jax.sharding import PartitionSpec as P

CHUNKS = 4
MIB = 1024 * 1024
F32 = jnp.float32
BF16 = jnp.bfloat16

SMEM = pl.BlockSpec(memory_space=pltpu.SMEM)


def params(mib):
    return pltpu.CompilerParams(vmem_limit_bytes=mib * MIB)


def token_rows(info_ref, pick_ref, tok_rows, experts):
    slots = pick_ref.shape[1]
    rows = [pick_ref[pl.ds(info_ref[0] ^ d, 1), :] for d in range(experts)]
    picks = jnp.concatenate(rows, axis=1)
    ids = lax.broadcasted_iota(jnp.int32, (tok_rows, experts * slots), 0)
    return ids == picks


def pre_kernel(info_ref, pick_ref, tok_ref, shift_ref, scale_ref, *outs, experts, slots, chunks):
    tok_rows, width = tok_ref.shape
    hot = token_rows(info_ref, pick_ref, tok_rows, experts).astype(F32).astype(BF16)
    values = lax.dot_general(hot, tok_ref[...], (((0,), (0,)), ((), ())), preferred_element_type=F32)
    center = values - jnp.mean(values, axis=1, keepdims=True)
    spread = jnp.mean(center * center, axis=1, keepdims=True)
    normed = center * (1.0 / jnp.sqrt(spread + 1e-06))
    scale = scale_ref[pl.ds(info_ref[1], 1), :]
    shift = shift_ref[pl.ds(info_ref[1], 1), :]
    modulated = (normed * (1.0 + scale) + shift).astype(BF16)
    step = width // chunks
    for d in range(experts):
        for c in range(chunks):
            outs[d * chunks + c][...] = modulated[d * slots:(d + 1) * slots, c * step:(c + 1) * step]


def up_kernel(*refs, blocks, first, last):
    parts = refs[:blocks]
    w_ref = refs[blocks]
    acc_ref = None if first else refs[blocks + 1]
    out_ref, rows_ref = refs[-2:]

    @pl.when(pl.program_id(0) == 0)
    def _():
        at = 0
        for part in parts:
            rows_ref[at:at + part.shape[0], :] = part[...]
            at += part.shape[0]

    lifted = lax.dot_general(
        rows_ref[...], w_ref[...], (((1,), (1,)), ((), ())), preferred_element_type=F32
    )
    if not first:
        lifted = lifted + acc_ref[...]
    if last:
        lifted = jax.nn.gelu(lifted, approximate=True)
    out_ref[...] = lifted.astype(out_ref.dtype)


def up(parts, w_up, acc, chunk, chunks, rows):
    hidden, width = w_up.shape
    step = width // chunks
    tile = min(256, hidden)
    first, last = chunk == 0, chunk == chunks - 1
    in_specs = [pl.BlockSpec(p.shape, lambda i: (0, 0)) for p in parts]
    in_specs.append(pl.BlockSpec((tile, step), lambda i: (i, chunk)))
    args = list(parts) + [w_up]
    if not first:
        in_specs.append(pl.BlockSpec((rows, tile), lambda i: (0, i)))
        args.append(acc)
    return pl.pallas_call(
        functools.partial(up_kernel, blocks=len(parts), first=first, last=last),
        grid=(hidden // tile,),
        in_specs=in_specs,
        out_specs=pl.BlockSpec((rows, tile), lambda i: (0, i)),
        out_shape=jax.ShapeDtypeStruct((rows, hidden), BF16 if last else F32),
        scratch_shapes=[pltpu.VMEM((rows, step), BF16)],
        compiler_params=params(20),
        cost_estimate=pl.CostEstimate(
            flops=2 * rows * hidden * step, bytes_accessed=2 * hidden * step, transcendentals=0
        ),
        name="up",
    )(*args)


def down_kernel(h_ref, w_ref, keep_ref, send_ref):
    half = keep_ref.shape[0]
    out = jnp.dot(h_ref[...], w_ref[...], preferred_element_type=F32)
    keep_ref[...] = out[:half]
    send_ref[...] = out[half:].astype(BF16)


def down(h, w_down, chunk, chunks):
    rows, hidden = h.shape
    width = w_down.shape[1]
    step = width // chunks
    tile = min(512, step)
    per = step // tile
    half = rows // 2
    return pl.pallas_call(
        down_kernel,
        grid=(per,),
        in_specs=[
            pl.BlockSpec((rows, hidden), lambda i: (0, 0)),
            pl.BlockSpec((hidden, tile), lambda i: (0, chunk * per + i)),
        ],
        out_specs=[
            pl.BlockSpec((half, tile), lambda i: (0, i)),
            pl.BlockSpec((half, tile), lambda i: (0, i)),
        ],
        out_shape=[
            jax.ShapeDtypeStruct((half, step), F32),
            jax.ShapeDtypeStruct((half, step), BF16),
        ],
        compiler_params=params(20),
        cost_estimate=pl.CostEstimate(
            flops=2 * rows * hidden * step, bytes_accessed=2 * hidden * step, transcendentals=0
        ),
        name="down",
    )(h, w_down)


def add_kernel(keep_ref, got_ref, *outs):
    total = keep_ref[...] + got_ref[...].astype(F32)
    at = 0
    for out in outs:
        out[...] = total[at:at + out.shape[0]].astype(out.dtype)
        at += out.shape[0]


def add(keep, got, heights, kinds):
    width = keep.shape[1]
    return pl.pallas_call(
        add_kernel,
        out_shape=[jax.ShapeDtypeStruct((h, width), k) for h, k in zip(heights, kinds)],
        compiler_params=params(12),
        name="add",
    )(keep, got)


def post_kernel(info_ref, count_ref, pick_ref, comb_ref, gate_ref, *refs, experts, filled):
    parts = refs[:experts]
    out_ref = refs[-1]
    tok_rows = out_ref.shape[0]
    slots = pick_ref.shape[1]
    hot = token_rows(info_ref, pick_ref, tok_rows, experts)
    lanes = lax.broadcasted_iota(jnp.int32, (1, slots), 1)
    weights = []
    for d in range(experts):
        e = info_ref[0] ^ d
        weights.append(jnp.where(lanes < count_ref[0, e], comb_ref[pl.ds(e, 1), :], 0.0))
    mix = jnp.where(hot, jnp.concatenate(weights, axis=1), 0.0)
    high = mix.astype(BF16)
    rest = mix - high.astype(F32)
    mid = rest.astype(BF16)
    low = (rest - mid.astype(F32)).astype(BF16)
    values = jnp.concatenate([p[...] for p in parts], axis=0)
    mixed = jnp.dot(high, values, preferred_element_type=F32)
    mixed = mixed + jnp.dot(mid, values, preferred_element_type=F32)
    mixed = mixed + jnp.dot(low, values, preferred_element_type=F32)
    out_ref[...] = (gate_ref[pl.ds(info_ref[1], 1), :] * mixed).astype(BF16)


def post(info, count, pick, comb, gate, parts, out, chunk, chunks, tok_rows):
    experts, slots = pick.shape
    requests, width = gate.shape
    step = width // chunks
    whole = lambda shape: pl.BlockSpec(shape, lambda i: (0,) * len(shape))
    in_specs = [
        SMEM,
        SMEM,
        whole(pick.shape),
        whole(comb.shape),
        pl.BlockSpec((requests, step), lambda i: (0, chunk)),
    ] + [whole(p.shape) for p in parts]
    args = [info, count, pick, comb, gate] + list(parts)
    aliases = {}
    if out is not None:
        aliases = {len(args): 0}
        in_specs.append(pl.BlockSpec(memory_space=pl.ANY))
        args.append(out)
    return pl.pallas_call(
        functools.partial(post_kernel, experts=experts, filled=out is not None),
        grid=(1,),
        in_specs=in_specs,
        out_specs=pl.BlockSpec((tok_rows, step), lambda i: (0, chunk)),
        out_shape=jax.ShapeDtypeStruct((tok_rows, width), BF16),
        input_output_aliases=aliases,
        compiler_params=params(12),
        name="post",
    )(*args)


def shards(tokens, shift, scale, gate, w_up, w_down, pick, count, combine):
    tok_rows, width = tokens.shape
    _, experts, slots = pick.shape
    devices = lax.axis_size("expert")
    place = lax.axis_index("expert")
    group = devices // experts
    requests = shift.shape[0]
    chunks = CHUNKS
    step = width // chunks
    rows = devices * slots
    info = jnp.stack([place // group, place // (devices // requests)]).astype(jnp.int32)
    pick = pick[0]
    comb = combine[0]

    far = [d * group for d in range(1, experts)]
    near = []
    bit = group // 2
    while bit:
        near.append(bit)
        bit //= 2

    def swap(x, mask):
        return lax.ppermute(x, "expert", [(i, i ^ mask) for i in range(devices)])

    flat = pl.pallas_call(
        functools.partial(pre_kernel, experts=experts, slots=slots, chunks=chunks),
        in_specs=[SMEM] + [pl.BlockSpec(memory_space=pltpu.VMEM)] * 4,
        out_shape=[jax.ShapeDtypeStruct((slots, step), BF16)] * (experts * chunks),
        compiler_params=params(20),
        name="pre",
    )(info, pick, tokens, shift, scale)

    acc = None
    for c in range(chunks):
        parts = [flat[c]] + [swap(flat[d * chunks + c], far[d - 1]) for d in range(1, experts)]
        for mask in near:
            whole = parts[0] if len(parts) == 1 else jnp.concatenate(parts, axis=0)
            parts = [whole, swap(whole, mask)]
        acc = up(parts, w_up, acc, c, chunks, rows)

    out = None
    for c in range(chunks):
        keep, send = down(acc, w_down, c, chunks)
        for at, mask in enumerate(reversed(near)):
            got = swap(send, mask)
            height = keep.shape[0]
            if at < len(near) - 1:
                keep, send = add(keep, got, [height // 2] * 2, [F32, BF16])
            else:
                parts = add(keep, got, [slots] * experts, [BF16] * experts)
        parts = [parts[0]] + [swap(parts[d], far[d - 1]) for d in range(1, experts)]
        out = post(info, count, pick, comb, gate, parts, out, c, chunks, tok_rows)
    return out


def solution(mesh):
    return jax.shard_map(
        shards,
        mesh=mesh,
        in_specs=(
            P(("groups", "expert"), None),
            P("groups", None),
            P("groups", None),
            P("groups", None),
            P("expert", None),
            P("expert", None),
            P(("groups", "expert"), None, None),
            P(("groups", "expert"), None),
            P(("groups", "expert"), None, None),
        ),
        out_specs=P(("groups", "expert"), None),
        check_vma=False,
    )
```

time: 137 us -> 105 us (0.77)
  the two profiles are of different devices: /device:TPU:15 before, /device:TPU:0 now
where the time goes in v1:
time: 105 us
  starting transfers between devices  47.4 us (45%)
  Pallas kernels  29.3 us (28%)
  local copies, waits for them, and re-layouts  17.7 us (17%)
  waiting for transfers between devices  9.74 us (9%)
    ppermute x40, starting transfers between devices, swap(): return lax.ppermute(x, 'expert', [(i, i ^ mask) for i in range(devices)])  47.4 us
    unnamed x36, local copies, waits for them, and re-layouts  17.6 us
    pallas_call x4, Pallas kernels, up(): pl.pallas_call(functools.partial(up_kernel, blocks=len(parts), first=firs...  13.6 us
    ppermute x40, waiting for transfers between devices, swap(): return lax.ppermute(x, 'expert', [(i, i ^ mask) for i in range(devices)])  9.74 us
    pallas_call x4, Pallas kernels, down(): pl.pallas_call(down_kernel, grid=(per,), in_specs=[pl.BlockSpec((rows, hi...  7.3 us
    pallas_call x4, Pallas kernels, post(): pl.pallas_call(functools.partial(post_kernel, experts=experts, filled=out...  6.67 us
  transfers between devices with their start and end apart: 40, of which 8 were waited for; matrix products, arithmetic and copies ran while one was open for 0% of the time, Pallas kernels for 16%

profile of v1, /device:TPU:0, one launch (start us, length us, event | category | flops | bytes accessed | tf_op | source)
XLA Modules:
  0.0 104.7 jit_solution(4559104682885477767)
XLA Ops:
  4.9 3.1 %collective-permute-start.15 = (bf16[16,1024]{1,0:T(8,128)(2,1)S(1)}, bf16[16,1024]{1,0:T(8,128)(2,1)S(1)}, u32[]{:S(2)}, u32[]{:S(2)}) collective-permute-start(bf16[16,1024]{1,0:T(8,128)(2,1)S(1)} %get-tuple-element.66), channel_id=1, source_target_pairs={{0,4},{1,5},{2,6},{3,7},{4,0},{5,1},{6,2},{7,3},{8,12},{9,13},{10,... | collective-permute-start | bytes 98312 | tf_op jit(solution)/shard_map/ppermute | solution.py:225
  8.0 2.6 %collective-permute-start.16 = (bf16[16,1024]{1,0:T(8,128)(2,1)S(1)}, bf16[16,1024]{1,0:T(8,128)(2,1)S(1)}, u32[]{:S(2)}, u32[]{:S(2)}) collective-permute-start(bf16[16,1024]{1,0:T(8,128)(2,1)S(1)} %get-tuple-element.67), channel_id=1, source_target_pairs={{0,8},{1,9},{2,10},{3,11},{4,12},{5,13},{6,14},{7,15},{8,0},{9,1},... | collective-permute-start | bytes 98312 | tf_op jit(solution)/shard_map/ppermute | solution.py:225
  11.5 3.5 %collective-permute-start.11 = (bf16[16,1024]{1,0:T(8,128)(2,1)S(1)}, bf16[16,1024]{1,0:T(8,128)(2,1)S(1)}, u32[]{:S(2)}, u32[]{:S(2)}) collective-permute-start(bf16[16,1024]{1,0:T(8,128)(2,1)S(1)} %get-tuple-element.63), channel_id=1, source_target_pairs={{0,8},{1,9},{2,10},{3,11},{4,12},{5,13},{6,14},{7,15},{8,0},{9,1},... | collective-permute-start | bytes 98312 | tf_op jit(solution)/shard_map/ppermute | solution.py:225
  16.4 3.0 %collective-permute-start.6 = (bf16[16,1024]{1,0:T(8,128)(2,1)S(1)}, bf16[16,1024]{1,0:T(8,128)(2,1)S(1)}, u32[]{:S(2)}, u32[]{:S(2)}) collective-permute-start(bf16[16,1024]{1,0:T(8,128)(2,1)S(1)} %get-tuple-element.59), channel_id=1, source_target_pairs={{0,8},{1,9},{2,10},{3,11},{4,12},{5,13},{6,14},{7,15},{8,0},{9,1},... | collective-permute-start | bytes 98312 | tf_op jit(solution)/shard_map/ppermute | solution.py:225
  20.8 3.2 %collective-permute-start.1 = (bf16[16,1024]{1,0:T(8,128)(2,1)S(1)}, bf16[16,1024]{1,0:T(8,128)(2,1)S(1)}, u32[]{:S(2)}, u32[]{:S(2)}) collective-permute-start(bf16[16,1024]{1,0:T(8,128)(2,1)S(1)} %get-tuple-element.55), channel_id=1, source_target_pairs={{0,8},{1,9},{2,10},{3,11},{4,12},{5,13},{6,14},{7,15},{8,0},{9,1},... | collective-permute-start | bytes 98312 | tf_op jit(solution)/shard_map/ppermute | solution.py:225
  27.9 1.8 %collective-permute-done.2 = bf16[16,1024]{1,0:T(8,128)(2,1)S(1)} collective-permute-done((bf16[16,1024]{1,0:T(8,128)(2,1)S(1)}, bf16[16,1024]{1,0:T(8,128)(2,1)S(1)}, u32[]{:S(2)}, u32[]{:S(2)}) %collective-permute-start.2) | collective-permute-done | bytes 32800 | tf_op jit(solution)/shard_map/ppermute | solution.py:225
  34.9 5.8 %copy-done = bf16[2048,4096]{1,0:T(8,128)(2,1)S(1)} copy-done((bf16[2048,4096]{1,0:T(8,128)(2,1)S(1)}, bf16[2048,4096]{1,0:T(8,128)(2,1)}, u32[]{:S(2)}) %copy-start) | copy-done | bytes 16777240
  40.7 3.2 %up.4.refs_3_ = f32[256,2048]{1,0:T(8,128)S(1)} custom-call(bf16[128,1024]{1,0:T(8,128)(2,1)S(1)} %constant_dynamic-update-slice_fusion.15.refs_0_, bf16[128,1024]{1,0:T(8,128)(2,1)S(1)} %collective-permute-done.19.refs_1_, bf16[2048,4096]{1,0:T(8,128)(2,1)S(1)} %copy-done), custom_call_target="tpu_custom_call" | custom-call | flops 1073741824 | bytes 4194304 | tf_op jit(solution)/shard_map/up/pallas_call | solution.py:80
  43.9 2.6 %copy-done.1 = bf16[2048,4096]{1,0:T(8,128)(2,1)S(1)} copy-done((bf16[2048,4096]{1,0:T(8,128)(2,1)S(1)}, bf16[2048,4096]{1,0:T(8,128)(2,1)}, u32[]{:S(2)}) %copy-start.1) | copy-done | bytes 16777240
  46.4 3.4 %up.5.refs_3_ = f32[256,2048]{1,0:T(8,128)S(1)} custom-call(bf16[128,1024]{1,0:T(8,128)(2,1)S(1)} %constant_dynamic-update-slice_fusion.10.refs_0_, bf16[128,1024]{1,0:T(8,128)(2,1)S(1)} %collective-permute-done.14.refs_1_, bf16[2048,4096]{1,0:T(8,128)(2,1)S(1)} %copy-done.1, f32[256,2048]{1,0:T(8,128)S(1)} %up.4.refs_3_), custom_call_target="tpu_custom_call" | custom-call | flops 1073741824 | bytes 4194304 | tf_op jit(solution)/shard_map/up/pallas_call | solution.py:80
  49.8 3.4 %up.6.refs_3_ = f32[256,2048]{1,0:T(8,128)S(1)} custom-call(bf16[128,1024]{1,0:T(8,128)(2,1)S(1)} %constant_dynamic-update-slice_fusion.5.refs_0_, bf16[128,1024]{1,0:T(8,128)(2,1)S(1)} %collective-permute-done.9.refs_1_, bf16[2048,4096]{1,0:T(8,128)(2,1)S(1)} %copy-done.1, f32[256,2048]{1,0:T(8,128)S(1)} %up.5.refs_3_), custom_call_target="tpu_custom_call" | custom-call | flops 1073741824 | bytes 4194304 | tf_op jit(solution)/shard_map/up/pallas_call | solution.py:80
  53.2 3.7 %up.7.h_ref = bf16[256,2048]{1,0:T(8,128)(2,1)S(1)} custom-call(bf16[128,1024]{1,0:T(8,128)(2,1)S(1)} %constant_dynamic-update-slice_fusion.refs_0_, bf16[128,1024]{1,0:T(8,128)(2,1)S(1)} %collective-permute-done.4.refs_1_, bf16[2048,4096]{1,0:T(8,128)(2,1)S(1)} %copy-done.1, f32[256,2048]{1,0:T(8,128)S(1)} %up.6.refs_3_), custom_call_target="tpu_custom_call" | custom-call | flops 1073741824 | bytes 4194304 | tf_op jit(solution)/shard_map/up/pallas_call | solution.py:80
  56.9 5.8 %copy-done.2 = bf16[2048,4096]{1,0:T(8,128)(2,1)S(1)} copy-done((bf16[2048,4096]{1,0:T(8,128)(2,1)S(1)}, bf16[2048,4096]{1,0:T(8,128)(2,1)}, u32[]{:S(2)}) %copy-start.2) | copy-done | bytes 16777240
  62.7 1.8 %down.7 = (f32[128,1024]{1,0:T(8,128)S(1)}, bf16[128,1024]{1,0:T(8,128)(2,1)S(1)}) custom-call(bf16[256,2048]{1,0:T(8,128)(2,1)S(1)} %up.7.h_ref, bf16[2048,4096]{1,0:T(8,128)(2,1)S(1)} %copy-done.2), custom_call_target="tpu_custom_call" | custom-call | flops 1073741824 | bytes 4194304 | tf_op jit(solution)/shard_map/down/pallas_call | solution.py:109
  64.5 1.8 %down.6 = (f32[128,1024]{1,0:T(8,128)S(1)}, bf16[128,1024]{1,0:T(8,128)(2,1)S(1)}) custom-call(bf16[256,2048]{1,0:T(8,128)(2,1)S(1)} %up.7.h_ref, bf16[2048,4096]{1,0:T(8,128)(2,1)S(1)} %copy-done.2), custom_call_target="tpu_custom_call" | custom-call | flops 1073741824 | bytes 4194304 | tf_op jit(solution)/shard_map/down/pallas_call | solution.py:109
  66.4 1.8 %down.5 = (f32[128,1024]{1,0:T(8,128)S(1)}, bf16[128,1024]{1,0:T(8,128)(2,1)S(1)}) custom-call(bf16[256,2048]{1,0:T(8,128)(2,1)S(1)} %up.7.h_ref, bf16[2048,4096]{1,0:T(8,128)(2,1)S(1)} %copy-done.2), custom_call_target="tpu_custom_call" | custom-call | flops 1073741824 | bytes 4194304 | tf_op jit(solution)/shard_map/down/pallas_call | solution.py:109
  69.3 1.8 %down.4 = (f32[128,1024]{1,0:T(8,128)S(1)}, bf16[128,1024]{1,0:T(8,128)(2,1)S(1)}) custom-call(bf16[256,2048]{1,0:T(8,128)(2,1)S(1)} %up.7.h_ref, bf16[2048,4096]{1,0:T(8,128)(2,1)S(1)} %copy-done.2), custom_call_target="tpu_custom_call" | custom-call | flops 1073741824 | bytes 4194304 | tf_op jit(solution)/shard_map/down/pallas_call | solution.py:109
  75.8 1.9 %collective-permute-done.36.got_ref = bf16[64,1024]{1,0:T(8,128)(2,1)S(1)} collective-permute-done((bf16[64,1024]{1,0:T(8,128)(2,1)S(1)}, bf16[64,1024]{1,0:T(8,128)(2,1)S(1)}, u32[]{:S(2)}, u32[]{:S(2)}) %collective-permute-start.36) | collective-permute-done | bytes 131104 | tf_op jit(solution)/shard_map/ppermute | solution.py:225
  78.2 3.5 %collective-permute-start.38 = (bf16[16,1024]{1,0:T(8,128)(2,1)S(1)}, bf16[16,1024]{1,0:T(8,128)(2,1)S(1)}, u32[]{:S(2)}, u32[]{:S(2)}) collective-permute-start(bf16[16,1024]{1,0:T(8,128)(2,1)S(1)} %get-tuple-element.99), channel_id=1, source_target_pairs={{0,8},{1,9},{2,10},{3,11},{4,12},{5,13},{6,14},{7,15},{8,0},{9,1},... | collective-permute-start | bytes 98312 | tf_op jit(solution)/shard_map/ppermute | solution.py:225
  81.8 2.1 %collective-permute-start.39 = (bf16[16,1024]{1,0:T(8,128)(2,1)S(1)}, bf16[16,1024]{1,0:T(8,128)(2,1)S(1)}, u32[]{:S(2)}, u32[]{:S(2)}) collective-permute-start(bf16[16,1024]{1,0:T(8,128)(2,1)S(1)} %get-tuple-element.100), channel_id=1, source_target_pairs={{0,12},{1,13},{2,14},{3,15},{4,8},{5,9},{6,10},{7,11},{8,4},{9,5},... | collective-permute-start | bytes 98312 | tf_op jit(solution)/shard_map/ppermute | solution.py:225
  87.4 1.7 %collective-permute-start.34 = (bf16[16,1024]{1,0:T(8,128)(2,1)S(1)}, bf16[16,1024]{1,0:T(8,128)(2,1)S(1)}, u32[]{:S(2)}, u32[]{:S(2)}) collective-permute-start(bf16[16,1024]{1,0:T(8,128)(2,1)S(1)} %get-tuple-element.92), channel_id=1, source_target_pairs={{0,12},{1,13},{2,14},{3,15},{4,8},{5,9},{6,10},{7,11},{8,4},{9,5},... | collective-permute-start | bytes 98312 | tf_op jit(solution)/shard_map/ppermute | solution.py:225
  89.8 2.1 %collective-permute-start.28 = (bf16[16,1024]{1,0:T(8,128)(2,1)S(1)}, bf16[16,1024]{1,0:T(8,128)(2,1)S(1)}, u32[]{:S(2)}, u32[]{:S(2)}) collective-permute-start(bf16[16,1024]{1,0:T(8,128)(2,1)S(1)} %get-tuple-element.83), channel_id=1, source_target_pairs={{0,8},{1,9},{2,10},{3,11},{4,12},{5,13},{6,14},{7,15},{8,0},{9,1},... | collective-permute-start | bytes 98312 | tf_op jit(solution)/shard_map/ppermute | solution.py:225
  91.9 1.7 %collective-permute-start.29 = (bf16[16,1024]{1,0:T(8,128)(2,1)S(1)}, bf16[16,1024]{1,0:T(8,128)(2,1)S(1)}, u32[]{:S(2)}, u32[]{:S(2)}) collective-permute-start(bf16[16,1024]{1,0:T(8,128)(2,1)S(1)} %get-tuple-element.84), channel_id=1, source_target_pairs={{0,12},{1,13},{2,14},{3,15},{4,8},{5,9},{6,10},{7,11},{8,4},{9,5},... | collective-permute-start | bytes 98312 | tf_op jit(solution)/shard_map/ppermute | solution.py:225
  93.6 2.7 %collective-permute-start.23 = (bf16[16,1024]{1,0:T(8,128)(2,1)S(1)}, bf16[16,1024]{1,0:T(8,128)(2,1)S(1)}, u32[]{:S(2)}, u32[]{:S(2)}) collective-permute-start(bf16[16,1024]{1,0:T(8,128)(2,1)S(1)} %get-tuple-element.75), channel_id=1, source_target_pairs={{0,8},{1,9},{2,10},{3,11},{4,12},{5,13},{6,14},{7,15},{8,0},{9,1},... | collective-permute-start | bytes 98312 | tf_op jit(solution)/shard_map/ppermute | solution.py:225
  (122 shorter events, 36.2 us)
Async XLA Ops:
  4.9 10.1 %collective-permute-start.15 = (bf16[16,1024]{1,0:T(8,128)(2,1)S(1)}, bf16[16,1024]{1,0:T(8,128)(2,1)S(1)}, u32[]{:S(2)}, u32[]{:S(2)}) collective-permute-start(bf16[16,1024]{1,0:T(8,128)(2,1)S(1)} %get-tuple-element.66), channel_id=1, source_target_pairs={{0,4},{1,5},{2,6},{3,7},{4,0},{5,1},{6,2},{7,3},{8,12},{9,13},{10,... | collective-permute-start | bytes 98312 | tf_op jit(solution)/shard_map/ppermute | solution.py:225
  10.6 8.9 %collective-permute-start.10 = (bf16[16,1024]{1,0:T(8,128)(2,1)S(1)}, bf16[16,1024]{1,0:T(8,128)(2,1)S(1)}, u32[]{:S(2)}, u32[]{:S(2)}) collective-permute-start(bf16[16,1024]{1,0:T(8,128)(2,1)S(1)} %get-tuple-element.62), channel_id=1, source_target_pairs={{0,4},{1,5},{2,6},{3,7},{4,0},{5,1},{6,2},{7,3},{8,12},{9,13},{10,... | collective-permute-start | bytes 98312 | tf_op jit(solution)/shard_map/ppermute | solution.py:225
  11.5 8.1 %collective-permute-start.11 = (bf16[16,1024]{1,0:T(8,128)(2,1)S(1)}, bf16[16,1024]{1,0:T(8,128)(2,1)S(1)}, u32[]{:S(2)}, u32[]{:S(2)}) collective-permute-start(bf16[16,1024]{1,0:T(8,128)(2,1)S(1)} %get-tuple-element.63), channel_id=1, source_target_pairs={{0,8},{1,9},{2,10},{3,11},{4,12},{5,13},{6,14},{7,15},{8,0},{9,1},... | collective-permute-start | bytes 98312 | tf_op jit(solution)/shard_map/ppermute | solution.py:225
  15.1 8.9 %collective-permute-start.5 = (bf16[16,1024]{1,0:T(8,128)(2,1)S(1)}, bf16[16,1024]{1,0:T(8,128)(2,1)S(1)}, u32[]{:S(2)}, u32[]{:S(2)}) collective-permute-start(bf16[16,1024]{1,0:T(8,128)(2,1)S(1)} %get-tuple-element.58), channel_id=1, source_target_pairs={{0,4},{1,5},{2,6},{3,7},{4,0},{5,1},{6,2},{7,3},{8,12},{9,13},{10,... | collective-permute-start | bytes 98312 | tf_op jit(solution)/shard_map/ppermute | solution.py:225
  16.4 7.7 %collective-permute-start.6 = (bf16[16,1024]{1,0:T(8,128)(2,1)S(1)}, bf16[16,1024]{1,0:T(8,128)(2,1)S(1)}, u32[]{:S(2)}, u32[]{:S(2)}) collective-permute-start(bf16[16,1024]{1,0:T(8,128)(2,1)S(1)} %get-tuple-element.59), channel_id=1, source_target_pairs={{0,8},{1,9},{2,10},{3,11},{4,12},{5,13},{6,14},{7,15},{8,0},{9,1},... | collective-permute-start | bytes 98312 | tf_op jit(solution)/shard_map/ppermute | solution.py:225
  19.6 7.2 %collective-permute-start = (bf16[16,1024]{1,0:T(8,128)(2,1)S(1)}, bf16[16,1024]{1,0:T(8,128)(2,1)S(1)}, u32[]{:S(2)}, u32[]{:S(2)}) collective-permute-start(bf16[16,1024]{1,0:T(8,128)(2,1)S(1)} %get-tuple-element.54), channel_id=1, source_target_pairs={{0,4},{1,5},{2,6},{3,7},{4,0},{5,1},{6,2},{7,3},{8,12},{9,13},{10,... | collective-permute-start | bytes 98312 | tf_op jit(solution)/shard_map/ppermute | solution.py:225
  20.8 7.1 %collective-permute-start.1 = (bf16[16,1024]{1,0:T(8,128)(2,1)S(1)}, bf16[16,1024]{1,0:T(8,128)(2,1)S(1)}, u32[]{:S(2)}, u32[]{:S(2)}) collective-permute-start(bf16[16,1024]{1,0:T(8,128)(2,1)S(1)} %get-tuple-element.55), channel_id=1, source_target_pairs={{0,8},{1,9},{2,10},{3,11},{4,12},{5,13},{6,14},{7,15},{8,0},{9,1},... | collective-permute-start | bytes 98312 | tf_op jit(solution)/shard_map/ppermute | solution.py:225
  24.1 7.4 %collective-permute-start.18 = (bf16[64,1024]{1,0:T(8,128)(2,1)S(1)}, bf16[64,1024]{1,0:T(8,128)(2,1)S(1)}, u32[]{:S(2)}, u32[]{:S(2)}) collective-permute-start(bf16[64,1024]{1,0:T(8,128)(2,1)S(1)} %pad_maximum_fusion.3), channel_id=1, source_target_pairs={{0,2},{1,3},{2,0},{3,1},{4,6},{5,7},{6,4},{7,5},{8,10},{9,11},{10,... | collective-permute-start | bytes 393224 | tf_op jit(solution)/shard_map/ppermute | solution.py:225
  31.9 11.9 %collective-permute-start.14 = (bf16[128,1024]{1,0:T(8,128)(2,1)S(1)}, bf16[128,1024]{1,0:T(8,128)(2,1)S(1)}, u32[]{:S(2)}, u32[]{:S(2)}) collective-permute-start(bf16[128,1024]{1,0:T(8,128)(2,1)S(1)} %constant_dynamic-update-slice_fusion.10.refs_0_), channel_id=1, source_target_pairs={{0,1},{1,0},{2,3},{3,2},{4,5},{5,4},{6,7},{7,6},{8,9},{9,8},{10,11... | collective-permute-start | bytes 786440 | tf_op jit(solution)/shard_map/ppermute | solution.py:225
  33.3 16.5 %collective-permute-start.9 = (bf16[128,1024]{1,0:T(8,128)(2,1)S(1)}, bf16[128,1024]{1,0:T(8,128)(2,1)S(1)}, u32[]{:S(2)}, u32[]{:S(2)}) collective-permute-start(bf16[128,1024]{1,0:T(8,128)(2,1)S(1)} %constant_dynamic-update-slice_fusion.5.refs_0_), channel_id=1, source_target_pairs={{0,1},{1,0},{2,3},{3,2},{4,5},{5,4},{6,7},{7,6},{8,9},{9,8},{10,11... | collective-permute-start | bytes 786440 | tf_op jit(solution)/shard_map/ppermute | solution.py:225
  34.8 18.4 %collective-permute-start.4 = (bf16[128,1024]{1,0:T(8,128)(2,1)S(1)}, bf16[128,1024]{1,0:T(8,128)(2,1)S(1)}, u32[]{:S(2)}, u32[]{:S(2)}) collective-permute-start(bf16[128,1024]{1,0:T(8,128)(2,1)S(1)} %constant_dynamic-update-slice_fusion.refs_0_), channel_id=1, source_target_pairs={{0,1},{1,0},{2,3},{3,2},{4,5},{5,4},{6,7},{7,6},{8,9},{9,8},{10,11... | collective-permute-start | bytes 786440 | tf_op jit(solution)/shard_map/ppermute | solution.py:225
  73.1 8.7 %collective-permute-start.31 = (bf16[64,1024]{1,0:T(8,128)(2,1)S(1)}, bf16[64,1024]{1,0:T(8,128)(2,1)S(1)}, u32[]{:S(2)}, u32[]{:S(2)}) collective-permute-start(bf16[64,1024]{1,0:T(8,128)(2,1)S(1)} %get-tuple-element.88), channel_id=1, source_target_pairs={{0,2},{1,3},{2,0},{3,1},{4,6},{5,7},{6,4},{7,5},{8,10},{9,11},{10,... | collective-permute-start | bytes 393224 | tf_op jit(solution)/shard_map/ppermute | solution.py:225
  73.6 10.3 %collective-permute-start.26 = (bf16[64,1024]{1,0:T(8,128)(2,1)S(1)}, bf16[64,1024]{1,0:T(8,128)(2,1)S(1)}, u32[]{:S(2)}, u32[]{:S(2)}) collective-permute-start(bf16[64,1024]{1,0:T(8,128)(2,1)S(1)} %get-tuple-element.80), channel_id=1, source_target_pairs={{0,2},{1,3},{2,0},{3,1},{4,6},{5,7},{6,4},{7,5},{8,10},{9,11},{10,... | collective-permute-start | bytes 393224 | tf_op jit(solution)/shard_map/ppermute | solution.py:225
  75.3 10.4 %collective-permute-start.21 = (bf16[64,1024]{1,0:T(8,128)(2,1)S(1)}, bf16[64,1024]{1,0:T(8,128)(2,1)S(1)}, u32[]{:S(2)}, u32[]{:S(2)}) collective-permute-start(bf16[64,1024]{1,0:T(8,128)(2,1)S(1)} %get-tuple-element.72), channel_id=1, source_target_pairs={{0,2},{1,3},{2,0},{3,1},{4,6},{5,7},{6,4},{7,5},{8,10},{9,11},{10,... | collective-permute-start | bytes 393224 | tf_op jit(solution)/shard_map/ppermute | solution.py:225
  77.7 9.6 %collective-permute-start.37 = (bf16[16,1024]{1,0:T(8,128)(2,1)S(1)}, bf16[16,1024]{1,0:T(8,128)(2,1)S(1)}, u32[]{:S(2)}, u32[]{:S(2)}) collective-permute-start(bf16[16,1024]{1,0:T(8,128)(2,1)S(1)} %get-tuple-element.98), channel_id=1, source_target_pairs={{0,4},{1,5},{2,6},{3,7},{4,0},{5,1},{6,2},{7,3},{8,12},{9,13},{10,... | collective-permute-start | bytes 98312 | tf_op jit(solution)/shard_map/ppermute | solution.py:225
  78.2 10.9 %collective-permute-start.38 = (bf16[16,1024]{1,0:T(8,128)(2,1)S(1)}, bf16[16,1024]{1,0:T(8,128)(2,1)S(1)}, u32[]{:S(2)}, u32[]{:S(2)}) collective-permute-start(bf16[16,1024]{1,0:T(8,128)(2,1)S(1)} %get-tuple-element.99), channel_id=1, source_target_pairs={{0,8},{1,9},{2,10},{3,11},{4,12},{5,13},{6,14},{7,15},{8,0},{9,1},... | collective-permute-start | bytes 98312 | tf_op jit(solution)/shard_map/ppermute | solution.py:225
  81.8 8.0 %collective-permute-start.39 = (bf16[16,1024]{1,0:T(8,128)(2,1)S(1)}, bf16[16,1024]{1,0:T(8,128)(2,1)S(1)}, u32[]{:S(2)}, u32[]{:S(2)}) collective-permute-start(bf16[16,1024]{1,0:T(8,128)(2,1)S(1)} %get-tuple-element.100), channel_id=1, source_target_pairs={{0,12},{1,13},{2,14},{3,15},{4,8},{5,9},{6,10},{7,11},{8,4},{9,5},... | collective-permute-start | bytes 98312 | tf_op jit(solution)/shard_map/ppermute | solution.py:225
  83.9 7.9 %collective-permute-start.32 = (bf16[16,1024]{1,0:T(8,128)(2,1)S(1)}, bf16[16,1024]{1,0:T(8,128)(2,1)S(1)}, u32[]{:S(2)}, u32[]{:S(2)}) collective-permute-start(bf16[16,1024]{1,0:T(8,128)(2,1)S(1)} %get-tuple-element.90), channel_id=1, source_target_pairs={{0,4},{1,5},{2,6},{3,7},{4,0},{5,1},{6,2},{7,3},{8,12},{9,13},{10,... | collective-permute-start | bytes 98312 | tf_op jit(solution)/shard_map/ppermute | solution.py:225
  85.7 7.9 %collective-permute-start.33 = (bf16[16,1024]{1,0:T(8,128)(2,1)S(1)}, bf16[16,1024]{1,0:T(8,128)(2,1)S(1)}, u32[]{:S(2)}, u32[]{:S(2)}) collective-permute-start(bf16[16,1024]{1,0:T(8,128)(2,1)S(1)} %get-tuple-element.91), channel_id=1, source_target_pairs={{0,8},{1,9},{2,10},{3,11},{4,12},{5,13},{6,14},{7,15},{8,0},{9,1},... | collective-permute-start | bytes 98312 | tf_op jit(solution)/shard_map/ppermute | solution.py:225
  89.1 7.2 %collective-permute-start.27 = (bf16[16,1024]{1,0:T(8,128)(2,1)S(1)}, bf16[16,1024]{1,0:T(8,128)(2,1)S(1)}, u32[]{:S(2)}, u32[]{:S(2)}) collective-permute-start(bf16[16,1024]{1,0:T(8,128)(2,1)S(1)} %get-tuple-element.82), channel_id=1, source_target_pairs={{0,4},{1,5},{2,6},{3,7},{4,0},{5,1},{6,2},{7,3},{8,12},{9,13},{10,... | collective-permute-start | bytes 98312 | tf_op jit(solution)/shard_map/ppermute | solution.py:225
  89.8 11.6 %collective-permute-start.28 = (bf16[16,1024]{1,0:T(8,128)(2,1)S(1)}, bf16[16,1024]{1,0:T(8,128)(2,1)S(1)}, u32[]{:S(2)}, u32[]{:S(2)}) collective-permute-start(bf16[16,1024]{1,0:T(8,128)(2,1)S(1)} %get-tuple-element.83), channel_id=1, source_target_pairs={{0,8},{1,9},{2,10},{3,11},{4,12},{5,13},{6,14},{7,15},{8,0},{9,1},... | collective-permute-start | bytes 98312 | tf_op jit(solution)/shard_map/ppermute | solution.py:225
  91.9 9.5 %collective-permute-start.29 = (bf16[16,1024]{1,0:T(8,128)(2,1)S(1)}, bf16[16,1024]{1,0:T(8,128)(2,1)S(1)}, u32[]{:S(2)}, u32[]{:S(2)}) collective-permute-start(bf16[16,1024]{1,0:T(8,128)(2,1)S(1)} %get-tuple-element.84), channel_id=1, source_target_pairs={{0,12},{1,13},{2,14},{3,15},{4,8},{5,9},{6,10},{7,11},{8,4},{9,5},... | collective-permute-start | bytes 98312 | tf_op jit(solution)/shard_map/ppermute | solution.py:225
  93.6 9.4 %collective-permute-start.22 = (bf16[16,1024]{1,0:T(8,128)(2,1)S(1)}, bf16[16,1024]{1,0:T(8,128)(2,1)S(1)}, u32[]{:S(2)}, u32[]{:S(2)}) collective-permute-start(bf16[16,1024]{1,0:T(8,128)(2,1)S(1)} %get-tuple-element.74), channel_id=1, source_target_pairs={{0,4},{1,5},{2,6},{3,7},{4,0},{5,1},{6,2},{7,3},{8,12},{9,13},{10,... | collective-permute-start | bytes 98312 | tf_op jit(solution)/shard_map/ppermute | solution.py:225
  93.6 9.4 %collective-permute-start.23 = (bf16[16,1024]{1,0:T(8,128)(2,1)S(1)}, bf16[16,1024]{1,0:T(8,128)(2,1)S(1)}, u32[]{:S(2)}, u32[]{:S(2)}) collective-permute-start(bf16[16,1024]{1,0:T(8,128)(2,1)S(1)} %get-tuple-element.75), channel_id=1, source_target_pairs={{0,8},{1,9},{2,10},{3,11},{4,12},{5,13},{6,14},{7,15},{8,0},{9,1},... | collective-permute-start | bytes 98312 | tf_op jit(solution)/shard_map/ppermute | solution.py:225
  (27 other events, 214.6 us)

commit v2 on v1

--- a/solution.py
+++ b/solution.py
@@ -7,7 +7,7 @@
 from jax.experimental.pallas import tpu as pltpu
 from jax.sharding import PartitionSpec as P
 
-CHUNKS = 4
+CHUNKS = 2
 MIB = 1024 * 1024
 F32 = jnp.float32
 BF16 = jnp.bfloat16
@@ -84,7 +84,7 @@
         out_specs=pl.BlockSpec((rows, tile), lambda i: (0, i)),
         out_shape=jax.ShapeDtypeStruct((rows, hidden), BF16 if last else F32),
         scratch_shapes=[pltpu.VMEM((rows, step), BF16)],
-        compiler_params=params(20),
+        compiler_params=params(48),
         cost_estimate=pl.CostEstimate(
             flops=2 * rows * hidden * step, bytes_accessed=2 * hidden * step, transcendentals=0
         ),
@@ -92,11 +92,8 @@
     )(*args)
 
 
-def down_kernel(h_ref, w_ref, keep_ref, send_ref):
-    half = keep_ref.shape[0]
-    out = jnp.dot(h_ref[...], w_ref[...], preferred_element_type=F32)
-    keep_ref[...] = out[:half]
-    send_ref[...] = out[half:].astype(BF16)
+def down_kernel(h_ref, w_ref, out_ref):
+    out_ref[...] = jnp.dot(h_ref[...], w_ref[...], preferred_element_type=F32).astype(BF16)
 
 
 def down(h, w_down, chunk, chunks):
@@ -105,7 +102,6 @@
     step = width // chunks
     tile = min(512, step)
     per = step // tile
-    half = rows // 2
     return pl.pallas_call(
         down_kernel,
         grid=(per,),
@@ -113,38 +109,14 @@
             pl.BlockSpec((rows, hidden), lambda i: (0, 0)),
             pl.BlockSpec((hidden, tile), lambda i: (0, chunk * per + i)),
         ],
-        out_specs=[
-            pl.BlockSpec((half, tile), lambda i: (0, i)),
-            pl.BlockSpec((half, tile), lambda i: (0, i)),
-        ],
-        out_shape=[
-            jax.ShapeDtypeStruct((half, step), F32),
-            jax.ShapeDtypeStruct((half, step), BF16),
-        ],
-        compiler_params=params(20),
+        out_specs=pl.BlockSpec((rows, tile), lambda i: (0, i)),
+        out_shape=jax.ShapeDtypeStruct((rows, step), BF16),
+        compiler_params=params(48),
         cost_estimate=pl.CostEstimate(
             flops=2 * rows * hidden * step, bytes_accessed=2 * hidden * step, transcendentals=0
         ),
         name="down",
     )(h, w_down)
-
-
-def add_kernel(keep_ref, got_ref, *outs):
-    total = keep_ref[...] + got_ref[...].astype(F32)
-    at = 0
-    for out in outs:
-        out[...] = total[at:at + out.shape[0]].astype(out.dtype)
-        at += out.shape[0]
-
-
-def add(keep, got, heights, kinds):
-    width = keep.shape[1]
-    return pl.pallas_call(
-        add_kernel,
-        out_shape=[jax.ShapeDtypeStruct((h, width), k) for h, k in zip(heights, kinds)],
-        compiler_params=params(12),
-        name="add",
-    )(keep, got)
 
 
 def post_kernel(info_ref, count_ref, pick_ref, comb_ref, gate_ref, *refs, experts, filled):
@@ -215,11 +187,6 @@
     comb = combine[0]
 
     far = [d * group for d in range(1, experts)]
-    near = []
-    bit = group // 2
-    while bit:
-        near.append(bit)
-        bit //= 2
 
     def swap(x, mask):
         return lax.ppermute(x, "expert", [(i, i ^ mask) for i in range(devices)])
@@ -232,24 +199,19 @@
         name="pre",
     )(info, pick, tokens, shift, scale)
 
+    groups = [[e * group + j for j in range(group)] for e in range(experts)]
     acc = None
     for c in range(chunks):
         parts = [flat[c]] + [swap(flat[d * chunks + c], far[d - 1]) for d in range(1, experts)]
-        for mask in near:
-            whole = parts[0] if len(parts) == 1 else jnp.concatenate(parts, axis=0)
-            parts = [whole, swap(whole, mask)]
-        acc = up(parts, w_up, acc, c, chunks, rows)
+        own = jnp.concatenate(parts, axis=0)
+        every = lax.all_gather(own, "expert", axis_index_groups=groups, axis=0, tiled=True)
+        acc = up([every], w_up, acc, c, chunks, rows)
 
     out = None
     for c in range(chunks):
-        keep, send = down(acc, w_down, c, chunks)
-        for at, mask in enumerate(reversed(near)):
-            got = swap(send, mask)
-            height = keep.shape[0]
-            if at < len(near) - 1:
-                keep, send = add(keep, got, [height // 2] * 2, [F32, BF16])
-            else:
-                parts = add(keep, got, [slots] * experts, [BF16] * experts)
+        part = down(acc, w_down, c, chunks)
+        got = lax.psum_scatter(part, "expert", scatter_dimension=0, axis_index_groups=groups, tiled=True)
+        parts = [got[d * slots:(d + 1) * slots] for d in range(experts)]
         parts = [parts[0]] + [swap(parts[d], far[d - 1]) for d in range(1, experts)]
         out = post(info, count, pick, comb, gate, parts, out, c, chunks, tok_rows)
     return out

time: 105 us -> 146 us (1.39)
  waiting for transfers between devices: 9.74 us -> 70.1 us
  starting transfers between devices: 47.4 us -> 19.2 us
  between operations: 0.45 us -> 13.2 us
  local copies, waits for them, and re-layouts: 17.7 us -> 7.8 us
  Pallas kernels: 29.3 us -> 33.5 us
    reduce_scatter x0 -> x2, waiting for transfers between devices: none -> 40.7 us  [shards(): lax.psum_scatter(part, 'expert', scatter_dimension=0, axis_index_groups=g...]
    ppermute x40 -> x12, starting transfers between devices: 47.4 us -> 19 us  [swap(): return lax.ppermute(x, 'expert', [(i, i ^ mask) for i in range(devices)])]
    all_gather x0 -> x2, waiting for transfers between devices: none -> 16.5 us  [shards(): lax.all_gather(own, 'expert', axis_index_groups=groups, axis=0, tiled=True)]
    unnamed x36 -> x20, local copies, waits for them, and re-layouts: 17.6 us -> 5.89 us
    pallas_call x4 -> x2, Pallas kernels: 7.3 us -> 12.6 us  [down(): pl.pallas_call(down_kernel, grid=(per,), in_specs=[pl.BlockSpec((rows, hi...]
    ppermute x40 -> x12, waiting for transfers between devices: 9.74 us -> 12.8 us  [swap(): return lax.ppermute(x, 'expert', [(i, i ^ mask) for i in range(devices)])]
    pallas_call x4 -> x2, Pallas kernels: 6.67 us -> 3.92 us  [post(): pl.pallas_call(functools.partial(post_kernel, experts=experts, filled=out...]
    pallas_call x4 -> x2, Pallas kernels: 13.6 us -> 15.5 us  [up(): pl.pallas_call(functools.partial(up_kernel, blocks=len(parts), first=firs...]
  transfers between devices with their start and end apart: 40 -> 16, of which waited for: 8 -> 10; matrix products, arithmetic and copies ran while one was open for 0% -> 2% of each run, Pallas kernels for 16% -> 11%
where the time goes in v2:
time: 146 us; the launch traced here: 145 us
  waiting for transfers between devices  70.1 us (48%)
  Pallas kernels  33.5 us (23%)
  starting transfers between devices  19.2 us (13%)
  between operations  13.2 us (9%)
  local copies, waits for them, and re-layouts  7.8 us (5%)
  other arithmetic  1.52 us (1%)
    reduce_scatter x2, waiting for transfers between devices, shards(): lax.psum_scatter(part, 'expert', scatter_dimension=0, axis_index_groups=g...  40.7 us
    ppermute x12, starting transfers between devices, swap(): return lax.ppermute(x, 'expert', [(i, i ^ mask) for i in range(devices)])  19 us
    all_gather x2, waiting for transfers between devices, shards(): lax.all_gather(own, 'expert', axis_index_groups=groups, axis=0, tiled=True)  16.5 us
    pallas_call x2, Pallas kernels, up(): pl.pallas_call(functools.partial(up_kernel, blocks=len(parts), first=firs...  15.5 us
    ppermute x12, waiting for transfers between devices, swap(): return lax.ppermute(x, 'expert', [(i, i ^ mask) for i in range(devices)])  12.8 us
    pallas_call x2, Pallas kernels, down(): pl.pallas_call(down_kernel, grid=(per,), in_specs=[pl.BlockSpec((rows, hi...  12.6 us
    unnamed x20, local copies, waits for them, and re-layouts  5.89 us
    pallas_call x2, Pallas kernels, post(): pl.pallas_call(functools.partial(post_kernel, experts=experts, filled=out...  3.92 us
  transfers between devices with their start and end apart: 16, of which 10 were waited for; matrix products, arithmetic and copies ran while one was open for 2% of the time, Pallas kernels for 11%

profile of v2, /device:TPU:0, one launch (start us, length us, event | category | flops | bytes accessed | tf_op | source)
XLA Modules:
  0.0 145.3 jit_solution(6230272292326210008)
XLA Ops:
  10.0 1.4 pre.1
  11.4 3.1 %collective-permute-start.3 = (bf16[16,2048]{1,0:T(8,128)(2,1)S(1)}, bf16[16,2048]{1,0:T(8,128)(2,1)S(1)}, u32[]{:S(2)}, u32[]{:S(2)}) collective-permute-start(bf16[16,2048]{1,0:T(8,128)(2,1)S(1)} %get-tuple-element.18), channel_id=1, source_target_pairs={{0,4},{1,5},{2,6},{3,7},{4,0},{5,1},{6,2},{7,3},{8,12},{9,13},{10,... | collective-permute-start | bytes 196616 | tf_op jit(solution)/shard_map/ppermute | solution.py:192
  14.5 2.6 %collective-permute-start.4 = (bf16[16,2048]{1,0:T(8,128)(2,1)S(1)}, bf16[16,2048]{1,0:T(8,128)(2,1)S(1)}, u32[]{:S(2)}, u32[]{:S(2)}) collective-permute-start(bf16[16,2048]{1,0:T(8,128)(2,1)S(1)} %get-tuple-element.19), channel_id=1, source_target_pairs={{0,8},{1,9},{2,10},{3,11},{4,12},{5,13},{6,14},{7,15},{8,0},{9,1},... | collective-permute-start | bytes 196616 | tf_op jit(solution)/shard_map/ppermute | solution.py:192
  17.1 4.7 %collective-permute-done.4 = bf16[16,2048]{1,0:T(8,128)(2,1)S(1)} collective-permute-done((bf16[16,2048]{1,0:T(8,128)(2,1)S(1)}, bf16[16,2048]{1,0:T(8,128)(2,1)S(1)}, u32[]{:S(2)}, u32[]{:S(2)}) %collective-permute-start.4) | collective-permute-done | bytes 65568 | tf_op jit(solution)/shard_map/ppermute | solution.py:192
  21.8 1.4 collective-permute-done.5
  24.1 2.3 %collective-permute-start.1 = (bf16[16,2048]{1,0:T(8,128)(2,1)S(1)}, bf16[16,2048]{1,0:T(8,128)(2,1)S(1)}, u32[]{:S(2)}, u32[]{:S(2)}) collective-permute-start(bf16[16,2048]{1,0:T(8,128)(2,1)S(1)} %get-tuple-element.15), channel_id=1, source_target_pairs={{0,8},{1,9},{2,10},{3,11},{4,12},{5,13},{6,14},{7,15},{8,0},{9,1},... | collective-permute-start | bytes 196616 | tf_op jit(solution)/shard_map/ppermute | solution.py:192
  26.4 2.0 %collective-permute-start.2 = (bf16[16,2048]{1,0:T(8,128)(2,1)S(1)}, bf16[16,2048]{1,0:T(8,128)(2,1)S(1)}, u32[]{:S(2)}, u32[]{:S(2)}) collective-permute-start(bf16[16,2048]{1,0:T(8,128)(2,1)S(1)} %get-tuple-element.16), channel_id=1, source_target_pairs={{0,12},{1,13},{2,14},{3,15},{4,8},{5,9},{6,10},{7,11},{8,4},{9,5},... | collective-permute-start | bytes 196616 | tf_op jit(solution)/shard_map/ppermute | solution.py:192
  28.5 1.4 collective-permute-done.1
  29.9 2.6 %collective-permute-done.2 = bf16[16,2048]{1,0:T(8,128)(2,1)S(1)} collective-permute-done((bf16[16,2048]{1,0:T(8,128)(2,1)S(1)}, bf16[16,2048]{1,0:T(8,128)(2,1)S(1)}, u32[]{:S(2)}, u32[]{:S(2)}) %collective-permute-start.2) | collective-permute-done | bytes 65568 | tf_op jit(solution)/shard_map/ppermute | solution.py:192
  33.3 7.0 %all-gather.5.cloned.1.call-done.refs_0_ = bf16[256,2048]{1,0:T(8,128)(2,1)} async-done(((bf16[64,2048]{1,0:T(8,128)(2,1)}), bf16[256,2048]{1,0:T(8,128)(2,1)}) %all-gather.5.cloned.1.call-update) | async-done | bytes 1048592 | tf_op jit(solution)/shard_map/all_gather | solution.py:207
  40.3 1.2 copy-done
  41.5 7.7 %up.2.refs_2_ = f32[256,2048]{1,0:T(8,128)S(1)} custom-call(bf16[256,2048]{1,0:T(8,128)(2,1)S(1)} %copy-done, bf16[2048,4096]{1,0:T(8,128)(2,1)} %refs_1_.3), custom_call_target="tpu_custom_call" | custom-call | flops 2147483648 | bytes 8388608 | tf_op jit(solution)/shard_map/up/pallas_call | solution.py:80
  49.2 9.5 %all-gather.3.cloned.1.call-done.refs_0_ = bf16[256,2048]{1,0:T(8,128)(2,1)} async-done(((bf16[64,2048]{1,0:T(8,128)(2,1)}), bf16[256,2048]{1,0:T(8,128)(2,1)}) %all-gather.3.cloned.1.call-update) | async-done | bytes 1048592 | tf_op jit(solution)/shard_map/all_gather | solution.py:207
  58.6 1.2 copy-done.1
  59.9 7.9 %up.3.h_ref = bf16[256,2048]{1,0:T(8,128)(2,1)S(1)} custom-call(bf16[256,2048]{1,0:T(8,128)(2,1)S(1)} %copy-done.1, bf16[2048,4096]{1,0:T(8,128)(2,1)} %refs_1_.3, f32[256,2048]{1,0:T(8,128)S(1)} %up.2.refs_2_), custom_call_target="tpu_custom_call" | custom-call | flops 2147483648 | bytes 8388608 | tf_op jit(solution)/shard_map/up/pallas_call | solution.py:80
  67.8 6.3 %down.3 = bf16[256,2048]{1,0:T(8,128)(2,1)} custom-call(bf16[256,2048]{1,0:T(8,128)(2,1)S(1)} %up.3.h_ref, bf16[2048,4096]{1,0:T(8,128)(2,1)} %w_ref.3), custom_call_target="tpu_custom_call" | custom-call | flops 2147483648 | bytes 8388608 | tf_op jit(solution)/shard_map/down/pallas_call | solution.py:105
  74.2 6.3 %down.2 = bf16[256,2048]{1,0:T(8,128)(2,1)} custom-call(bf16[256,2048]{1,0:T(8,128)(2,1)S(1)} %up.3.h_ref, bf16[2048,4096]{1,0:T(8,128)(2,1)} %w_ref.3), custom_call_target="tpu_custom_call" | custom-call | flops 2147483648 | bytes 8388608 | tf_op jit(solution)/shard_map/down/pallas_call | solution.py:105
  80.5 18.6 %reduce-scatter.5.cloned.1.call-done = bf16[64,2048]{1,0:T(8,128)(2,1)} async-done(((bf16[256,2048]{1,0:T(8,128)(2,1)}), bf16[64,2048]{1,0:T(8,128)(2,1)}) %reduce-scatter.5.cloned.1.call-update) | async-done | bytes 262160 | tf_op jit(solution)/shard_map/reduce_scatter | solution.py:213
  100.1 3.4 %collective-permute-start.11 = (bf16[16,2048]{1,0:T(8,128)(2,1)S(1)}, bf16[16,2048]{1,0:T(8,128)(2,1)S(1)}, u32[]{:S(2)}, u32[]{:S(2)}) collective-permute-start(bf16[16,2048]{1,0:T(8,128)(2,1)S(1)} %get-tuple-element.21), channel_id=1, source_target_pairs={{0,12},{1,13},{2,14},{3,15},{4,8},{5,9},{6,10},{7,11},{8,4},{9,5},... | collective-permute-start | bytes 196616 | tf_op jit(solution)/shard_map/ppermute | solution.py:192
  104.6 22.1 %reduce-scatter.3.cloned.1.call-done = bf16[64,2048]{1,0:T(8,128)(2,1)} async-done(((bf16[256,2048]{1,0:T(8,128)(2,1)}), bf16[64,2048]{1,0:T(8,128)(2,1)}) %reduce-scatter.3.cloned.1.call-update) | async-done | bytes 262160 | tf_op jit(solution)/shard_map/reduce_scatter | solution.py:213
  127.6 3.4 %collective-permute-start.8 = (bf16[16,2048]{1,0:T(8,128)(2,1)S(1)}, bf16[16,2048]{1,0:T(8,128)(2,1)S(1)}, u32[]{:S(2)}, u32[]{:S(2)}) collective-permute-start(bf16[16,2048]{1,0:T(8,128)(2,1)S(1)} %get-tuple-element.25), channel_id=1, source_target_pairs={{0,12},{1,13},{2,14},{3,15},{4,8},{5,9},{6,10},{7,11},{8,4},{9,5},... | collective-permute-start | bytes 196616 | tf_op jit(solution)/shard_map/ppermute | solution.py:192
  132.1 2.0 %post.2.refs_4_ = bf16[128,4096]{1,0:T(8,128)(2,1)} custom-call(s32[2]{0:T(128)S(1)} %pad_add_fusion.info_ref, s32[1,4]{1,0:T(1,128)S(1)} %copy-done.9, s32[4,16]{1,0:T(4,128)S(1)} %bitcast.5, f32[4,16]{1,0:T(4,128)S(1)} %bitcast.7, f32[2,4096]{1,0:T(2,128)S(1)} %copy-done.3, bf16[16,2048]{1,0:T(8,128)(2,1)S(1)} %get-tuple-element.24.refs_0_, ...), custom_call_target="tpu_custom_call" | custom-call | tf_op jit(solution)/shard_map/post/pallas_call | solution.py:163
  134.4 2.4 %collective-permute-done.7.refs_2_ = bf16[16,2048]{1,0:T(8,128)(2,1)S(1)} collective-permute-done((bf16[16,2048]{1,0:T(8,128)(2,1)S(1)}, bf16[16,2048]{1,0:T(8,128)(2,1)S(1)}, u32[]{:S(2)}, u32[]{:S(2)}) %collective-permute-start.7) | collective-permute-done | bytes 65568 | tf_op jit(solution)/shard_map/ppermute | solution.py:192
  136.8 2.0 %post.3 = bf16[128,4096]{1,0:T(8,128)(2,1)} custom-call(s32[2]{0:T(128)S(1)} %pad_add_fusion.info_ref, s32[1,4]{1,0:T(1,128)S(1)} %copy-done.9, s32[4,16]{1,0:T(4,128)S(1)} %bitcast.6, f32[4,16]{1,0:T(4,128)S(1)} %bitcast.8, f32[2,4096]{1,0:T(2,128)S(1)} %copy-done.3, ...), custom_call_target="tpu_custom_call", output_to_operand_aliasing={{}: (9, {})} | custom-call | tf_op jit(solution)/shard_map/post/pallas_call | solution.py:163
  (44 shorter events, 9.6 us)
Async XLA Ops:
  6.5 33.7 %all-gather.5.cloned.1.call-start = ((), (), s32[]{:S(2)}) async-start(), calls=%async_computation.3 | async-start | bytes 1310720 | tf_op jit(solution)/shard_map/all_gather | solution.py:207
  6.6 1.2 copy-start.2
  7.8 0.8 copy-start.4
  11.4 5.7 %collective-permute-start.3 = (bf16[16,2048]{1,0:T(8,128)(2,1)S(1)}, bf16[16,2048]{1,0:T(8,128)(2,1)S(1)}, u32[]{:S(2)}, u32[]{:S(2)}) collective-permute-start(bf16[16,2048]{1,0:T(8,128)(2,1)S(1)} %get-tuple-element.18), channel_id=1, source_target_pairs={{0,4},{1,5},{2,6},{3,7},{4,0},{5,1},{6,2},{7,3},{8,12},{9,13},{10,... | collective-permute-start | bytes 196616 | tf_op jit(solution)/shard_map/ppermute | solution.py:192
  14.5 7.3 %collective-permute-start.4 = (bf16[16,2048]{1,0:T(8,128)(2,1)S(1)}, bf16[16,2048]{1,0:T(8,128)(2,1)S(1)}, u32[]{:S(2)}, u32[]{:S(2)}) collective-permute-start(bf16[16,2048]{1,0:T(8,128)(2,1)S(1)} %get-tuple-element.19), channel_id=1, source_target_pairs={{0,8},{1,9},{2,10},{3,11},{4,12},{5,13},{6,14},{7,15},{8,0},{9,1},... | collective-permute-start | bytes 196616 | tf_op jit(solution)/shard_map/ppermute | solution.py:192
  17.1 6.1 %collective-permute-start.5 = (bf16[16,2048]{1,0:T(8,128)(2,1)S(1)}, bf16[16,2048]{1,0:T(8,128)(2,1)S(1)}, u32[]{:S(2)}, u32[]{:S(2)}) collective-permute-start(bf16[16,2048]{1,0:T(8,128)(2,1)S(1)} %get-tuple-element.20), channel_id=1, source_target_pairs={{0,12},{1,13},{2,14},{3,15},{4,8},{5,9},{6,10},{7,11},{8,4},{9,5},... | collective-permute-start | bytes 196616 | tf_op jit(solution)/shard_map/ppermute | solution.py:192
  24.0 34.7 %all-gather.3.cloned.1.call-start = ((), (), s32[]{:S(2)}) async-start(), calls=%async_computation.2 | async-start | bytes 1310720 | tf_op jit(solution)/shard_map/all_gather | solution.py:207
  24.0 4.5 %collective-permute-start = (bf16[16,2048]{1,0:T(8,128)(2,1)S(1)}, bf16[16,2048]{1,0:T(8,128)(2,1)S(1)}, u32[]{:S(2)}, u32[]{:S(2)}) collective-permute-start(bf16[16,2048]{1,0:T(8,128)(2,1)S(1)} %get-tuple-element.14), channel_id=1, source_target_pairs={{0,4},{1,5},{2,6},{3,7},{4,0},{5,1},{6,2},{7,3},{8,12},{9,13},{10,... | collective-permute-start | bytes 196616 | tf_op jit(solution)/shard_map/ppermute | solution.py:192
  24.1 5.8 %collective-permute-start.1 = (bf16[16,2048]{1,0:T(8,128)(2,1)S(1)}, bf16[16,2048]{1,0:T(8,128)(2,1)S(1)}, u32[]{:S(2)}, u32[]{:S(2)}) collective-permute-start(bf16[16,2048]{1,0:T(8,128)(2,1)S(1)} %get-tuple-element.15), channel_id=1, source_target_pairs={{0,8},{1,9},{2,10},{3,11},{4,12},{5,13},{6,14},{7,15},{8,0},{9,1},... | collective-permute-start | bytes 196616 | tf_op jit(solution)/shard_map/ppermute | solution.py:192
  26.4 6.1 %collective-permute-start.2 = (bf16[16,2048]{1,0:T(8,128)(2,1)S(1)}, bf16[16,2048]{1,0:T(8,128)(2,1)S(1)}, u32[]{:S(2)}, u32[]{:S(2)}) collective-permute-start(bf16[16,2048]{1,0:T(8,128)(2,1)S(1)} %get-tuple-element.16), channel_id=1, source_target_pairs={{0,12},{1,13},{2,14},{3,15},{4,8},{5,9},{6,10},{7,11},{8,4},{9,5},... | collective-permute-start | bytes 196616 | tf_op jit(solution)/shard_map/ppermute | solution.py:192
  33.2 66.0 %reduce-scatter.5.cloned.1.call-start = ((), (), s32[]{:S(2)}) async-start(), calls=%async_computation.5 | async-start | bytes 1310720 | tf_op jit(solution)/shard_map/reduce_scatter | solution.py:213
  40.3 1.2 copy-start
  58.6 1.2 copy-start.1
  67.8 64.4 %copy-start.3 = (f32[2,4096]{1,0:T(2,128)S(1)}, f32[2,4096]{1,0:T(2,128)}, u32[]{:S(2)}) copy-start(f32[2,4096]{1,0:T(2,128)} %gate_ref.3) | copy-start | bytes 98308
  67.8 64.3 %copy-start.7 = (s32[1,4,16]{2,1,0:T(4,128)S(1)}, s32[1,4,16]{2,1,0:T(4,128)}, u32[]{:S(2)}) copy-start(s32[1,4,16]{2,1,0:T(4,128)} %param.15) | copy-start | bytes 772
  67.8 64.3 %copy-start.8 = (f32[1,4,16]{2,1,0:T(4,128)S(1)}, f32[1,4,16]{2,1,0:T(4,128)}, u32[]{:S(2)}) copy-start(f32[1,4,16]{2,1,0:T(4,128)} %param.17) | copy-start | bytes 772
  67.8 64.3 %copy-start.9 = (s32[1,4]{1,0:T(1,128)S(1)}, s32[1,4]{1,0:T(1,128)}, u32[]{:S(2)}) copy-start(s32[1,4]{1,0:T(1,128)} %count_ref.3) | copy-start | bytes 52
  74.2 52.5 %reduce-scatter.3.cloned.1.call-start = ((), (), s32[]{:S(2)}) async-start(), calls=%async_computation.4 | async-start | bytes 1310720 | tf_op jit(solution)/shard_map/reduce_scatter | solution.py:213
  100.1 30.9 %collective-permute-start.11 = (bf16[16,2048]{1,0:T(8,128)(2,1)S(1)}, bf16[16,2048]{1,0:T(8,128)(2,1)S(1)}, u32[]{:S(2)}, u32[]{:S(2)}) collective-permute-start(bf16[16,2048]{1,0:T(8,128)(2,1)S(1)} %get-tuple-element.21), channel_id=1, source_target_pairs={{0,12},{1,13},{2,14},{3,15},{4,8},{5,9},{6,10},{7,11},{8,4},{9,5},... | collective-permute-start | bytes 196616 | tf_op jit(solution)/shard_map/ppermute | solution.py:192
  103.5 28.6 %collective-permute-start.10 = (bf16[16,2048]{1,0:T(8,128)(2,1)S(1)}, bf16[16,2048]{1,0:T(8,128)(2,1)S(1)}, u32[]{:S(2)}, u32[]{:S(2)}) collective-permute-start(bf16[16,2048]{1,0:T(8,128)(2,1)S(1)} %get-tuple-element.22), channel_id=1, source_target_pairs={{0,8},{1,9},{2,10},{3,11},{4,12},{5,13},{6,14},{7,15},{8,0},{9,1},... | collective-permute-start | bytes 196616 | tf_op jit(solution)/shard_map/ppermute | solution.py:192
  103.5 28.6 %collective-permute-start.9 = (bf16[16,2048]{1,0:T(8,128)(2,1)S(1)}, bf16[16,2048]{1,0:T(8,128)(2,1)S(1)}, u32[]{:S(2)}, u32[]{:S(2)}) collective-permute-start(bf16[16,2048]{1,0:T(8,128)(2,1)S(1)} %get-tuple-element.23), channel_id=1, source_target_pairs={{0,4},{1,5},{2,6},{3,7},{4,0},{5,1},{6,2},{7,3},{8,12},{9,13},{10,... | collective-permute-start | bytes 196616 | tf_op jit(solution)/shard_map/ppermute | solution.py:192
  127.6 6.8 %collective-permute-start.8 = (bf16[16,2048]{1,0:T(8,128)(2,1)S(1)}, bf16[16,2048]{1,0:T(8,128)(2,1)S(1)}, u32[]{:S(2)}, u32[]{:S(2)}) collective-permute-start(bf16[16,2048]{1,0:T(8,128)(2,1)S(1)} %get-tuple-element.25), channel_id=1, source_target_pairs={{0,12},{1,13},{2,14},{3,15},{4,8},{5,9},{6,10},{7,11},{8,4},{9,5},... | collective-permute-start | bytes 196616 | tf_op jit(solution)/shard_map/ppermute | solution.py:192
  131.0 5.8 %collective-permute-start.7 = (bf16[16,2048]{1,0:T(8,128)(2,1)S(1)}, bf16[16,2048]{1,0:T(8,128)(2,1)S(1)}, u32[]{:S(2)}, u32[]{:S(2)}) collective-permute-start(bf16[16,2048]{1,0:T(8,128)(2,1)S(1)} %get-tuple-element.26), channel_id=1, source_target_pairs={{0,8},{1,9},{2,10},{3,11},{4,12},{5,13},{6,14},{7,15},{8,0},{9,1},... | collective-permute-start | bytes 196616 | tf_op jit(solution)/shard_map/ppermute | solution.py:192
  131.0 5.8 %collective-permute-start.6 = (bf16[16,2048]{1,0:T(8,128)(2,1)S(1)}, bf16[16,2048]{1,0:T(8,128)(2,1)S(1)}, u32[]{:S(2)}, u32[]{:S(2)}) collective-permute-start(bf16[16,2048]{1,0:T(8,128)(2,1)S(1)} %get-tuple-element.27), channel_id=1, source_target_pairs={{0,4},{1,5},{2,6},{3,7},{4,0},{5,1},{6,2},{7,3},{8,12},{9,13},{10,... | collective-permute-start | bytes 196616 | tf_op jit(solution)/shard_map/ppermute | solution.py:192
  (2 other events, 1.4 us)
Sparse Core Ops, SparseCore 0:
  24.1 16.1 all-gather.4
  41.8 16.7 all-gather.2
  74.3 24.8 reduce-scatter.4
  101.7 24.9 reduce-scatter.2

commit v3 on v1

v3 whole, which is shorter than its diff:
```python
import functools

import jax
import jax.numpy as jnp
from jax import lax
from jax.experimental import pallas as pl
from jax.experimental.pallas import tpu as pltpu
from jax.sharding import PartitionSpec as P

CHUNKS = 2
MIB = 1024 * 1024
F32 = jnp.float32
BF16 = jnp.bfloat16

SMEM = pl.BlockSpec(memory_space=pltpu.SMEM)
VMEM = pl.BlockSpec(memory_space=pltpu.VMEM)
HBM = pl.BlockSpec(memory_space=pltpu.HBM)
ANY = pl.BlockSpec(memory_space=pl.ANY)


FREE = pl.CostEstimate(flops=1, bytes_accessed=1, transcendentals=0)


def params(mib):
    return pltpu.CompilerParams(vmem_limit_bytes=mib * MIB)


def fetch(pairs, sems):
    copies = [pltpu.make_async_copy(src, dst, sems.at[i]) for i, (src, dst) in enumerate(pairs)]
    for copy in copies:
        copy.start()
    for copy in copies:
        copy.wait()


def slot_tokens(info_ref, pick_ref, tok_rows):
    experts, slots = pick_ref.shape
    rows = [pick_ref[pl.ds(info_ref[1] ^ d, 1), :] for d in range(experts)]
    picks = jnp.concatenate(rows, axis=1)
    return lax.broadcasted_iota(jnp.int32, (tok_rows, experts * slots), 0) == picks


def pre_kernel(info_ref, pick_hbm, tok_hbm, shift_hbm, scale_hbm, *refs, chunks):
    outs = refs[:-5]
    pick_ref, tok_ref, shift_ref, scale_ref, sems = refs[-5:]
    experts, slots = pick_ref.shape
    fetch(
        [(tok_hbm, tok_ref), (pick_hbm, pick_ref), (shift_hbm, shift_ref), (scale_hbm, scale_ref)],
        sems,
    )
    tok_rows, width = tok_ref.shape
    hot = slot_tokens(info_ref, pick_ref, tok_rows).astype(F32).astype(BF16)
    values = lax.dot_general(hot, tok_ref[...], (((0,), (0,)), ((), ())), preferred_element_type=F32)
    center = values - jnp.mean(values, axis=1, keepdims=True)
    spread = jnp.mean(center * center, axis=1, keepdims=True)
    normed = center * (1.0 / jnp.sqrt(spread + 1e-06))
    scale = scale_ref[pl.ds(info_ref[0], 1), :]
    shift = shift_ref[pl.ds(info_ref[0], 1), :]
    modulated = (normed * (1.0 + scale) + shift).astype(BF16)
    step = width // chunks
    outs[-1][...] = modulated[:slots]
    for c in range(chunks):
        for d in range(1, experts):
            outs[c * (experts - 1) + d - 1][...] = modulated[d * slots:(d + 1) * slots, c * step:(c + 1) * step]


def pre(info, pick, tokens, shift, scale, chunks):
    experts, slots = pick.shape
    width = tokens.shape[1]
    return pl.pallas_call(
        functools.partial(pre_kernel, chunks=chunks),
        in_specs=[SMEM] + [HBM] * 4,
        out_specs=[VMEM] * (chunks * (experts - 1) + 1),
        out_shape=[jax.ShapeDtypeStruct((slots, width // chunks), BF16)] * (chunks * (experts - 1))
        + [jax.ShapeDtypeStruct((slots, width), BF16)],
        scratch_shapes=[
            pltpu.VMEM(pick.shape, jnp.int32),
            pltpu.VMEM(tokens.shape, BF16),
            pltpu.VMEM(shift.shape, F32),
            pltpu.VMEM(scale.shape, F32),
            pltpu.SemaphoreType.DMA((4,)),
        ],
        compiler_params=params(16),
        cost_estimate=FREE,
        name="pre",
    )(info, pick, tokens, shift, scale)


def mixer_kernel(info_ref, count_ref, pick_hbm, comb_hbm, gate_hbm, after_ref, mix_ref, row_ref, pick_ref, comb_ref, gate_ref, sems):
    fetch([(pick_hbm, pick_ref), (comb_hbm, comb_ref), (gate_hbm, gate_ref)], sems)
    experts, slots = pick_ref.shape
    tok_rows = mix_ref.shape[0]
    hot = slot_tokens(info_ref, pick_ref, tok_rows)
    lanes = lax.broadcasted_iota(jnp.int32, (1, slots), 1)
    weights = []
    for d in range(experts):
        e = info_ref[1] ^ d
        weights.append(jnp.where(lanes < count_ref[0, e], comb_ref[pl.ds(e, 1), :], 0.0))
    mix = jnp.where(hot, jnp.concatenate(weights, axis=1), 0.0)
    high = mix.astype(BF16).astype(F32)
    rest = mix - high
    mid = rest.astype(BF16).astype(F32)
    mix_ref[...] = jnp.concatenate([high, mid, rest - mid], axis=1).astype(BF16)
    row_ref[...] = gate_ref[pl.ds(info_ref[0], 1), :]


def mixer(info, count, pick, comb, gate, after, tok_rows):
    experts, slots = pick.shape
    return pl.pallas_call(
        mixer_kernel,
        in_specs=[SMEM, SMEM] + [HBM] * 3 + [ANY],
        out_specs=[VMEM] * 2,
        out_shape=[
            jax.ShapeDtypeStruct((tok_rows, 3 * experts * slots), BF16),
            jax.ShapeDtypeStruct((1, gate.shape[1]), F32),
        ],
        scratch_shapes=[
            pltpu.VMEM(pick.shape, jnp.int32),
            pltpu.VMEM(comb.shape, F32),
            pltpu.VMEM(gate.shape, F32),
            pltpu.SemaphoreType.DMA((3,)),
        ],
        compiler_params=params(8),
        cost_estimate=FREE,
        name="mixer",
    )(info, count, pick, comb, gate, after)


def load_kernel(w_hbm, after_ref, out_ref, sems, *, chunk, pieces):
    rows, step = out_ref.shape
    part = rows // pieces
    fetch(
        [
            (
                w_hbm.at[pl.ds(p * part, part), pl.ds(chunk * step, step)],
                out_ref.at[pl.ds(p * part, part), :],
            )
            for p in range(pieces)
        ],
        sems,
    )


def load(w, after, chunk, chunks):
    rows, width = w.shape
    step = width // chunks
    pieces = 8
    return pl.pallas_call(
        functools.partial(load_kernel, chunk=chunk, pieces=pieces),
        in_specs=[HBM, ANY],
        out_specs=VMEM,
        out_shape=pltpu.VMEM((rows, step), w.dtype),
        scratch_shapes=[pltpu.SemaphoreType.DMA((pieces,))],
        compiler_params=params(4),
        cost_estimate=FREE,
        name="load",
    )(w, after)


def join_kernel(*refs, cuts):
    out_ref = refs[-1]
    at = 0
    for ref, cut in zip(refs, cuts):
        out_ref[at:at + ref.shape[0], :] = ref[...] if cut is None else ref[:, cut[0]:cut[1]]
        at += ref.shape[0]


def join(parts, after):
    arrays = [p[0] if isinstance(p, tuple) else p for p in parts]
    cuts = [p[1] if isinstance(p, tuple) else None for p in parts]
    step = min(a.shape[1] for a in arrays)
    return pl.pallas_call(
        functools.partial(join_kernel, cuts=cuts),
        in_specs=[VMEM] * len(arrays) + [ANY] * len(after),
        out_specs=VMEM,
        out_shape=jax.ShapeDtypeStruct((sum(a.shape[0] for a in arrays), step), BF16),
        compiler_params=params(4),
        cost_estimate=FREE,
        name="join",
    )(*arrays, *after)


def up_kernel(*refs, blocks, first, last):
    parts = refs[:blocks]
    w_ref = refs[blocks]
    acc_ref = None if first else refs[blocks + 1]
    out_ref, rows_ref = refs[-2:]
    at = 0
    for part in parts:
        rows_ref[at:at + part.shape[0], :] = part[...]
        at += part.shape[0]
    hidden = w_ref.shape[0]
    tile = min(256, hidden)

    @pl.loop(0, hidden // tile)
    def _(i):
        cut = pl.ds(pl.multiple_of(i * tile, tile), tile)
        lifted = lax.dot_general(
            rows_ref[...], w_ref[cut, :], (((1,), (1,)), ((), ())), preferred_element_type=F32
        )
        if not first:
            lifted = lifted + acc_ref[:, cut]
        if last:
            lifted = jax.nn.gelu(lifted, approximate=True)
        out_ref[:, cut] = lifted.astype(out_ref.dtype)


def up(parts, w, acc, first, last):
    hidden, step = w.shape
    rows = sum(p.shape[0] for p in parts)
    args = list(parts) + [w] + ([] if first else [acc])
    return pl.pallas_call(
        functools.partial(up_kernel, blocks=len(parts), first=first, last=last),
        in_specs=[VMEM] * len(args),
        out_specs=VMEM,
        out_shape=jax.ShapeDtypeStruct((rows, hidden), BF16 if last else F32),
        scratch_shapes=[pltpu.VMEM((rows, step), BF16)],
        compiler_params=params(16),
        cost_estimate=FREE,
        name="up",
    )(*args)


def down_kernel(h_ref, w_ref, after_ref, keep_ref, send_ref):
    half, step = keep_ref.shape
    tile = min(256, step)

    @pl.loop(0, step // tile)
    def _(i):
        cut = pl.ds(pl.multiple_of(i * tile, tile), tile)
        out = jnp.dot(h_ref[...], w_ref[:, cut], preferred_element_type=F32)
        keep_ref[:, cut] = out[:half]
        send_ref[:, cut] = out[half:].astype(BF16)


def down(h, w, after):
    rows, hidden = h.shape
    step = w.shape[1]
    half = rows // 2
    return pl.pallas_call(
        down_kernel,
        in_specs=[VMEM] * 2 + [ANY],
        out_specs=[VMEM] * 2,
        out_shape=[
            jax.ShapeDtypeStruct((half, step), F32),
            jax.ShapeDtypeStruct((half, step), BF16),
        ],
        compiler_params=params(16),
        cost_estimate=FREE,
        name="down",
    )(h, w, after)


def add_kernel(keep_ref, got_ref, *outs):
    at = 0
    for out in outs:
        cut = slice(at, at + out.shape[0])
        out[...] = (keep_ref[cut] + got_ref[cut].astype(F32)).astype(out.dtype)
        at += out.shape[0]


def add(keep, got, heights, kinds):
    width = keep.shape[1]
    return pl.pallas_call(
        add_kernel,
        in_specs=[VMEM] * 2,
        out_specs=[VMEM] * len(heights),
        out_shape=[jax.ShapeDtypeStruct((h, width), k) for h, k in zip(heights, kinds)],
        compiler_params=params(12),
        cost_estimate=FREE,
        name="add",
    )(keep, got)


def post_kernel(mix_ref, row_ref, *refs, experts):
    out_ref = refs[-1]
    values = jnp.concatenate([ref[...] for ref in refs[:experts]] * 3, axis=0)
    mixed = jnp.dot(mix_ref[...], values, preferred_element_type=F32)
    out_ref[...] = (row_ref[...] * mixed).astype(BF16)


def post(mix, row, parts, out, chunk, chunks):
    tok_rows = mix.shape[0]
    width = row.shape[1]
    step = width // chunks
    in_specs = [
        pl.BlockSpec(mix.shape, lambda i: (0, 0)),
        pl.BlockSpec((1, step), lambda i: (0, chunk)),
    ] + [pl.BlockSpec(p.shape, lambda i: (0, 0)) for p in parts]
    args = [mix, row] + list(parts)
    aliases = {}
    if out is not None:
        aliases = {len(args): 0}
        in_specs.append(ANY)
        args.append(out)
    return pl.pallas_call(
        functools.partial(post_kernel, experts=len(parts)),
        grid=(1,),
        in_specs=in_specs,
        out_specs=pl.BlockSpec((tok_rows, step), lambda i: (0, chunk)),
        out_shape=jax.ShapeDtypeStruct((tok_rows, width), BF16),
        input_output_aliases=aliases,
        compiler_params=params(12),
        cost_estimate=FREE,
        name="post",
    )(*args)


def shards(tokens, shift, scale, gate, w_up, w_down, pick, count, combine):
    tok_rows, width = tokens.shape
    _, experts, slots = pick.shape
    devices = lax.axis_size("expert")
    place = lax.axis_index("expert")
    group = devices // experts
    requests = shift.shape[0]
    chunks = CHUNKS
    step = width // chunks
    info = jnp.stack([place // (devices // requests), place // group]).astype(jnp.int32)
    pick = pick[0]
    comb = combine[0]

    far = [d * group for d in range(1, experts)]
    near = []
    bit = group // 2
    while bit:
        near.append(bit)
        bit //= 2

    def swap(x, mask):
        return lax.ppermute(x, "expert", [(i, i ^ mask) for i in range(devices)])

    tokens, shift, scale, gate, w_up, w_down, pick, comb = [
        pltpu.with_memory_space_constraint(x, pltpu.HBM)
        for x in (tokens, shift, scale, gate, w_up, w_down, pick, comb)
    ]
    *flat, own = pre(info, pick, tokens, shift, scale, chunks)
    got = []
    for c in range(chunks):
        got.append([swap(flat[c * (experts - 1) + d - 1], far[d - 1]) for d in range(1, experts)])
    own_near = swap(own, near[0])

    acc = None
    downs = []
    after = own
    mix, row = mixer(info, count, pick, comb, gate, own, tok_rows)
    for c in range(chunks):
        cut = (c * step, (c + 1) * step)
        w = load(w_up, after, c, chunks)
        block = join(got[c], [w, own_near])
        after = block
        parts = [(own, cut), block, (own_near, cut), swap(block, near[0])]
        for mask in near[1:]:
            block = join(parts, [])
            parts = [block, swap(block, mask)]
        downs.append(load(w_down, block, c, chunks))
        acc = up(parts, w, acc, c == 0, c == chunks - 1)

    out = None
    for c in range(chunks):
        keep, send = down(acc, downs[c], downs[-1])
        for at, mask in enumerate(reversed(near)):
            arrived = swap(send, mask)
            height = keep.shape[0]
            if at < len(near) - 1:
                keep, send = add(keep, arrived, [height // 2] * 2, [F32, BF16])
            else:
                parts = add(keep, arrived, [slots] * experts, [BF16] * experts)
        parts = [parts[0]] + [swap(parts[d], far[d - 1]) for d in range(1, experts)]
        out = post(mix, row, parts, out, c, chunks)
    return out


def solution(mesh):
    return jax.shard_map(
        shards,
        mesh=mesh,
        in_specs=(
            P(("groups", "expert"), None),
            P("groups", None),
            P("groups", None),
            P("groups", None),
            P("expert", None),
            P("expert", None),
            P(("groups", "expert"), None, None),
            P(("groups", "expert"), None),
            P(("groups", "expert"), None, None),
        ),
        out_specs=P(("groups", "expert"), None),
        check_vma=False,
    )
```

time: 105 us -> 83.2 us (0.79)
  local copies, waits for them, and re-layouts: 17.7 us -> 0.01 us
  starting transfers between devices: 47.4 us -> 31.5 us
  Pallas kernels: 29.3 us -> 39.2 us
  waiting for transfers between devices: 9.74 us -> 12 us
    unnamed x36 -> x6, local copies, waits for them, and re-layouts: 17.6 us -> 0.01 us
    ppermute x40 -> x21, starting transfers between devices: 47.4 us -> 31.5 us  [swap(): return lax.ppermute(x, 'expert', [(i, i ^ mask) for i in range(devices)])]
    pallas_call x17 -> x18, Pallas kernels: 15.7 us -> 31.2 us  [the longest x4 16.9 us: load(): pl.pallas_call(functools.partial(load_kernel, chunk=chunk, pieces=pieces)...]
    pallas_call x4 -> x2, Pallas kernels: 13.6 us -> 8.02 us  [up(): pl.pallas_call(functools.partial(up_kernel, blocks=len(parts), first=firs...]
    ppermute x40 -> x21, waiting for transfers between devices: 9.74 us -> 12 us  [swap(): return lax.ppermute(x, 'expert', [(i, i ^ mask) for i in range(devices)])]
  transfers between devices with their start and end apart: 40 -> 21, of which waited for: 8 -> 6; matrix products, arithmetic and copies ran while one was open for 0% -> 0% of each run, Pallas kernels for 16% -> 33%
where the time goes in v3:
time: 83.2 us; the launch traced here: 83 us
  Pallas kernels  39.2 us (47%)
  starting transfers between devices  31.5 us (38%)
  waiting for transfers between devices  12 us (14%)
    ppermute x21, starting transfers between devices, swap(): return lax.ppermute(x, 'expert', [(i, i ^ mask) for i in range(devices)])  31.5 us
    pallas_call x4, Pallas kernels, load(): pl.pallas_call(functools.partial(load_kernel, chunk=chunk, pieces=pieces)...  16.9 us
    ppermute x21, waiting for transfers between devices, swap(): return lax.ppermute(x, 'expert', [(i, i ^ mask) for i in range(devices)])  12 us
    pallas_call x2, Pallas kernels, up(): pl.pallas_call(functools.partial(up_kernel, blocks=len(parts), first=firs...  8.02 us
    pallas_call x2, Pallas kernels, down(): pl.pallas_call(down_kernel, in_specs=[VMEM] * 2 + [ANY], out_specs=[VMEM]...  7.48 us
    pallas_call x1, Pallas kernels, pre(): pl.pallas_call(functools.partial(pre_kernel, chunks=chunks), in_specs=[SM...  2.67 us
    pallas_call x2, Pallas kernels, post(): pl.pallas_call(functools.partial(post_kernel, experts=len(parts)), grid=(...  2.18 us
  transfers between devices with their start and end apart: 21, of which 6 were waited for; matrix products, arithmetic and copies ran while one was open for 0% of the time, Pallas kernels for 33%

profile of v3, /device:TPU:0, one launch (start us, length us, event | category | flops | bytes accessed | tf_op | source)
XLA Modules:
  0.0 83.0 jit_solution(1122790314194974905)
XLA Ops:
  0.1 2.7 %pre.1 = (bf16[16,2048]{1,0:T(8,128)(2,1)S(1)}, bf16[16,2048]{1,0:T(8,128)(2,1)S(1)}, bf16[16,2048]{1,0:T(8,128)(2,1)S(1)}, bf16[16,2048]{1,0:T(8,128)(2,1)S(1)}...) custom-call(s32[2]{0:T(128)S(1)} %pad_add_fusion.info_ref, ...), custom_call_target="tpu_custom_call" | custom-call | flops 1 | bytes 1 | tf_op jit(solution)/shard_map/pre/pallas_call | solution.py:70
  2.8 3.0 %collective-permute-start.6 = (bf16[16,4096]{1,0:T(8,128)(2,1)S(1)}, bf16[16,4096]{1,0:T(8,128)(2,1)S(1)}, u32[]{:S(2)}, u32[]{:S(2)}) collective-permute-start(bf16[16,4096]{1,0:T(8,128)(2,1)S(1)} %get-tuple-element.30.after_ref.refs_0_), channel_id=1, source_target_pairs={{0,2},{1,3},{2,0},{3,1},{4,6},{5,7},{6,4},{7,5},{8,10},{9,11},{10,... | collective-permute-start | bytes 393224 | tf_op jit(solution)/shard_map/ppermute | solution.py:330
  5.8 1.6 %collective-permute-start.3 = (bf16[16,2048]{1,0:T(8,128)(2,1)S(1)}, bf16[16,2048]{1,0:T(8,128)(2,1)S(1)}, u32[]{:S(2)}, u32[]{:S(2)}) collective-permute-start(bf16[16,2048]{1,0:T(8,128)(2,1)S(1)} %get-tuple-element.36), channel_id=1, source_target_pairs={{0,4},{1,5},{2,6},{3,7},{4,0},{5,1},{6,2},{7,3},{8,12},{9,13},{10,... | collective-permute-start | bytes 196616 | tf_op jit(solution)/shard_map/ppermute | solution.py:330
  7.4 2.6 %collective-permute-start.4 = (bf16[16,2048]{1,0:T(8,128)(2,1)S(1)}, bf16[16,2048]{1,0:T(8,128)(2,1)S(1)}, u32[]{:S(2)}, u32[]{:S(2)}) collective-permute-start(bf16[16,2048]{1,0:T(8,128)(2,1)S(1)} %get-tuple-element.37), channel_id=1, source_target_pairs={{0,8},{1,9},{2,10},{3,11},{4,12},{5,13},{6,14},{7,15},{8,0},{9,1},... | collective-permute-start | bytes 196616 | tf_op jit(solution)/shard_map/ppermute | solution.py:330
  10.9 3.5 %collective-permute-start.1 = (bf16[16,2048]{1,0:T(8,128)(2,1)S(1)}, bf16[16,2048]{1,0:T(8,128)(2,1)S(1)}, u32[]{:S(2)}, u32[]{:S(2)}) collective-permute-start(bf16[16,2048]{1,0:T(8,128)(2,1)S(1)} %get-tuple-element.34), channel_id=1, source_target_pairs={{0,8},{1,9},{2,10},{3,11},{4,12},{5,13},{6,14},{7,15},{8,0},{9,1},... | collective-permute-start | bytes 196616 | tf_op jit(solution)/shard_map/ppermute | solution.py:330
  14.6 4.9 %collective-permute-start.2 = (bf16[16,2048]{1,0:T(8,128)(2,1)S(1)}, bf16[16,2048]{1,0:T(8,128)(2,1)S(1)}, u32[]{:S(2)}, u32[]{:S(2)}) collective-permute-start(bf16[16,2048]{1,0:T(8,128)(2,1)S(1)} %get-tuple-element.35), channel_id=1, source_target_pairs={{0,12},{1,13},{2,14},{3,15},{4,8},{5,9},{6,10},{7,11},{8,4},{9,5},... | collective-permute-start | bytes 196616 | tf_op jit(solution)/shard_map/ppermute | solution.py:330
  19.4 3.5 %load.4.refs_3_.refs_2_ = bf16[2048,2048]{1,0:T(8,128)(2,1)S(1)} custom-call(bf16[2048,4096]{1,0:T(8,128)(2,1)} %w_hbm.5, bf16[16,4096]{1,0:T(8,128)(2,1)S(1)} %get-tuple-element.30.after_ref.refs_0_), custom_call_target="tpu_custom_call" | custom-call | flops 1 | bytes 1 | tf_op jit(solution)/shard_map/load/pallas_call | solution.py:148
  23.5 3.5 %load.5.refs_3_.refs_2_ = bf16[2048,2048]{1,0:T(8,128)(2,1)S(1)} custom-call(bf16[2048,4096]{1,0:T(8,128)(2,1)} %w_hbm.5, bf16[48,2048]{1,0:T(8,128)(2,1)S(1)} %join.4.after_ref.refs_1_), custom_call_target="tpu_custom_call" | custom-call | flops 1 | bytes 1 | tf_op jit(solution)/shard_map/load/pallas_call | solution.py:148
  27.0 1.6 %collective-permute-start.7 = (bf16[48,2048]{1,0:T(8,128)(2,1)S(1)}, bf16[48,2048]{1,0:T(8,128)(2,1)S(1)}, u32[]{:S(2)}, u32[]{:S(2)}) collective-permute-start(bf16[48,2048]{1,0:T(8,128)(2,1)S(1)} %join.5.refs_1_), channel_id=1, source_target_pairs={{0,2},{1,3},{2,0},{3,1},{4,6},{5,7},{6,4},{7,5},{8,10},{9,11},{10,... | collective-permute-start | bytes 589832 | tf_op jit(solution)/shard_map/ppermute | solution.py:330
  28.8 4.0 %collective-permute-done.7.refs_3_ = bf16[48,2048]{1,0:T(8,128)(2,1)S(1)} collective-permute-done((bf16[48,2048]{1,0:T(8,128)(2,1)S(1)}, bf16[48,2048]{1,0:T(8,128)(2,1)S(1)}, u32[]{:S(2)}, u32[]{:S(2)}) %collective-permute-start.7) | collective-permute-done | bytes 196640 | tf_op jit(solution)/shard_map/ppermute | solution.py:330
  32.9 3.5 %load.7.w_ref = bf16[2048,2048]{1,0:T(8,128)(2,1)S(1)} custom-call(bf16[2048,4096]{1,0:T(8,128)(2,1)} %w_hbm.7, bf16[128,2048]{1,0:T(8,128)(2,1)S(1)} %join.7.refs_0_.after_ref), custom_call_target="tpu_custom_call" | custom-call | flops 1 | bytes 1 | tf_op jit(solution)/shard_map/load/pallas_call | solution.py:148
  36.4 6.5 %load.6.w_ref.after_ref = bf16[2048,2048]{1,0:T(8,128)(2,1)S(1)} custom-call(bf16[2048,4096]{1,0:T(8,128)(2,1)} %w_hbm.7, bf16[128,2048]{1,0:T(8,128)(2,1)S(1)} %join.6.refs_0_.after_ref), custom_call_target="tpu_custom_call" | custom-call | flops 1 | bytes 1 | tf_op jit(solution)/shard_map/load/pallas_call | solution.py:148
  42.9 3.8 %up.2.refs_3_ = f32[256,2048]{1,0:T(8,128)S(1)} custom-call(bf16[128,2048]{1,0:T(8,128)(2,1)S(1)} %join.7.refs_0_.after_ref, bf16[128,2048]{1,0:T(8,128)(2,1)S(1)} %collective-permute-done.10.refs_1_, bf16[2048,2048]{1,0:T(8,128)(2,1)S(1)} %load.4.refs_3_.refs_2_), custom_call_target="tpu_custom_call" | custom-call | flops 1 | bytes 1 | tf_op jit(solution)/shard_map/up/pallas_call | solution.py:212
  46.8 4.2 %up.3.h_ref = bf16[256,2048]{1,0:T(8,128)(2,1)S(1)} custom-call(bf16[128,2048]{1,0:T(8,128)(2,1)S(1)} %join.6.refs_0_.after_ref, bf16[128,2048]{1,0:T(8,128)(2,1)S(1)} %collective-permute-done.8.refs_1_, bf16[2048,2048]{1,0:T(8,128)(2,1)S(1)} %load.5.refs_3_.refs_2_, f32[256,2048]{1,0:T(8,128)S(1)} %up.2.refs_3_), custom_call_target="tpu_custom_call" | custom-call | flops 1 | bytes 1 | tf_op jit(solution)/shard_map/up/pallas_call | solution.py:212
  51.0 3.7 %down.3 = (f32[128,2048]{1,0:T(8,128)S(1)}, bf16[128,2048]{1,0:T(8,128)(2,1)S(1)}) custom-call(bf16[256,2048]{1,0:T(8,128)(2,1)S(1)} %up.3.h_ref, bf16[2048,2048]{1,0:T(8,128)(2,1)S(1)} %copy-done.1, bf16[2048,2048]{1,0:T(8,128)(2,1)S(1)} %load.6.w_ref.after_ref), custom_call_target="tpu_custom_call" | custom-call | flops 1 | bytes 1 | tf_op jit(solution)/shard_map/down/pallas_call | solution.py:240
  55.3 3.7 %down.2 = (f32[128,2048]{1,0:T(8,128)S(1)}, bf16[128,2048]{1,0:T(8,128)(2,1)S(1)}) custom-call(bf16[256,2048]{1,0:T(8,128)(2,1)S(1)} %up.3.h_ref, bf16[2048,2048]{1,0:T(8,128)(2,1)S(1)} %load.6.w_ref.after_ref, bf16[2048,2048]{1,0:T(8,128)(2,1)S(1)} %load.6.w_ref.after_ref), custom_call_target="tpu_custom_call" | custom-call | flops 1 | bytes 1 | tf_op jit(solution)/shard_map/down/pallas_call | solution.py:240
  59.2 1.6 %collective-permute-start.17 = (bf16[64,2048]{1,0:T(8,128)(2,1)S(1)}, bf16[64,2048]{1,0:T(8,128)(2,1)S(1)}, u32[]{:S(2)}, u32[]{:S(2)}) collective-permute-start(bf16[64,2048]{1,0:T(8,128)(2,1)S(1)} %get-tuple-element.50), channel_id=1, source_target_pairs={{0,2},{1,3},{2,0},{3,1},{4,6},{5,7},{6,4},{7,5},{8,10},{9,11},{10,... | collective-permute-start | bytes 786440 | tf_op jit(solution)/shard_map/ppermute | solution.py:330
  61.1 1.6 %collective-permute-start.12 = (bf16[64,2048]{1,0:T(8,128)(2,1)S(1)}, bf16[64,2048]{1,0:T(8,128)(2,1)S(1)}, u32[]{:S(2)}, u32[]{:S(2)}) collective-permute-start(bf16[64,2048]{1,0:T(8,128)(2,1)S(1)} %get-tuple-element.42), channel_id=1, source_target_pairs={{0,2},{1,3},{2,0},{3,1},{4,6},{5,7},{6,4},{7,5},{8,10},{9,11},{10,... | collective-permute-start | bytes 786440 | tf_op jit(solution)/shard_map/ppermute | solution.py:330
  62.7 5.7 %collective-permute-done.17.got_ref = bf16[64,2048]{1,0:T(8,128)(2,1)S(1)} collective-permute-done((bf16[64,2048]{1,0:T(8,128)(2,1)S(1)}, bf16[64,2048]{1,0:T(8,128)(2,1)S(1)}, u32[]{:S(2)}, u32[]{:S(2)}) %collective-permute-start.17) | collective-permute-done | bytes 262176 | tf_op jit(solution)/shard_map/ppermute | solution.py:330
  69.1 3.8 %collective-permute-start.20 = (bf16[16,2048]{1,0:T(8,128)(2,1)S(1)}, bf16[16,2048]{1,0:T(8,128)(2,1)S(1)}, u32[]{:S(2)}, u32[]{:S(2)}) collective-permute-start(bf16[16,2048]{1,0:T(8,128)(2,1)S(1)} %get-tuple-element.54), channel_id=1, source_target_pairs={{0,12},{1,13},{2,14},{3,15},{4,8},{5,9},{6,10},{7,11},{8,4},{9,5},... | collective-permute-start | bytes 196616 | tf_op jit(solution)/shard_map/ppermute | solution.py:330
  74.3 3.8 %collective-permute-start.15 = (bf16[16,2048]{1,0:T(8,128)(2,1)S(1)}, bf16[16,2048]{1,0:T(8,128)(2,1)S(1)}, u32[]{:S(2)}, u32[]{:S(2)}) collective-permute-start(bf16[16,2048]{1,0:T(8,128)(2,1)S(1)} %get-tuple-element.46), channel_id=1, source_target_pairs={{0,12},{1,13},{2,14},{3,15},{4,8},{5,9},{6,10},{7,11},{8,4},{9,5},... | collective-permute-start | bytes 196616 | tf_op jit(solution)/shard_map/ppermute | solution.py:330
  78.1 1.5 %mixer.1 = (bf16[128,192]{1,0:T(8,128)(2,1)S(1)}, f32[1,4096]{1,0:T(1,128)S(1)}) custom-call(s32[2]{0:T(128)S(1)} %pad_add_fusion.info_ref, s32[1,4]{1,0:T(1,128)S(1)} %copy-done.2, s32[4,16]{1,0:T(4,128)} %bitcast.5, f32[4,16]{1,0:T(4,128)} %bitcast.6, f32[2,4096]{1,0:T(2,128)} %gate_hbm.1, bf16[16,4096]{1,0:T(8,128)(2,1)S(1)} %get-tuple-element.30.after_ref.refs_0_), custom_call_target="tpu_custom_call" | custom-call | flops 1 | bytes 1 | tf_op jit(solution)/shard_map/mixer/pallas_call | solution.py:109
  79.7 1.1 %post.2.refs_4_ = bf16[128,4096]{1,0:T(8,128)(2,1)} custom-call(bf16[128,192]{1,0:T(8,128)(2,1)S(1)} %get-tuple-element.31.mix_ref, f32[1,4096]{1,0:T(1,128)S(1)} %get-tuple-element.32.row_ref, bf16[16,2048]{1,0:T(8,128)(2,1)S(1)} %get-tuple-element.51.refs_0_, bf16[16,2048]{1,0:T(8,128)(2,1)S(1)} %collective-permute-done.18.refs_1_, ...), custom_call_target="tpu_custom_call" | custom-call | flops 1 | bytes 1 | tf_op jit(solution)/shard_map/post/pallas_call | solution.py:296
  80.8 1.1 %collective-permute-done.14.refs_2_ = bf16[16,2048]{1,0:T(8,128)(2,1)S(1)} collective-permute-done((bf16[16,2048]{1,0:T(8,128)(2,1)S(1)}, bf16[16,2048]{1,0:T(8,128)(2,1)S(1)}, u32[]{:S(2)}, u32[]{:S(2)}) %collective-permute-start.14) | collective-permute-done | bytes 65568 | tf_op jit(solution)/shard_map/ppermute | solution.py:330
  (45 shorter events, 6.2 us)
Async XLA Ops:
  2.8 20.1 %collective-permute-start.6 = (bf16[16,4096]{1,0:T(8,128)(2,1)S(1)}, bf16[16,4096]{1,0:T(8,128)(2,1)S(1)}, u32[]{:S(2)}, u32[]{:S(2)}) collective-permute-start(bf16[16,4096]{1,0:T(8,128)(2,1)S(1)} %get-tuple-element.30.after_ref.refs_0_), channel_id=1, source_target_pairs={{0,2},{1,3},{2,0},{3,1},{4,6},{5,7},{6,4},{7,5},{8,10},{9,11},{10,... | collective-permute-start | bytes 393224 | tf_op jit(solution)/shard_map/ppermute | solution.py:330
  5.8 5.1 %collective-permute-start.3 = (bf16[16,2048]{1,0:T(8,128)(2,1)S(1)}, bf16[16,2048]{1,0:T(8,128)(2,1)S(1)}, u32[]{:S(2)}, u32[]{:S(2)}) collective-permute-start(bf16[16,2048]{1,0:T(8,128)(2,1)S(1)} %get-tuple-element.36), channel_id=1, source_target_pairs={{0,4},{1,5},{2,6},{3,7},{4,0},{5,1},{6,2},{7,3},{8,12},{9,13},{10,... | collective-permute-start | bytes 196616 | tf_op jit(solution)/shard_map/ppermute | solution.py:330
  7.4 7.2 %collective-permute-start.4 = (bf16[16,2048]{1,0:T(8,128)(2,1)S(1)}, bf16[16,2048]{1,0:T(8,128)(2,1)S(1)}, u32[]{:S(2)}, u32[]{:S(2)}) collective-permute-start(bf16[16,2048]{1,0:T(8,128)(2,1)S(1)} %get-tuple-element.37), channel_id=1, source_target_pairs={{0,8},{1,9},{2,10},{3,11},{4,12},{5,13},{6,14},{7,15},{8,0},{9,1},... | collective-permute-start | bytes 196616 | tf_op jit(solution)/shard_map/ppermute | solution.py:330
  10.0 12.9 %collective-permute-start.5 = (bf16[16,2048]{1,0:T(8,128)(2,1)S(1)}, bf16[16,2048]{1,0:T(8,128)(2,1)S(1)}, u32[]{:S(2)}, u32[]{:S(2)}) collective-permute-start(bf16[16,2048]{1,0:T(8,128)(2,1)S(1)} %get-tuple-element.38), channel_id=1, source_target_pairs={{0,12},{1,13},{2,14},{3,15},{4,8},{5,9},{6,10},{7,11},{8,4},{9,5},... | collective-permute-start | bytes 196616 | tf_op jit(solution)/shard_map/ppermute | solution.py:330
  10.2 16.8 %collective-permute-start = (bf16[16,2048]{1,0:T(8,128)(2,1)S(1)}, bf16[16,2048]{1,0:T(8,128)(2,1)S(1)}, u32[]{:S(2)}, u32[]{:S(2)}) collective-permute-start(bf16[16,2048]{1,0:T(8,128)(2,1)S(1)} %get-tuple-element.33), channel_id=1, source_target_pairs={{0,4},{1,5},{2,6},{3,7},{4,0},{5,1},{6,2},{7,3},{8,12},{9,13},{10,... | collective-permute-start | bytes 196616 | tf_op jit(solution)/shard_map/ppermute | solution.py:330
  10.9 16.1 %collective-permute-start.1 = (bf16[16,2048]{1,0:T(8,128)(2,1)S(1)}, bf16[16,2048]{1,0:T(8,128)(2,1)S(1)}, u32[]{:S(2)}, u32[]{:S(2)}) collective-permute-start(bf16[16,2048]{1,0:T(8,128)(2,1)S(1)} %get-tuple-element.34), channel_id=1, source_target_pairs={{0,8},{1,9},{2,10},{3,11},{4,12},{5,13},{6,14},{7,15},{8,0},{9,1},... | collective-permute-start | bytes 196616 | tf_op jit(solution)/shard_map/ppermute | solution.py:330
  14.6 12.5 %collective-permute-start.2 = (bf16[16,2048]{1,0:T(8,128)(2,1)S(1)}, bf16[16,2048]{1,0:T(8,128)(2,1)S(1)}, u32[]{:S(2)}, u32[]{:S(2)}) collective-permute-start(bf16[16,2048]{1,0:T(8,128)(2,1)S(1)} %get-tuple-element.35), channel_id=1, source_target_pairs={{0,12},{1,13},{2,14},{3,15},{4,8},{5,9},{6,10},{7,11},{8,4},{9,5},... | collective-permute-start | bytes 196616 | tf_op jit(solution)/shard_map/ppermute | solution.py:330
  22.9 5.7 %collective-permute-start.9 = (bf16[48,2048]{1,0:T(8,128)(2,1)S(1)}, bf16[48,2048]{1,0:T(8,128)(2,1)S(1)}, u32[]{:S(2)}, u32[]{:S(2)}) collective-permute-start(bf16[48,2048]{1,0:T(8,128)(2,1)S(1)} %join.4.after_ref.refs_1_), channel_id=1, source_target_pairs={{0,2},{1,3},{2,0},{3,1},{4,6},{5,7},{6,4},{7,5},{8,10},{9,11},{10,... | collective-permute-start | bytes 589832 | tf_op jit(solution)/shard_map/ppermute | solution.py:330
  27.0 5.7 %collective-permute-start.7 = (bf16[48,2048]{1,0:T(8,128)(2,1)S(1)}, bf16[48,2048]{1,0:T(8,128)(2,1)S(1)}, u32[]{:S(2)}, u32[]{:S(2)}) collective-permute-start(bf16[48,2048]{1,0:T(8,128)(2,1)S(1)} %join.5.refs_1_), channel_id=1, source_target_pairs={{0,2},{1,3},{2,0},{3,1},{4,6},{5,7},{6,4},{7,5},{8,10},{9,11},{10,... | collective-permute-start | bytes 589832 | tf_op jit(solution)/shard_map/ppermute | solution.py:330
  28.7 14.2 %collective-permute-start.10 = (bf16[128,2048]{1,0:T(8,128)(2,1)S(1)}, bf16[128,2048]{1,0:T(8,128)(2,1)S(1)}, u32[]{:S(2)}, u32[]{:S(2)}) collective-permute-start(bf16[128,2048]{1,0:T(8,128)(2,1)S(1)} %join.7.refs_0_.after_ref), channel_id=1, source_target_pairs={{0,1},{1,0},{2,3},{3,2},{4,5},{5,4},{6,7},{7,6},{8,9},{9,8},{10,11... | collective-permute-start | bytes 1572872 | tf_op jit(solution)/shard_map/ppermute | solution.py:330
  32.8 14.0 %collective-permute-start.8 = (bf16[128,2048]{1,0:T(8,128)(2,1)S(1)}, bf16[128,2048]{1,0:T(8,128)(2,1)S(1)}, u32[]{:S(2)}, u32[]{:S(2)}) collective-permute-start(bf16[128,2048]{1,0:T(8,128)(2,1)S(1)} %join.6.refs_0_.after_ref), channel_id=1, source_target_pairs={{0,1},{1,0},{2,3},{3,2},{4,5},{5,4},{6,7},{7,6},{8,9},{9,8},{10,11... | collective-permute-start | bytes 1572872 | tf_op jit(solution)/shard_map/ppermute | solution.py:330
  36.4 6.5 %copy-start = (bf16[2048,2048]{1,0:T(8,128)(2,1)}, bf16[2048,2048]{1,0:T(8,128)(2,1)S(1)}, u32[]{:S(2)}) copy-start(bf16[2048,2048]{1,0:T(8,128)(2,1)S(1)} %load.7.w_ref) | copy-start | bytes 25165828
  46.8 4.2 %copy-start.1 = (bf16[2048,2048]{1,0:T(8,128)(2,1)S(1)}, bf16[2048,2048]{1,0:T(8,128)(2,1)}, u32[]{:S(2)}) copy-start(bf16[2048,2048]{1,0:T(8,128)(2,1)} %copy-done) | copy-start | bytes 25165828
  54.7 23.4 %copy-start.2 = (s32[1,4]{1,0:T(1,128)S(1)}, s32[1,4]{1,0:T(1,128)}, u32[]{:S(2)}) copy-start(s32[1,4]{1,0:T(1,128)} %count_ref.1) | copy-start | bytes 52
  54.8 4.4 %collective-permute-start.16 = (bf16[128,2048]{1,0:T(8,128)(2,1)S(1)}, bf16[128,2048]{1,0:T(8,128)(2,1)S(1)}, u32[]{:S(2)}, u32[]{:S(2)}) collective-permute-start(bf16[128,2048]{1,0:T(8,128)(2,1)S(1)} %get-tuple-element.48), channel_id=1, source_target_pairs={{0,1},{1,0},{2,3},{3,2},{4,5},{5,4},{6,7},{7,6},{8,9},{9,8},{10,11... | collective-permute-start | bytes 1572872 | tf_op jit(solution)/shard_map/ppermute | solution.py:330
  59.1 2.0 %collective-permute-start.11 = (bf16[128,2048]{1,0:T(8,128)(2,1)S(1)}, bf16[128,2048]{1,0:T(8,128)(2,1)S(1)}, u32[]{:S(2)}, u32[]{:S(2)}) collective-permute-start(bf16[128,2048]{1,0:T(8,128)(2,1)S(1)} %get-tuple-element.40), channel_id=1, source_target_pairs={{0,1},{1,0},{2,3},{3,2},{4,5},{5,4},{6,7},{7,6},{8,9},{9,8},{10,11... | collective-permute-start | bytes 1572872 | tf_op jit(solution)/shard_map/ppermute | solution.py:330
  59.2 9.2 %collective-permute-start.17 = (bf16[64,2048]{1,0:T(8,128)(2,1)S(1)}, bf16[64,2048]{1,0:T(8,128)(2,1)S(1)}, u32[]{:S(2)}, u32[]{:S(2)}) collective-permute-start(bf16[64,2048]{1,0:T(8,128)(2,1)S(1)} %get-tuple-element.50), channel_id=1, source_target_pairs={{0,2},{1,3},{2,0},{3,1},{4,6},{5,7},{6,4},{7,5},{8,10},{9,11},{10,... | collective-permute-start | bytes 786440 | tf_op jit(solution)/shard_map/ppermute | solution.py:330
  61.1 12.5 %collective-permute-start.12 = (bf16[64,2048]{1,0:T(8,128)(2,1)S(1)}, bf16[64,2048]{1,0:T(8,128)(2,1)S(1)}, u32[]{:S(2)}, u32[]{:S(2)}) collective-permute-start(bf16[64,2048]{1,0:T(8,128)(2,1)S(1)} %get-tuple-element.42), channel_id=1, source_target_pairs={{0,2},{1,3},{2,0},{3,1},{4,6},{5,7},{6,4},{7,5},{8,10},{9,11},{10,... | collective-permute-start | bytes 786440 | tf_op jit(solution)/shard_map/ppermute | solution.py:330
  68.5 5.8 %collective-permute-start.18 = (bf16[16,2048]{1,0:T(8,128)(2,1)S(1)}, bf16[16,2048]{1,0:T(8,128)(2,1)S(1)}, u32[]{:S(2)}, u32[]{:S(2)}) collective-permute-start(bf16[16,2048]{1,0:T(8,128)(2,1)S(1)} %get-tuple-element.52), channel_id=1, source_target_pairs={{0,4},{1,5},{2,6},{3,7},{4,0},{5,1},{6,2},{7,3},{8,12},{9,13},{10,... | collective-permute-start | bytes 196616 | tf_op jit(solution)/shard_map/ppermute | solution.py:330
  68.5 11.1 %collective-permute-start.19 = (bf16[16,2048]{1,0:T(8,128)(2,1)S(1)}, bf16[16,2048]{1,0:T(8,128)(2,1)S(1)}, u32[]{:S(2)}, u32[]{:S(2)}) collective-permute-start(bf16[16,2048]{1,0:T(8,128)(2,1)S(1)} %get-tuple-element.53), channel_id=1, source_target_pairs={{0,8},{1,9},{2,10},{3,11},{4,12},{5,13},{6,14},{7,15},{8,0},{9,1},... | collective-permute-start | bytes 196616 | tf_op jit(solution)/shard_map/ppermute | solution.py:330
  69.1 10.6 %collective-permute-start.20 = (bf16[16,2048]{1,0:T(8,128)(2,1)S(1)}, bf16[16,2048]{1,0:T(8,128)(2,1)S(1)}, u32[]{:S(2)}, u32[]{:S(2)}) collective-permute-start(bf16[16,2048]{1,0:T(8,128)(2,1)S(1)} %get-tuple-element.54), channel_id=1, source_target_pairs={{0,12},{1,13},{2,14},{3,15},{4,8},{5,9},{6,10},{7,11},{8,4},{9,5},... | collective-permute-start | bytes 196616 | tf_op jit(solution)/shard_map/ppermute | solution.py:330
  73.7 7.1 %collective-permute-start.13 = (bf16[16,2048]{1,0:T(8,128)(2,1)S(1)}, bf16[16,2048]{1,0:T(8,128)(2,1)S(1)}, u32[]{:S(2)}, u32[]{:S(2)}) collective-permute-start(bf16[16,2048]{1,0:T(8,128)(2,1)S(1)} %get-tuple-element.44), channel_id=1, source_target_pairs={{0,4},{1,5},{2,6},{3,7},{4,0},{5,1},{6,2},{7,3},{8,12},{9,13},{10,... | collective-permute-start | bytes 196616 | tf_op jit(solution)/shard_map/ppermute | solution.py:330
  73.8 8.2 %collective-permute-start.14 = (bf16[16,2048]{1,0:T(8,128)(2,1)S(1)}, bf16[16,2048]{1,0:T(8,128)(2,1)S(1)}, u32[]{:S(2)}, u32[]{:S(2)}) collective-permute-start(bf16[16,2048]{1,0:T(8,128)(2,1)S(1)} %get-tuple-element.45), channel_id=1, source_target_pairs={{0,8},{1,9},{2,10},{3,11},{4,12},{5,13},{6,14},{7,15},{8,0},{9,1},... | collective-permute-start | bytes 196616 | tf_op jit(solution)/shard_map/ppermute | solution.py:330
  74.3 7.6 %collective-permute-start.15 = (bf16[16,2048]{1,0:T(8,128)(2,1)S(1)}, bf16[16,2048]{1,0:T(8,128)(2,1)S(1)}, u32[]{:S(2)}, u32[]{:S(2)}) collective-permute-start(bf16[16,2048]{1,0:T(8,128)(2,1)S(1)} %get-tuple-element.46), channel_id=1, source_target_pairs={{0,12},{1,13},{2,14},{3,15},{4,8},{5,9},{6,10},{7,11},{8,4},{9,5},... | collective-permute-start | bytes 196616 | tf_op jit(solution)/shard_map/ppermute | solution.py:330

commit v4 on v3

--- a/solution.py
+++ b/solution.py
@@ -8,6 +8,7 @@
 from jax.sharding import PartitionSpec as P
 
 CHUNKS = 2
+PIECES = 8
 MIB = 1024 * 1024
 F32 = jnp.float32
 BF16 = jnp.bfloat16
@@ -33,9 +34,13 @@
         copy.wait()
 
 
+def turns(experts):
+    return [0] + list(range(experts - 1, 0, -1))
+
+
 def slot_tokens(info_ref, pick_ref, tok_rows):
     experts, slots = pick_ref.shape
-    rows = [pick_ref[pl.ds(info_ref[1] ^ d, 1), :] for d in range(experts)]
+    rows = [pick_ref[pl.ds(info_ref[1] ^ d, 1), :] for d in turns(experts)]
     picks = jnp.concatenate(rows, axis=1)
     return lax.broadcasted_iota(jnp.int32, (tok_rows, experts * slots), 0) == picks
 
@@ -93,7 +98,7 @@
     hot = slot_tokens(info_ref, pick_ref, tok_rows)
     lanes = lax.broadcasted_iota(jnp.int32, (1, slots), 1)
     weights = []
-    for d in range(experts):
+    for d in turns(experts):
         e = info_ref[1] ^ d
         weights.append(jnp.where(lanes < count_ref[0, e], comb_ref[pl.ds(e, 1), :], 0.0))
     mix = jnp.where(hot, jnp.concatenate(weights, axis=1), 0.0)
@@ -126,37 +131,6 @@
     )(info, count, pick, comb, gate, after)
 
 
-def load_kernel(w_hbm, after_ref, out_ref, sems, *, chunk, pieces):
-    rows, step = out_ref.shape
-    part = rows // pieces
-    fetch(
-        [
-            (
-                w_hbm.at[pl.ds(p * part, part), pl.ds(chunk * step, step)],
-                out_ref.at[pl.ds(p * part, part), :],
-            )
-            for p in range(pieces)
-        ],
-        sems,
-    )
-
-
-def load(w, after, chunk, chunks):
-    rows, width = w.shape
-    step = width // chunks
-    pieces = 8
-    return pl.pallas_call(
-        functools.partial(load_kernel, chunk=chunk, pieces=pieces),
-        in_specs=[HBM, ANY],
-        out_specs=VMEM,
-        out_shape=pltpu.VMEM((rows, step), w.dtype),
-        scratch_shapes=[pltpu.SemaphoreType.DMA((pieces,))],
-        compiler_params=params(4),
-        cost_estimate=FREE,
-        name="load",
-    )(w, after)
-
-
 def join_kernel(*refs, cuts):
     out_ref = refs[-1]
     at = 0
@@ -180,50 +154,102 @@
     )(*arrays, *after)
 
 
-def up_kernel(*refs, blocks, first, last):
+def stream(w_hbm, out_ref, sems, chunk):
+    rows, step = out_ref.shape
+    pieces = sems.shape[0]
+    part = rows // pieces
+    return [
+        pltpu.make_async_copy(
+            w_hbm.at[pl.ds(p * part, part), pl.ds(chunk * step, step)],
+            out_ref.at[pl.ds(p * part, part), :],
+            sems.at[p],
+        )
+        for p in range(pieces)
+    ]
+
+
+def load_kernel(w_hbm, after_ref, out_ref, sems, *, chunk):
+    copies = stream(w_hbm, out_ref, sems, chunk)
+    for copy in copies:
+        copy.start()
+    for copy in copies:
+        copy.wait()
+
+
+def load(w, after, chunk, chunks):
+    rows, width = w.shape
+    step = width // chunks
+    return pl.pallas_call(
+        functools.partial(load_kernel, chunk=chunk),
+        in_specs=[HBM, ANY],
+        out_specs=VMEM,
+        out_shape=pltpu.VMEM((rows, step), w.dtype),
+        scratch_shapes=[pltpu.SemaphoreType.DMA((PIECES,))],
+        compiler_params=params(2),
+        cost_estimate=FREE,
+        name="load",
+    )(w, after)
+
+
+def up_kernel(*refs, blocks, first, last, chunk):
     parts = refs[:blocks]
-    w_ref = refs[blocks]
-    acc_ref = None if first else refs[blocks + 1]
-    out_ref, rows_ref = refs[-2:]
+    w_ref, next_hbm = refs[blocks:blocks + 2]
+    acc_ref = None if first else refs[blocks + 2]
+    out_ref, next_ref, rows_ref, sems = refs[-4:]
+    copies = stream(next_hbm, next_ref, sems, chunk)
+    for copy in copies:
+        copy.start()
     at = 0
     for part in parts:
         rows_ref[at:at + part.shape[0], :] = part[...]
         at += part.shape[0]
     hidden = w_ref.shape[0]
-    tile = min(256, hidden)
-
-    @pl.loop(0, hidden // tile)
-    def _(i):
-        cut = pl.ds(pl.multiple_of(i * tile, tile), tile)
+    tile = min(1024, hidden)
+
+    for i in range(hidden // tile):
+        cut = slice(i * tile, (i + 1) * tile)
         lifted = lax.dot_general(
-            rows_ref[...], w_ref[cut, :], (((1,), (1,)), ((), ())), preferred_element_type=F32
+            w_ref[cut, :], rows_ref[...], (((1,), (1,)), ((), ())), preferred_element_type=F32
         )
         if not first:
-            lifted = lifted + acc_ref[:, cut]
+            lifted = lifted + acc_ref[cut, :]
         if last:
-            lifted = jax.nn.gelu(lifted, approximate=True)
-        out_ref[:, cut] = lifted.astype(out_ref.dtype)
-
-
-def up(parts, w, acc, first, last):
+            out_ref[:, cut] = jax.nn.gelu(lifted, approximate=True).astype(BF16).T
+        else:
+            out_ref[cut, :] = lifted
+    for copy in copies:
+        copy.wait()
+
+
+def up(parts, w, acc, last, following, chunk, chunks):
     hidden, step = w.shape
     rows = sum(p.shape[0] for p in parts)
-    args = list(parts) + [w] + ([] if first else [acc])
-    return pl.pallas_call(
-        functools.partial(up_kernel, blocks=len(parts), first=first, last=last),
-        in_specs=[VMEM] * len(args),
-        out_specs=VMEM,
-        out_shape=jax.ShapeDtypeStruct((rows, hidden), BF16 if last else F32),
-        scratch_shapes=[pltpu.VMEM((rows, step), BF16)],
-        compiler_params=params(16),
+    first = acc is None
+    args = list(parts) + [w, following] + ([] if first else [acc])
+    out = jax.ShapeDtypeStruct((rows, hidden), BF16) if last else jax.ShapeDtypeStruct((hidden, rows), F32)
+    return pl.pallas_call(
+        functools.partial(up_kernel, blocks=len(parts), first=first, last=last, chunk=chunk),
+        in_specs=[VMEM] * len(parts) + [VMEM, HBM] + [VMEM] * (0 if first else 1),
+        out_specs=[VMEM] * 2,
+        out_shape=[out, pltpu.VMEM((following.shape[0], following.shape[1] // chunks), BF16)],
+        scratch_shapes=[pltpu.VMEM((rows, step), BF16), pltpu.SemaphoreType.DMA((PIECES,))],
+        compiler_params=params(12),
         cost_estimate=FREE,
         name="up",
     )(*args)
 
 
-def down_kernel(h_ref, w_ref, after_ref, keep_ref, send_ref):
+def down_kernel(h_ref, w_ref, *refs, chunk):
+    if chunk is not None:
+        next_hbm, keep_ref, send_ref, next_ref, sems = refs
+        copies = stream(next_hbm, next_ref, sems, chunk)
+    else:
+        keep_ref, send_ref = refs
+        copies = []
+    for copy in copies:
+        copy.start()
     half, step = keep_ref.shape
-    tile = min(256, step)
+    tile = min(512, step)
 
     @pl.loop(0, step // tile)
     def _(i):
@@ -232,23 +258,29 @@
         keep_ref[:, cut] = out[:half]
         send_ref[:, cut] = out[half:].astype(BF16)
 
-
-def down(h, w, after):
-    rows, hidden = h.shape
+    for copy in copies:
+        copy.wait()
+
+
+def down(h, w, following, chunk):
+    rows = h.shape[0]
     step = w.shape[1]
     half = rows // 2
-    return pl.pallas_call(
-        down_kernel,
-        in_specs=[VMEM] * 2 + [ANY],
-        out_specs=[VMEM] * 2,
+    more = chunk is not None
+    return pl.pallas_call(
+        functools.partial(down_kernel, chunk=chunk),
+        in_specs=[VMEM] * 2 + [HBM] * more,
+        out_specs=[VMEM] * (2 + more),
         out_shape=[
             jax.ShapeDtypeStruct((half, step), F32),
             jax.ShapeDtypeStruct((half, step), BF16),
-        ],
-        compiler_params=params(16),
+        ]
+        + [pltpu.VMEM(w.shape, BF16)] * more,
+        scratch_shapes=[pltpu.SemaphoreType.DMA((PIECES,))] * more,
+        compiler_params=params(8),
         cost_estimate=FREE,
         name="down",
-    )(h, w, after)
+    )(*([h, w] + [following] * more))
 
 
 def add_kernel(keep_ref, got_ref, *outs):
@@ -319,7 +351,7 @@
     pick = pick[0]
     comb = combine[0]
 
-    far = [d * group for d in range(1, experts)]
+    far = [d * group for d in turns(experts)[1:]]
     near = []
     bit = group // 2
     while bit:
@@ -336,28 +368,28 @@
     *flat, own = pre(info, pick, tokens, shift, scale, chunks)
     got = []
     for c in range(chunks):
-        got.append([swap(flat[c * (experts - 1) + d - 1], far[d - 1]) for d in range(1, experts)])
+        got.append([swap(flat[c * (experts - 1) + i], mask) for i, mask in enumerate(far)])
     own_near = swap(own, near[0])
 
+    mix, row = mixer(info, count, pick, comb, gate, own, tok_rows)
+    w = load(w_up, mix, 0, chunks)
     acc = None
-    downs = []
-    after = own
-    mix, row = mixer(info, count, pick, comb, gate, own, tok_rows)
     for c in range(chunks):
         cut = (c * step, (c + 1) * step)
-        w = load(w_up, after, c, chunks)
-        block = join(got[c], [w, own_near])
-        after = block
+        block = join(got[c], [own_near, w] if c == 0 else [])
         parts = [(own, cut), block, (own_near, cut), swap(block, near[0])]
         for mask in near[1:]:
             block = join(parts, [])
             parts = [block, swap(block, mask)]
-        downs.append(load(w_down, block, c, chunks))
-        acc = up(parts, w, acc, c == 0, c == chunks - 1)
+        last = c == chunks - 1
+        acc, w = up(parts, w, acc, last, w_down if last else w_up, 0 if last else c + 1, chunks)
 
     out = None
     for c in range(chunks):
-        keep, send = down(acc, downs[c], downs[-1])
+        if c < chunks - 1:
+            keep, send, w = down(acc, w, w_down, c + 1)
+        else:
+            keep, send = down(acc, w, None, None)
         for at, mask in enumerate(reversed(near)):
             arrived = swap(send, mask)
             height = keep.shape[0]
@@ -365,7 +397,7 @@
                 keep, send = add(keep, arrived, [height // 2] * 2, [F32, BF16])
             else:
                 parts = add(keep, arrived, [slots] * experts, [BF16] * experts)
-        parts = [parts[0]] + [swap(parts[d], far[d - 1]) for d in range(1, experts)]
+        parts = [parts[0]] + [swap(part, mask) for part, mask in zip(parts[1:], far)]
         out = post(mix, row, parts, out, c, chunks)
     return out
 

time: 83.2 us -> 72.7 us (0.87)
  Pallas kernels: 39.2 us -> 25.5 us
  waiting for transfers between devices: 12 us -> 20.7 us
  starting transfers between devices: 31.5 us -> 25.4 us
    pallas_call x6 -> x3, Pallas kernels: 24.4 us -> 9.81 us  [the longest x2 6.34 us: down(): pl.pallas_call(functools.partial(down_kernel, chunk=chunk), in_specs=[VME...]
    ppermute x21, waiting for transfers between devices: 12 us -> 20.7 us  [swap(): return lax.ppermute(x, 'expert', [(i, i ^ mask) for i in range(devices)])]
    ppermute x21, starting transfers between devices: 31.5 us -> 25.4 us  [swap(): return lax.ppermute(x, 'expert', [(i, i ^ mask) for i in range(devices)])]
    pallas_call x2, Pallas kernels: 8.02 us -> 8.96 us  [up(): pl.pallas_call(functools.partial(up_kernel, blocks=len(parts), first=firs...]
  transfers between devices with their start and end apart: 21 -> 21, of which waited for: 6 -> 9; matrix products, arithmetic and copies ran while one was open for 0% -> 0% of each run, Pallas kernels for 33% -> 20%
where the time goes in v4:
time: 72.7 us; the launch traced here: 72.5 us
  Pallas kernels  25.5 us (35%)
  starting transfers between devices  25.4 us (35%)
  waiting for transfers between devices  20.7 us (28%)
    ppermute x21, starting transfers between devices, swap(): return lax.ppermute(x, 'expert', [(i, i ^ mask) for i in range(devices)])  25.4 us
    ppermute x21, waiting for transfers between devices, swap(): return lax.ppermute(x, 'expert', [(i, i ^ mask) for i in range(devices)])  20.7 us
    pallas_call x2, Pallas kernels, up(): pl.pallas_call(functools.partial(up_kernel, blocks=len(parts), first=firs...  8.96 us
    pallas_call x2, Pallas kernels, down(): pl.pallas_call(functools.partial(down_kernel, chunk=chunk), in_specs=[VME...  6.34 us
    pallas_call x1, Pallas kernels, load(): pl.pallas_call(functools.partial(load_kernel, chunk=chunk), in_specs=[HBM...  3.48 us
    pallas_call x1, Pallas kernels, pre(): pl.pallas_call(functools.partial(pre_kernel, chunks=chunks), in_specs=[SM...  2.67 us
    pallas_call x2, Pallas kernels, post(): pl.pallas_call(functools.partial(post_kernel, experts=len(parts)), grid=(...  2.18 us
    pallas_call x1, Pallas kernels, mixer(): pl.pallas_call(mixer_kernel, in_specs=[SMEM, SMEM] + [HBM] * 3 + [ANY], o...  1.53 us
  transfers between devices with their start and end apart: 21, of which 9 were waited for; matrix products, arithmetic and copies ran while one was open for 0% of the time, Pallas kernels for 20%

profile of v4, /device:TPU:0, one launch (start us, length us, event | category | flops | bytes accessed | tf_op | source)
XLA Modules:
  0.0 72.5 jit_solution(1127168427516868409)
XLA Ops:
  0.1 2.7 %pre.1 = (bf16[16,2048]{1,0:T(8,128)(2,1)S(1)}, bf16[16,2048]{1,0:T(8,128)(2,1)S(1)}, bf16[16,2048]{1,0:T(8,128)(2,1)S(1)}, bf16[16,2048]{1,0:T(8,128)(2,1)S(1)}...) custom-call(s32[2]{0:T(128)S(1)} %pad_add_fusion.info_ref, ...), custom_call_target="tpu_custom_call" | custom-call | flops 1 | bytes 1 | tf_op jit(solution)/shard_map/pre/pallas_call | solution.py:75
  2.8 5.1 %collective-permute-start.6 = (bf16[16,2048]{1,0:T(8,128)(2,1)S(1)}, bf16[16,2048]{1,0:T(8,128)(2,1)S(1)}, u32[]{:S(2)}, u32[]{:S(2)}) collective-permute-start(bf16[16,2048]{1,0:T(8,128)(2,1)S(1)} %get-tuple-element.41), channel_id=1, source_target_pairs={{0,12},{1,13},{2,14},{3,15},{4,8},{5,9},{6,10},{7,11},{8,4},{9,5},... | collective-permute-start | bytes 196616 | tf_op jit(solution)/shard_map/ppermute | solution.py:362
  7.9 1.5 %collective-permute-start.3 = (bf16[16,4096]{1,0:T(8,128)(2,1)S(1)}, bf16[16,4096]{1,0:T(8,128)(2,1)S(1)}, u32[]{:S(2)}, u32[]{:S(2)}) collective-permute-start(bf16[16,4096]{1,0:T(8,128)(2,1)S(1)} %get-tuple-element.35.after_ref.refs_0_), channel_id=1, source_target_pairs={{0,2},{1,3},{2,0},{3,1},{4,6},{5,7},{6,4},{7,5},{8,10},{9,11},{10,... | collective-permute-start | bytes 393224 | tf_op jit(solution)/shard_map/ppermute | solution.py:362
  9.4 1.9 %collective-permute-start = (bf16[16,2048]{1,0:T(8,128)(2,1)S(1)}, bf16[16,2048]{1,0:T(8,128)(2,1)S(1)}, u32[]{:S(2)}, u32[]{:S(2)}) collective-permute-start(bf16[16,2048]{1,0:T(8,128)(2,1)S(1)} %get-tuple-element.38), channel_id=1, source_target_pairs={{0,12},{1,13},{2,14},{3,15},{4,8},{5,9},{6,10},{7,11},{8,4},{9,5},... | collective-permute-start | bytes 196616 | tf_op jit(solution)/shard_map/ppermute | solution.py:362
  11.3 1.6 %collective-permute-start.8 = (bf16[16,2048]{1,0:T(8,128)(2,1)S(1)}, bf16[16,2048]{1,0:T(8,128)(2,1)S(1)}, u32[]{:S(2)}, u32[]{:S(2)}) collective-permute-start(bf16[16,2048]{1,0:T(8,128)(2,1)S(1)} %get-tuple-element.43), channel_id=1, source_target_pairs={{0,4},{1,5},{2,6},{3,7},{4,0},{5,1},{6,2},{7,3},{8,12},{9,13},{10,... | collective-permute-start | bytes 196616 | tf_op jit(solution)/shard_map/ppermute | solution.py:362
  12.9 0.9 %collective-permute-start.1 = (bf16[16,2048]{1,0:T(8,128)(2,1)S(1)}, bf16[16,2048]{1,0:T(8,128)(2,1)S(1)}, u32[]{:S(2)}, u32[]{:S(2)}) collective-permute-start(bf16[16,2048]{1,0:T(8,128)(2,1)S(1)} %get-tuple-element.39), channel_id=1, source_target_pairs={{0,8},{1,9},{2,10},{3,11},{4,12},{5,13},{6,14},{7,15},{8,0},{9,1},... | collective-permute-start | bytes 196616 | tf_op jit(solution)/shard_map/ppermute | solution.py:362
  13.8 3.5 %collective-permute-done.7.refs_1_ = bf16[16,2048]{1,0:T(8,128)(2,1)S(1)} collective-permute-done((bf16[16,2048]{1,0:T(8,128)(2,1)S(1)}, bf16[16,2048]{1,0:T(8,128)(2,1)S(1)}, u32[]{:S(2)}, u32[]{:S(2)}) %collective-permute-start.7) | collective-permute-done | bytes 65568 | tf_op jit(solution)/shard_map/ppermute | solution.py:362
  17.9 1.5 %mixer.1 = (bf16[128,192]{1,0:T(8,128)(2,1)S(1)}, f32[1,4096]{1,0:T(1,128)S(1)}) custom-call(s32[2]{0:T(128)S(1)} %pad_add_fusion.info_ref, s32[1,4]{1,0:T(1,128)S(1)} %copy-done, s32[4,16]{1,0:T(4,128)} %bitcast.5, f32[4,16]{1,0:T(4,128)} %bitcast.6, f32[2,4096]{1,0:T(2,128)} %gate_hbm.1, bf16[16,4096]{1,0:T(8,128)(2,1)S(1)} %get-tuple-element.35.after_ref.refs_0_), custom_call_target="tpu_custom_call" | custom-call | flops 1 | bytes 1 | tf_op jit(solution)/shard_map/mixer/pallas_call | solution.py:114
  19.4 3.5 %load.1.refs_4_.refs_2_ = bf16[2048,2048]{1,0:T(8,128)(2,1)S(1)} custom-call(bf16[2048,4096]{1,0:T(8,128)(2,1)} %refs_3_.2, bf16[128,192]{1,0:T(8,128)(2,1)S(1)} %get-tuple-element.36.after_ref.mix_ref), custom_call_target="tpu_custom_call" | custom-call | flops 1 | bytes 1 | tf_op jit(solution)/shard_map/load/pallas_call | solution.py:182
  23.5 1.6 %collective-permute-start.4 = (bf16[48,2048]{1,0:T(8,128)(2,1)S(1)}, bf16[48,2048]{1,0:T(8,128)(2,1)S(1)}, u32[]{:S(2)}, u32[]{:S(2)}) collective-permute-start(bf16[48,2048]{1,0:T(8,128)(2,1)S(1)} %join.4.refs_1_), channel_id=1, source_target_pairs={{0,2},{1,3},{2,0},{3,1},{4,6},{5,7},{6,4},{7,5},{8,10},{9,11},{10,... | collective-permute-start | bytes 589832 | tf_op jit(solution)/shard_map/ppermute | solution.py:362
  25.2 3.5 %collective-permute-done.9.refs_3_ = bf16[48,2048]{1,0:T(8,128)(2,1)S(1)} collective-permute-done((bf16[48,2048]{1,0:T(8,128)(2,1)S(1)}, bf16[48,2048]{1,0:T(8,128)(2,1)S(1)}, u32[]{:S(2)}, u32[]{:S(2)}) %collective-permute-start.9) | collective-permute-done | bytes 196640 | tf_op jit(solution)/shard_map/ppermute | solution.py:362
  28.8 2.0 %collective-permute-done.4.refs_3_ = bf16[48,2048]{1,0:T(8,128)(2,1)S(1)} collective-permute-done((bf16[48,2048]{1,0:T(8,128)(2,1)S(1)}, bf16[48,2048]{1,0:T(8,128)(2,1)S(1)}, u32[]{:S(2)}, u32[]{:S(2)}) %collective-permute-start.4) | collective-permute-done | bytes 196640 | tf_op jit(solution)/shard_map/ppermute | solution.py:362
  30.9 5.5 %up.2 = (f32[2048,256]{1,0:T(8,128)S(1)}, bf16[2048,2048]{1,0:T(8,128)(2,1)S(1)}) custom-call(bf16[128,2048]{1,0:T(8,128)(2,1)S(1)} %join.7.refs_0_, bf16[128,2048]{1,0:T(8,128)(2,1)S(1)} %collective-permute-done.10.refs_1_, bf16[2048,2048]{1,0:T(8,128)(2,1)S(1)} %load.1.refs_4_.refs_2_, bf16[2048,4096]{1,0:T(8,128)(2,1)} %refs_3_.2), custom_call_target="tpu_custom_call" | custom-call | flops 1 | bytes 1 | tf_op jit(solution)/shard_map/up/pallas_call | solution.py:230
  36.4 3.5 %up.3 = (bf16[256,2048]{1,0:T(8,128)(2,1)S(1)}, bf16[2048,2048]{1,0:T(8,128)(2,1)S(1)}) custom-call(bf16[128,2048]{1,0:T(8,128)(2,1)S(1)} %join.5.refs_0_, bf16[128,2048]{1,0:T(8,128)(2,1)S(1)} %collective-permute-done.5.refs_1_, bf16[2048,2048]{1,0:T(8,128)(2,1)S(1)} %get-tuple-element.44.refs_2_, bf16[2048,4096]{1,0:T(8,128)(2,1)} %refs_0_.1, ...), custom_call_target="tpu_custom_call" | custom-call | flops 1 | bytes 1 | tf_op jit(solution)/shard_map/up/pallas_call | solution.py:230
  39.9 3.5 %down.2 = (f32[128,2048]{1,0:T(8,128)S(1)}, bf16[128,2048]{1,0:T(8,128)(2,1)S(1)}, bf16[2048,2048]{1,0:T(8,128)(2,1)S(1)}) custom-call(bf16[256,2048]{1,0:T(8,128)(2,1)S(1)} %get-tuple-element.46.h_ref, bf16[2048,2048]{1,0:T(8,128)(2,1)S(1)} %get-tuple-element.47.w_ref, bf16[2048,4096]{1,0:T(8,128)(2,1)} %refs_0_.1), custom_call_target="tpu_custom_call" | custom-call | flops 1 | bytes 1 | tf_op jit(solution)/shard_map/down/pallas_call | solution.py:270
  44.0 2.9 %down.3 = (f32[128,2048]{1,0:T(8,128)S(1)}, bf16[128,2048]{1,0:T(8,128)(2,1)S(1)}) custom-call(bf16[256,2048]{1,0:T(8,128)(2,1)S(1)} %get-tuple-element.46.h_ref, bf16[2048,2048]{1,0:T(8,128)(2,1)S(1)} %get-tuple-element.48.w_ref), custom_call_target="tpu_custom_call" | custom-call | flops 1 | bytes 1 | tf_op jit(solution)/shard_map/down/pallas_call | solution.py:270
  47.0 1.3 %collective-permute-start.17 = (bf16[64,2048]{1,0:T(8,128)(2,1)S(1)}, bf16[64,2048]{1,0:T(8,128)(2,1)S(1)}, u32[]{:S(2)}, u32[]{:S(2)}) collective-permute-start(bf16[64,2048]{1,0:T(8,128)(2,1)S(1)} %get-tuple-element.60), channel_id=1, source_target_pairs={{0,2},{1,3},{2,0},{3,1},{4,6},{5,7},{6,4},{7,5},{8,10},{9,11},{10,... | collective-permute-start | bytes 786440 | tf_op jit(solution)/shard_map/ppermute | solution.py:362
  48.9 1.3 %collective-permute-start.12 = (bf16[64,2048]{1,0:T(8,128)(2,1)S(1)}, bf16[64,2048]{1,0:T(8,128)(2,1)S(1)}, u32[]{:S(2)}, u32[]{:S(2)}) collective-permute-start(bf16[64,2048]{1,0:T(8,128)(2,1)S(1)} %get-tuple-element.52), channel_id=1, source_target_pairs={{0,2},{1,3},{2,0},{3,1},{4,6},{5,7},{6,4},{7,5},{8,10},{9,11},{10,... | collective-permute-start | bytes 786440 | tf_op jit(solution)/shard_map/ppermute | solution.py:362
  50.1 6.0 %collective-permute-done.17.got_ref = bf16[64,2048]{1,0:T(8,128)(2,1)S(1)} collective-permute-done((bf16[64,2048]{1,0:T(8,128)(2,1)S(1)}, bf16[64,2048]{1,0:T(8,128)(2,1)S(1)}, u32[]{:S(2)}, u32[]{:S(2)}) %collective-permute-start.17) | collective-permute-done | bytes 262176 | tf_op jit(solution)/shard_map/ppermute | solution.py:362
  56.2 3.5 %collective-permute-start.18 = (bf16[16,2048]{1,0:T(8,128)(2,1)S(1)}, bf16[16,2048]{1,0:T(8,128)(2,1)S(1)}, u32[]{:S(2)}, u32[]{:S(2)}) collective-permute-start(bf16[16,2048]{1,0:T(8,128)(2,1)S(1)} %get-tuple-element.62), channel_id=1, source_target_pairs={{0,12},{1,13},{2,14},{3,15},{4,8},{5,9},{6,10},{7,11},{8,4},{9,5},... | collective-permute-start | bytes 196616 | tf_op jit(solution)/shard_map/ppermute | solution.py:362
  61.4 3.5 %collective-permute-start.13 = (bf16[16,2048]{1,0:T(8,128)(2,1)S(1)}, bf16[16,2048]{1,0:T(8,128)(2,1)S(1)}, u32[]{:S(2)}, u32[]{:S(2)}) collective-permute-start(bf16[16,2048]{1,0:T(8,128)(2,1)S(1)} %get-tuple-element.54), channel_id=1, source_target_pairs={{0,12},{1,13},{2,14},{3,15},{4,8},{5,9},{6,10},{7,11},{8,4},{9,5},... | collective-permute-start | bytes 196616 | tf_op jit(solution)/shard_map/ppermute | solution.py:362
  66.3 1.1 %post.2.refs_4_ = bf16[128,4096]{1,0:T(8,128)(2,1)} custom-call(bf16[128,192]{1,0:T(8,128)(2,1)S(1)} %get-tuple-element.36.after_ref.mix_ref, f32[1,4096]{1,0:T(1,128)S(1)} %get-tuple-element.37.row_ref, bf16[16,2048]{1,0:T(8,128)(2,1)S(1)} %get-tuple-element.61.refs_0_, bf16[16,2048]{1,0:T(8,128)(2,1)S(1)} %collective-permute-done.18.refs_1_, ...), custom_call_target="tpu_custom_call" | custom-call | flops 1 | bytes 1 | tf_op jit(solution)/shard_map/post/pallas_call | solution.py:328
  67.8 3.6 %collective-permute-done.14.refs_2_ = bf16[16,2048]{1,0:T(8,128)(2,1)S(1)} collective-permute-done((bf16[16,2048]{1,0:T(8,128)(2,1)S(1)}, bf16[16,2048]{1,0:T(8,128)(2,1)S(1)}, u32[]{:S(2)}, u32[]{:S(2)}) %collective-permute-start.14) | collective-permute-done | bytes 65568 | tf_op jit(solution)/shard_map/ppermute | solution.py:362
  71.4 1.1 %post.3 = bf16[128,4096]{1,0:T(8,128)(2,1)} custom-call(bf16[128,192]{1,0:T(8,128)(2,1)S(1)} %get-tuple-element.36.after_ref.mix_ref, f32[1,4096]{1,0:T(1,128)S(1)} %get-tuple-element.37.row_ref, bf16[16,2048]{1,0:T(8,128)(2,1)S(1)} %get-tuple-element.53.refs_0_, ...), custom_call_target="tpu_custom_call", output_to_operand_aliasing={{}: (6, {})} | custom-call | flops 1 | bytes 1 | tf_op jit(solution)/shard_map/post/pallas_call | solution.py:328
  (38 shorter events, 6.3 us)
Async XLA Ops:
  2.8 10.1 %collective-permute-start.6 = (bf16[16,2048]{1,0:T(8,128)(2,1)S(1)}, bf16[16,2048]{1,0:T(8,128)(2,1)S(1)}, u32[]{:S(2)}, u32[]{:S(2)}) collective-permute-start(bf16[16,2048]{1,0:T(8,128)(2,1)S(1)} %get-tuple-element.41), channel_id=1, source_target_pairs={{0,12},{1,13},{2,14},{3,15},{4,8},{5,9},{6,10},{7,11},{8,4},{9,5},... | collective-permute-start | bytes 196616 | tf_op jit(solution)/shard_map/ppermute | solution.py:362
  7.9 15.1 %collective-permute-start.3 = (bf16[16,4096]{1,0:T(8,128)(2,1)S(1)}, bf16[16,4096]{1,0:T(8,128)(2,1)S(1)}, u32[]{:S(2)}, u32[]{:S(2)}) collective-permute-start(bf16[16,4096]{1,0:T(8,128)(2,1)S(1)} %get-tuple-element.35.after_ref.refs_0_), channel_id=1, source_target_pairs={{0,2},{1,3},{2,0},{3,1},{4,6},{5,7},{6,4},{7,5},{8,10},{9,11},{10,... | collective-permute-start | bytes 393224 | tf_op jit(solution)/shard_map/ppermute | solution.py:362
  9.4 7.8 %collective-permute-start.7 = (bf16[16,2048]{1,0:T(8,128)(2,1)S(1)}, bf16[16,2048]{1,0:T(8,128)(2,1)S(1)}, u32[]{:S(2)}, u32[]{:S(2)}) collective-permute-start(bf16[16,2048]{1,0:T(8,128)(2,1)S(1)} %get-tuple-element.42), channel_id=1, source_target_pairs={{0,8},{1,9},{2,10},{3,11},{4,12},{5,13},{6,14},{7,15},{8,0},{9,1},... | collective-permute-start | bytes 196616 | tf_op jit(solution)/shard_map/ppermute | solution.py:362
  9.4 14.1 %collective-permute-start = (bf16[16,2048]{1,0:T(8,128)(2,1)S(1)}, bf16[16,2048]{1,0:T(8,128)(2,1)S(1)}, u32[]{:S(2)}, u32[]{:S(2)}) collective-permute-start(bf16[16,2048]{1,0:T(8,128)(2,1)S(1)} %get-tuple-element.38), channel_id=1, source_target_pairs={{0,12},{1,13},{2,14},{3,15},{4,8},{5,9},{6,10},{7,11},{8,4},{9,5},... | collective-permute-start | bytes 196616 | tf_op jit(solution)/shard_map/ppermute | solution.py:362
  11.3 11.6 %collective-permute-start.8 = (bf16[16,2048]{1,0:T(8,128)(2,1)S(1)}, bf16[16,2048]{1,0:T(8,128)(2,1)S(1)}, u32[]{:S(2)}, u32[]{:S(2)}) collective-permute-start(bf16[16,2048]{1,0:T(8,128)(2,1)S(1)} %get-tuple-element.43), channel_id=1, source_target_pairs={{0,4},{1,5},{2,6},{3,7},{4,0},{5,1},{6,2},{7,3},{8,12},{9,13},{10,... | collective-permute-start | bytes 196616 | tf_op jit(solution)/shard_map/ppermute | solution.py:362
  12.9 10.6 %collective-permute-start.1 = (bf16[16,2048]{1,0:T(8,128)(2,1)S(1)}, bf16[16,2048]{1,0:T(8,128)(2,1)S(1)}, u32[]{:S(2)}, u32[]{:S(2)}) collective-permute-start(bf16[16,2048]{1,0:T(8,128)(2,1)S(1)} %get-tuple-element.39), channel_id=1, source_target_pairs={{0,8},{1,9},{2,10},{3,11},{4,12},{5,13},{6,14},{7,15},{8,0},{9,1},... | collective-permute-start | bytes 196616 | tf_op jit(solution)/shard_map/ppermute | solution.py:362
  17.2 6.3 %collective-permute-start.2 = (bf16[16,2048]{1,0:T(8,128)(2,1)S(1)}, bf16[16,2048]{1,0:T(8,128)(2,1)S(1)}, u32[]{:S(2)}, u32[]{:S(2)}) collective-permute-start(bf16[16,2048]{1,0:T(8,128)(2,1)S(1)} %get-tuple-element.40), channel_id=1, source_target_pairs={{0,4},{1,5},{2,6},{3,7},{4,0},{5,1},{6,2},{7,3},{8,12},{9,13},{10,... | collective-permute-start | bytes 196616 | tf_op jit(solution)/shard_map/ppermute | solution.py:362
  17.2 0.7 copy-start
  23.0 5.7 %collective-permute-start.9 = (bf16[48,2048]{1,0:T(8,128)(2,1)S(1)}, bf16[48,2048]{1,0:T(8,128)(2,1)S(1)}, u32[]{:S(2)}, u32[]{:S(2)}) collective-permute-start(bf16[48,2048]{1,0:T(8,128)(2,1)S(1)} %join.6.refs_1_), channel_id=1, source_target_pairs={{0,2},{1,3},{2,0},{3,1},{4,6},{5,7},{6,4},{7,5},{8,10},{9,11},{10,... | collective-permute-start | bytes 589832 | tf_op jit(solution)/shard_map/ppermute | solution.py:362
  23.5 7.3 %collective-permute-start.4 = (bf16[48,2048]{1,0:T(8,128)(2,1)S(1)}, bf16[48,2048]{1,0:T(8,128)(2,1)S(1)}, u32[]{:S(2)}, u32[]{:S(2)}) collective-permute-start(bf16[48,2048]{1,0:T(8,128)(2,1)S(1)} %join.4.refs_1_), channel_id=1, source_target_pairs={{0,2},{1,3},{2,0},{3,1},{4,6},{5,7},{6,4},{7,5},{8,10},{9,11},{10,... | collective-permute-start | bytes 589832 | tf_op jit(solution)/shard_map/ppermute | solution.py:362
  28.7 2.2 %collective-permute-start.10 = (bf16[128,2048]{1,0:T(8,128)(2,1)S(1)}, bf16[128,2048]{1,0:T(8,128)(2,1)S(1)}, u32[]{:S(2)}, u32[]{:S(2)}) collective-permute-start(bf16[128,2048]{1,0:T(8,128)(2,1)S(1)} %join.7.refs_0_), channel_id=1, source_target_pairs={{0,1},{1,0},{2,3},{3,2},{4,5},{5,4},{6,7},{7,6},{8,9},{9,8},{10,11... | collective-permute-start | bytes 1572872 | tf_op jit(solution)/shard_map/ppermute | solution.py:362
  30.8 5.6 %collective-permute-start.5 = (bf16[128,2048]{1,0:T(8,128)(2,1)S(1)}, bf16[128,2048]{1,0:T(8,128)(2,1)S(1)}, u32[]{:S(2)}, u32[]{:S(2)}) collective-permute-start(bf16[128,2048]{1,0:T(8,128)(2,1)S(1)} %join.5.refs_0_), channel_id=1, source_target_pairs={{0,1},{1,0},{2,3},{3,2},{4,5},{5,4},{6,7},{7,6},{8,9},{9,8},{10,11... | collective-permute-start | bytes 1572872 | tf_op jit(solution)/shard_map/ppermute | solution.py:362
  43.4 3.5 %collective-permute-start.16 = (bf16[128,2048]{1,0:T(8,128)(2,1)S(1)}, bf16[128,2048]{1,0:T(8,128)(2,1)S(1)}, u32[]{:S(2)}, u32[]{:S(2)}) collective-permute-start(bf16[128,2048]{1,0:T(8,128)(2,1)S(1)} %get-tuple-element.58), channel_id=1, source_target_pairs={{0,1},{1,0},{2,3},{3,2},{4,5},{5,4},{6,7},{7,6},{8,9},{9,8},{10,11... | collective-permute-start | bytes 1572872 | tf_op jit(solution)/shard_map/ppermute | solution.py:362
  46.8 2.0 %collective-permute-start.11 = (bf16[128,2048]{1,0:T(8,128)(2,1)S(1)}, bf16[128,2048]{1,0:T(8,128)(2,1)S(1)}, u32[]{:S(2)}, u32[]{:S(2)}) collective-permute-start(bf16[128,2048]{1,0:T(8,128)(2,1)S(1)} %get-tuple-element.50), channel_id=1, source_target_pairs={{0,1},{1,0},{2,3},{3,2},{4,5},{5,4},{6,7},{7,6},{8,9},{9,8},{10,11... | collective-permute-start | bytes 1572872 | tf_op jit(solution)/shard_map/ppermute | solution.py:362
  47.0 9.2 %collective-permute-start.17 = (bf16[64,2048]{1,0:T(8,128)(2,1)S(1)}, bf16[64,2048]{1,0:T(8,128)(2,1)S(1)}, u32[]{:S(2)}, u32[]{:S(2)}) collective-permute-start(bf16[64,2048]{1,0:T(8,128)(2,1)S(1)} %get-tuple-element.60), channel_id=1, source_target_pairs={{0,2},{1,3},{2,0},{3,1},{4,6},{5,7},{6,4},{7,5},{8,10},{9,11},{10,... | collective-permute-start | bytes 786440 | tf_op jit(solution)/shard_map/ppermute | solution.py:362
  48.9 12.5 %collective-permute-start.12 = (bf16[64,2048]{1,0:T(8,128)(2,1)S(1)}, bf16[64,2048]{1,0:T(8,128)(2,1)S(1)}, u32[]{:S(2)}, u32[]{:S(2)}) collective-permute-start(bf16[64,2048]{1,0:T(8,128)(2,1)S(1)} %get-tuple-element.52), channel_id=1, source_target_pairs={{0,2},{1,3},{2,0},{3,1},{4,6},{5,7},{6,4},{7,5},{8,10},{9,11},{10,... | collective-permute-start | bytes 786440 | tf_op jit(solution)/shard_map/ppermute | solution.py:362
  56.2 9.1 %collective-permute-start.18 = (bf16[16,2048]{1,0:T(8,128)(2,1)S(1)}, bf16[16,2048]{1,0:T(8,128)(2,1)S(1)}, u32[]{:S(2)}, u32[]{:S(2)}) collective-permute-start(bf16[16,2048]{1,0:T(8,128)(2,1)S(1)} %get-tuple-element.62), channel_id=1, source_target_pairs={{0,12},{1,13},{2,14},{3,15},{4,8},{5,9},{6,10},{7,11},{8,4},{9,5},... | collective-permute-start | bytes 196616 | tf_op jit(solution)/shard_map/ppermute | solution.py:362
  59.8 6.5 %collective-permute-start.19 = (bf16[16,2048]{1,0:T(8,128)(2,1)S(1)}, bf16[16,2048]{1,0:T(8,128)(2,1)S(1)}, u32[]{:S(2)}, u32[]{:S(2)}) collective-permute-start(bf16[16,2048]{1,0:T(8,128)(2,1)S(1)} %get-tuple-element.63), channel_id=1, source_target_pairs={{0,8},{1,9},{2,10},{3,11},{4,12},{5,13},{6,14},{7,15},{8,0},{9,1},... | collective-permute-start | bytes 196616 | tf_op jit(solution)/shard_map/ppermute | solution.py:362
  60.1 6.2 %collective-permute-start.20 = (bf16[16,2048]{1,0:T(8,128)(2,1)S(1)}, bf16[16,2048]{1,0:T(8,128)(2,1)S(1)}, u32[]{:S(2)}, u32[]{:S(2)}) collective-permute-start(bf16[16,2048]{1,0:T(8,128)(2,1)S(1)} %get-tuple-element.64), channel_id=1, source_target_pairs={{0,4},{1,5},{2,6},{3,7},{4,0},{5,1},{6,2},{7,3},{8,12},{9,13},{10,... | collective-permute-start | bytes 196616 | tf_op jit(solution)/shard_map/ppermute | solution.py:362
  61.4 6.3 %collective-permute-start.13 = (bf16[16,2048]{1,0:T(8,128)(2,1)S(1)}, bf16[16,2048]{1,0:T(8,128)(2,1)S(1)}, u32[]{:S(2)}, u32[]{:S(2)}) collective-permute-start(bf16[16,2048]{1,0:T(8,128)(2,1)S(1)} %get-tuple-element.54), channel_id=1, source_target_pairs={{0,12},{1,13},{2,14},{3,15},{4,8},{5,9},{6,10},{7,11},{8,4},{9,5},... | collective-permute-start | bytes 196616 | tf_op jit(solution)/shard_map/ppermute | solution.py:362
  65.0 6.4 %collective-permute-start.14 = (bf16[16,2048]{1,0:T(8,128)(2,1)S(1)}, bf16[16,2048]{1,0:T(8,128)(2,1)S(1)}, u32[]{:S(2)}, u32[]{:S(2)}) collective-permute-start(bf16[16,2048]{1,0:T(8,128)(2,1)S(1)} %get-tuple-element.55), channel_id=1, source_target_pairs={{0,8},{1,9},{2,10},{3,11},{4,12},{5,13},{6,14},{7,15},{8,0},{9,1},... | collective-permute-start | bytes 196616 | tf_op jit(solution)/shard_map/ppermute | solution.py:362
  65.3 6.1 %collective-permute-start.15 = (bf16[16,2048]{1,0:T(8,128)(2,1)S(1)}, bf16[16,2048]{1,0:T(8,128)(2,1)S(1)}, u32[]{:S(2)}, u32[]{:S(2)}) collective-permute-start(bf16[16,2048]{1,0:T(8,128)(2,1)S(1)} %get-tuple-element.56), channel_id=1, source_target_pairs={{0,4},{1,5},{2,6},{3,7},{4,0},{5,1},{6,2},{7,3},{8,12},{9,13},{10,... | collective-permute-start | bytes 196616 | tf_op jit(solution)/shard_map/ppermute | solution.py:362

commit v5 on v4

--- a/solution.py
+++ b/solution.py
@@ -8,7 +8,7 @@
 from jax.sharding import PartitionSpec as P
 
 CHUNKS = 2
-PIECES = 8
+PIECES = 16
 MIB = 1024 * 1024
 F32 = jnp.float32
 BF16 = jnp.bfloat16
@@ -193,8 +193,8 @@
 
 def up_kernel(*refs, blocks, first, last, chunk):
     parts = refs[:blocks]
-    w_ref, next_hbm = refs[blocks:blocks + 2]
-    acc_ref = None if first else refs[blocks + 2]
+    w_ref, next_hbm, after_ref = refs[blocks:blocks + 3]
+    acc_ref = None if first else refs[blocks + 3]
     out_ref, next_ref, rows_ref, sems = refs[-4:]
     copies = stream(next_hbm, next_ref, sems, chunk)
     for copy in copies:
@@ -204,7 +204,7 @@
         rows_ref[at:at + part.shape[0], :] = part[...]
         at += part.shape[0]
     hidden = w_ref.shape[0]
-    tile = min(1024, hidden)
+    tile = min(2048, hidden)
 
     for i in range(hidden // tile):
         cut = slice(i * tile, (i + 1) * tile)
@@ -221,15 +221,15 @@
         copy.wait()
 
 
-def up(parts, w, acc, last, following, chunk, chunks):
+def up(parts, w, acc, last, after, following, chunk, chunks):
     hidden, step = w.shape
     rows = sum(p.shape[0] for p in parts)
     first = acc is None
-    args = list(parts) + [w, following] + ([] if first else [acc])
+    args = list(parts) + [w, following, after] + ([] if first else [acc])
     out = jax.ShapeDtypeStruct((rows, hidden), BF16) if last else jax.ShapeDtypeStruct((hidden, rows), F32)
     return pl.pallas_call(
         functools.partial(up_kernel, blocks=len(parts), first=first, last=last, chunk=chunk),
-        in_specs=[VMEM] * len(parts) + [VMEM, HBM] + [VMEM] * (0 if first else 1),
+        in_specs=[VMEM] * len(parts) + [VMEM, HBM, ANY] + [VMEM] * (0 if first else 1),
         out_specs=[VMEM] * 2,
         out_shape=[out, pltpu.VMEM((following.shape[0], following.shape[1] // chunks), BF16)],
         scratch_shapes=[pltpu.VMEM((rows, step), BF16), pltpu.SemaphoreType.DMA((PIECES,))],
@@ -239,7 +239,7 @@
     )(*args)
 
 
-def down_kernel(h_ref, w_ref, *refs, chunk):
+def down_kernel(h_ref, w_ref, after_ref, *refs, chunk):
     if chunk is not None:
         next_hbm, keep_ref, send_ref, next_ref, sems = refs
         copies = stream(next_hbm, next_ref, sems, chunk)
@@ -249,11 +249,9 @@
     for copy in copies:
         copy.start()
     half, step = keep_ref.shape
-    tile = min(512, step)
-
-    @pl.loop(0, step // tile)
-    def _(i):
-        cut = pl.ds(pl.multiple_of(i * tile, tile), tile)
+    tile = min(1024, step)
+    for i in range(step // tile):
+        cut = slice(i * tile, (i + 1) * tile)
         out = jnp.dot(h_ref[...], w_ref[:, cut], preferred_element_type=F32)
         keep_ref[:, cut] = out[:half]
         send_ref[:, cut] = out[half:].astype(BF16)
@@ -262,14 +260,14 @@
         copy.wait()
 
 
-def down(h, w, following, chunk):
+def down(h, w, after, following, chunk):
     rows = h.shape[0]
     step = w.shape[1]
     half = rows // 2
     more = chunk is not None
     return pl.pallas_call(
         functools.partial(down_kernel, chunk=chunk),
-        in_specs=[VMEM] * 2 + [HBM] * more,
+        in_specs=[VMEM] * 2 + [ANY] + [HBM] * more,
         out_specs=[VMEM] * (2 + more),
         out_shape=[
             jax.ShapeDtypeStruct((half, step), F32),
@@ -280,53 +278,64 @@
         compiler_params=params(8),
         cost_estimate=FREE,
         name="down",
-    )(*([h, w] + [following] * more))
-
-
-def add_kernel(keep_ref, got_ref, *outs):
-    at = 0
-    for out in outs:
-        cut = slice(at, at + out.shape[0])
-        out[...] = (keep_ref[cut] + got_ref[cut].astype(F32)).astype(out.dtype)
-        at += out.shape[0]
-
-
-def add(keep, got, heights, kinds):
+    )(*([h, w, after] + [following] * more))
+
+
+def add_kernel(keep_ref, got_ref, *refs, cuts):
+    width = keep_ref.shape[1]
+    for ref, (low, high) in zip(refs[-len(cuts):], cuts):
+        start = ref.shape[1] - width
+        if start:
+            ref[:, :start] = refs[0][...]
+        total = keep_ref[low:high] + got_ref[low:high].astype(F32)
+        ref[:, start:] = total.astype(ref.dtype)
+
+
+def add(keep, got, cuts, kinds, before=None):
     width = keep.shape[1]
-    return pl.pallas_call(
-        add_kernel,
-        in_specs=[VMEM] * 2,
-        out_specs=[VMEM] * len(heights),
-        out_shape=[jax.ShapeDtypeStruct((h, width), k) for h, k in zip(heights, kinds)],
+    shapes = [[high - low, width] for low, high in cuts]
+    args = [keep, got]
+    if before is not None:
+        shapes[-1][1] += before.shape[1]
+        args.append(before)
+    return pl.pallas_call(
+        functools.partial(add_kernel, cuts=cuts),
+        in_specs=[VMEM] * len(args),
+        out_specs=[VMEM] * len(cuts),
+        out_shape=[jax.ShapeDtypeStruct(shape, k) for shape, k in zip(shapes, kinds)],
         compiler_params=params(12),
         cost_estimate=FREE,
         name="add",
-    )(keep, got)
-
-
-def post_kernel(mix_ref, row_ref, *refs, experts):
+    )(*args)
+
+
+def post_kernel(mix_ref, row_ref, keep_ref, near_ref, *refs, experts):
     out_ref = refs[-1]
-    values = jnp.concatenate([ref[...] for ref in refs[:experts]] * 3, axis=0)
+    own = (keep_ref[...] + near_ref[...].astype(F32)).astype(BF16)
+    values = jnp.concatenate([own] + [ref[...] for ref in refs[:experts - 1]], axis=0)
+    values = jnp.concatenate([values] * 3, axis=0)
     mixed = jnp.dot(mix_ref[...], values, preferred_element_type=F32)
     out_ref[...] = (row_ref[...] * mixed).astype(BF16)
 
 
-def post(mix, row, parts, out, chunk, chunks):
+def post(mix, row, keep, own, parts, out, chunk, chunks):
     tok_rows = mix.shape[0]
     width = row.shape[1]
     step = width // chunks
     in_specs = [
         pl.BlockSpec(mix.shape, lambda i: (0, 0)),
         pl.BlockSpec((1, step), lambda i: (0, chunk)),
+        pl.BlockSpec((own.shape[0], step), lambda i: (0, 0)),
+        pl.BlockSpec((own.shape[0], step), lambda i: (0, chunk)),
     ] + [pl.BlockSpec(p.shape, lambda i: (0, 0)) for p in parts]
-    args = [mix, row] + list(parts)
+    args = [mix, row, keep, own] + list(parts)
     aliases = {}
     if out is not None:
         aliases = {len(args): 0}
         in_specs.append(ANY)
         args.append(out)
     return pl.pallas_call(
-        functools.partial(post_kernel, experts=len(parts)),
+        functools.partial(post_kernel, experts=len(parts) + 1),
         grid=(1,),
         in_specs=in_specs,
         out_specs=pl.BlockSpec((tok_rows, step), lambda i: (0, chunk)),
@@ -371,34 +380,55 @@
         got.append([swap(flat[c * (experts - 1) + i], mask) for i, mask in enumerate(far)])
     own_near = swap(own, near[0])
 
-    mix, row = mixer(info, count, pick, comb, gate, own, tok_rows)
-    w = load(w_up, mix, 0, chunks)
+    blocks = []
+    w = None
+    for c in range(chunks):
+        blocks.append(join(got[c], [own_near] if c == 0 else [w]))
+        if c == 0:
+            w = load(w_up, blocks[0], 0, chunks)
     acc = None
+    mix = None
     for c in range(chunks):
         cut = (c * step, (c + 1) * step)
-        block = join(got[c], [own_near, w] if c == 0 else [])
-        parts = [(own, cut), block, (own_near, cut), swap(block, near[0])]
+        parts = [(own, cut), blocks[c], (own_near, cut), swap(blocks[c], near[0])]
         for mask in near[1:]:
-            block = join(parts, [])
+            block = join(parts, [] if c == 0 else [acc])
             parts = [block, swap(block, mask)]
+        if c == 0:
+            mix, row = mixer(info, count, pick, comb, gate, parts[0], tok_rows)
         last = c == chunks - 1
-        acc, w = up(parts, w, acc, last, w_down if last else w_up, 0 if last else c + 1, chunks)
-
-    out = None
+        acc, w = up(parts, w, acc, last, mix, w_down if last else w_up, 0 if last else c + 1, chunks)
+
+    halves = []
+    after = mix
+    before = None
     for c in range(chunks):
         if c < chunks - 1:
-            keep, send, w = down(acc, w, w_down, c + 1)
+            keep, send, w = down(acc, w, after, w_down, c + 1)
         else:
-            keep, send = down(acc, w, None, None)
-        for at, mask in enumerate(reversed(near)):
+            keep, send = down(acc, w, after, None, None)
+        for mask in reversed(near[1:]):
             arrived = swap(send, mask)
-            height = keep.shape[0]
-            if at < len(near) - 1:
-                keep, send = add(keep, arrived, [height // 2] * 2, [F32, BF16])
+            height = keep.shape[0] // 2
+            if height > experts * slots:
+                keep, send = add(keep, arrived, [(0, height), (height, 2 * height)], [F32, BF16])
             else:
-                parts = add(keep, arrived, [slots] * experts, [BF16] * experts)
-        parts = [parts[0]] + [swap(part, mask) for part, mask in zip(parts[1:], far)]
-        out = post(mix, row, parts, out, c, chunks)
+                keep, send, before = add(
+                    keep,
+                    arrived,
+                    [(0, height), (height + slots, 2 * height), (height, height + slots)],
+                    [F32, BF16, BF16],
+                    before,
+                )
+        halves.append((keep, send))
+    own_near = swap(before, near[0])
+    out = None
+    for c, (keep, send) in enumerate(halves):
+        arrived = swap(send, near[0])
+        cuts = [(i * slots, (i + 1) * slots) for i in range(experts - 1)]
+        parts = add(keep[slots:], arrived, cuts, [BF16] * (experts - 1))
+        parts = [swap(part, mask) for part, mask in zip(parts, far)]
+        out = post(mix, row, keep, own_near, parts, out, c, chunks)
     return out
 
 

time: 72.7 us -> 78.3 us (1.077)
  Pallas kernels: 25.5 us -> 29.2 us
  waiting for transfers between devices: 20.7 us -> 22.1 us
  starting transfers between devices: 25.4 us -> 26.5 us
    pallas_call x2, Pallas kernels: 8.96 us -> 11.4 us  [up(): pl.pallas_call(functools.partial(up_kernel, blocks=len(parts), first=firs...]
    ppermute x21 -> x22, waiting for transfers between devices: 20.7 us -> 22.1 us  [swap(): return lax.ppermute(x, 'expert', [(i, i ^ mask) for i in range(devices)])]
    pallas_call x2, Pallas kernels: 6.34 us -> 7.59 us  [down(): pl.pallas_call(functools.partial(down_kernel, chunk=chunk), in_specs=[VME...]
    ppermute x21 -> x22, starting transfers between devices: 25.4 us -> 26.5 us  [swap(): return lax.ppermute(x, 'expert', [(i, i ^ mask) for i in range(devices)])]
  transfers between devices with their start and end apart: 21 -> 22, of which waited for: 9 -> 10; matrix products, arithmetic and copies ran while one was open for 0% -> 0% of each run, Pallas kernels for 20% -> 18%
where the time goes in v5:
time: 78.3 us; the launch traced here: 78.1 us
  Pallas kernels  29.2 us (37%)
  starting transfers between devices  26.5 us (34%)
  waiting for transfers between devices  22.1 us (28%)
    ppermute x22, starting transfers between devices, swap(): return lax.ppermute(x, 'expert', [(i, i ^ mask) for i in range(devices)])  26.5 us
    ppermute x22, waiting for transfers between devices, swap(): return lax.ppermute(x, 'expert', [(i, i ^ mask) for i in range(devices)])  22.1 us
    pallas_call x2, Pallas kernels, up(): pl.pallas_call(functools.partial(up_kernel, blocks=len(parts), first=firs...  11.4 us
    pallas_call x2, Pallas kernels, down(): pl.pallas_call(functools.partial(down_kernel, chunk=chunk), in_specs=[VME...  7.59 us
    pallas_call x1, Pallas kernels, load(): pl.pallas_call(functools.partial(load_kernel, chunk=chunk), in_specs=[HBM...  3.51 us
    pallas_call x1, Pallas kernels, pre(): pl.pallas_call(functools.partial(pre_kernel, chunks=chunks), in_specs=[SM...  2.67 us
    pallas_call x2, Pallas kernels, post(): pl.pallas_call(functools.partial(post_kernel, experts=len(parts) + 1), gr...  2.19 us
  transfers between devices with their start and end apart: 22, of which 10 were waited for; matrix products, arithmetic and copies ran while one was open for 0% of the time, Pallas kernels for 18%

profile of v5, /device:TPU:0, one launch (start us, length us, event | category | flops | bytes accessed | tf_op | source)
XLA Modules:
  0.0 78.1 jit_solution(3808436847348939875)
XLA Ops:
  0.1 2.7 %pre.1 = (bf16[16,2048]{1,0:T(8,128)(2,1)S(1)}, bf16[16,2048]{1,0:T(8,128)(2,1)S(1)}, bf16[16,2048]{1,0:T(8,128)(2,1)S(1)}, bf16[16,2048]{1,0:T(8,128)(2,1)S(1)}...) custom-call(s32[2]{0:T(128)S(1)} %pad_add_fusion.info_ref, ...), custom_call_target="tpu_custom_call" | custom-call | flops 1 | bytes 1 | tf_op jit(solution)/shard_map/pre/pallas_call | solution.py:75
  2.8 3.0 %collective-permute-start.3 = (bf16[16,4096]{1,0:T(8,128)(2,1)S(1)}, bf16[16,4096]{1,0:T(8,128)(2,1)S(1)}, u32[]{:S(2)}, u32[]{:S(2)}) collective-permute-start(bf16[16,4096]{1,0:T(8,128)(2,1)S(1)} %get-tuple-element.35.refs_0_), channel_id=1, source_target_pairs={{0,2},{1,3},{2,0},{3,1},{4,6},{5,7},{6,4},{7,5},{8,10},{9,11},{10,... | collective-permute-start | bytes 393224 | tf_op jit(solution)/shard_map/ppermute | solution.py:371
  5.8 3.6 %collective-permute-start = (bf16[16,2048]{1,0:T(8,128)(2,1)S(1)}, bf16[16,2048]{1,0:T(8,128)(2,1)S(1)}, u32[]{:S(2)}, u32[]{:S(2)}) collective-permute-start(bf16[16,2048]{1,0:T(8,128)(2,1)S(1)} %get-tuple-element.36), channel_id=1, source_target_pairs={{0,12},{1,13},{2,14},{3,15},{4,8},{5,9},{6,10},{7,11},{8,4},{9,5},... | collective-permute-start | bytes 196616 | tf_op jit(solution)/shard_map/ppermute | solution.py:371
  10.2 2.5 %collective-permute-done.refs_0_ = bf16[16,2048]{1,0:T(8,128)(2,1)S(1)} collective-permute-done((bf16[16,2048]{1,0:T(8,128)(2,1)S(1)}, bf16[16,2048]{1,0:T(8,128)(2,1)S(1)}, u32[]{:S(2)}, u32[]{:S(2)}) %collective-permute-start) | collective-permute-done | bytes 65568 | tf_op jit(solution)/shard_map/ppermute | solution.py:371
  12.6 2.1 %collective-permute-done.1.refs_1_ = bf16[16,2048]{1,0:T(8,128)(2,1)S(1)} collective-permute-done((bf16[16,2048]{1,0:T(8,128)(2,1)S(1)}, bf16[16,2048]{1,0:T(8,128)(2,1)S(1)}, u32[]{:S(2)}, u32[]{:S(2)}) %collective-permute-start.1) | collective-permute-done | bytes 65568 | tf_op jit(solution)/shard_map/ppermute | solution.py:371
  15.3 5.8 %collective-permute-done.4.refs_3_ = bf16[48,2048]{1,0:T(8,128)(2,1)S(1)} collective-permute-done((bf16[48,2048]{1,0:T(8,128)(2,1)S(1)}, bf16[48,2048]{1,0:T(8,128)(2,1)S(1)}, u32[]{:S(2)}, u32[]{:S(2)}) %collective-permute-start.4) | collective-permute-done | bytes 196640 | tf_op jit(solution)/shard_map/ppermute | solution.py:371
  21.2 2.1 %collective-permute-start.5 = (bf16[16,2048]{1,0:T(8,128)(2,1)S(1)}, bf16[16,2048]{1,0:T(8,128)(2,1)S(1)}, u32[]{:S(2)}, u32[]{:S(2)}) collective-permute-start(bf16[16,2048]{1,0:T(8,128)(2,1)S(1)} %get-tuple-element.41), channel_id=1, source_target_pairs={{0,12},{1,13},{2,14},{3,15},{4,8},{5,9},{6,10},{7,11},{8,4},{9,5},... | collective-permute-start | bytes 196616 | tf_op jit(solution)/shard_map/ppermute | solution.py:371
  23.3 2.4 %collective-permute-start.7 = (bf16[16,2048]{1,0:T(8,128)(2,1)S(1)}, bf16[16,2048]{1,0:T(8,128)(2,1)S(1)}, u32[]{:S(2)}, u32[]{:S(2)}) collective-permute-start(bf16[16,2048]{1,0:T(8,128)(2,1)S(1)} %get-tuple-element.43), channel_id=1, source_target_pairs={{0,4},{1,5},{2,6},{3,7},{4,0},{5,1},{6,2},{7,3},{8,12},{9,13},{10,... | collective-permute-start | bytes 196616 | tf_op jit(solution)/shard_map/ppermute | solution.py:371
  25.7 3.5 %load.1.refs_3_.refs_2_ = bf16[2048,2048]{1,0:T(8,128)(2,1)S(1)} custom-call(bf16[2048,4096]{1,0:T(8,128)(2,1)} %refs_3_.2, bf16[48,2048]{1,0:T(8,128)(2,1)S(1)} %join.4.refs_1_.after_ref), custom_call_target="tpu_custom_call" | custom-call | flops 1 | bytes 1 | tf_op jit(solution)/shard_map/load/pallas_call | solution.py:182
  30.9 1.5 %mixer.1 = (bf16[128,192]{1,0:T(8,128)(2,1)S(1)}, f32[1,4096]{1,0:T(1,128)S(1)}) custom-call(s32[2]{0:T(128)S(1)} %pad_add_fusion.info_ref, s32[1,4]{1,0:T(1,128)S(1)} %copy-done, s32[4,16]{1,0:T(4,128)} %bitcast.5, f32[4,16]{1,0:T(4,128)} %bitcast.6, f32[2,4096]{1,0:T(2,128)} %gate_hbm.1, bf16[128,2048]{1,0:T(8,128)(2,1)S(1)} %join.5.after_ref.refs_0_), custom_call_target="tpu_custom_call" | custom-call | flops 1 | bytes 1 | tf_op jit(solution)/shard_map/mixer/pallas_call | solution.py:114
  32.5 5.3 %up.2 = (f32[2048,256]{1,0:T(8,128)S(1)}, bf16[2048,2048]{1,0:T(8,128)(2,1)S(1)}) custom-call(bf16[128,2048]{1,0:T(8,128)(2,1)S(1)} %join.5.after_ref.refs_0_, bf16[128,2048]{1,0:T(8,128)(2,1)S(1)} %collective-permute-done.9.refs_1_, bf16[2048,2048]{1,0:T(8,128)(2,1)S(1)} %load.1.refs_3_.refs_2_, bf16[2048,4096]{1,0:T(8,128)(2,1)} %refs_3_.2, ...), custom_call_target="tpu_custom_call" | custom-call | flops 1 | bytes 1 | tf_op jit(solution)/shard_map/up/pallas_call | solution.py:230
  37.9 1.9 %collective-permute-done.10.refs_1_ = bf16[128,2048]{1,0:T(8,128)(2,1)S(1)} collective-permute-done((bf16[128,2048]{1,0:T(8,128)(2,1)S(1)}, bf16[128,2048]{1,0:T(8,128)(2,1)S(1)}, u32[]{:S(2)}, u32[]{:S(2)}) %collective-permute-start.10) | collective-permute-done | bytes 524320 | tf_op jit(solution)/shard_map/ppermute | solution.py:371
  39.8 6.1 %up.3 = (bf16[256,2048]{1,0:T(8,128)(2,1)S(1)}, bf16[2048,2048]{1,0:T(8,128)(2,1)S(1)}) custom-call(bf16[128,2048]{1,0:T(8,128)(2,1)S(1)} %join.7.refs_0_, bf16[128,2048]{1,0:T(8,128)(2,1)S(1)} %collective-permute-done.10.refs_1_, bf16[2048,2048]{1,0:T(8,128)(2,1)S(1)} %get-tuple-element.45.refs_2_, bf16[2048,4096]{1,0:T(8,128)(2,1)} %refs_0_.1, ...), custom_call_target="tpu_custom_call" | custom-call | flops 1 | bytes 1 | tf_op jit(solution)/shard_map/up/pallas_call | solution.py:230
  45.9 5.3 %down.2 = (f32[128,2048]{1,0:T(8,128)S(1)}, bf16[128,2048]{1,0:T(8,128)(2,1)S(1)}, bf16[2048,2048]{1,0:T(8,128)(2,1)S(1)}) custom-call(bf16[256,2048]{1,0:T(8,128)(2,1)S(1)} %get-tuple-element.46.h_ref, bf16[2048,2048]{1,0:T(8,128)(2,1)S(1)} %get-tuple-element.47.w_ref, bf16[128,192]{1,0:T(8,128)(2,1)S(1)} %get-tuple-element.39.refs_4_.after_ref.mix_ref, ...), custom_call_target="tpu_custom_call" | custom-call | flops 1 | bytes 1 | tf_op jit(solution)/shard_map/down/pallas_call | solution.py:268
  51.4 2.3 %down.3 = (f32[128,2048]{1,0:T(8,128)S(1)}, bf16[128,2048]{1,0:T(8,128)(2,1)S(1)}) custom-call(bf16[256,2048]{1,0:T(8,128)(2,1)S(1)} %get-tuple-element.46.h_ref, bf16[2048,2048]{1,0:T(8,128)(2,1)S(1)} %get-tuple-element.48.w_ref, bf16[128,192]{1,0:T(8,128)(2,1)S(1)} %get-tuple-element.39.refs_4_.after_ref.mix_ref), custom_call_target="tpu_custom_call" | custom-call | flops 1 | bytes 1 | tf_op jit(solution)/shard_map/down/pallas_call | solution.py:268
  54.2 1.6 %collective-permute-start.18 = (bf16[48,2048]{1,0:T(8,128)(2,1)S(1)}, bf16[48,2048]{1,0:T(8,128)(2,1)S(1)}, u32[]{:S(2)}, u32[]{:S(2)}) collective-permute-start(bf16[48,2048]{1,0:T(8,128)(2,1)S(1)} %get-tuple-element.61), channel_id=1, source_target_pairs={{0,2},{1,3},{2,0},{3,1},{4,6},{5,7},{6,4},{7,5},{8,10},{9,11},{10,... | collective-permute-start | bytes 589832 | tf_op jit(solution)/shard_map/ppermute | solution.py:371
  55.9 1.5 %collective-permute-start.14 = (bf16[48,2048]{1,0:T(8,128)(2,1)S(1)}, bf16[48,2048]{1,0:T(8,128)(2,1)S(1)}, u32[]{:S(2)}, u32[]{:S(2)}) collective-permute-start(bf16[48,2048]{1,0:T(8,128)(2,1)S(1)} %get-tuple-element.56), channel_id=1, source_target_pairs={{0,2},{1,3},{2,0},{3,1},{4,6},{5,7},{6,4},{7,5},{8,10},{9,11},{10,... | collective-permute-start | bytes 589832 | tf_op jit(solution)/shard_map/ppermute | solution.py:371
  58.0 4.0 %collective-permute-done.18.got_ref = bf16[48,2048]{1,0:T(8,128)(2,1)S(1)} collective-permute-done((bf16[48,2048]{1,0:T(8,128)(2,1)S(1)}, bf16[48,2048]{1,0:T(8,128)(2,1)S(1)}, u32[]{:S(2)}, u32[]{:S(2)}) %collective-permute-start.18) | collective-permute-done | bytes 196640 | tf_op jit(solution)/shard_map/ppermute | solution.py:371
  62.1 2.1 %collective-permute-start.19 = (bf16[16,2048]{1,0:T(8,128)(2,1)S(1)}, bf16[16,2048]{1,0:T(8,128)(2,1)S(1)}, u32[]{:S(2)}, u32[]{:S(2)}) collective-permute-start(bf16[16,2048]{1,0:T(8,128)(2,1)S(1)} %get-tuple-element.62), channel_id=1, source_target_pairs={{0,12},{1,13},{2,14},{3,15},{4,8},{5,9},{6,10},{7,11},{8,4},{9,5},... | collective-permute-start | bytes 196616 | tf_op jit(solution)/shard_map/ppermute | solution.py:371
  64.2 2.1 %collective-permute-done.14.got_ref = bf16[48,2048]{1,0:T(8,128)(2,1)S(1)} collective-permute-done((bf16[48,2048]{1,0:T(8,128)(2,1)S(1)}, bf16[48,2048]{1,0:T(8,128)(2,1)S(1)}, u32[]{:S(2)}, u32[]{:S(2)}) %collective-permute-start.14) | collective-permute-done | bytes 196640 | tf_op jit(solution)/shard_map/ppermute | solution.py:371
  66.3 2.1 %collective-permute-start.15 = (bf16[16,2048]{1,0:T(8,128)(2,1)S(1)}, bf16[16,2048]{1,0:T(8,128)(2,1)S(1)}, u32[]{:S(2)}, u32[]{:S(2)}) collective-permute-start(bf16[16,2048]{1,0:T(8,128)(2,1)S(1)} %get-tuple-element.57), channel_id=1, source_target_pairs={{0,12},{1,13},{2,14},{3,15},{4,8},{5,9},{6,10},{7,11},{8,4},{9,5},... | collective-permute-start | bytes 196616 | tf_op jit(solution)/shard_map/ppermute | solution.py:371
  68.4 2.4 %collective-permute-start.21 = (bf16[16,2048]{1,0:T(8,128)(2,1)S(1)}, bf16[16,2048]{1,0:T(8,128)(2,1)S(1)}, u32[]{:S(2)}, u32[]{:S(2)}) collective-permute-start(bf16[16,2048]{1,0:T(8,128)(2,1)S(1)} %get-tuple-element.64), channel_id=1, source_target_pairs={{0,4},{1,5},{2,6},{3,7},{4,0},{5,1},{6,2},{7,3},{8,12},{9,13},{10,... | collective-permute-start | bytes 196616 | tf_op jit(solution)/shard_map/ppermute | solution.py:371
  71.3 2.0 %collective-permute-start.17 = (bf16[16,2048]{1,0:T(8,128)(2,1)S(1)}, bf16[16,2048]{1,0:T(8,128)(2,1)S(1)}, u32[]{:S(2)}, u32[]{:S(2)}) collective-permute-start(bf16[16,2048]{1,0:T(8,128)(2,1)S(1)} %get-tuple-element.59), channel_id=1, source_target_pairs={{0,4},{1,5},{2,6},{3,7},{4,0},{5,1},{6,2},{7,3},{8,12},{9,13},{10,... | collective-permute-start | bytes 196616 | tf_op jit(solution)/shard_map/ppermute | solution.py:371
  73.3 2.3 %collective-permute-done.20.refs_1_ = bf16[16,2048]{1,0:T(8,128)(2,1)S(1)} collective-permute-done((bf16[16,2048]{1,0:T(8,128)(2,1)S(1)}, bf16[16,2048]{1,0:T(8,128)(2,1)S(1)}, u32[]{:S(2)}, u32[]{:S(2)}) %collective-permute-start.20) | collective-permute-done | bytes 65568 | tf_op jit(solution)/shard_map/ppermute | solution.py:371
  (42 shorter events, 8.0 us)
Async XLA Ops:
  2.8 12.1 %collective-permute-start.3 = (bf16[16,4096]{1,0:T(8,128)(2,1)S(1)}, bf16[16,4096]{1,0:T(8,128)(2,1)S(1)}, u32[]{:S(2)}, u32[]{:S(2)}) collective-permute-start(bf16[16,4096]{1,0:T(8,128)(2,1)S(1)} %get-tuple-element.35.refs_0_), channel_id=1, source_target_pairs={{0,2},{1,3},{2,0},{3,1},{4,6},{5,7},{6,4},{7,5},{8,10},{9,11},{10,... | collective-permute-start | bytes 393224 | tf_op jit(solution)/shard_map/ppermute | solution.py:371
  5.8 6.9 %collective-permute-start = (bf16[16,2048]{1,0:T(8,128)(2,1)S(1)}, bf16[16,2048]{1,0:T(8,128)(2,1)S(1)}, u32[]{:S(2)}, u32[]{:S(2)}) collective-permute-start(bf16[16,2048]{1,0:T(8,128)(2,1)S(1)} %get-tuple-element.36), channel_id=1, source_target_pairs={{0,12},{1,13},{2,14},{3,15},{4,8},{5,9},{6,10},{7,11},{8,4},{9,5},... | collective-permute-start | bytes 196616 | tf_op jit(solution)/shard_map/ppermute | solution.py:371
  9.4 5.4 %collective-permute-start.1 = (bf16[16,2048]{1,0:T(8,128)(2,1)S(1)}, bf16[16,2048]{1,0:T(8,128)(2,1)S(1)}, u32[]{:S(2)}, u32[]{:S(2)}) collective-permute-start(bf16[16,2048]{1,0:T(8,128)(2,1)S(1)} %get-tuple-element.37), channel_id=1, source_target_pairs={{0,8},{1,9},{2,10},{3,11},{4,12},{5,13},{6,14},{7,15},{8,0},{9,1},... | collective-permute-start | bytes 196616 | tf_op jit(solution)/shard_map/ppermute | solution.py:371
  9.4 5.4 %collective-permute-start.2 = (bf16[16,2048]{1,0:T(8,128)(2,1)S(1)}, bf16[16,2048]{1,0:T(8,128)(2,1)S(1)}, u32[]{:S(2)}, u32[]{:S(2)}) collective-permute-start(bf16[16,2048]{1,0:T(8,128)(2,1)S(1)} %get-tuple-element.38), channel_id=1, source_target_pairs={{0,4},{1,5},{2,6},{3,7},{4,0},{5,1},{6,2},{7,3},{8,12},{9,13},{10,... | collective-permute-start | bytes 196616 | tf_op jit(solution)/shard_map/ppermute | solution.py:371
  14.8 6.3 %collective-permute-start.4 = (bf16[48,2048]{1,0:T(8,128)(2,1)S(1)}, bf16[48,2048]{1,0:T(8,128)(2,1)S(1)}, u32[]{:S(2)}, u32[]{:S(2)}) collective-permute-start(bf16[48,2048]{1,0:T(8,128)(2,1)S(1)} %join.4.refs_1_.after_ref), channel_id=1, source_target_pairs={{0,2},{1,3},{2,0},{3,1},{4,6},{5,7},{6,4},{7,5},{8,10},{9,11},{10,... | collective-permute-start | bytes 589832 | tf_op jit(solution)/shard_map/ppermute | solution.py:371
  21.1 11.3 %collective-permute-start.9 = (bf16[128,2048]{1,0:T(8,128)(2,1)S(1)}, bf16[128,2048]{1,0:T(8,128)(2,1)S(1)}, u32[]{:S(2)}, u32[]{:S(2)}) collective-permute-start(bf16[128,2048]{1,0:T(8,128)(2,1)S(1)} %join.5.after_ref.refs_0_), channel_id=1, source_target_pairs={{0,1},{1,0},{2,3},{3,2},{4,5},{5,4},{6,7},{7,6},{8,9},{9,8},{10,11... | collective-permute-start | bytes 1572872 | tf_op jit(solution)/shard_map/ppermute | solution.py:371
  21.2 8.0 %collective-permute-start.5 = (bf16[16,2048]{1,0:T(8,128)(2,1)S(1)}, bf16[16,2048]{1,0:T(8,128)(2,1)S(1)}, u32[]{:S(2)}, u32[]{:S(2)}) collective-permute-start(bf16[16,2048]{1,0:T(8,128)(2,1)S(1)} %get-tuple-element.41), channel_id=1, source_target_pairs={{0,12},{1,13},{2,14},{3,15},{4,8},{5,9},{6,10},{7,11},{8,4},{9,5},... | collective-permute-start | bytes 196616 | tf_op jit(solution)/shard_map/ppermute | solution.py:371
  23.3 7.0 %collective-permute-start.6 = (bf16[16,2048]{1,0:T(8,128)(2,1)S(1)}, bf16[16,2048]{1,0:T(8,128)(2,1)S(1)}, u32[]{:S(2)}, u32[]{:S(2)}) collective-permute-start(bf16[16,2048]{1,0:T(8,128)(2,1)S(1)} %get-tuple-element.42), channel_id=1, source_target_pairs={{0,8},{1,9},{2,10},{3,11},{4,12},{5,13},{6,14},{7,15},{8,0},{9,1},... | collective-permute-start | bytes 196616 | tf_op jit(solution)/shard_map/ppermute | solution.py:371
  23.3 7.0 %collective-permute-start.7 = (bf16[16,2048]{1,0:T(8,128)(2,1)S(1)}, bf16[16,2048]{1,0:T(8,128)(2,1)S(1)}, u32[]{:S(2)}, u32[]{:S(2)}) collective-permute-start(bf16[16,2048]{1,0:T(8,128)(2,1)S(1)} %get-tuple-element.43), channel_id=1, source_target_pairs={{0,4},{1,5},{2,6},{3,7},{4,0},{5,1},{6,2},{7,3},{8,12},{9,13},{10,... | collective-permute-start | bytes 196616 | tf_op jit(solution)/shard_map/ppermute | solution.py:371
  29.2 1.7 %copy-start = (s32[1,4]{1,0:T(1,128)S(1)}, s32[1,4]{1,0:T(1,128)}, u32[]{:S(2)}) copy-start(s32[1,4]{1,0:T(1,128)} %count_ref.1) | copy-start | bytes 52
  30.4 7.4 %collective-permute-start.8 = (bf16[48,2048]{1,0:T(8,128)(2,1)S(1)}, bf16[48,2048]{1,0:T(8,128)(2,1)S(1)}, u32[]{:S(2)}, u32[]{:S(2)}) collective-permute-start(bf16[48,2048]{1,0:T(8,128)(2,1)S(1)} %join.6.refs_1_), channel_id=1, source_target_pairs={{0,2},{1,3},{2,0},{3,1},{4,6},{5,7},{6,4},{7,5},{8,10},{9,11},{10,... | collective-permute-start | bytes 589832 | tf_op jit(solution)/shard_map/ppermute | solution.py:371
  37.8 2.0 %collective-permute-start.10 = (bf16[128,2048]{1,0:T(8,128)(2,1)S(1)}, bf16[128,2048]{1,0:T(8,128)(2,1)S(1)}, u32[]{:S(2)}, u32[]{:S(2)}) collective-permute-start(bf16[128,2048]{1,0:T(8,128)(2,1)S(1)} %join.7.refs_0_), channel_id=1, source_target_pairs={{0,1},{1,0},{2,3},{3,2},{4,5},{5,4},{6,7},{7,6},{8,9},{9,8},{10,11... | collective-permute-start | bytes 1572872 | tf_op jit(solution)/shard_map/ppermute | solution.py:371
  51.2 3.0 %collective-permute-start.12 = (bf16[128,2048]{1,0:T(8,128)(2,1)S(1)}, bf16[128,2048]{1,0:T(8,128)(2,1)S(1)}, u32[]{:S(2)}, u32[]{:S(2)}) collective-permute-start(bf16[128,2048]{1,0:T(8,128)(2,1)S(1)} %get-tuple-element.52), channel_id=1, source_target_pairs={{0,1},{1,0},{2,3},{3,2},{4,5},{5,4},{6,7},{7,6},{8,9},{9,8},{10,11... | collective-permute-start | bytes 1572872 | tf_op jit(solution)/shard_map/ppermute | solution.py:371
  53.7 2.1 %collective-permute-start.11 = (bf16[128,2048]{1,0:T(8,128)(2,1)S(1)}, bf16[128,2048]{1,0:T(8,128)(2,1)S(1)}, u32[]{:S(2)}, u32[]{:S(2)}) collective-permute-start(bf16[128,2048]{1,0:T(8,128)(2,1)S(1)} %get-tuple-element.50), channel_id=1, source_target_pairs={{0,1},{1,0},{2,3},{3,2},{4,5},{5,4},{6,7},{7,6},{8,9},{9,8},{10,11... | collective-permute-start | bytes 1572872 | tf_op jit(solution)/shard_map/ppermute | solution.py:371
  54.2 7.8 %collective-permute-start.18 = (bf16[48,2048]{1,0:T(8,128)(2,1)S(1)}, bf16[48,2048]{1,0:T(8,128)(2,1)S(1)}, u32[]{:S(2)}, u32[]{:S(2)}) collective-permute-start(bf16[48,2048]{1,0:T(8,128)(2,1)S(1)} %get-tuple-element.61), channel_id=1, source_target_pairs={{0,2},{1,3},{2,0},{3,1},{4,6},{5,7},{6,4},{7,5},{8,10},{9,11},{10,... | collective-permute-start | bytes 589832 | tf_op jit(solution)/shard_map/ppermute | solution.py:371
  55.9 10.3 %collective-permute-start.14 = (bf16[48,2048]{1,0:T(8,128)(2,1)S(1)}, bf16[48,2048]{1,0:T(8,128)(2,1)S(1)}, u32[]{:S(2)}, u32[]{:S(2)}) collective-permute-start(bf16[48,2048]{1,0:T(8,128)(2,1)S(1)} %get-tuple-element.56), channel_id=1, source_target_pairs={{0,2},{1,3},{2,0},{3,1},{4,6},{5,7},{6,4},{7,5},{8,10},{9,11},{10,... | collective-permute-start | bytes 589832 | tf_op jit(solution)/shard_map/ppermute | solution.py:371
  57.4 13.4 %collective-permute-start.13 = (bf16[16,4096]{1,0:T(8,128)(2,1)S(1)}, bf16[16,4096]{1,0:T(8,128)(2,1)S(1)}, u32[]{:S(2)}, u32[]{:S(2)}) collective-permute-start(bf16[16,4096]{1,0:T(8,128)(2,1)S(1)} %get-tuple-element.55), channel_id=1, source_target_pairs={{0,2},{1,3},{2,0},{3,1},{4,6},{5,7},{6,4},{7,5},{8,10},{9,11},{10,... | collective-permute-start | bytes 393224 | tf_op jit(solution)/shard_map/ppermute | solution.py:371
  62.1 9.2 %collective-permute-start.19 = (bf16[16,2048]{1,0:T(8,128)(2,1)S(1)}, bf16[16,2048]{1,0:T(8,128)(2,1)S(1)}, u32[]{:S(2)}, u32[]{:S(2)}) collective-permute-start(bf16[16,2048]{1,0:T(8,128)(2,1)S(1)} %get-tuple-element.62), channel_id=1, source_target_pairs={{0,12},{1,13},{2,14},{3,15},{4,8},{5,9},{6,10},{7,11},{8,4},{9,5},... | collective-permute-start | bytes 196616 | tf_op jit(solution)/shard_map/ppermute | solution.py:371
  66.3 10.4 %collective-permute-start.15 = (bf16[16,2048]{1,0:T(8,128)(2,1)S(1)}, bf16[16,2048]{1,0:T(8,128)(2,1)S(1)}, u32[]{:S(2)}, u32[]{:S(2)}) collective-permute-start(bf16[16,2048]{1,0:T(8,128)(2,1)S(1)} %get-tuple-element.57), channel_id=1, source_target_pairs={{0,12},{1,13},{2,14},{3,15},{4,8},{5,9},{6,10},{7,11},{8,4},{9,5},... | collective-permute-start | bytes 196616 | tf_op jit(solution)/shard_map/ppermute | solution.py:371
  68.4 7.2 %collective-permute-start.20 = (bf16[16,2048]{1,0:T(8,128)(2,1)S(1)}, bf16[16,2048]{1,0:T(8,128)(2,1)S(1)}, u32[]{:S(2)}, u32[]{:S(2)}) collective-permute-start(bf16[16,2048]{1,0:T(8,128)(2,1)S(1)} %get-tuple-element.63), channel_id=1, source_target_pairs={{0,8},{1,9},{2,10},{3,11},{4,12},{5,13},{6,14},{7,15},{8,0},{9,1},... | collective-permute-start | bytes 196616 | tf_op jit(solution)/shard_map/ppermute | solution.py:371
  68.4 7.2 %collective-permute-start.21 = (bf16[16,2048]{1,0:T(8,128)(2,1)S(1)}, bf16[16,2048]{1,0:T(8,128)(2,1)S(1)}, u32[]{:S(2)}, u32[]{:S(2)}) collective-permute-start(bf16[16,2048]{1,0:T(8,128)(2,1)S(1)} %get-tuple-element.64), channel_id=1, source_target_pairs={{0,4},{1,5},{2,6},{3,7},{4,0},{5,1},{6,2},{7,3},{8,12},{9,13},{10,... | collective-permute-start | bytes 196616 | tf_op jit(solution)/shard_map/ppermute | solution.py:371
  70.8 6.2 %collective-permute-start.16 = (bf16[16,2048]{1,0:T(8,128)(2,1)S(1)}, bf16[16,2048]{1,0:T(8,128)(2,1)S(1)}, u32[]{:S(2)}, u32[]{:S(2)}) collective-permute-start(bf16[16,2048]{1,0:T(8,128)(2,1)S(1)} %get-tuple-element.58), channel_id=1, source_target_pairs={{0,8},{1,9},{2,10},{3,11},{4,12},{5,13},{6,14},{7,15},{8,0},{9,1},... | collective-permute-start | bytes 196616 | tf_op jit(solution)/shard_map/ppermute | solution.py:371
  71.3 5.7 %collective-permute-start.17 = (bf16[16,2048]{1,0:T(8,128)(2,1)S(1)}, bf16[16,2048]{1,0:T(8,128)(2,1)S(1)}, u32[]{:S(2)}, u32[]{:S(2)}) collective-permute-start(bf16[16,2048]{1,0:T(8,128)(2,1)S(1)} %get-tuple-element.59), channel_id=1, source_target_pairs={{0,4},{1,5},{2,6},{3,7},{4,0},{5,1},{6,2},{7,3},{8,12},{9,13},{10,... | collective-permute-start | bytes 196616 | tf_op jit(solution)/shard_map/ppermute | solution.py:371

commit v6 on v3

v6 whole, which is shorter than its diff:
```python
import functools

import jax
import jax.numpy as jnp
from jax import lax
from jax.experimental import pallas as pl
from jax.experimental.pallas import tpu as pltpu
from jax.sharding import PartitionSpec as P

PIECES = 8
MIB = 1024 * 1024
F32 = jnp.float32
BF16 = jnp.bfloat16

SMEM = pl.BlockSpec(memory_space=pltpu.SMEM)
VMEM = pl.BlockSpec(memory_space=pltpu.VMEM)
HBM = pl.BlockSpec(memory_space=pltpu.HBM)
ANY = pl.BlockSpec(memory_space=pl.ANY)


FREE = pl.CostEstimate(flops=1, bytes_accessed=1, transcendentals=0)


def params(mib):
    return pltpu.CompilerParams(vmem_limit_bytes=mib * MIB)


def fetch(pairs, sems):
    copies = [pltpu.make_async_copy(src, dst, sems.at[i]) for i, (src, dst) in enumerate(pairs)]
    for copy in copies:
        copy.start()
    for copy in copies:
        copy.wait()


def turns(experts):
    return [0] + list(range(experts - 1, 0, -1))


def slot_tokens(info_ref, pick_ref, tok_rows):
    experts, slots = pick_ref.shape
    rows = [pick_ref[pl.ds(info_ref[1] ^ d, 1), :] for d in turns(experts)]
    picks = jnp.concatenate(rows, axis=1)
    return lax.broadcasted_iota(jnp.int32, (tok_rows, experts * slots), 0) == picks


def pre_kernel(info_ref, pick_hbm, tok_hbm, shift_hbm, scale_hbm, *refs):
    outs = refs[:-5]
    pick_ref, tok_ref, shift_ref, scale_ref, sems = refs[-5:]
    slots = pick_ref.shape[1]
    fetch(
        [(tok_hbm, tok_ref), (pick_hbm, pick_ref), (shift_hbm, shift_ref), (scale_hbm, scale_ref)],
        sems,
    )
    hot = slot_tokens(info_ref, pick_ref, tok_ref.shape[0]).astype(F32).astype(BF16)
    values = lax.dot_general(hot, tok_ref[...], (((0,), (0,)), ((), ())), preferred_element_type=F32)
    center = values - jnp.mean(values, axis=1, keepdims=True)
    spread = jnp.mean(center * center, axis=1, keepdims=True)
    normed = center * (1.0 / jnp.sqrt(spread + 1e-06))
    scale = scale_ref[pl.ds(info_ref[0], 1), :]
    shift = shift_ref[pl.ds(info_ref[0], 1), :]
    modulated = (normed * (1.0 + scale) + shift).astype(BF16)
    for i, out in enumerate(outs):
        out[...] = modulated[i * slots:(i + 1) * slots]


def pre(info, pick, tokens, shift, scale):
    experts, slots = pick.shape
    width = tokens.shape[1]
    return pl.pallas_call(
        pre_kernel,
        in_specs=[SMEM] + [HBM] * 4,
        out_specs=[VMEM] * experts,
        out_shape=[jax.ShapeDtypeStruct((slots, width), BF16)] * experts,
        scratch_shapes=[
            pltpu.VMEM(pick.shape, jnp.int32),
            pltpu.VMEM(tokens.shape, BF16),
            pltpu.VMEM(shift.shape, F32),
            pltpu.VMEM(scale.shape, F32),
            pltpu.SemaphoreType.DMA((4,)),
        ],
        compiler_params=params(12),
        cost_estimate=FREE,
        name="pre",
    )(info, pick, tokens, shift, scale)


def mixer_kernel(info_ref, count_ref, pick_hbm, comb_hbm, gate_hbm, after_ref, mix_ref, row_ref, pick_ref, comb_ref, gate_ref, sems):
    fetch([(pick_hbm, pick_ref), (comb_hbm, comb_ref), (gate_hbm, gate_ref)], sems)
    experts, slots = pick_ref.shape
    tok_rows = mix_ref.shape[0]
    hot = slot_tokens(info_ref, pick_ref, tok_rows)
    lanes = lax.broadcasted_iota(jnp.int32, (1, slots), 1)
    weights = []
    for d in turns(experts):
        e = info_ref[1] ^ d
        weights.append(jnp.where(lanes < count_ref[0, e], comb_ref[pl.ds(e, 1), :], 0.0))
    mix = jnp.where(hot, jnp.concatenate(weights, axis=1), 0.0)
    high = mix.astype(BF16).astype(F32)
    rest = mix - high
    mid = rest.astype(BF16).astype(F32)
    mix_ref[...] = jnp.concatenate([high, mid, rest - mid], axis=1).astype(BF16)
    row_ref[...] = gate_ref[pl.ds(info_ref[0], 1), :]


def mixer(info, count, pick, comb, gate, after, tok_rows):
    experts, slots = pick.shape
    return pl.pallas_call(
        mixer_kernel,
        in_specs=[SMEM, SMEM] + [HBM] * 3 + [ANY],
        out_specs=[VMEM] * 2,
        out_shape=[
            jax.ShapeDtypeStruct((tok_rows, 3 * experts * slots), BF16),
            jax.ShapeDtypeStruct((1, gate.shape[1]), F32),
        ],
        scratch_shapes=[
            pltpu.VMEM(pick.shape, jnp.int32),
            pltpu.VMEM(comb.shape, F32),
            pltpu.VMEM(gate.shape, F32),
            pltpu.SemaphoreType.DMA((3,)),
        ],
        compiler_params=params(8),
        cost_estimate=FREE,
        name="mixer",
    )(info, count, pick, comb, gate, after)


def join_kernel(*refs, cuts):
    out_ref = refs[-1]
    at = 0
    for ref, cut in zip(refs, cuts):
        out_ref[at:at + ref.shape[0], :] = ref[...] if cut is None else ref[:, cut[0]:cut[1]]
        at += ref.shape[0]


def join(parts, after):
    arrays = [p[0] if isinstance(p, tuple) else p for p in parts]
    cuts = [p[1] if isinstance(p, tuple) else None for p in parts]
    step = min(a.shape[1] for a in arrays)
    return pl.pallas_call(
        functools.partial(join_kernel, cuts=cuts),
        in_specs=[VMEM] * len(arrays) + [ANY] * len(after),
        out_specs=VMEM,
        out_shape=jax.ShapeDtypeStruct((sum(a.shape[0] for a in arrays), step), BF16),
        compiler_params=params(4),
        cost_estimate=FREE,
        name="join",
    )(*arrays, *after)


def stream(w_hbm, out_ref, sems, at):
    rows, columns = out_ref.shape
    pieces = sems.shape[0]
    part = rows // pieces
    return [
        pltpu.make_async_copy(
            w_hbm.at[pl.ds(at[0] + p * part, part), pl.ds(at[1], columns)],
            out_ref.at[pl.ds(p * part, part), :],
            sems.at[p],
        )
        for p in range(pieces)
    ]


def load_kernel(w_hbm, *refs, at):
    out_ref, sems = refs[-2:]
    copies = stream(w_hbm, out_ref, sems, at)
    for copy in copies:
        copy.start()
    for copy in copies:
        copy.wait()


def load(w, at, shape, after):
    return pl.pallas_call(
        functools.partial(load_kernel, at=at),
        in_specs=[HBM] + [ANY] * len(after),
        out_specs=VMEM,
        out_shape=pltpu.VMEM(shape, w.dtype),
        scratch_shapes=[pltpu.SemaphoreType.DMA((PIECES,))],
        compiler_params=params(2),
        cost_estimate=FREE,
        name="load",
    )(w, *after)


def join_kernel(*refs, count):
    out_ref = refs[-1]
    at = 0
    for ref in refs[:count]:
        out_ref[at:at + ref.shape[0], :] = ref[...]
        at += ref.shape[0]


def join(parts, after):
    return pl.pallas_call(
        functools.partial(join_kernel, count=len(parts)),
        in_specs=[VMEM] * len(parts) + [ANY] * len(after),
        out_specs=VMEM,
        out_shape=jax.ShapeDtypeStruct((sum(p.shape[0] for p in parts), parts[0].shape[1]), BF16),
        compiler_params=params(2),
        cost_estimate=FREE,
        name="join",
    )(*parts, *after)


def up_kernel(*refs, sources, count, at):
    w_ref, next_hbm = refs[count:count + 2]
    if sources is None:
        rows_ref = refs[0]
        out_ref, next_ref, sems = refs[-3:]
    else:
        out_ref, next_ref, rows_ref, sems = refs[-4:]
    copies = stream(next_hbm, next_ref, sems, at)
    for copy in copies:
        copy.start()
    if sources is not None:
        to = 0
        for source, low, high in sources:
            rows_ref[to:to + high - low, :] = refs[source][low:high, :]
            to += high - low
    hidden = w_ref.shape[0]
    tile = min(512, hidden)

    @pl.loop(0, hidden // tile)
    def _(i):
        cut = pl.ds(pl.multiple_of(i * tile, tile), tile)
        lifted = lax.dot_general(
            rows_ref[...], w_ref[cut, :], (((1,), (1,)), ((), ())), preferred_element_type=F32
        )
        out_ref[:, cut] = jax.nn.gelu(lifted, approximate=True).astype(BF16)

    for copy in copies:
        copy.wait()


def up(parts, sources, w, following, at, shape):
    hidden, width = w.shape
    rows = parts[0].shape[0] if sources is None else sum(high - low for _, low, high in sources)
    out_shape = [jax.ShapeDtypeStruct((rows, hidden), BF16), pltpu.VMEM(shape, BF16)]
    if sources is not None:
        out_shape.append(jax.ShapeDtypeStruct((rows, width), BF16))
    return pl.pallas_call(
        functools.partial(up_kernel, sources=sources, count=len(parts), at=at),
        in_specs=[VMEM] * len(parts) + [VMEM, HBM],
        out_specs=[VMEM] * len(out_shape),
        out_shape=out_shape,
        scratch_shapes=[pltpu.SemaphoreType.DMA((PIECES,))],
        compiler_params=params(12),
        cost_estimate=FREE,
        name="up",
    )(*parts, w, following)


def down_kernel(*refs, count):
    w_ref, keep_ref, send_ref = refs[count:]
    half, step = keep_ref.shape
    tile = min(1024, step)

    @pl.loop(0, step // tile)
    def _(i):
        cut = pl.ds(pl.multiple_of(i * tile, tile), tile)
        at = 0
        out = None
        for h_ref in refs[:count]:
            part = jnp.dot(
                h_ref[...], w_ref[at:at + h_ref.shape[1], cut], preferred_element_type=F32
            )
            out = part if out is None else out + part
            at += h_ref.shape[1]
        keep_ref[:, cut] = out[:half]
        send_ref[:, cut] = out[half:].astype(BF16)


def down(hiddens, w):
    half = hiddens[0].shape[0] // 2
    step = w.shape[1]
    return pl.pallas_call(
        functools.partial(down_kernel, count=len(hiddens)),
        in_specs=[VMEM] * (len(hiddens) + 1),
        out_specs=[VMEM] * 2,
        out_shape=[
            jax.ShapeDtypeStruct((half, step), F32),
            jax.ShapeDtypeStruct((half, step), BF16),
        ],
        compiler_params=params(12),
        cost_estimate=FREE,
        name="down",
    )(*hiddens, w)


def add_kernel(*refs, count, cuts):
    at = 0
    for i in range(count):
        keep_ref, got_ref = refs[2 * i:2 * i + 2]
        step = keep_ref.shape[1]
        for ref, (low, high) in zip(refs[2 * count:], cuts):
            total = keep_ref[low:high] + got_ref[low:high].astype(F32)
            ref[:, at:at + step] = total.astype(ref.dtype)
        at += step


def add(pairs, cuts, kinds):
    width = sum(keep.shape[1] for keep, _ in pairs)
    args = [x for pair in pairs for x in pair]
    return pl.pallas_call(
        functools.partial(add_kernel, count=len(pairs), cuts=cuts),
        in_specs=[VMEM] * len(args),
        out_specs=[VMEM] * len(cuts),
        out_shape=[jax.ShapeDtypeStruct((high - low, width), k) for (low, high), k in zip(cuts, kinds)],
        compiler_params=params(8),
        cost_estimate=FREE,
        name="add",
    )(*args)


def post_kernel(mix_ref, row_ref, keep_ref, near_ref, *refs):
    out_ref = refs[-1]
    step = out_ref.shape[1]
    cut = pl.ds(pl.multiple_of(pl.program_id(0) * step, step), step)
    own = (keep_ref[:, cut] + near_ref[:, cut].astype(F32)).astype(BF16)
    values = jnp.concatenate([own] + [ref[:, cut] for ref in refs[:-1]], axis=0)
    values = jnp.concatenate([values] * 3, axis=0)
    mixed = jnp.dot(mix_ref[...], values, preferred_element_type=F32)
    out_ref[...] = (row_ref[:, cut] * mixed).astype(BF16)


def post(mix, row, keep, near, parts):
    tok_rows = mix.shape[0]
    width = row.shape[1]
    step = min(1024, width)
    return pl.pallas_call(
        post_kernel,
        grid=(width // step,),
        in_specs=[VMEM] * (4 + len(parts)),
        out_specs=pl.BlockSpec((tok_rows, step), lambda i: (0, i)),
        out_shape=jax.ShapeDtypeStruct((tok_rows, width), BF16),
        compiler_params=params(8),
        cost_estimate=FREE,
        name="post",
    )(mix, row, keep, near, *parts)


def shards(tokens, shift, scale, gate, w_up, w_down, pick, count, combine):
    tok_rows, width = tokens.shape
    _, experts, slots = pick.shape
    devices = lax.axis_size("expert")
    place = lax.axis_index("expert")
    group = devices // experts
    requests = shift.shape[0]
    hidden = w_up.shape[0]
    info = jnp.stack([place // (devices // requests), place // group]).astype(jnp.int32)
    pick = pick[0]
    comb = combine[0]

    far = [d * group for d in turns(experts)[1:]]
    near = []
    bit = group // 2
    while bit:
        near.append(bit)
        bit //= 2

    def swap(x, mask):
        return lax.ppermute(x, "expert", [(i, i ^ mask) for i in range(devices)])

    tokens, shift, scale, gate, w_up, w_down, pick, comb = [
        pltpu.with_memory_space_constraint(x, pltpu.HBM)
        for x in (tokens, shift, scale, gate, w_up, w_down, pick, comb)
    ]
    own, *flat = pre(info, pick, tokens, shift, scale)
    mix, row = mixer(info, count, pick, comb, gate, own, tok_rows)

    blocks = [own] + [swap(x, mask) for x, mask in zip(flat, far)]
    beside = [swap(block, near[0]) for block in blocks]
    block_up = (hidden // 2, width)
    ups = [load(w_up, (0, 0), block_up, [blocks[-1], mix])]
    ups.append(load(w_up, (hidden // 2, 0), block_up, [blocks[1], ups[0]]))
    early, late = [0, experts - 1], list(range(1, experts - 1))
    parts = []
    sources = []
    for members, after in ((early, []), (late, ups[1:])):
        pieces = [join([x for i in members for x in (blocks[i], beside[i])], after)]
        height = pieces[0].shape[0]
        for mask in near[1:]:
            block = pieces[0] if len(pieces) == 1 else join(pieces, [])
            pieces = [block, swap(block, mask)]
        cuts = []
        for piece in pieces:
            cuts += [(len(parts), at, at + height) for at in range(0, piece.shape[0], height)]
            parts.append(piece)
        sources.append(cuts)
    sources = [cut for pair in zip(*sources) for cut in pair]

    step = width // 2
    hid, down_a, rows = up(parts, sources, ups[0], w_down, (0, 0), (hidden, step))
    hid_b, down_b = up([rows], None, ups[1], w_down, (0, step), (hidden, step))

    pairs = []
    for w in (down_a, down_b):
        keep, send = down([hid, hid_b], w)
        for i, mask in enumerate(reversed(near[1:])):
            if i:
                half = keep.shape[0] // 2
                keep, send = add([(keep, got)], [(0, half), (half, 2 * half)], [F32, BF16])
            got = swap(send, mask)
        pairs.append((keep, got))
    places = {}
    for at, i in enumerate(early + late):
        places[i] = (2 * at * slots, (2 * at + 1) * slots)
    order = list(range(1, experts)) + [0]
    keeps = [places[i] for i in order]
    sends = [(high, high + slots) for _, high in keeps]
    summed = add(pairs, sends + keeps, [BF16] * experts + [F32] * experts)
    sends, keeps = summed[:experts], summed[experts:]
    arrived = [swap(send, near[0]) for send in sends]
    back = []
    for i, mask in enumerate(far):
        (part,) = add([(keeps[i], arrived[i])], [(0, slots)], [BF16])
        back.append(swap(part, mask))
    return post(mix, row, keeps[-1], arrived[-1], back)


def solution(mesh):
    return jax.shard_map(
        shards,
        mesh=mesh,
        in_specs=(
            P(("groups", "expert"), None),
            P("groups", None),
            P("groups", None),
            P("groups", None),
            P("expert", None),
            P("expert", None),
            P(("groups", "expert"), None, None),
            P(("groups", "expert"), None),
            P(("groups", "expert"), None, None),
        ),
        out_specs=P(("groups", "expert"), None),
        check_vma=False,
    )
```

time: 83.2 us -> 70.3 us (0.84)
  Pallas kernels: 39.2 us -> 25.5 us
  waiting for transfers between devices: 12 us -> 23.2 us
  starting transfers between devices: 31.5 us -> 20.5 us
    pallas_call x19 -> x14, Pallas kernels: 37.7 us -> 24 us  [the longest x2 6.96 us: load(): pl.pallas_call(functools.partial(load_kernel, at=at), in_specs=[HBM] + [A...]
    ppermute x21 -> x18, waiting for transfers between devices: 12 us -> 23.2 us  [swap(): return lax.ppermute(x, 'expert', [(i, i ^ mask) for i in range(devices)])]
    ppermute x21 -> x18, starting transfers between devices: 31.5 us -> 20.5 us  [swap(): return lax.ppermute(x, 'expert', [(i, i ^ mask) for i in range(devices)])]
  transfers between devices with their start and end apart: 21 -> 18, of which waited for: 6 -> 13; matrix products, arithmetic and copies ran while one was open for 0% -> 0% of each run, Pallas kernels for 33% -> 12%
where the time goes in v6:
time: 70.3 us; the launch traced here: 70.1 us
  Pallas kernels  25.5 us (36%)
  waiting for transfers between devices  23.2 us (33%)
  starting transfers between devices  20.5 us (29%)
    ppermute x18, waiting for transfers between devices, swap(): return lax.ppermute(x, 'expert', [(i, i ^ mask) for i in range(devices)])  23.2 us
    ppermute x18, starting transfers between devices, swap(): return lax.ppermute(x, 'expert', [(i, i ^ mask) for i in range(devices)])  20.5 us
    pallas_call x2, Pallas kernels, load(): pl.pallas_call(functools.partial(load_kernel, at=at), in_specs=[HBM] + [A...  6.96 us
    pallas_call x2, Pallas kernels, up(): pl.pallas_call(functools.partial(up_kernel, sources=sources, count=len(pa...  6.95 us
    pallas_call x2, Pallas kernels, down(): pl.pallas_call(functools.partial(down_kernel, count=len(hiddens)), in_spe...  5 us
    pallas_call x1, Pallas kernels, pre(): pl.pallas_call(pre_kernel, in_specs=[SMEM] + [HBM] * 4, out_specs=[VMEM]...  2.67 us
    pallas_call x1, Pallas kernels, post(): pl.pallas_call(post_kernel, grid=(width // step,), in_specs=[VMEM] * (4 +...  2.11 us
    pallas_call x1, Pallas kernels, mixer(): pl.pallas_call(mixer_kernel, in_specs=[SMEM, SMEM] + [HBM] * 3 + [ANY], o...  1.53 us
  transfers between devices with their start and end apart: 18, of which 13 were waited for; matrix products, arithmetic and copies ran while one was open for 0% of the time, Pallas kernels for 12%

profile of v6, /device:TPU:0, one launch (start us, length us, event | category | flops | bytes accessed | tf_op | source)
XLA Modules:
  0.0 70.1 jit_solution(11936263352307205393)
XLA Ops:
  0.1 2.7 %pre.1 = (bf16[16,4096]{1,0:T(8,128)(2,1)S(1)}, bf16[16,4096]{1,0:T(8,128)(2,1)S(1)}, bf16[16,4096]{1,0:T(8,128)(2,1)S(1)}, bf16[16,4096]{1,0:T(8,128)(2,1)S(1)}) custom-call(s32[2]{0:T(128)S(1)} %pad_add_fusion.info_ref, s32[4,16]{1,0:T(4,128)} %bitcast.4, bf16[128,4096]{1,0:T(8,128)(2,1)} %tok_hbm.1, f32[2,4096]{1,0:T(2,128)} %shift_hbm.1, f32[2,4096]{1,0:T(2,128)} %scale_hbm.1), custom_call_target="tpu_custom_call" | custom-call | flops 1 | bytes 1 | tf_op jit(solution)/shard_map/pre/pallas_call | solution.py:70
  2.8 3.1 %collective-permute-start.1 = (bf16[16,4096]{1,0:T(8,128)(2,1)S(1)}, bf16[16,4096]{1,0:T(8,128)(2,1)S(1)}, u32[]{:S(2)}, u32[]{:S(2)}) collective-permute-start(bf16[16,4096]{1,0:T(8,128)(2,1)S(1)} %get-tuple-element.31), channel_id=1, source_target_pairs={{0,4},{1,5},{2,6},{3,7},{4,0},{5,1},{6,2},{7,3},{8,12},{9,13},{10,... | collective-permute-start | bytes 393224 | tf_op jit(solution)/shard_map/ppermute | solution.py:364
  5.8 2.5 %collective-permute-start.4 = (bf16[16,4096]{1,0:T(8,128)(2,1)S(1)}, bf16[16,4096]{1,0:T(8,128)(2,1)S(1)}, u32[]{:S(2)}, u32[]{:S(2)}) collective-permute-start(bf16[16,4096]{1,0:T(8,128)(2,1)S(1)} %get-tuple-element.32), channel_id=1, source_target_pairs={{0,12},{1,13},{2,14},{3,15},{4,8},{5,9},{6,10},{7,11},{8,4},{9,5},... | collective-permute-start | bytes 393224 | tf_op jit(solution)/shard_map/ppermute | solution.py:364
  8.4 1.5 %collective-permute-start = (bf16[16,4096]{1,0:T(8,128)(2,1)S(1)}, bf16[16,4096]{1,0:T(8,128)(2,1)S(1)}, u32[]{:S(2)}, u32[]{:S(2)}) collective-permute-start(bf16[16,4096]{1,0:T(8,128)(2,1)S(1)} %get-tuple-element.28.after_ref.refs_0_), channel_id=1, source_target_pairs={{0,2},{1,3},{2,0},{3,1},{4,6},{5,7},{6,4},{7,5},{8,10},{9,11},{10,... | collective-permute-start | bytes 393224 | tf_op jit(solution)/shard_map/ppermute | solution.py:364
  11.0 4.6 %collective-permute-done.4.refs_0_ = bf16[16,4096]{1,0:T(8,128)(2,1)S(1)} collective-permute-done((bf16[16,4096]{1,0:T(8,128)(2,1)S(1)}, bf16[16,4096]{1,0:T(8,128)(2,1)S(1)}, u32[]{:S(2)}, u32[]{:S(2)}) %collective-permute-start.4) | collective-permute-done | bytes 131104 | tf_op jit(solution)/shard_map/ppermute | solution.py:364
  15.6 1.5 %collective-permute-start.5 = (bf16[16,4096]{1,0:T(8,128)(2,1)S(1)}, bf16[16,4096]{1,0:T(8,128)(2,1)S(1)}, u32[]{:S(2)}, u32[]{:S(2)}) collective-permute-start(bf16[16,4096]{1,0:T(8,128)(2,1)S(1)} %collective-permute-done.4.refs_0_), channel_id=1, source_target_pairs={{0,2},{1,3},{2,0},{3,1},{4,6},{5,7},{6,4},{7,5},{8,10},{9,11},{10,... | collective-permute-start | bytes 393224 | tf_op jit(solution)/shard_map/ppermute | solution.py:364
  17.1 3.0 %collective-permute-done.6.refs_2_ = bf16[16,4096]{1,0:T(8,128)(2,1)S(1)} collective-permute-done((bf16[16,4096]{1,0:T(8,128)(2,1)S(1)}, bf16[16,4096]{1,0:T(8,128)(2,1)S(1)}, u32[]{:S(2)}, u32[]{:S(2)}) %collective-permute-start.6) | collective-permute-done | bytes 131104 | tf_op jit(solution)/shard_map/ppermute | solution.py:364
  20.1 1.5 %collective-permute-start.7 = (bf16[16,4096]{1,0:T(8,128)(2,1)S(1)}, bf16[16,4096]{1,0:T(8,128)(2,1)S(1)}, u32[]{:S(2)}, u32[]{:S(2)}) collective-permute-start(bf16[16,4096]{1,0:T(8,128)(2,1)S(1)} %collective-permute-done.6.refs_2_), channel_id=1, source_target_pairs={{0,2},{1,3},{2,0},{3,1},{4,6},{5,7},{6,4},{7,5},{8,10},{9,11},{10,... | collective-permute-start | bytes 393224 | tf_op jit(solution)/shard_map/ppermute | solution.py:364
  22.3 1.5 %mixer.1 = (bf16[128,192]{1,0:T(8,128)(2,1)S(1)}, f32[1,4096]{1,0:T(1,128)S(1)}) custom-call(s32[2]{0:T(128)S(1)} %pad_add_fusion.info_ref, s32[1,4]{1,0:T(1,128)S(1)} %copy-done, s32[4,16]{1,0:T(4,128)} %bitcast.5, f32[4,16]{1,0:T(4,128)} %bitcast.6, f32[2,4096]{1,0:T(2,128)} %gate_hbm.1, bf16[16,4096]{1,0:T(8,128)(2,1)S(1)} %get-tuple-element.28.after_ref.refs_0_), custom_call_target="tpu_custom_call" | custom-call | flops 1 | bytes 1 | tf_op jit(solution)/shard_map/mixer/pallas_call | solution.py:108
  23.8 3.5 %load.2.refs_1_.refs_4_ = bf16[1024,4096]{1,0:T(8,128)(2,1)S(1)} custom-call(bf16[2048,4096]{1,0:T(8,128)(2,1)} %w_hbm.3, bf16[16,4096]{1,0:T(8,128)(2,1)S(1)} %collective-permute-done.1.refs_2_.refs_0_, bf16[128,192]{1,0:T(8,128)(2,1)S(1)} %get-tuple-element.29.refs_1_.mix_ref), custom_call_target="tpu_custom_call" | custom-call | flops 1 | bytes 1 | tf_op jit(solution)/shard_map/load/pallas_call | solution.py:175
  27.3 3.5 %load.3.refs_4_.refs_1_ = bf16[1024,4096]{1,0:T(8,128)(2,1)S(1)} custom-call(bf16[2048,4096]{1,0:T(8,128)(2,1)} %w_hbm.3, bf16[16,4096]{1,0:T(8,128)(2,1)S(1)} %collective-permute-done.4.refs_0_, bf16[1024,4096]{1,0:T(8,128)(2,1)S(1)} %load.2.refs_1_.refs_4_), custom_call_target="tpu_custom_call" | custom-call | flops 1 | bytes 1 | tf_op jit(solution)/shard_map/load/pallas_call | solution.py:175
  33.5 3.5 %up.2 = (bf16[256,1024]{1,0:T(8,128)(2,1)S(1)}, bf16[2048,2048]{1,0:T(8,128)(2,1)S(1)}, bf16[256,4096]{1,0:T(8,128)(2,1)S(1)}) custom-call(bf16[64,4096]{1,0:T(8,128)(2,1)S(1)} %join.2.refs_0_, bf16[64,4096]{1,0:T(8,128)(2,1)S(1)} %collective-permute-done.3.refs_1_, bf16[64,4096]{1,0:T(8,128)(2,1)S(1)} %join.3.refs_2_, ...), custom_call_target="tpu_custom_call" | custom-call | flops 1 | bytes 1 | tf_op jit(solution)/shard_map/up/pallas_call | solution.py:243
  37.0 3.5 %up.3 = (bf16[256,1024]{1,0:T(8,128)(2,1)S(1)}, bf16[2048,2048]{1,0:T(8,128)(2,1)S(1)}) custom-call(bf16[256,4096]{1,0:T(8,128)(2,1)S(1)} %get-tuple-element.35.refs_0_, bf16[1024,4096]{1,0:T(8,128)(2,1)S(1)} %load.3.refs_4_.refs_1_, bf16[2048,4096]{1,0:T(8,128)(2,1)} %refs_2_.1), custom_call_target="tpu_custom_call" | custom-call | flops 1 | bytes 1 | tf_op jit(solution)/shard_map/up/pallas_call | solution.py:243
  40.5 2.5 %down.2 = (f32[128,2048]{1,0:T(8,128)S(1)}, bf16[128,2048]{1,0:T(8,128)(2,1)S(1)}) custom-call(bf16[256,1024]{1,0:T(8,128)(2,1)S(1)} %get-tuple-element.34.refs_0_, bf16[256,1024]{1,0:T(8,128)(2,1)S(1)} %get-tuple-element.36.refs_1_, bf16[2048,2048]{1,0:T(8,128)(2,1)S(1)} %get-tuple-element.37.refs_2_), custom_call_target="tpu_custom_call" | custom-call | flops 1 | bytes 1 | tf_op jit(solution)/shard_map/down/pallas_call | solution.py:278
  43.0 2.5 %down.3 = (f32[128,2048]{1,0:T(8,128)S(1)}, bf16[128,2048]{1,0:T(8,128)(2,1)S(1)}) custom-call(bf16[256,1024]{1,0:T(8,128)(2,1)S(1)} %get-tuple-element.34.refs_0_, bf16[256,1024]{1,0:T(8,128)(2,1)S(1)} %get-tuple-element.36.refs_1_, bf16[2048,2048]{1,0:T(8,128)(2,1)S(1)} %get-tuple-element.40.refs_2_), custom_call_target="tpu_custom_call" | custom-call | flops 1 | bytes 1 | tf_op jit(solution)/shard_map/down/pallas_call | solution.py:278
  46.1 1.4 %collective-permute-done.9.refs_1_ = bf16[128,2048]{1,0:T(8,128)(2,1)S(1)} collective-permute-done((bf16[128,2048]{1,0:T(8,128)(2,1)S(1)}, bf16[128,2048]{1,0:T(8,128)(2,1)S(1)}, u32[]{:S(2)}, u32[]{:S(2)}) %collective-permute-start.9) | collective-permute-done | bytes 524320 | tf_op jit(solution)/shard_map/ppermute | solution.py:364
  49.0 1.5 %collective-permute-start.14 = (bf16[16,4096]{1,0:T(8,128)(2,1)S(1)}, bf16[16,4096]{1,0:T(8,128)(2,1)S(1)}, u32[]{:S(2)}, u32[]{:S(2)}) collective-permute-start(bf16[16,4096]{1,0:T(8,128)(2,1)S(1)} %get-tuple-element.48), channel_id=1, source_target_pairs={{0,2},{1,3},{2,0},{3,1},{4,6},{5,7},{6,4},{7,5},{8,10},{9,11},{10,... | collective-permute-start | bytes 393224 | tf_op jit(solution)/shard_map/ppermute | solution.py:364
  51.0 1.5 %collective-permute-start.11 = (bf16[16,4096]{1,0:T(8,128)(2,1)S(1)}, bf16[16,4096]{1,0:T(8,128)(2,1)S(1)}, u32[]{:S(2)}, u32[]{:S(2)}) collective-permute-start(bf16[16,4096]{1,0:T(8,128)(2,1)S(1)} %get-tuple-element.44), channel_id=1, source_target_pairs={{0,2},{1,3},{2,0},{3,1},{4,6},{5,7},{6,4},{7,5},{8,10},{9,11},{10,... | collective-permute-start | bytes 393224 | tf_op jit(solution)/shard_map/ppermute | solution.py:364
  52.6 2.3 %collective-permute-done.12.refs_1_ = bf16[16,4096]{1,0:T(8,128)(2,1)S(1)} collective-permute-done((bf16[16,4096]{1,0:T(8,128)(2,1)S(1)}, bf16[16,4096]{1,0:T(8,128)(2,1)S(1)}, u32[]{:S(2)}, u32[]{:S(2)}) %collective-permute-start.12) | collective-permute-done | bytes 131104 | tf_op jit(solution)/shard_map/ppermute | solution.py:364
  54.9 2.7 %collective-permute-start.13 = (bf16[16,4096]{1,0:T(8,128)(2,1)S(1)}, bf16[16,4096]{1,0:T(8,128)(2,1)S(1)}, u32[]{:S(2)}, u32[]{:S(2)}) collective-permute-start(bf16[16,4096]{1,0:T(8,128)(2,1)S(1)} %add.9), channel_id=1, source_target_pairs={{0,12},{1,13},{2,14},{3,15},{4,8},{5,9},{6,10},{7,11},{8,4},{9,5},... | collective-permute-start | bytes 393224 | tf_op jit(solution)/shard_map/ppermute | solution.py:364
  58.3 2.1 %collective-permute-done.16.refs_1_ = bf16[16,4096]{1,0:T(8,128)(2,1)S(1)} collective-permute-done((bf16[16,4096]{1,0:T(8,128)(2,1)S(1)}, bf16[16,4096]{1,0:T(8,128)(2,1)S(1)}, u32[]{:S(2)}, u32[]{:S(2)}) %collective-permute-start.16) | collective-permute-done | bytes 131104 | tf_op jit(solution)/shard_map/ppermute | solution.py:364
  61.1 1.4 %collective-permute-done.11.near_ref = bf16[16,4096]{1,0:T(8,128)(2,1)S(1)} collective-permute-done((bf16[16,4096]{1,0:T(8,128)(2,1)S(1)}, bf16[16,4096]{1,0:T(8,128)(2,1)S(1)}, u32[]{:S(2)}, u32[]{:S(2)}) %collective-permute-start.11) | collective-permute-done | bytes 131104 | tf_op jit(solution)/shard_map/ppermute | solution.py:364
  62.6 5.0 %collective-permute-done.15.refs_1_ = bf16[16,4096]{1,0:T(8,128)(2,1)S(1)} collective-permute-done((bf16[16,4096]{1,0:T(8,128)(2,1)S(1)}, bf16[16,4096]{1,0:T(8,128)(2,1)S(1)}, u32[]{:S(2)}, u32[]{:S(2)}) %collective-permute-start.15) | collective-permute-done | bytes 131104 | tf_op jit(solution)/shard_map/ppermute | solution.py:364
  68.0 2.1 %post.1 = bf16[128,4096]{1,0:T(8,128)(2,1)} custom-call(bf16[128,192]{1,0:T(8,128)(2,1)S(1)} %get-tuple-element.29.refs_1_.mix_ref, f32[1,4096]{1,0:T(1,128)S(1)} %get-tuple-element.30.row_ref, f32[16,4096]{1,0:T(8,128)S(1)} %get-tuple-element.43.keep_ref, bf16[16,4096]{1,0:T(8,128)(2,1)S(1)} %collective-permute-done.11.near_ref, ...), custom_call_target="tpu_custom_call" | custom-call | flops 1 | bytes 1 | tf_op jit(solution)/shard_map/post/pallas_call | solution.py:332
  (30 shorter events, 9.1 us)
Async XLA Ops:
  2.8 7.2 %collective-permute-start.1 = (bf16[16,4096]{1,0:T(8,128)(2,1)S(1)}, bf16[16,4096]{1,0:T(8,128)(2,1)S(1)}, u32[]{:S(2)}, u32[]{:S(2)}) collective-permute-start(bf16[16,4096]{1,0:T(8,128)(2,1)S(1)} %get-tuple-element.31), channel_id=1, source_target_pairs={{0,4},{1,5},{2,6},{3,7},{4,0},{5,1},{6,2},{7,3},{8,12},{9,13},{10,... | collective-permute-start | bytes 393224 | tf_op jit(solution)/shard_map/ppermute | solution.py:364
  5.8 9.7 %collective-permute-start.4 = (bf16[16,4096]{1,0:T(8,128)(2,1)S(1)}, bf16[16,4096]{1,0:T(8,128)(2,1)S(1)}, u32[]{:S(2)}, u32[]{:S(2)}) collective-permute-start(bf16[16,4096]{1,0:T(8,128)(2,1)S(1)} %get-tuple-element.32), channel_id=1, source_target_pairs={{0,12},{1,13},{2,14},{3,15},{4,8},{5,9},{6,10},{7,11},{8,4},{9,5},... | collective-permute-start | bytes 393224 | tf_op jit(solution)/shard_map/ppermute | solution.py:364
  8.3 11.8 %collective-permute-start.6 = (bf16[16,4096]{1,0:T(8,128)(2,1)S(1)}, bf16[16,4096]{1,0:T(8,128)(2,1)S(1)}, u32[]{:S(2)}, u32[]{:S(2)}) collective-permute-start(bf16[16,4096]{1,0:T(8,128)(2,1)S(1)} %get-tuple-element.33), channel_id=1, source_target_pairs={{0,8},{1,9},{2,10},{3,11},{4,12},{5,13},{6,14},{7,15},{8,0},{9,1},... | collective-permute-start | bytes 393224 | tf_op jit(solution)/shard_map/ppermute | solution.py:364
  8.4 22.3 %collective-permute-start = (bf16[16,4096]{1,0:T(8,128)(2,1)S(1)}, bf16[16,4096]{1,0:T(8,128)(2,1)S(1)}, u32[]{:S(2)}, u32[]{:S(2)}) collective-permute-start(bf16[16,4096]{1,0:T(8,128)(2,1)S(1)} %get-tuple-element.28.after_ref.refs_0_), channel_id=1, source_target_pairs={{0,2},{1,3},{2,0},{3,1},{4,6},{5,7},{6,4},{7,5},{8,10},{9,11},{10,... | collective-permute-start | bytes 393224 | tf_op jit(solution)/shard_map/ppermute | solution.py:364
  10.0 20.8 %collective-permute-start.2 = (bf16[16,4096]{1,0:T(8,128)(2,1)S(1)}, bf16[16,4096]{1,0:T(8,128)(2,1)S(1)}, u32[]{:S(2)}, u32[]{:S(2)}) collective-permute-start(bf16[16,4096]{1,0:T(8,128)(2,1)S(1)} %collective-permute-done.1.refs_2_.refs_0_), channel_id=1, source_target_pairs={{0,2},{1,3},{2,0},{3,1},{4,6},{5,7},{6,4},{7,5},{8,10},{9,11},{10,... | collective-permute-start | bytes 393224 | tf_op jit(solution)/shard_map/ppermute | solution.py:364
  15.6 15.3 %collective-permute-start.5 = (bf16[16,4096]{1,0:T(8,128)(2,1)S(1)}, bf16[16,4096]{1,0:T(8,128)(2,1)S(1)}, u32[]{:S(2)}, u32[]{:S(2)}) collective-permute-start(bf16[16,4096]{1,0:T(8,128)(2,1)S(1)} %collective-permute-done.4.refs_0_), channel_id=1, source_target_pairs={{0,2},{1,3},{2,0},{3,1},{4,6},{5,7},{6,4},{7,5},{8,10},{9,11},{10,... | collective-permute-start | bytes 393224 | tf_op jit(solution)/shard_map/ppermute | solution.py:364
  20.1 10.8 %collective-permute-start.7 = (bf16[16,4096]{1,0:T(8,128)(2,1)S(1)}, bf16[16,4096]{1,0:T(8,128)(2,1)S(1)}, u32[]{:S(2)}, u32[]{:S(2)}) collective-permute-start(bf16[16,4096]{1,0:T(8,128)(2,1)S(1)} %collective-permute-done.6.refs_2_), channel_id=1, source_target_pairs={{0,2},{1,3},{2,0},{3,1},{4,6},{5,7},{6,4},{7,5},{8,10},{9,11},{10,... | collective-permute-start | bytes 393224 | tf_op jit(solution)/shard_map/ppermute | solution.py:364
  21.6 0.7 copy-start
  30.8 2.0 %collective-permute-start.3 = (bf16[64,4096]{1,0:T(8,128)(2,1)S(1)}, bf16[64,4096]{1,0:T(8,128)(2,1)S(1)}, u32[]{:S(2)}, u32[]{:S(2)}) collective-permute-start(bf16[64,4096]{1,0:T(8,128)(2,1)S(1)} %join.2.refs_0_), channel_id=1, source_target_pairs={{0,1},{1,0},{2,3},{3,2},{4,5},{5,4},{6,7},{7,6},{8,9},{9,8},{10,11... | collective-permute-start | bytes 1572872 | tf_op jit(solution)/shard_map/ppermute | solution.py:364
  31.0 2.6 %collective-permute-start.8 = (bf16[64,4096]{1,0:T(8,128)(2,1)S(1)}, bf16[64,4096]{1,0:T(8,128)(2,1)S(1)}, u32[]{:S(2)}, u32[]{:S(2)}) collective-permute-start(bf16[64,4096]{1,0:T(8,128)(2,1)S(1)} %join.3.refs_2_), channel_id=1, source_target_pairs={{0,1},{1,0},{2,3},{3,2},{4,5},{5,4},{6,7},{7,6},{8,9},{9,8},{10,11... | collective-permute-start | bytes 1572872 | tf_op jit(solution)/shard_map/ppermute | solution.py:364
  45.5 2.0 %collective-permute-start.9 = (bf16[128,2048]{1,0:T(8,128)(2,1)S(1)}, bf16[128,2048]{1,0:T(8,128)(2,1)S(1)}, u32[]{:S(2)}, u32[]{:S(2)}) collective-permute-start(bf16[128,2048]{1,0:T(8,128)(2,1)S(1)} %get-tuple-element.39), channel_id=1, source_target_pairs={{0,1},{1,0},{2,3},{3,2},{4,5},{5,4},{6,7},{7,6},{8,9},{9,8},{10,11... | collective-permute-start | bytes 1572872 | tf_op jit(solution)/shard_map/ppermute | solution.py:364
  45.7 2.5 %collective-permute-start.10 = (bf16[128,2048]{1,0:T(8,128)(2,1)S(1)}, bf16[128,2048]{1,0:T(8,128)(2,1)S(1)}, u32[]{:S(2)}, u32[]{:S(2)}) collective-permute-start(bf16[128,2048]{1,0:T(8,128)(2,1)S(1)} %get-tuple-element.42), channel_id=1, source_target_pairs={{0,1},{1,0},{2,3},{3,2},{4,5},{5,4},{6,7},{7,6},{8,9},{9,8},{10,11... | collective-permute-start | bytes 1572872 | tf_op jit(solution)/shard_map/ppermute | solution.py:364
  48.4 6.4 %collective-permute-start.12 = (bf16[16,4096]{1,0:T(8,128)(2,1)S(1)}, bf16[16,4096]{1,0:T(8,128)(2,1)S(1)}, u32[]{:S(2)}, u32[]{:S(2)}) collective-permute-start(bf16[16,4096]{1,0:T(8,128)(2,1)S(1)} %get-tuple-element.46), channel_id=1, source_target_pairs={{0,2},{1,3},{2,0},{3,1},{4,6},{5,7},{6,4},{7,5},{8,10},{9,11},{10,... | collective-permute-start | bytes 393224 | tf_op jit(solution)/shard_map/ppermute | solution.py:364
  49.0 8.7 %collective-permute-start.14 = (bf16[16,4096]{1,0:T(8,128)(2,1)S(1)}, bf16[16,4096]{1,0:T(8,128)(2,1)S(1)}, u32[]{:S(2)}, u32[]{:S(2)}) collective-permute-start(bf16[16,4096]{1,0:T(8,128)(2,1)S(1)} %get-tuple-element.48), channel_id=1, source_target_pairs={{0,2},{1,3},{2,0},{3,1},{4,6},{5,7},{6,4},{7,5},{8,10},{9,11},{10,... | collective-permute-start | bytes 393224 | tf_op jit(solution)/shard_map/ppermute | solution.py:364
  50.5 9.9 %collective-permute-start.16 = (bf16[16,4096]{1,0:T(8,128)(2,1)S(1)}, bf16[16,4096]{1,0:T(8,128)(2,1)S(1)}, u32[]{:S(2)}, u32[]{:S(2)}) collective-permute-start(bf16[16,4096]{1,0:T(8,128)(2,1)S(1)} %get-tuple-element.50), channel_id=1, source_target_pairs={{0,2},{1,3},{2,0},{3,1},{4,6},{5,7},{6,4},{7,5},{8,10},{9,11},{10,... | collective-permute-start | bytes 393224 | tf_op jit(solution)/shard_map/ppermute | solution.py:364
  51.0 11.4 %collective-permute-start.11 = (bf16[16,4096]{1,0:T(8,128)(2,1)S(1)}, bf16[16,4096]{1,0:T(8,128)(2,1)S(1)}, u32[]{:S(2)}, u32[]{:S(2)}) collective-permute-start(bf16[16,4096]{1,0:T(8,128)(2,1)S(1)} %get-tuple-element.44), channel_id=1, source_target_pairs={{0,2},{1,3},{2,0},{3,1},{4,6},{5,7},{6,4},{7,5},{8,10},{9,11},{10,... | collective-permute-start | bytes 393224 | tf_op jit(solution)/shard_map/ppermute | solution.py:364
  54.9 7.8 %collective-permute-start.13 = (bf16[16,4096]{1,0:T(8,128)(2,1)S(1)}, bf16[16,4096]{1,0:T(8,128)(2,1)S(1)}, u32[]{:S(2)}, u32[]{:S(2)}) collective-permute-start(bf16[16,4096]{1,0:T(8,128)(2,1)S(1)} %add.9), channel_id=1, source_target_pairs={{0,12},{1,13},{2,14},{3,15},{4,8},{5,9},{6,10},{7,11},{8,4},{9,5},... | collective-permute-start | bytes 393224 | tf_op jit(solution)/shard_map/ppermute | solution.py:364
  57.7 10.0 %collective-permute-start.15 = (bf16[16,4096]{1,0:T(8,128)(2,1)S(1)}, bf16[16,4096]{1,0:T(8,128)(2,1)S(1)}, u32[]{:S(2)}, u32[]{:S(2)}) collective-permute-start(bf16[16,4096]{1,0:T(8,128)(2,1)S(1)} %add.10), channel_id=1, source_target_pairs={{0,8},{1,9},{2,10},{3,11},{4,12},{5,13},{6,14},{7,15},{8,0},{9,1},... | collective-permute-start | bytes 393224 | tf_op jit(solution)/shard_map/ppermute | solution.py:364
  60.5 7.5 %collective-permute-start.17 = (bf16[16,4096]{1,0:T(8,128)(2,1)S(1)}, bf16[16,4096]{1,0:T(8,128)(2,1)S(1)}, u32[]{:S(2)}, u32[]{:S(2)}) collective-permute-start(bf16[16,4096]{1,0:T(8,128)(2,1)S(1)} %add.11), channel_id=1, source_target_pairs={{0,4},{1,5},{2,6},{3,7},{4,0},{5,1},{6,2},{7,3},{8,12},{9,13},{10,... | collective-permute-start | bytes 393224 | tf_op jit(solution)/shard_map/ppermute | solution.py:364

commit v7 on v6

v7 whole, which is shorter than its diff:
```python
import functools

import jax
import jax.numpy as jnp
from jax import lax
from jax.experimental import pallas as pl
from jax.experimental.pallas import tpu as pltpu
from jax.sharding import PartitionSpec as P

PIECES = 8
MIB = 1024 * 1024
F32 = jnp.float32
BF16 = jnp.bfloat16

SMEM = pl.BlockSpec(memory_space=pltpu.SMEM)
VMEM = pl.BlockSpec(memory_space=pltpu.VMEM)
HBM = pl.BlockSpec(memory_space=pltpu.HBM)
ANY = pl.BlockSpec(memory_space=pl.ANY)


FREE = pl.CostEstimate(flops=1, bytes_accessed=1, transcendentals=0)


def params(mib):
    return pltpu.CompilerParams(vmem_limit_bytes=mib * MIB)


def fetch(pairs, sems):
    copies = [pltpu.make_async_copy(src, dst, sems.at[i]) for i, (src, dst) in enumerate(pairs)]
    for copy in copies:
        copy.start()
    for copy in copies:
        copy.wait()


def turns(experts):
    return [0] + list(range(experts - 1, 0, -1))


def hot_rows(picks, tok_rows):
    return lax.broadcasted_iota(jnp.int32, (tok_rows, picks.shape[1]), 0) == picks


def modulate(picks, tok_ref, table_ref):
    hot = hot_rows(picks, tok_ref.shape[0]).astype(F32).astype(BF16)
    values = lax.dot_general(hot, tok_ref[...], (((0,), (0,)), ((), ())), preferred_element_type=F32)
    center = values - jnp.mean(values, axis=1, keepdims=True)
    spread = jnp.mean(center * center, axis=1, keepdims=True)
    normed = center * (1.0 / jnp.sqrt(spread + 1e-06))
    return (normed * table_ref[0:1, :] + table_ref[1:2, :]).astype(BF16)


def first_kernel(info_ref, *refs):
    sources = refs[:7]
    far_ref, tok_ref, table_ref, picks_ref, weights_ref = refs[7:12]
    pick_ref, comb_ref, count_ref, shift_ref, scale_ref, gate_ref, sems = refs[12:]
    fetch(
        list(zip(sources, (tok_ref, pick_ref, shift_ref, scale_ref, gate_ref, comb_ref, count_ref))),
        sems,
    )
    experts, slots = pick_ref.shape
    which = pl.ds(info_ref[0], 1)
    table_ref[0:1, :] = 1.0 + scale_ref[which, :]
    table_ref[1:2, :] = shift_ref[which, :]
    table_ref[2:3, :] = gate_ref[which, :]
    lanes = lax.broadcasted_iota(jnp.int32, (1, slots), 1)
    for i, d in enumerate(turns(experts)):
        e = info_ref[1] ^ d
        picks_ref[i:i + 1, :] = pick_ref[pl.ds(e, 1), :]
        weights_ref[i:i + 1, :] = jnp.where(lanes < count_ref[0, e], comb_ref[pl.ds(e, 1), :], 0.0)
    far_ref[...] = modulate(picks_ref[1:2, :], tok_ref, table_ref)


def first(info, tokens, pick, shift, scale, gate, comb, count):
    experts, slots = pick.shape
    width = tokens.shape[1]
    return pl.pallas_call(
        first_kernel,
        in_specs=[SMEM] + [HBM] * 7,
        out_specs=[VMEM] * 5,
        out_shape=[
            jax.ShapeDtypeStruct((slots, width), BF16),
            jax.ShapeDtypeStruct(tokens.shape, BF16),
            jax.ShapeDtypeStruct((3, width), F32),
            jax.ShapeDtypeStruct(pick.shape, jnp.int32),
            jax.ShapeDtypeStruct(comb.shape, F32),
        ],
        scratch_shapes=[
            pltpu.VMEM(pick.shape, jnp.int32),
            pltpu.VMEM(comb.shape, F32),
            pltpu.SMEM(count.shape, jnp.int32),
            pltpu.VMEM(shift.shape, F32),
            pltpu.VMEM(scale.shape, F32),
            pltpu.VMEM(gate.shape, F32),
            pltpu.SemaphoreType.DMA((7,)),
        ],
        compiler_params=params(8),
        cost_estimate=FREE,
        name="first",
    )(info, tokens, pick, shift, scale, gate, comb, count)


def rest_kernel(tok_ref, table_ref, picks_ref, *outs):
    experts, slots = picks_ref.shape
    order = [0] + list(range(2, experts))
    picks = jnp.concatenate([picks_ref[i:i + 1, :] for i in order], axis=1)
    rows = modulate(picks, tok_ref, table_ref)
    for i, out in enumerate(outs):
        out[...] = rows[i * slots:(i + 1) * slots]


def rest(tok, table, picks):
    experts, slots = picks.shape
    return pl.pallas_call(
        rest_kernel,
        in_specs=[VMEM] * 3,
        out_specs=[VMEM] * (experts - 1),
        out_shape=[jax.ShapeDtypeStruct((slots, tok.shape[1]), BF16)] * (experts - 1),
        compiler_params=params(8),
        cost_estimate=FREE,
        name="rest",
    )(tok, table, picks)


def mixer_kernel(picks_ref, weights_ref, after_ref, *outs):
    for i, out in enumerate(outs):
        each = picks_ref.shape[0] // len(outs)
        rows = range(i * each, (i + 1) * each)
        picks = jnp.concatenate([picks_ref[r:r + 1, :] for r in rows], axis=1)
        weights = jnp.concatenate([weights_ref[r:r + 1, :] for r in rows], axis=1)
        mix = jnp.where(hot_rows(picks, out.shape[0]), weights, 0.0)
        high = mix.astype(BF16).astype(F32)
        out[...] = jnp.concatenate([high, mix - high], axis=1).astype(BF16)


def mixer(picks, weights, after, tok_rows):
    experts, slots = picks.shape
    return pl.pallas_call(
        mixer_kernel,
        in_specs=[VMEM] * 2 + [ANY],
        out_specs=[VMEM] * 2,
        out_shape=[jax.ShapeDtypeStruct((tok_rows, experts * slots), BF16)] * 2,
        compiler_params=params(4),
        cost_estimate=FREE,
        name="mixer",
    )(picks, weights, after)


def stream(w_hbm, out_ref, sems, at):
    rows, columns = out_ref.shape
    pieces = sems.shape[0]
    part = rows // pieces
    return [
        pltpu.make_async_copy(
            w_hbm.at[pl.ds(at[0] + p * part, part), pl.ds(at[1], columns)],
            out_ref.at[pl.ds(p * part, part), :],
            sems.at[p],
        )
        for p in range(pieces)
    ]


def load_kernel(w_hbm, *refs, at):
    out_ref, sems = refs[-2:]
    copies = stream(w_hbm, out_ref, sems, at)
    for copy in copies:
        copy.start()
    for copy in copies:
        copy.wait()


def load(w, at, shape, after):
    return pl.pallas_call(
        functools.partial(load_kernel, at=at),
        in_specs=[HBM] + [ANY] * len(after),
        out_specs=VMEM,
        out_shape=pltpu.VMEM(shape, w.dtype),
        scratch_shapes=[pltpu.SemaphoreType.DMA((PIECES,))],
        compiler_params=params(2),
        cost_estimate=FREE,
        name="load",
    )(w, *after)


def join_kernel(*refs, count):
    out_ref = refs[-1]
    at = 0
    for ref in refs[:count]:
        out_ref[at:at + ref.shape[0], :] = ref[...]
        at += ref.shape[0]


def join(parts, after):
    return pl.pallas_call(
        functools.partial(join_kernel, count=len(parts)),
        in_specs=[VMEM] * len(parts) + [ANY] * len(after),
        out_specs=VMEM,
        out_shape=jax.ShapeDtypeStruct((sum(p.shape[0] for p in parts), parts[0].shape[1]), BF16),
        compiler_params=params(2),
        cost_estimate=FREE,
        name="join",
    )(*parts, *after)


def up_kernel(*refs, sources, count, at):
    w_ref, next_hbm = refs[count:count + 2]
    if sources is None:
        rows_ref = refs[0]
        out_ref, next_ref, sems = refs[-3:]
    else:
        out_ref, next_ref, rows_ref, sems = refs[-4:]
    copies = stream(next_hbm, next_ref, sems, at)
    for copy in copies:
        copy.start()
    if sources is not None:
        to = 0
        for source, low, high in sources:
            rows_ref[to:to + high - low, :] = refs[source][low:high, :]
            to += high - low
    hidden = w_ref.shape[0]
    tile = min(512, hidden)

    @pl.loop(0, hidden // tile)
    def _(i):
        cut = pl.ds(pl.multiple_of(i * tile, tile), tile)
        lifted = lax.dot_general(
            rows_ref[...], w_ref[cut, :], (((1,), (1,)), ((), ())), preferred_element_type=F32
        )
        out_ref[:, cut] = jax.nn.gelu(lifted, approximate=True).astype(BF16)

    for copy in copies:
        copy.wait()


def up(parts, sources, w, following, at, shape):
    hidden, width = w.shape
    rows = parts[0].shape[0] if sources is None else sum(high - low for _, low, high in sources)
    out_shape = [jax.ShapeDtypeStruct((rows, hidden), BF16), pltpu.VMEM(shape, BF16)]
    if sources is not None:
        out_shape.append(jax.ShapeDtypeStruct((rows, width), BF16))
    return pl.pallas_call(
        functools.partial(up_kernel, sources=sources, count=len(parts), at=at),
        in_specs=[VMEM] * len(parts) + [VMEM, HBM],
        out_specs=[VMEM] * len(out_shape),
        out_shape=out_shape,
        scratch_shapes=[pltpu.SemaphoreType.DMA((PIECES,))],
        compiler_params=params(12),
        cost_estimate=FREE,
        name="up",
    )(*parts, w, following)


def down_kernel(*refs, count, blocks, at):
    weights = refs[count:count + blocks]
    if at is None:
        keep_ref, send_ref = refs[count + blocks:]
        copies = []
    else:
        next_hbm, keep_ref, send_ref, next_ref, sems = refs[count + blocks:]
        copies = stream(next_hbm, next_ref, sems, at)
    for copy in copies:
        copy.start()
    half = keep_ref.shape[0]
    base = 0
    for w_ref in weights:
        step = w_ref.shape[1]
        tile = step // 2

        @pl.loop(0, 2)
        def _(i):
            cut = pl.ds(pl.multiple_of(i * tile, tile), tile)
            to = pl.ds(pl.multiple_of(base + i * tile, tile), tile)
            low = 0
            out = None
            for h_ref in refs[:count]:
                part = jnp.dot(
                    h_ref[...], w_ref[low:low + h_ref.shape[1], cut], preferred_element_type=F32
                )
                out = part if out is None else out + part
                low += h_ref.shape[1]
            keep_ref[:, to] = out[:half]
            send_ref[:, to] = out[half:].astype(BF16)

        base += step
    for copy in copies:
        copy.wait()


def down(hiddens, weights, following, at, shape):
    half = hiddens[0].shape[0] // 2
    step = sum(w.shape[1] for w in weights)
    more = following is not None
    return pl.pallas_call(
        functools.partial(down_kernel, count=len(hiddens), blocks=len(weights), at=at),
        in_specs=[VMEM] * (len(hiddens) + len(weights)) + [HBM] * more,
        out_specs=[VMEM] * (2 + more),
        out_shape=[
            jax.ShapeDtypeStruct((half, step), F32),
            jax.ShapeDtypeStruct((half, step), BF16),
        ]
        + ([pltpu.VMEM(shape, BF16)] if more else []),
        scratch_shapes=[pltpu.SemaphoreType.DMA((PIECES,))] * more,
        compiler_params=params(12),
        cost_estimate=FREE,
        name="down",
    )(*hiddens, *weights, *([following] if more else []))


def add_kernel(*refs, count, cuts):
    at = 0
    for i in range(count):
        keep_ref, got_ref = refs[2 * i:2 * i + 2]
        step = keep_ref.shape[1]
        for ref, (low, high) in zip(refs[2 * count:], cuts):
            total = keep_ref[low:high] + got_ref[low:high].astype(F32)
            ref[:, at:at + step] = total.astype(ref.dtype)
        at += step


def add(pairs, cuts, kinds):
    width = sum(keep.shape[1] for keep, _ in pairs)
    args = [x for pair in pairs for x in pair]
    return pl.pallas_call(
        functools.partial(add_kernel, count=len(pairs), cuts=cuts),
        in_specs=[VMEM] * len(args),
        out_specs=[VMEM] * len(cuts),
        out_shape=[jax.ShapeDtypeStruct((high - low, width), k) for (low, high), k in zip(cuts, kinds)],
        compiler_params=params(8),
        cost_estimate=FREE,
        name="add",
    )(*args)


def own_kernel(mix_ref, keep_ref, near_ref, got_ref, acc_ref):
    own = (keep_ref[...] + near_ref[...].astype(F32)).astype(BF16)
    values = jnp.concatenate([own, got_ref[...]] * 2, axis=0)
    acc_ref[...] = jnp.dot(mix_ref[...], values, preferred_element_type=F32)


def own_part(mix, keep, near, got):
    return pl.pallas_call(
        own_kernel,
        in_specs=[VMEM] * 4,
        out_specs=VMEM,
        out_shape=jax.ShapeDtypeStruct((mix.shape[0], keep.shape[1]), F32),
        compiler_params=params(12),
        cost_estimate=FREE,
        name="own_part",
    )(mix, keep, near, got)


def post_kernel(mix_ref, table_ref, acc_ref, *refs):
    out_ref = refs[-1]
    step = out_ref.shape[1]
    cut = pl.ds(pl.multiple_of(pl.program_id(0) * step, step), step)
    values = jnp.concatenate([ref[:, cut] for ref in refs[:-1]] * 2, axis=0)
    mixed = acc_ref[:, cut] + jnp.dot(mix_ref[...], values, preferred_element_type=F32)
    out_ref[...] = (table_ref[2:3, cut] * mixed).astype(BF16)


def post(mix, table, acc, parts):
    tok_rows, width = acc.shape
    step = min(2048, width)
    return pl.pallas_call(
        post_kernel,
        grid=(width // step,),
        in_specs=[VMEM] * (3 + len(parts)),
        out_specs=pl.BlockSpec((tok_rows, step), lambda i: (0, i)),
        out_shape=jax.ShapeDtypeStruct((tok_rows, width), BF16),
        compiler_params=params(8),
        cost_estimate=FREE,
        name="post",
    )(mix, table, acc, *parts)


def shards(tokens, shift, scale, gate, w_up, w_down, pick, count, combine):
    tok_rows, width = tokens.shape
    _, experts, slots = pick.shape
    devices = lax.axis_size("expert")
    place = lax.axis_index("expert")
    group = devices // experts
    requests = shift.shape[0]
    hidden = w_up.shape[0]
    info = jnp.stack([place // (devices // requests), place // group]).astype(jnp.int32)
    pick = pick[0]
    comb = combine[0]

    far = [d * group for d in turns(experts)[1:]]
    near = []
    bit = group // 2
    while bit:
        near.append(bit)
        bit //= 2

    def swap(x, mask):
        return lax.ppermute(x, "expert", [(i, i ^ mask) for i in range(devices)])

    tokens, shift, scale, gate, w_up, w_down, pick, comb, count = [
        pltpu.with_memory_space_constraint(x, pltpu.HBM)
        for x in (tokens, shift, scale, gate, w_up, w_down, pick, comb, count)
    ]
    farthest, tok, table, picks, weights = first(info, tokens, pick, shift, scale, gate, comb, count)
    own, *others = rest(tok, table, picks)
    mixes = mixer(picks, weights, own, tok_rows)

    flat = [farthest] + others
    blocks = [own] + [swap(x, mask) for x, mask in zip(flat, far)]
    block_up = (hidden // 2, width)
    ups = [load(w_up, (0, 0), block_up, [blocks[1], mixes[0]])]
    blocks[2] = join([blocks[2]], [ups[0]])
    beside = [swap(block, near[0]) for block in blocks]
    early, late = list(range(experts // 2)), list(range(experts // 2, experts))
    parts = []
    sources = []
    for members in (early, late):
        pieces = [join([x for i in members for x in (blocks[i], beside[i])], ups[1:])]
        if members is early:
            ups.append(load(w_up, (hidden // 2, 0), block_up, [pieces[0], ups[0]]))
        height = pieces[0].shape[0]
        for mask in near[1:]:
            block = pieces[0] if len(pieces) == 1 else join(pieces, [])
            pieces = [block, swap(block, mask)]
        cuts = []
        for piece in pieces:
            cuts += [(len(parts), at, at + height) for at in range(0, piece.shape[0], height)]
            parts.append(piece)
        sources.append(cuts)
    sources = [cut for pair in zip(*sources) for cut in pair]

    step = 3 * width // 8
    last = width - 2 * step
    hid, down_a, rows = up(parts, sources, ups[0], w_down, (0, 0), (hidden, step))
    hid_b, down_b = up([rows], None, ups[1], w_down, (0, step), (hidden, step))

    keep_a, send_a, down_c = down([hid, hid_b], [down_a, down_b], w_down, (0, 2 * step), (hidden, last))
    keep_b, send_b = down([hid, hid_b], [down_c], None, None, None)
    pairs = []
    for keep, send in ((keep_a, send_a), (keep_b, send_b)):
        for i, mask in enumerate(reversed(near[1:])):
            if i:
                half = keep.shape[0] // 2
                keep, send = add([(keep, got)], [(0, half), (half, 2 * half)], [F32, BF16])
            if pairs:
                send = join([send], [pairs[0][1]])
            got = swap(send, mask)
        pairs.append((keep, got))
    keeps = [(2 * i * slots, (2 * i + 1) * slots) for i in range(experts)]
    sends = [(high, high + slots) for _, high in keeps]
    summed = add(pairs, sends + keeps, [BF16] * experts + [F32] * experts)
    sends, keeps = summed[:experts], summed[experts:]
    arrived = {i: swap(sends[i], near[0]) for i in list(range(1, experts)) + [0]}
    back = []
    for i, mask in enumerate(far, 1):
        (part,) = add([(keeps[i], arrived[i])], [(0, slots)], [BF16])
        back.append(swap(part, mask))
    acc = own_part(mixes[0], keeps[0], arrived[0], back[0])
    return post(mixes[1], table, acc, back[1:])


def solution(mesh):
    return jax.shard_map(
        shards,
        mesh=mesh,
        in_specs=(
            P(("groups", "expert"), None),
            P("groups", None),
            P("groups", None),
            P("groups", None),
            P("expert", None),
            P("expert", None),
            P(("groups", "expert"), None, None),
            P(("groups", "expert"), None),
            P(("groups", "expert"), None, None),
        ),
        out_specs=P(("groups", "expert"), None),
        check_vma=False,
    )
```

time: 70.3 us -> 62.8 us (0.89)
  waiting for transfers between devices: 23.2 us -> 17 us
  Pallas kernels: 25.5 us -> 23.8 us
  starting transfers between devices: 20.5 us -> 21.6 us
    ppermute x18, waiting for transfers between devices: 23.2 us -> 17 us  [swap(): return lax.ppermute(x, 'expert', [(i, i ^ mask) for i in range(devices)])]
    pallas_call x2, Pallas kernels: 6.95 us -> 5.87 us  [up(): pl.pallas_call(functools.partial(up_kernel, sources=sources, count=len(pa...]
    ppermute x18, starting transfers between devices: 20.5 us -> 21.6 us  [swap(): return lax.ppermute(x, 'expert', [(i, i ^ mask) for i in range(devices)])]
    pallas_call x5 -> x7, Pallas kernels: 11.3 us -> 10.6 us  [the longest x2 5.52 us: down(): pl.pallas_call(functools.partial(down_kernel, count=len(hiddens), blocks=...]
  transfers between devices with their start and end apart: 18 -> 18, of which waited for: 13 -> 11; matrix products, arithmetic and copies ran while one was open for 0% -> 0% of each run, Pallas kernels for 12% -> 16%
where the time goes in v7:
time: 62.8 us; the launch traced here: 62.6 us
  Pallas kernels  23.8 us (38%)
  starting transfers between devices  21.6 us (34%)
  waiting for transfers between devices  17 us (27%)
    ppermute x18, starting transfers between devices, swap(): return lax.ppermute(x, 'expert', [(i, i ^ mask) for i in range(devices)])  21.6 us
    ppermute x18, waiting for transfers between devices, swap(): return lax.ppermute(x, 'expert', [(i, i ^ mask) for i in range(devices)])  17 us
    pallas_call x2, Pallas kernels, load(): pl.pallas_call(functools.partial(load_kernel, at=at), in_specs=[HBM] + [A...  6.95 us
    pallas_call x2, Pallas kernels, up(): pl.pallas_call(functools.partial(up_kernel, sources=sources, count=len(pa...  5.87 us
    pallas_call x2, Pallas kernels, down(): pl.pallas_call(functools.partial(down_kernel, count=len(hiddens), blocks=...  5.52 us
    pallas_call x1, Pallas kernels, first(): pl.pallas_call(first_kernel, in_specs=[SMEM] + [HBM] * 7, out_specs=[VMEM...  2.39 us
    pallas_call x1, Pallas kernels, post(): pl.pallas_call(post_kernel, grid=(width // step,), in_specs=[VMEM] * (3 +...  1.36 us
  transfers between devices with their start and end apart: 18, of which 11 were waited for; matrix products, arithmetic and copies ran while one was open for 0% of the time, Pallas kernels for 16%

profile of v7, /device:TPU:0, one launch (start us, length us, event | category | flops | bytes accessed | tf_op | source)
XLA Modules:
  0.0 62.6 jit_solution(18083498924674037130)
XLA Ops:
  0.1 2.4 %first.1 = (bf16[16,4096]{1,0:T(8,128)(2,1)S(1)}, bf16[128,4096]{1,0:T(8,128)(2,1)S(1)}, f32[3,4096]{1,0:T(4,128)S(1)}, s32[4,16]{1,0:T(4,128)S(1)}, f32[4,16]{1,0:T(4,128)S(1)}) custom-call(s32[2]{0:T(128)S(1)} %pad_add_fusion.info_ref, bf16[128,4096]{1,0:T(8,128)(2,1)} %refs_0_.1, s32[4,16]{1,0:T(4,128)} %bitcast.4, f32[2,4096]{1,0:T(2,128)} %refs_2_.2, ...), custom_call_target="tpu_custom_call" | custom-call | flops 1 | bytes 1 | tf_op jit(solution)/shard_map/first/pallas_call | solution.py:77
  2.5 5.1 %collective-permute-start.1 = (bf16[16,4096]{1,0:T(8,128)(2,1)S(1)}, bf16[16,4096]{1,0:T(8,128)(2,1)S(1)}, u32[]{:S(2)}, u32[]{:S(2)}) collective-permute-start(bf16[16,4096]{1,0:T(8,128)(2,1)S(1)} %get-tuple-element.40), channel_id=1, source_target_pairs={{0,12},{1,13},{2,14},{3,15},{4,8},{5,9},{6,10},{7,11},{8,4},{9,5},... | collective-permute-start | bytes 393224 | tf_op jit(solution)/shard_map/ppermute | solution.py:396
  9.0 1.7 %collective-permute-start = (bf16[16,4096]{1,0:T(8,128)(2,1)S(1)}, bf16[16,4096]{1,0:T(8,128)(2,1)S(1)}, u32[]{:S(2)}, u32[]{:S(2)}) collective-permute-start(bf16[16,4096]{1,0:T(8,128)(2,1)S(1)} %get-tuple-element.37.after_ref.refs_0_), channel_id=1, source_target_pairs={{0,2},{1,3},{2,0},{3,1},{4,6},{5,7},{6,4},{7,5},{8,10},{9,11},{10,... | collective-permute-start | bytes 393224 | tf_op jit(solution)/shard_map/ppermute | solution.py:396
  10.9 1.1 %collective-permute-done.1.refs_2_.refs_0_ = bf16[16,4096]{1,0:T(8,128)(2,1)S(1)} collective-permute-done((bf16[16,4096]{1,0:T(8,128)(2,1)S(1)}, bf16[16,4096]{1,0:T(8,128)(2,1)S(1)}, u32[]{:S(2)}, u32[]{:S(2)}) %collective-permute-start.1) | collective-permute-done | bytes 131104 | tf_op jit(solution)/shard_map/ppermute | solution.py:396
  12.0 1.8 %collective-permute-start.2 = (bf16[16,4096]{1,0:T(8,128)(2,1)S(1)}, bf16[16,4096]{1,0:T(8,128)(2,1)S(1)}, u32[]{:S(2)}, u32[]{:S(2)}) collective-permute-start(bf16[16,4096]{1,0:T(8,128)(2,1)S(1)} %collective-permute-done.1.refs_2_.refs_0_), channel_id=1, source_target_pairs={{0,2},{1,3},{2,0},{3,1},{4,6},{5,7},{6,4},{7,5},{8,10},{9,11},{10,... | collective-permute-start | bytes 393224 | tf_op jit(solution)/shard_map/ppermute | solution.py:396
  13.7 1.3 %collective-permute-done.6.refs_2_ = bf16[16,4096]{1,0:T(8,128)(2,1)S(1)} collective-permute-done((bf16[16,4096]{1,0:T(8,128)(2,1)S(1)}, bf16[16,4096]{1,0:T(8,128)(2,1)S(1)}, u32[]{:S(2)}, u32[]{:S(2)}) %collective-permute-start.6) | collective-permute-done | bytes 131104 | tf_op jit(solution)/shard_map/ppermute | solution.py:396
  15.1 1.6 %collective-permute-start.7 = (bf16[16,4096]{1,0:T(8,128)(2,1)S(1)}, bf16[16,4096]{1,0:T(8,128)(2,1)S(1)}, u32[]{:S(2)}, u32[]{:S(2)}) collective-permute-start(bf16[16,4096]{1,0:T(8,128)(2,1)S(1)} %collective-permute-done.6.refs_2_), channel_id=1, source_target_pairs={{0,2},{1,3},{2,0},{3,1},{4,6},{5,7},{6,4},{7,5},{8,10},{9,11},{10,... | collective-permute-start | bytes 393224 | tf_op jit(solution)/shard_map/ppermute | solution.py:396
  16.7 3.5 %load.2.refs_1_.refs_4_ = bf16[1024,4096]{1,0:T(8,128)(2,1)S(1)} custom-call(bf16[2048,4096]{1,0:T(8,128)(2,1)} %w_hbm.3, bf16[16,4096]{1,0:T(8,128)(2,1)S(1)} %collective-permute-done.1.refs_2_.refs_0_, bf16[128,64]{1,0:T(8,128)(2,1)S(1)} %get-tuple-element.39.refs_1_.mix_ref), custom_call_target="tpu_custom_call" | custom-call | flops 1 | bytes 1 | tf_op jit(solution)/shard_map/load/pallas_call | solution.py:173
  20.8 3.5 %load.3.refs_4_.refs_1_ = bf16[1024,4096]{1,0:T(8,128)(2,1)S(1)} custom-call(bf16[2048,4096]{1,0:T(8,128)(2,1)} %w_hbm.3, bf16[64,4096]{1,0:T(8,128)(2,1)S(1)} %join.4.refs_0_, bf16[1024,4096]{1,0:T(8,128)(2,1)S(1)} %load.2.refs_1_.refs_4_), custom_call_target="tpu_custom_call" | custom-call | flops 1 | bytes 1 | tf_op jit(solution)/shard_map/load/pallas_call | solution.py:173
  24.3 0.9 %collective-permute-done.5.refs_1_ = bf16[16,4096]{1,0:T(8,128)(2,1)S(1)} collective-permute-done((bf16[16,4096]{1,0:T(8,128)(2,1)S(1)}, bf16[16,4096]{1,0:T(8,128)(2,1)S(1)}, u32[]{:S(2)}, u32[]{:S(2)}) %collective-permute-start.5) | collective-permute-done | bytes 131104 | tf_op jit(solution)/shard_map/ppermute | solution.py:396
  25.4 1.9 %collective-permute-done.8.refs_3_ = bf16[64,4096]{1,0:T(8,128)(2,1)S(1)} collective-permute-done((bf16[64,4096]{1,0:T(8,128)(2,1)S(1)}, bf16[64,4096]{1,0:T(8,128)(2,1)S(1)}, u32[]{:S(2)}, u32[]{:S(2)}) %collective-permute-start.8) | collective-permute-done | bytes 524320 | tf_op jit(solution)/shard_map/ppermute | solution.py:396
  27.2 3.0 %up.2 = (bf16[256,1024]{1,0:T(8,128)(2,1)S(1)}, bf16[2048,1536]{1,0:T(8,128)(2,1)S(1)}, bf16[256,4096]{1,0:T(8,128)(2,1)S(1)}) custom-call(bf16[64,4096]{1,0:T(8,128)(2,1)S(1)} %join.4.refs_0_, bf16[64,4096]{1,0:T(8,128)(2,1)S(1)} %collective-permute-done.3.refs_1_, bf16[64,4096]{1,0:T(8,128)(2,1)S(1)} %join.6.refs_2_, ...), custom_call_target="tpu_custom_call" | custom-call | flops 1 | bytes 1 | tf_op jit(solution)/shard_map/up/pallas_call | solution.py:241
  30.2 2.9 %up.3 = (bf16[256,1024]{1,0:T(8,128)(2,1)S(1)}, bf16[2048,1536]{1,0:T(8,128)(2,1)S(1)}) custom-call(bf16[256,4096]{1,0:T(8,128)(2,1)S(1)} %get-tuple-element.44.refs_0_, bf16[1024,4096]{1,0:T(8,128)(2,1)S(1)} %load.3.refs_4_.refs_1_, bf16[2048,4096]{1,0:T(8,128)(2,1)} %refs_4_.3), custom_call_target="tpu_custom_call" | custom-call | flops 1 | bytes 1 | tf_op jit(solution)/shard_map/up/pallas_call | solution.py:241
  33.1 4.1 %down.2 = (f32[128,3072]{1,0:T(8,128)S(1)}, bf16[128,3072]{1,0:T(8,128)(2,1)S(1)}, bf16[2048,1024]{1,0:T(8,128)(2,1)S(1)}) custom-call(bf16[256,1024]{1,0:T(8,128)(2,1)S(1)} %get-tuple-element.43.refs_0_, bf16[256,1024]{1,0:T(8,128)(2,1)S(1)} %get-tuple-element.45.refs_1_, bf16[2048,1536]{1,0:T(8,128)(2,1)S(1)} %get-tuple-element.46.refs_2_, ...), custom_call_target="tpu_custom_call" | custom-call | flops 1 | bytes 1 | tf_op jit(solution)/shard_map/down/pallas_call | solution.py:293
  37.4 1.4 %down.3 = (f32[128,1024]{1,0:T(8,128)S(1)}, bf16[128,1024]{1,0:T(8,128)(2,1)S(1)}) custom-call(bf16[256,1024]{1,0:T(8,128)(2,1)S(1)} %get-tuple-element.43.refs_0_, bf16[256,1024]{1,0:T(8,128)(2,1)S(1)} %get-tuple-element.45.refs_1_, bf16[2048,1024]{1,0:T(8,128)(2,1)S(1)} %get-tuple-element.50.refs_2_), custom_call_target="tpu_custom_call" | custom-call | flops 1 | bytes 1 | tf_op jit(solution)/shard_map/down/pallas_call | solution.py:293
  39.8 1.4 %collective-permute-done.10.refs_3_ = bf16[128,1024]{1,0:T(8,128)(2,1)S(1)} collective-permute-done((bf16[128,1024]{1,0:T(8,128)(2,1)S(1)}, bf16[128,1024]{1,0:T(8,128)(2,1)S(1)}, u32[]{:S(2)}, u32[]{:S(2)}) %collective-permute-start.10) | collective-permute-done | bytes 262176 | tf_op jit(solution)/shard_map/ppermute | solution.py:396
  42.3 1.2 %collective-permute-start.14 = (bf16[16,4096]{1,0:T(8,128)(2,1)S(1)}, bf16[16,4096]{1,0:T(8,128)(2,1)S(1)}, u32[]{:S(2)}, u32[]{:S(2)}) collective-permute-start(bf16[16,4096]{1,0:T(8,128)(2,1)S(1)} %get-tuple-element.58), channel_id=1, source_target_pairs={{0,2},{1,3},{2,0},{3,1},{4,6},{5,7},{6,4},{7,5},{8,10},{9,11},{10,... | collective-permute-start | bytes 393224 | tf_op jit(solution)/shard_map/ppermute | solution.py:396
  44.3 1.2 %collective-permute-start.11 = (bf16[16,4096]{1,0:T(8,128)(2,1)S(1)}, bf16[16,4096]{1,0:T(8,128)(2,1)S(1)}, u32[]{:S(2)}, u32[]{:S(2)}) collective-permute-start(bf16[16,4096]{1,0:T(8,128)(2,1)S(1)} %get-tuple-element.54), channel_id=1, source_target_pairs={{0,2},{1,3},{2,0},{3,1},{4,6},{5,7},{6,4},{7,5},{8,10},{9,11},{10,... | collective-permute-start | bytes 393224 | tf_op jit(solution)/shard_map/ppermute | solution.py:396
  45.5 2.3 %collective-permute-done.12.refs_1_ = bf16[16,4096]{1,0:T(8,128)(2,1)S(1)} collective-permute-done((bf16[16,4096]{1,0:T(8,128)(2,1)S(1)}, bf16[16,4096]{1,0:T(8,128)(2,1)S(1)}, u32[]{:S(2)}, u32[]{:S(2)}) %collective-permute-start.12) | collective-permute-done | bytes 131104 | tf_op jit(solution)/shard_map/ppermute | solution.py:396
  47.8 3.2 %collective-permute-start.13 = (bf16[16,4096]{1,0:T(8,128)(2,1)S(1)}, bf16[16,4096]{1,0:T(8,128)(2,1)S(1)}, u32[]{:S(2)}, u32[]{:S(2)}) collective-permute-start(bf16[16,4096]{1,0:T(8,128)(2,1)S(1)} %add.9), channel_id=1, source_target_pairs={{0,12},{1,13},{2,14},{3,15},{4,8},{5,9},{6,10},{7,11},{8,4},{9,5},... | collective-permute-start | bytes 393224 | tf_op jit(solution)/shard_map/ppermute | solution.py:396
  51.7 1.7 %collective-permute-done.16.refs_1_ = bf16[16,4096]{1,0:T(8,128)(2,1)S(1)} collective-permute-done((bf16[16,4096]{1,0:T(8,128)(2,1)S(1)}, bf16[16,4096]{1,0:T(8,128)(2,1)S(1)}, u32[]{:S(2)}, u32[]{:S(2)}) %collective-permute-start.16) | collective-permute-done | bytes 131104 | tf_op jit(solution)/shard_map/ppermute | solution.py:396
  53.4 1.7 %collective-permute-start.17 = (bf16[16,4096]{1,0:T(8,128)(2,1)S(1)}, bf16[16,4096]{1,0:T(8,128)(2,1)S(1)}, u32[]{:S(2)}, u32[]{:S(2)}) collective-permute-start(bf16[16,4096]{1,0:T(8,128)(2,1)S(1)} %add.11), channel_id=1, source_target_pairs={{0,4},{1,5},{2,6},{3,7},{4,0},{5,1},{6,2},{7,3},{8,12},{9,13},{10,... | collective-permute-start | bytes 393224 | tf_op jit(solution)/shard_map/ppermute | solution.py:396
  56.1 5.1 %collective-permute-done.15.refs_0_ = bf16[16,4096]{1,0:T(8,128)(2,1)S(1)} collective-permute-done((bf16[16,4096]{1,0:T(8,128)(2,1)S(1)}, bf16[16,4096]{1,0:T(8,128)(2,1)S(1)}, u32[]{:S(2)}, u32[]{:S(2)}) %collective-permute-start.15) | collective-permute-done | bytes 131104 | tf_op jit(solution)/shard_map/ppermute | solution.py:396
  61.3 1.4 %post.1 = bf16[128,4096]{1,0:T(8,128)(2,1)} custom-call(bf16[128,64]{1,0:T(8,128)(2,1)S(1)} %get-tuple-element.38.mix_ref, f32[3,4096]{1,0:T(4,128)S(1)} %get-tuple-element.36.table_ref, f32[128,4096]{1,0:T(8,128)S(1)} %own_part.1.acc_ref, bf16[16,4096]{1,0:T(8,128)(2,1)S(1)} %collective-permute-done.15.refs_0_, ...), custom_call_target="tpu_custom_call" | custom-call | flops 1 | bytes 1 | tf_op jit(solution)/shard_map/post/pallas_call | solution.py:364
  (32 shorter events, 7.1 us)
Async XLA Ops:
  2.5 9.5 %collective-permute-start.1 = (bf16[16,4096]{1,0:T(8,128)(2,1)S(1)}, bf16[16,4096]{1,0:T(8,128)(2,1)S(1)}, u32[]{:S(2)}, u32[]{:S(2)}) collective-permute-start(bf16[16,4096]{1,0:T(8,128)(2,1)S(1)} %get-tuple-element.40), channel_id=1, source_target_pairs={{0,12},{1,13},{2,14},{3,15},{4,8},{5,9},{6,10},{7,11},{8,4},{9,5},... | collective-permute-start | bytes 393224 | tf_op jit(solution)/shard_map/ppermute | solution.py:396
  8.4 6.7 %collective-permute-start.6 = (bf16[16,4096]{1,0:T(8,128)(2,1)S(1)}, bf16[16,4096]{1,0:T(8,128)(2,1)S(1)}, u32[]{:S(2)}, u32[]{:S(2)}) collective-permute-start(bf16[16,4096]{1,0:T(8,128)(2,1)S(1)} %get-tuple-element.42), channel_id=1, source_target_pairs={{0,4},{1,5},{2,6},{3,7},{4,0},{5,1},{6,2},{7,3},{8,12},{9,13},{10,... | collective-permute-start | bytes 393224 | tf_op jit(solution)/shard_map/ppermute | solution.py:396
  8.4 11.7 %collective-permute-start.4 = (bf16[16,4096]{1,0:T(8,128)(2,1)S(1)}, bf16[16,4096]{1,0:T(8,128)(2,1)S(1)}, u32[]{:S(2)}, u32[]{:S(2)}) collective-permute-start(bf16[16,4096]{1,0:T(8,128)(2,1)S(1)} %get-tuple-element.41), channel_id=1, source_target_pairs={{0,8},{1,9},{2,10},{3,11},{4,12},{5,13},{6,14},{7,15},{8,0},{9,1},... | collective-permute-start | bytes 393224 | tf_op jit(solution)/shard_map/ppermute | solution.py:396
  9.0 11.7 %collective-permute-start = (bf16[16,4096]{1,0:T(8,128)(2,1)S(1)}, bf16[16,4096]{1,0:T(8,128)(2,1)S(1)}, u32[]{:S(2)}, u32[]{:S(2)}) collective-permute-start(bf16[16,4096]{1,0:T(8,128)(2,1)S(1)} %get-tuple-element.37.after_ref.refs_0_), channel_id=1, source_target_pairs={{0,2},{1,3},{2,0},{3,1},{4,6},{5,7},{6,4},{7,5},{8,10},{9,11},{10,... | collective-permute-start | bytes 393224 | tf_op jit(solution)/shard_map/ppermute | solution.py:396
  12.0 8.7 %collective-permute-start.2 = (bf16[16,4096]{1,0:T(8,128)(2,1)S(1)}, bf16[16,4096]{1,0:T(8,128)(2,1)S(1)}, u32[]{:S(2)}, u32[]{:S(2)}) collective-permute-start(bf16[16,4096]{1,0:T(8,128)(2,1)S(1)} %collective-permute-done.1.refs_2_.refs_0_), channel_id=1, source_target_pairs={{0,2},{1,3},{2,0},{3,1},{4,6},{5,7},{6,4},{7,5},{8,10},{9,11},{10,... | collective-permute-start | bytes 393224 | tf_op jit(solution)/shard_map/ppermute | solution.py:396
  15.1 9.2 %collective-permute-start.7 = (bf16[16,4096]{1,0:T(8,128)(2,1)S(1)}, bf16[16,4096]{1,0:T(8,128)(2,1)S(1)}, u32[]{:S(2)}, u32[]{:S(2)}) collective-permute-start(bf16[16,4096]{1,0:T(8,128)(2,1)S(1)} %collective-permute-done.6.refs_2_), channel_id=1, source_target_pairs={{0,2},{1,3},{2,0},{3,1},{4,6},{5,7},{6,4},{7,5},{8,10},{9,11},{10,... | collective-permute-start | bytes 393224 | tf_op jit(solution)/shard_map/ppermute | solution.py:396
  20.2 5.0 %collective-permute-start.5 = (bf16[16,4096]{1,0:T(8,128)(2,1)S(1)}, bf16[16,4096]{1,0:T(8,128)(2,1)S(1)}, u32[]{:S(2)}, u32[]{:S(2)}) collective-permute-start(bf16[16,4096]{1,0:T(8,128)(2,1)S(1)} %join.5.refs_0_), channel_id=1, source_target_pairs={{0,2},{1,3},{2,0},{3,1},{4,6},{5,7},{6,4},{7,5},{8,10},{9,11},{10,... | collective-permute-start | bytes 393224 | tf_op jit(solution)/shard_map/ppermute | solution.py:396
  20.7 4.6 %collective-permute-start.3 = (bf16[64,4096]{1,0:T(8,128)(2,1)S(1)}, bf16[64,4096]{1,0:T(8,128)(2,1)S(1)}, u32[]{:S(2)}, u32[]{:S(2)}) collective-permute-start(bf16[64,4096]{1,0:T(8,128)(2,1)S(1)} %join.4.refs_0_), channel_id=1, source_target_pairs={{0,1},{1,0},{2,3},{3,2},{4,5},{5,4},{6,7},{7,6},{8,9},{9,8},{10,11... | collective-permute-start | bytes 1572872 | tf_op jit(solution)/shard_map/ppermute | solution.py:396
  25.3 2.0 %collective-permute-start.8 = (bf16[64,4096]{1,0:T(8,128)(2,1)S(1)}, bf16[64,4096]{1,0:T(8,128)(2,1)S(1)}, u32[]{:S(2)}, u32[]{:S(2)}) collective-permute-start(bf16[64,4096]{1,0:T(8,128)(2,1)S(1)} %join.6.refs_2_), channel_id=1, source_target_pairs={{0,1},{1,0},{2,3},{3,2},{4,5},{5,4},{6,7},{7,6},{8,9},{9,8},{10,11... | collective-permute-start | bytes 1572872 | tf_op jit(solution)/shard_map/ppermute | solution.py:396
  37.2 2.4 %collective-permute-start.9 = (bf16[128,3072]{1,0:T(8,128)(2,1)S(1)}, bf16[128,3072]{1,0:T(8,128)(2,1)S(1)}, u32[]{:S(2)}, u32[]{:S(2)}) collective-permute-start(bf16[128,3072]{1,0:T(8,128)(2,1)S(1)} %get-tuple-element.49), channel_id=1, source_target_pairs={{0,1},{1,0},{2,3},{3,2},{4,5},{5,4},{6,7},{7,6},{8,9},{9,8},{10,11... | collective-permute-start | bytes 2359304 | tf_op jit(solution)/shard_map/ppermute | solution.py:396
  39.6 1.6 %collective-permute-start.10 = (bf16[128,1024]{1,0:T(8,128)(2,1)S(1)}, bf16[128,1024]{1,0:T(8,128)(2,1)S(1)}, u32[]{:S(2)}, u32[]{:S(2)}) collective-permute-start(bf16[128,1024]{1,0:T(8,128)(2,1)S(1)} %join.7), channel_id=1, source_target_pairs={{0,1},{1,0},{2,3},{3,2},{4,5},{5,4},{6,7},{7,6},{8,9},{9,8},{10,11... | collective-permute-start | bytes 786440 | tf_op jit(solution)/shard_map/ppermute | solution.py:396
  41.4 6.4 %collective-permute-start.12 = (bf16[16,4096]{1,0:T(8,128)(2,1)S(1)}, bf16[16,4096]{1,0:T(8,128)(2,1)S(1)}, u32[]{:S(2)}, u32[]{:S(2)}) collective-permute-start(bf16[16,4096]{1,0:T(8,128)(2,1)S(1)} %get-tuple-element.56), channel_id=1, source_target_pairs={{0,2},{1,3},{2,0},{3,1},{4,6},{5,7},{6,4},{7,5},{8,10},{9,11},{10,... | collective-permute-start | bytes 393224 | tf_op jit(solution)/shard_map/ppermute | solution.py:396
  42.3 8.7 %collective-permute-start.14 = (bf16[16,4096]{1,0:T(8,128)(2,1)S(1)}, bf16[16,4096]{1,0:T(8,128)(2,1)S(1)}, u32[]{:S(2)}, u32[]{:S(2)}) collective-permute-start(bf16[16,4096]{1,0:T(8,128)(2,1)S(1)} %get-tuple-element.58), channel_id=1, source_target_pairs={{0,2},{1,3},{2,0},{3,1},{4,6},{5,7},{6,4},{7,5},{8,10},{9,11},{10,... | collective-permute-start | bytes 393224 | tf_op jit(solution)/shard_map/ppermute | solution.py:396
  43.5 9.9 %collective-permute-start.16 = (bf16[16,4096]{1,0:T(8,128)(2,1)S(1)}, bf16[16,4096]{1,0:T(8,128)(2,1)S(1)}, u32[]{:S(2)}, u32[]{:S(2)}) collective-permute-start(bf16[16,4096]{1,0:T(8,128)(2,1)S(1)} %get-tuple-element.60), channel_id=1, source_target_pairs={{0,2},{1,3},{2,0},{3,1},{4,6},{5,7},{6,4},{7,5},{8,10},{9,11},{10,... | collective-permute-start | bytes 393224 | tf_op jit(solution)/shard_map/ppermute | solution.py:396
  44.3 11.1 %collective-permute-start.11 = (bf16[16,4096]{1,0:T(8,128)(2,1)S(1)}, bf16[16,4096]{1,0:T(8,128)(2,1)S(1)}, u32[]{:S(2)}, u32[]{:S(2)}) collective-permute-start(bf16[16,4096]{1,0:T(8,128)(2,1)S(1)} %get-tuple-element.54), channel_id=1, source_target_pairs={{0,2},{1,3},{2,0},{3,1},{4,6},{5,7},{6,4},{7,5},{8,10},{9,11},{10,... | collective-permute-start | bytes 393224 | tf_op jit(solution)/shard_map/ppermute | solution.py:396
  47.8 7.9 %collective-permute-start.13 = (bf16[16,4096]{1,0:T(8,128)(2,1)S(1)}, bf16[16,4096]{1,0:T(8,128)(2,1)S(1)}, u32[]{:S(2)}, u32[]{:S(2)}) collective-permute-start(bf16[16,4096]{1,0:T(8,128)(2,1)S(1)} %add.9), channel_id=1, source_target_pairs={{0,12},{1,13},{2,14},{3,15},{4,8},{5,9},{6,10},{7,11},{8,4},{9,5},... | collective-permute-start | bytes 393224 | tf_op jit(solution)/shard_map/ppermute | solution.py:396
  51.0 10.2 %collective-permute-start.15 = (bf16[16,4096]{1,0:T(8,128)(2,1)S(1)}, bf16[16,4096]{1,0:T(8,128)(2,1)S(1)}, u32[]{:S(2)}, u32[]{:S(2)}) collective-permute-start(bf16[16,4096]{1,0:T(8,128)(2,1)S(1)} %add.10), channel_id=1, source_target_pairs={{0,8},{1,9},{2,10},{3,11},{4,12},{5,13},{6,14},{7,15},{8,0},{9,1},... | collective-permute-start | bytes 393224 | tf_op jit(solution)/shard_map/ppermute | solution.py:396
  53.4 7.8 %collective-permute-start.17 = (bf16[16,4096]{1,0:T(8,128)(2,1)S(1)}, bf16[16,4096]{1,0:T(8,128)(2,1)S(1)}, u32[]{:S(2)}, u32[]{:S(2)}) collective-permute-start(bf16[16,4096]{1,0:T(8,128)(2,1)S(1)} %add.11), channel_id=1, source_target_pairs={{0,4},{1,5},{2,6},{3,7},{4,0},{5,1},{6,2},{7,3},{8,12},{9,13},{10,... | collective-permute-start | bytes 393224 | tf_op jit(solution)/shard_map/ppermute | solution.py:396

commit v8 on v7

v8 whole, which is shorter than its diff:
```python
import functools

import jax
import jax.numpy as jnp
from jax import lax
from jax.experimental import pallas as pl
from jax.experimental.pallas import tpu as pltpu
from jax.sharding import PartitionSpec as P

PIECES = 8
MIB = 1024 * 1024
F32 = jnp.float32
BF16 = jnp.bfloat16

SMEM = pl.BlockSpec(memory_space=pltpu.SMEM)
VMEM = pl.BlockSpec(memory_space=pltpu.VMEM)
HBM = pl.BlockSpec(memory_space=pltpu.HBM)
ANY = pl.BlockSpec(memory_space=pl.ANY)


FREE = pl.CostEstimate(flops=1, bytes_accessed=1, transcendentals=0)


def params(mib):
    return pltpu.CompilerParams(vmem_limit_bytes=mib * MIB)


def stream(w_hbm, out_ref, sems, at):
    rows, columns = out_ref.shape
    pieces = sems.shape[0]
    part = rows // pieces
    return [
        pltpu.make_async_copy(
            w_hbm.at[pl.ds(at[0] + p * part, part), pl.ds(at[1], columns)],
            out_ref.at[pl.ds(p * part, part), :],
            sems.at[p],
        )
        for p in range(pieces)
    ]


def turns(experts):
    return [0] + list(range(experts - 1, 0, -1))


def hot_rows(picks, tok_rows):
    return lax.broadcasted_iota(jnp.int32, (tok_rows, picks.shape[1]), 0) == picks


def modulate(picks, tok_ref, table_ref):
    hot = hot_rows(picks, tok_ref.shape[0]).astype(F32).astype(BF16)
    values = lax.dot_general(hot, tok_ref[...], (((0,), (0,)), ((), ())), preferred_element_type=F32)
    center = values - jnp.mean(values, axis=1, keepdims=True)
    spread = jnp.mean(center * center, axis=1, keepdims=True)
    normed = center * (1.0 / jnp.sqrt(spread + 1e-06))
    return (normed * table_ref[0:1, :] + table_ref[1:2, :]).astype(BF16)


def first_kernel(info_ref, w_hbm, *refs):
    sources = refs[:7]
    far_ref, tok_ref, table_ref, picks_ref, weights_ref, w_ref = refs[7:13]
    pick_ref, comb_ref, count_ref, shift_ref, scale_ref, gate_ref, sems, w_sems = refs[13:]
    targets = (tok_ref, pick_ref, shift_ref, scale_ref, gate_ref, comb_ref, count_ref)
    copies = [
        pltpu.make_async_copy(src, dst, sems.at[i])
        for i, (src, dst) in enumerate(zip(sources, targets))
    ]
    loads = stream(w_hbm, w_ref, w_sems, (0, 0))
    for copy in copies + loads:
        copy.start()
    for copy in copies:
        copy.wait()
    experts, slots = pick_ref.shape
    which = pl.ds(info_ref[0], 1)
    table_ref[0:1, :] = 1.0 + scale_ref[which, :]
    table_ref[1:2, :] = shift_ref[which, :]
    table_ref[2:3, :] = gate_ref[which, :]
    lanes = lax.broadcasted_iota(jnp.int32, (1, slots), 1)
    for i, d in enumerate(turns(experts)):
        e = info_ref[1] ^ d
        picks_ref[i:i + 1, :] = pick_ref[pl.ds(e, 1), :]
        weights_ref[i:i + 1, :] = jnp.where(lanes < count_ref[0, e], comb_ref[pl.ds(e, 1), :], 0.0)
    far_ref[...] = modulate(picks_ref[1:2, :], tok_ref, table_ref)
    for copy in loads:
        copy.wait()


def first(info, w, shape, tokens, pick, shift, scale, gate, comb, count):
    experts, slots = pick.shape
    width = tokens.shape[1]
    return pl.pallas_call(
        first_kernel,
        in_specs=[SMEM] + [HBM] * 8,
        out_specs=[VMEM] * 6,
        out_shape=[
            jax.ShapeDtypeStruct((slots, width), BF16),
            jax.ShapeDtypeStruct(tokens.shape, BF16),
            jax.ShapeDtypeStruct((3, width), F32),
            jax.ShapeDtypeStruct(pick.shape, jnp.int32),
            jax.ShapeDtypeStruct(comb.shape, F32),
            pltpu.VMEM(shape, BF16),
        ],
        scratch_shapes=[
            pltpu.VMEM(pick.shape, jnp.int32),
            pltpu.VMEM(comb.shape, F32),
            pltpu.SMEM(count.shape, jnp.int32),
            pltpu.VMEM(shift.shape, F32),
            pltpu.VMEM(scale.shape, F32),
            pltpu.VMEM(gate.shape, F32),
            pltpu.SemaphoreType.DMA((7,)),
            pltpu.SemaphoreType.DMA((PIECES,)),
        ],
        compiler_params=params(8),
        cost_estimate=FREE,
        name="first",
    )(info, w, tokens, pick, shift, scale, gate, comb, count)


def rest_kernel(tok_ref, table_ref, picks_ref, *outs):
    experts, slots = picks_ref.shape
    order = [0] + list(range(2, experts))
    picks = jnp.concatenate([picks_ref[i:i + 1, :] for i in order], axis=1)
    rows = modulate(picks, tok_ref, table_ref)
    for i, out in enumerate(outs):
        out[...] = rows[i * slots:(i + 1) * slots]


def rest(tok, table, picks):
    experts, slots = picks.shape
    return pl.pallas_call(
        rest_kernel,
        in_specs=[VMEM] * 3,
        out_specs=[VMEM] * (experts - 1),
        out_shape=[jax.ShapeDtypeStruct((slots, tok.shape[1]), BF16)] * (experts - 1),
        compiler_params=params(8),
        cost_estimate=FREE,
        name="rest",
    )(tok, table, picks)


def mixer_kernel(picks_ref, weights_ref, after_ref, *outs):
    for i, out in enumerate(outs):
        each = picks_ref.shape[0] // len(outs)
        rows = range(i * each, (i + 1) * each)
        picks = jnp.concatenate([picks_ref[r:r + 1, :] for r in rows], axis=1)
        weights = jnp.concatenate([weights_ref[r:r + 1, :] for r in rows], axis=1)
        mix = jnp.where(hot_rows(picks, out.shape[0]), weights, 0.0)
        high = mix.astype(BF16).astype(F32)
        out[...] = jnp.concatenate([high, mix - high], axis=1).astype(BF16)


def mixer(picks, weights, after, tok_rows):
    experts, slots = picks.shape
    return pl.pallas_call(
        mixer_kernel,
        in_specs=[VMEM] * 2 + [ANY],
        out_specs=[VMEM] * 2,
        out_shape=[jax.ShapeDtypeStruct((tok_rows, experts * slots), BF16)] * 2,
        compiler_params=params(4),
        cost_estimate=FREE,
        name="mixer",
    )(picks, weights, after)


def load_kernel(w_hbm, *refs, at):
    out_ref, sems = refs[-2:]
    copies = stream(w_hbm, out_ref, sems, at)
    for copy in copies:
        copy.start()
    for copy in copies:
        copy.wait()


def load(w, at, shape, after):
    return pl.pallas_call(
        functools.partial(load_kernel, at=at),
        in_specs=[HBM] + [ANY] * len(after),
        out_specs=VMEM,
        out_shape=pltpu.VMEM(shape, w.dtype),
        scratch_shapes=[pltpu.SemaphoreType.DMA((PIECES,))],
        compiler_params=params(2),
        cost_estimate=FREE,
        name="load",
    )(w, *after)


def join_kernel(*refs, count):
    out_ref = refs[-1]
    at = 0
    for ref in refs[:count]:
        out_ref[at:at + ref.shape[0], :] = ref[...]
        at += ref.shape[0]


def join(parts, after):
    return pl.pallas_call(
        functools.partial(join_kernel, count=len(parts)),
        in_specs=[VMEM] * len(parts) + [ANY] * len(after),
        out_specs=VMEM,
        out_shape=jax.ShapeDtypeStruct((sum(p.shape[0] for p in parts), parts[0].shape[1]), BF16),
        compiler_params=params(2),
        cost_estimate=FREE,
        name="join",
    )(*parts, *after)


def up_kernel(*refs, sources, count, blocks, at):
    weights = refs[count:count + blocks]
    next_hbm = refs[count + blocks]
    if sources is None:
        rows_ref = refs[0]
        out_ref, next_ref, sems = refs[-3:]
    else:
        out_ref, next_ref, rows_ref, sems = refs[-4:]
    copies = stream(next_hbm, next_ref, sems, at)
    for copy in copies:
        copy.start()
    if sources is not None:
        to = 0
        for source, low, high in sources:
            rows_ref[to:to + high - low, :] = refs[source][low:high, :]
            to += high - low
    base = 0
    for w_ref in weights:
        hidden = w_ref.shape[0]
        tile = min(512, hidden)

        @pl.loop(0, hidden // tile)
        def _(i):
            lifted = lax.dot_general(
                rows_ref[...],
                w_ref[pl.ds(pl.multiple_of(i * tile, tile), tile), :],
                (((1,), (1,)), ((), ())),
                preferred_element_type=F32,
            )
            to = pl.ds(pl.multiple_of(base + i * tile, tile), tile)
            out_ref[:, to] = jax.nn.gelu(lifted, approximate=True).astype(BF16)

        base += hidden
    for copy in copies:
        copy.wait()


def up(parts, sources, weights, following, at, shape):
    hidden = sum(w.shape[0] for w in weights)
    width = weights[0].shape[1]
    rows = parts[0].shape[0] if sources is None else sum(high - low for _, low, high in sources)
    out_shape = [jax.ShapeDtypeStruct((rows, hidden), BF16), pltpu.VMEM(shape, BF16)]
    if sources is not None:
        out_shape.append(jax.ShapeDtypeStruct((rows, width), BF16))
    return pl.pallas_call(
        functools.partial(
            up_kernel, sources=sources, count=len(parts), blocks=len(weights), at=at
        ),
        in_specs=[VMEM] * (len(parts) + len(weights)) + [HBM],
        out_specs=[VMEM] * len(out_shape),
        out_shape=out_shape,
        scratch_shapes=[pltpu.SemaphoreType.DMA((PIECES,))],
        compiler_params=params(12),
        cost_estimate=FREE,
        name="up",
    )(*parts, *weights, following)


def down_kernel(*refs, count, at):
    hiddens, weights = refs[:count], refs[count:2 * count]
    if at is None:
        keep_ref, send_ref = refs[2 * count:]
        copies = []
    else:
        next_hbm, keep_ref, send_ref = refs[2 * count:2 * count + 3]
        nexts, sems = refs[2 * count + 3:-1], refs[-1]
        copies = []
        for i, ref in enumerate(nexts):
            copies += stream(next_hbm, ref, sems.at[pl.ds(i * PIECES, PIECES)], at[i])
    for copy in copies:
        copy.start()
    half, step = keep_ref.shape
    tile = min(1024, step)

    @pl.loop(0, step // tile)
    def _(i):
        cut = pl.ds(pl.multiple_of(i * tile, tile), tile)
        out = None
        for h_ref, w_ref in zip(hiddens, weights):
            part = jnp.dot(h_ref[...], w_ref[:, cut], preferred_element_type=F32)
            out = part if out is None else out + part
        keep_ref[:, cut] = out[:half]
        send_ref[:, cut] = out[half:].astype(BF16)

    for copy in copies:
        copy.wait()


def down(hiddens, weights, following, at, shapes):
    half = hiddens[0].shape[0] // 2
    step = weights[0].shape[1]
    more = following is not None
    return pl.pallas_call(
        functools.partial(down_kernel, count=len(hiddens), at=at),
        in_specs=[VMEM] * (2 * len(hiddens)) + [HBM] * more,
        out_specs=[VMEM] * (2 + len(shapes)),
        out_shape=[
            jax.ShapeDtypeStruct((half, step), F32),
            jax.ShapeDtypeStruct((half, step), BF16),
        ]
        + [pltpu.VMEM(shape, BF16) for shape in shapes],
        scratch_shapes=[pltpu.SemaphoreType.DMA((len(shapes) * PIECES,))] * more,
        compiler_params=params(12),
        cost_estimate=FREE,
        name="down",
    )(*hiddens, *weights, *([following] if more else []))


def add_kernel(*refs, count, cuts, carried):
    at = 0
    outs = refs[2 * count + carried:]
    for i in range(count):
        keep_ref, got_ref = refs[2 * i:2 * i + 2]
        step = keep_ref.shape[1]
        for ref, (low, high) in zip(outs, cuts):
            total = keep_ref[low:high] + got_ref[low:high].astype(F32)
            ref[:, at:at + step] = total.astype(ref.dtype)
        at += step
    for i in range(carried):
        outs[len(cuts) + i][...] = refs[2 * count + i][...]


def add(pairs, cuts, kinds, carry=()):
    width = sum(keep.shape[1] for keep, _ in pairs)
    args = [x for pair in pairs for x in pair] + list(carry)
    return pl.pallas_call(
        functools.partial(add_kernel, count=len(pairs), cuts=cuts, carried=len(carry)),
        in_specs=[VMEM] * len(args),
        out_specs=[VMEM] * (len(cuts) + len(carry)),
        out_shape=[jax.ShapeDtypeStruct((high - low, width), k) for (low, high), k in zip(cuts, kinds)]
        + [jax.ShapeDtypeStruct(x.shape, x.dtype) for x in carry],
        compiler_params=params(8),
        cost_estimate=FREE,
        name="add",
    )(*args)


def own_kernel(mix_ref, keep_ref, near_ref, got_ref, acc_ref):
    own = (keep_ref[...] + near_ref[near_ref.shape[0] - keep_ref.shape[0]:].astype(F32)).astype(BF16)
    values = jnp.concatenate([own, got_ref[...]] * 2, axis=0)
    acc_ref[...] = jnp.dot(mix_ref[...], values, preferred_element_type=F32)


def own_part(mix, keep, near, got):
    return pl.pallas_call(
        own_kernel,
        in_specs=[VMEM] * 4,
        out_specs=VMEM,
        out_shape=jax.ShapeDtypeStruct((mix.shape[0], keep.shape[1]), F32),
        compiler_params=params(12),
        cost_estimate=FREE,
        name="own_part",
    )(mix, keep, near, got)


def post_kernel(mix_ref, table_ref, acc_ref, *refs):
    out_ref = refs[-1]
    step = out_ref.shape[1]
    cut = pl.ds(pl.multiple_of(pl.program_id(0) * step, step), step)
    values = jnp.concatenate([ref[:, cut] for ref in refs[:-1]] * 2, axis=0)
    mixed = acc_ref[:, cut] + jnp.dot(mix_ref[...], values, preferred_element_type=F32)
    out_ref[...] = (table_ref[2:3, cut] * mixed).astype(BF16)


def post(mix, table, acc, parts):
    tok_rows, width = acc.shape
    step = min(2048, width)
    return pl.pallas_call(
        post_kernel,
        grid=(width // step,),
        in_specs=[VMEM] * (3 + len(parts)),
        out_specs=pl.BlockSpec((tok_rows, step), lambda i: (0, i)),
        out_shape=jax.ShapeDtypeStruct((tok_rows, width), BF16),
        compiler_params=params(8),
        cost_estimate=FREE,
        name="post",
    )(mix, table, acc, *parts)


def shards(tokens, shift, scale, gate, w_up, w_down, pick, count, combine):
    tok_rows, width = tokens.shape
    _, experts, slots = pick.shape
    devices = lax.axis_size("expert")
    place = lax.axis_index("expert")
    group = devices // experts
    requests = shift.shape[0]
    hidden = w_up.shape[0]
    info = jnp.stack([place // (devices // requests), place // group]).astype(jnp.int32)
    pick = pick[0]
    comb = combine[0]

    far = [d * group for d in turns(experts)[1:]]
    near = []
    bit = group // 2
    while bit:
        near.append(bit)
        bit //= 2

    def swap(x, mask):
        return lax.ppermute(x, "expert", [(i, i ^ mask) for i in range(devices)])

    tokens, shift, scale, gate, w_up, w_down, pick, comb, count = [
        pltpu.with_memory_space_constraint(x, pltpu.HBM)
        for x in (tokens, shift, scale, gate, w_up, w_down, pick, comb, count)
    ]
    quarter = hidden // 4
    farthest, tok, table, picks, weights, w_first = first(
        info, w_up, (quarter, width), tokens, pick, shift, scale, gate, comb, count
    )
    own, *others = rest(tok, table, picks)
    mixes = mixer(picks, weights, own, tok_rows)

    flat = [farthest] + others
    blocks = [own] + [swap(x, mask) for x, mask in zip(flat, far)]
    beside = [swap(block, near[0]) for block in blocks]
    w_second = load(w_up, (2 * quarter, 0), (2 * quarter, width), [blocks[2], mixes[0]])
    early, late = list(range(experts // 2)), list(range(experts // 2, experts))
    parts = []
    sources = []
    for members in (early, late):
        after = [] if members is early else [w_second]
        pieces = [join([x for i in members for x in (blocks[i], beside[i])], after)]
        if members is late:
            w_third = load(w_up, (quarter, 0), (quarter, width), [pieces[0]])
        height = pieces[0].shape[0]
        for mask in near[1:]:
            block = pieces[0] if len(pieces) == 1 else join(pieces, [])
            pieces = [block, swap(block, mask)]
        cuts = []
        for piece in pieces:
            cuts += [(len(parts), at, at + height) for at in range(0, piece.shape[0], height)]
            parts.append(piece)
        sources.append(cuts)
    sources = [cut for pair in zip(*sources) for cut in pair]

    half = 2 * quarter
    step = 3 * width // 4
    hid_b, down_b, rows = up(parts, sources, [w_second], w_down, (half, 0), (half, step))
    hid_a, down_a = up([rows], None, [w_first, w_third], w_down, (0, 0), (half, step))

    hiddens = [hid_a, hid_b]
    tall, last = (half, width - step), [(0, step), (half, step)]
    keep_a, send_a, *downs = down(hiddens, [down_a, down_b], w_down, last, [tall, tall])
    keep_b, send_b = down(hiddens, downs, None, None, [])
    pairs = []
    for keep, send in ((keep_a, send_a), (keep_b, send_b)):
        for i, mask in enumerate(reversed(near[1:])):
            if i:
                middle = keep.shape[0] // 2
                keep, send = add(
                    [(keep, got)], [(0, middle), (middle, 2 * middle)], [F32, BF16]
                )
            if pairs:
                send = join([send], [pairs[0][1]])
            got = swap(send, mask)
        pairs.append((keep, got))
    keeps = [(2 * i * slots, (2 * i + 1) * slots) for i in range(experts)]
    sends = [(high, high + slots) for _, high in keeps]
    summed = add(pairs, sends + keeps, [BF16] * experts + [F32] * experts)
    sends, keeps = summed[:experts], summed[experts:]
    arrived = [swap(send, near[0]) for send in sends[1:]]
    parts = [
        add([(keep, got)], [(0, slots)], [BF16])[0] for keep, got in zip(keeps[1:], arrived)
    ]
    back = [swap(part, mask) for part, mask in zip(parts, far)]
    arrived = swap(join([sends[0]], [parts[0]]), near[0])
    acc = own_part(mixes[0], keeps[0], arrived, back[0])
    return post(mixes[1], table, acc, back[1:])


def solution(mesh):
    return jax.shard_map(
        shards,
        mesh=mesh,
        in_specs=(
            P(("groups", "expert"), None),
            P("groups", None),
            P("groups", None),
            P("groups", None),
            P("expert", None),
            P("expert", None),
            P(("groups", "expert"), None, None),
            P(("groups", "expert"), None),
            P(("groups", "expert"), None, None),
        ),
        out_specs=P(("groups", "expert"), None),
        check_vma=False,
    )
```

time: 62.8 us -> 66.9 us (1.065)
  waiting for transfers between devices: 17 us -> 20 us
  Pallas kernels: 23.8 us -> 25.3 us
    ppermute x18, waiting for transfers between devices: 17 us -> 20 us  [swap(): return lax.ppermute(x, 'expert', [(i, i ^ mask) for i in range(devices)])]
    pallas_call x2, Pallas kernels: 5.87 us -> 8.14 us  [up(): pl.pallas_call(functools.partial(up_kernel, sources=sources, count=len(pa...]
    pallas_call x2, Pallas kernels: 6.95 us -> 5.7 us  [load(): pl.pallas_call(functools.partial(load_kernel, at=at), in_specs=[HBM] + [A...]
  transfers between devices with their start and end apart: 18 -> 18, of which waited for: 11 -> 11; matrix products, arithmetic and copies ran while one was open for 0% -> 0% of each run, Pallas kernels for 16% -> 13%
where the time goes in v8:
time: 66.9 us; the launch traced here: 66.8 us
  Pallas kernels  25.3 us (38%)
  starting transfers between devices  21.2 us (32%)
  waiting for transfers between devices  20 us (30%)
    ppermute x18, starting transfers between devices, swap(): return lax.ppermute(x, 'expert', [(i, i ^ mask) for i in range(devices)])  21.2 us
    ppermute x18, waiting for transfers between devices, swap(): return lax.ppermute(x, 'expert', [(i, i ^ mask) for i in range(devices)])  20 us
    pallas_call x2, Pallas kernels, up(): pl.pallas_call(functools.partial(up_kernel, sources=sources, count=len(pa...  8.14 us
    pallas_call x2, Pallas kernels, load(): pl.pallas_call(functools.partial(load_kernel, at=at), in_specs=[HBM] + [A...  5.7 us
    pallas_call x2, Pallas kernels, down(): pl.pallas_call(functools.partial(down_kernel, count=len(hiddens), at=at),...  5.19 us
    pallas_call x1, Pallas kernels, first(): pl.pallas_call(first_kernel, in_specs=[SMEM] + [HBM] * 8, out_specs=[VMEM...  3.24 us
    pallas_call x1, Pallas kernels, post(): pl.pallas_call(post_kernel, grid=(width // step,), in_specs=[VMEM] * (3 +...  1.36 us
  transfers between devices with their start and end apart: 18, of which 11 were waited for; matrix products, arithmetic and copies ran while one was open for 0% of the time, Pallas kernels for 13%

profile of v8, /device:TPU:0, one launch (start us, length us, event | category | flops | bytes accessed | tf_op | source)
XLA Modules:
  0.0 66.8 jit_solution(888152774520662616)
XLA Ops:
  0.1 3.2 %first.1 = (bf16[16,4096]{1,0:T(8,128)(2,1)S(1)}, bf16[128,4096]{1,0:T(8,128)(2,1)S(1)}, f32[3,4096]{1,0:T(4,128)S(1)}, s32[4,16]{1,0:T(4,128)S(1)}, f32[4,16]{1,0:T(4,128)S(1)}, /*index=5*/bf16[512,4096]{1,0:T(8,128)(2,1)S(1)}) custom-call(s32[2]{0:T(128)S(1)} %pad_add_fusion.info_ref, bf16[2048,4096]{1,0:T(8,128)(2,1)} %w_hbm.5, ...), custom_call_target="tpu_custom_call" | custom-call | flops 1 | bytes 1 | tf_op jit(solution)/shard_map/first/pallas_call | solution.py:91
  3.3 5.1 %collective-permute-start.1 = (bf16[16,4096]{1,0:T(8,128)(2,1)S(1)}, bf16[16,4096]{1,0:T(8,128)(2,1)S(1)}, u32[]{:S(2)}, u32[]{:S(2)}) collective-permute-start(bf16[16,4096]{1,0:T(8,128)(2,1)S(1)} %get-tuple-element.42), channel_id=1, source_target_pairs={{0,12},{1,13},{2,14},{3,15},{4,8},{5,9},{6,10},{7,11},{8,4},{9,5},... | collective-permute-start | bytes 393224 | tf_op jit(solution)/shard_map/ppermute | solution.py:406
  9.8 1.7 %collective-permute-start = (bf16[16,4096]{1,0:T(8,128)(2,1)S(1)}, bf16[16,4096]{1,0:T(8,128)(2,1)S(1)}, u32[]{:S(2)}, u32[]{:S(2)}) collective-permute-start(bf16[16,4096]{1,0:T(8,128)(2,1)S(1)} %get-tuple-element.39.after_ref.refs_0_), channel_id=1, source_target_pairs={{0,2},{1,3},{2,0},{3,1},{4,6},{5,7},{6,4},{7,5},{8,10},{9,11},{10,... | collective-permute-start | bytes 393224 | tf_op jit(solution)/shard_map/ppermute | solution.py:406
  12.7 1.6 %collective-permute-start.2 = (bf16[16,4096]{1,0:T(8,128)(2,1)S(1)}, bf16[16,4096]{1,0:T(8,128)(2,1)S(1)}, u32[]{:S(2)}, u32[]{:S(2)}) collective-permute-start(bf16[16,4096]{1,0:T(8,128)(2,1)S(1)} %collective-permute-done.1.refs_2_), channel_id=1, source_target_pairs={{0,2},{1,3},{2,0},{3,1},{4,6},{5,7},{6,4},{7,5},{8,10},{9,11},{10,... | collective-permute-start | bytes 393224 | tf_op jit(solution)/shard_map/ppermute | solution.py:406
  14.2 5.3 %collective-permute-done.4.refs_0_ = bf16[16,4096]{1,0:T(8,128)(2,1)S(1)} collective-permute-done((bf16[16,4096]{1,0:T(8,128)(2,1)S(1)}, bf16[16,4096]{1,0:T(8,128)(2,1)S(1)}, u32[]{:S(2)}, u32[]{:S(2)}) %collective-permute-start.4) | collective-permute-done | bytes 131104 | tf_op jit(solution)/shard_map/ppermute | solution.py:406
  19.5 1.5 %collective-permute-start.5 = (bf16[16,4096]{1,0:T(8,128)(2,1)S(1)}, bf16[16,4096]{1,0:T(8,128)(2,1)S(1)}, u32[]{:S(2)}, u32[]{:S(2)}) collective-permute-start(bf16[16,4096]{1,0:T(8,128)(2,1)S(1)} %collective-permute-done.4.refs_0_), channel_id=1, source_target_pairs={{0,2},{1,3},{2,0},{3,1},{4,6},{5,7},{6,4},{7,5},{8,10},{9,11},{10,... | collective-permute-start | bytes 393224 | tf_op jit(solution)/shard_map/ppermute | solution.py:406
  21.7 3.5 %load.2.refs_4_ = bf16[1024,4096]{1,0:T(8,128)(2,1)S(1)} custom-call(bf16[2048,4096]{1,0:T(8,128)(2,1)} %w_hbm.5, bf16[16,4096]{1,0:T(8,128)(2,1)S(1)} %collective-permute-done.4.refs_0_, bf16[128,64]{1,0:T(8,128)(2,1)S(1)} %get-tuple-element.41.refs_1_.mix_ref), custom_call_target="tpu_custom_call" | custom-call | flops 1 | bytes 1 | tf_op jit(solution)/shard_map/load/pallas_call | solution.py:175
  25.5 1.4 %collective-permute-done.7.refs_3_ = bf16[16,4096]{1,0:T(8,128)(2,1)S(1)} collective-permute-done((bf16[16,4096]{1,0:T(8,128)(2,1)S(1)}, bf16[16,4096]{1,0:T(8,128)(2,1)S(1)}, u32[]{:S(2)}, u32[]{:S(2)}) %collective-permute-start.7) | collective-permute-done | bytes 131104 | tf_op jit(solution)/shard_map/ppermute | solution.py:406
  27.0 2.2 %load.3.refs_2_ = bf16[512,4096]{1,0:T(8,128)(2,1)S(1)} custom-call(bf16[2048,4096]{1,0:T(8,128)(2,1)} %w_hbm.5, bf16[64,4096]{1,0:T(8,128)(2,1)S(1)} %join.5.refs_2_.refs_0_), custom_call_target="tpu_custom_call" | custom-call | flops 1 | bytes 1 | tf_op jit(solution)/shard_map/load/pallas_call | solution.py:175
  29.2 3.0 %up.2 = (bf16[256,1024]{1,0:T(8,128)(2,1)S(1)}, bf16[1024,3072]{1,0:T(8,128)(2,1)S(1)}, bf16[256,4096]{1,0:T(8,128)(2,1)S(1)}) custom-call(bf16[64,4096]{1,0:T(8,128)(2,1)S(1)} %join.4.refs_0_, bf16[64,4096]{1,0:T(8,128)(2,1)S(1)} %collective-permute-done.3.refs_1_, bf16[64,4096]{1,0:T(8,128)(2,1)S(1)} %join.5.refs_2_.refs_0_, ...), custom_call_target="tpu_custom_call" | custom-call | flops 1 | bytes 1 | tf_op jit(solution)/shard_map/up/pallas_call | solution.py:251
  32.2 5.1 %up.3 = (bf16[256,1024]{1,0:T(8,128)(2,1)S(1)}, bf16[1024,3072]{1,0:T(8,128)(2,1)S(1)}) custom-call(bf16[256,4096]{1,0:T(8,128)(2,1)S(1)} %get-tuple-element.45.refs_0_, bf16[512,4096]{1,0:T(8,128)(2,1)S(1)} %get-tuple-element.46.refs_1_, bf16[512,4096]{1,0:T(8,128)(2,1)S(1)} %load.3.refs_2_, bf16[2048,4096]{1,0:T(8,128)(2,1)} %refs_4_.3), custom_call_target="tpu_custom_call" | custom-call | flops 1 | bytes 1 | tf_op jit(solution)/shard_map/up/pallas_call | solution.py:251
  37.4 3.9 %down.2 = (f32[128,3072]{1,0:T(8,128)S(1)}, bf16[128,3072]{1,0:T(8,128)(2,1)S(1)}, bf16[1024,1024]{1,0:T(8,128)(2,1)S(1)}, bf16[1024,1024]{1,0:T(8,128)(2,1)S(1)}) custom-call(bf16[256,1024]{1,0:T(8,128)(2,1)S(1)} %get-tuple-element.47.refs_0_, bf16[256,1024]{1,0:T(8,128)(2,1)S(1)} %get-tuple-element.48.refs_1_, ...), custom_call_target="tpu_custom_call" | custom-call | flops 1 | bytes 1 | tf_op jit(solution)/shard_map/down/pallas_call | solution.py:299
  41.9 1.2 %down.3 = (f32[128,1024]{1,0:T(8,128)S(1)}, bf16[128,1024]{1,0:T(8,128)(2,1)S(1)}) custom-call(bf16[256,1024]{1,0:T(8,128)(2,1)S(1)} %get-tuple-element.47.refs_0_, bf16[256,1024]{1,0:T(8,128)(2,1)S(1)} %get-tuple-element.48.refs_1_, bf16[1024,1024]{1,0:T(8,128)(2,1)S(1)} %get-tuple-element.53.refs_2_, bf16[1024,1024]{1,0:T(8,128)(2,1)S(1)} %get-tuple-element.54.refs_3_), custom_call_target="tpu_custom_call" | custom-call | flops 1 | bytes 1 | tf_op jit(solution)/shard_map/down/pallas_call | solution.py:299
  44.3 1.2 %collective-permute-done.10.refs_3_ = bf16[128,1024]{1,0:T(8,128)(2,1)S(1)} collective-permute-done((bf16[128,1024]{1,0:T(8,128)(2,1)S(1)}, bf16[128,1024]{1,0:T(8,128)(2,1)S(1)}, u32[]{:S(2)}, u32[]{:S(2)}) %collective-permute-start.10) | collective-permute-done | bytes 262176 | tf_op jit(solution)/shard_map/ppermute | solution.py:406
  45.6 1.6 %collective-permute-start.11 = (bf16[16,4096]{1,0:T(8,128)(2,1)S(1)}, bf16[16,4096]{1,0:T(8,128)(2,1)S(1)}, u32[]{:S(2)}, u32[]{:S(2)}) collective-permute-start(bf16[16,4096]{1,0:T(8,128)(2,1)S(1)} %get-tuple-element.60), channel_id=1, source_target_pairs={{0,2},{1,3},{2,0},{3,1},{4,6},{5,7},{6,4},{7,5},{8,10},{9,11},{10,... | collective-permute-start | bytes 393224 | tf_op jit(solution)/shard_map/ppermute | solution.py:406
  47.7 1.5 %collective-permute-start.16 = (bf16[16,4096]{1,0:T(8,128)(2,1)S(1)}, bf16[16,4096]{1,0:T(8,128)(2,1)S(1)}, u32[]{:S(2)}, u32[]{:S(2)}) collective-permute-start(bf16[16,4096]{1,0:T(8,128)(2,1)S(1)} %get-tuple-element.64), channel_id=1, source_target_pairs={{0,2},{1,3},{2,0},{3,1},{4,6},{5,7},{6,4},{7,5},{8,10},{9,11},{10,... | collective-permute-start | bytes 393224 | tf_op jit(solution)/shard_map/ppermute | solution.py:406
  49.2 2.8 %collective-permute-done.11.refs_1_ = bf16[16,4096]{1,0:T(8,128)(2,1)S(1)} collective-permute-done((bf16[16,4096]{1,0:T(8,128)(2,1)S(1)}, bf16[16,4096]{1,0:T(8,128)(2,1)S(1)}, u32[]{:S(2)}, u32[]{:S(2)}) %collective-permute-start.11) | collective-permute-done | bytes 131104 | tf_op jit(solution)/shard_map/ppermute | solution.py:406
  52.0 2.5 %collective-permute-start.13 = (bf16[16,4096]{1,0:T(8,128)(2,1)S(1)}, bf16[16,4096]{1,0:T(8,128)(2,1)S(1)}, u32[]{:S(2)}, u32[]{:S(2)}) collective-permute-start(bf16[16,4096]{1,0:T(8,128)(2,1)S(1)} %add.9.refs_1_), channel_id=1, source_target_pairs={{0,12},{1,13},{2,14},{3,15},{4,8},{5,9},{6,10},{7,11},{8,4},{9,5},... | collective-permute-start | bytes 393224 | tf_op jit(solution)/shard_map/ppermute | solution.py:406
  54.6 1.6 %collective-permute-start.12 = (bf16[16,4096]{1,0:T(8,128)(2,1)S(1)}, bf16[16,4096]{1,0:T(8,128)(2,1)S(1)}, u32[]{:S(2)}, u32[]{:S(2)}) collective-permute-start(bf16[16,4096]{1,0:T(8,128)(2,1)S(1)} %join.7), channel_id=1, source_target_pairs={{0,2},{1,3},{2,0},{3,1},{4,6},{5,7},{6,4},{7,5},{8,10},{9,11},{10,... | collective-permute-start | bytes 393224 | tf_op jit(solution)/shard_map/ppermute | solution.py:406
  56.3 1.3 %collective-permute-done.16.refs_1_ = bf16[16,4096]{1,0:T(8,128)(2,1)S(1)} collective-permute-done((bf16[16,4096]{1,0:T(8,128)(2,1)S(1)}, bf16[16,4096]{1,0:T(8,128)(2,1)S(1)}, u32[]{:S(2)}, u32[]{:S(2)}) %collective-permute-start.16) | collective-permute-done | bytes 131104 | tf_op jit(solution)/shard_map/ppermute | solution.py:406
  57.7 1.1 %collective-permute-start.17 = (bf16[16,4096]{1,0:T(8,128)(2,1)S(1)}, bf16[16,4096]{1,0:T(8,128)(2,1)S(1)}, u32[]{:S(2)}, u32[]{:S(2)}) collective-permute-start(bf16[16,4096]{1,0:T(8,128)(2,1)S(1)} %add.11), channel_id=1, source_target_pairs={{0,4},{1,5},{2,6},{3,7},{4,0},{5,1},{6,2},{7,3},{8,12},{9,13},{10,... | collective-permute-start | bytes 393224 | tf_op jit(solution)/shard_map/ppermute | solution.py:406
  58.8 1.1 %collective-permute-done.12.near_ref = bf16[16,4096]{1,0:T(8,128)(2,1)S(1)} collective-permute-done((bf16[16,4096]{1,0:T(8,128)(2,1)S(1)}, bf16[16,4096]{1,0:T(8,128)(2,1)S(1)}, u32[]{:S(2)}, u32[]{:S(2)}) %collective-permute-start.12) | collective-permute-done | bytes 131104 | tf_op jit(solution)/shard_map/ppermute | solution.py:406
  60.4 5.0 %collective-permute-done.15.refs_0_ = bf16[16,4096]{1,0:T(8,128)(2,1)S(1)} collective-permute-done((bf16[16,4096]{1,0:T(8,128)(2,1)S(1)}, bf16[16,4096]{1,0:T(8,128)(2,1)S(1)}, u32[]{:S(2)}, u32[]{:S(2)}) %collective-permute-start.15) | collective-permute-done | bytes 131104 | tf_op jit(solution)/shard_map/ppermute | solution.py:406
  65.4 1.4 %post.1 = bf16[128,4096]{1,0:T(8,128)(2,1)} custom-call(bf16[128,64]{1,0:T(8,128)(2,1)S(1)} %get-tuple-element.40.mix_ref, f32[3,4096]{1,0:T(4,128)S(1)} %get-tuple-element.38.table_ref, f32[128,4096]{1,0:T(8,128)S(1)} %own_part.1.acc_ref, bf16[16,4096]{1,0:T(8,128)(2,1)S(1)} %collective-permute-done.15.refs_0_, ...), custom_call_target="tpu_custom_call" | custom-call | flops 1 | bytes 1 | tf_op jit(solution)/shard_map/post/pallas_call | solution.py:374
  (32 shorter events, 6.7 us)
Async XLA Ops:
  3.3 9.3 %collective-permute-start.1 = (bf16[16,4096]{1,0:T(8,128)(2,1)S(1)}, bf16[16,4096]{1,0:T(8,128)(2,1)S(1)}, u32[]{:S(2)}, u32[]{:S(2)}) collective-permute-start(bf16[16,4096]{1,0:T(8,128)(2,1)S(1)} %get-tuple-element.42), channel_id=1, source_target_pairs={{0,12},{1,13},{2,14},{3,15},{4,8},{5,9},{6,10},{7,11},{8,4},{9,5},... | collective-permute-start | bytes 393224 | tf_op jit(solution)/shard_map/ppermute | solution.py:406
  9.2 10.3 %collective-permute-start.4 = (bf16[16,4096]{1,0:T(8,128)(2,1)S(1)}, bf16[16,4096]{1,0:T(8,128)(2,1)S(1)}, u32[]{:S(2)}, u32[]{:S(2)}) collective-permute-start(bf16[16,4096]{1,0:T(8,128)(2,1)S(1)} %get-tuple-element.43), channel_id=1, source_target_pairs={{0,8},{1,9},{2,10},{3,11},{4,12},{5,13},{6,14},{7,15},{8,0},{9,1},... | collective-permute-start | bytes 393224 | tf_op jit(solution)/shard_map/ppermute | solution.py:406
  9.3 11.8 %collective-permute-start.6 = (bf16[16,4096]{1,0:T(8,128)(2,1)S(1)}, bf16[16,4096]{1,0:T(8,128)(2,1)S(1)}, u32[]{:S(2)}, u32[]{:S(2)}) collective-permute-start(bf16[16,4096]{1,0:T(8,128)(2,1)S(1)} %get-tuple-element.44), channel_id=1, source_target_pairs={{0,4},{1,5},{2,6},{3,7},{4,0},{5,1},{6,2},{7,3},{8,12},{9,13},{10,... | collective-permute-start | bytes 393224 | tf_op jit(solution)/shard_map/ppermute | solution.py:406
  9.8 15.4 %collective-permute-start = (bf16[16,4096]{1,0:T(8,128)(2,1)S(1)}, bf16[16,4096]{1,0:T(8,128)(2,1)S(1)}, u32[]{:S(2)}, u32[]{:S(2)}) collective-permute-start(bf16[16,4096]{1,0:T(8,128)(2,1)S(1)} %get-tuple-element.39.after_ref.refs_0_), channel_id=1, source_target_pairs={{0,2},{1,3},{2,0},{3,1},{4,6},{5,7},{6,4},{7,5},{8,10},{9,11},{10,... | collective-permute-start | bytes 393224 | tf_op jit(solution)/shard_map/ppermute | solution.py:406
  12.7 12.6 %collective-permute-start.2 = (bf16[16,4096]{1,0:T(8,128)(2,1)S(1)}, bf16[16,4096]{1,0:T(8,128)(2,1)S(1)}, u32[]{:S(2)}, u32[]{:S(2)}) collective-permute-start(bf16[16,4096]{1,0:T(8,128)(2,1)S(1)} %collective-permute-done.1.refs_2_), channel_id=1, source_target_pairs={{0,2},{1,3},{2,0},{3,1},{4,6},{5,7},{6,4},{7,5},{8,10},{9,11},{10,... | collective-permute-start | bytes 393224 | tf_op jit(solution)/shard_map/ppermute | solution.py:406
  19.5 6.0 %collective-permute-start.5 = (bf16[16,4096]{1,0:T(8,128)(2,1)S(1)}, bf16[16,4096]{1,0:T(8,128)(2,1)S(1)}, u32[]{:S(2)}, u32[]{:S(2)}) collective-permute-start(bf16[16,4096]{1,0:T(8,128)(2,1)S(1)} %collective-permute-done.4.refs_0_), channel_id=1, source_target_pairs={{0,2},{1,3},{2,0},{3,1},{4,6},{5,7},{6,4},{7,5},{8,10},{9,11},{10,... | collective-permute-start | bytes 393224 | tf_op jit(solution)/shard_map/ppermute | solution.py:406
  21.0 5.8 %collective-permute-start.7 = (bf16[16,4096]{1,0:T(8,128)(2,1)S(1)}, bf16[16,4096]{1,0:T(8,128)(2,1)S(1)}, u32[]{:S(2)}, u32[]{:S(2)}) collective-permute-start(bf16[16,4096]{1,0:T(8,128)(2,1)S(1)} %collective-permute-done.6.refs_2_), channel_id=1, source_target_pairs={{0,2},{1,3},{2,0},{3,1},{4,6},{5,7},{6,4},{7,5},{8,10},{9,11},{10,... | collective-permute-start | bytes 393224 | tf_op jit(solution)/shard_map/ppermute | solution.py:406
  25.3 3.9 %collective-permute-start.3 = (bf16[64,4096]{1,0:T(8,128)(2,1)S(1)}, bf16[64,4096]{1,0:T(8,128)(2,1)S(1)}, u32[]{:S(2)}, u32[]{:S(2)}) collective-permute-start(bf16[64,4096]{1,0:T(8,128)(2,1)S(1)} %join.4.refs_0_), channel_id=1, source_target_pairs={{0,1},{1,0},{2,3},{3,2},{4,5},{5,4},{6,7},{7,6},{8,9},{9,8},{10,11... | collective-permute-start | bytes 1572872 | tf_op jit(solution)/shard_map/ppermute | solution.py:406
  26.9 2.3 %collective-permute-start.8 = (bf16[64,4096]{1,0:T(8,128)(2,1)S(1)}, bf16[64,4096]{1,0:T(8,128)(2,1)S(1)}, u32[]{:S(2)}, u32[]{:S(2)}) collective-permute-start(bf16[64,4096]{1,0:T(8,128)(2,1)S(1)} %join.5.refs_2_.refs_0_), channel_id=1, source_target_pairs={{0,1},{1,0},{2,3},{3,2},{4,5},{5,4},{6,7},{7,6},{8,9},{9,8},{10,11... | collective-permute-start | bytes 1572872 | tf_op jit(solution)/shard_map/ppermute | solution.py:406
  41.3 2.5 %collective-permute-start.9 = (bf16[128,3072]{1,0:T(8,128)(2,1)S(1)}, bf16[128,3072]{1,0:T(8,128)(2,1)S(1)}, u32[]{:S(2)}, u32[]{:S(2)}) collective-permute-start(bf16[128,3072]{1,0:T(8,128)(2,1)S(1)} %get-tuple-element.52), channel_id=1, source_target_pairs={{0,1},{1,0},{2,3},{3,2},{4,5},{5,4},{6,7},{7,6},{8,9},{9,8},{10,11... | collective-permute-start | bytes 2359304 | tf_op jit(solution)/shard_map/ppermute | solution.py:406
  43.8 1.6 %collective-permute-start.10 = (bf16[128,1024]{1,0:T(8,128)(2,1)S(1)}, bf16[128,1024]{1,0:T(8,128)(2,1)S(1)}, u32[]{:S(2)}, u32[]{:S(2)}) collective-permute-start(bf16[128,1024]{1,0:T(8,128)(2,1)S(1)} %join.6), channel_id=1, source_target_pairs={{0,1},{1,0},{2,3},{3,2},{4,5},{5,4},{6,7},{7,6},{8,9},{9,8},{10,11... | collective-permute-start | bytes 786440 | tf_op jit(solution)/shard_map/ppermute | solution.py:406
  45.6 6.4 %collective-permute-start.11 = (bf16[16,4096]{1,0:T(8,128)(2,1)S(1)}, bf16[16,4096]{1,0:T(8,128)(2,1)S(1)}, u32[]{:S(2)}, u32[]{:S(2)}) collective-permute-start(bf16[16,4096]{1,0:T(8,128)(2,1)S(1)} %get-tuple-element.60), channel_id=1, source_target_pairs={{0,2},{1,3},{2,0},{3,1},{4,6},{5,7},{6,4},{7,5},{8,10},{9,11},{10,... | collective-permute-start | bytes 393224 | tf_op jit(solution)/shard_map/ppermute | solution.py:406
  47.2 9.0 %collective-permute-start.14 = (bf16[16,4096]{1,0:T(8,128)(2,1)S(1)}, bf16[16,4096]{1,0:T(8,128)(2,1)S(1)}, u32[]{:S(2)}, u32[]{:S(2)}) collective-permute-start(bf16[16,4096]{1,0:T(8,128)(2,1)S(1)} %get-tuple-element.62), channel_id=1, source_target_pairs={{0,2},{1,3},{2,0},{3,1},{4,6},{5,7},{6,4},{7,5},{8,10},{9,11},{10,... | collective-permute-start | bytes 393224 | tf_op jit(solution)/shard_map/ppermute | solution.py:406
  47.7 9.9 %collective-permute-start.16 = (bf16[16,4096]{1,0:T(8,128)(2,1)S(1)}, bf16[16,4096]{1,0:T(8,128)(2,1)S(1)}, u32[]{:S(2)}, u32[]{:S(2)}) collective-permute-start(bf16[16,4096]{1,0:T(8,128)(2,1)S(1)} %get-tuple-element.64), channel_id=1, source_target_pairs={{0,2},{1,3},{2,0},{3,1},{4,6},{5,7},{6,4},{7,5},{8,10},{9,11},{10,... | collective-permute-start | bytes 393224 | tf_op jit(solution)/shard_map/ppermute | solution.py:406
  52.0 8.0 %collective-permute-start.13 = (bf16[16,4096]{1,0:T(8,128)(2,1)S(1)}, bf16[16,4096]{1,0:T(8,128)(2,1)S(1)}, u32[]{:S(2)}, u32[]{:S(2)}) collective-permute-start(bf16[16,4096]{1,0:T(8,128)(2,1)S(1)} %add.9.refs_1_), channel_id=1, source_target_pairs={{0,12},{1,13},{2,14},{3,15},{4,8},{5,9},{6,10},{7,11},{8,4},{9,5},... | collective-permute-start | bytes 393224 | tf_op jit(solution)/shard_map/ppermute | solution.py:406
  54.6 5.3 %collective-permute-start.12 = (bf16[16,4096]{1,0:T(8,128)(2,1)S(1)}, bf16[16,4096]{1,0:T(8,128)(2,1)S(1)}, u32[]{:S(2)}, u32[]{:S(2)}) collective-permute-start(bf16[16,4096]{1,0:T(8,128)(2,1)S(1)} %join.7), channel_id=1, source_target_pairs={{0,2},{1,3},{2,0},{3,1},{4,6},{5,7},{6,4},{7,5},{8,10},{9,11},{10,... | collective-permute-start | bytes 393224 | tf_op jit(solution)/shard_map/ppermute | solution.py:406
  56.2 9.2 %collective-permute-start.15 = (bf16[16,4096]{1,0:T(8,128)(2,1)S(1)}, bf16[16,4096]{1,0:T(8,128)(2,1)S(1)}, u32[]{:S(2)}, u32[]{:S(2)}) collective-permute-start(bf16[16,4096]{1,0:T(8,128)(2,1)S(1)} %add.10), channel_id=1, source_target_pairs={{0,8},{1,9},{2,10},{3,11},{4,12},{5,13},{6,14},{7,15},{8,0},{9,1},... | collective-permute-start | bytes 393224 | tf_op jit(solution)/shard_map/ppermute | solution.py:406
  57.7 7.8 %collective-permute-start.17 = (bf16[16,4096]{1,0:T(8,128)(2,1)S(1)}, bf16[16,4096]{1,0:T(8,128)(2,1)S(1)}, u32[]{:S(2)}, u32[]{:S(2)}) collective-permute-start(bf16[16,4096]{1,0:T(8,128)(2,1)S(1)} %add.11), channel_id=1, source_target_pairs={{0,4},{1,5},{2,6},{3,7},{4,0},{5,1},{6,2},{7,3},{8,12},{9,13},{10,... | collective-permute-start | bytes 393224 | tf_op jit(solution)/shard_map/ppermute | solution.py:406

commit v9 on v7

--- a/solution.py
+++ b/solution.py
@@ -31,6 +31,20 @@
         copy.start()
     for copy in copies:
         copy.wait()
+
+
+def stream(w_hbm, out_ref, sems, at, first=0, rows=None):
+    rows = out_ref.shape[0] if rows is None else rows
+    columns = out_ref.shape[1]
+    part = rows // PIECES
+    return [
+        pltpu.make_async_copy(
+            w_hbm.at[pl.ds(at[0] + p * part, part), pl.ds(at[1], columns)],
+            out_ref.at[pl.ds(first + p * part, part), :],
+            sems.at[p],
+        )
+        for p in range(PIECES)
+    ]
 
 
 def turns(experts):
@@ -100,26 +114,34 @@
     )(info, tokens, pick, shift, scale, gate, comb, count)
 
 
-def rest_kernel(tok_ref, table_ref, picks_ref, *outs):
+def rest_kernel(tok_ref, table_ref, picks_ref, w_hbm, *refs):
+    outs, w_ref, sems = refs[:-2], refs[-2], refs[-1]
+    copies = stream(w_hbm, w_ref, sems, (0, 0), rows=w_ref.shape[0] // 2)
+    for copy in copies:
+        copy.start()
     experts, slots = picks_ref.shape
     order = [0] + list(range(2, experts))
     picks = jnp.concatenate([picks_ref[i:i + 1, :] for i in order], axis=1)
     rows = modulate(picks, tok_ref, table_ref)
     for i, out in enumerate(outs):
         out[...] = rows[i * slots:(i + 1) * slots]
-
-
-def rest(tok, table, picks):
+    for copy in copies:
+        copy.wait()
+
+
+def rest(tok, table, picks, w, shape):
     experts, slots = picks.shape
     return pl.pallas_call(
         rest_kernel,
-        in_specs=[VMEM] * 3,
-        out_specs=[VMEM] * (experts - 1),
-        out_shape=[jax.ShapeDtypeStruct((slots, tok.shape[1]), BF16)] * (experts - 1),
+        in_specs=[VMEM] * 3 + [HBM],
+        out_specs=[VMEM] * experts,
+        out_shape=[jax.ShapeDtypeStruct((slots, tok.shape[1]), BF16)] * (experts - 1)
+        + [pltpu.VMEM(shape, BF16)],
+        scratch_shapes=[pltpu.SemaphoreType.DMA((PIECES,))],
         compiler_params=params(8),
         cost_estimate=FREE,
         name="rest",
-    )(tok, table, picks)
+    )(tok, table, picks, w)
 
 
 def mixer_kernel(picks_ref, weights_ref, after_ref, *outs):
@@ -146,23 +168,9 @@
     )(picks, weights, after)
 
 
-def stream(w_hbm, out_ref, sems, at):
-    rows, columns = out_ref.shape
-    pieces = sems.shape[0]
-    part = rows // pieces
-    return [
-        pltpu.make_async_copy(
-            w_hbm.at[pl.ds(at[0] + p * part, part), pl.ds(at[1], columns)],
-            out_ref.at[pl.ds(p * part, part), :],
-            sems.at[p],
-        )
-        for p in range(pieces)
-    ]
-
-
-def load_kernel(w_hbm, *refs, at):
+def load_kernel(w_hbm, *refs, at, first, rows):
     out_ref, sems = refs[-2:]
-    copies = stream(w_hbm, out_ref, sems, at)
+    copies = stream(w_hbm, out_ref, sems, at, first, rows)
     for copy in copies:
         copy.start()
     for copy in copies:
@@ -171,7 +179,7 @@
 
 def load(w, at, shape, after):
     return pl.pallas_call(
-        functools.partial(load_kernel, at=at),
+        functools.partial(load_kernel, at=at, first=0, rows=shape[0]),
         in_specs=[HBM] + [ANY] * len(after),
         out_specs=VMEM,
         out_shape=pltpu.VMEM(shape, w.dtype),
@@ -180,6 +188,21 @@
         cost_estimate=FREE,
         name="load",
     )(w, *after)
+
+
+def load_more(w, at, buffer, after):
+    rows = buffer.shape[0] // 2
+    return pl.pallas_call(
+        functools.partial(load_kernel, at=at, first=rows, rows=rows),
+        in_specs=[HBM, VMEM] + [ANY] * len(after),
+        out_specs=VMEM,
+        out_shape=pltpu.VMEM(buffer.shape, w.dtype),
+        input_output_aliases={1: 0},
+        scratch_shapes=[pltpu.SemaphoreType.DMA((PIECES,))],
+        compiler_params=params(2),
+        cost_estimate=FREE,
+        name="load_more",
+    )(w, buffer, *after)
 
 
 def join_kernel(*refs, count):
@@ -250,81 +273,78 @@
     )(*parts, w, following)
 
 
-def down_kernel(*refs, count, blocks, at):
-    weights = refs[count:count + blocks]
+def down_kernel(*refs, count, at):
+    hiddens, weights = refs[:count], refs[count:2 * count]
     if at is None:
-        keep_ref, send_ref = refs[count + blocks:]
+        keep_ref, send_ref = refs[2 * count:]
         copies = []
     else:
-        next_hbm, keep_ref, send_ref, next_ref, sems = refs[count + blocks:]
-        copies = stream(next_hbm, next_ref, sems, at)
+        next_hbm, keep_ref, send_ref = refs[2 * count:2 * count + 3]
+        nexts, sems = refs[2 * count + 3:-1], refs[-1]
+        copies = []
+        for i, ref in enumerate(nexts):
+            copies += stream(next_hbm, ref, sems.at[pl.ds(i * PIECES, PIECES)], at[i])
     for copy in copies:
         copy.start()
-    half = keep_ref.shape[0]
-    base = 0
-    for w_ref in weights:
-        step = w_ref.shape[1]
-        tile = step // 2
-
-        @pl.loop(0, 2)
-        def _(i):
-            cut = pl.ds(pl.multiple_of(i * tile, tile), tile)
-            to = pl.ds(pl.multiple_of(base + i * tile, tile), tile)
-            low = 0
-            out = None
-            for h_ref in refs[:count]:
-                part = jnp.dot(
-                    h_ref[...], w_ref[low:low + h_ref.shape[1], cut], preferred_element_type=F32
-                )
-                out = part if out is None else out + part
-                low += h_ref.shape[1]
-            keep_ref[:, to] = out[:half]
-            send_ref[:, to] = out[half:].astype(BF16)
-
-        base += step
+    half, step = keep_ref.shape
+    tile = step if step <= 1536 else step // 2
+
+    @pl.loop(0, step // tile)
+    def _(i):
+        cut = pl.ds(pl.multiple_of(i * tile, tile), tile)
+        out = None
+        for h_ref, w_ref in zip(hiddens, weights):
+            part = jnp.dot(h_ref[...], w_ref[:, cut], preferred_element_type=F32)
+            out = part if out is None else out + part
+        keep_ref[:, cut] = out[:half]
+        send_ref[:, cut] = out[half:].astype(BF16)
+
     for copy in copies:
         copy.wait()
 
 
-def down(hiddens, weights, following, at, shape):
+def down(hiddens, weights, following, at, shapes):
     half = hiddens[0].shape[0] // 2
-    step = sum(w.shape[1] for w in weights)
+    step = weights[0].shape[1]
     more = following is not None
     return pl.pallas_call(
-        functools.partial(down_kernel, count=len(hiddens), blocks=len(weights), at=at),
-        in_specs=[VMEM] * (len(hiddens) + len(weights)) + [HBM] * more,
-        out_specs=[VMEM] * (2 + more),
+        functools.partial(down_kernel, count=len(hiddens), at=at),
+        in_specs=[VMEM] * (2 * len(hiddens)) + [HBM] * more,
+        out_specs=[VMEM] * (2 + len(shapes)),
         out_shape=[
             jax.ShapeDtypeStruct((half, step), F32),
             jax.ShapeDtypeStruct((half, step), BF16),
         ]
-        + ([pltpu.VMEM(shape, BF16)] if more else []),
-        scratch_shapes=[pltpu.SemaphoreType.DMA((PIECES,))] * more,
+        + [pltpu.VMEM(shape, BF16) for shape in shapes],
+        scratch_shapes=[pltpu.SemaphoreType.DMA((len(shapes) * PIECES,))] * more,
         compiler_params=params(12),
         cost_estimate=FREE,
         name="down",
     )(*hiddens, *weights, *([following] if more else []))
 
 
-def add_kernel(*refs, count, cuts):
-    at = 0
-    for i in range(count):
-        keep_ref, got_ref = refs[2 * i:2 * i + 2]
-        step = keep_ref.shape[1]
-        for ref, (low, high) in zip(refs[2 * count:], cuts):
+def add_kernel(*refs, count, outs):
+    for ref, pieces in zip(refs[2 * count:], outs):
+        at = 0
+        for i, low, high in pieces:
+            keep_ref, got_ref = refs[2 * i:2 * i + 2]
+            step = keep_ref.shape[1]
             total = keep_ref[low:high] + got_ref[low:high].astype(F32)
             ref[:, at:at + step] = total.astype(ref.dtype)
-        at += step
-
-
-def add(pairs, cuts, kinds):
-    width = sum(keep.shape[1] for keep, _ in pairs)
+            at += step
+
+
+def add(pairs, outs, kinds):
     args = [x for pair in pairs for x in pair]
-    return pl.pallas_call(
-        functools.partial(add_kernel, count=len(pairs), cuts=cuts),
+    shapes = [
+        (pieces[0][2] - pieces[0][1], sum(pairs[i][0].shape[1] for i, _, _ in pieces))
+        for pieces in outs
+    ]
+    return pl.pallas_call(
+        functools.partial(add_kernel, count=len(pairs), outs=outs),
         in_specs=[VMEM] * len(args),
-        out_specs=[VMEM] * len(cuts),
-        out_shape=[jax.ShapeDtypeStruct((high - low, width), k) for (low, high), k in zip(cuts, kinds)],
+        out_specs=[VMEM] * len(outs),
+        out_shape=[jax.ShapeDtypeStruct(shape, k) for shape, k in zip(shapes, kinds)],
         compiler_params=params(8),
         cost_estimate=FREE,
         name="add",
@@ -350,27 +370,34 @@
 
 
 def post_kernel(mix_ref, table_ref, acc_ref, *refs):
-    out_ref = refs[-1]
-    step = out_ref.shape[1]
-    cut = pl.ds(pl.multiple_of(pl.program_id(0) * step, step), step)
-    values = jnp.concatenate([ref[:, cut] for ref in refs[:-1]] * 2, axis=0)
-    mixed = acc_ref[:, cut] + jnp.dot(mix_ref[...], values, preferred_element_type=F32)
-    out_ref[...] = (table_ref[2:3, cut] * mixed).astype(BF16)
-
-
-def post(mix, table, acc, parts):
+    blocks = refs[:-3]
+    out_hbm, out_ref, sems = refs[-3:]
+    step = out_ref.shape[1] // sems.shape[0]
+    copies = []
+    for i in range(sems.shape[0]):
+        cut = pl.ds(i * step, step)
+        values = jnp.concatenate([ref[:, cut] for ref in blocks] * 2, axis=0)
+        mixed = acc_ref[:, cut] + jnp.dot(mix_ref[...], values, preferred_element_type=F32)
+        out_ref[:, cut] = (table_ref[2:3, cut] * mixed).astype(BF16)
+        copy = pltpu.make_async_copy(out_ref.at[:, cut], out_hbm.at[:, cut], sems.at[i])
+        copy.start()
+        copies.append(copy)
+    for copy in copies:
+        copy.wait()
+
+
+def post(mix, table, acc, blocks):
     tok_rows, width = acc.shape
-    step = min(2048, width)
     return pl.pallas_call(
         post_kernel,
-        grid=(width // step,),
-        in_specs=[VMEM] * (3 + len(parts)),
-        out_specs=pl.BlockSpec((tok_rows, step), lambda i: (0, i)),
+        in_specs=[VMEM] * (3 + len(blocks)),
+        out_specs=HBM,
         out_shape=jax.ShapeDtypeStruct((tok_rows, width), BF16),
+        scratch_shapes=[pltpu.VMEM((tok_rows, width), BF16), pltpu.SemaphoreType.DMA((4,))],
         compiler_params=params(8),
         cost_estimate=FREE,
         name="post",
-    )(mix, table, acc, *parts)
+    )(mix, table, acc, *blocks)
 
 
 def shards(tokens, shift, scale, gate, w_up, w_down, pick, count, combine):
@@ -399,23 +426,26 @@
         pltpu.with_memory_space_constraint(x, pltpu.HBM)
         for x in (tokens, shift, scale, gate, w_up, w_down, pick, comb, count)
     ]
+    half = hidden // 2
     farthest, tok, table, picks, weights = first(info, tokens, pick, shift, scale, gate, comb, count)
-    own, *others = rest(tok, table, picks)
-    mixes = mixer(picks, weights, own, tok_rows)
+    own, *others, w_low = rest(tok, table, picks, w_up, (half, width))
 
     flat = [farthest] + others
     blocks = [own] + [swap(x, mask) for x, mask in zip(flat, far)]
-    block_up = (hidden // 2, width)
-    ups = [load(w_up, (0, 0), block_up, [blocks[1], mixes[0]])]
-    blocks[2] = join([blocks[2]], [ups[0]])
+    mixes = mixer(picks, weights, blocks[1], tok_rows)
+    blocks[2] = join([blocks[2]], [mixes[0]])
     beside = [swap(block, near[0]) for block in blocks]
+    beside[-1] = join([beside[-1]], [])
     early, late = list(range(experts // 2)), list(range(experts // 2, experts))
     parts = []
     sources = []
     for members in (early, late):
-        pieces = [join([x for i in members for x in (blocks[i], beside[i])], ups[1:])]
+        after = [] if members is early else [w_high]
+        pieces = [join([x for i in members for x in (blocks[i], beside[i])], after)]
         if members is early:
-            ups.append(load(w_up, (hidden // 2, 0), block_up, [pieces[0], ups[0]]))
+            w_high = load(w_up, (half, 0), (half, width), [pieces[0]])
+        else:
+            w_low = load_more(w_up, (half // 2, 0), w_low, [pieces[0]])
         height = pieces[0].shape[0]
         for mask in near[1:]:
             block = pieces[0] if len(pieces) == 1 else join(pieces, [])
@@ -427,34 +457,45 @@
         sources.append(cuts)
     sources = [cut for pair in zip(*sources) for cut in pair]
 
-    step = 3 * width // 8
-    last = width - 2 * step
-    hid, down_a, rows = up(parts, sources, ups[0], w_down, (0, 0), (hidden, step))
-    hid_b, down_b = up([rows], None, ups[1], w_down, (0, step), (hidden, step))
-
-    keep_a, send_a, down_c = down([hid, hid_b], [down_a, down_b], w_down, (0, 2 * step), (hidden, last))
-    keep_b, send_b = down([hid, hid_b], [down_c], None, None, None)
+    step = 5 * width // 8
+    hid_high, down_high, rows = up(parts, sources, w_high, w_down, (half, 0), (half, step))
+    hid_low, down_low = up([rows], None, w_low, w_down, (0, 0), (half, step))
+
+    hiddens = [hid_low, hid_high]
+    tall = (half, width - step)
+    keep_a, send_a, *downs = down(
+        hiddens, [down_low, down_high], w_down, [(0, step), (half, step)], [tall, tall]
+    )
+    keep_b, send_b = down(hiddens, downs, None, None, [])
     pairs = []
     for keep, send in ((keep_a, send_a), (keep_b, send_b)):
         for i, mask in enumerate(reversed(near[1:])):
             if i:
-                half = keep.shape[0] // 2
-                keep, send = add([(keep, got)], [(0, half), (half, 2 * half)], [F32, BF16])
+                middle = keep.shape[0] // 2
+                keep, send = add(
+                    [(keep, got)], [[(0, 0, middle)], [(0, middle, 2 * middle)]], [F32, BF16]
+                )
             if pairs:
                 send = join([send], [pairs[0][1]])
             got = swap(send, mask)
         pairs.append((keep, got))
-    keeps = [(2 * i * slots, (2 * i + 1) * slots) for i in range(experts)]
-    sends = [(high, high + slots) for _, high in keeps]
-    summed = add(pairs, sends + keeps, [BF16] * experts + [F32] * experts)
-    sends, keeps = summed[:experts], summed[experts:]
-    arrived = {i: swap(sends[i], near[0]) for i in list(range(1, experts)) + [0]}
-    back = []
-    for i, mask in enumerate(far, 1):
-        (part,) = add([(keeps[i], arrived[i])], [(0, slots)], [BF16])
-        back.append(swap(part, mask))
-    acc = own_part(mixes[0], keeps[0], arrived[0], back[0])
-    return post(mixes[1], table, acc, back[1:])
+
+    def outs(side):
+        rows = [(2 * i + side) * slots for i in range(experts)]
+        return [[(piece, at, at + slots) for piece in range(len(pairs))] for at in rows]
+
+    sums = add(pairs, outs(1) + outs(0), [BF16] * experts + [F32] * experts)
+    sends, keeps = sums[:experts], sums[experts:]
+    back = {}
+    for i in range(1, experts):
+        got = swap(sends[i], near[0])
+        (part,) = add([(keeps[i], got)], [[(0, 0, slots)]], [BF16])
+        back[i] = swap(part, far[i - 1])
+        if i == 1:
+            own_send = join(sends[:1], [part])
+    got = swap(own_send, near[0])
+    acc = own_part(mixes[0], keeps[0], got, back[1])
+    return post(mixes[1], table, acc, [back[i] for i in range(2, experts)])
 
 
 def solution(mesh):

time: 62.8 us -> 61.1 us (0.973)
  waiting for transfers between devices: 17 us -> 14.8 us
  starting transfers between devices: 21.6 us -> 22.5 us
    ppermute x18, waiting for transfers between devices: 17 us -> 14.8 us  [swap(): return lax.ppermute(x, 'expert', [(i, i ^ mask) for i in range(devices)])]
    ppermute x18, starting transfers between devices: 21.6 us -> 22.5 us  [swap(): return lax.ppermute(x, 'expert', [(i, i ^ mask) for i in range(devices)])]
  transfers between devices with their start and end apart: 18 -> 18, of which waited for: 11 -> 7; matrix products, arithmetic and copies ran while one was open for 0% -> 0% of each run, Pallas kernels for 16% -> 17%
where the time goes in v9:
time: 61.1 us; the launch traced here: 61 us
  Pallas kernels  23.4 us (38%)
  starting transfers between devices  22.5 us (37%)
  waiting for transfers between devices  14.8 us (24%)
    ppermute x18, starting transfers between devices, swap(): return lax.ppermute(x, 'expert', [(i, i ^ mask) for i in range(devices)])  22.5 us
    ppermute x18, waiting for transfers between devices, swap(): return lax.ppermute(x, 'expert', [(i, i ^ mask) for i in range(devices)])  14.8 us
    pallas_call x2, Pallas kernels, up(): pl.pallas_call(functools.partial(up_kernel, sources=sources, count=len(pa...  5.86 us
    pallas_call x2, Pallas kernels, down(): pl.pallas_call(functools.partial(down_kernel, count=len(hiddens), at=at),...  5.05 us
    pallas_call x1, Pallas kernels, load(): pl.pallas_call(functools.partial(load_kernel, at=at, first=0, rows=shape[...  3.48 us
    pallas_call x1, Pallas kernels, first(): pl.pallas_call(first_kernel, in_specs=[SMEM] + [HBM] * 7, out_specs=[VMEM...  2.39 us
    pallas_call x1, Pallas kernels, rest(): pl.pallas_call(rest_kernel, in_specs=[VMEM] * 3 + [HBM], out_specs=[VMEM]...  2.22 us
    pallas_call x1, Pallas kernels, load_more(): pl.pallas_call(functools.partial(load_kernel, at=at, first=rows, rows=row...  2.21 us
  transfers between devices with their start and end apart: 18, of which 7 were waited for; matrix products, arithmetic and copies ran while one was open for 0% of the time, Pallas kernels for 17%

profile of v9, /device:TPU:0, one launch (start us, length us, event | category | flops | bytes accessed | tf_op | source)
XLA Modules:
  0.0 61.0 jit_solution(17824904063558417493)
XLA Ops:
  0.1 2.4 %first.1 = (bf16[16,4096]{1,0:T(8,128)(2,1)S(1)}, bf16[128,4096]{1,0:T(8,128)(2,1)S(1)}, f32[3,4096]{1,0:T(4,128)S(1)}, s32[4,16]{1,0:T(4,128)S(1)}, f32[4,16]{1,0:T(4,128)S(1)}) custom-call(s32[2]{0:T(128)S(1)} %pad_add_fusion.info_ref, bf16[128,4096]{1,0:T(8,128)(2,1)} %refs_0_.1, s32[4,16]{1,0:T(4,128)} %bitcast.4, f32[2,4096]{1,0:T(2,128)} %refs_2_.2, ...), custom_call_target="tpu_custom_call" | custom-call | flops 1 | bytes 1 | tf_op jit(solution)/shard_map/first/pallas_call | solution.py:91
  2.5 5.1 %collective-permute-start = (bf16[16,4096]{1,0:T(8,128)(2,1)S(1)}, bf16[16,4096]{1,0:T(8,128)(2,1)S(1)}, u32[]{:S(2)}, u32[]{:S(2)}) collective-permute-start(bf16[16,4096]{1,0:T(8,128)(2,1)S(1)} %get-tuple-element.37), channel_id=1, source_target_pairs={{0,12},{1,13},{2,14},{3,15},{4,8},{5,9},{6,10},{7,11},{8,4},{9,5},... | collective-permute-start | bytes 393224 | tf_op jit(solution)/shard_map/ppermute | solution.py:423
  7.6 2.2 %rest.1 = (bf16[16,4096]{1,0:T(8,128)(2,1)S(1)}, bf16[16,4096]{1,0:T(8,128)(2,1)S(1)}, bf16[16,4096]{1,0:T(8,128)(2,1)S(1)}, bf16[1024,4096]{1,0:T(8,128)(2,1)S(1)}) custom-call(bf16[128,4096]{1,0:T(8,128)(2,1)S(1)} %get-tuple-element.41.tok_ref, f32[3,4096]{1,0:T(4,128)S(1)} %get-tuple-element.39.table_ref, s32[4,16]{1,0:T(4,128)S(1)} %get-tuple-element.35.picks_ref, ...), custom_call_target="tpu_custom_call" | custom-call | flops 1 | bytes 1 | tf_op jit(solution)/shard_map/rest/pallas_call | solution.py:134
  10.5 1.7 %collective-permute-start.1 = (bf16[16,4096]{1,0:T(8,128)(2,1)S(1)}, bf16[16,4096]{1,0:T(8,128)(2,1)S(1)}, u32[]{:S(2)}, u32[]{:S(2)}) collective-permute-start(bf16[16,4096]{1,0:T(8,128)(2,1)S(1)} %get-tuple-element.42.refs_0_), channel_id=1, source_target_pairs={{0,2},{1,3},{2,0},{3,1},{4,6},{5,7},{6,4},{7,5},{8,10},{9,11},{10,... | collective-permute-start | bytes 393224 | tf_op jit(solution)/shard_map/ppermute | solution.py:423
  13.0 3.2 %collective-permute-done.6.refs_2_ = bf16[16,4096]{1,0:T(8,128)(2,1)S(1)} collective-permute-done((bf16[16,4096]{1,0:T(8,128)(2,1)S(1)}, bf16[16,4096]{1,0:T(8,128)(2,1)S(1)}, u32[]{:S(2)}, u32[]{:S(2)}) %collective-permute-start.6) | collective-permute-done | bytes 131104 | tf_op jit(solution)/shard_map/ppermute | solution.py:423
  16.1 1.5 %collective-permute-start.7 = (bf16[16,4096]{1,0:T(8,128)(2,1)S(1)}, bf16[16,4096]{1,0:T(8,128)(2,1)S(1)}, u32[]{:S(2)}, u32[]{:S(2)}) collective-permute-start(bf16[16,4096]{1,0:T(8,128)(2,1)S(1)} %collective-permute-done.6.refs_2_), channel_id=1, source_target_pairs={{0,2},{1,3},{2,0},{3,1},{4,6},{5,7},{6,4},{7,5},{8,10},{9,11},{10,... | collective-permute-start | bytes 393224 | tf_op jit(solution)/shard_map/ppermute | solution.py:423
  17.7 1.0 %collective-permute-done.4.refs_0_ = bf16[16,4096]{1,0:T(8,128)(2,1)S(1)} collective-permute-done((bf16[16,4096]{1,0:T(8,128)(2,1)S(1)}, bf16[16,4096]{1,0:T(8,128)(2,1)S(1)}, u32[]{:S(2)}, u32[]{:S(2)}) %collective-permute-start.4) | collective-permute-done | bytes 131104 | tf_op jit(solution)/shard_map/ppermute | solution.py:423
  18.7 1.6 %collective-permute-start.5 = (bf16[16,4096]{1,0:T(8,128)(2,1)S(1)}, bf16[16,4096]{1,0:T(8,128)(2,1)S(1)}, u32[]{:S(2)}, u32[]{:S(2)}) collective-permute-start(bf16[16,4096]{1,0:T(8,128)(2,1)S(1)} %join.7.refs_0_), channel_id=1, source_target_pairs={{0,2},{1,3},{2,0},{3,1},{4,6},{5,7},{6,4},{7,5},{8,10},{9,11},{10,... | collective-permute-start | bytes 393224 | tf_op jit(solution)/shard_map/ppermute | solution.py:423
  20.4 3.5 %load.1.refs_4_ = bf16[1024,4096]{1,0:T(8,128)(2,1)S(1)} custom-call(bf16[2048,4096]{1,0:T(8,128)(2,1)} %w_hbm.5, bf16[64,4096]{1,0:T(8,128)(2,1)S(1)} %join.6.refs_0_), custom_call_target="tpu_custom_call" | custom-call | flops 1 | bytes 1 | tf_op jit(solution)/shard_map/load/pallas_call | solution.py:181
  24.6 2.2 %load_more.1.refs_1_ = bf16[1024,4096]{1,0:T(8,128)(2,1)S(1)} custom-call(bf16[2048,4096]{1,0:T(8,128)(2,1)} %w_hbm.5, bf16[1024,4096]{1,0:T(8,128)(2,1)S(1)} %get-tuple-element.46.refs_0_, bf16[64,4096]{1,0:T(8,128)(2,1)S(1)} %join.9.refs_2_.refs_1_), custom_call_target="tpu_custom_call", output_to_operand_aliasing={{}: (1, {})} | custom-call | flops 1 | bytes 1 | tf_op jit(solution)/shard_map/load_more/pallas_call | solution.py:195
  26.8 3.0 %up.2 = (bf16[256,1024]{1,0:T(8,128)(2,1)S(1)}, bf16[1024,2560]{1,0:T(8,128)(2,1)S(1)}, bf16[256,4096]{1,0:T(8,128)(2,1)S(1)}) custom-call(bf16[64,4096]{1,0:T(8,128)(2,1)S(1)} %join.6.refs_0_, bf16[64,4096]{1,0:T(8,128)(2,1)S(1)} %collective-permute-done.3.refs_1_, bf16[64,4096]{1,0:T(8,128)(2,1)S(1)} %join.9.refs_2_.refs_1_, ...), custom_call_target="tpu_custom_call" | custom-call | flops 1 | bytes 1 | tf_op jit(solution)/shard_map/up/pallas_call | solution.py:264
  29.8 2.9 %up.3 = (bf16[256,1024]{1,0:T(8,128)(2,1)S(1)}, bf16[1024,2560]{1,0:T(8,128)(2,1)S(1)}) custom-call(bf16[256,4096]{1,0:T(8,128)(2,1)S(1)} %get-tuple-element.45.refs_0_, bf16[1024,4096]{1,0:T(8,128)(2,1)S(1)} %load_more.1.refs_1_, bf16[2048,4096]{1,0:T(8,128)(2,1)} %refs_4_.3), custom_call_target="tpu_custom_call" | custom-call | flops 1 | bytes 1 | tf_op jit(solution)/shard_map/up/pallas_call | solution.py:264
  32.7 3.3 %down.2 = (f32[128,2560]{1,0:T(8,128)S(1)}, bf16[128,2560]{1,0:T(8,128)(2,1)S(1)}, bf16[1024,1536]{1,0:T(8,128)(2,1)S(1)}, bf16[1024,1536]{1,0:T(8,128)(2,1)S(1)}) custom-call(bf16[256,1024]{1,0:T(8,128)(2,1)S(1)} %get-tuple-element.47.refs_0_, bf16[256,1024]{1,0:T(8,128)(2,1)S(1)} %get-tuple-element.48.refs_1_, ...), custom_call_target="tpu_custom_call" | custom-call | flops 1 | bytes 1 | tf_op jit(solution)/shard_map/down/pallas_call | solution.py:310
  36.0 1.8 %down.3 = (f32[128,1536]{1,0:T(8,128)S(1)}, bf16[128,1536]{1,0:T(8,128)(2,1)S(1)}) custom-call(bf16[256,1024]{1,0:T(8,128)(2,1)S(1)} %get-tuple-element.47.refs_0_, bf16[256,1024]{1,0:T(8,128)(2,1)S(1)} %get-tuple-element.48.refs_1_, bf16[1024,1536]{1,0:T(8,128)(2,1)S(1)} %get-tuple-element.53.refs_2_, bf16[1024,1536]{1,0:T(8,128)(2,1)S(1)} %get-tuple-element.54.refs_3_), custom_call_target="tpu_custom_call" | custom-call | flops 1 | bytes 1 | tf_op jit(solution)/shard_map/down/pallas_call | solution.py:310
  38.4 1.5 %collective-permute-done.10.refs_3_ = bf16[128,1536]{1,0:T(8,128)(2,1)S(1)} collective-permute-done((bf16[128,1536]{1,0:T(8,128)(2,1)S(1)}, bf16[128,1536]{1,0:T(8,128)(2,1)S(1)}, u32[]{:S(2)}, u32[]{:S(2)}) %collective-permute-start.10) | collective-permute-done | bytes 393248 | tf_op jit(solution)/shard_map/ppermute | solution.py:423
  40.1 1.3 %collective-permute-start.11 = (bf16[16,4096]{1,0:T(8,128)(2,1)S(1)}, bf16[16,4096]{1,0:T(8,128)(2,1)S(1)}, u32[]{:S(2)}, u32[]{:S(2)}) collective-permute-start(bf16[16,4096]{1,0:T(8,128)(2,1)S(1)} %get-tuple-element.60), channel_id=1, source_target_pairs={{0,2},{1,3},{2,0},{3,1},{4,6},{5,7},{6,4},{7,5},{8,10},{9,11},{10,... | collective-permute-start | bytes 393224 | tf_op jit(solution)/shard_map/ppermute | solution.py:423
  42.2 1.2 %collective-permute-start.16 = (bf16[16,4096]{1,0:T(8,128)(2,1)S(1)}, bf16[16,4096]{1,0:T(8,128)(2,1)S(1)}, u32[]{:S(2)}, u32[]{:S(2)}) collective-permute-start(bf16[16,4096]{1,0:T(8,128)(2,1)S(1)} %get-tuple-element.64), channel_id=1, source_target_pairs={{0,2},{1,3},{2,0},{3,1},{4,6},{5,7},{6,4},{7,5},{8,10},{9,11},{10,... | collective-permute-start | bytes 393224 | tf_op jit(solution)/shard_map/ppermute | solution.py:423
  43.4 3.1 %collective-permute-done.11.refs_1_ = bf16[16,4096]{1,0:T(8,128)(2,1)S(1)} collective-permute-done((bf16[16,4096]{1,0:T(8,128)(2,1)S(1)}, bf16[16,4096]{1,0:T(8,128)(2,1)S(1)}, u32[]{:S(2)}, u32[]{:S(2)}) %collective-permute-start.11) | collective-permute-done | bytes 131104 | tf_op jit(solution)/shard_map/ppermute | solution.py:423
  46.5 3.6 %collective-permute-start.13 = (bf16[16,4096]{1,0:T(8,128)(2,1)S(1)}, bf16[16,4096]{1,0:T(8,128)(2,1)S(1)}, u32[]{:S(2)}, u32[]{:S(2)}) collective-permute-start(bf16[16,4096]{1,0:T(8,128)(2,1)S(1)} %add.9.refs_1_), channel_id=1, source_target_pairs={{0,12},{1,13},{2,14},{3,15},{4,8},{5,9},{6,10},{7,11},{8,4},{9,5},... | collective-permute-start | bytes 393224 | tf_op jit(solution)/shard_map/ppermute | solution.py:423
  50.2 1.6 %collective-permute-start.12 = (bf16[16,4096]{1,0:T(8,128)(2,1)S(1)}, bf16[16,4096]{1,0:T(8,128)(2,1)S(1)}, u32[]{:S(2)}, u32[]{:S(2)}) collective-permute-start(bf16[16,4096]{1,0:T(8,128)(2,1)S(1)} %join.11), channel_id=1, source_target_pairs={{0,2},{1,3},{2,0},{3,1},{4,6},{5,7},{6,4},{7,5},{8,10},{9,11},{10,... | collective-permute-start | bytes 393224 | tf_op jit(solution)/shard_map/ppermute | solution.py:423
  51.9 1.7 %collective-permute-start.17 = (bf16[16,4096]{1,0:T(8,128)(2,1)S(1)}, bf16[16,4096]{1,0:T(8,128)(2,1)S(1)}, u32[]{:S(2)}, u32[]{:S(2)}) collective-permute-start(bf16[16,4096]{1,0:T(8,128)(2,1)S(1)} %add.11), channel_id=1, source_target_pairs={{0,4},{1,5},{2,6},{3,7},{4,0},{5,1},{6,2},{7,3},{8,12},{9,13},{10,... | collective-permute-start | bytes 393224 | tf_op jit(solution)/shard_map/ppermute | solution.py:423
  53.6 1.6 %collective-permute-done.12.near_ref = bf16[16,4096]{1,0:T(8,128)(2,1)S(1)} collective-permute-done((bf16[16,4096]{1,0:T(8,128)(2,1)S(1)}, bf16[16,4096]{1,0:T(8,128)(2,1)S(1)}, u32[]{:S(2)}, u32[]{:S(2)}) %collective-permute-start.12) | collective-permute-done | bytes 131104 | tf_op jit(solution)/shard_map/ppermute | solution.py:423
  55.6 4.1 %collective-permute-done.15.refs_0_ = bf16[16,4096]{1,0:T(8,128)(2,1)S(1)} collective-permute-done((bf16[16,4096]{1,0:T(8,128)(2,1)S(1)}, bf16[16,4096]{1,0:T(8,128)(2,1)S(1)}, u32[]{:S(2)}, u32[]{:S(2)}) %collective-permute-start.15) | collective-permute-done | bytes 131104 | tf_op jit(solution)/shard_map/ppermute | solution.py:423
  59.8 1.2 %post.1 = bf16[128,4096]{1,0:T(8,128)(2,1)} custom-call(bf16[128,64]{1,0:T(8,128)(2,1)S(1)} %get-tuple-element.38.mix_ref, f32[3,4096]{1,0:T(4,128)S(1)} %get-tuple-element.39.table_ref, f32[128,4096]{1,0:T(8,128)S(1)} %own_part.1.acc_ref, bf16[16,4096]{1,0:T(8,128)(2,1)S(1)} %collective-permute-done.15.refs_0_, ...), custom_call_target="tpu_custom_call" | custom-call | flops 1 | bytes 1 | tf_op jit(solution)/shard_map/post/pallas_call | solution.py:391
  (34 shorter events, 4.5 us)
Async XLA Ops:
  2.5 9.7 %collective-permute-start = (bf16[16,4096]{1,0:T(8,128)(2,1)S(1)}, bf16[16,4096]{1,0:T(8,128)(2,1)S(1)}, u32[]{:S(2)}, u32[]{:S(2)}) collective-permute-start(bf16[16,4096]{1,0:T(8,128)(2,1)S(1)} %get-tuple-element.37), channel_id=1, source_target_pairs={{0,12},{1,13},{2,14},{3,15},{4,8},{5,9},{6,10},{7,11},{8,4},{9,5},... | collective-permute-start | bytes 393224 | tf_op jit(solution)/shard_map/ppermute | solution.py:423
  9.8 6.3 %collective-permute-start.6 = (bf16[16,4096]{1,0:T(8,128)(2,1)S(1)}, bf16[16,4096]{1,0:T(8,128)(2,1)S(1)}, u32[]{:S(2)}, u32[]{:S(2)}) collective-permute-start(bf16[16,4096]{1,0:T(8,128)(2,1)S(1)} %get-tuple-element.44), channel_id=1, source_target_pairs={{0,4},{1,5},{2,6},{3,7},{4,0},{5,1},{6,2},{7,3},{8,12},{9,13},{10,... | collective-permute-start | bytes 393224 | tf_op jit(solution)/shard_map/ppermute | solution.py:423
  9.9 8.8 %collective-permute-start.4 = (bf16[16,4096]{1,0:T(8,128)(2,1)S(1)}, bf16[16,4096]{1,0:T(8,128)(2,1)S(1)}, u32[]{:S(2)}, u32[]{:S(2)}) collective-permute-start(bf16[16,4096]{1,0:T(8,128)(2,1)S(1)} %get-tuple-element.43), channel_id=1, source_target_pairs={{0,8},{1,9},{2,10},{3,11},{4,12},{5,13},{6,14},{7,15},{8,0},{9,1},... | collective-permute-start | bytes 393224 | tf_op jit(solution)/shard_map/ppermute | solution.py:423
  10.5 9.8 %collective-permute-start.1 = (bf16[16,4096]{1,0:T(8,128)(2,1)S(1)}, bf16[16,4096]{1,0:T(8,128)(2,1)S(1)}, u32[]{:S(2)}, u32[]{:S(2)}) collective-permute-start(bf16[16,4096]{1,0:T(8,128)(2,1)S(1)} %get-tuple-element.42.refs_0_), channel_id=1, source_target_pairs={{0,2},{1,3},{2,0},{3,1},{4,6},{5,7},{6,4},{7,5},{8,10},{9,11},{10,... | collective-permute-start | bytes 393224 | tf_op jit(solution)/shard_map/ppermute | solution.py:423
  12.2 8.1 %collective-permute-start.2 = (bf16[16,4096]{1,0:T(8,128)(2,1)S(1)}, bf16[16,4096]{1,0:T(8,128)(2,1)S(1)}, u32[]{:S(2)}, u32[]{:S(2)}) collective-permute-start(bf16[16,4096]{1,0:T(8,128)(2,1)S(1)} %collective-permute-done.after_ref.refs_2_), channel_id=1, source_target_pairs={{0,2},{1,3},{2,0},{3,1},{4,6},{5,7},{6,4},{7,5},{8,10},{9,11},{10,... | collective-permute-start | bytes 393224 | tf_op jit(solution)/shard_map/ppermute | solution.py:423
  16.1 7.8 %collective-permute-start.7 = (bf16[16,4096]{1,0:T(8,128)(2,1)S(1)}, bf16[16,4096]{1,0:T(8,128)(2,1)S(1)}, u32[]{:S(2)}, u32[]{:S(2)}) collective-permute-start(bf16[16,4096]{1,0:T(8,128)(2,1)S(1)} %collective-permute-done.6.refs_2_), channel_id=1, source_target_pairs={{0,2},{1,3},{2,0},{3,1},{4,6},{5,7},{6,4},{7,5},{8,10},{9,11},{10,... | collective-permute-start | bytes 393224 | tf_op jit(solution)/shard_map/ppermute | solution.py:423
  18.7 5.2 %collective-permute-start.5 = (bf16[16,4096]{1,0:T(8,128)(2,1)S(1)}, bf16[16,4096]{1,0:T(8,128)(2,1)S(1)}, u32[]{:S(2)}, u32[]{:S(2)}) collective-permute-start(bf16[16,4096]{1,0:T(8,128)(2,1)S(1)} %join.7.refs_0_), channel_id=1, source_target_pairs={{0,2},{1,3},{2,0},{3,1},{4,6},{5,7},{6,4},{7,5},{8,10},{9,11},{10,... | collective-permute-start | bytes 393224 | tf_op jit(solution)/shard_map/ppermute | solution.py:423
  20.4 6.4 %collective-permute-start.3 = (bf16[64,4096]{1,0:T(8,128)(2,1)S(1)}, bf16[64,4096]{1,0:T(8,128)(2,1)S(1)}, u32[]{:S(2)}, u32[]{:S(2)}) collective-permute-start(bf16[64,4096]{1,0:T(8,128)(2,1)S(1)} %join.6.refs_0_), channel_id=1, source_target_pairs={{0,1},{1,0},{2,3},{3,2},{4,5},{5,4},{6,7},{7,6},{8,9},{9,8},{10,11... | collective-permute-start | bytes 1572872 | tf_op jit(solution)/shard_map/ppermute | solution.py:423
  24.0 2.8 %collective-permute-start.8 = (bf16[64,4096]{1,0:T(8,128)(2,1)S(1)}, bf16[64,4096]{1,0:T(8,128)(2,1)S(1)}, u32[]{:S(2)}, u32[]{:S(2)}) collective-permute-start(bf16[64,4096]{1,0:T(8,128)(2,1)S(1)} %join.9.refs_2_.refs_1_), channel_id=1, source_target_pairs={{0,1},{1,0},{2,3},{3,2},{4,5},{5,4},{6,7},{7,6},{8,9},{9,8},{10,11... | collective-permute-start | bytes 1572872 | tf_op jit(solution)/shard_map/ppermute | solution.py:423
  36.0 2.2 %collective-permute-start.9 = (bf16[128,2560]{1,0:T(8,128)(2,1)S(1)}, bf16[128,2560]{1,0:T(8,128)(2,1)S(1)}, u32[]{:S(2)}, u32[]{:S(2)}) collective-permute-start(bf16[128,2560]{1,0:T(8,128)(2,1)S(1)} %get-tuple-element.52), channel_id=1, source_target_pairs={{0,1},{1,0},{2,3},{3,2},{4,5},{5,4},{6,7},{7,6},{8,9},{9,8},{10,11... | collective-permute-start | bytes 1966088 | tf_op jit(solution)/shard_map/ppermute | solution.py:423
  38.1 1.8 %collective-permute-start.10 = (bf16[128,1536]{1,0:T(8,128)(2,1)S(1)}, bf16[128,1536]{1,0:T(8,128)(2,1)S(1)}, u32[]{:S(2)}, u32[]{:S(2)}) collective-permute-start(bf16[128,1536]{1,0:T(8,128)(2,1)S(1)} %join.10), channel_id=1, source_target_pairs={{0,1},{1,0},{2,3},{3,2},{4,5},{5,4},{6,7},{7,6},{8,9},{9,8},{10,11... | collective-permute-start | bytes 1179656 | tf_op jit(solution)/shard_map/ppermute | solution.py:423
  40.1 6.4 %collective-permute-start.11 = (bf16[16,4096]{1,0:T(8,128)(2,1)S(1)}, bf16[16,4096]{1,0:T(8,128)(2,1)S(1)}, u32[]{:S(2)}, u32[]{:S(2)}) collective-permute-start(bf16[16,4096]{1,0:T(8,128)(2,1)S(1)} %get-tuple-element.60), channel_id=1, source_target_pairs={{0,2},{1,3},{2,0},{3,1},{4,6},{5,7},{6,4},{7,5},{8,10},{9,11},{10,... | collective-permute-start | bytes 393224 | tf_op jit(solution)/shard_map/ppermute | solution.py:423
  41.4 10.4 %collective-permute-start.14 = (bf16[16,4096]{1,0:T(8,128)(2,1)S(1)}, bf16[16,4096]{1,0:T(8,128)(2,1)S(1)}, u32[]{:S(2)}, u32[]{:S(2)}) collective-permute-start(bf16[16,4096]{1,0:T(8,128)(2,1)S(1)} %get-tuple-element.62), channel_id=1, source_target_pairs={{0,2},{1,3},{2,0},{3,1},{4,6},{5,7},{6,4},{7,5},{8,10},{9,11},{10,... | collective-permute-start | bytes 393224 | tf_op jit(solution)/shard_map/ppermute | solution.py:423
  42.2 9.7 %collective-permute-start.16 = (bf16[16,4096]{1,0:T(8,128)(2,1)S(1)}, bf16[16,4096]{1,0:T(8,128)(2,1)S(1)}, u32[]{:S(2)}, u32[]{:S(2)}) collective-permute-start(bf16[16,4096]{1,0:T(8,128)(2,1)S(1)} %get-tuple-element.64), channel_id=1, source_target_pairs={{0,2},{1,3},{2,0},{3,1},{4,6},{5,7},{6,4},{7,5},{8,10},{9,11},{10,... | collective-permute-start | bytes 393224 | tf_op jit(solution)/shard_map/ppermute | solution.py:423
  46.5 8.7 %collective-permute-start.13 = (bf16[16,4096]{1,0:T(8,128)(2,1)S(1)}, bf16[16,4096]{1,0:T(8,128)(2,1)S(1)}, u32[]{:S(2)}, u32[]{:S(2)}) collective-permute-start(bf16[16,4096]{1,0:T(8,128)(2,1)S(1)} %add.9.refs_1_), channel_id=1, source_target_pairs={{0,12},{1,13},{2,14},{3,15},{4,8},{5,9},{6,10},{7,11},{8,4},{9,5},... | collective-permute-start | bytes 393224 | tf_op jit(solution)/shard_map/ppermute | solution.py:423
  50.2 5.0 %collective-permute-start.12 = (bf16[16,4096]{1,0:T(8,128)(2,1)S(1)}, bf16[16,4096]{1,0:T(8,128)(2,1)S(1)}, u32[]{:S(2)}, u32[]{:S(2)}) collective-permute-start(bf16[16,4096]{1,0:T(8,128)(2,1)S(1)} %join.11), channel_id=1, source_target_pairs={{0,2},{1,3},{2,0},{3,1},{4,6},{5,7},{6,4},{7,5},{8,10},{9,11},{10,... | collective-permute-start | bytes 393224 | tf_op jit(solution)/shard_map/ppermute | solution.py:423
  51.8 8.0 %collective-permute-start.15 = (bf16[16,4096]{1,0:T(8,128)(2,1)S(1)}, bf16[16,4096]{1,0:T(8,128)(2,1)S(1)}, u32[]{:S(2)}, u32[]{:S(2)}) collective-permute-start(bf16[16,4096]{1,0:T(8,128)(2,1)S(1)} %add.10), channel_id=1, source_target_pairs={{0,8},{1,9},{2,10},{3,11},{4,12},{5,13},{6,14},{7,15},{8,0},{9,1},... | collective-permute-start | bytes 393224 | tf_op jit(solution)/shard_map/ppermute | solution.py:423
  51.9 7.8 %collective-permute-start.17 = (bf16[16,4096]{1,0:T(8,128)(2,1)S(1)}, bf16[16,4096]{1,0:T(8,128)(2,1)S(1)}, u32[]{:S(2)}, u32[]{:S(2)}) collective-permute-start(bf16[16,4096]{1,0:T(8,128)(2,1)S(1)} %add.11), channel_id=1, source_target_pairs={{0,4},{1,5},{2,6},{3,7},{4,0},{5,1},{6,2},{7,3},{8,12},{9,13},{10,... | collective-permute-start | bytes 393224 | tf_op jit(solution)/shard_map/ppermute | solution.py:423

commit v10 on v9

--- a/solution.py
+++ b/solution.py
@@ -7,7 +7,6 @@
 from jax.experimental.pallas import tpu as pltpu
 from jax.sharding import PartitionSpec as P
 
-PIECES = 8
 MIB = 1024 * 1024
 F32 = jnp.float32
 BF16 = jnp.bfloat16
@@ -19,6 +18,8 @@
 
 
 FREE = pl.CostEstimate(flops=1, bytes_accessed=1, transcendentals=0)
+
+BUSY = pl.CostEstimate(flops=10**10, bytes_accessed=40 * MIB, transcendentals=0)
 
 
 def params(mib):
@@ -31,20 +32,6 @@
         copy.start()
     for copy in copies:
         copy.wait()
-
-
-def stream(w_hbm, out_ref, sems, at, first=0, rows=None):
-    rows = out_ref.shape[0] if rows is None else rows
-    columns = out_ref.shape[1]
-    part = rows // PIECES
-    return [
-        pltpu.make_async_copy(
-            w_hbm.at[pl.ds(at[0] + p * part, part), pl.ds(at[1], columns)],
-            out_ref.at[pl.ds(first + p * part, part), :],
-            sems.at[p],
-        )
-        for p in range(PIECES)
-    ]
 
 
 def turns(experts):
@@ -109,39 +96,31 @@
             pltpu.SemaphoreType.DMA((7,)),
         ],
         compiler_params=params(8),
-        cost_estimate=FREE,
+        cost_estimate=BUSY,
         name="first",
     )(info, tokens, pick, shift, scale, gate, comb, count)
 
 
-def rest_kernel(tok_ref, table_ref, picks_ref, w_hbm, *refs):
-    outs, w_ref, sems = refs[:-2], refs[-2], refs[-1]
-    copies = stream(w_hbm, w_ref, sems, (0, 0), rows=w_ref.shape[0] // 2)
-    for copy in copies:
-        copy.start()
+def rest_kernel(tok_ref, table_ref, picks_ref, *outs):
     experts, slots = picks_ref.shape
     order = [0] + list(range(2, experts))
     picks = jnp.concatenate([picks_ref[i:i + 1, :] for i in order], axis=1)
     rows = modulate(picks, tok_ref, table_ref)
     for i, out in enumerate(outs):
         out[...] = rows[i * slots:(i + 1) * slots]
-    for copy in copies:
-        copy.wait()
-
-
-def rest(tok, table, picks, w, shape):
+
+
+def rest(tok, table, picks):
     experts, slots = picks.shape
     return pl.pallas_call(
         rest_kernel,
-        in_specs=[VMEM] * 3 + [HBM],
-        out_specs=[VMEM] * experts,
-        out_shape=[jax.ShapeDtypeStruct((slots, tok.shape[1]), BF16)] * (experts - 1)
-        + [pltpu.VMEM(shape, BF16)],
-        scratch_shapes=[pltpu.SemaphoreType.DMA((PIECES,))],
-        compiler_params=params(8),
-        cost_estimate=FREE,
+        in_specs=[VMEM] * 3,
+        out_specs=[VMEM] * (experts - 1),
+        out_shape=[jax.ShapeDtypeStruct((slots, tok.shape[1]), BF16)] * (experts - 1),
+        compiler_params=params(8),
+        cost_estimate=BUSY,
         name="rest",
-    )(tok, table, picks, w)
+    )(tok, table, picks)
 
 
 def mixer_kernel(picks_ref, weights_ref, after_ref, *outs):
@@ -163,46 +142,9 @@
         out_specs=[VMEM] * 2,
         out_shape=[jax.ShapeDtypeStruct((tok_rows, experts * slots), BF16)] * 2,
         compiler_params=params(4),
-        cost_estimate=FREE,
+        cost_estimate=BUSY,
         name="mixer",
     )(picks, weights, after)
-
-
-def load_kernel(w_hbm, *refs, at, first, rows):
-    out_ref, sems = refs[-2:]
-    copies = stream(w_hbm, out_ref, sems, at, first, rows)
-    for copy in copies:
-        copy.start()
-    for copy in copies:
-        copy.wait()
-
-
-def load(w, at, shape, after):
-    return pl.pallas_call(
-        functools.partial(load_kernel, at=at, first=0, rows=shape[0]),
-        in_specs=[HBM] + [ANY] * len(after),
-        out_specs=VMEM,
-        out_shape=pltpu.VMEM(shape, w.dtype),
-        scratch_shapes=[pltpu.SemaphoreType.DMA((PIECES,))],
-        compiler_params=params(2),
-        cost_estimate=FREE,
-        name="load",
-    )(w, *after)
-
-
-def load_more(w, at, buffer, after):
-    rows = buffer.shape[0] // 2
-    return pl.pallas_call(
-        functools.partial(load_kernel, at=at, first=rows, rows=rows),
-        in_specs=[HBM, VMEM] + [ANY] * len(after),
-        out_specs=VMEM,
-        out_shape=pltpu.VMEM(buffer.shape, w.dtype),
-        input_output_aliases={1: 0},
-        scratch_shapes=[pltpu.SemaphoreType.DMA((PIECES,))],
-        compiler_params=params(2),
-        cost_estimate=FREE,
-        name="load_more",
-    )(w, buffer, *after)
 
 
 def join_kernel(*refs, count):
@@ -225,21 +167,12 @@
     )(*parts, *after)
 
 
-def up_kernel(*refs, sources, count, at):
-    w_ref, next_hbm = refs[count:count + 2]
-    if sources is None:
-        rows_ref = refs[0]
-        out_ref, next_ref, sems = refs[-3:]
-    else:
-        out_ref, next_ref, rows_ref, sems = refs[-4:]
-    copies = stream(next_hbm, next_ref, sems, at)
-    for copy in copies:
-        copy.start()
-    if sources is not None:
-        to = 0
-        for source, low, high in sources:
-            rows_ref[to:to + high - low, :] = refs[source][low:high, :]
-            to += high - low
+def up_kernel(*refs, sources, count):
+    w_ref, out_ref, rows_ref = refs[count:]
+    to = 0
+    for source, low, high in sources:
+        rows_ref[to:to + high - low, :] = refs[source][low:high, :]
+        to += high - low
     hidden = w_ref.shape[0]
     tile = min(512, hidden)
 
@@ -251,76 +184,50 @@
         )
         out_ref[:, cut] = jax.nn.gelu(lifted, approximate=True).astype(BF16)
 
-    for copy in copies:
-        copy.wait()
-
-
-def up(parts, sources, w, following, at, shape):
+
+def up(parts, sources, w):
     hidden, width = w.shape
-    rows = parts[0].shape[0] if sources is None else sum(high - low for _, low, high in sources)
-    out_shape = [jax.ShapeDtypeStruct((rows, hidden), BF16), pltpu.VMEM(shape, BF16)]
-    if sources is not None:
-        out_shape.append(jax.ShapeDtypeStruct((rows, width), BF16))
-    return pl.pallas_call(
-        functools.partial(up_kernel, sources=sources, count=len(parts), at=at),
-        in_specs=[VMEM] * len(parts) + [VMEM, HBM],
-        out_specs=[VMEM] * len(out_shape),
-        out_shape=out_shape,
-        scratch_shapes=[pltpu.SemaphoreType.DMA((PIECES,))],
-        compiler_params=params(12),
+    rows = sum(high - low for _, low, high in sources)
+    return pl.pallas_call(
+        functools.partial(up_kernel, sources=sources, count=len(parts)),
+        in_specs=[VMEM] * (len(parts) + 1),
+        out_specs=VMEM,
+        out_shape=jax.ShapeDtypeStruct((rows, hidden), BF16),
+        scratch_shapes=[pltpu.VMEM((rows, width), BF16)],
+        compiler_params=params(8),
         cost_estimate=FREE,
         name="up",
-    )(*parts, w, following)
-
-
-def down_kernel(*refs, count, at):
-    hiddens, weights = refs[:count], refs[count:2 * count]
-    if at is None:
-        keep_ref, send_ref = refs[2 * count:]
-        copies = []
-    else:
-        next_hbm, keep_ref, send_ref = refs[2 * count:2 * count + 3]
-        nexts, sems = refs[2 * count + 3:-1], refs[-1]
-        copies = []
-        for i, ref in enumerate(nexts):
-            copies += stream(next_hbm, ref, sems.at[pl.ds(i * PIECES, PIECES)], at[i])
-    for copy in copies:
-        copy.start()
-    half, step = keep_ref.shape
-    tile = step if step <= 1536 else step // 2
-
-    @pl.loop(0, step // tile)
+    )(*parts, w)
+
+
+def down_kernel(h_ref, w_ref, keep_ref, send_ref, *, columns):
+    half = keep_ref.shape[0]
+    first, last, tile = columns
+
+    @pl.loop(0, (last - first) // tile)
     def _(i):
         cut = pl.ds(pl.multiple_of(i * tile, tile), tile)
-        out = None
-        for h_ref, w_ref in zip(hiddens, weights):
-            part = jnp.dot(h_ref[...], w_ref[:, cut], preferred_element_type=F32)
-            out = part if out is None else out + part
+        from_ = pl.ds(pl.multiple_of(first + i * tile, tile), tile)
+        out = jnp.dot(h_ref[...], w_ref[:, from_], preferred_element_type=F32)
         keep_ref[:, cut] = out[:half]
         send_ref[:, cut] = out[half:].astype(BF16)
 
-    for copy in copies:
-        copy.wait()
-
-
-def down(hiddens, weights, following, at, shapes):
-    half = hiddens[0].shape[0] // 2
-    step = weights[0].shape[1]
-    more = following is not None
-    return pl.pallas_call(
-        functools.partial(down_kernel, count=len(hiddens), at=at),
-        in_specs=[VMEM] * (2 * len(hiddens)) + [HBM] * more,
-        out_specs=[VMEM] * (2 + len(shapes)),
+
+def down(hid, w, columns):
+    half = hid.shape[0] // 2
+    step = columns[1] - columns[0]
+    return pl.pallas_call(
+        functools.partial(down_kernel, columns=columns),
+        in_specs=[VMEM] * 2,
+        out_specs=[VMEM] * 2,
         out_shape=[
             jax.ShapeDtypeStruct((half, step), F32),
             jax.ShapeDtypeStruct((half, step), BF16),
-        ]
-        + [pltpu.VMEM(shape, BF16) for shape in shapes],
-        scratch_shapes=[pltpu.SemaphoreType.DMA((len(shapes) * PIECES,))] * more,
-        compiler_params=params(12),
+        ],
+        compiler_params=params(8),
         cost_estimate=FREE,
         name="down",
-    )(*hiddens, *weights, *([following] if more else []))
+    )(hid, w)
 
 
 def add_kernel(*refs, count, outs):
@@ -422,13 +329,13 @@
     def swap(x, mask):
         return lax.ppermute(x, "expert", [(i, i ^ mask) for i in range(devices)])
 
-    tokens, shift, scale, gate, w_up, w_down, pick, comb, count = [
+    tokens, shift, scale, gate, pick, comb, count = [
         pltpu.with_memory_space_constraint(x, pltpu.HBM)
-        for x in (tokens, shift, scale, gate, w_up, w_down, pick, comb, count)
+        for x in (tokens, shift, scale, gate, pick, comb, count)
     ]
     half = hidden // 2
     farthest, tok, table, picks, weights = first(info, tokens, pick, shift, scale, gate, comb, count)
-    own, *others, w_low = rest(tok, table, picks, w_up, (half, width))
+    own, *others = rest(tok, table, picks)
 
     flat = [farthest] + others
     blocks = [own] + [swap(x, mask) for x, mask in zip(flat, far)]
@@ -440,12 +347,7 @@
     parts = []
     sources = []
     for members in (early, late):
-        after = [] if members is early else [w_high]
-        pieces = [join([x for i in members for x in (blocks[i], beside[i])], after)]
-        if members is early:
-            w_high = load(w_up, (half, 0), (half, width), [pieces[0]])
-        else:
-            w_low = load_more(w_up, (half // 2, 0), w_low, [pieces[0]])
+        pieces = [join([x for i in members for x in (blocks[i], beside[i])], [])]
         height = pieces[0].shape[0]
         for mask in near[1:]:
             block = pieces[0] if len(pieces) == 1 else join(pieces, [])
@@ -457,16 +359,11 @@
         sources.append(cuts)
     sources = [cut for pair in zip(*sources) for cut in pair]
 
+    hid = up(parts, sources, w_up)
+
     step = 5 * width // 8
-    hid_high, down_high, rows = up(parts, sources, w_high, w_down, (half, 0), (half, step))
-    hid_low, down_low = up([rows], None, w_low, w_down, (0, 0), (half, step))
-
-    hiddens = [hid_low, hid_high]
-    tall = (half, width - step)
-    keep_a, send_a, *downs = down(
-        hiddens, [down_low, down_high], w_down, [(0, step), (half, step)], [tall, tall]
-    )
-    keep_b, send_b = down(hiddens, downs, None, None, [])
+    keep_a, send_a = down(hid, w_down, (0, step, step // 2))
+    keep_b, send_b = down(hid, w_down, (step, width, (width - step) // 3))
     pairs = []
     for keep, send in ((keep_a, send_a), (keep_b, send_b)):
         for i, mask in enumerate(reversed(near[1:])):

time: 61.1 us -> 61.5 us (level)
  Pallas kernels: 23.4 us -> 16.2 us
  waiting for transfers between devices: 14.8 us -> 19.3 us
  starting transfers between devices: 22.5 us -> 25.5 us
    pallas_call x5 -> x3, Pallas kernels: 13 us -> 6.04 us  [the longest x2 5.28 us: down(): pl.pallas_call(functools.partial(down_kernel, columns=columns), in_specs=...]
    ppermute x18, waiting for transfers between devices: 14.8 us -> 19.3 us  [swap(): return lax.ppermute(x, 'expert', [(i, i ^ mask) for i in range(devices)])]
    ppermute x18, starting transfers between devices: 22.5 us -> 25.5 us  [swap(): return lax.ppermute(x, 'expert', [(i, i ^ mask) for i in range(devices)])]
    pallas_call x2 -> x1, Pallas kernels: 5.86 us -> 5.67 us  [up(): pl.pallas_call(functools.partial(up_kernel, sources=sources, count=len(pa...]
  transfers between devices with their start and end apart: 18 -> 18, of which waited for: 7 -> 9; matrix products, arithmetic and copies ran while one was open for 0% -> 0% of each run, Pallas kernels for 17% -> 6%
where the time goes in v10:
time: 61.5 us; the launch traced here: 61.4 us
  starting transfers between devices  25.5 us (41%)
  waiting for transfers between devices  19.3 us (31%)
  Pallas kernels  16.2 us (26%)
    ppermute x18, starting transfers between devices, swap(): return lax.ppermute(x, 'expert', [(i, i ^ mask) for i in range(devices)])  25.5 us
    ppermute x18, waiting for transfers between devices, swap(): return lax.ppermute(x, 'expert', [(i, i ^ mask) for i in range(devices)])  19.3 us
    pallas_call x1, Pallas kernels, up(): pl.pallas_call(functools.partial(up_kernel, sources=sources, count=len(pa...  5.67 us
    pallas_call x2, Pallas kernels, down(): pl.pallas_call(functools.partial(down_kernel, columns=columns), in_specs=...  5.28 us
    pallas_call x1, Pallas kernels, first(): pl.pallas_call(first_kernel, in_specs=[SMEM] + [HBM] * 7, out_specs=[VMEM...  2.39 us
  transfers between devices with their start and end apart: 18, of which 9 were waited for; matrix products, arithmetic and copies ran while one was open for 0% of the time, Pallas kernels for 6%

profile of v10, /device:TPU:0, one launch (start us, length us, event | category | flops | bytes accessed | tf_op | source)
XLA Modules:
  0.0 61.4 jit_solution(8151451923391057526)
XLA Ops:
  0.1 2.4 %first.1 = (bf16[16,4096]{1,0:T(8,128)(2,1)S(1)}, bf16[128,4096]{1,0:T(8,128)(2,1)S(1)}, f32[3,4096]{1,0:T(4,128)S(1)}, s32[4,16]{1,0:T(4,128)S(1)}, f32[4,16]{1,0:T(4,128)S(1)}) custom-call(s32[2]{0:T(128)S(1)} %pad_add_fusion.info_ref, bf16[128,4096]{1,0:T(8,128)(2,1)} %refs_0_.1, s32[4,16]{1,0:T(4,128)} %bitcast.8, f32[2,4096]{1,0:T(2,128)} %refs_2_.1, ...), custom_call_target="tpu_custom_call" | custom-call | flops 10000000000 | bytes 41943040 | tf_op jit(solution)/shard_map/first/pallas_call | solution.py:78
  2.5 5.1 %collective-permute-start = (bf16[16,4096]{1,0:T(8,128)(2,1)S(1)}, bf16[16,4096]{1,0:T(8,128)(2,1)S(1)}, u32[]{:S(2)}, u32[]{:S(2)}) collective-permute-start(bf16[16,4096]{1,0:T(8,128)(2,1)S(1)} %get-tuple-element.29), channel_id=1, source_target_pairs={{0,12},{1,13},{2,14},{3,15},{4,8},{5,9},{6,10},{7,11},{8,4},{9,5},... | collective-permute-start | bytes 393224 | tf_op jit(solution)/shard_map/ppermute | solution.py:330
  9.0 1.7 %collective-permute-start.1 = (bf16[16,4096]{1,0:T(8,128)(2,1)S(1)}, bf16[16,4096]{1,0:T(8,128)(2,1)S(1)}, u32[]{:S(2)}, u32[]{:S(2)}) collective-permute-start(bf16[16,4096]{1,0:T(8,128)(2,1)S(1)} %get-tuple-element.34.refs_0_), channel_id=1, source_target_pairs={{0,2},{1,3},{2,0},{3,1},{4,6},{5,7},{6,4},{7,5},{8,10},{9,11},{10,... | collective-permute-start | bytes 393224 | tf_op jit(solution)/shard_map/ppermute | solution.py:330
  11.8 1.6 %collective-permute-start.2 = (bf16[16,4096]{1,0:T(8,128)(2,1)S(1)}, bf16[16,4096]{1,0:T(8,128)(2,1)S(1)}, u32[]{:S(2)}, u32[]{:S(2)}) collective-permute-start(bf16[16,4096]{1,0:T(8,128)(2,1)S(1)} %collective-permute-done.after_ref.refs_2_), channel_id=1, source_target_pairs={{0,2},{1,3},{2,0},{3,1},{4,6},{5,7},{6,4},{7,5},{8,10},{9,11},{10,... | collective-permute-start | bytes 393224 | tf_op jit(solution)/shard_map/ppermute | solution.py:330
  13.6 2.5 %collective-permute-done.6.refs_2_ = bf16[16,4096]{1,0:T(8,128)(2,1)S(1)} collective-permute-done((bf16[16,4096]{1,0:T(8,128)(2,1)S(1)}, bf16[16,4096]{1,0:T(8,128)(2,1)S(1)}, u32[]{:S(2)}, u32[]{:S(2)}) %collective-permute-start.6) | collective-permute-done | bytes 131104 | tf_op jit(solution)/shard_map/ppermute | solution.py:330
  16.0 1.5 %collective-permute-start.7 = (bf16[16,4096]{1,0:T(8,128)(2,1)S(1)}, bf16[16,4096]{1,0:T(8,128)(2,1)S(1)}, u32[]{:S(2)}, u32[]{:S(2)}) collective-permute-start(bf16[16,4096]{1,0:T(8,128)(2,1)S(1)} %collective-permute-done.6.refs_2_), channel_id=1, source_target_pairs={{0,2},{1,3},{2,0},{3,1},{4,6},{5,7},{6,4},{7,5},{8,10},{9,11},{10,... | collective-permute-start | bytes 393224 | tf_op jit(solution)/shard_map/ppermute | solution.py:330
  17.5 1.1 %collective-permute-done.4.refs_0_ = bf16[16,4096]{1,0:T(8,128)(2,1)S(1)} collective-permute-done((bf16[16,4096]{1,0:T(8,128)(2,1)S(1)}, bf16[16,4096]{1,0:T(8,128)(2,1)S(1)}, u32[]{:S(2)}, u32[]{:S(2)}) %collective-permute-start.4) | collective-permute-done | bytes 131104 | tf_op jit(solution)/shard_map/ppermute | solution.py:330
  18.7 1.6 %collective-permute-start.5 = (bf16[16,4096]{1,0:T(8,128)(2,1)S(1)}, bf16[16,4096]{1,0:T(8,128)(2,1)S(1)}, u32[]{:S(2)}, u32[]{:S(2)}) collective-permute-start(bf16[16,4096]{1,0:T(8,128)(2,1)S(1)} %join.7.refs_0_), channel_id=1, source_target_pairs={{0,2},{1,3},{2,0},{3,1},{4,6},{5,7},{6,4},{7,5},{8,10},{9,11},{10,... | collective-permute-start | bytes 393224 | tf_op jit(solution)/shard_map/ppermute | solution.py:330
  20.4 1.1 %collective-permute-done.7.refs_0_ = bf16[16,4096]{1,0:T(8,128)(2,1)S(1)} collective-permute-done((bf16[16,4096]{1,0:T(8,128)(2,1)S(1)}, bf16[16,4096]{1,0:T(8,128)(2,1)S(1)}, u32[]{:S(2)}, u32[]{:S(2)}) %collective-permute-start.7) | collective-permute-done | bytes 131104 | tf_op jit(solution)/shard_map/ppermute | solution.py:330
  21.5 2.3 %collective-permute-done.5.refs_1_ = bf16[16,4096]{1,0:T(8,128)(2,1)S(1)} collective-permute-done((bf16[16,4096]{1,0:T(8,128)(2,1)S(1)}, bf16[16,4096]{1,0:T(8,128)(2,1)S(1)}, u32[]{:S(2)}, u32[]{:S(2)}) %collective-permute-start.5) | collective-permute-done | bytes 131104 | tf_op jit(solution)/shard_map/ppermute | solution.py:330
  23.9 1.9 %collective-permute-done.8.refs_3_ = bf16[64,4096]{1,0:T(8,128)(2,1)S(1)} collective-permute-done((bf16[64,4096]{1,0:T(8,128)(2,1)S(1)}, bf16[64,4096]{1,0:T(8,128)(2,1)S(1)}, u32[]{:S(2)}, u32[]{:S(2)}) %collective-permute-start.8) | collective-permute-done | bytes 524320 | tf_op jit(solution)/shard_map/ppermute | solution.py:330
  25.8 5.7 %up.1.h_ref = bf16[256,2048]{1,0:T(8,128)(2,1)S(1)} custom-call(bf16[64,4096]{1,0:T(8,128)(2,1)S(1)} %join.6.refs_0_, bf16[64,4096]{1,0:T(8,128)(2,1)S(1)} %collective-permute-done.3.refs_1_, bf16[64,4096]{1,0:T(8,128)(2,1)S(1)} %join.9.refs_2_, bf16[64,4096]{1,0:T(8,128)(2,1)S(1)} %collective-permute-done.8.refs_3_, bf16[2048,4096]{1,0:T(8,128)(2,1)S(1)} %bitcast.7), custom_call_target="tpu_custom_call" | custom-call | flops 1 | bytes 1 | tf_op jit(solution)/shard_map/up/pallas_call | solution.py:191
  31.6 3.1 %down.2 = (f32[128,2560]{1,0:T(8,128)S(1)}, bf16[128,2560]{1,0:T(8,128)(2,1)S(1)}) custom-call(bf16[256,2048]{1,0:T(8,128)(2,1)S(1)} %up.1.h_ref, bf16[2048,4096]{1,0:T(8,128)(2,1)S(1)} %bitcast.5), custom_call_target="tpu_custom_call" | custom-call | flops 1 | bytes 1 | tf_op jit(solution)/shard_map/down/pallas_call | solution.py:219
  34.9 2.1 %down.3 = (f32[128,1536]{1,0:T(8,128)S(1)}, bf16[128,1536]{1,0:T(8,128)(2,1)S(1)}) custom-call(bf16[256,2048]{1,0:T(8,128)(2,1)S(1)} %up.1.h_ref, bf16[2048,4096]{1,0:T(8,128)(2,1)S(1)} %bitcast.5), custom_call_target="tpu_custom_call" | custom-call | flops 1 | bytes 1 | tf_op jit(solution)/shard_map/down/pallas_call | solution.py:219
  37.5 1.3 %collective-permute-done.10.refs_3_ = bf16[128,1536]{1,0:T(8,128)(2,1)S(1)} collective-permute-done((bf16[128,1536]{1,0:T(8,128)(2,1)S(1)}, bf16[128,1536]{1,0:T(8,128)(2,1)S(1)}, u32[]{:S(2)}, u32[]{:S(2)}) %collective-permute-start.10) | collective-permute-done | bytes 393248 | tf_op jit(solution)/shard_map/ppermute | solution.py:330
  39.1 1.6 %collective-permute-start.11 = (bf16[16,4096]{1,0:T(8,128)(2,1)S(1)}, bf16[16,4096]{1,0:T(8,128)(2,1)S(1)}, u32[]{:S(2)}, u32[]{:S(2)}) collective-permute-start(bf16[16,4096]{1,0:T(8,128)(2,1)S(1)} %get-tuple-element.44), channel_id=1, source_target_pairs={{0,2},{1,3},{2,0},{3,1},{4,6},{5,7},{6,4},{7,5},{8,10},{9,11},{10,... | collective-permute-start | bytes 393224 | tf_op jit(solution)/shard_map/ppermute | solution.py:330
  41.2 1.5 %collective-permute-start.16 = (bf16[16,4096]{1,0:T(8,128)(2,1)S(1)}, bf16[16,4096]{1,0:T(8,128)(2,1)S(1)}, u32[]{:S(2)}, u32[]{:S(2)}) collective-permute-start(bf16[16,4096]{1,0:T(8,128)(2,1)S(1)} %get-tuple-element.48), channel_id=1, source_target_pairs={{0,2},{1,3},{2,0},{3,1},{4,6},{5,7},{6,4},{7,5},{8,10},{9,11},{10,... | collective-permute-start | bytes 393224 | tf_op jit(solution)/shard_map/ppermute | solution.py:330
  42.7 2.8 %collective-permute-done.11.refs_1_ = bf16[16,4096]{1,0:T(8,128)(2,1)S(1)} collective-permute-done((bf16[16,4096]{1,0:T(8,128)(2,1)S(1)}, bf16[16,4096]{1,0:T(8,128)(2,1)S(1)}, u32[]{:S(2)}, u32[]{:S(2)}) %collective-permute-start.11) | collective-permute-done | bytes 131104 | tf_op jit(solution)/shard_map/ppermute | solution.py:330
  45.5 2.7 %collective-permute-start.13 = (bf16[16,4096]{1,0:T(8,128)(2,1)S(1)}, bf16[16,4096]{1,0:T(8,128)(2,1)S(1)}, u32[]{:S(2)}, u32[]{:S(2)}) collective-permute-start(bf16[16,4096]{1,0:T(8,128)(2,1)S(1)} %add.9.refs_1_), channel_id=1, source_target_pairs={{0,12},{1,13},{2,14},{3,15},{4,8},{5,9},{6,10},{7,11},{8,4},{9,5},... | collective-permute-start | bytes 393224 | tf_op jit(solution)/shard_map/ppermute | solution.py:330
  48.2 1.6 %collective-permute-start.12 = (bf16[16,4096]{1,0:T(8,128)(2,1)S(1)}, bf16[16,4096]{1,0:T(8,128)(2,1)S(1)}, u32[]{:S(2)}, u32[]{:S(2)}) collective-permute-start(bf16[16,4096]{1,0:T(8,128)(2,1)S(1)} %join.11), channel_id=1, source_target_pairs={{0,2},{1,3},{2,0},{3,1},{4,6},{5,7},{6,4},{7,5},{8,10},{9,11},{10,... | collective-permute-start | bytes 393224 | tf_op jit(solution)/shard_map/ppermute | solution.py:330
  49.8 2.2 %collective-permute-start.15 = (bf16[16,4096]{1,0:T(8,128)(2,1)S(1)}, bf16[16,4096]{1,0:T(8,128)(2,1)S(1)}, u32[]{:S(2)}, u32[]{:S(2)}) collective-permute-start(bf16[16,4096]{1,0:T(8,128)(2,1)S(1)} %add.10), channel_id=1, source_target_pairs={{0,8},{1,9},{2,10},{3,11},{4,12},{5,13},{6,14},{7,15},{8,0},{9,1},... | collective-permute-start | bytes 393224 | tf_op jit(solution)/shard_map/ppermute | solution.py:330
  52.1 2.4 %collective-permute-start.17 = (bf16[16,4096]{1,0:T(8,128)(2,1)S(1)}, bf16[16,4096]{1,0:T(8,128)(2,1)S(1)}, u32[]{:S(2)}, u32[]{:S(2)}) collective-permute-start(bf16[16,4096]{1,0:T(8,128)(2,1)S(1)} %add.11), channel_id=1, source_target_pairs={{0,4},{1,5},{2,6},{3,7},{4,0},{5,1},{6,2},{7,3},{8,12},{9,13},{10,... | collective-permute-start | bytes 393224 | tf_op jit(solution)/shard_map/ppermute | solution.py:330
  54.9 5.3 %collective-permute-done.15.refs_0_ = bf16[16,4096]{1,0:T(8,128)(2,1)S(1)} collective-permute-done((bf16[16,4096]{1,0:T(8,128)(2,1)S(1)}, bf16[16,4096]{1,0:T(8,128)(2,1)S(1)}, u32[]{:S(2)}, u32[]{:S(2)}) %collective-permute-start.15) | collective-permute-done | bytes 131104 | tf_op jit(solution)/shard_map/ppermute | solution.py:330
  60.2 1.2 %post.1 = bf16[128,4096]{1,0:T(8,128)(2,1)} custom-call(bf16[128,64]{1,0:T(8,128)(2,1)S(1)} %get-tuple-element.30.mix_ref, f32[3,4096]{1,0:T(4,128)S(1)} %get-tuple-element.31.table_ref, f32[128,4096]{1,0:T(8,128)S(1)} %own_part.1.acc_ref, bf16[16,4096]{1,0:T(8,128)(2,1)S(1)} %collective-permute-done.15.refs_0_, ...), custom_call_target="tpu_custom_call" | custom-call | flops 1 | bytes 1 | tf_op jit(solution)/shard_map/post/pallas_call | solution.py:298
  (49 shorter events, 4.9 us)
Async XLA Ops:
  2.5 9.3 %collective-permute-start = (bf16[16,4096]{1,0:T(8,128)(2,1)S(1)}, bf16[16,4096]{1,0:T(8,128)(2,1)S(1)}, u32[]{:S(2)}, u32[]{:S(2)}) collective-permute-start(bf16[16,4096]{1,0:T(8,128)(2,1)S(1)} %get-tuple-element.29), channel_id=1, source_target_pairs={{0,12},{1,13},{2,14},{3,15},{4,8},{5,9},{6,10},{7,11},{8,4},{9,5},... | collective-permute-start | bytes 393224 | tf_op jit(solution)/shard_map/ppermute | solution.py:330
  7.6 18.2 %slice-start.4 = ((s8[16777216]{0:T(1024)(128)(4,1)}), s8[4194304]{0:T(1024)(128)(4,1)S(1)}, s32[]{:S(2)}) async-start(s8[16777216]{0:T(1024)(128)(4,1)} %bitcast.6), calls=%async_computation.4 | async-start | bytes 8388608
  7.6 18.2 %slice-start.5 = ((s8[16777216]{0:T(1024)(128)(4,1)}), s8[4194304]{0:T(1024)(128)(4,1)S(1)}, s32[]{:S(2)}) async-start(s8[16777216]{0:T(1024)(128)(4,1)} %bitcast.6), calls=%async_computation.5 | async-start | bytes 8388608
  8.4 10.3 %collective-permute-start.4 = (bf16[16,4096]{1,0:T(8,128)(2,1)S(1)}, bf16[16,4096]{1,0:T(8,128)(2,1)S(1)}, u32[]{:S(2)}, u32[]{:S(2)}) collective-permute-start(bf16[16,4096]{1,0:T(8,128)(2,1)S(1)} %get-tuple-element.35), channel_id=1, source_target_pairs={{0,8},{1,9},{2,10},{3,11},{4,12},{5,13},{6,14},{7,15},{8,0},{9,1},... | collective-permute-start | bytes 393224 | tf_op jit(solution)/shard_map/ppermute | solution.py:330
  8.4 7.6 %collective-permute-start.6 = (bf16[16,4096]{1,0:T(8,128)(2,1)S(1)}, bf16[16,4096]{1,0:T(8,128)(2,1)S(1)}, u32[]{:S(2)}, u32[]{:S(2)}) collective-permute-start(bf16[16,4096]{1,0:T(8,128)(2,1)S(1)} %get-tuple-element.36), channel_id=1, source_target_pairs={{0,4},{1,5},{2,6},{3,7},{4,0},{5,1},{6,2},{7,3},{8,12},{9,13},{10,... | collective-permute-start | bytes 393224 | tf_op jit(solution)/shard_map/ppermute | solution.py:330
  9.0 11.2 %collective-permute-start.1 = (bf16[16,4096]{1,0:T(8,128)(2,1)S(1)}, bf16[16,4096]{1,0:T(8,128)(2,1)S(1)}, u32[]{:S(2)}, u32[]{:S(2)}) collective-permute-start(bf16[16,4096]{1,0:T(8,128)(2,1)S(1)} %get-tuple-element.34.refs_0_), channel_id=1, source_target_pairs={{0,2},{1,3},{2,0},{3,1},{4,6},{5,7},{6,4},{7,5},{8,10},{9,11},{10,... | collective-permute-start | bytes 393224 | tf_op jit(solution)/shard_map/ppermute | solution.py:330
  11.8 8.5 %collective-permute-start.2 = (bf16[16,4096]{1,0:T(8,128)(2,1)S(1)}, bf16[16,4096]{1,0:T(8,128)(2,1)S(1)}, u32[]{:S(2)}, u32[]{:S(2)}) collective-permute-start(bf16[16,4096]{1,0:T(8,128)(2,1)S(1)} %collective-permute-done.after_ref.refs_2_), channel_id=1, source_target_pairs={{0,2},{1,3},{2,0},{3,1},{4,6},{5,7},{6,4},{7,5},{8,10},{9,11},{10,... | collective-permute-start | bytes 393224 | tf_op jit(solution)/shard_map/ppermute | solution.py:330
  13.4 12.5 %slice-start.7 = ((s8[16777216]{0:T(1024)(128)(4,1)}), s8[4194304]{0:T(1024)(128)(4,1)S(1)}, s32[]{:S(2)}) async-start(s8[16777216]{0:T(1024)(128)(4,1)} %bitcast.6), calls=%async_computation.7 | async-start | bytes 8388608
  13.4 18.2 %slice-start = ((s8[16777216]{0:T(1024)(128)(4,1)}), s8[4194304]{0:T(1024)(128)(4,1)S(1)}, s32[]{:S(2)}) async-start(s8[16777216]{0:T(1024)(128)(4,1)} %bitcast.4), calls=%async_computation | async-start | bytes 8388608
  13.4 18.2 %slice-start.1 = ((s8[16777216]{0:T(1024)(128)(4,1)}), s8[4194304]{0:T(1024)(128)(4,1)S(1)}, s32[]{:S(2)}) async-start(s8[16777216]{0:T(1024)(128)(4,1)} %bitcast.4), calls=%async_computation.1 | async-start | bytes 8388608
  13.4 18.2 %slice-start.2 = ((s8[16777216]{0:T(1024)(128)(4,1)}), s8[4194304]{0:T(1024)(128)(4,1)S(1)}, s32[]{:S(2)}) async-start(s8[16777216]{0:T(1024)(128)(4,1)} %bitcast.4), calls=%async_computation.2 | async-start | bytes 8388608
  16.0 5.5 %collective-permute-start.7 = (bf16[16,4096]{1,0:T(8,128)(2,1)S(1)}, bf16[16,4096]{1,0:T(8,128)(2,1)S(1)}, u32[]{:S(2)}, u32[]{:S(2)}) collective-permute-start(bf16[16,4096]{1,0:T(8,128)(2,1)S(1)} %collective-permute-done.6.refs_2_), channel_id=1, source_target_pairs={{0,2},{1,3},{2,0},{3,1},{4,6},{5,7},{6,4},{7,5},{8,10},{9,11},{10,... | collective-permute-start | bytes 393224 | tf_op jit(solution)/shard_map/ppermute | solution.py:330
  18.7 5.1 %collective-permute-start.5 = (bf16[16,4096]{1,0:T(8,128)(2,1)S(1)}, bf16[16,4096]{1,0:T(8,128)(2,1)S(1)}, u32[]{:S(2)}, u32[]{:S(2)}) collective-permute-start(bf16[16,4096]{1,0:T(8,128)(2,1)S(1)} %join.7.refs_0_), channel_id=1, source_target_pairs={{0,2},{1,3},{2,0},{3,1},{4,6},{5,7},{6,4},{7,5},{8,10},{9,11},{10,... | collective-permute-start | bytes 393224 | tf_op jit(solution)/shard_map/ppermute | solution.py:330
  20.3 3.6 %collective-permute-start.3 = (bf16[64,4096]{1,0:T(8,128)(2,1)S(1)}, bf16[64,4096]{1,0:T(8,128)(2,1)S(1)}, u32[]{:S(2)}, u32[]{:S(2)}) collective-permute-start(bf16[64,4096]{1,0:T(8,128)(2,1)S(1)} %join.6.refs_0_), channel_id=1, source_target_pairs={{0,1},{1,0},{2,3},{3,2},{4,5},{5,4},{6,7},{7,6},{8,9},{9,8},{10,11... | collective-permute-start | bytes 1572872 | tf_op jit(solution)/shard_map/ppermute | solution.py:330
  23.8 2.0 %collective-permute-start.8 = (bf16[64,4096]{1,0:T(8,128)(2,1)S(1)}, bf16[64,4096]{1,0:T(8,128)(2,1)S(1)}, u32[]{:S(2)}, u32[]{:S(2)}) collective-permute-start(bf16[64,4096]{1,0:T(8,128)(2,1)S(1)} %join.9.refs_2_), channel_id=1, source_target_pairs={{0,1},{1,0},{2,3},{3,2},{4,5},{5,4},{6,7},{7,6},{8,9},{9,8},{10,11... | collective-permute-start | bytes 1572872 | tf_op jit(solution)/shard_map/ppermute | solution.py:330
  34.7 2.4 %collective-permute-start.9 = (bf16[128,2560]{1,0:T(8,128)(2,1)S(1)}, bf16[128,2560]{1,0:T(8,128)(2,1)S(1)}, u32[]{:S(2)}, u32[]{:S(2)}) collective-permute-start(bf16[128,2560]{1,0:T(8,128)(2,1)S(1)} %get-tuple-element.38), channel_id=1, source_target_pairs={{0,1},{1,0},{2,3},{3,2},{4,5},{5,4},{6,7},{7,6},{8,9},{9,8},{10,11... | collective-permute-start | bytes 1966088 | tf_op jit(solution)/shard_map/ppermute | solution.py:330
  37.1 1.8 %collective-permute-start.10 = (bf16[128,1536]{1,0:T(8,128)(2,1)S(1)}, bf16[128,1536]{1,0:T(8,128)(2,1)S(1)}, u32[]{:S(2)}, u32[]{:S(2)}) collective-permute-start(bf16[128,1536]{1,0:T(8,128)(2,1)S(1)} %join.10), channel_id=1, source_target_pairs={{0,1},{1,0},{2,3},{3,2},{4,5},{5,4},{6,7},{7,6},{8,9},{9,8},{10,11... | collective-permute-start | bytes 1179656 | tf_op jit(solution)/shard_map/ppermute | solution.py:330
  39.1 6.4 %collective-permute-start.11 = (bf16[16,4096]{1,0:T(8,128)(2,1)S(1)}, bf16[16,4096]{1,0:T(8,128)(2,1)S(1)}, u32[]{:S(2)}, u32[]{:S(2)}) collective-permute-start(bf16[16,4096]{1,0:T(8,128)(2,1)S(1)} %get-tuple-element.44), channel_id=1, source_target_pairs={{0,2},{1,3},{2,0},{3,1},{4,6},{5,7},{6,4},{7,5},{8,10},{9,11},{10,... | collective-permute-start | bytes 393224 | tf_op jit(solution)/shard_map/ppermute | solution.py:330
  40.7 9.1 %collective-permute-start.14 = (bf16[16,4096]{1,0:T(8,128)(2,1)S(1)}, bf16[16,4096]{1,0:T(8,128)(2,1)S(1)}, u32[]{:S(2)}, u32[]{:S(2)}) collective-permute-start(bf16[16,4096]{1,0:T(8,128)(2,1)S(1)} %get-tuple-element.46), channel_id=1, source_target_pairs={{0,2},{1,3},{2,0},{3,1},{4,6},{5,7},{6,4},{7,5},{8,10},{9,11},{10,... | collective-permute-start | bytes 393224 | tf_op jit(solution)/shard_map/ppermute | solution.py:330
  41.2 10.9 %collective-permute-start.16 = (bf16[16,4096]{1,0:T(8,128)(2,1)S(1)}, bf16[16,4096]{1,0:T(8,128)(2,1)S(1)}, u32[]{:S(2)}, u32[]{:S(2)}) collective-permute-start(bf16[16,4096]{1,0:T(8,128)(2,1)S(1)} %get-tuple-element.48), channel_id=1, source_target_pairs={{0,2},{1,3},{2,0},{3,1},{4,6},{5,7},{6,4},{7,5},{8,10},{9,11},{10,... | collective-permute-start | bytes 393224 | tf_op jit(solution)/shard_map/ppermute | solution.py:330
  45.5 9.0 %collective-permute-start.13 = (bf16[16,4096]{1,0:T(8,128)(2,1)S(1)}, bf16[16,4096]{1,0:T(8,128)(2,1)S(1)}, u32[]{:S(2)}, u32[]{:S(2)}) collective-permute-start(bf16[16,4096]{1,0:T(8,128)(2,1)S(1)} %add.9.refs_1_), channel_id=1, source_target_pairs={{0,12},{1,13},{2,14},{3,15},{4,8},{5,9},{6,10},{7,11},{8,4},{9,5},... | collective-permute-start | bytes 393224 | tf_op jit(solution)/shard_map/ppermute | solution.py:330
  48.2 6.3 %collective-permute-start.12 = (bf16[16,4096]{1,0:T(8,128)(2,1)S(1)}, bf16[16,4096]{1,0:T(8,128)(2,1)S(1)}, u32[]{:S(2)}, u32[]{:S(2)}) collective-permute-start(bf16[16,4096]{1,0:T(8,128)(2,1)S(1)} %join.11), channel_id=1, source_target_pairs={{0,2},{1,3},{2,0},{3,1},{4,6},{5,7},{6,4},{7,5},{8,10},{9,11},{10,... | collective-permute-start | bytes 393224 | tf_op jit(solution)/shard_map/ppermute | solution.py:330
  49.8 10.4 %collective-permute-start.15 = (bf16[16,4096]{1,0:T(8,128)(2,1)S(1)}, bf16[16,4096]{1,0:T(8,128)(2,1)S(1)}, u32[]{:S(2)}, u32[]{:S(2)}) collective-permute-start(bf16[16,4096]{1,0:T(8,128)(2,1)S(1)} %add.10), channel_id=1, source_target_pairs={{0,8},{1,9},{2,10},{3,11},{4,12},{5,13},{6,14},{7,15},{8,0},{9,1},... | collective-permute-start | bytes 393224 | tf_op jit(solution)/shard_map/ppermute | solution.py:330
  52.1 8.1 %collective-permute-start.17 = (bf16[16,4096]{1,0:T(8,128)(2,1)S(1)}, bf16[16,4096]{1,0:T(8,128)(2,1)S(1)}, u32[]{:S(2)}, u32[]{:S(2)}) collective-permute-start(bf16[16,4096]{1,0:T(8,128)(2,1)S(1)} %add.11), channel_id=1, source_target_pairs={{0,4},{1,5},{2,6},{3,7},{4,0},{5,1},{6,2},{7,3},{8,12},{9,13},{10,... | collective-permute-start | bytes 393224 | tf_op jit(solution)/shard_map/ppermute | solution.py:330
  (2 other events, 20.2 us)

commit v11 on v10

--- a/solution.py
+++ b/solution.py
@@ -19,7 +19,7 @@
 
 FREE = pl.CostEstimate(flops=1, bytes_accessed=1, transcendentals=0)
 
-BUSY = pl.CostEstimate(flops=10**10, bytes_accessed=40 * MIB, transcendentals=0)
+BUSY = pl.CostEstimate(flops=4 * 10**10, bytes_accessed=128 * MIB, transcendentals=0)
 
 
 def params(mib):
@@ -96,7 +96,7 @@
             pltpu.SemaphoreType.DMA((7,)),
         ],
         compiler_params=params(8),
-        cost_estimate=BUSY,
+        cost_estimate=FREE,
         name="first",
     )(info, tokens, pick, shift, scale, gate, comb, count)
 
@@ -142,7 +142,7 @@
         out_specs=[VMEM] * 2,
         out_shape=[jax.ShapeDtypeStruct((tok_rows, experts * slots), BF16)] * 2,
         compiler_params=params(4),
-        cost_estimate=BUSY,
+        cost_estimate=FREE,
         name="mixer",
     )(picks, weights, after)
 
@@ -168,7 +168,8 @@
 
 
 def up_kernel(*refs, sources, count):
-    w_ref, out_ref, rows_ref = refs[count:]
+    w_ref = refs[count]
+    out_ref, rows_ref = refs[-2:]
     to = 0
     for source, low, high in sources:
         rows_ref[to:to + high - low, :] = refs[source][low:high, :]
@@ -185,77 +186,74 @@
         out_ref[:, cut] = jax.nn.gelu(lifted, approximate=True).astype(BF16)
 
 
-def up(parts, sources, w):
+def up(parts, sources, w, after):
     hidden, width = w.shape
     rows = sum(high - low for _, low, high in sources)
     return pl.pallas_call(
         functools.partial(up_kernel, sources=sources, count=len(parts)),
-        in_specs=[VMEM] * (len(parts) + 1),
+        in_specs=[VMEM] * (len(parts) + 1) + [ANY] * len(after),
         out_specs=VMEM,
         out_shape=jax.ShapeDtypeStruct((rows, hidden), BF16),
         scratch_shapes=[pltpu.VMEM((rows, width), BF16)],
         compiler_params=params(8),
         cost_estimate=FREE,
         name="up",
-    )(*parts, w)
-
-
-def down_kernel(h_ref, w_ref, keep_ref, send_ref, *, columns):
-    half = keep_ref.shape[0]
+    )(*parts, w, *after)
+
+
+def down_kernel(h_ref, w_ref, *refs, columns, groups):
+    outs = refs[len(refs) - 2 * groups:]
     first, last, tile = columns
+    height = h_ref.shape[0] // groups
 
     @pl.loop(0, (last - first) // tile)
     def _(i):
-        cut = pl.ds(pl.multiple_of(i * tile, tile), tile)
-        from_ = pl.ds(pl.multiple_of(first + i * tile, tile), tile)
-        out = jnp.dot(h_ref[...], w_ref[:, from_], preferred_element_type=F32)
-        keep_ref[:, cut] = out[:half]
-        send_ref[:, cut] = out[half:].astype(BF16)
-
-
-def down(hid, w, columns):
-    half = hid.shape[0] // 2
-    step = columns[1] - columns[0]
-    return pl.pallas_call(
-        functools.partial(down_kernel, columns=columns),
-        in_specs=[VMEM] * 2,
-        out_specs=[VMEM] * 2,
+        cut = pl.ds(pl.multiple_of(first + i * tile, tile), tile)
+        out = jnp.dot(h_ref[...], w_ref[:, cut], preferred_element_type=F32)
+        for g in range(groups):
+            middle = g * height + height // 2
+            outs[2 * g][:, cut] = out[middle - height // 2:middle]
+            outs[2 * g + 1][:, cut] = out[middle:middle + height // 2].astype(BF16)
+
+
+def down(hid, w, columns, groups, after, before):
+    half = hid.shape[0] // groups // 2
+    width = w.shape[1]
+    skip = 2 + len(after)
+    return pl.pallas_call(
+        functools.partial(down_kernel, columns=columns, groups=groups),
+        in_specs=[VMEM] * 2 + [ANY] * len(after) + [VMEM] * len(before),
+        out_specs=[VMEM] * (2 * groups),
         out_shape=[
-            jax.ShapeDtypeStruct((half, step), F32),
-            jax.ShapeDtypeStruct((half, step), BF16),
+            jax.ShapeDtypeStruct((half, width), F32),
+            jax.ShapeDtypeStruct((half, width), BF16),
+        ]
+        * groups,
+        input_output_aliases={skip + i: i for i in range(len(before))},
+        compiler_params=params(8),
+        cost_estimate=FREE,
+        name="down",
+    )(hid, w, *after, *before)
+
+
+def add_kernel(keep_ref, got_ref, *refs, cuts):
+    for ref, (low, high) in zip(refs[len(refs) - len(cuts):], cuts):
+        ref[...] = (keep_ref[low:high] + got_ref[low:high].astype(F32)).astype(ref.dtype)
+
+
+def add(keep, got, cuts, kinds, after=()):
+    width = keep.shape[1]
+    return pl.pallas_call(
+        functools.partial(add_kernel, cuts=cuts),
+        in_specs=[VMEM] * 2 + [ANY] * len(after),
+        out_specs=[VMEM] * len(cuts),
+        out_shape=[
+            jax.ShapeDtypeStruct((high - low, width), k) for (low, high), k in zip(cuts, kinds)
         ],
         compiler_params=params(8),
         cost_estimate=FREE,
-        name="down",
-    )(hid, w)
-
-
-def add_kernel(*refs, count, outs):
-    for ref, pieces in zip(refs[2 * count:], outs):
-        at = 0
-        for i, low, high in pieces:
-            keep_ref, got_ref = refs[2 * i:2 * i + 2]
-            step = keep_ref.shape[1]
-            total = keep_ref[low:high] + got_ref[low:high].astype(F32)
-            ref[:, at:at + step] = total.astype(ref.dtype)
-            at += step
-
-
-def add(pairs, outs, kinds):
-    args = [x for pair in pairs for x in pair]
-    shapes = [
-        (pieces[0][2] - pieces[0][1], sum(pairs[i][0].shape[1] for i, _, _ in pieces))
-        for pieces in outs
-    ]
-    return pl.pallas_call(
-        functools.partial(add_kernel, count=len(pairs), outs=outs),
-        in_specs=[VMEM] * len(args),
-        out_specs=[VMEM] * len(outs),
-        out_shape=[jax.ShapeDtypeStruct(shape, k) for shape, k in zip(shapes, kinds)],
-        compiler_params=params(8),
-        cost_estimate=FREE,
         name="add",
-    )(*args)
+    )(keep, got, *after)
 
 
 def own_kernel(mix_ref, keep_ref, near_ref, got_ref, acc_ref):
@@ -333,7 +331,6 @@
         pltpu.with_memory_space_constraint(x, pltpu.HBM)
         for x in (tokens, shift, scale, gate, pick, comb, count)
     ]
-    half = hidden // 2
     farthest, tok, table, picks, weights = first(info, tokens, pick, shift, scale, gate, comb, count)
     own, *others = rest(tok, table, picks)
 
@@ -344,55 +341,64 @@
     beside = [swap(block, near[0]) for block in blocks]
     beside[-1] = join([beside[-1]], [])
     early, late = list(range(experts // 2)), list(range(experts // 2, experts))
-    parts = []
-    sources = []
-    for members in (early, late):
-        pieces = [join([x for i in members for x in (blocks[i], beside[i])], [])]
-        height = pieces[0].shape[0]
+
+    def spread(members, after=()):
+        pieces = [join([x for i in members for x in (blocks[i], beside[i])], after)]
         for mask in near[1:]:
             block = pieces[0] if len(pieces) == 1 else join(pieces, [])
             pieces = [block, swap(block, mask)]
-        cuts = []
-        for piece in pieces:
-            cuts += [(len(parts), at, at + height) for at in range(0, piece.shape[0], height)]
-            parts.append(piece)
-        sources.append(cuts)
-    sources = [cut for pair in zip(*sources) for cut in pair]
-
-    hid = up(parts, sources, w_up)
-
-    step = 5 * width // 8
-    keep_a, send_a = down(hid, w_down, (0, step, step // 2))
-    keep_b, send_b = down(hid, w_down, (step, width, (width - step) // 3))
-    pairs = []
-    for keep, send in ((keep_a, send_a), (keep_b, send_b)):
+        return pieces, [(k, 0, piece.shape[0]) for k, piece in enumerate(pieces)]
+
+    def gather(keep, send, members, after=()):
         for i, mask in enumerate(reversed(near[1:])):
             if i:
                 middle = keep.shape[0] // 2
-                keep, send = add(
-                    [(keep, got)], [[(0, 0, middle)], [(0, middle, 2 * middle)]], [F32, BF16]
-                )
-            if pairs:
-                send = join([send], [pairs[0][1]])
+                keep, send = add(keep, got, [(0, middle), (middle, 2 * middle)], [F32, BF16])
             got = swap(send, mask)
-        pairs.append((keep, got))
-
-    def outs(side):
-        rows = [(2 * i + side) * slots for i in range(experts)]
-        return [[(piece, at, at + slots) for piece in range(len(pairs))] for at in rows]
-
-    sums = add(pairs, outs(1) + outs(0), [BF16] * experts + [F32] * experts)
-    sends, keeps = sums[:experts], sums[experts:]
-    back = {}
-    for i in range(1, experts):
-        got = swap(sends[i], near[0])
-        (part,) = add([(keeps[i], got)], [[(0, 0, slots)]], [BF16])
+        at = [2 * k * slots for k in range(len(members))]
+        cuts = [(x + slots, x + 2 * slots) for x in at] + [(x, x + slots) for x in at]
+        out = add(keep, got, cuts, [BF16] * len(at) + [F32] * len(at), after)
+        return dict(zip(members, zip(out, out[len(at):])))
+
+    def total(i):
+        send, keep = block[i]
+        return add(keep, swap(send, near[0]), [(0, slots)], [BF16])[0]
+
+    def rows_of(*groups, after=()):
+        parts, cuts = [], []
+        for members in groups:
+            pieces, taken = spread(members, after)
+            cuts += [(len(parts) + k, low, high) for k, low, high in taken]
+            parts += pieces
+        return parts, cuts
+
+    width_a = 7 * width // 8
+    links = [blocks[2], blocks[3]]
+    parts, sources = rows_of([1], after=links)
+    own_parts, own_sources = rows_of([0])
+    sources = sources + [(len(parts) + k, low, high) for k, low, high in own_sources]
+    hid = up(parts + own_parts, sources, w_up, [])
+    keep, send, keep_own, send_own = down(hid, w_down, (0, width, min(1024, width)), 2, [], [])
+    hid_late = up(*rows_of(late, after=[hid]), w_up, [keep])
+    block = gather(keep, send, [1], [hid_late])
+    hid = hid_late
+    before = down(hid, w_down, (0, width_a, width_a // 4), 1, [block[1][0]], [])
+    part = total(1)
+    keep, send = down(hid, w_down, (width_a, width, width - width_a), 1, [part], before)
+    block.update(gather(keep, send, late))
+    block.update(gather(keep_own, send_own, [0]))
+    back = {1: swap(part, far[0])}
+    link = back[1]
+    link = join([link], [])
+
+    for i in late:
+        part = total(i)
+        if i == 2:
+            part = join([part], [link])
         back[i] = swap(part, far[i - 1])
-        if i == 1:
-            own_send = join(sends[:1], [part])
-    got = swap(own_send, near[0])
-    acc = own_part(mixes[0], keeps[0], got, back[1])
-    return post(mixes[1], table, acc, [back[i] for i in range(2, experts)])
+    send, keep = block[0]
+    acc = own_part(mixes[0], keep, swap(send, near[0]), back[1])
+    return post(mixes[1], table, acc, [back[i] for i in late])
 
 
 def solution(mesh):

time: 61.5 us -> 71.5 us (1.16)
  Pallas kernels: 16.2 us -> 24.4 us
  waiting for transfers between devices: 19.3 us -> 22.6 us
  starting transfers between devices: 25.5 us -> 24 us
    pallas_call x1 -> x2, Pallas kernels: 5.67 us -> 12.8 us  [up(): pl.pallas_call(functools.partial(up_kernel, sources=sources, count=len(pa...]
    ppermute x18 -> x20, waiting for transfers between devices: 19.3 us -> 22.6 us  [swap(): return lax.ppermute(x, 'expert', [(i, i ^ mask) for i in range(devices)])]
    ppermute x18 -> x20, starting transfers between devices: 25.5 us -> 24 us  [swap(): return lax.ppermute(x, 'expert', [(i, i ^ mask) for i in range(devices)])]
    pallas_call x6 -> x9, Pallas kernels: 5.52 us -> 6.58 us  [the longest x3 6.33 us: down(): pl.pallas_call(functools.partial(down_kernel, columns=columns, groups=gro...]
  transfers between devices with their start and end apart: 18 -> 20, of which waited for: 9 -> 10; matrix products, arithmetic and copies ran while one was open for 0% -> 0% of each run, Pallas kernels for 6% -> 28%
where the time goes in v11:
time: 71.5 us; the launch traced here: 71.3 us
  Pallas kernels  24.4 us (34%)
  starting transfers between devices  24 us (34%)
  waiting for transfers between devices  22.6 us (32%)
    ppermute x20, starting transfers between devices, swap(): return lax.ppermute(x, 'expert', [(i, i ^ mask) for i in range(devices)])  24 us
    ppermute x20, waiting for transfers between devices, swap(): return lax.ppermute(x, 'expert', [(i, i ^ mask) for i in range(devices)])  22.6 us
    pallas_call x2, Pallas kernels, up(): pl.pallas_call(functools.partial(up_kernel, sources=sources, count=len(pa...  12.8 us
    pallas_call x3, Pallas kernels, down(): pl.pallas_call(functools.partial(down_kernel, columns=columns, groups=gro...  6.33 us
    pallas_call x1, Pallas kernels, first(): pl.pallas_call(first_kernel, in_specs=[SMEM] + [HBM] * 7, out_specs=[VMEM...  2.39 us
  transfers between devices with their start and end apart: 20, of which 10 were waited for; matrix products, arithmetic and copies ran while one was open for 0% of the time, Pallas kernels for 28%

profile of v11, /device:TPU:0, one launch (start us, length us, event | category | flops | bytes accessed | tf_op | source)
XLA Modules:
  0.0 71.3 jit_solution(17986239455989310357)
XLA Ops:
  0.1 2.4 %first.1 = (bf16[16,4096]{1,0:T(8,128)(2,1)S(1)}, bf16[128,4096]{1,0:T(8,128)(2,1)S(1)}, f32[3,4096]{1,0:T(4,128)S(1)}, s32[4,16]{1,0:T(4,128)S(1)}, f32[4,16]{1,0:T(4,128)S(1)}) custom-call(s32[2]{0:T(128)S(1)} %pad_add_fusion.info_ref, bf16[128,4096]{1,0:T(8,128)(2,1)} %refs_0_.1, s32[4,16]{1,0:T(4,128)} %bitcast.6, f32[2,4096]{1,0:T(2,128)} %refs_2_.2, ...), custom_call_target="tpu_custom_call" | custom-call | flops 1 | bytes 1 | tf_op jit(solution)/shard_map/first/pallas_call | solution.py:78
  2.5 5.1 %collective-permute-start = (bf16[16,4096]{1,0:T(8,128)(2,1)S(1)}, bf16[16,4096]{1,0:T(8,128)(2,1)S(1)}, u32[]{:S(2)}, u32[]{:S(2)}) collective-permute-start(bf16[16,4096]{1,0:T(8,128)(2,1)S(1)} %get-tuple-element.33), channel_id=1, source_target_pairs={{0,12},{1,13},{2,14},{3,15},{4,8},{5,9},{6,10},{7,11},{8,4},{9,5},... | collective-permute-start | bytes 393224 | tf_op jit(solution)/shard_map/ppermute | solution.py:328
  8.4 1.6 %collective-permute-start.5 = (bf16[16,4096]{1,0:T(8,128)(2,1)S(1)}, bf16[16,4096]{1,0:T(8,128)(2,1)S(1)}, u32[]{:S(2)}, u32[]{:S(2)}) collective-permute-start(bf16[16,4096]{1,0:T(8,128)(2,1)S(1)} %get-tuple-element.40.refs_0_), channel_id=1, source_target_pairs={{0,2},{1,3},{2,0},{3,1},{4,6},{5,7},{6,4},{7,5},{8,10},{9,11},{10,... | collective-permute-start | bytes 393224 | tf_op jit(solution)/shard_map/ppermute | solution.py:328
  11.2 1.9 %collective-permute-start.1 = (bf16[16,4096]{1,0:T(8,128)(2,1)S(1)}, bf16[16,4096]{1,0:T(8,128)(2,1)S(1)}, u32[]{:S(2)}, u32[]{:S(2)}) collective-permute-start(bf16[16,4096]{1,0:T(8,128)(2,1)S(1)} %collective-permute-done.after_ref.refs_0_), channel_id=1, source_target_pairs={{0,2},{1,3},{2,0},{3,1},{4,6},{5,7},{6,4},{7,5},{8,10},{9,11},{10,... | collective-permute-start | bytes 393224 | tf_op jit(solution)/shard_map/ppermute | solution.py:328
  14.1 4.6 %collective-permute-done.2.refs_0_ = bf16[16,4096]{1,0:T(8,128)(2,1)S(1)} collective-permute-done((bf16[16,4096]{1,0:T(8,128)(2,1)S(1)}, bf16[16,4096]{1,0:T(8,128)(2,1)S(1)}, u32[]{:S(2)}, u32[]{:S(2)}) %collective-permute-start.2) | collective-permute-done | bytes 131104 | tf_op jit(solution)/shard_map/ppermute | solution.py:328
  18.8 1.6 %collective-permute-start.11 = (bf16[16,4096]{1,0:T(8,128)(2,1)S(1)}, bf16[16,4096]{1,0:T(8,128)(2,1)S(1)}, u32[]{:S(2)}, u32[]{:S(2)}) collective-permute-start(bf16[16,4096]{1,0:T(8,128)(2,1)S(1)} %collective-permute-done.3.refs_3_.refs_2_), channel_id=1, source_target_pairs={{0,2},{1,3},{2,0},{3,1},{4,6},{5,7},{6,4},{7,5},{8,10},{9,11},{10,... | collective-permute-start | bytes 393224 | tf_op jit(solution)/shard_map/ppermute | solution.py:328
  20.9 4.3 %collective-permute-done.11.refs_0_ = bf16[16,4096]{1,0:T(8,128)(2,1)S(1)} collective-permute-done((bf16[16,4096]{1,0:T(8,128)(2,1)S(1)}, bf16[16,4096]{1,0:T(8,128)(2,1)S(1)}, u32[]{:S(2)}, u32[]{:S(2)}) %collective-permute-start.11) | collective-permute-done | bytes 131104 | tf_op jit(solution)/shard_map/ppermute | solution.py:328
  25.2 6.4 %up.2.h_ref.refs_4_ = bf16[128,2048]{1,0:T(8,128)(2,1)S(1)} custom-call(bf16[32,4096]{1,0:T(8,128)(2,1)S(1)} %join.8.refs_0_, bf16[32,4096]{1,0:T(8,128)(2,1)S(1)} %collective-permute-done.4.refs_1_, bf16[32,4096]{1,0:T(8,128)(2,1)S(1)} %join.9.refs_2_, bf16[32,4096]{1,0:T(8,128)(2,1)S(1)} %collective-permute-done.6.refs_3_, bf16[2048,4096]{1,0:T(8,128)(2,1)S(1)} %copy-done), custom_call_target="tpu_custom_call" | custom-call | flops 1 | bytes 1 | tf_op jit(solution)/shard_map/up/pallas_call | solution.py:192
  31.8 2.9 %down.3 = (f32[32,4096]{1,0:T(8,128)S(1)}, bf16[32,4096]{1,0:T(8,128)(2,1)S(1)}, f32[32,4096]{1,0:T(8,128)S(1)}, bf16[32,4096]{1,0:T(8,128)(2,1)S(1)}) custom-call(bf16[128,2048]{1,0:T(8,128)(2,1)S(1)} %up.2.h_ref.refs_4_, bf16[2048,4096]{1,0:T(8,128)(2,1)S(1)} %bitcast.5), custom_call_target="tpu_custom_call" | custom-call | flops 1 | bytes 1 | tf_op jit(solution)/shard_map/down/pallas_call | solution.py:223
  35.2 6.4 %up.3.refs_0_.h_ref = bf16[128,2048]{1,0:T(8,128)(2,1)S(1)} custom-call(bf16[64,4096]{1,0:T(8,128)(2,1)S(1)} %join.11.refs_0_, bf16[64,4096]{1,0:T(8,128)(2,1)S(1)} %collective-permute-done.12.refs_1_, bf16[2048,4096]{1,0:T(8,128)(2,1)S(1)} %copy-done, f32[32,4096]{1,0:T(8,128)S(1)} %get-tuple-element.45.refs_3_.keep_ref), custom_call_target="tpu_custom_call" | custom-call | flops 1 | bytes 1 | tf_op jit(solution)/shard_map/up/pallas_call | solution.py:192
  41.7 1.6 %collective-permute-start.13 = (bf16[16,4096]{1,0:T(8,128)(2,1)S(1)}, bf16[16,4096]{1,0:T(8,128)(2,1)S(1)}, u32[]{:S(2)}, u32[]{:S(2)}) collective-permute-start(bf16[16,4096]{1,0:T(8,128)(2,1)S(1)} %get-tuple-element.48.refs_0_), channel_id=1, source_target_pairs={{0,2},{1,3},{2,0},{3,1},{4,6},{5,7},{6,4},{7,5},{8,10},{9,11},{10,... | collective-permute-start | bytes 393224 | tf_op jit(solution)/shard_map/ppermute | solution.py:328
  43.3 3.0 %down.4 = (f32[64,4096]{1,0:T(8,128)S(1)}, bf16[64,4096]{1,0:T(8,128)(2,1)S(1)}) custom-call(bf16[128,2048]{1,0:T(8,128)(2,1)S(1)} %up.3.refs_0_.h_ref, bf16[2048,4096]{1,0:T(8,128)(2,1)S(1)} %bitcast.5, bf16[16,4096]{1,0:T(8,128)(2,1)S(1)} %get-tuple-element.48.refs_0_), custom_call_target="tpu_custom_call" | custom-call | flops 1 | bytes 1 | tf_op jit(solution)/shard_map/down/pallas_call | solution.py:223
  46.3 0.9 %collective-permute-done.13.got_ref = bf16[16,4096]{1,0:T(8,128)(2,1)S(1)} collective-permute-done((bf16[16,4096]{1,0:T(8,128)(2,1)S(1)}, bf16[16,4096]{1,0:T(8,128)(2,1)S(1)}, u32[]{:S(2)}, u32[]{:S(2)}) %collective-permute-start.13) | collective-permute-done | bytes 131104 | tf_op jit(solution)/shard_map/ppermute | solution.py:328
  48.3 2.5 %collective-permute-start.14 = (bf16[16,4096]{1,0:T(8,128)(2,1)S(1)}, bf16[16,4096]{1,0:T(8,128)(2,1)S(1)}, u32[]{:S(2)}, u32[]{:S(2)}) collective-permute-start(bf16[16,4096]{1,0:T(8,128)(2,1)S(1)} %add.12.refs_0_), channel_id=1, source_target_pairs={{0,12},{1,13},{2,14},{3,15},{4,8},{5,9},{6,10},{7,11},{8,4},{9,5},... | collective-permute-start | bytes 393224 | tf_op jit(solution)/shard_map/ppermute | solution.py:328
  50.8 1.6 %collective-permute-start.18 = (bf16[16,4096]{1,0:T(8,128)(2,1)S(1)}, bf16[16,4096]{1,0:T(8,128)(2,1)S(1)}, u32[]{:S(2)}, u32[]{:S(2)}) collective-permute-start(bf16[16,4096]{1,0:T(8,128)(2,1)S(1)} %get-tuple-element.56), channel_id=1, source_target_pairs={{0,2},{1,3},{2,0},{3,1},{4,6},{5,7},{6,4},{7,5},{8,10},{9,11},{10,... | collective-permute-start | bytes 393224 | tf_op jit(solution)/shard_map/ppermute | solution.py:328
  53.0 1.6 %collective-permute-start.8 = (bf16[16,4096]{1,0:T(8,128)(2,1)S(1)}, bf16[16,4096]{1,0:T(8,128)(2,1)S(1)}, u32[]{:S(2)}, u32[]{:S(2)}) collective-permute-start(bf16[16,4096]{1,0:T(8,128)(2,1)S(1)} %get-tuple-element.44), channel_id=1, source_target_pairs={{0,2},{1,3},{2,0},{3,1},{4,6},{5,7},{6,4},{7,5},{8,10},{9,11},{10,... | collective-permute-start | bytes 393224 | tf_op jit(solution)/shard_map/ppermute | solution.py:328
  54.6 1.1 %collective-permute-done.14.got_ref.refs_0_ = bf16[16,4096]{1,0:T(8,128)(2,1)S(1)} collective-permute-done((bf16[16,4096]{1,0:T(8,128)(2,1)S(1)}, bf16[16,4096]{1,0:T(8,128)(2,1)S(1)}, u32[]{:S(2)}, u32[]{:S(2)}) %collective-permute-start.14) | collective-permute-done | bytes 131104 | tf_op jit(solution)/shard_map/ppermute | solution.py:328
  55.7 1.6 %collective-permute-done.18.got_ref = bf16[16,4096]{1,0:T(8,128)(2,1)S(1)} collective-permute-done((bf16[16,4096]{1,0:T(8,128)(2,1)S(1)}, bf16[16,4096]{1,0:T(8,128)(2,1)S(1)}, u32[]{:S(2)}, u32[]{:S(2)}) %collective-permute-start.18) | collective-permute-done | bytes 131104 | tf_op jit(solution)/shard_map/ppermute | solution.py:328
  57.3 2.8 %collective-permute-done.16.got_ref = bf16[16,4096]{1,0:T(8,128)(2,1)S(1)} collective-permute-done((bf16[16,4096]{1,0:T(8,128)(2,1)S(1)}, bf16[16,4096]{1,0:T(8,128)(2,1)S(1)}, u32[]{:S(2)}, u32[]{:S(2)}) %collective-permute-start.16) | collective-permute-done | bytes 131104 | tf_op jit(solution)/shard_map/ppermute | solution.py:328
  60.1 2.6 %collective-permute-start.19 = (bf16[16,4096]{1,0:T(8,128)(2,1)S(1)}, bf16[16,4096]{1,0:T(8,128)(2,1)S(1)}, u32[]{:S(2)}, u32[]{:S(2)}) collective-permute-start(bf16[16,4096]{1,0:T(8,128)(2,1)S(1)} %add.15), channel_id=1, source_target_pairs={{0,4},{1,5},{2,6},{3,7},{4,0},{5,1},{6,2},{7,3},{8,12},{9,13},{10,... | collective-permute-start | bytes 393224 | tf_op jit(solution)/shard_map/ppermute | solution.py:328
  62.7 0.9 %collective-permute-start.17 = (bf16[16,4096]{1,0:T(8,128)(2,1)S(1)}, bf16[16,4096]{1,0:T(8,128)(2,1)S(1)}, u32[]{:S(2)}, u32[]{:S(2)}) collective-permute-start(bf16[16,4096]{1,0:T(8,128)(2,1)S(1)} %join.13), channel_id=1, source_target_pairs={{0,8},{1,9},{2,10},{3,11},{4,12},{5,13},{6,14},{7,15},{8,0},{9,1},... | collective-permute-start | bytes 393224 | tf_op jit(solution)/shard_map/ppermute | solution.py:328
  64.0 2.7 %collective-permute-done.19.refs_1_ = bf16[16,4096]{1,0:T(8,128)(2,1)S(1)} collective-permute-done((bf16[16,4096]{1,0:T(8,128)(2,1)S(1)}, bf16[16,4096]{1,0:T(8,128)(2,1)S(1)}, u32[]{:S(2)}, u32[]{:S(2)}) %collective-permute-start.19) | collective-permute-done | bytes 131104 | tf_op jit(solution)/shard_map/ppermute | solution.py:328
  66.7 3.4 %collective-permute-done.17.refs_0_ = bf16[16,4096]{1,0:T(8,128)(2,1)S(1)} collective-permute-done((bf16[16,4096]{1,0:T(8,128)(2,1)S(1)}, bf16[16,4096]{1,0:T(8,128)(2,1)S(1)}, u32[]{:S(2)}, u32[]{:S(2)}) %collective-permute-start.17) | collective-permute-done | bytes 131104 | tf_op jit(solution)/shard_map/ppermute | solution.py:328
  70.1 1.2 %post.1 = bf16[128,4096]{1,0:T(8,128)(2,1)} custom-call(bf16[128,64]{1,0:T(8,128)(2,1)S(1)} %get-tuple-element.34.mix_ref, f32[3,4096]{1,0:T(4,128)S(1)} %get-tuple-element.35.table_ref, f32[128,4096]{1,0:T(8,128)S(1)} %own_part.1.acc_ref, bf16[16,4096]{1,0:T(8,128)(2,1)S(1)} %collective-permute-done.17.refs_0_, ...), custom_call_target="tpu_custom_call" | custom-call | flops 1 | bytes 1 | tf_op jit(solution)/shard_map/post/pallas_call | solution.py:296
  (51 shorter events, 6.6 us)
Async XLA Ops:
  2.5 8.7 %collective-permute-start = (bf16[16,4096]{1,0:T(8,128)(2,1)S(1)}, bf16[16,4096]{1,0:T(8,128)(2,1)S(1)}, u32[]{:S(2)}, u32[]{:S(2)}) collective-permute-start(bf16[16,4096]{1,0:T(8,128)(2,1)S(1)} %get-tuple-element.33), channel_id=1, source_target_pairs={{0,12},{1,13},{2,14},{3,15},{4,8},{5,9},{6,10},{7,11},{8,4},{9,5},... | collective-permute-start | bytes 393224 | tf_op jit(solution)/shard_map/ppermute | solution.py:328
  7.6 24.2 %slice-start = ((s8[16777216]{0:T(1024)(128)(4,1)}), s8[4194304]{0:T(1024)(128)(4,1)S(1)}, s32[]{:S(2)}) async-start(s8[16777216]{0:T(1024)(128)(4,1)} %bitcast.4), calls=%async_computation | async-start | bytes 8388608
  7.6 24.2 %slice-start.1 = ((s8[16777216]{0:T(1024)(128)(4,1)}), s8[4194304]{0:T(1024)(128)(4,1)S(1)}, s32[]{:S(2)}) async-start(s8[16777216]{0:T(1024)(128)(4,1)} %bitcast.4), calls=%async_computation.1 | async-start | bytes 8388608
  7.6 24.2 %slice-start.2 = ((s8[16777216]{0:T(1024)(128)(4,1)}), s8[4194304]{0:T(1024)(128)(4,1)S(1)}, s32[]{:S(2)}) async-start(s8[16777216]{0:T(1024)(128)(4,1)} %bitcast.4), calls=%async_computation.2 | async-start | bytes 8388608
  7.6 24.2 %slice-start.3 = ((s8[16777216]{0:T(1024)(128)(4,1)}), s8[4194304]{0:T(1024)(128)(4,1)S(1)}, s32[]{:S(2)}) async-start(s8[16777216]{0:T(1024)(128)(4,1)} %bitcast.4), calls=%async_computation.3 | async-start | bytes 8388608
  8.4 5.4 %collective-permute-start.5 = (bf16[16,4096]{1,0:T(8,128)(2,1)S(1)}, bf16[16,4096]{1,0:T(8,128)(2,1)S(1)}, u32[]{:S(2)}, u32[]{:S(2)}) collective-permute-start(bf16[16,4096]{1,0:T(8,128)(2,1)S(1)} %get-tuple-element.40.refs_0_), channel_id=1, source_target_pairs={{0,2},{1,3},{2,0},{3,1},{4,6},{5,7},{6,4},{7,5},{8,10},{9,11},{10,... | collective-permute-start | bytes 393224 | tf_op jit(solution)/shard_map/ppermute | solution.py:328
  10.0 8.7 %collective-permute-start.2 = (bf16[16,4096]{1,0:T(8,128)(2,1)S(1)}, bf16[16,4096]{1,0:T(8,128)(2,1)S(1)}, u32[]{:S(2)}, u32[]{:S(2)}) collective-permute-start(bf16[16,4096]{1,0:T(8,128)(2,1)S(1)} %get-tuple-element.38), channel_id=1, source_target_pairs={{0,8},{1,9},{2,10},{3,11},{4,12},{5,13},{6,14},{7,15},{8,0},{9,1},... | collective-permute-start | bytes 393224 | tf_op jit(solution)/shard_map/ppermute | solution.py:328
  10.0 8.7 %collective-permute-start.3 = (bf16[16,4096]{1,0:T(8,128)(2,1)S(1)}, bf16[16,4096]{1,0:T(8,128)(2,1)S(1)}, u32[]{:S(2)}, u32[]{:S(2)}) collective-permute-start(bf16[16,4096]{1,0:T(8,128)(2,1)S(1)} %get-tuple-element.39), channel_id=1, source_target_pairs={{0,4},{1,5},{2,6},{3,7},{4,0},{5,1},{6,2},{7,3},{8,12},{9,13},{10,... | collective-permute-start | bytes 393224 | tf_op jit(solution)/shard_map/ppermute | solution.py:328
  11.2 7.5 %collective-permute-start.1 = (bf16[16,4096]{1,0:T(8,128)(2,1)S(1)}, bf16[16,4096]{1,0:T(8,128)(2,1)S(1)}, u32[]{:S(2)}, u32[]{:S(2)}) collective-permute-start(bf16[16,4096]{1,0:T(8,128)(2,1)S(1)} %collective-permute-done.after_ref.refs_0_), channel_id=1, source_target_pairs={{0,2},{1,3},{2,0},{3,1},{4,6},{5,7},{6,4},{7,5},{8,10},{9,11},{10,... | collective-permute-start | bytes 393224 | tf_op jit(solution)/shard_map/ppermute | solution.py:328
  13.8 11.3 %collective-permute-start.6 = (bf16[32,4096]{1,0:T(8,128)(2,1)S(1)}, bf16[32,4096]{1,0:T(8,128)(2,1)S(1)}, u32[]{:S(2)}, u32[]{:S(2)}) collective-permute-start(bf16[32,4096]{1,0:T(8,128)(2,1)S(1)} %join.9.refs_2_), channel_id=1, source_target_pairs={{0,1},{1,0},{2,3},{3,2},{4,5},{5,4},{6,7},{7,6},{8,9},{9,8},{10,11... | collective-permute-start | bytes 786440 | tf_op jit(solution)/shard_map/ppermute | solution.py:328
  18.7 6.5 %collective-permute-start.4 = (bf16[32,4096]{1,0:T(8,128)(2,1)S(1)}, bf16[32,4096]{1,0:T(8,128)(2,1)S(1)}, u32[]{:S(2)}, u32[]{:S(2)}) collective-permute-start(bf16[32,4096]{1,0:T(8,128)(2,1)S(1)} %join.8.refs_0_), channel_id=1, source_target_pairs={{0,1},{1,0},{2,3},{3,2},{4,5},{5,4},{6,7},{7,6},{8,9},{9,8},{10,11... | collective-permute-start | bytes 786440 | tf_op jit(solution)/shard_map/ppermute | solution.py:328
  18.8 6.4 %collective-permute-start.11 = (bf16[16,4096]{1,0:T(8,128)(2,1)S(1)}, bf16[16,4096]{1,0:T(8,128)(2,1)S(1)}, u32[]{:S(2)}, u32[]{:S(2)}) collective-permute-start(bf16[16,4096]{1,0:T(8,128)(2,1)S(1)} %collective-permute-done.3.refs_3_.refs_2_), channel_id=1, source_target_pairs={{0,2},{1,3},{2,0},{3,1},{4,6},{5,7},{6,4},{7,5},{8,10},{9,11},{10,... | collective-permute-start | bytes 393224 | tf_op jit(solution)/shard_map/ppermute | solution.py:328
  20.4 11.2 %collective-permute-start.10 = (bf16[16,4096]{1,0:T(8,128)(2,1)S(1)}, bf16[16,4096]{1,0:T(8,128)(2,1)S(1)}, u32[]{:S(2)}, u32[]{:S(2)}) collective-permute-start(bf16[16,4096]{1,0:T(8,128)(2,1)S(1)} %join.7.refs_2_.refs_0_), channel_id=1, source_target_pairs={{0,2},{1,3},{2,0},{3,1},{4,6},{5,7},{6,4},{7,5},{8,10},{9,11},{10,... | collective-permute-start | bytes 393224 | tf_op jit(solution)/shard_map/ppermute | solution.py:328
  31.7 3.6 %collective-permute-start.12 = (bf16[64,4096]{1,0:T(8,128)(2,1)S(1)}, bf16[64,4096]{1,0:T(8,128)(2,1)S(1)}, u32[]{:S(2)}, u32[]{:S(2)}) collective-permute-start(bf16[64,4096]{1,0:T(8,128)(2,1)S(1)} %join.11.refs_0_), channel_id=1, source_target_pairs={{0,1},{1,0},{2,3},{3,2},{4,5},{5,4},{6,7},{7,6},{8,9},{9,8},{10,11... | collective-permute-start | bytes 1572872 | tf_op jit(solution)/shard_map/ppermute | solution.py:328
  34.7 6.9 %collective-permute-start.9 = (bf16[32,4096]{1,0:T(8,128)(2,1)S(1)}, bf16[32,4096]{1,0:T(8,128)(2,1)S(1)}, u32[]{:S(2)}, u32[]{:S(2)}) collective-permute-start(bf16[32,4096]{1,0:T(8,128)(2,1)S(1)} %get-tuple-element.46), channel_id=1, source_target_pairs={{0,1},{1,0},{2,3},{3,2},{4,5},{5,4},{6,7},{7,6},{8,9},{9,8},{10,11... | collective-permute-start | bytes 786440 | tf_op jit(solution)/shard_map/ppermute | solution.py:328
  41.7 5.5 %collective-permute-start.13 = (bf16[16,4096]{1,0:T(8,128)(2,1)S(1)}, bf16[16,4096]{1,0:T(8,128)(2,1)S(1)}, u32[]{:S(2)}, u32[]{:S(2)}) collective-permute-start(bf16[16,4096]{1,0:T(8,128)(2,1)S(1)} %get-tuple-element.48.refs_0_), channel_id=1, source_target_pairs={{0,2},{1,3},{2,0},{3,1},{4,6},{5,7},{6,4},{7,5},{8,10},{9,11},{10,... | collective-permute-start | bytes 393224 | tf_op jit(solution)/shard_map/ppermute | solution.py:328
  47.7 3.1 %collective-permute-start.15 = (bf16[64,4096]{1,0:T(8,128)(2,1)S(1)}, bf16[64,4096]{1,0:T(8,128)(2,1)S(1)}, u32[]{:S(2)}, u32[]{:S(2)}) collective-permute-start(bf16[64,4096]{1,0:T(8,128)(2,1)S(1)} %get-tuple-element.52), channel_id=1, source_target_pairs={{0,1},{1,0},{2,3},{3,2},{4,5},{5,4},{6,7},{7,6},{8,9},{9,8},{10,11... | collective-permute-start | bytes 1572872 | tf_op jit(solution)/shard_map/ppermute | solution.py:328
  47.8 5.2 %collective-permute-start.7 = (bf16[32,4096]{1,0:T(8,128)(2,1)S(1)}, bf16[32,4096]{1,0:T(8,128)(2,1)S(1)}, u32[]{:S(2)}, u32[]{:S(2)}) collective-permute-start(bf16[32,4096]{1,0:T(8,128)(2,1)S(1)} %get-tuple-element.42), channel_id=1, source_target_pairs={{0,1},{1,0},{2,3},{3,2},{4,5},{5,4},{6,7},{7,6},{8,9},{9,8},{10,11... | collective-permute-start | bytes 786440 | tf_op jit(solution)/shard_map/ppermute | solution.py:328
  48.3 7.4 %collective-permute-start.14 = (bf16[16,4096]{1,0:T(8,128)(2,1)S(1)}, bf16[16,4096]{1,0:T(8,128)(2,1)S(1)}, u32[]{:S(2)}, u32[]{:S(2)}) collective-permute-start(bf16[16,4096]{1,0:T(8,128)(2,1)S(1)} %add.12.refs_0_), channel_id=1, source_target_pairs={{0,12},{1,13},{2,14},{3,15},{4,8},{5,9},{6,10},{7,11},{8,4},{9,5},... | collective-permute-start | bytes 393224 | tf_op jit(solution)/shard_map/ppermute | solution.py:328
  50.8 6.5 %collective-permute-start.18 = (bf16[16,4096]{1,0:T(8,128)(2,1)S(1)}, bf16[16,4096]{1,0:T(8,128)(2,1)S(1)}, u32[]{:S(2)}, u32[]{:S(2)}) collective-permute-start(bf16[16,4096]{1,0:T(8,128)(2,1)S(1)} %get-tuple-element.56), channel_id=1, source_target_pairs={{0,2},{1,3},{2,0},{3,1},{4,6},{5,7},{6,4},{7,5},{8,10},{9,11},{10,... | collective-permute-start | bytes 393224 | tf_op jit(solution)/shard_map/ppermute | solution.py:328
  52.4 7.7 %collective-permute-start.16 = (bf16[16,4096]{1,0:T(8,128)(2,1)S(1)}, bf16[16,4096]{1,0:T(8,128)(2,1)S(1)}, u32[]{:S(2)}, u32[]{:S(2)}) collective-permute-start(bf16[16,4096]{1,0:T(8,128)(2,1)S(1)} %get-tuple-element.54), channel_id=1, source_target_pairs={{0,2},{1,3},{2,0},{3,1},{4,6},{5,7},{6,4},{7,5},{8,10},{9,11},{10,... | collective-permute-start | bytes 393224 | tf_op jit(solution)/shard_map/ppermute | solution.py:328
  53.0 10.6 %collective-permute-start.8 = (bf16[16,4096]{1,0:T(8,128)(2,1)S(1)}, bf16[16,4096]{1,0:T(8,128)(2,1)S(1)}, u32[]{:S(2)}, u32[]{:S(2)}) collective-permute-start(bf16[16,4096]{1,0:T(8,128)(2,1)S(1)} %get-tuple-element.44), channel_id=1, source_target_pairs={{0,2},{1,3},{2,0},{3,1},{4,6},{5,7},{6,4},{7,5},{8,10},{9,11},{10,... | collective-permute-start | bytes 393224 | tf_op jit(solution)/shard_map/ppermute | solution.py:328
  60.1 6.6 %collective-permute-start.19 = (bf16[16,4096]{1,0:T(8,128)(2,1)S(1)}, bf16[16,4096]{1,0:T(8,128)(2,1)S(1)}, u32[]{:S(2)}, u32[]{:S(2)}) collective-permute-start(bf16[16,4096]{1,0:T(8,128)(2,1)S(1)} %add.15), channel_id=1, source_target_pairs={{0,4},{1,5},{2,6},{3,7},{4,0},{5,1},{6,2},{7,3},{8,12},{9,13},{10,... | collective-permute-start | bytes 393224 | tf_op jit(solution)/shard_map/ppermute | solution.py:328
  62.7 7.4 %collective-permute-start.17 = (bf16[16,4096]{1,0:T(8,128)(2,1)S(1)}, bf16[16,4096]{1,0:T(8,128)(2,1)S(1)}, u32[]{:S(2)}, u32[]{:S(2)}) collective-permute-start(bf16[16,4096]{1,0:T(8,128)(2,1)S(1)} %join.13), channel_id=1, source_target_pairs={{0,8},{1,9},{2,10},{3,11},{4,12},{5,13},{6,14},{7,15},{8,0},{9,1},... | collective-permute-start | bytes 393224 | tf_op jit(solution)/shard_map/ppermute | solution.py:328
  (1 other events, 17.6 us)

commit v12 on v11

--- a/solution.py
+++ b/solution.py
@@ -201,34 +201,31 @@
     )(*parts, w, *after)
 
 
-def down_kernel(h_ref, w_ref, *refs, columns, groups):
-    outs = refs[len(refs) - 2 * groups:]
+def down_kernel(h_ref, w_ref, *refs, columns, low):
+    keep_ref, send_ref = refs[-2:]
     first, last, tile = columns
-    height = h_ref.shape[0] // groups
+    half = keep_ref.shape[0]
 
     @pl.loop(0, (last - first) // tile)
     def _(i):
         cut = pl.ds(pl.multiple_of(first + i * tile, tile), tile)
-        out = jnp.dot(h_ref[...], w_ref[:, cut], preferred_element_type=F32)
-        for g in range(groups):
-            middle = g * height + height // 2
-            outs[2 * g][:, cut] = out[middle - height // 2:middle]
-            outs[2 * g + 1][:, cut] = out[middle:middle + height // 2].astype(BF16)
-
-
-def down(hid, w, columns, groups, after, before):
-    half = hid.shape[0] // groups // 2
+        out = jnp.dot(h_ref[low:low + 2 * half, :], w_ref[:, cut], preferred_element_type=F32)
+        keep_ref[:, cut] = out[:half]
+        send_ref[:, cut] = out[half:].astype(BF16)
+
+
+def down(hid, rows, w, columns, after, before):
+    half = (rows[1] - rows[0]) // 2
     width = w.shape[1]
     skip = 2 + len(after)
     return pl.pallas_call(
-        functools.partial(down_kernel, columns=columns, groups=groups),
+        functools.partial(down_kernel, columns=columns, low=rows[0]),
         in_specs=[VMEM] * 2 + [ANY] * len(after) + [VMEM] * len(before),
-        out_specs=[VMEM] * (2 * groups),
+        out_specs=[VMEM] * 2,
         out_shape=[
             jax.ShapeDtypeStruct((half, width), F32),
             jax.ShapeDtypeStruct((half, width), BF16),
-        ]
-        * groups,
+        ],
         input_output_aliases={skip + i: i for i in range(len(before))},
         compiler_params=params(8),
         cost_estimate=FREE,
@@ -341,13 +338,24 @@
     beside = [swap(block, near[0]) for block in blocks]
     beside[-1] = join([beside[-1]], [])
     early, late = list(range(experts // 2)), list(range(experts // 2, experts))
-
-    def spread(members, after=()):
-        pieces = [join([x for i in members for x in (blocks[i], beside[i])], after)]
+    parts = []
+    segments = {}
+    for members in (early, late):
+        pieces = [join([x for i in members for x in (blocks[i], beside[i])], [])]
+        height = pieces[0].shape[0]
         for mask in near[1:]:
             block = pieces[0] if len(pieces) == 1 else join(pieces, [])
             pieces = [block, swap(block, mask)]
-        return pieces, [(k, 0, piece.shape[0]) for k, piece in enumerate(pieces)]
+        for at, i in enumerate(members):
+            segments[i] = []
+            for k, piece in enumerate(pieces):
+                for base in range(2 * at * slots, piece.shape[0], height):
+                    segments[i].append((len(parts) + k, base, base + 2 * slots))
+        parts += pieces
+    others = list(range(2, experts)) + [0]
+    sources = segments[1] + [cut for cuts in zip(*[segments[i] for i in others]) for cut in cuts]
+    count = sum(high - low for _, low, high in sources)
+    skip = 2 * slots * len(segments[1])
 
     def gather(keep, send, members, after=()):
         for i, mask in enumerate(reversed(near[1:])):
@@ -364,40 +372,28 @@
         send, keep = block[i]
         return add(keep, swap(send, near[0]), [(0, slots)], [BF16])[0]
 
-    def rows_of(*groups, after=()):
-        parts, cuts = [], []
-        for members in groups:
-            pieces, taken = spread(members, after)
-            cuts += [(len(parts) + k, low, high) for k, low, high in taken]
-            parts += pieces
-        return parts, cuts
-
-    width_a = 7 * width // 8
-    links = [blocks[2], blocks[3]]
-    parts, sources = rows_of([1], after=links)
-    own_parts, own_sources = rows_of([0])
-    sources = sources + [(len(parts) + k, low, high) for k, low, high in own_sources]
-    hid = up(parts + own_parts, sources, w_up, [])
-    keep, send, keep_own, send_own = down(hid, w_down, (0, width, min(1024, width)), 2, [], [])
-    hid_late = up(*rows_of(late, after=[hid]), w_up, [keep])
-    block = gather(keep, send, [1], [hid_late])
-    hid = hid_late
-    before = down(hid, w_down, (0, width_a, width_a // 4), 1, [block[1][0]], [])
+    hid = up(parts, sources, w_up, [])
+
+    eighth = width // 8
+    ends = [0, 2 * eighth, 7 * eighth, width]
+    tiles = [2 * eighth, 5 * eighth // 2, eighth]
+    steps = list(zip(ends, ends[1:], tiles))
+    keep, send = down(hid, (0, skip), w_down, (0, width, 2 * eighth), [], [])
+    before = down(hid, (skip, count), w_down, steps[0], [keep], [])
+    block = gather(keep, send, [1], before[:1])
+    before = down(hid, (skip, count), w_down, steps[1], [block[1][0]], before)
     part = total(1)
-    keep, send = down(hid, w_down, (width_a, width, width - width_a), 1, [part], before)
-    block.update(gather(keep, send, late))
-    block.update(gather(keep_own, send_own, [0]))
+    keep, send = down(hid, (skip, count), w_down, steps[2], [part], before)
+    block.update(gather(keep, send, others))
     back = {1: swap(part, far[0])}
-    link = back[1]
-    link = join([link], [])
-
+    link = join([back[1]], [])
     for i in late:
         part = total(i)
         if i == 2:
             part = join([part], [link])
         back[i] = swap(part, far[i - 1])
-    send, keep = block[0]
-    acc = own_part(mixes[0], keep, swap(send, near[0]), back[1])
+    own_send = join([block[0][0]], [part])
+    acc = own_part(mixes[0], block[0][1], swap(own_send, near[0]), back[1])
     return post(mixes[1], table, acc, [back[i] for i in late])
 
 

time: 71.5 us -> 64.1 us (0.90)
  Pallas kernels: 24.4 us -> 18.4 us
  waiting for transfers between devices: 22.6 us -> 21.7 us
    pallas_call x2 -> x1, Pallas kernels: 12.8 us -> 5.67 us  [up(): pl.pallas_call(functools.partial(up_kernel, sources=sources, count=len(pa...]
    pallas_call x3 -> x4, Pallas kernels: 6.33 us -> 7.42 us  [down(): pl.pallas_call(functools.partial(down_kernel, columns=columns, low=rows[0...]
    ppermute x20 -> x18, waiting for transfers between devices: 22.6 us -> 21.7 us  [swap(): return lax.ppermute(x, 'expert', [(i, i ^ mask) for i in range(devices)])]
    ppermute x20 -> x18, starting transfers between devices: 24 us -> 23.4 us  [swap(): return lax.ppermute(x, 'expert', [(i, i ^ mask) for i in range(devices)])]
  transfers between devices with their start and end apart: 20 -> 18, of which waited for: 10 -> 12; matrix products, arithmetic and copies ran while one was open for 0% -> 0% of each run, Pallas kernels for 28% -> 8%
where the time goes in v12:
time: 64.1 us; the launch traced here: 63.9 us
  starting transfers between devices  23.4 us (37%)
  waiting for transfers between devices  21.7 us (34%)
  Pallas kernels  18.4 us (29%)
    ppermute x18, starting transfers between devices, swap(): return lax.ppermute(x, 'expert', [(i, i ^ mask) for i in range(devices)])  23.4 us
    ppermute x18, waiting for transfers between devices, swap(): return lax.ppermute(x, 'expert', [(i, i ^ mask) for i in range(devices)])  21.7 us
    pallas_call x4, Pallas kernels, down(): pl.pallas_call(functools.partial(down_kernel, columns=columns, low=rows[0...  7.42 us
    pallas_call x1, Pallas kernels, up(): pl.pallas_call(functools.partial(up_kernel, sources=sources, count=len(pa...  5.67 us
    pallas_call x1, Pallas kernels, first(): pl.pallas_call(first_kernel, in_specs=[SMEM] + [HBM] * 7, out_specs=[VMEM...  2.39 us
  transfers between devices with their start and end apart: 18, of which 12 were waited for; matrix products, arithmetic and copies ran while one was open for 0% of the time, Pallas kernels for 8%

profile of v12, /device:TPU:0, one launch (start us, length us, event | category | flops | bytes accessed | tf_op | source)
XLA Modules:
  0.0 63.9 jit_solution(11594744292246010845)
XLA Ops:
  0.1 2.4 %first.1 = (bf16[16,4096]{1,0:T(8,128)(2,1)S(1)}, bf16[128,4096]{1,0:T(8,128)(2,1)S(1)}, f32[3,4096]{1,0:T(4,128)S(1)}, s32[4,16]{1,0:T(4,128)S(1)}, f32[4,16]{1,0:T(4,128)S(1)}) custom-call(s32[2]{0:T(128)S(1)} %pad_add_fusion.info_ref, bf16[128,4096]{1,0:T(8,128)(2,1)} %refs_0_.1, s32[4,16]{1,0:T(4,128)} %bitcast.6, f32[2,4096]{1,0:T(2,128)} %refs_2_.1, ...), custom_call_target="tpu_custom_call" | custom-call | flops 1 | bytes 1 | tf_op jit(solution)/shard_map/first/pallas_call | solution.py:78
  2.5 5.1 %collective-permute-start = (bf16[16,4096]{1,0:T(8,128)(2,1)S(1)}, bf16[16,4096]{1,0:T(8,128)(2,1)S(1)}, u32[]{:S(2)}, u32[]{:S(2)}) collective-permute-start(bf16[16,4096]{1,0:T(8,128)(2,1)S(1)} %get-tuple-element.33), channel_id=1, source_target_pairs={{0,12},{1,13},{2,14},{3,15},{4,8},{5,9},{6,10},{7,11},{8,4},{9,5},... | collective-permute-start | bytes 393224 | tf_op jit(solution)/shard_map/ppermute | solution.py:325
  9.0 1.7 %collective-permute-start.1 = (bf16[16,4096]{1,0:T(8,128)(2,1)S(1)}, bf16[16,4096]{1,0:T(8,128)(2,1)S(1)}, u32[]{:S(2)}, u32[]{:S(2)}) collective-permute-start(bf16[16,4096]{1,0:T(8,128)(2,1)S(1)} %get-tuple-element.38.refs_0_), channel_id=1, source_target_pairs={{0,2},{1,3},{2,0},{3,1},{4,6},{5,7},{6,4},{7,5},{8,10},{9,11},{10,... | collective-permute-start | bytes 393224 | tf_op jit(solution)/shard_map/ppermute | solution.py:325
  10.7 1.2 %collective-permute-done.after_ref.refs_2_ = bf16[16,4096]{1,0:T(8,128)(2,1)S(1)} collective-permute-done((bf16[16,4096]{1,0:T(8,128)(2,1)S(1)}, bf16[16,4096]{1,0:T(8,128)(2,1)S(1)}, u32[]{:S(2)}, u32[]{:S(2)}) %collective-permute-start) | collective-permute-done | bytes 131104 | tf_op jit(solution)/shard_map/ppermute | solution.py:325
  12.0 1.8 %collective-permute-start.2 = (bf16[16,4096]{1,0:T(8,128)(2,1)S(1)}, bf16[16,4096]{1,0:T(8,128)(2,1)S(1)}, u32[]{:S(2)}, u32[]{:S(2)}) collective-permute-start(bf16[16,4096]{1,0:T(8,128)(2,1)S(1)} %collective-permute-done.after_ref.refs_2_), channel_id=1, source_target_pairs={{0,2},{1,3},{2,0},{3,1},{4,6},{5,7},{6,4},{7,5},{8,10},{9,11},{10,... | collective-permute-start | bytes 393224 | tf_op jit(solution)/shard_map/ppermute | solution.py:325
  13.9 1.2 %collective-permute-done.6.refs_2_ = bf16[16,4096]{1,0:T(8,128)(2,1)S(1)} collective-permute-done((bf16[16,4096]{1,0:T(8,128)(2,1)S(1)}, bf16[16,4096]{1,0:T(8,128)(2,1)S(1)}, u32[]{:S(2)}, u32[]{:S(2)}) %collective-permute-start.6) | collective-permute-done | bytes 131104 | tf_op jit(solution)/shard_map/ppermute | solution.py:325
  15.1 1.6 %collective-permute-start.7 = (bf16[16,4096]{1,0:T(8,128)(2,1)S(1)}, bf16[16,4096]{1,0:T(8,128)(2,1)S(1)}, u32[]{:S(2)}, u32[]{:S(2)}) collective-permute-start(bf16[16,4096]{1,0:T(8,128)(2,1)S(1)} %collective-permute-done.6.refs_2_), channel_id=1, source_target_pairs={{0,2},{1,3},{2,0},{3,1},{4,6},{5,7},{6,4},{7,5},{8,10},{9,11},{10,... | collective-permute-start | bytes 393224 | tf_op jit(solution)/shard_map/ppermute | solution.py:325
  16.7 2.0 %collective-permute-done.4.refs_0_ = bf16[16,4096]{1,0:T(8,128)(2,1)S(1)} collective-permute-done((bf16[16,4096]{1,0:T(8,128)(2,1)S(1)}, bf16[16,4096]{1,0:T(8,128)(2,1)S(1)}, u32[]{:S(2)}, u32[]{:S(2)}) %collective-permute-start.4) | collective-permute-done | bytes 131104 | tf_op jit(solution)/shard_map/ppermute | solution.py:325
  18.7 1.6 %collective-permute-start.5 = (bf16[16,4096]{1,0:T(8,128)(2,1)S(1)}, bf16[16,4096]{1,0:T(8,128)(2,1)S(1)}, u32[]{:S(2)}, u32[]{:S(2)}) collective-permute-start(bf16[16,4096]{1,0:T(8,128)(2,1)S(1)} %join.8.refs_0_), channel_id=1, source_target_pairs={{0,2},{1,3},{2,0},{3,1},{4,6},{5,7},{6,4},{7,5},{8,10},{9,11},{10,... | collective-permute-start | bytes 393224 | tf_op jit(solution)/shard_map/ppermute | solution.py:325
  20.4 3.3 %collective-permute-done.5.refs_1_ = bf16[16,4096]{1,0:T(8,128)(2,1)S(1)} collective-permute-done((bf16[16,4096]{1,0:T(8,128)(2,1)S(1)}, bf16[16,4096]{1,0:T(8,128)(2,1)S(1)}, u32[]{:S(2)}, u32[]{:S(2)}) %collective-permute-start.5) | collective-permute-done | bytes 131104 | tf_op jit(solution)/shard_map/ppermute | solution.py:325
  23.8 1.9 %collective-permute-done.8.refs_3_ = bf16[64,4096]{1,0:T(8,128)(2,1)S(1)} collective-permute-done((bf16[64,4096]{1,0:T(8,128)(2,1)S(1)}, bf16[64,4096]{1,0:T(8,128)(2,1)S(1)}, u32[]{:S(2)}, u32[]{:S(2)}) %collective-permute-start.8) | collective-permute-done | bytes 524320 | tf_op jit(solution)/shard_map/ppermute | solution.py:325
  25.8 5.7 %up.1.h_ref = bf16[256,2048]{1,0:T(8,128)(2,1)S(1)} custom-call(bf16[64,4096]{1,0:T(8,128)(2,1)S(1)} %join.7.refs_0_, bf16[64,4096]{1,0:T(8,128)(2,1)S(1)} %collective-permute-done.3.refs_1_, bf16[64,4096]{1,0:T(8,128)(2,1)S(1)} %join.10.refs_2_, bf16[64,4096]{1,0:T(8,128)(2,1)S(1)} %collective-permute-done.8.refs_3_, bf16[2048,4096]{1,0:T(8,128)(2,1)S(1)} %bitcast.5), custom_call_target="tpu_custom_call" | custom-call | flops 1 | bytes 1 | tf_op jit(solution)/shard_map/up/pallas_call | solution.py:192
  31.5 3.4 %down.4 = (f32[32,4096]{1,0:T(8,128)S(1)}, bf16[32,4096]{1,0:T(8,128)(2,1)S(1)}) custom-call(bf16[256,2048]{1,0:T(8,128)(2,1)S(1)} %up.1.h_ref, bf16[2048,4096]{1,0:T(8,128)(2,1)S(1)} %copy-done), custom_call_target="tpu_custom_call" | custom-call | flops 1 | bytes 1 | tf_op jit(solution)/shard_map/down/pallas_call | solution.py:221
  36.6 1.6 %collective-permute-start.10 = (bf16[16,4096]{1,0:T(8,128)(2,1)S(1)}, bf16[16,4096]{1,0:T(8,128)(2,1)S(1)}, u32[]{:S(2)}, u32[]{:S(2)}) collective-permute-start(bf16[16,4096]{1,0:T(8,128)(2,1)S(1)} %get-tuple-element.45.refs_0_), channel_id=1, source_target_pairs={{0,2},{1,3},{2,0},{3,1},{4,6},{5,7},{6,4},{7,5},{8,10},{9,11},{10,... | collective-permute-start | bytes 393224 | tf_op jit(solution)/shard_map/ppermute | solution.py:325
  38.2 2.5 %down.6 = (f32[96,4096]{1,0:T(8,128)S(1)}, bf16[96,4096]{1,0:T(8,128)(2,1)S(1)}) custom-call(bf16[256,2048]{1,0:T(8,128)(2,1)S(1)} %up.1.h_ref, bf16[2048,4096]{1,0:T(8,128)(2,1)S(1)} %copy-done, bf16[16,4096]{1,0:T(8,128)(2,1)S(1)} %get-tuple-element.45.refs_0_, ...), custom_call_target="tpu_custom_call", output_to_operand_aliasing={{0}: (3, {}), {1}: (4, {})} | custom-call | flops 1 | bytes 1 | tf_op jit(solution)/shard_map/down/pallas_call | solution.py:221
  40.6 1.6 %collective-permute-done.10.got_ref = bf16[16,4096]{1,0:T(8,128)(2,1)S(1)} collective-permute-done((bf16[16,4096]{1,0:T(8,128)(2,1)S(1)}, bf16[16,4096]{1,0:T(8,128)(2,1)S(1)}, u32[]{:S(2)}, u32[]{:S(2)}) %collective-permute-start.10) | collective-permute-done | bytes 131104 | tf_op jit(solution)/shard_map/ppermute | solution.py:325
  42.9 2.5 %collective-permute-start.14 = (bf16[16,4096]{1,0:T(8,128)(2,1)S(1)}, bf16[16,4096]{1,0:T(8,128)(2,1)S(1)}, u32[]{:S(2)}, u32[]{:S(2)}) collective-permute-start(bf16[16,4096]{1,0:T(8,128)(2,1)S(1)} %add.10.refs_0_), channel_id=1, source_target_pairs={{0,12},{1,13},{2,14},{3,15},{4,8},{5,9},{6,10},{7,11},{8,4},{9,5},... | collective-permute-start | bytes 393224 | tf_op jit(solution)/shard_map/ppermute | solution.py:325
  45.5 1.6 %collective-permute-start.12 = (bf16[16,4096]{1,0:T(8,128)(2,1)S(1)}, bf16[16,4096]{1,0:T(8,128)(2,1)S(1)}, u32[]{:S(2)}, u32[]{:S(2)}) collective-permute-start(bf16[16,4096]{1,0:T(8,128)(2,1)S(1)} %get-tuple-element.54), channel_id=1, source_target_pairs={{0,2},{1,3},{2,0},{3,1},{4,6},{5,7},{6,4},{7,5},{8,10},{9,11},{10,... | collective-permute-start | bytes 393224 | tf_op jit(solution)/shard_map/ppermute | solution.py:325
  47.6 3.1 %collective-permute-done.14.got_ref.refs_0_ = bf16[16,4096]{1,0:T(8,128)(2,1)S(1)} collective-permute-done((bf16[16,4096]{1,0:T(8,128)(2,1)S(1)}, bf16[16,4096]{1,0:T(8,128)(2,1)S(1)}, u32[]{:S(2)}, u32[]{:S(2)}) %collective-permute-start.14) | collective-permute-done | bytes 131104 | tf_op jit(solution)/shard_map/ppermute | solution.py:325
  50.7 1.2 %collective-permute-done.12.got_ref = bf16[16,4096]{1,0:T(8,128)(2,1)S(1)} collective-permute-done((bf16[16,4096]{1,0:T(8,128)(2,1)S(1)}, bf16[16,4096]{1,0:T(8,128)(2,1)S(1)}, u32[]{:S(2)}, u32[]{:S(2)}) %collective-permute-start.12) | collective-permute-done | bytes 131104 | tf_op jit(solution)/shard_map/ppermute | solution.py:325
  52.0 1.6 %collective-permute-start.13 = (bf16[16,4096]{1,0:T(8,128)(2,1)S(1)}, bf16[16,4096]{1,0:T(8,128)(2,1)S(1)}, u32[]{:S(2)}, u32[]{:S(2)}) collective-permute-start(bf16[16,4096]{1,0:T(8,128)(2,1)S(1)} %join.11), channel_id=1, source_target_pairs={{0,2},{1,3},{2,0},{3,1},{4,6},{5,7},{6,4},{7,5},{8,10},{9,11},{10,... | collective-permute-start | bytes 393224 | tf_op jit(solution)/shard_map/ppermute | solution.py:325
  55.0 2.4 %collective-permute-start.17 = (bf16[16,4096]{1,0:T(8,128)(2,1)S(1)}, bf16[16,4096]{1,0:T(8,128)(2,1)S(1)}, u32[]{:S(2)}, u32[]{:S(2)}) collective-permute-start(bf16[16,4096]{1,0:T(8,128)(2,1)S(1)} %add.12.refs_1_), channel_id=1, source_target_pairs={{0,4},{1,5},{2,6},{3,7},{4,0},{5,1},{6,2},{7,3},{8,12},{9,13},{10,... | collective-permute-start | bytes 393224 | tf_op jit(solution)/shard_map/ppermute | solution.py:325
  57.9 4.8 %collective-permute-done.16.refs_0_ = bf16[16,4096]{1,0:T(8,128)(2,1)S(1)} collective-permute-done((bf16[16,4096]{1,0:T(8,128)(2,1)S(1)}, bf16[16,4096]{1,0:T(8,128)(2,1)S(1)}, u32[]{:S(2)}, u32[]{:S(2)}) %collective-permute-start.16) | collective-permute-done | bytes 131104 | tf_op jit(solution)/shard_map/ppermute | solution.py:325
  62.7 1.2 %post.1 = bf16[128,4096]{1,0:T(8,128)(2,1)} custom-call(bf16[128,64]{1,0:T(8,128)(2,1)S(1)} %get-tuple-element.34.mix_ref, f32[3,4096]{1,0:T(4,128)S(1)} %get-tuple-element.35.table_ref, f32[128,4096]{1,0:T(8,128)S(1)} %own_part.1.acc_ref, bf16[16,4096]{1,0:T(8,128)(2,1)S(1)} %collective-permute-done.16.refs_0_, ...), custom_call_target="tpu_custom_call" | custom-call | flops 1 | bytes 1 | tf_op jit(solution)/shard_map/post/pallas_call | solution.py:293
  (46 shorter events, 6.8 us)
Async XLA Ops:
  2.5 9.5 %collective-permute-start = (bf16[16,4096]{1,0:T(8,128)(2,1)S(1)}, bf16[16,4096]{1,0:T(8,128)(2,1)S(1)}, u32[]{:S(2)}, u32[]{:S(2)}) collective-permute-start(bf16[16,4096]{1,0:T(8,128)(2,1)S(1)} %get-tuple-element.33), channel_id=1, source_target_pairs={{0,12},{1,13},{2,14},{3,15},{4,8},{5,9},{6,10},{7,11},{8,4},{9,5},... | collective-permute-start | bytes 393224 | tf_op jit(solution)/shard_map/ppermute | solution.py:325
  7.6 18.1 %slice-start = ((s8[16777216]{0:T(1024)(128)(4,1)}), s8[4194304]{0:T(1024)(128)(4,1)S(1)}, s32[]{:S(2)}) async-start(s8[16777216]{0:T(1024)(128)(4,1)} %bitcast.4), calls=%async_computation | async-start | bytes 8388608
  7.6 18.1 %slice-start.1 = ((s8[16777216]{0:T(1024)(128)(4,1)}), s8[4194304]{0:T(1024)(128)(4,1)S(1)}, s32[]{:S(2)}) async-start(s8[16777216]{0:T(1024)(128)(4,1)} %bitcast.4), calls=%async_computation.1 | async-start | bytes 8388608
  7.6 18.1 %slice-start.2 = ((s8[16777216]{0:T(1024)(128)(4,1)}), s8[4194304]{0:T(1024)(128)(4,1)S(1)}, s32[]{:S(2)}) async-start(s8[16777216]{0:T(1024)(128)(4,1)} %bitcast.4), calls=%async_computation.2 | async-start | bytes 8388608
  7.6 18.1 %slice-start.3 = ((s8[16777216]{0:T(1024)(128)(4,1)}), s8[4194304]{0:T(1024)(128)(4,1)S(1)}, s32[]{:S(2)}) async-start(s8[16777216]{0:T(1024)(128)(4,1)} %bitcast.4), calls=%async_computation.3 | async-start | bytes 8388608
  8.4 6.7 %collective-permute-start.6 = (bf16[16,4096]{1,0:T(8,128)(2,1)S(1)}, bf16[16,4096]{1,0:T(8,128)(2,1)S(1)}, u32[]{:S(2)}, u32[]{:S(2)}) collective-permute-start(bf16[16,4096]{1,0:T(8,128)(2,1)S(1)} %get-tuple-element.40), channel_id=1, source_target_pairs={{0,4},{1,5},{2,6},{3,7},{4,0},{5,1},{6,2},{7,3},{8,12},{9,13},{10,... | collective-permute-start | bytes 393224 | tf_op jit(solution)/shard_map/ppermute | solution.py:325
  8.4 10.2 %collective-permute-start.4 = (bf16[16,4096]{1,0:T(8,128)(2,1)S(1)}, bf16[16,4096]{1,0:T(8,128)(2,1)S(1)}, u32[]{:S(2)}, u32[]{:S(2)}) collective-permute-start(bf16[16,4096]{1,0:T(8,128)(2,1)S(1)} %get-tuple-element.39), channel_id=1, source_target_pairs={{0,8},{1,9},{2,10},{3,11},{4,12},{5,13},{6,14},{7,15},{8,0},{9,1},... | collective-permute-start | bytes 393224 | tf_op jit(solution)/shard_map/ppermute | solution.py:325
  9.0 11.2 %collective-permute-start.1 = (bf16[16,4096]{1,0:T(8,128)(2,1)S(1)}, bf16[16,4096]{1,0:T(8,128)(2,1)S(1)}, u32[]{:S(2)}, u32[]{:S(2)}) collective-permute-start(bf16[16,4096]{1,0:T(8,128)(2,1)S(1)} %get-tuple-element.38.refs_0_), channel_id=1, source_target_pairs={{0,2},{1,3},{2,0},{3,1},{4,6},{5,7},{6,4},{7,5},{8,10},{9,11},{10,... | collective-permute-start | bytes 393224 | tf_op jit(solution)/shard_map/ppermute | solution.py:325
  12.0 8.3 %collective-permute-start.2 = (bf16[16,4096]{1,0:T(8,128)(2,1)S(1)}, bf16[16,4096]{1,0:T(8,128)(2,1)S(1)}, u32[]{:S(2)}, u32[]{:S(2)}) collective-permute-start(bf16[16,4096]{1,0:T(8,128)(2,1)S(1)} %collective-permute-done.after_ref.refs_2_), channel_id=1, source_target_pairs={{0,2},{1,3},{2,0},{3,1},{4,6},{5,7},{6,4},{7,5},{8,10},{9,11},{10,... | collective-permute-start | bytes 393224 | tf_op jit(solution)/shard_map/ppermute | solution.py:325
  15.1 5.3 %collective-permute-start.7 = (bf16[16,4096]{1,0:T(8,128)(2,1)S(1)}, bf16[16,4096]{1,0:T(8,128)(2,1)S(1)}, u32[]{:S(2)}, u32[]{:S(2)}) collective-permute-start(bf16[16,4096]{1,0:T(8,128)(2,1)S(1)} %collective-permute-done.6.refs_2_), channel_id=1, source_target_pairs={{0,2},{1,3},{2,0},{3,1},{4,6},{5,7},{6,4},{7,5},{8,10},{9,11},{10,... | collective-permute-start | bytes 393224 | tf_op jit(solution)/shard_map/ppermute | solution.py:325
  18.7 5.0 %collective-permute-start.5 = (bf16[16,4096]{1,0:T(8,128)(2,1)S(1)}, bf16[16,4096]{1,0:T(8,128)(2,1)S(1)}, u32[]{:S(2)}, u32[]{:S(2)}) collective-permute-start(bf16[16,4096]{1,0:T(8,128)(2,1)S(1)} %join.8.refs_0_), channel_id=1, source_target_pairs={{0,2},{1,3},{2,0},{3,1},{4,6},{5,7},{6,4},{7,5},{8,10},{9,11},{10,... | collective-permute-start | bytes 393224 | tf_op jit(solution)/shard_map/ppermute | solution.py:325
  20.3 3.5 %collective-permute-start.3 = (bf16[64,4096]{1,0:T(8,128)(2,1)S(1)}, bf16[64,4096]{1,0:T(8,128)(2,1)S(1)}, u32[]{:S(2)}, u32[]{:S(2)}) collective-permute-start(bf16[64,4096]{1,0:T(8,128)(2,1)S(1)} %join.7.refs_0_), channel_id=1, source_target_pairs={{0,1},{1,0},{2,3},{3,2},{4,5},{5,4},{6,7},{7,6},{8,9},{9,8},{10,11... | collective-permute-start | bytes 1572872 | tf_op jit(solution)/shard_map/ppermute | solution.py:325
  23.7 2.0 %collective-permute-start.8 = (bf16[64,4096]{1,0:T(8,128)(2,1)S(1)}, bf16[64,4096]{1,0:T(8,128)(2,1)S(1)}, u32[]{:S(2)}, u32[]{:S(2)}) collective-permute-start(bf16[64,4096]{1,0:T(8,128)(2,1)S(1)} %join.10.refs_2_), channel_id=1, source_target_pairs={{0,1},{1,0},{2,3},{3,2},{4,5},{5,4},{6,7},{7,6},{8,9},{9,8},{10,11... | collective-permute-start | bytes 1572872 | tf_op jit(solution)/shard_map/ppermute | solution.py:325
  25.8 5.8 %copy-start = (bf16[2048,4096]{1,0:T(8,128)(2,1)S(1)}, bf16[2048,4096]{1,0:T(8,128)(2,1)}, u32[]{:S(2)}) copy-start(bf16[2048,4096]{1,0:T(8,128)(2,1)} %w_ref.7) | copy-start | bytes 50331652
  34.9 1.6 %collective-permute-start.9 = (bf16[32,4096]{1,0:T(8,128)(2,1)S(1)}, bf16[32,4096]{1,0:T(8,128)(2,1)S(1)}, u32[]{:S(2)}, u32[]{:S(2)}) collective-permute-start(bf16[32,4096]{1,0:T(8,128)(2,1)S(1)} %get-tuple-element.42), channel_id=1, source_target_pairs={{0,1},{1,0},{2,3},{3,2},{4,5},{5,4},{6,7},{7,6},{8,9},{9,8},{10,11... | collective-permute-start | bytes 786440 | tf_op jit(solution)/shard_map/ppermute | solution.py:325
  36.6 5.6 %collective-permute-start.10 = (bf16[16,4096]{1,0:T(8,128)(2,1)S(1)}, bf16[16,4096]{1,0:T(8,128)(2,1)S(1)}, u32[]{:S(2)}, u32[]{:S(2)}) collective-permute-start(bf16[16,4096]{1,0:T(8,128)(2,1)S(1)} %get-tuple-element.45.refs_0_), channel_id=1, source_target_pairs={{0,2},{1,3},{2,0},{3,1},{4,6},{5,7},{6,4},{7,5},{8,10},{9,11},{10,... | collective-permute-start | bytes 393224 | tf_op jit(solution)/shard_map/ppermute | solution.py:325
  42.8 2.6 %collective-permute-start.11 = (bf16[96,4096]{1,0:T(8,128)(2,1)S(1)}, bf16[96,4096]{1,0:T(8,128)(2,1)S(1)}, u32[]{:S(2)}, u32[]{:S(2)}) collective-permute-start(bf16[96,4096]{1,0:T(8,128)(2,1)S(1)} %get-tuple-element.50), channel_id=1, source_target_pairs={{0,1},{1,0},{2,3},{3,2},{4,5},{5,4},{6,7},{7,6},{8,9},{9,8},{10,11... | collective-permute-start | bytes 2359304 | tf_op jit(solution)/shard_map/ppermute | solution.py:325
  42.9 7.8 %collective-permute-start.14 = (bf16[16,4096]{1,0:T(8,128)(2,1)S(1)}, bf16[16,4096]{1,0:T(8,128)(2,1)S(1)}, u32[]{:S(2)}, u32[]{:S(2)}) collective-permute-start(bf16[16,4096]{1,0:T(8,128)(2,1)S(1)} %add.10.refs_0_), channel_id=1, source_target_pairs={{0,12},{1,13},{2,14},{3,15},{4,8},{5,9},{6,10},{7,11},{8,4},{9,5},... | collective-permute-start | bytes 393224 | tf_op jit(solution)/shard_map/ppermute | solution.py:325
  45.5 6.4 %collective-permute-start.12 = (bf16[16,4096]{1,0:T(8,128)(2,1)S(1)}, bf16[16,4096]{1,0:T(8,128)(2,1)S(1)}, u32[]{:S(2)}, u32[]{:S(2)}) collective-permute-start(bf16[16,4096]{1,0:T(8,128)(2,1)S(1)} %get-tuple-element.54), channel_id=1, source_target_pairs={{0,2},{1,3},{2,0},{3,1},{4,6},{5,7},{6,4},{7,5},{8,10},{9,11},{10,... | collective-permute-start | bytes 393224 | tf_op jit(solution)/shard_map/ppermute | solution.py:325
  47.2 7.5 %collective-permute-start.15 = (bf16[16,4096]{1,0:T(8,128)(2,1)S(1)}, bf16[16,4096]{1,0:T(8,128)(2,1)S(1)}, u32[]{:S(2)}, u32[]{:S(2)}) collective-permute-start(bf16[16,4096]{1,0:T(8,128)(2,1)S(1)} %get-tuple-element.56), channel_id=1, source_target_pairs={{0,2},{1,3},{2,0},{3,1},{4,6},{5,7},{6,4},{7,5},{8,10},{9,11},{10,... | collective-permute-start | bytes 393224 | tf_op jit(solution)/shard_map/ppermute | solution.py:325
  52.0 5.4 %collective-permute-start.13 = (bf16[16,4096]{1,0:T(8,128)(2,1)S(1)}, bf16[16,4096]{1,0:T(8,128)(2,1)S(1)}, u32[]{:S(2)}, u32[]{:S(2)}) collective-permute-start(bf16[16,4096]{1,0:T(8,128)(2,1)S(1)} %join.11), channel_id=1, source_target_pairs={{0,2},{1,3},{2,0},{3,1},{4,6},{5,7},{6,4},{7,5},{8,10},{9,11},{10,... | collective-permute-start | bytes 393224 | tf_op jit(solution)/shard_map/ppermute | solution.py:325
  54.7 7.9 %collective-permute-start.16 = (bf16[16,4096]{1,0:T(8,128)(2,1)S(1)}, bf16[16,4096]{1,0:T(8,128)(2,1)S(1)}, u32[]{:S(2)}, u32[]{:S(2)}) collective-permute-start(bf16[16,4096]{1,0:T(8,128)(2,1)S(1)} %join.13), channel_id=1, source_target_pairs={{0,8},{1,9},{2,10},{3,11},{4,12},{5,13},{6,14},{7,15},{8,0},{9,1},... | collective-permute-start | bytes 393224 | tf_op jit(solution)/shard_map/ppermute | solution.py:325
  55.0 7.7 %collective-permute-start.17 = (bf16[16,4096]{1,0:T(8,128)(2,1)S(1)}, bf16[16,4096]{1,0:T(8,128)(2,1)S(1)}, u32[]{:S(2)}, u32[]{:S(2)}) collective-permute-start(bf16[16,4096]{1,0:T(8,128)(2,1)S(1)} %add.12.refs_1_), channel_id=1, source_target_pairs={{0,4},{1,5},{2,6},{3,7},{4,0},{5,1},{6,2},{7,3},{8,12},{9,13},{10,... | collective-permute-start | bytes 393224 | tf_op jit(solution)/shard_map/ppermute | solution.py:325

commit v13 on v10

--- a/solution.py
+++ b/solution.py
@@ -19,7 +19,7 @@
 
 FREE = pl.CostEstimate(flops=1, bytes_accessed=1, transcendentals=0)
 
-BUSY = pl.CostEstimate(flops=10**10, bytes_accessed=40 * MIB, transcendentals=0)
+BUSY = pl.CostEstimate(flops=4 * 10**10, bytes_accessed=128 * MIB, transcendentals=0)
 
 
 def params(mib):
@@ -96,7 +96,7 @@
             pltpu.SemaphoreType.DMA((7,)),
         ],
         compiler_params=params(8),
-        cost_estimate=BUSY,
+        cost_estimate=FREE,
         name="first",
     )(info, tokens, pick, shift, scale, gate, comb, count)
 
@@ -142,7 +142,7 @@
         out_specs=[VMEM] * 2,
         out_shape=[jax.ShapeDtypeStruct((tok_rows, experts * slots), BF16)] * 2,
         compiler_params=params(4),
-        cost_estimate=BUSY,
+        cost_estimate=FREE,
         name="mixer",
     )(picks, weights, after)
 
@@ -168,7 +168,8 @@
 
 
 def up_kernel(*refs, sources, count):
-    w_ref, out_ref, rows_ref = refs[count:]
+    w_ref = refs[count]
+    out_ref, rows_ref = refs[-2:]
     to = 0
     for source, low, high in sources:
         rows_ref[to:to + high - low, :] = refs[source][low:high, :]
@@ -180,24 +181,24 @@
     def _(i):
         cut = pl.ds(pl.multiple_of(i * tile, tile), tile)
         lifted = lax.dot_general(
-            rows_ref[...], w_ref[cut, :], (((1,), (1,)), ((), ())), preferred_element_type=F32
+            w_ref[cut, :], rows_ref[...], (((1,), (1,)), ((), ())), preferred_element_type=F32
         )
-        out_ref[:, cut] = jax.nn.gelu(lifted, approximate=True).astype(BF16)
-
-
-def up(parts, sources, w):
+        out_ref[:, cut] = jax.nn.gelu(lifted, approximate=True).astype(BF16).T
+
+
+def up(parts, sources, w, after):
     hidden, width = w.shape
     rows = sum(high - low for _, low, high in sources)
     return pl.pallas_call(
         functools.partial(up_kernel, sources=sources, count=len(parts)),
-        in_specs=[VMEM] * (len(parts) + 1),
+        in_specs=[VMEM] * (len(parts) + 1) + [ANY] * len(after),
         out_specs=VMEM,
         out_shape=jax.ShapeDtypeStruct((rows, hidden), BF16),
         scratch_shapes=[pltpu.VMEM((rows, width), BF16)],
         compiler_params=params(8),
         cost_estimate=FREE,
         name="up",
-    )(*parts, w)
+    )(*parts, w, *after)
 
 
 def down_kernel(h_ref, w_ref, keep_ref, send_ref, *, columns):
@@ -333,7 +334,6 @@
         pltpu.with_memory_space_constraint(x, pltpu.HBM)
         for x in (tokens, shift, scale, gate, pick, comb, count)
     ]
-    half = hidden // 2
     farthest, tok, table, picks, weights = first(info, tokens, pick, shift, scale, gate, comb, count)
     own, *others = rest(tok, table, picks)
 
@@ -359,11 +359,11 @@
         sources.append(cuts)
     sources = [cut for pair in zip(*sources) for cut in pair]
 
-    hid = up(parts, sources, w_up)
+    hid = up(parts, sources, w_up, [])
 
     step = 5 * width // 8
     keep_a, send_a = down(hid, w_down, (0, step, step // 2))
-    keep_b, send_b = down(hid, w_down, (step, width, (width - step) // 3))
+    keep_b, send_b = down(hid, w_down, (step, width, width - step))
     pairs = []
     for keep, send in ((keep_a, send_a), (keep_b, send_b)):
         for i, mask in enumerate(reversed(near[1:])):

time: 61.5 us -> 59.8 us (0.972)
  starting transfers between devices: 25.5 us -> 21.8 us
  waiting for transfers between devices: 19.3 us -> 21.6 us
    ppermute x18, starting transfers between devices: 25.5 us -> 21.8 us  [swap(): return lax.ppermute(x, 'expert', [(i, i ^ mask) for i in range(devices)])]
    ppermute x18, waiting for transfers between devices: 19.3 us -> 21.6 us  [swap(): return lax.ppermute(x, 'expert', [(i, i ^ mask) for i in range(devices)])]
  transfers between devices with their start and end apart: 18 -> 18, of which waited for: 9 -> 13; matrix products, arithmetic and copies ran while one was open for 0% -> 0% of each run, Pallas kernels for 6% -> 6%
where the time goes in v13:
time: 59.8 us; the launch traced here: 59.7 us
  starting transfers between devices  21.8 us (36%)
  waiting for transfers between devices  21.6 us (36%)
  Pallas kernels  15.9 us (27%)
    ppermute x18, starting transfers between devices, swap(): return lax.ppermute(x, 'expert', [(i, i ^ mask) for i in range(devices)])  21.8 us
    ppermute x18, waiting for transfers between devices, swap(): return lax.ppermute(x, 'expert', [(i, i ^ mask) for i in range(devices)])  21.6 us
    pallas_call x1, Pallas kernels, up(): pl.pallas_call(functools.partial(up_kernel, sources=sources, count=len(pa...  5.72 us
    pallas_call x2, Pallas kernels, down(): pl.pallas_call(functools.partial(down_kernel, columns=columns), in_specs=...  4.92 us
    pallas_call x1, Pallas kernels, first(): pl.pallas_call(first_kernel, in_specs=[SMEM] + [HBM] * 7, out_specs=[VMEM...  2.39 us
    pallas_call x1, Pallas kernels, post(): pl.pallas_call(post_kernel, in_specs=[VMEM] * (3 + len(blocks)), out_spec...  1.2 us
  transfers between devices with their start and end apart: 18, of which 13 were waited for; matrix products, arithmetic and copies ran while one was open for 0% of the time, Pallas kernels for 6%

profile of v13, /device:TPU:0, one launch (start us, length us, event | category | flops | bytes accessed | tf_op | source)
XLA Modules:
  0.0 59.7 jit_solution(2450758571095713561)
XLA Ops:
  0.1 2.4 %first.1 = (bf16[16,4096]{1,0:T(8,128)(2,1)S(1)}, bf16[128,4096]{1,0:T(8,128)(2,1)S(1)}, f32[3,4096]{1,0:T(4,128)S(1)}, s32[4,16]{1,0:T(4,128)S(1)}, f32[4,16]{1,0:T(4,128)S(1)}) custom-call(s32[2]{0:T(128)S(1)} %pad_add_fusion.info_ref, bf16[128,4096]{1,0:T(8,128)(2,1)} %refs_0_.1, s32[4,16]{1,0:T(4,128)} %bitcast.6, f32[2,4096]{1,0:T(2,128)} %refs_2_.1, ...), custom_call_target="tpu_custom_call" | custom-call | flops 1 | bytes 1 | tf_op jit(solution)/shard_map/first/pallas_call | solution.py:78
  2.5 5.1 %collective-permute-start = (bf16[16,4096]{1,0:T(8,128)(2,1)S(1)}, bf16[16,4096]{1,0:T(8,128)(2,1)S(1)}, u32[]{:S(2)}, u32[]{:S(2)}) collective-permute-start(bf16[16,4096]{1,0:T(8,128)(2,1)S(1)} %get-tuple-element.29), channel_id=1, source_target_pairs={{0,12},{1,13},{2,14},{3,15},{4,8},{5,9},{6,10},{7,11},{8,4},{9,5},... | collective-permute-start | bytes 393224 | tf_op jit(solution)/shard_map/ppermute | solution.py:331
  9.1 1.7 %collective-permute-start.1 = (bf16[16,4096]{1,0:T(8,128)(2,1)S(1)}, bf16[16,4096]{1,0:T(8,128)(2,1)S(1)}, u32[]{:S(2)}, u32[]{:S(2)}) collective-permute-start(bf16[16,4096]{1,0:T(8,128)(2,1)S(1)} %get-tuple-element.34.refs_0_), channel_id=1, source_target_pairs={{0,2},{1,3},{2,0},{3,1},{4,6},{5,7},{6,4},{7,5},{8,10},{9,11},{10,... | collective-permute-start | bytes 393224 | tf_op jit(solution)/shard_map/ppermute | solution.py:331
  10.8 1.2 %collective-permute-done.after_ref.refs_2_ = bf16[16,4096]{1,0:T(8,128)(2,1)S(1)} collective-permute-done((bf16[16,4096]{1,0:T(8,128)(2,1)S(1)}, bf16[16,4096]{1,0:T(8,128)(2,1)S(1)}, u32[]{:S(2)}, u32[]{:S(2)}) %collective-permute-start) | collective-permute-done | bytes 131104 | tf_op jit(solution)/shard_map/ppermute | solution.py:331
  12.0 1.8 %collective-permute-start.2 = (bf16[16,4096]{1,0:T(8,128)(2,1)S(1)}, bf16[16,4096]{1,0:T(8,128)(2,1)S(1)}, u32[]{:S(2)}, u32[]{:S(2)}) collective-permute-start(bf16[16,4096]{1,0:T(8,128)(2,1)S(1)} %collective-permute-done.after_ref.refs_2_), channel_id=1, source_target_pairs={{0,2},{1,3},{2,0},{3,1},{4,6},{5,7},{6,4},{7,5},{8,10},{9,11},{10,... | collective-permute-start | bytes 393224 | tf_op jit(solution)/shard_map/ppermute | solution.py:331
  13.9 1.2 %collective-permute-done.6.refs_2_ = bf16[16,4096]{1,0:T(8,128)(2,1)S(1)} collective-permute-done((bf16[16,4096]{1,0:T(8,128)(2,1)S(1)}, bf16[16,4096]{1,0:T(8,128)(2,1)S(1)}, u32[]{:S(2)}, u32[]{:S(2)}) %collective-permute-start.6) | collective-permute-done | bytes 131104 | tf_op jit(solution)/shard_map/ppermute | solution.py:331
  15.1 1.6 %collective-permute-start.7 = (bf16[16,4096]{1,0:T(8,128)(2,1)S(1)}, bf16[16,4096]{1,0:T(8,128)(2,1)S(1)}, u32[]{:S(2)}, u32[]{:S(2)}) collective-permute-start(bf16[16,4096]{1,0:T(8,128)(2,1)S(1)} %collective-permute-done.6.refs_2_), channel_id=1, source_target_pairs={{0,2},{1,3},{2,0},{3,1},{4,6},{5,7},{6,4},{7,5},{8,10},{9,11},{10,... | collective-permute-start | bytes 393224 | tf_op jit(solution)/shard_map/ppermute | solution.py:331
  16.7 2.0 %collective-permute-done.4.refs_0_ = bf16[16,4096]{1,0:T(8,128)(2,1)S(1)} collective-permute-done((bf16[16,4096]{1,0:T(8,128)(2,1)S(1)}, bf16[16,4096]{1,0:T(8,128)(2,1)S(1)}, u32[]{:S(2)}, u32[]{:S(2)}) %collective-permute-start.4) | collective-permute-done | bytes 131104 | tf_op jit(solution)/shard_map/ppermute | solution.py:331
  18.7 1.6 %collective-permute-start.5 = (bf16[16,4096]{1,0:T(8,128)(2,1)S(1)}, bf16[16,4096]{1,0:T(8,128)(2,1)S(1)}, u32[]{:S(2)}, u32[]{:S(2)}) collective-permute-start(bf16[16,4096]{1,0:T(8,128)(2,1)S(1)} %join.7.refs_0_), channel_id=1, source_target_pairs={{0,2},{1,3},{2,0},{3,1},{4,6},{5,7},{6,4},{7,5},{8,10},{9,11},{10,... | collective-permute-start | bytes 393224 | tf_op jit(solution)/shard_map/ppermute | solution.py:331
  20.4 3.3 %collective-permute-done.5.refs_1_ = bf16[16,4096]{1,0:T(8,128)(2,1)S(1)} collective-permute-done((bf16[16,4096]{1,0:T(8,128)(2,1)S(1)}, bf16[16,4096]{1,0:T(8,128)(2,1)S(1)}, u32[]{:S(2)}, u32[]{:S(2)}) %collective-permute-start.5) | collective-permute-done | bytes 131104 | tf_op jit(solution)/shard_map/ppermute | solution.py:331
  23.8 1.9 %collective-permute-done.8.refs_3_ = bf16[64,4096]{1,0:T(8,128)(2,1)S(1)} collective-permute-done((bf16[64,4096]{1,0:T(8,128)(2,1)S(1)}, bf16[64,4096]{1,0:T(8,128)(2,1)S(1)}, u32[]{:S(2)}, u32[]{:S(2)}) %collective-permute-start.8) | collective-permute-done | bytes 524320 | tf_op jit(solution)/shard_map/ppermute | solution.py:331
  25.7 5.7 %up.1.h_ref = bf16[256,2048]{1,0:T(8,128)(2,1)S(1)} custom-call(bf16[64,4096]{1,0:T(8,128)(2,1)S(1)} %join.6.refs_0_, bf16[64,4096]{1,0:T(8,128)(2,1)S(1)} %collective-permute-done.3.refs_1_, bf16[64,4096]{1,0:T(8,128)(2,1)S(1)} %join.9.refs_2_, bf16[64,4096]{1,0:T(8,128)(2,1)S(1)} %collective-permute-done.8.refs_3_, bf16[2048,4096]{1,0:T(8,128)(2,1)S(1)} %copy-done), custom_call_target="tpu_custom_call" | custom-call | flops 1 | bytes 1 | tf_op jit(solution)/shard_map/up/pallas_call | solution.py:192
  31.5 3.1 %down.2 = (f32[128,2560]{1,0:T(8,128)S(1)}, bf16[128,2560]{1,0:T(8,128)(2,1)S(1)}) custom-call(bf16[256,2048]{1,0:T(8,128)(2,1)S(1)} %up.1.h_ref, bf16[2048,4096]{1,0:T(8,128)(2,1)S(1)} %bitcast.5), custom_call_target="tpu_custom_call" | custom-call | flops 1 | bytes 1 | tf_op jit(solution)/shard_map/down/pallas_call | solution.py:220
  34.8 1.8 %down.3 = (f32[128,1536]{1,0:T(8,128)S(1)}, bf16[128,1536]{1,0:T(8,128)(2,1)S(1)}) custom-call(bf16[256,2048]{1,0:T(8,128)(2,1)S(1)} %up.1.h_ref, bf16[2048,4096]{1,0:T(8,128)(2,1)S(1)} %bitcast.5), custom_call_target="tpu_custom_call" | custom-call | flops 1 | bytes 1 | tf_op jit(solution)/shard_map/down/pallas_call | solution.py:220
  37.1 1.5 %collective-permute-done.10.refs_3_ = bf16[128,1536]{1,0:T(8,128)(2,1)S(1)} collective-permute-done((bf16[128,1536]{1,0:T(8,128)(2,1)S(1)}, bf16[128,1536]{1,0:T(8,128)(2,1)S(1)}, u32[]{:S(2)}, u32[]{:S(2)}) %collective-permute-start.10) | collective-permute-done | bytes 393248 | tf_op jit(solution)/shard_map/ppermute | solution.py:331
  38.8 1.6 %collective-permute-start.11 = (bf16[16,4096]{1,0:T(8,128)(2,1)S(1)}, bf16[16,4096]{1,0:T(8,128)(2,1)S(1)}, u32[]{:S(2)}, u32[]{:S(2)}) collective-permute-start(bf16[16,4096]{1,0:T(8,128)(2,1)S(1)} %get-tuple-element.44), channel_id=1, source_target_pairs={{0,2},{1,3},{2,0},{3,1},{4,6},{5,7},{6,4},{7,5},{8,10},{9,11},{10,... | collective-permute-start | bytes 393224 | tf_op jit(solution)/shard_map/ppermute | solution.py:331
  40.9 1.5 %collective-permute-start.16 = (bf16[16,4096]{1,0:T(8,128)(2,1)S(1)}, bf16[16,4096]{1,0:T(8,128)(2,1)S(1)}, u32[]{:S(2)}, u32[]{:S(2)}) collective-permute-start(bf16[16,4096]{1,0:T(8,128)(2,1)S(1)} %get-tuple-element.48), channel_id=1, source_target_pairs={{0,2},{1,3},{2,0},{3,1},{4,6},{5,7},{6,4},{7,5},{8,10},{9,11},{10,... | collective-permute-start | bytes 393224 | tf_op jit(solution)/shard_map/ppermute | solution.py:331
  42.4 2.8 %collective-permute-done.11.refs_1_ = bf16[16,4096]{1,0:T(8,128)(2,1)S(1)} collective-permute-done((bf16[16,4096]{1,0:T(8,128)(2,1)S(1)}, bf16[16,4096]{1,0:T(8,128)(2,1)S(1)}, u32[]{:S(2)}, u32[]{:S(2)}) %collective-permute-start.11) | collective-permute-done | bytes 131104 | tf_op jit(solution)/shard_map/ppermute | solution.py:331
  45.2 2.5 %collective-permute-start.13 = (bf16[16,4096]{1,0:T(8,128)(2,1)S(1)}, bf16[16,4096]{1,0:T(8,128)(2,1)S(1)}, u32[]{:S(2)}, u32[]{:S(2)}) collective-permute-start(bf16[16,4096]{1,0:T(8,128)(2,1)S(1)} %add.9.refs_1_), channel_id=1, source_target_pairs={{0,12},{1,13},{2,14},{3,15},{4,8},{5,9},{6,10},{7,11},{8,4},{9,5},... | collective-permute-start | bytes 393224 | tf_op jit(solution)/shard_map/ppermute | solution.py:331
  47.8 1.6 %collective-permute-start.12 = (bf16[16,4096]{1,0:T(8,128)(2,1)S(1)}, bf16[16,4096]{1,0:T(8,128)(2,1)S(1)}, u32[]{:S(2)}, u32[]{:S(2)}) collective-permute-start(bf16[16,4096]{1,0:T(8,128)(2,1)S(1)} %join.11), channel_id=1, source_target_pairs={{0,2},{1,3},{2,0},{3,1},{4,6},{5,7},{6,4},{7,5},{8,10},{9,11},{10,... | collective-permute-start | bytes 393224 | tf_op jit(solution)/shard_map/ppermute | solution.py:331
  49.5 1.3 %collective-permute-done.16.refs_1_ = bf16[16,4096]{1,0:T(8,128)(2,1)S(1)} collective-permute-done((bf16[16,4096]{1,0:T(8,128)(2,1)S(1)}, bf16[16,4096]{1,0:T(8,128)(2,1)S(1)}, u32[]{:S(2)}, u32[]{:S(2)}) %collective-permute-start.16) | collective-permute-done | bytes 131104 | tf_op jit(solution)/shard_map/ppermute | solution.py:331
  51.8 1.1 %collective-permute-done.12.near_ref = bf16[16,4096]{1,0:T(8,128)(2,1)S(1)} collective-permute-done((bf16[16,4096]{1,0:T(8,128)(2,1)S(1)}, bf16[16,4096]{1,0:T(8,128)(2,1)S(1)}, u32[]{:S(2)}, u32[]{:S(2)}) %collective-permute-start.12) | collective-permute-done | bytes 131104 | tf_op jit(solution)/shard_map/ppermute | solution.py:331
  54.0 4.2 %collective-permute-done.15.refs_0_ = bf16[16,4096]{1,0:T(8,128)(2,1)S(1)} collective-permute-done((bf16[16,4096]{1,0:T(8,128)(2,1)S(1)}, bf16[16,4096]{1,0:T(8,128)(2,1)S(1)}, u32[]{:S(2)}, u32[]{:S(2)}) %collective-permute-start.15) | collective-permute-done | bytes 131104 | tf_op jit(solution)/shard_map/ppermute | solution.py:331
  58.5 1.2 %post.1 = bf16[128,4096]{1,0:T(8,128)(2,1)} custom-call(bf16[128,64]{1,0:T(8,128)(2,1)S(1)} %get-tuple-element.30.mix_ref, f32[3,4096]{1,0:T(4,128)S(1)} %get-tuple-element.31.table_ref, f32[128,4096]{1,0:T(8,128)S(1)} %own_part.1.acc_ref, bf16[16,4096]{1,0:T(8,128)(2,1)S(1)} %collective-permute-done.15.refs_0_, ...), custom_call_target="tpu_custom_call" | custom-call | flops 1 | bytes 1 | tf_op jit(solution)/shard_map/post/pallas_call | solution.py:299
  (42 shorter events, 5.7 us)
Async XLA Ops:
  2.5 9.5 %collective-permute-start = (bf16[16,4096]{1,0:T(8,128)(2,1)S(1)}, bf16[16,4096]{1,0:T(8,128)(2,1)S(1)}, u32[]{:S(2)}, u32[]{:S(2)}) collective-permute-start(bf16[16,4096]{1,0:T(8,128)(2,1)S(1)} %get-tuple-element.29), channel_id=1, source_target_pairs={{0,12},{1,13},{2,14},{3,15},{4,8},{5,9},{6,10},{7,11},{8,4},{9,5},... | collective-permute-start | bytes 393224 | tf_op jit(solution)/shard_map/ppermute | solution.py:331
  7.6 23.9 %slice-start = ((s8[16777216]{0:T(1024)(128)(4,1)}), s8[4194304]{0:T(1024)(128)(4,1)S(1)}, s32[]{:S(2)}) async-start(s8[16777216]{0:T(1024)(128)(4,1)} %bitcast.4), calls=%async_computation | async-start | bytes 8388608
  7.6 18.1 %copy-start = (bf16[2048,4096]{1,0:T(8,128)(2,1)S(1)}, bf16[2048,4096]{1,0:T(8,128)(2,1)}, u32[]{:S(2)}) copy-start(bf16[2048,4096]{1,0:T(8,128)(2,1)} %refs_4_.3) | copy-start | bytes 50331652
  7.6 23.9 %slice-start.1 = ((s8[16777216]{0:T(1024)(128)(4,1)}), s8[4194304]{0:T(1024)(128)(4,1)S(1)}, s32[]{:S(2)}) async-start(s8[16777216]{0:T(1024)(128)(4,1)} %bitcast.4), calls=%async_computation.1 | async-start | bytes 8388608
  7.6 23.9 %slice-start.2 = ((s8[16777216]{0:T(1024)(128)(4,1)}), s8[4194304]{0:T(1024)(128)(4,1)S(1)}, s32[]{:S(2)}) async-start(s8[16777216]{0:T(1024)(128)(4,1)} %bitcast.4), calls=%async_computation.2 | async-start | bytes 8388608
  7.6 23.9 %slice-start.3 = ((s8[16777216]{0:T(1024)(128)(4,1)}), s8[4194304]{0:T(1024)(128)(4,1)S(1)}, s32[]{:S(2)}) async-start(s8[16777216]{0:T(1024)(128)(4,1)} %bitcast.4), calls=%async_computation.3 | async-start | bytes 8388608
  8.4 6.7 %collective-permute-start.6 = (bf16[16,4096]{1,0:T(8,128)(2,1)S(1)}, bf16[16,4096]{1,0:T(8,128)(2,1)S(1)}, u32[]{:S(2)}, u32[]{:S(2)}) collective-permute-start(bf16[16,4096]{1,0:T(8,128)(2,1)S(1)} %get-tuple-element.36), channel_id=1, source_target_pairs={{0,4},{1,5},{2,6},{3,7},{4,0},{5,1},{6,2},{7,3},{8,12},{9,13},{10,... | collective-permute-start | bytes 393224 | tf_op jit(solution)/shard_map/ppermute | solution.py:331
  8.5 10.2 %collective-permute-start.4 = (bf16[16,4096]{1,0:T(8,128)(2,1)S(1)}, bf16[16,4096]{1,0:T(8,128)(2,1)S(1)}, u32[]{:S(2)}, u32[]{:S(2)}) collective-permute-start(bf16[16,4096]{1,0:T(8,128)(2,1)S(1)} %get-tuple-element.35), channel_id=1, source_target_pairs={{0,8},{1,9},{2,10},{3,11},{4,12},{5,13},{6,14},{7,15},{8,0},{9,1},... | collective-permute-start | bytes 393224 | tf_op jit(solution)/shard_map/ppermute | solution.py:331
  9.1 11.2 %collective-permute-start.1 = (bf16[16,4096]{1,0:T(8,128)(2,1)S(1)}, bf16[16,4096]{1,0:T(8,128)(2,1)S(1)}, u32[]{:S(2)}, u32[]{:S(2)}) collective-permute-start(bf16[16,4096]{1,0:T(8,128)(2,1)S(1)} %get-tuple-element.34.refs_0_), channel_id=1, source_target_pairs={{0,2},{1,3},{2,0},{3,1},{4,6},{5,7},{6,4},{7,5},{8,10},{9,11},{10,... | collective-permute-start | bytes 393224 | tf_op jit(solution)/shard_map/ppermute | solution.py:331
  12.0 8.3 %collective-permute-start.2 = (bf16[16,4096]{1,0:T(8,128)(2,1)S(1)}, bf16[16,4096]{1,0:T(8,128)(2,1)S(1)}, u32[]{:S(2)}, u32[]{:S(2)}) collective-permute-start(bf16[16,4096]{1,0:T(8,128)(2,1)S(1)} %collective-permute-done.after_ref.refs_2_), channel_id=1, source_target_pairs={{0,2},{1,3},{2,0},{3,1},{4,6},{5,7},{6,4},{7,5},{8,10},{9,11},{10,... | collective-permute-start | bytes 393224 | tf_op jit(solution)/shard_map/ppermute | solution.py:331
  15.1 5.3 %collective-permute-start.7 = (bf16[16,4096]{1,0:T(8,128)(2,1)S(1)}, bf16[16,4096]{1,0:T(8,128)(2,1)S(1)}, u32[]{:S(2)}, u32[]{:S(2)}) collective-permute-start(bf16[16,4096]{1,0:T(8,128)(2,1)S(1)} %collective-permute-done.6.refs_2_), channel_id=1, source_target_pairs={{0,2},{1,3},{2,0},{3,1},{4,6},{5,7},{6,4},{7,5},{8,10},{9,11},{10,... | collective-permute-start | bytes 393224 | tf_op jit(solution)/shard_map/ppermute | solution.py:331
  18.7 5.0 %collective-permute-start.5 = (bf16[16,4096]{1,0:T(8,128)(2,1)S(1)}, bf16[16,4096]{1,0:T(8,128)(2,1)S(1)}, u32[]{:S(2)}, u32[]{:S(2)}) collective-permute-start(bf16[16,4096]{1,0:T(8,128)(2,1)S(1)} %join.7.refs_0_), channel_id=1, source_target_pairs={{0,2},{1,3},{2,0},{3,1},{4,6},{5,7},{6,4},{7,5},{8,10},{9,11},{10,... | collective-permute-start | bytes 393224 | tf_op jit(solution)/shard_map/ppermute | solution.py:331
  20.3 3.5 %collective-permute-start.3 = (bf16[64,4096]{1,0:T(8,128)(2,1)S(1)}, bf16[64,4096]{1,0:T(8,128)(2,1)S(1)}, u32[]{:S(2)}, u32[]{:S(2)}) collective-permute-start(bf16[64,4096]{1,0:T(8,128)(2,1)S(1)} %join.6.refs_0_), channel_id=1, source_target_pairs={{0,1},{1,0},{2,3},{3,2},{4,5},{5,4},{6,7},{7,6},{8,9},{9,8},{10,11... | collective-permute-start | bytes 1572872 | tf_op jit(solution)/shard_map/ppermute | solution.py:331
  23.7 2.0 %collective-permute-start.8 = (bf16[64,4096]{1,0:T(8,128)(2,1)S(1)}, bf16[64,4096]{1,0:T(8,128)(2,1)S(1)}, u32[]{:S(2)}, u32[]{:S(2)}) collective-permute-start(bf16[64,4096]{1,0:T(8,128)(2,1)S(1)} %join.9.refs_2_), channel_id=1, source_target_pairs={{0,1},{1,0},{2,3},{3,2},{4,5},{5,4},{6,7},{7,6},{8,9},{9,8},{10,11... | collective-permute-start | bytes 1572872 | tf_op jit(solution)/shard_map/ppermute | solution.py:331
  34.6 2.2 %collective-permute-start.9 = (bf16[128,2560]{1,0:T(8,128)(2,1)S(1)}, bf16[128,2560]{1,0:T(8,128)(2,1)S(1)}, u32[]{:S(2)}, u32[]{:S(2)}) collective-permute-start(bf16[128,2560]{1,0:T(8,128)(2,1)S(1)} %get-tuple-element.38), channel_id=1, source_target_pairs={{0,1},{1,0},{2,3},{3,2},{4,5},{5,4},{6,7},{7,6},{8,9},{9,8},{10,11... | collective-permute-start | bytes 1966088 | tf_op jit(solution)/shard_map/ppermute | solution.py:331
  36.8 1.8 %collective-permute-start.10 = (bf16[128,1536]{1,0:T(8,128)(2,1)S(1)}, bf16[128,1536]{1,0:T(8,128)(2,1)S(1)}, u32[]{:S(2)}, u32[]{:S(2)}) collective-permute-start(bf16[128,1536]{1,0:T(8,128)(2,1)S(1)} %join.10), channel_id=1, source_target_pairs={{0,1},{1,0},{2,3},{3,2},{4,5},{5,4},{6,7},{7,6},{8,9},{9,8},{10,11... | collective-permute-start | bytes 1179656 | tf_op jit(solution)/shard_map/ppermute | solution.py:331
  38.8 6.4 %collective-permute-start.11 = (bf16[16,4096]{1,0:T(8,128)(2,1)S(1)}, bf16[16,4096]{1,0:T(8,128)(2,1)S(1)}, u32[]{:S(2)}, u32[]{:S(2)}) collective-permute-start(bf16[16,4096]{1,0:T(8,128)(2,1)S(1)} %get-tuple-element.44), channel_id=1, source_target_pairs={{0,2},{1,3},{2,0},{3,1},{4,6},{5,7},{6,4},{7,5},{8,10},{9,11},{10,... | collective-permute-start | bytes 393224 | tf_op jit(solution)/shard_map/ppermute | solution.py:331
  40.4 9.0 %collective-permute-start.14 = (bf16[16,4096]{1,0:T(8,128)(2,1)S(1)}, bf16[16,4096]{1,0:T(8,128)(2,1)S(1)}, u32[]{:S(2)}, u32[]{:S(2)}) collective-permute-start(bf16[16,4096]{1,0:T(8,128)(2,1)S(1)} %get-tuple-element.46), channel_id=1, source_target_pairs={{0,2},{1,3},{2,0},{3,1},{4,6},{5,7},{6,4},{7,5},{8,10},{9,11},{10,... | collective-permute-start | bytes 393224 | tf_op jit(solution)/shard_map/ppermute | solution.py:331
  40.9 9.9 %collective-permute-start.16 = (bf16[16,4096]{1,0:T(8,128)(2,1)S(1)}, bf16[16,4096]{1,0:T(8,128)(2,1)S(1)}, u32[]{:S(2)}, u32[]{:S(2)}) collective-permute-start(bf16[16,4096]{1,0:T(8,128)(2,1)S(1)} %get-tuple-element.48), channel_id=1, source_target_pairs={{0,2},{1,3},{2,0},{3,1},{4,6},{5,7},{6,4},{7,5},{8,10},{9,11},{10,... | collective-permute-start | bytes 393224 | tf_op jit(solution)/shard_map/ppermute | solution.py:331
  45.2 8.4 %collective-permute-start.13 = (bf16[16,4096]{1,0:T(8,128)(2,1)S(1)}, bf16[16,4096]{1,0:T(8,128)(2,1)S(1)}, u32[]{:S(2)}, u32[]{:S(2)}) collective-permute-start(bf16[16,4096]{1,0:T(8,128)(2,1)S(1)} %add.9.refs_1_), channel_id=1, source_target_pairs={{0,12},{1,13},{2,14},{3,15},{4,8},{5,9},{6,10},{7,11},{8,4},{9,5},... | collective-permute-start | bytes 393224 | tf_op jit(solution)/shard_map/ppermute | solution.py:331
  47.8 5.1 %collective-permute-start.12 = (bf16[16,4096]{1,0:T(8,128)(2,1)S(1)}, bf16[16,4096]{1,0:T(8,128)(2,1)S(1)}, u32[]{:S(2)}, u32[]{:S(2)}) collective-permute-start(bf16[16,4096]{1,0:T(8,128)(2,1)S(1)} %join.11), channel_id=1, source_target_pairs={{0,2},{1,3},{2,0},{3,1},{4,6},{5,7},{6,4},{7,5},{8,10},{9,11},{10,... | collective-permute-start | bytes 393224 | tf_op jit(solution)/shard_map/ppermute | solution.py:331
  49.4 8.9 %collective-permute-start.15 = (bf16[16,4096]{1,0:T(8,128)(2,1)S(1)}, bf16[16,4096]{1,0:T(8,128)(2,1)S(1)}, u32[]{:S(2)}, u32[]{:S(2)}) collective-permute-start(bf16[16,4096]{1,0:T(8,128)(2,1)S(1)} %add.10), channel_id=1, source_target_pairs={{0,8},{1,9},{2,10},{3,11},{4,12},{5,13},{6,14},{7,15},{8,0},{9,1},... | collective-permute-start | bytes 393224 | tf_op jit(solution)/shard_map/ppermute | solution.py:331
  50.8 7.7 %collective-permute-start.17 = (bf16[16,4096]{1,0:T(8,128)(2,1)S(1)}, bf16[16,4096]{1,0:T(8,128)(2,1)S(1)}, u32[]{:S(2)}, u32[]{:S(2)}) collective-permute-start(bf16[16,4096]{1,0:T(8,128)(2,1)S(1)} %add.11), channel_id=1, source_target_pairs={{0,4},{1,5},{2,6},{3,7},{4,0},{5,1},{6,2},{7,3},{8,12},{9,13},{10,... | collective-permute-start | bytes 393224 | tf_op jit(solution)/shard_map/ppermute | solution.py:331

commit v14 on v13

--- a/solution.py
+++ b/solution.py
@@ -124,11 +124,10 @@
 
 
 def mixer_kernel(picks_ref, weights_ref, after_ref, *outs):
-    for i, out in enumerate(outs):
-        each = picks_ref.shape[0] // len(outs)
-        rows = range(i * each, (i + 1) * each)
-        picks = jnp.concatenate([picks_ref[r:r + 1, :] for r in rows], axis=1)
-        weights = jnp.concatenate([weights_ref[r:r + 1, :] for r in rows], axis=1)
+    experts = picks_ref.shape[0]
+    for members, out in zip((range(2), range(1, experts)), outs):
+        picks = jnp.concatenate([picks_ref[r:r + 1, :] for r in members], axis=1)
+        weights = jnp.concatenate([weights_ref[r:r + 1, :] for r in members], axis=1)
         mix = jnp.where(hot_rows(picks, out.shape[0]), weights, 0.0)
         high = mix.astype(BF16).astype(F32)
         out[...] = jnp.concatenate([high, mix - high], axis=1).astype(BF16)
@@ -140,7 +139,10 @@
         mixer_kernel,
         in_specs=[VMEM] * 2 + [ANY],
         out_specs=[VMEM] * 2,
-        out_shape=[jax.ShapeDtypeStruct((tok_rows, experts * slots), BF16)] * 2,
+        out_shape=[
+            jax.ShapeDtypeStruct((tok_rows, 4 * slots), BF16),
+            jax.ShapeDtypeStruct((tok_rows, 2 * (experts - 1) * slots), BF16),
+        ],
         compiler_params=params(4),
         cost_estimate=FREE,
         name="mixer",
@@ -175,7 +177,7 @@
         rows_ref[to:to + high - low, :] = refs[source][low:high, :]
         to += high - low
     hidden = w_ref.shape[0]
-    tile = min(512, hidden)
+    tile = min(1024, hidden)
 
     @pl.loop(0, hidden // tile)
     def _(i):
@@ -260,9 +262,16 @@
 
 
 def own_kernel(mix_ref, keep_ref, near_ref, got_ref, acc_ref):
+    slots = keep_ref.shape[0]
+    step = got_ref.shape[1]
     own = (keep_ref[...] + near_ref[...].astype(F32)).astype(BF16)
-    values = jnp.concatenate([own, got_ref[...]] * 2, axis=0)
-    acc_ref[...] = jnp.dot(mix_ref[...], values, preferred_element_type=F32)
+    values = jnp.concatenate([own[:, :step], got_ref[...]] * 2, axis=0)
+    acc_ref[:, :step] = jnp.dot(mix_ref[...], values, preferred_element_type=F32)
+    for_own = jnp.concatenate(
+        [mix_ref[:, i * slots:(i + 1) * slots] for i in range(0, mix_ref.shape[1] // slots, 2)], axis=1
+    )
+    values = jnp.concatenate([own[:, step:]] * 2, axis=0)
+    acc_ref[:, step:] = jnp.dot(for_own, values, preferred_element_type=F32)
 
 
 def own_part(mix, keep, near, got):
@@ -277,16 +286,30 @@
     )(mix, keep, near, got)
 
 
-def post_kernel(mix_ref, table_ref, acc_ref, *refs):
+def post_kernel(mix_ref, table_ref, acc_ref, tail_ref, *refs):
     blocks = refs[:-3]
     out_hbm, out_ref, sems = refs[-3:]
-    step = out_ref.shape[1] // sems.shape[0]
+    width = out_ref.shape[1]
+    slots = tail_ref.shape[0]
+    begin = width - tail_ref.shape[1]
+    count = mix_ref.shape[1] // 2
+    for_head = jnp.concatenate([mix_ref[:, i + slots:i + count] for i in (0, count)], axis=1)
+    step = width // sems.shape[0]
     copies = []
     for i in range(sems.shape[0]):
+        cuts = [(i * step, (i + 1) * step)]
+        if cuts[0][0] < begin < cuts[0][1]:
+            cuts = [(i * step, begin), (begin, (i + 1) * step)]
+        for low, high in cuts:
+            values = [ref[:, low:high] for ref in blocks]
+            mix = for_head
+            if low >= begin:
+                values = [tail_ref[:, low - begin:high - begin]] + values
+                mix = mix_ref[...]
+            values = jnp.concatenate(values * 2, axis=0)
+            mixed = acc_ref[:, low:high] + jnp.dot(mix, values, preferred_element_type=F32)
+            out_ref[:, low:high] = (table_ref[2:3, low:high] * mixed).astype(BF16)
         cut = pl.ds(i * step, step)
-        values = jnp.concatenate([ref[:, cut] for ref in blocks] * 2, axis=0)
-        mixed = acc_ref[:, cut] + jnp.dot(mix_ref[...], values, preferred_element_type=F32)
-        out_ref[:, cut] = (table_ref[2:3, cut] * mixed).astype(BF16)
         copy = pltpu.make_async_copy(out_ref.at[:, cut], out_hbm.at[:, cut], sems.at[i])
         copy.start()
         copies.append(copy)
@@ -294,18 +317,18 @@
         copy.wait()
 
 
-def post(mix, table, acc, blocks):
+def post(mix, table, acc, tail, blocks):
     tok_rows, width = acc.shape
     return pl.pallas_call(
         post_kernel,
-        in_specs=[VMEM] * (3 + len(blocks)),
+        in_specs=[VMEM] * (4 + len(blocks)),
         out_specs=HBM,
         out_shape=jax.ShapeDtypeStruct((tok_rows, width), BF16),
         scratch_shapes=[pltpu.VMEM((tok_rows, width), BF16), pltpu.SemaphoreType.DMA((4,))],
         compiler_params=params(8),
         cost_estimate=FREE,
         name="post",
-    )(mix, table, acc, *blocks)
+    )(mix, table, acc, tail, *blocks)
 
 
 def shards(tokens, shift, scale, gate, w_up, w_down, pick, count, combine):
@@ -377,22 +400,39 @@
             got = swap(send, mask)
         pairs.append((keep, got))
 
-    def outs(side):
-        rows = [(2 * i + side) * slots for i in range(experts)]
-        return [[(piece, at, at + slots) for piece in range(len(pairs))] for at in rows]
-
-    sums = add(pairs, outs(1) + outs(0), [BF16] * experts + [F32] * experts)
-    sends, keeps = sums[:experts], sums[experts:]
+    def outs(i, side, pieces):
+        at = (2 * i + side) * slots
+        return [(piece, at, at + slots) for piece in pieces]
+
+    rest_of = list(range(2, experts)) + [0]
+    head = add(pairs[:1], [outs(1, side, [0]) for side in (1, 0)], [BF16, F32])
+    sums = add(
+        pairs,
+        [outs(i, side, [0, 1]) for i in rest_of for side in (1, 0)]
+        + [outs(1, side, [1]) for side in (1, 0)],
+        [BF16, F32] * (len(rest_of) + 1),
+    )
+    block = {i: sums[2 * k:2 * k + 2] for k, i in enumerate(rest_of)}
+
+    def total(send, keep):
+        return add([(keep, swap(send, near[0]))], [[(0, 0, slots)]], [BF16])[0]
+
+    head = swap(total(*head), far[0])
+    link = head
     back = {}
-    for i in range(1, experts):
-        got = swap(sends[i], near[0])
-        (part,) = add([(keeps[i], got)], [[(0, 0, slots)]], [BF16])
+    for i in range(2, experts):
+        part = total(*block[i])
+        if i > 2:
+            part = join([part], [link])
         back[i] = swap(part, far[i - 1])
-        if i == 1:
-            own_send = join(sends[:1], [part])
-    got = swap(own_send, near[0])
-    acc = own_part(mixes[0], keeps[0], got, back[1])
-    return post(mixes[1], table, acc, [back[i] for i in range(2, experts)])
+        if i == 2:
+            first_part = part
+    tail_part = total(*sums[-2:])
+    tail = swap(tail_part, far[0])
+    send, keep = block[0]
+    beside_own = swap(join([send], [first_part, tail_part]), near[0])
+    acc = own_part(mixes[0], keep, beside_own, head)
+    return post(mixes[1], table, acc, tail, [back[i] for i in range(2, experts)])
 
 
 def solution(mesh):

time: 59.8 us -> 60.7 us (1.015)
  starting transfers between devices: 21.8 us -> 27 us
  waiting for transfers between devices: 21.6 us -> 17.7 us
    ppermute x18 -> x20, starting transfers between devices: 21.8 us -> 27 us  [swap(): return lax.ppermute(x, 'expert', [(i, i ^ mask) for i in range(devices)])]
    ppermute x18 -> x20, waiting for transfers between devices: 21.6 us -> 17.7 us  [swap(): return lax.ppermute(x, 'expert', [(i, i ^ mask) for i in range(devices)])]
  transfers between devices with their start and end apart: 18 -> 20, of which waited for: 13 -> 10; matrix products, arithmetic and copies ran while one was open for 0% -> 0% of each run, Pallas kernels for 6% -> 6%
where the time goes in v14:
time: 60.7 us; the launch traced here: 60.5 us
  starting transfers between devices  27 us (44%)
  waiting for transfers between devices  17.7 us (29%)
  Pallas kernels  15.6 us (26%)
    ppermute x20, starting transfers between devices, swap(): return lax.ppermute(x, 'expert', [(i, i ^ mask) for i in range(devices)])  27 us
    ppermute x20, waiting for transfers between devices, swap(): return lax.ppermute(x, 'expert', [(i, i ^ mask) for i in range(devices)])  17.7 us
    pallas_call x1, Pallas kernels, up(): pl.pallas_call(functools.partial(up_kernel, sources=sources, count=len(pa...  5.27 us
    pallas_call x2, Pallas kernels, down(): pl.pallas_call(functools.partial(down_kernel, columns=columns), in_specs=...  4.92 us
    pallas_call x1, Pallas kernels, first(): pl.pallas_call(first_kernel, in_specs=[SMEM] + [HBM] * 7, out_specs=[VMEM...  2.39 us
    pallas_call x1, Pallas kernels, post(): pl.pallas_call(post_kernel, in_specs=[VMEM] * (4 + len(blocks)), out_spec...  1.27 us
  transfers between devices with their start and end apart: 20, of which 10 were waited for; matrix products, arithmetic and copies ran while one was open for 0% of the time, Pallas kernels for 6%

profile of v14, /device:TPU:0, one launch (start us, length us, event | category | flops | bytes accessed | tf_op | source)
XLA Modules:
  0.0 60.5 jit_solution(5177715109782366494)
XLA Ops:
  0.1 2.4 %first.1 = (bf16[16,4096]{1,0:T(8,128)(2,1)S(1)}, bf16[128,4096]{1,0:T(8,128)(2,1)S(1)}, f32[3,4096]{1,0:T(4,128)S(1)}, s32[4,16]{1,0:T(4,128)S(1)}, f32[4,16]{1,0:T(4,128)S(1)}) custom-call(s32[2]{0:T(128)S(1)} %pad_add_fusion.info_ref, bf16[128,4096]{1,0:T(8,128)(2,1)} %refs_0_.1, s32[4,16]{1,0:T(4,128)} %bitcast.6, f32[2,4096]{1,0:T(2,128)} %refs_2_.1, ...), custom_call_target="tpu_custom_call" | custom-call | flops 1 | bytes 1 | tf_op jit(solution)/shard_map/first/pallas_call | solution.py:78
  2.5 5.1 %collective-permute-start = (bf16[16,4096]{1,0:T(8,128)(2,1)S(1)}, bf16[16,4096]{1,0:T(8,128)(2,1)S(1)}, u32[]{:S(2)}, u32[]{:S(2)}) collective-permute-start(bf16[16,4096]{1,0:T(8,128)(2,1)S(1)} %get-tuple-element.31), channel_id=1, source_target_pairs={{0,12},{1,13},{2,14},{3,15},{4,8},{5,9},{6,10},{7,11},{8,4},{9,5},... | collective-permute-start | bytes 393224 | tf_op jit(solution)/shard_map/ppermute | solution.py:354
  9.1 1.7 %collective-permute-start.1 = (bf16[16,4096]{1,0:T(8,128)(2,1)S(1)}, bf16[16,4096]{1,0:T(8,128)(2,1)S(1)}, u32[]{:S(2)}, u32[]{:S(2)}) collective-permute-start(bf16[16,4096]{1,0:T(8,128)(2,1)S(1)} %get-tuple-element.36.refs_0_), channel_id=1, source_target_pairs={{0,2},{1,3},{2,0},{3,1},{4,6},{5,7},{6,4},{7,5},{8,10},{9,11},{10,... | collective-permute-start | bytes 393224 | tf_op jit(solution)/shard_map/ppermute | solution.py:354
  10.8 1.2 %collective-permute-done.after_ref.refs_2_ = bf16[16,4096]{1,0:T(8,128)(2,1)S(1)} collective-permute-done((bf16[16,4096]{1,0:T(8,128)(2,1)S(1)}, bf16[16,4096]{1,0:T(8,128)(2,1)S(1)}, u32[]{:S(2)}, u32[]{:S(2)}) %collective-permute-start) | collective-permute-done | bytes 131104 | tf_op jit(solution)/shard_map/ppermute | solution.py:354
  12.0 1.8 %collective-permute-start.2 = (bf16[16,4096]{1,0:T(8,128)(2,1)S(1)}, bf16[16,4096]{1,0:T(8,128)(2,1)S(1)}, u32[]{:S(2)}, u32[]{:S(2)}) collective-permute-start(bf16[16,4096]{1,0:T(8,128)(2,1)S(1)} %collective-permute-done.after_ref.refs_2_), channel_id=1, source_target_pairs={{0,2},{1,3},{2,0},{3,1},{4,6},{5,7},{6,4},{7,5},{8,10},{9,11},{10,... | collective-permute-start | bytes 393224 | tf_op jit(solution)/shard_map/ppermute | solution.py:354
  13.9 1.2 %collective-permute-done.6.refs_2_ = bf16[16,4096]{1,0:T(8,128)(2,1)S(1)} collective-permute-done((bf16[16,4096]{1,0:T(8,128)(2,1)S(1)}, bf16[16,4096]{1,0:T(8,128)(2,1)S(1)}, u32[]{:S(2)}, u32[]{:S(2)}) %collective-permute-start.6) | collective-permute-done | bytes 131104 | tf_op jit(solution)/shard_map/ppermute | solution.py:354
  15.1 1.6 %collective-permute-start.7 = (bf16[16,4096]{1,0:T(8,128)(2,1)S(1)}, bf16[16,4096]{1,0:T(8,128)(2,1)S(1)}, u32[]{:S(2)}, u32[]{:S(2)}) collective-permute-start(bf16[16,4096]{1,0:T(8,128)(2,1)S(1)} %collective-permute-done.6.refs_2_), channel_id=1, source_target_pairs={{0,2},{1,3},{2,0},{3,1},{4,6},{5,7},{6,4},{7,5},{8,10},{9,11},{10,... | collective-permute-start | bytes 393224 | tf_op jit(solution)/shard_map/ppermute | solution.py:354
  16.7 2.0 %collective-permute-done.4.refs_0_ = bf16[16,4096]{1,0:T(8,128)(2,1)S(1)} collective-permute-done((bf16[16,4096]{1,0:T(8,128)(2,1)S(1)}, bf16[16,4096]{1,0:T(8,128)(2,1)S(1)}, u32[]{:S(2)}, u32[]{:S(2)}) %collective-permute-start.4) | collective-permute-done | bytes 131104 | tf_op jit(solution)/shard_map/ppermute | solution.py:354
  18.7 1.6 %collective-permute-start.5 = (bf16[16,4096]{1,0:T(8,128)(2,1)S(1)}, bf16[16,4096]{1,0:T(8,128)(2,1)S(1)}, u32[]{:S(2)}, u32[]{:S(2)}) collective-permute-start(bf16[16,4096]{1,0:T(8,128)(2,1)S(1)} %join.8.refs_0_), channel_id=1, source_target_pairs={{0,2},{1,3},{2,0},{3,1},{4,6},{5,7},{6,4},{7,5},{8,10},{9,11},{10,... | collective-permute-start | bytes 393224 | tf_op jit(solution)/shard_map/ppermute | solution.py:354
  20.4 3.3 %collective-permute-done.5.refs_1_ = bf16[16,4096]{1,0:T(8,128)(2,1)S(1)} collective-permute-done((bf16[16,4096]{1,0:T(8,128)(2,1)S(1)}, bf16[16,4096]{1,0:T(8,128)(2,1)S(1)}, u32[]{:S(2)}, u32[]{:S(2)}) %collective-permute-start.5) | collective-permute-done | bytes 131104 | tf_op jit(solution)/shard_map/ppermute | solution.py:354
  23.8 1.9 %collective-permute-done.8.refs_3_ = bf16[64,4096]{1,0:T(8,128)(2,1)S(1)} collective-permute-done((bf16[64,4096]{1,0:T(8,128)(2,1)S(1)}, bf16[64,4096]{1,0:T(8,128)(2,1)S(1)}, u32[]{:S(2)}, u32[]{:S(2)}) %collective-permute-start.8) | collective-permute-done | bytes 524320 | tf_op jit(solution)/shard_map/ppermute | solution.py:354
  25.7 5.3 %up.1.h_ref = bf16[256,2048]{1,0:T(8,128)(2,1)S(1)} custom-call(bf16[64,4096]{1,0:T(8,128)(2,1)S(1)} %join.7.refs_0_, bf16[64,4096]{1,0:T(8,128)(2,1)S(1)} %collective-permute-done.3.refs_1_, bf16[64,4096]{1,0:T(8,128)(2,1)S(1)} %join.10.refs_2_, bf16[64,4096]{1,0:T(8,128)(2,1)S(1)} %collective-permute-done.8.refs_3_, bf16[2048,4096]{1,0:T(8,128)(2,1)S(1)} %copy-done), custom_call_target="tpu_custom_call" | custom-call | flops 1 | bytes 1 | tf_op jit(solution)/shard_map/up/pallas_call | solution.py:194
  31.0 3.1 %down.2 = (f32[128,2560]{1,0:T(8,128)S(1)}, bf16[128,2560]{1,0:T(8,128)(2,1)S(1)}) custom-call(bf16[256,2048]{1,0:T(8,128)(2,1)S(1)} %up.1.h_ref, bf16[2048,4096]{1,0:T(8,128)(2,1)S(1)} %bitcast.5), custom_call_target="tpu_custom_call" | custom-call | flops 1 | bytes 1 | tf_op jit(solution)/shard_map/down/pallas_call | solution.py:222
  34.4 1.8 %down.3 = (f32[128,1536]{1,0:T(8,128)S(1)}, bf16[128,1536]{1,0:T(8,128)(2,1)S(1)}) custom-call(bf16[256,2048]{1,0:T(8,128)(2,1)S(1)} %up.1.h_ref, bf16[2048,4096]{1,0:T(8,128)(2,1)S(1)} %bitcast.5), custom_call_target="tpu_custom_call" | custom-call | flops 1 | bytes 1 | tf_op jit(solution)/shard_map/down/pallas_call | solution.py:222
  36.7 1.6 %collective-permute-start.14 = (bf16[16,2560]{1,0:T(8,128)(2,1)S(1)}, bf16[16,2560]{1,0:T(8,128)(2,1)S(1)}, u32[]{:S(2)}, u32[]{:S(2)}) collective-permute-start(bf16[16,2560]{1,0:T(8,128)(2,1)S(1)} %get-tuple-element.50), channel_id=1, source_target_pairs={{0,2},{1,3},{2,0},{3,1},{4,6},{5,7},{6,4},{7,5},{8,10},{9,11},{10,... | collective-permute-start | bytes 245768 | tf_op jit(solution)/shard_map/ppermute | solution.py:354
  38.4 1.5 %collective-permute-start.11 = (bf16[16,4096]{1,0:T(8,128)(2,1)S(1)}, bf16[16,4096]{1,0:T(8,128)(2,1)S(1)}, u32[]{:S(2)}, u32[]{:S(2)}) collective-permute-start(bf16[16,4096]{1,0:T(8,128)(2,1)S(1)} %get-tuple-element.46), channel_id=1, source_target_pairs={{0,2},{1,3},{2,0},{3,1},{4,6},{5,7},{6,4},{7,5},{8,10},{9,11},{10,... | collective-permute-start | bytes 393224 | tf_op jit(solution)/shard_map/ppermute | solution.py:354
  41.7 2.5 %collective-permute-start.15 = (bf16[16,2560]{1,0:T(8,128)(2,1)S(1)}, bf16[16,2560]{1,0:T(8,128)(2,1)S(1)}, u32[]{:S(2)}, u32[]{:S(2)}) collective-permute-start(bf16[16,2560]{1,0:T(8,128)(2,1)S(1)} %add.14), channel_id=1, source_target_pairs={{0,12},{1,13},{2,14},{3,15},{4,8},{5,9},{6,10},{7,11},{8,4},{9,5},... | collective-permute-start | bytes 245768 | tf_op jit(solution)/shard_map/ppermute | solution.py:354
  44.2 1.5 %collective-permute-start.12 = (bf16[16,1536]{1,0:T(8,128)(2,1)S(1)}, bf16[16,1536]{1,0:T(8,128)(2,1)S(1)}, u32[]{:S(2)}, u32[]{:S(2)}) collective-permute-start(bf16[16,1536]{1,0:T(8,128)(2,1)S(1)} %get-tuple-element.48), channel_id=1, source_target_pairs={{0,2},{1,3},{2,0},{3,1},{4,6},{5,7},{6,4},{7,5},{8,10},{9,11},{10,... | collective-permute-start | bytes 147464 | tf_op jit(solution)/shard_map/ppermute | solution.py:354
  45.7 2.6 %collective-permute-done.12.refs_1_ = bf16[16,1536]{1,0:T(8,128)(2,1)S(1)} collective-permute-done((bf16[16,1536]{1,0:T(8,128)(2,1)S(1)}, bf16[16,1536]{1,0:T(8,128)(2,1)S(1)}, u32[]{:S(2)}, u32[]{:S(2)}) %collective-permute-start.12) | collective-permute-done | bytes 49184 | tf_op jit(solution)/shard_map/ppermute | solution.py:354
  49.4 1.2 %collective-permute-start.13 = (bf16[16,4096]{1,0:T(8,128)(2,1)S(1)}, bf16[16,4096]{1,0:T(8,128)(2,1)S(1)}, u32[]{:S(2)}, u32[]{:S(2)}) collective-permute-start(bf16[16,4096]{1,0:T(8,128)(2,1)S(1)} %join.12), channel_id=1, source_target_pairs={{0,2},{1,3},{2,0},{3,1},{4,6},{5,7},{6,4},{7,5},{8,10},{9,11},{10,... | collective-permute-start | bytes 393224 | tf_op jit(solution)/shard_map/ppermute | solution.py:354
  50.7 2.3 %collective-permute-start.19 = (bf16[16,4096]{1,0:T(8,128)(2,1)S(1)}, bf16[16,4096]{1,0:T(8,128)(2,1)S(1)}, u32[]{:S(2)}, u32[]{:S(2)}) collective-permute-start(bf16[16,4096]{1,0:T(8,128)(2,1)S(1)} %join.13), channel_id=1, source_target_pairs={{0,4},{1,5},{2,6},{3,7},{4,0},{5,1},{6,2},{7,3},{8,12},{9,13},{10,... | collective-permute-start | bytes 393224 | tf_op jit(solution)/shard_map/ppermute | solution.py:354
  53.0 1.6 %collective-permute-start.16 = (bf16[16,1536]{1,0:T(8,128)(2,1)S(1)}, bf16[16,1536]{1,0:T(8,128)(2,1)S(1)}, u32[]{:S(2)}, u32[]{:S(2)}) collective-permute-start(bf16[16,1536]{1,0:T(8,128)(2,1)S(1)} %add.12.refs_2_), channel_id=1, source_target_pairs={{0,12},{1,13},{2,14},{3,15},{4,8},{5,9},{6,10},{7,11},{8,4},{9,5},... | collective-permute-start | bytes 147464 | tf_op jit(solution)/shard_map/ppermute | solution.py:354
  55.0 4.0 %collective-permute-done.16.tail_ref = bf16[16,1536]{1,0:T(8,128)(2,1)S(1)} collective-permute-done((bf16[16,1536]{1,0:T(8,128)(2,1)S(1)}, bf16[16,1536]{1,0:T(8,128)(2,1)S(1)}, u32[]{:S(2)}, u32[]{:S(2)}) %collective-permute-start.16) | collective-permute-done | bytes 49184 | tf_op jit(solution)/shard_map/ppermute | solution.py:354
  59.3 1.3 %post.1 = bf16[128,4096]{1,0:T(8,128)(2,1)} custom-call(bf16[128,96]{1,0:T(8,128)(2,1)S(1)} %get-tuple-element.32.mix_ref, f32[3,4096]{1,0:T(4,128)S(1)} %get-tuple-element.33.table_ref, f32[128,4096]{1,0:T(8,128)S(1)} %own_part.1.acc_ref, bf16[16,1536]{1,0:T(8,128)(2,1)S(1)} %collective-permute-done.16.tail_ref, ...), custom_call_target="tpu_custom_call" | custom-call | flops 1 | bytes 1 | tf_op jit(solution)/shard_map/post/pallas_call | solution.py:322
  (49 shorter events, 6.4 us)
Async XLA Ops:
  2.5 9.5 %collective-permute-start = (bf16[16,4096]{1,0:T(8,128)(2,1)S(1)}, bf16[16,4096]{1,0:T(8,128)(2,1)S(1)}, u32[]{:S(2)}, u32[]{:S(2)}) collective-permute-start(bf16[16,4096]{1,0:T(8,128)(2,1)S(1)} %get-tuple-element.31), channel_id=1, source_target_pairs={{0,12},{1,13},{2,14},{3,15},{4,8},{5,9},{6,10},{7,11},{8,4},{9,5},... | collective-permute-start | bytes 393224 | tf_op jit(solution)/shard_map/ppermute | solution.py:354
  7.6 23.4 %slice-start = ((s8[16777216]{0:T(1024)(128)(4,1)}), s8[4194304]{0:T(1024)(128)(4,1)S(1)}, s32[]{:S(2)}) async-start(s8[16777216]{0:T(1024)(128)(4,1)} %bitcast.4), calls=%async_computation | async-start | bytes 8388608
  7.6 23.4 %slice-start.1 = ((s8[16777216]{0:T(1024)(128)(4,1)}), s8[4194304]{0:T(1024)(128)(4,1)S(1)}, s32[]{:S(2)}) async-start(s8[16777216]{0:T(1024)(128)(4,1)} %bitcast.4), calls=%async_computation.1 | async-start | bytes 8388608
  7.6 23.4 %slice-start.2 = ((s8[16777216]{0:T(1024)(128)(4,1)}), s8[4194304]{0:T(1024)(128)(4,1)S(1)}, s32[]{:S(2)}) async-start(s8[16777216]{0:T(1024)(128)(4,1)} %bitcast.4), calls=%async_computation.2 | async-start | bytes 8388608
  7.6 23.4 %slice-start.3 = ((s8[16777216]{0:T(1024)(128)(4,1)}), s8[4194304]{0:T(1024)(128)(4,1)S(1)}, s32[]{:S(2)}) async-start(s8[16777216]{0:T(1024)(128)(4,1)} %bitcast.4), calls=%async_computation.3 | async-start | bytes 8388608
  8.4 6.7 %collective-permute-start.6 = (bf16[16,4096]{1,0:T(8,128)(2,1)S(1)}, bf16[16,4096]{1,0:T(8,128)(2,1)S(1)}, u32[]{:S(2)}, u32[]{:S(2)}) collective-permute-start(bf16[16,4096]{1,0:T(8,128)(2,1)S(1)} %get-tuple-element.38), channel_id=1, source_target_pairs={{0,4},{1,5},{2,6},{3,7},{4,0},{5,1},{6,2},{7,3},{8,12},{9,13},{10,... | collective-permute-start | bytes 393224 | tf_op jit(solution)/shard_map/ppermute | solution.py:354
  8.5 10.2 %collective-permute-start.4 = (bf16[16,4096]{1,0:T(8,128)(2,1)S(1)}, bf16[16,4096]{1,0:T(8,128)(2,1)S(1)}, u32[]{:S(2)}, u32[]{:S(2)}) collective-permute-start(bf16[16,4096]{1,0:T(8,128)(2,1)S(1)} %get-tuple-element.37), channel_id=1, source_target_pairs={{0,8},{1,9},{2,10},{3,11},{4,12},{5,13},{6,14},{7,15},{8,0},{9,1},... | collective-permute-start | bytes 393224 | tf_op jit(solution)/shard_map/ppermute | solution.py:354
  9.1 11.2 %collective-permute-start.1 = (bf16[16,4096]{1,0:T(8,128)(2,1)S(1)}, bf16[16,4096]{1,0:T(8,128)(2,1)S(1)}, u32[]{:S(2)}, u32[]{:S(2)}) collective-permute-start(bf16[16,4096]{1,0:T(8,128)(2,1)S(1)} %get-tuple-element.36.refs_0_), channel_id=1, source_target_pairs={{0,2},{1,3},{2,0},{3,1},{4,6},{5,7},{6,4},{7,5},{8,10},{9,11},{10,... | collective-permute-start | bytes 393224 | tf_op jit(solution)/shard_map/ppermute | solution.py:354
  12.0 8.3 %collective-permute-start.2 = (bf16[16,4096]{1,0:T(8,128)(2,1)S(1)}, bf16[16,4096]{1,0:T(8,128)(2,1)S(1)}, u32[]{:S(2)}, u32[]{:S(2)}) collective-permute-start(bf16[16,4096]{1,0:T(8,128)(2,1)S(1)} %collective-permute-done.after_ref.refs_2_), channel_id=1, source_target_pairs={{0,2},{1,3},{2,0},{3,1},{4,6},{5,7},{6,4},{7,5},{8,10},{9,11},{10,... | collective-permute-start | bytes 393224 | tf_op jit(solution)/shard_map/ppermute | solution.py:354
  15.1 5.3 %collective-permute-start.7 = (bf16[16,4096]{1,0:T(8,128)(2,1)S(1)}, bf16[16,4096]{1,0:T(8,128)(2,1)S(1)}, u32[]{:S(2)}, u32[]{:S(2)}) collective-permute-start(bf16[16,4096]{1,0:T(8,128)(2,1)S(1)} %collective-permute-done.6.refs_2_), channel_id=1, source_target_pairs={{0,2},{1,3},{2,0},{3,1},{4,6},{5,7},{6,4},{7,5},{8,10},{9,11},{10,... | collective-permute-start | bytes 393224 | tf_op jit(solution)/shard_map/ppermute | solution.py:354
  18.7 5.0 %collective-permute-start.5 = (bf16[16,4096]{1,0:T(8,128)(2,1)S(1)}, bf16[16,4096]{1,0:T(8,128)(2,1)S(1)}, u32[]{:S(2)}, u32[]{:S(2)}) collective-permute-start(bf16[16,4096]{1,0:T(8,128)(2,1)S(1)} %join.8.refs_0_), channel_id=1, source_target_pairs={{0,2},{1,3},{2,0},{3,1},{4,6},{5,7},{6,4},{7,5},{8,10},{9,11},{10,... | collective-permute-start | bytes 393224 | tf_op jit(solution)/shard_map/ppermute | solution.py:354
  20.3 3.5 %collective-permute-start.3 = (bf16[64,4096]{1,0:T(8,128)(2,1)S(1)}, bf16[64,4096]{1,0:T(8,128)(2,1)S(1)}, u32[]{:S(2)}, u32[]{:S(2)}) collective-permute-start(bf16[64,4096]{1,0:T(8,128)(2,1)S(1)} %join.7.refs_0_), channel_id=1, source_target_pairs={{0,1},{1,0},{2,3},{3,2},{4,5},{5,4},{6,7},{7,6},{8,9},{9,8},{10,11... | collective-permute-start | bytes 1572872 | tf_op jit(solution)/shard_map/ppermute | solution.py:354
  23.7 2.0 %collective-permute-start.8 = (bf16[64,4096]{1,0:T(8,128)(2,1)S(1)}, bf16[64,4096]{1,0:T(8,128)(2,1)S(1)}, u32[]{:S(2)}, u32[]{:S(2)}) collective-permute-start(bf16[64,4096]{1,0:T(8,128)(2,1)S(1)} %join.10.refs_2_), channel_id=1, source_target_pairs={{0,1},{1,0},{2,3},{3,2},{4,5},{5,4},{6,7},{7,6},{8,9},{9,8},{10,11... | collective-permute-start | bytes 1572872 | tf_op jit(solution)/shard_map/ppermute | solution.py:354
  34.2 2.2 %collective-permute-start.9 = (bf16[128,2560]{1,0:T(8,128)(2,1)S(1)}, bf16[128,2560]{1,0:T(8,128)(2,1)S(1)}, u32[]{:S(2)}, u32[]{:S(2)}) collective-permute-start(bf16[128,2560]{1,0:T(8,128)(2,1)S(1)} %get-tuple-element.40), channel_id=1, source_target_pairs={{0,1},{1,0},{2,3},{3,2},{4,5},{5,4},{6,7},{7,6},{8,9},{9,8},{10,11... | collective-permute-start | bytes 1966088 | tf_op jit(solution)/shard_map/ppermute | solution.py:354
  36.4 1.9 %collective-permute-start.10 = (bf16[128,1536]{1,0:T(8,128)(2,1)S(1)}, bf16[128,1536]{1,0:T(8,128)(2,1)S(1)}, u32[]{:S(2)}, u32[]{:S(2)}) collective-permute-start(bf16[128,1536]{1,0:T(8,128)(2,1)S(1)} %join.11), channel_id=1, source_target_pairs={{0,1},{1,0},{2,3},{3,2},{4,5},{5,4},{6,7},{7,6},{8,9},{9,8},{10,11... | collective-permute-start | bytes 1179656 | tf_op jit(solution)/shard_map/ppermute | solution.py:354
  36.7 4.9 %collective-permute-start.14 = (bf16[16,2560]{1,0:T(8,128)(2,1)S(1)}, bf16[16,2560]{1,0:T(8,128)(2,1)S(1)}, u32[]{:S(2)}, u32[]{:S(2)}) collective-permute-start(bf16[16,2560]{1,0:T(8,128)(2,1)S(1)} %get-tuple-element.50), channel_id=1, source_target_pairs={{0,2},{1,3},{2,0},{3,1},{4,6},{5,7},{6,4},{7,5},{8,10},{9,11},{10,... | collective-permute-start | bytes 245768 | tf_op jit(solution)/shard_map/ppermute | solution.py:354
  38.4 9.9 %collective-permute-start.11 = (bf16[16,4096]{1,0:T(8,128)(2,1)S(1)}, bf16[16,4096]{1,0:T(8,128)(2,1)S(1)}, u32[]{:S(2)}, u32[]{:S(2)}) collective-permute-start(bf16[16,4096]{1,0:T(8,128)(2,1)S(1)} %get-tuple-element.46), channel_id=1, source_target_pairs={{0,2},{1,3},{2,0},{3,1},{4,6},{5,7},{6,4},{7,5},{8,10},{9,11},{10,... | collective-permute-start | bytes 393224 | tf_op jit(solution)/shard_map/ppermute | solution.py:354
  39.9 10.7 %collective-permute-start.18 = (bf16[16,4096]{1,0:T(8,128)(2,1)S(1)}, bf16[16,4096]{1,0:T(8,128)(2,1)S(1)}, u32[]{:S(2)}, u32[]{:S(2)}) collective-permute-start(bf16[16,4096]{1,0:T(8,128)(2,1)S(1)} %get-tuple-element.52), channel_id=1, source_target_pairs={{0,2},{1,3},{2,0},{3,1},{4,6},{5,7},{6,4},{7,5},{8,10},{9,11},{10,... | collective-permute-start | bytes 393224 | tf_op jit(solution)/shard_map/ppermute | solution.py:354
  41.7 9.0 %collective-permute-start.15 = (bf16[16,2560]{1,0:T(8,128)(2,1)S(1)}, bf16[16,2560]{1,0:T(8,128)(2,1)S(1)}, u32[]{:S(2)}, u32[]{:S(2)}) collective-permute-start(bf16[16,2560]{1,0:T(8,128)(2,1)S(1)} %add.14), channel_id=1, source_target_pairs={{0,12},{1,13},{2,14},{3,15},{4,8},{5,9},{6,10},{7,11},{8,4},{9,5},... | collective-permute-start | bytes 245768 | tf_op jit(solution)/shard_map/ppermute | solution.py:354
  44.2 4.1 %collective-permute-start.12 = (bf16[16,1536]{1,0:T(8,128)(2,1)S(1)}, bf16[16,1536]{1,0:T(8,128)(2,1)S(1)}, u32[]{:S(2)}, u32[]{:S(2)}) collective-permute-start(bf16[16,1536]{1,0:T(8,128)(2,1)S(1)} %get-tuple-element.48), channel_id=1, source_target_pairs={{0,2},{1,3},{2,0},{3,1},{4,6},{5,7},{6,4},{7,5},{8,10},{9,11},{10,... | collective-permute-start | bytes 147464 | tf_op jit(solution)/shard_map/ppermute | solution.py:354
  48.4 10.6 %collective-permute-start.17 = (bf16[16,4096]{1,0:T(8,128)(2,1)S(1)}, bf16[16,4096]{1,0:T(8,128)(2,1)S(1)}, u32[]{:S(2)}, u32[]{:S(2)}) collective-permute-start(bf16[16,4096]{1,0:T(8,128)(2,1)S(1)} %add.11.refs_1_), channel_id=1, source_target_pairs={{0,8},{1,9},{2,10},{3,11},{4,12},{5,13},{6,14},{7,15},{8,0},{9,1},... | collective-permute-start | bytes 393224 | tf_op jit(solution)/shard_map/ppermute | solution.py:354
  49.4 5.1 %collective-permute-start.13 = (bf16[16,4096]{1,0:T(8,128)(2,1)S(1)}, bf16[16,4096]{1,0:T(8,128)(2,1)S(1)}, u32[]{:S(2)}, u32[]{:S(2)}) collective-permute-start(bf16[16,4096]{1,0:T(8,128)(2,1)S(1)} %join.12), channel_id=1, source_target_pairs={{0,2},{1,3},{2,0},{3,1},{4,6},{5,7},{6,4},{7,5},{8,10},{9,11},{10,... | collective-permute-start | bytes 393224 | tf_op jit(solution)/shard_map/ppermute | solution.py:354
  50.7 8.6 %collective-permute-start.19 = (bf16[16,4096]{1,0:T(8,128)(2,1)S(1)}, bf16[16,4096]{1,0:T(8,128)(2,1)S(1)}, u32[]{:S(2)}, u32[]{:S(2)}) collective-permute-start(bf16[16,4096]{1,0:T(8,128)(2,1)S(1)} %join.13), channel_id=1, source_target_pairs={{0,4},{1,5},{2,6},{3,7},{4,0},{5,1},{6,2},{7,3},{8,12},{9,13},{10,... | collective-permute-start | bytes 393224 | tf_op jit(solution)/shard_map/ppermute | solution.py:354
  53.0 6.0 %collective-permute-start.16 = (bf16[16,1536]{1,0:T(8,128)(2,1)S(1)}, bf16[16,1536]{1,0:T(8,128)(2,1)S(1)}, u32[]{:S(2)}, u32[]{:S(2)}) collective-permute-start(bf16[16,1536]{1,0:T(8,128)(2,1)S(1)} %add.12.refs_2_), channel_id=1, source_target_pairs={{0,12},{1,13},{2,14},{3,15},{4,8},{5,9},{6,10},{7,11},{8,4},{9,5},... | collective-permute-start | bytes 147464 | tf_op jit(solution)/shard_map/ppermute | solution.py:354
  (1 other events, 18.1 us)

commit v15 on v14

--- a/solution.py
+++ b/solution.py
@@ -427,10 +427,9 @@
         back[i] = swap(part, far[i - 1])
         if i == 2:
             first_part = part
-    tail_part = total(*sums[-2:])
-    tail = swap(tail_part, far[0])
+    tail = swap(total(*sums[-2:]), far[0])
     send, keep = block[0]
-    beside_own = swap(join([send], [first_part, tail_part]), near[0])
+    beside_own = swap(join([send], [first_part]), near[0])
     acc = own_part(mixes[0], keep, beside_own, head)
     return post(mixes[1], table, acc, tail, [back[i] for i in range(2, experts)])
 

time: 60.7 us -> 61.1 us (level)
  waiting for transfers between devices: 17.7 us -> 19.7 us
  starting transfers between devices: 27 us -> 25.3 us
    ppermute x20, waiting for transfers between devices: 17.7 us -> 19.7 us  [swap(): return lax.ppermute(x, 'expert', [(i, i ^ mask) for i in range(devices)])]
    ppermute x20, starting transfers between devices: 27 us -> 25.3 us  [swap(): return lax.ppermute(x, 'expert', [(i, i ^ mask) for i in range(devices)])]
  transfers between devices with their start and end apart: 20 -> 20, of which waited for: 10 -> 11; matrix products, arithmetic and copies ran while one was open for 0% -> 0% of each run, Pallas kernels for 6% -> 6%
where the time goes in v15:
time: 61.1 us; the launch traced here: 60.9 us
  starting transfers between devices  25.3 us (41%)
  waiting for transfers between devices  19.7 us (32%)
  Pallas kernels  15.6 us (26%)
    ppermute x20, starting transfers between devices, swap(): return lax.ppermute(x, 'expert', [(i, i ^ mask) for i in range(devices)])  25.3 us
    ppermute x20, waiting for transfers between devices, swap(): return lax.ppermute(x, 'expert', [(i, i ^ mask) for i in range(devices)])  19.7 us
    pallas_call x1, Pallas kernels, up(): pl.pallas_call(functools.partial(up_kernel, sources=sources, count=len(pa...  5.27 us
    pallas_call x2, Pallas kernels, down(): pl.pallas_call(functools.partial(down_kernel, columns=columns), in_specs=...  4.92 us
    pallas_call x1, Pallas kernels, first(): pl.pallas_call(first_kernel, in_specs=[SMEM] + [HBM] * 7, out_specs=[VMEM...  2.39 us
    pallas_call x1, Pallas kernels, post(): pl.pallas_call(post_kernel, in_specs=[VMEM] * (4 + len(blocks)), out_spec...  1.27 us
  transfers between devices with their start and end apart: 20, of which 11 were waited for; matrix products, arithmetic and copies ran while one was open for 0% of the time, Pallas kernels for 6%

profile of v15, /device:TPU:0, one launch (start us, length us, event | category | flops | bytes accessed | tf_op | source)
XLA Modules:
  0.0 60.9 jit_solution(11759804359866064235)
XLA Ops:
  0.1 2.4 %first.1 = (bf16[16,4096]{1,0:T(8,128)(2,1)S(1)}, bf16[128,4096]{1,0:T(8,128)(2,1)S(1)}, f32[3,4096]{1,0:T(4,128)S(1)}, s32[4,16]{1,0:T(4,128)S(1)}, f32[4,16]{1,0:T(4,128)S(1)}) custom-call(s32[2]{0:T(128)S(1)} %pad_add_fusion.info_ref, bf16[128,4096]{1,0:T(8,128)(2,1)} %refs_0_.1, s32[4,16]{1,0:T(4,128)} %bitcast.6, f32[2,4096]{1,0:T(2,128)} %refs_2_.1, ...), custom_call_target="tpu_custom_call" | custom-call | flops 1 | bytes 1 | tf_op jit(solution)/shard_map/first/pallas_call | solution.py:78
  2.5 5.1 %collective-permute-start = (bf16[16,4096]{1,0:T(8,128)(2,1)S(1)}, bf16[16,4096]{1,0:T(8,128)(2,1)S(1)}, u32[]{:S(2)}, u32[]{:S(2)}) collective-permute-start(bf16[16,4096]{1,0:T(8,128)(2,1)S(1)} %get-tuple-element.31), channel_id=1, source_target_pairs={{0,12},{1,13},{2,14},{3,15},{4,8},{5,9},{6,10},{7,11},{8,4},{9,5},... | collective-permute-start | bytes 393224 | tf_op jit(solution)/shard_map/ppermute | solution.py:354
  9.1 1.7 %collective-permute-start.1 = (bf16[16,4096]{1,0:T(8,128)(2,1)S(1)}, bf16[16,4096]{1,0:T(8,128)(2,1)S(1)}, u32[]{:S(2)}, u32[]{:S(2)}) collective-permute-start(bf16[16,4096]{1,0:T(8,128)(2,1)S(1)} %get-tuple-element.36.refs_0_), channel_id=1, source_target_pairs={{0,2},{1,3},{2,0},{3,1},{4,6},{5,7},{6,4},{7,5},{8,10},{9,11},{10,... | collective-permute-start | bytes 393224 | tf_op jit(solution)/shard_map/ppermute | solution.py:354
  10.8 1.2 %collective-permute-done.after_ref.refs_2_ = bf16[16,4096]{1,0:T(8,128)(2,1)S(1)} collective-permute-done((bf16[16,4096]{1,0:T(8,128)(2,1)S(1)}, bf16[16,4096]{1,0:T(8,128)(2,1)S(1)}, u32[]{:S(2)}, u32[]{:S(2)}) %collective-permute-start) | collective-permute-done | bytes 131104 | tf_op jit(solution)/shard_map/ppermute | solution.py:354
  12.0 1.8 %collective-permute-start.2 = (bf16[16,4096]{1,0:T(8,128)(2,1)S(1)}, bf16[16,4096]{1,0:T(8,128)(2,1)S(1)}, u32[]{:S(2)}, u32[]{:S(2)}) collective-permute-start(bf16[16,4096]{1,0:T(8,128)(2,1)S(1)} %collective-permute-done.after_ref.refs_2_), channel_id=1, source_target_pairs={{0,2},{1,3},{2,0},{3,1},{4,6},{5,7},{6,4},{7,5},{8,10},{9,11},{10,... | collective-permute-start | bytes 393224 | tf_op jit(solution)/shard_map/ppermute | solution.py:354
  13.9 1.2 %collective-permute-done.6.refs_2_ = bf16[16,4096]{1,0:T(8,128)(2,1)S(1)} collective-permute-done((bf16[16,4096]{1,0:T(8,128)(2,1)S(1)}, bf16[16,4096]{1,0:T(8,128)(2,1)S(1)}, u32[]{:S(2)}, u32[]{:S(2)}) %collective-permute-start.6) | collective-permute-done | bytes 131104 | tf_op jit(solution)/shard_map/ppermute | solution.py:354
  15.1 1.6 %collective-permute-start.7 = (bf16[16,4096]{1,0:T(8,128)(2,1)S(1)}, bf16[16,4096]{1,0:T(8,128)(2,1)S(1)}, u32[]{:S(2)}, u32[]{:S(2)}) collective-permute-start(bf16[16,4096]{1,0:T(8,128)(2,1)S(1)} %collective-permute-done.6.refs_2_), channel_id=1, source_target_pairs={{0,2},{1,3},{2,0},{3,1},{4,6},{5,7},{6,4},{7,5},{8,10},{9,11},{10,... | collective-permute-start | bytes 393224 | tf_op jit(solution)/shard_map/ppermute | solution.py:354
  16.7 2.0 %collective-permute-done.4.refs_0_ = bf16[16,4096]{1,0:T(8,128)(2,1)S(1)} collective-permute-done((bf16[16,4096]{1,0:T(8,128)(2,1)S(1)}, bf16[16,4096]{1,0:T(8,128)(2,1)S(1)}, u32[]{:S(2)}, u32[]{:S(2)}) %collective-permute-start.4) | collective-permute-done | bytes 131104 | tf_op jit(solution)/shard_map/ppermute | solution.py:354
  18.7 1.6 %collective-permute-start.5 = (bf16[16,4096]{1,0:T(8,128)(2,1)S(1)}, bf16[16,4096]{1,0:T(8,128)(2,1)S(1)}, u32[]{:S(2)}, u32[]{:S(2)}) collective-permute-start(bf16[16,4096]{1,0:T(8,128)(2,1)S(1)} %join.8.refs_0_), channel_id=1, source_target_pairs={{0,2},{1,3},{2,0},{3,1},{4,6},{5,7},{6,4},{7,5},{8,10},{9,11},{10,... | collective-permute-start | bytes 393224 | tf_op jit(solution)/shard_map/ppermute | solution.py:354
  20.4 3.3 %collective-permute-done.5.refs_1_ = bf16[16,4096]{1,0:T(8,128)(2,1)S(1)} collective-permute-done((bf16[16,4096]{1,0:T(8,128)(2,1)S(1)}, bf16[16,4096]{1,0:T(8,128)(2,1)S(1)}, u32[]{:S(2)}, u32[]{:S(2)}) %collective-permute-start.5) | collective-permute-done | bytes 131104 | tf_op jit(solution)/shard_map/ppermute | solution.py:354
  23.8 1.9 %collective-permute-done.8.refs_3_ = bf16[64,4096]{1,0:T(8,128)(2,1)S(1)} collective-permute-done((bf16[64,4096]{1,0:T(8,128)(2,1)S(1)}, bf16[64,4096]{1,0:T(8,128)(2,1)S(1)}, u32[]{:S(2)}, u32[]{:S(2)}) %collective-permute-start.8) | collective-permute-done | bytes 524320 | tf_op jit(solution)/shard_map/ppermute | solution.py:354
  25.7 5.3 %up.1.h_ref = bf16[256,2048]{1,0:T(8,128)(2,1)S(1)} custom-call(bf16[64,4096]{1,0:T(8,128)(2,1)S(1)} %join.7.refs_0_, bf16[64,4096]{1,0:T(8,128)(2,1)S(1)} %collective-permute-done.3.refs_1_, bf16[64,4096]{1,0:T(8,128)(2,1)S(1)} %join.10.refs_2_, bf16[64,4096]{1,0:T(8,128)(2,1)S(1)} %collective-permute-done.8.refs_3_, bf16[2048,4096]{1,0:T(8,128)(2,1)S(1)} %copy-done), custom_call_target="tpu_custom_call" | custom-call | flops 1 | bytes 1 | tf_op jit(solution)/shard_map/up/pallas_call | solution.py:194
  31.0 3.1 %down.2 = (f32[128,2560]{1,0:T(8,128)S(1)}, bf16[128,2560]{1,0:T(8,128)(2,1)S(1)}) custom-call(bf16[256,2048]{1,0:T(8,128)(2,1)S(1)} %up.1.h_ref, bf16[2048,4096]{1,0:T(8,128)(2,1)S(1)} %bitcast.5), custom_call_target="tpu_custom_call" | custom-call | flops 1 | bytes 1 | tf_op jit(solution)/shard_map/down/pallas_call | solution.py:222
  34.4 1.8 %down.3 = (f32[128,1536]{1,0:T(8,128)S(1)}, bf16[128,1536]{1,0:T(8,128)(2,1)S(1)}) custom-call(bf16[256,2048]{1,0:T(8,128)(2,1)S(1)} %up.1.h_ref, bf16[2048,4096]{1,0:T(8,128)(2,1)S(1)} %bitcast.5), custom_call_target="tpu_custom_call" | custom-call | flops 1 | bytes 1 | tf_op jit(solution)/shard_map/down/pallas_call | solution.py:222
  36.7 1.6 %collective-permute-start.13 = (bf16[16,2560]{1,0:T(8,128)(2,1)S(1)}, bf16[16,2560]{1,0:T(8,128)(2,1)S(1)}, u32[]{:S(2)}, u32[]{:S(2)}) collective-permute-start(bf16[16,2560]{1,0:T(8,128)(2,1)S(1)} %get-tuple-element.48), channel_id=1, source_target_pairs={{0,2},{1,3},{2,0},{3,1},{4,6},{5,7},{6,4},{7,5},{8,10},{9,11},{10,... | collective-permute-start | bytes 245768 | tf_op jit(solution)/shard_map/ppermute | solution.py:354
  38.4 1.5 %collective-permute-start.11 = (bf16[16,4096]{1,0:T(8,128)(2,1)S(1)}, bf16[16,4096]{1,0:T(8,128)(2,1)S(1)}, u32[]{:S(2)}, u32[]{:S(2)}) collective-permute-start(bf16[16,4096]{1,0:T(8,128)(2,1)S(1)} %get-tuple-element.46), channel_id=1, source_target_pairs={{0,2},{1,3},{2,0},{3,1},{4,6},{5,7},{6,4},{7,5},{8,10},{9,11},{10,... | collective-permute-start | bytes 393224 | tf_op jit(solution)/shard_map/ppermute | solution.py:354
  40.5 1.1 %collective-permute-done.13.refs_1_ = bf16[16,2560]{1,0:T(8,128)(2,1)S(1)} collective-permute-done((bf16[16,2560]{1,0:T(8,128)(2,1)S(1)}, bf16[16,2560]{1,0:T(8,128)(2,1)S(1)}, u32[]{:S(2)}, u32[]{:S(2)}) %collective-permute-start.13) | collective-permute-done | bytes 81952 | tf_op jit(solution)/shard_map/ppermute | solution.py:354
  41.7 2.5 %collective-permute-start.14 = (bf16[16,2560]{1,0:T(8,128)(2,1)S(1)}, bf16[16,2560]{1,0:T(8,128)(2,1)S(1)}, u32[]{:S(2)}, u32[]{:S(2)}) collective-permute-start(bf16[16,2560]{1,0:T(8,128)(2,1)S(1)} %add.13), channel_id=1, source_target_pairs={{0,12},{1,13},{2,14},{3,15},{4,8},{5,9},{6,10},{7,11},{8,4},{9,5},... | collective-permute-start | bytes 245768 | tf_op jit(solution)/shard_map/ppermute | solution.py:354
  46.0 1.2 %collective-permute-start.12 = (bf16[16,4096]{1,0:T(8,128)(2,1)S(1)}, bf16[16,4096]{1,0:T(8,128)(2,1)S(1)}, u32[]{:S(2)}, u32[]{:S(2)}) collective-permute-start(bf16[16,4096]{1,0:T(8,128)(2,1)S(1)} %join.12), channel_id=1, source_target_pairs={{0,2},{1,3},{2,0},{3,1},{4,6},{5,7},{6,4},{7,5},{8,10},{9,11},{10,... | collective-permute-start | bytes 393224 | tf_op jit(solution)/shard_map/ppermute | solution.py:354
  47.3 1.4 %collective-permute-done.14.got_ref.refs_1_ = bf16[16,2560]{1,0:T(8,128)(2,1)S(1)} collective-permute-done((bf16[16,2560]{1,0:T(8,128)(2,1)S(1)}, bf16[16,2560]{1,0:T(8,128)(2,1)S(1)}, u32[]{:S(2)}, u32[]{:S(2)}) %collective-permute-start.14) | collective-permute-done | bytes 81952 | tf_op jit(solution)/shard_map/ppermute | solution.py:354
  50.2 3.5 %collective-permute-done.15.refs_1_ = bf16[16,1536]{1,0:T(8,128)(2,1)S(1)} collective-permute-done((bf16[16,1536]{1,0:T(8,128)(2,1)S(1)}, bf16[16,1536]{1,0:T(8,128)(2,1)S(1)}, u32[]{:S(2)}, u32[]{:S(2)}) %collective-permute-start.15) | collective-permute-done | bytes 49184 | tf_op jit(solution)/shard_map/ppermute | solution.py:354
  53.7 2.1 %collective-permute-start.16 = (bf16[16,1536]{1,0:T(8,128)(2,1)S(1)}, bf16[16,1536]{1,0:T(8,128)(2,1)S(1)}, u32[]{:S(2)}, u32[]{:S(2)}) collective-permute-start(bf16[16,1536]{1,0:T(8,128)(2,1)S(1)} %add.14), channel_id=1, source_target_pairs={{0,12},{1,13},{2,14},{3,15},{4,8},{5,9},{6,10},{7,11},{8,4},{9,5},... | collective-permute-start | bytes 147464 | tf_op jit(solution)/shard_map/ppermute | solution.py:354
  56.2 3.5 %collective-permute-done.16.tail_ref = bf16[16,1536]{1,0:T(8,128)(2,1)S(1)} collective-permute-done((bf16[16,1536]{1,0:T(8,128)(2,1)S(1)}, bf16[16,1536]{1,0:T(8,128)(2,1)S(1)}, u32[]{:S(2)}, u32[]{:S(2)}) %collective-permute-start.16) | collective-permute-done | bytes 49184 | tf_op jit(solution)/shard_map/ppermute | solution.py:354
  59.6 1.3 %post.1 = bf16[128,4096]{1,0:T(8,128)(2,1)} custom-call(bf16[128,96]{1,0:T(8,128)(2,1)S(1)} %get-tuple-element.32.mix_ref, f32[3,4096]{1,0:T(4,128)S(1)} %get-tuple-element.33.table_ref, f32[128,4096]{1,0:T(8,128)S(1)} %own_part.1.acc_ref, bf16[16,1536]{1,0:T(8,128)(2,1)S(1)} %collective-permute-done.16.tail_ref, ...), custom_call_target="tpu_custom_call" | custom-call | flops 1 | bytes 1 | tf_op jit(solution)/shard_map/post/pallas_call | solution.py:322
  (49 shorter events, 7.3 us)
Async XLA Ops:
  2.5 9.5 %collective-permute-start = (bf16[16,4096]{1,0:T(8,128)(2,1)S(1)}, bf16[16,4096]{1,0:T(8,128)(2,1)S(1)}, u32[]{:S(2)}, u32[]{:S(2)}) collective-permute-start(bf16[16,4096]{1,0:T(8,128)(2,1)S(1)} %get-tuple-element.31), channel_id=1, source_target_pairs={{0,12},{1,13},{2,14},{3,15},{4,8},{5,9},{6,10},{7,11},{8,4},{9,5},... | collective-permute-start | bytes 393224 | tf_op jit(solution)/shard_map/ppermute | solution.py:354
  7.6 23.4 %slice-start = ((s8[16777216]{0:T(1024)(128)(4,1)}), s8[4194304]{0:T(1024)(128)(4,1)S(1)}, s32[]{:S(2)}) async-start(s8[16777216]{0:T(1024)(128)(4,1)} %bitcast.4), calls=%async_computation | async-start | bytes 8388608
  7.6 23.4 %slice-start.1 = ((s8[16777216]{0:T(1024)(128)(4,1)}), s8[4194304]{0:T(1024)(128)(4,1)S(1)}, s32[]{:S(2)}) async-start(s8[16777216]{0:T(1024)(128)(4,1)} %bitcast.4), calls=%async_computation.1 | async-start | bytes 8388608
  7.6 23.4 %slice-start.2 = ((s8[16777216]{0:T(1024)(128)(4,1)}), s8[4194304]{0:T(1024)(128)(4,1)S(1)}, s32[]{:S(2)}) async-start(s8[16777216]{0:T(1024)(128)(4,1)} %bitcast.4), calls=%async_computation.2 | async-start | bytes 8388608
  7.6 23.4 %slice-start.3 = ((s8[16777216]{0:T(1024)(128)(4,1)}), s8[4194304]{0:T(1024)(128)(4,1)S(1)}, s32[]{:S(2)}) async-start(s8[16777216]{0:T(1024)(128)(4,1)} %bitcast.4), calls=%async_computation.3 | async-start | bytes 8388608
  8.4 6.7 %collective-permute-start.6 = (bf16[16,4096]{1,0:T(8,128)(2,1)S(1)}, bf16[16,4096]{1,0:T(8,128)(2,1)S(1)}, u32[]{:S(2)}, u32[]{:S(2)}) collective-permute-start(bf16[16,4096]{1,0:T(8,128)(2,1)S(1)} %get-tuple-element.38), channel_id=1, source_target_pairs={{0,4},{1,5},{2,6},{3,7},{4,0},{5,1},{6,2},{7,3},{8,12},{9,13},{10,... | collective-permute-start | bytes 393224 | tf_op jit(solution)/shard_map/ppermute | solution.py:354
  8.5 10.2 %collective-permute-start.4 = (bf16[16,4096]{1,0:T(8,128)(2,1)S(1)}, bf16[16,4096]{1,0:T(8,128)(2,1)S(1)}, u32[]{:S(2)}, u32[]{:S(2)}) collective-permute-start(bf16[16,4096]{1,0:T(8,128)(2,1)S(1)} %get-tuple-element.37), channel_id=1, source_target_pairs={{0,8},{1,9},{2,10},{3,11},{4,12},{5,13},{6,14},{7,15},{8,0},{9,1},... | collective-permute-start | bytes 393224 | tf_op jit(solution)/shard_map/ppermute | solution.py:354
  9.1 11.2 %collective-permute-start.1 = (bf16[16,4096]{1,0:T(8,128)(2,1)S(1)}, bf16[16,4096]{1,0:T(8,128)(2,1)S(1)}, u32[]{:S(2)}, u32[]{:S(2)}) collective-permute-start(bf16[16,4096]{1,0:T(8,128)(2,1)S(1)} %get-tuple-element.36.refs_0_), channel_id=1, source_target_pairs={{0,2},{1,3},{2,0},{3,1},{4,6},{5,7},{6,4},{7,5},{8,10},{9,11},{10,... | collective-permute-start | bytes 393224 | tf_op jit(solution)/shard_map/ppermute | solution.py:354
  12.0 8.3 %collective-permute-start.2 = (bf16[16,4096]{1,0:T(8,128)(2,1)S(1)}, bf16[16,4096]{1,0:T(8,128)(2,1)S(1)}, u32[]{:S(2)}, u32[]{:S(2)}) collective-permute-start(bf16[16,4096]{1,0:T(8,128)(2,1)S(1)} %collective-permute-done.after_ref.refs_2_), channel_id=1, source_target_pairs={{0,2},{1,3},{2,0},{3,1},{4,6},{5,7},{6,4},{7,5},{8,10},{9,11},{10,... | collective-permute-start | bytes 393224 | tf_op jit(solution)/shard_map/ppermute | solution.py:354
  15.1 5.3 %collective-permute-start.7 = (bf16[16,4096]{1,0:T(8,128)(2,1)S(1)}, bf16[16,4096]{1,0:T(8,128)(2,1)S(1)}, u32[]{:S(2)}, u32[]{:S(2)}) collective-permute-start(bf16[16,4096]{1,0:T(8,128)(2,1)S(1)} %collective-permute-done.6.refs_2_), channel_id=1, source_target_pairs={{0,2},{1,3},{2,0},{3,1},{4,6},{5,7},{6,4},{7,5},{8,10},{9,11},{10,... | collective-permute-start | bytes 393224 | tf_op jit(solution)/shard_map/ppermute | solution.py:354
  18.7 5.0 %collective-permute-start.5 = (bf16[16,4096]{1,0:T(8,128)(2,1)S(1)}, bf16[16,4096]{1,0:T(8,128)(2,1)S(1)}, u32[]{:S(2)}, u32[]{:S(2)}) collective-permute-start(bf16[16,4096]{1,0:T(8,128)(2,1)S(1)} %join.8.refs_0_), channel_id=1, source_target_pairs={{0,2},{1,3},{2,0},{3,1},{4,6},{5,7},{6,4},{7,5},{8,10},{9,11},{10,... | collective-permute-start | bytes 393224 | tf_op jit(solution)/shard_map/ppermute | solution.py:354
  20.3 3.5 %collective-permute-start.3 = (bf16[64,4096]{1,0:T(8,128)(2,1)S(1)}, bf16[64,4096]{1,0:T(8,128)(2,1)S(1)}, u32[]{:S(2)}, u32[]{:S(2)}) collective-permute-start(bf16[64,4096]{1,0:T(8,128)(2,1)S(1)} %join.7.refs_0_), channel_id=1, source_target_pairs={{0,1},{1,0},{2,3},{3,2},{4,5},{5,4},{6,7},{7,6},{8,9},{9,8},{10,11... | collective-permute-start | bytes 1572872 | tf_op jit(solution)/shard_map/ppermute | solution.py:354
  23.7 2.0 %collective-permute-start.8 = (bf16[64,4096]{1,0:T(8,128)(2,1)S(1)}, bf16[64,4096]{1,0:T(8,128)(2,1)S(1)}, u32[]{:S(2)}, u32[]{:S(2)}) collective-permute-start(bf16[64,4096]{1,0:T(8,128)(2,1)S(1)} %join.10.refs_2_), channel_id=1, source_target_pairs={{0,1},{1,0},{2,3},{3,2},{4,5},{5,4},{6,7},{7,6},{8,9},{9,8},{10,11... | collective-permute-start | bytes 1572872 | tf_op jit(solution)/shard_map/ppermute | solution.py:354
  34.2 2.2 %collective-permute-start.9 = (bf16[128,2560]{1,0:T(8,128)(2,1)S(1)}, bf16[128,2560]{1,0:T(8,128)(2,1)S(1)}, u32[]{:S(2)}, u32[]{:S(2)}) collective-permute-start(bf16[128,2560]{1,0:T(8,128)(2,1)S(1)} %get-tuple-element.40), channel_id=1, source_target_pairs={{0,1},{1,0},{2,3},{3,2},{4,5},{5,4},{6,7},{7,6},{8,9},{9,8},{10,11... | collective-permute-start | bytes 1966088 | tf_op jit(solution)/shard_map/ppermute | solution.py:354
  36.4 1.9 %collective-permute-start.10 = (bf16[128,1536]{1,0:T(8,128)(2,1)S(1)}, bf16[128,1536]{1,0:T(8,128)(2,1)S(1)}, u32[]{:S(2)}, u32[]{:S(2)}) collective-permute-start(bf16[128,1536]{1,0:T(8,128)(2,1)S(1)} %join.11), channel_id=1, source_target_pairs={{0,1},{1,0},{2,3},{3,2},{4,5},{5,4},{6,7},{7,6},{8,9},{9,8},{10,11... | collective-permute-start | bytes 1179656 | tf_op jit(solution)/shard_map/ppermute | solution.py:354
  36.7 4.9 %collective-permute-start.13 = (bf16[16,2560]{1,0:T(8,128)(2,1)S(1)}, bf16[16,2560]{1,0:T(8,128)(2,1)S(1)}, u32[]{:S(2)}, u32[]{:S(2)}) collective-permute-start(bf16[16,2560]{1,0:T(8,128)(2,1)S(1)} %get-tuple-element.48), channel_id=1, source_target_pairs={{0,2},{1,3},{2,0},{3,1},{4,6},{5,7},{6,4},{7,5},{8,10},{9,11},{10,... | collective-permute-start | bytes 245768 | tf_op jit(solution)/shard_map/ppermute | solution.py:354
  38.4 6.4 %collective-permute-start.11 = (bf16[16,4096]{1,0:T(8,128)(2,1)S(1)}, bf16[16,4096]{1,0:T(8,128)(2,1)S(1)}, u32[]{:S(2)}, u32[]{:S(2)}) collective-permute-start(bf16[16,4096]{1,0:T(8,128)(2,1)S(1)} %get-tuple-element.46), channel_id=1, source_target_pairs={{0,2},{1,3},{2,0},{3,1},{4,6},{5,7},{6,4},{7,5},{8,10},{9,11},{10,... | collective-permute-start | bytes 393224 | tf_op jit(solution)/shard_map/ppermute | solution.py:354
  39.9 7.3 %collective-permute-start.18 = (bf16[16,4096]{1,0:T(8,128)(2,1)S(1)}, bf16[16,4096]{1,0:T(8,128)(2,1)S(1)}, u32[]{:S(2)}, u32[]{:S(2)}) collective-permute-start(bf16[16,4096]{1,0:T(8,128)(2,1)S(1)} %get-tuple-element.52), channel_id=1, source_target_pairs={{0,2},{1,3},{2,0},{3,1},{4,6},{5,7},{6,4},{7,5},{8,10},{9,11},{10,... | collective-permute-start | bytes 393224 | tf_op jit(solution)/shard_map/ppermute | solution.py:354
  41.7 7.0 %collective-permute-start.14 = (bf16[16,2560]{1,0:T(8,128)(2,1)S(1)}, bf16[16,2560]{1,0:T(8,128)(2,1)S(1)}, u32[]{:S(2)}, u32[]{:S(2)}) collective-permute-start(bf16[16,2560]{1,0:T(8,128)(2,1)S(1)} %add.13), channel_id=1, source_target_pairs={{0,12},{1,13},{2,14},{3,15},{4,8},{5,9},{6,10},{7,11},{8,4},{9,5},... | collective-permute-start | bytes 245768 | tf_op jit(solution)/shard_map/ppermute | solution.py:354
  44.9 14.8 %collective-permute-start.17 = (bf16[16,4096]{1,0:T(8,128)(2,1)S(1)}, bf16[16,4096]{1,0:T(8,128)(2,1)S(1)}, u32[]{:S(2)}, u32[]{:S(2)}) collective-permute-start(bf16[16,4096]{1,0:T(8,128)(2,1)S(1)} %add.11.refs_1_), channel_id=1, source_target_pairs={{0,8},{1,9},{2,10},{3,11},{4,12},{5,13},{6,14},{7,15},{8,0},{9,1},... | collective-permute-start | bytes 393224 | tf_op jit(solution)/shard_map/ppermute | solution.py:354
  46.0 9.7 %collective-permute-start.12 = (bf16[16,4096]{1,0:T(8,128)(2,1)S(1)}, bf16[16,4096]{1,0:T(8,128)(2,1)S(1)}, u32[]{:S(2)}, u32[]{:S(2)}) collective-permute-start(bf16[16,4096]{1,0:T(8,128)(2,1)S(1)} %join.12), channel_id=1, source_target_pairs={{0,2},{1,3},{2,0},{3,1},{4,6},{5,7},{6,4},{7,5},{8,10},{9,11},{10,... | collective-permute-start | bytes 393224 | tf_op jit(solution)/shard_map/ppermute | solution.py:354
  48.6 11.0 %collective-permute-start.19 = (bf16[16,4096]{1,0:T(8,128)(2,1)S(1)}, bf16[16,4096]{1,0:T(8,128)(2,1)S(1)}, u32[]{:S(2)}, u32[]{:S(2)}) collective-permute-start(bf16[16,4096]{1,0:T(8,128)(2,1)S(1)} %join.13), channel_id=1, source_target_pairs={{0,4},{1,5},{2,6},{3,7},{4,0},{5,1},{6,2},{7,3},{8,12},{9,13},{10,... | collective-permute-start | bytes 393224 | tf_op jit(solution)/shard_map/ppermute | solution.py:354
  49.6 4.1 %collective-permute-start.15 = (bf16[16,1536]{1,0:T(8,128)(2,1)S(1)}, bf16[16,1536]{1,0:T(8,128)(2,1)S(1)}, u32[]{:S(2)}, u32[]{:S(2)}) collective-permute-start(bf16[16,1536]{1,0:T(8,128)(2,1)S(1)} %get-tuple-element.50), channel_id=1, source_target_pairs={{0,2},{1,3},{2,0},{3,1},{4,6},{5,7},{6,4},{7,5},{8,10},{9,11},{10,... | collective-permute-start | bytes 147464 | tf_op jit(solution)/shard_map/ppermute | solution.py:354
  53.7 6.0 %collective-permute-start.16 = (bf16[16,1536]{1,0:T(8,128)(2,1)S(1)}, bf16[16,1536]{1,0:T(8,128)(2,1)S(1)}, u32[]{:S(2)}, u32[]{:S(2)}) collective-permute-start(bf16[16,1536]{1,0:T(8,128)(2,1)S(1)} %add.14), channel_id=1, source_target_pairs={{0,12},{1,13},{2,14},{3,15},{4,8},{5,9},{6,10},{7,11},{8,4},{9,5},... | collective-permute-start | bytes 147464 | tf_op jit(solution)/shard_map/ppermute | solution.py:354
  (1 other events, 18.1 us)

commit v16 on v12

--- a/solution.py
+++ b/solution.py
@@ -175,15 +175,15 @@
         rows_ref[to:to + high - low, :] = refs[source][low:high, :]
         to += high - low
     hidden = w_ref.shape[0]
-    tile = min(512, hidden)
+    tile = min(1024, hidden)
 
     @pl.loop(0, hidden // tile)
     def _(i):
         cut = pl.ds(pl.multiple_of(i * tile, tile), tile)
         lifted = lax.dot_general(
-            rows_ref[...], w_ref[cut, :], (((1,), (1,)), ((), ())), preferred_element_type=F32
+            w_ref[cut, :], rows_ref[...], (((1,), (1,)), ((), ())), preferred_element_type=F32
         )
-        out_ref[:, cut] = jax.nn.gelu(lifted, approximate=True).astype(BF16)
+        out_ref[:, cut] = jax.nn.gelu(lifted, approximate=True).astype(BF16).T
 
 
 def up(parts, sources, w, after):
@@ -201,56 +201,64 @@
     )(*parts, w, *after)
 
 
-def down_kernel(h_ref, w_ref, *refs, columns, low):
-    keep_ref, send_ref = refs[-2:]
+def down_kernel(h_ref, w_ref, *refs, low, columns, pieces):
+    keep_ref, sends = refs[-pieces - 1], refs[-pieces:]
+    half = keep_ref.shape[0]
+    height = half // pieces
     first, last, tile = columns
-    half = keep_ref.shape[0]
 
     @pl.loop(0, (last - first) // tile)
     def _(i):
         cut = pl.ds(pl.multiple_of(first + i * tile, tile), tile)
         out = jnp.dot(h_ref[low:low + 2 * half, :], w_ref[:, cut], preferred_element_type=F32)
         keep_ref[:, cut] = out[:half]
-        send_ref[:, cut] = out[half:].astype(BF16)
-
-
-def down(hid, rows, w, columns, after, before):
+        for k, send_ref in enumerate(sends):
+            at = half + k * height
+            send_ref[:, cut] = out[at:at + height].astype(BF16)
+
+
+def down(hid, rows, w, columns, pieces, after, before):
     half = (rows[1] - rows[0]) // 2
     width = w.shape[1]
-    skip = 2 + len(after)
-    return pl.pallas_call(
-        functools.partial(down_kernel, columns=columns, low=rows[0]),
+    return pl.pallas_call(
+        functools.partial(down_kernel, low=rows[0], columns=columns, pieces=pieces),
         in_specs=[VMEM] * 2 + [ANY] * len(after) + [VMEM] * len(before),
-        out_specs=[VMEM] * 2,
-        out_shape=[
-            jax.ShapeDtypeStruct((half, width), F32),
-            jax.ShapeDtypeStruct((half, width), BF16),
-        ],
-        input_output_aliases={skip + i: i for i in range(len(before))},
+        out_specs=[VMEM] * (1 + pieces),
+        out_shape=[jax.ShapeDtypeStruct((half, width), F32)]
+        + [jax.ShapeDtypeStruct((half // pieces, width), BF16)] * pieces,
+        input_output_aliases={2 + len(after) + i: i for i in range(len(before))},
         compiler_params=params(8),
         cost_estimate=FREE,
         name="down",
     )(hid, w, *after, *before)
 
 
-def add_kernel(keep_ref, got_ref, *refs, cuts):
-    for ref, (low, high) in zip(refs[len(refs) - len(cuts):], cuts):
-        ref[...] = (keep_ref[low:high] + got_ref[low:high].astype(F32)).astype(ref.dtype)
-
-
-def add(keep, got, cuts, kinds, after=()):
-    width = keep.shape[1]
-    return pl.pallas_call(
-        functools.partial(add_kernel, cuts=cuts),
-        in_specs=[VMEM] * 2 + [ANY] * len(after),
+def add_kernel(keep_ref, *refs, pieces, cuts):
+    gots, outs = refs[:pieces], refs[len(refs) - len(cuts):]
+    height = gots[0].shape[0]
+    for ref, (low, high, first, last) in zip(outs, cuts):
+        step = min(height, high - low)
+        for at in range(low, high, step):
+            from_ = at % height
+            total = keep_ref[at:at + step, first:last] + gots[at // height][
+                from_:from_ + step, first:last
+            ].astype(F32)
+            ref[at - low:at - low + step, :] = total.astype(ref.dtype)
+
+
+def add(keep, gots, cuts, kinds):
+    return pl.pallas_call(
+        functools.partial(add_kernel, pieces=len(gots), cuts=cuts),
+        in_specs=[VMEM] * (1 + len(gots)),
         out_specs=[VMEM] * len(cuts),
         out_shape=[
-            jax.ShapeDtypeStruct((high - low, width), k) for (low, high), k in zip(cuts, kinds)
+            jax.ShapeDtypeStruct((high - low, last - first), k)
+            for (low, high, first, last), k in zip(cuts, kinds)
         ],
         compiler_params=params(8),
         cost_estimate=FREE,
         name="add",
-    )(keep, got, *after)
+    )(keep, *gots)
 
 
 def own_kernel(mix_ref, keep_ref, near_ref, got_ref, acc_ref):
@@ -271,14 +279,20 @@
     )(mix, keep, near, got)
 
 
-def post_kernel(mix_ref, table_ref, acc_ref, *refs):
-    blocks = refs[:-3]
+def post_kernel(mix_ref, table_ref, acc_ref, *refs, counts):
     out_hbm, out_ref, sems = refs[-3:]
     step = out_ref.shape[1] // sems.shape[0]
     copies = []
     for i in range(sems.shape[0]):
+        values = []
+        at = 0
+        for count in counts:
+            each = out_ref.shape[1] // count
+            piece, low = divmod(i * step, each)
+            values.append(refs[at + piece][:, low:low + step])
+            at += count
+        values = jnp.concatenate(values * 2, axis=0)
         cut = pl.ds(i * step, step)
-        values = jnp.concatenate([ref[:, cut] for ref in blocks] * 2, axis=0)
         mixed = acc_ref[:, cut] + jnp.dot(mix_ref[...], values, preferred_element_type=F32)
         out_ref[:, cut] = (table_ref[2:3, cut] * mixed).astype(BF16)
         copy = pltpu.make_async_copy(out_ref.at[:, cut], out_hbm.at[:, cut], sems.at[i])
@@ -290,16 +304,17 @@
 
 def post(mix, table, acc, blocks):
     tok_rows, width = acc.shape
-    return pl.pallas_call(
-        post_kernel,
-        in_specs=[VMEM] * (3 + len(blocks)),
+    args = [x for block in blocks for x in block]
+    return pl.pallas_call(
+        functools.partial(post_kernel, counts=[len(block) for block in blocks]),
+        in_specs=[VMEM] * (3 + len(args)),
         out_specs=HBM,
         out_shape=jax.ShapeDtypeStruct((tok_rows, width), BF16),
         scratch_shapes=[pltpu.VMEM((tok_rows, width), BF16), pltpu.SemaphoreType.DMA((4,))],
         compiler_params=params(8),
         cost_estimate=FREE,
         name="post",
-    )(mix, table, acc, *blocks)
+    )(mix, table, acc, *args)
 
 
 def shards(tokens, shift, scale, gate, w_up, w_down, pick, count, combine):
@@ -352,49 +367,63 @@
                 for base in range(2 * at * slots, piece.shape[0], height):
                     segments[i].append((len(parts) + k, base, base + 2 * slots))
         parts += pieces
-    others = list(range(2, experts)) + [0]
-    sources = segments[1] + [cut for cuts in zip(*[segments[i] for i in others]) for cut in cuts]
+    far_blocks, near_blocks = [2, 1], list(range(3, experts)) + [0]
+    sources = [
+        cut
+        for members in (far_blocks, near_blocks)
+        for cuts in zip(*[segments[i] for i in members])
+        for cut in cuts
+    ]
     count = sum(high - low for _, low, high in sources)
-    skip = 2 * slots * len(segments[1])
-
-    def gather(keep, send, members, after=()):
+    skip = 2 * slots * len(far_blocks) * len(segments[1])
+    hid = up(parts, sources, w_up, [])
+
+    def gather(keep, sends, columns):
         for i, mask in enumerate(reversed(near[1:])):
             if i:
                 middle = keep.shape[0] // 2
-                keep, send = add(keep, got, [(0, middle), (middle, 2 * middle)], [F32, BF16])
-            got = swap(send, mask)
-        at = [2 * k * slots for k in range(len(members))]
-        cuts = [(x + slots, x + 2 * slots) for x in at] + [(x, x + slots) for x in at]
-        out = add(keep, got, cuts, [BF16] * len(at) + [F32] * len(at), after)
-        return dict(zip(members, zip(out, out[len(at):])))
-
-    def total(i):
-        send, keep = block[i]
-        return add(keep, swap(send, near[0]), [(0, slots)], [BF16])[0]
-
-    hid = up(parts, sources, w_up, [])
-
-    eighth = width // 8
-    ends = [0, 2 * eighth, 7 * eighth, width]
-    tiles = [2 * eighth, 5 * eighth // 2, eighth]
-    steps = list(zip(ends, ends[1:], tiles))
-    keep, send = down(hid, (0, skip), w_down, (0, width, 2 * eighth), [], [])
-    before = down(hid, (skip, count), w_down, steps[0], [keep], [])
-    block = gather(keep, send, [1], before[:1])
-    before = down(hid, (skip, count), w_down, steps[1], [block[1][0]], before)
-    part = total(1)
-    keep, send = down(hid, (skip, count), w_down, steps[2], [part], before)
-    block.update(gather(keep, send, others))
-    back = {1: swap(part, far[0])}
-    link = join([back[1]], [])
-    for i in late:
-        part = total(i)
-        if i == 2:
-            part = join([part], [link])
-        back[i] = swap(part, far[i - 1])
-    own_send = join([block[0][0]], [part])
-    acc = own_part(mixes[0], block[0][1], swap(own_send, near[0]), back[1])
-    return post(mixes[1], table, acc, [back[i] for i in late])
+                height = middle // len(sends)
+                cuts = [(0, middle, 0, width)] + [
+                    (at, at + height, 0, width) for at in range(middle, 2 * middle, height)
+                ]
+                keep, *sends = add(keep, gots, cuts, [F32] + [BF16] * len(sends))
+            gots = [swap(send, mask) for send in sends]
+        cuts = []
+        for at, pieces in enumerate(columns):
+            each = width // pieces
+            for c in range(pieces):
+                for side in (1, 0):
+                    low = (2 * at + side) * slots
+                    cuts.append((low, low + slots, c * each, (c + 1) * each))
+        out = add(keep, gots, cuts, [BF16, F32] * (len(cuts) // 2))
+        split = []
+        for pieces in columns:
+            split.append([out[2 * c:2 * c + 2] for c in range(pieces)])
+            out = out[2 * pieces:]
+        return split
+
+    def total(send, keep):
+        cuts = [(0, slots, 0, keep.shape[1])]
+        return add(keep, [swap(send, near[0])], cuts, [BF16])[0]
+
+    tile = width // 4
+    keep, *sends = down(hid, (0, skip), w_down, (0, width, tile), 1, [], [])
+    far_rows = gather(keep, sends, [1, 1])
+    after = [far_rows[0][0][0]]
+    keep, *sends = down(hid, (skip, count), w_down, (0, width, tile), 4, after, [])
+    near_rows = gather(keep, sends, [2] * (experts - 3) + [1])
+    back = []
+    for block, mask in zip(far_rows[::-1] + near_rows[:-1], far):
+        parts_of = [total(*piece) for piece in block]
+        back.append([swap(part, mask) for part in parts_of])
+        if mask == far[1]:
+            far_part = parts_of[0]
+    for i in range(2):
+        for _ in range(2):
+            back[i] = [join(back[i], [])]
+    ((send, keep),) = near_rows[-1]
+    acc = own_part(mixes[0], keep, swap(join([send], [far_part]), near[0]), back[0][0])
+    return post(mixes[1], table, acc, back[1:])
 
 
 def solution(mesh):

time: 64.1 us -> 61.1 us (0.953)
  waiting for transfers between devices: 21.7 us -> 18.7 us
  Pallas kernels: 18.4 us -> 16.4 us
  starting transfers between devices: 23.4 us -> 25.4 us
    ppermute x18 -> x23, waiting for transfers between devices: 21.7 us -> 18.7 us  [swap(): return lax.ppermute(x, 'expert', [(i, i ^ mask) for i in range(devices)])]
    ppermute x18 -> x23, starting transfers between devices: 23.4 us -> 25.4 us  [swap(): return lax.ppermute(x, 'expert', [(i, i ^ mask) for i in range(devices)])]
    pallas_call x10 -> x9, Pallas kernels: 8.88 us -> 7.25 us  [the longest x2 5.8 us: down(): pl.pallas_call(functools.partial(down_kernel, low=rows[0], columns=column...]
  transfers between devices with their start and end apart: 18 -> 23, of which waited for: 12 -> 13; matrix products, arithmetic and copies ran while one was open for 0% -> 0% of each run, Pallas kernels for 8% -> 7%
where the time goes in v16:
time: 61.1 us; the launch traced here: 60.9 us
  starting transfers between devices  25.4 us (42%)
  waiting for transfers between devices  18.7 us (31%)
  Pallas kernels  16.4 us (27%)
    ppermute x23, starting transfers between devices, swap(): return lax.ppermute(x, 'expert', [(i, i ^ mask) for i in range(devices)])  25.4 us
    ppermute x23, waiting for transfers between devices, swap(): return lax.ppermute(x, 'expert', [(i, i ^ mask) for i in range(devices)])  18.7 us
    pallas_call x2, Pallas kernels, down(): pl.pallas_call(functools.partial(down_kernel, low=rows[0], columns=column...  5.8 us
    pallas_call x1, Pallas kernels, up(): pl.pallas_call(functools.partial(up_kernel, sources=sources, count=len(pa...  5.27 us
    pallas_call x1, Pallas kernels, first(): pl.pallas_call(first_kernel, in_specs=[SMEM] + [HBM] * 7, out_specs=[VMEM...  2.39 us
  transfers between devices with their start and end apart: 23, of which 13 were waited for; matrix products, arithmetic and copies ran while one was open for 0% of the time, Pallas kernels for 7%

profile of v16, /device:TPU:0, one launch (start us, length us, event | category | flops | bytes accessed | tf_op | source)
XLA Modules:
  0.0 60.9 jit_solution(14152514454500036085)
XLA Ops:
  0.1 2.4 %first.1 = (bf16[16,4096]{1,0:T(8,128)(2,1)S(1)}, bf16[128,4096]{1,0:T(8,128)(2,1)S(1)}, f32[3,4096]{1,0:T(4,128)S(1)}, s32[4,16]{1,0:T(4,128)S(1)}, f32[4,16]{1,0:T(4,128)S(1)}) custom-call(s32[2]{0:T(128)S(1)} %pad_add_fusion.info_ref, bf16[128,4096]{1,0:T(8,128)(2,1)} %refs_0_.1, s32[4,16]{1,0:T(4,128)} %bitcast.6, f32[2,4096]{1,0:T(2,128)} %refs_2_.1, ...), custom_call_target="tpu_custom_call" | custom-call | flops 1 | bytes 1 | tf_op jit(solution)/shard_map/first/pallas_call | solution.py:78
  2.5 5.1 %collective-permute-start = (bf16[16,4096]{1,0:T(8,128)(2,1)S(1)}, bf16[16,4096]{1,0:T(8,128)(2,1)S(1)}, u32[]{:S(2)}, u32[]{:S(2)}) collective-permute-start(bf16[16,4096]{1,0:T(8,128)(2,1)S(1)} %get-tuple-element.34), channel_id=1, source_target_pairs={{0,12},{1,13},{2,14},{3,15},{4,8},{5,9},{6,10},{7,11},{8,4},{9,5},... | collective-permute-start | bytes 393224 | tf_op jit(solution)/shard_map/ppermute | solution.py:340
  9.1 1.7 %collective-permute-start.1 = (bf16[16,4096]{1,0:T(8,128)(2,1)S(1)}, bf16[16,4096]{1,0:T(8,128)(2,1)S(1)}, u32[]{:S(2)}, u32[]{:S(2)}) collective-permute-start(bf16[16,4096]{1,0:T(8,128)(2,1)S(1)} %get-tuple-element.39.refs_0_), channel_id=1, source_target_pairs={{0,2},{1,3},{2,0},{3,1},{4,6},{5,7},{6,4},{7,5},{8,10},{9,11},{10,... | collective-permute-start | bytes 393224 | tf_op jit(solution)/shard_map/ppermute | solution.py:340
  10.8 1.2 %collective-permute-done.after_ref.refs_2_ = bf16[16,4096]{1,0:T(8,128)(2,1)S(1)} collective-permute-done((bf16[16,4096]{1,0:T(8,128)(2,1)S(1)}, bf16[16,4096]{1,0:T(8,128)(2,1)S(1)}, u32[]{:S(2)}, u32[]{:S(2)}) %collective-permute-start) | collective-permute-done | bytes 131104 | tf_op jit(solution)/shard_map/ppermute | solution.py:340
  12.0 1.8 %collective-permute-start.2 = (bf16[16,4096]{1,0:T(8,128)(2,1)S(1)}, bf16[16,4096]{1,0:T(8,128)(2,1)S(1)}, u32[]{:S(2)}, u32[]{:S(2)}) collective-permute-start(bf16[16,4096]{1,0:T(8,128)(2,1)S(1)} %collective-permute-done.after_ref.refs_2_), channel_id=1, source_target_pairs={{0,2},{1,3},{2,0},{3,1},{4,6},{5,7},{6,4},{7,5},{8,10},{9,11},{10,... | collective-permute-start | bytes 393224 | tf_op jit(solution)/shard_map/ppermute | solution.py:340
  15.1 1.6 %collective-permute-start.7 = (bf16[16,4096]{1,0:T(8,128)(2,1)S(1)}, bf16[16,4096]{1,0:T(8,128)(2,1)S(1)}, u32[]{:S(2)}, u32[]{:S(2)}) collective-permute-start(bf16[16,4096]{1,0:T(8,128)(2,1)S(1)} %collective-permute-done.6.refs_2_), channel_id=1, source_target_pairs={{0,2},{1,3},{2,0},{3,1},{4,6},{5,7},{6,4},{7,5},{8,10},{9,11},{10,... | collective-permute-start | bytes 393224 | tf_op jit(solution)/shard_map/ppermute | solution.py:340
  16.7 2.0 %collective-permute-done.4.refs_0_ = bf16[16,4096]{1,0:T(8,128)(2,1)S(1)} collective-permute-done((bf16[16,4096]{1,0:T(8,128)(2,1)S(1)}, bf16[16,4096]{1,0:T(8,128)(2,1)S(1)}, u32[]{:S(2)}, u32[]{:S(2)}) %collective-permute-start.4) | collective-permute-done | bytes 131104 | tf_op jit(solution)/shard_map/ppermute | solution.py:340
  18.7 1.6 %collective-permute-start.5 = (bf16[16,4096]{1,0:T(8,128)(2,1)S(1)}, bf16[16,4096]{1,0:T(8,128)(2,1)S(1)}, u32[]{:S(2)}, u32[]{:S(2)}) collective-permute-start(bf16[16,4096]{1,0:T(8,128)(2,1)S(1)} %join.10.refs_0_), channel_id=1, source_target_pairs={{0,2},{1,3},{2,0},{3,1},{4,6},{5,7},{6,4},{7,5},{8,10},{9,11},{10,... | collective-permute-start | bytes 393224 | tf_op jit(solution)/shard_map/ppermute | solution.py:340
  20.4 3.3 %collective-permute-done.5.refs_1_ = bf16[16,4096]{1,0:T(8,128)(2,1)S(1)} collective-permute-done((bf16[16,4096]{1,0:T(8,128)(2,1)S(1)}, bf16[16,4096]{1,0:T(8,128)(2,1)S(1)}, u32[]{:S(2)}, u32[]{:S(2)}) %collective-permute-start.5) | collective-permute-done | bytes 131104 | tf_op jit(solution)/shard_map/ppermute | solution.py:340
  23.8 1.9 %collective-permute-done.8.refs_3_ = bf16[64,4096]{1,0:T(8,128)(2,1)S(1)} collective-permute-done((bf16[64,4096]{1,0:T(8,128)(2,1)S(1)}, bf16[64,4096]{1,0:T(8,128)(2,1)S(1)}, u32[]{:S(2)}, u32[]{:S(2)}) %collective-permute-start.8) | collective-permute-done | bytes 524320 | tf_op jit(solution)/shard_map/ppermute | solution.py:340
  25.7 5.3 %up.1.h_ref = bf16[256,2048]{1,0:T(8,128)(2,1)S(1)} custom-call(bf16[64,4096]{1,0:T(8,128)(2,1)S(1)} %join.9.refs_0_, bf16[64,4096]{1,0:T(8,128)(2,1)S(1)} %collective-permute-done.3.refs_1_, bf16[64,4096]{1,0:T(8,128)(2,1)S(1)} %join.12.refs_2_, bf16[64,4096]{1,0:T(8,128)(2,1)S(1)} %collective-permute-done.8.refs_3_, bf16[2048,4096]{1,0:T(8,128)(2,1)S(1)} %copy-done), custom_call_target="tpu_custom_call" | custom-call | flops 1 | bytes 1 | tf_op jit(solution)/shard_map/up/pallas_call | solution.py:192
  31.0 2.9 %down.2 = (f32[64,4096]{1,0:T(8,128)S(1)}, bf16[64,4096]{1,0:T(8,128)(2,1)S(1)}) custom-call(bf16[256,2048]{1,0:T(8,128)(2,1)S(1)} %up.1.h_ref, bf16[2048,4096]{1,0:T(8,128)(2,1)S(1)} %bitcast.5), custom_call_target="tpu_custom_call" | custom-call | flops 1 | bytes 1 | tf_op jit(solution)/shard_map/down/pallas_call | solution.py:223
  34.2 1.8 %collective-permute-done.9.refs_0_ = bf16[64,4096]{1,0:T(8,128)(2,1)S(1)} collective-permute-done((bf16[64,4096]{1,0:T(8,128)(2,1)S(1)}, bf16[64,4096]{1,0:T(8,128)(2,1)S(1)}, u32[]{:S(2)}, u32[]{:S(2)}) %collective-permute-start.9) | collective-permute-done | bytes 524320 | tf_op jit(solution)/shard_map/ppermute | solution.py:340
  36.0 1.6 %collective-permute-start.16 = (bf16[16,4096]{1,0:T(8,128)(2,1)S(1)}, bf16[16,4096]{1,0:T(8,128)(2,1)S(1)}, u32[]{:S(2)}, u32[]{:S(2)}) collective-permute-start(bf16[16,4096]{1,0:T(8,128)(2,1)S(1)} %get-tuple-element.54), channel_id=1, source_target_pairs={{0,2},{1,3},{2,0},{3,1},{4,6},{5,7},{6,4},{7,5},{8,10},{9,11},{10,... | collective-permute-start | bytes 393224 | tf_op jit(solution)/shard_map/ppermute | solution.py:340
  38.1 2.9 %down.3 = (f32[64,4096]{1,0:T(8,128)S(1)}, bf16[16,4096]{1,0:T(8,128)(2,1)S(1)}, bf16[16,4096]{1,0:T(8,128)(2,1)S(1)}, bf16[16,4096]{1,0:T(8,128)(2,1)S(1)}, bf16[16,4096]{1,0:T(8,128)(2,1)S(1)}) custom-call(bf16[256,2048]{1,0:T(8,128)(2,1)S(1)} %up.1.h_ref, bf16[2048,4096]{1,0:T(8,128)(2,1)S(1)} %bitcast.5, bf16[16,4096]{1,0:T(8,128)(2,1)S(1)} %get-tuple-element.44.refs_0_), custom_call_target="tpu_custom_call" | custom-call | flops 1 | bytes 1 | tf_op jit(solution)/shard_map/down/pallas_call | solution.py:223
  42.4 2.0 %collective-permute-done.14.refs_0_ = bf16[16,4096]{1,0:T(8,128)(2,1)S(1)} collective-permute-done((bf16[16,4096]{1,0:T(8,128)(2,1)S(1)}, bf16[16,4096]{1,0:T(8,128)(2,1)S(1)}, u32[]{:S(2)}, u32[]{:S(2)}) %collective-permute-start.14) | collective-permute-done | bytes 131104 | tf_op jit(solution)/shard_map/ppermute | solution.py:340
  44.4 2.5 %collective-permute-start.17 = (bf16[16,4096]{1,0:T(8,128)(2,1)S(1)}, bf16[16,4096]{1,0:T(8,128)(2,1)S(1)}, u32[]{:S(2)}, u32[]{:S(2)}) collective-permute-start(bf16[16,4096]{1,0:T(8,128)(2,1)S(1)} %add.13), channel_id=1, source_target_pairs={{0,12},{1,13},{2,14},{3,15},{4,8},{5,9},{6,10},{7,11},{8,4},{9,5},... | collective-permute-start | bytes 393224 | tf_op jit(solution)/shard_map/ppermute | solution.py:340
  47.1 1.6 %collective-permute-start.19 = (bf16[16,2048]{1,0:T(8,128)(2,1)S(1)}, bf16[16,2048]{1,0:T(8,128)(2,1)S(1)}, u32[]{:S(2)}, u32[]{:S(2)}) collective-permute-start(bf16[16,2048]{1,0:T(8,128)(2,1)S(1)} %get-tuple-element.56), channel_id=1, source_target_pairs={{0,2},{1,3},{2,0},{3,1},{4,6},{5,7},{6,4},{7,5},{8,10},{9,11},{10,... | collective-permute-start | bytes 196616 | tf_op jit(solution)/shard_map/ppermute | solution.py:340
  49.3 1.5 %collective-permute-start.21 = (bf16[16,2048]{1,0:T(8,128)(2,1)S(1)}, bf16[16,2048]{1,0:T(8,128)(2,1)S(1)}, u32[]{:S(2)}, u32[]{:S(2)}) collective-permute-start(bf16[16,2048]{1,0:T(8,128)(2,1)S(1)} %get-tuple-element.58), channel_id=1, source_target_pairs={{0,2},{1,3},{2,0},{3,1},{4,6},{5,7},{6,4},{7,5},{8,10},{9,11},{10,... | collective-permute-start | bytes 196616 | tf_op jit(solution)/shard_map/ppermute | solution.py:340
  50.8 1.3 %collective-permute-done.19.refs_0_ = bf16[16,2048]{1,0:T(8,128)(2,1)S(1)} collective-permute-done((bf16[16,2048]{1,0:T(8,128)(2,1)S(1)}, bf16[16,2048]{1,0:T(8,128)(2,1)S(1)}, u32[]{:S(2)}, u32[]{:S(2)}) %collective-permute-start.19) | collective-permute-done | bytes 65568 | tf_op jit(solution)/shard_map/ppermute | solution.py:340
  52.1 2.0 %collective-permute-start.20 = (bf16[16,2048]{1,0:T(8,128)(2,1)S(1)}, bf16[16,2048]{1,0:T(8,128)(2,1)S(1)}, u32[]{:S(2)}, u32[]{:S(2)}) collective-permute-start(bf16[16,2048]{1,0:T(8,128)(2,1)S(1)} %add.14), channel_id=1, source_target_pairs={{0,4},{1,5},{2,6},{3,7},{4,0},{5,1},{6,2},{7,3},{8,12},{9,13},{10,... | collective-permute-start | bytes 196616 | tf_op jit(solution)/shard_map/ppermute | solution.py:340
  55.1 1.7 %collective-permute-start.22 = (bf16[16,2048]{1,0:T(8,128)(2,1)S(1)}, bf16[16,2048]{1,0:T(8,128)(2,1)S(1)}, u32[]{:S(2)}, u32[]{:S(2)}) collective-permute-start(bf16[16,2048]{1,0:T(8,128)(2,1)S(1)} %add.15), channel_id=1, source_target_pairs={{0,4},{1,5},{2,6},{3,7},{4,0},{5,1},{6,2},{7,3},{8,12},{9,13},{10,... | collective-permute-start | bytes 196616 | tf_op jit(solution)/shard_map/ppermute | solution.py:340
  56.7 1.3 %collective-permute-done.18.refs_0_ = bf16[16,4096]{1,0:T(8,128)(2,1)S(1)} collective-permute-done((bf16[16,4096]{1,0:T(8,128)(2,1)S(1)}, bf16[16,4096]{1,0:T(8,128)(2,1)S(1)}, u32[]{:S(2)}, u32[]{:S(2)}) %collective-permute-start.18) | collective-permute-done | bytes 131104 | tf_op jit(solution)/shard_map/ppermute | solution.py:340
  59.7 1.2 %post.1 = bf16[128,4096]{1,0:T(8,128)(2,1)} custom-call(bf16[128,64]{1,0:T(8,128)(2,1)S(1)} %get-tuple-element.35.mix_ref, f32[3,4096]{1,0:T(4,128)S(1)} %get-tuple-element.36.table_ref, f32[128,4096]{1,0:T(8,128)S(1)} %own_part.1.acc_ref, bf16[16,4096]{1,0:T(8,128)(2,1)S(1)} %join.17.refs_0_, bf16[16,2048]{1,0:T(8,128)(2,1)S(1)} %collective-permute-done.20.refs_1_, ...), custom_call_target="tpu_custom_call" | custom-call | flops 1 | bytes 1 | tf_op jit(solution)/shard_map/post/pallas_call | solution.py:308
  (57 shorter events, 8.7 us)
Async XLA Ops:
  2.5 9.5 %collective-permute-start = (bf16[16,4096]{1,0:T(8,128)(2,1)S(1)}, bf16[16,4096]{1,0:T(8,128)(2,1)S(1)}, u32[]{:S(2)}, u32[]{:S(2)}) collective-permute-start(bf16[16,4096]{1,0:T(8,128)(2,1)S(1)} %get-tuple-element.34), channel_id=1, source_target_pairs={{0,12},{1,13},{2,14},{3,15},{4,8},{5,9},{6,10},{7,11},{8,4},{9,5},... | collective-permute-start | bytes 393224 | tf_op jit(solution)/shard_map/ppermute | solution.py:340
  7.6 23.4 %slice-start.3 = ((s8[16777216]{0:T(1024)(128)(4,1)}), s8[4194304]{0:T(1024)(128)(4,1)S(1)}, s32[]{:S(2)}) async-start(s8[16777216]{0:T(1024)(128)(4,1)} %bitcast.4), calls=%async_computation.3 | async-start | bytes 8388608
  8.4 6.7 %collective-permute-start.6 = (bf16[16,4096]{1,0:T(8,128)(2,1)S(1)}, bf16[16,4096]{1,0:T(8,128)(2,1)S(1)}, u32[]{:S(2)}, u32[]{:S(2)}) collective-permute-start(bf16[16,4096]{1,0:T(8,128)(2,1)S(1)} %get-tuple-element.41), channel_id=1, source_target_pairs={{0,4},{1,5},{2,6},{3,7},{4,0},{5,1},{6,2},{7,3},{8,12},{9,13},{10,... | collective-permute-start | bytes 393224 | tf_op jit(solution)/shard_map/ppermute | solution.py:340
  8.5 10.2 %collective-permute-start.4 = (bf16[16,4096]{1,0:T(8,128)(2,1)S(1)}, bf16[16,4096]{1,0:T(8,128)(2,1)S(1)}, u32[]{:S(2)}, u32[]{:S(2)}) collective-permute-start(bf16[16,4096]{1,0:T(8,128)(2,1)S(1)} %get-tuple-element.40), channel_id=1, source_target_pairs={{0,8},{1,9},{2,10},{3,11},{4,12},{5,13},{6,14},{7,15},{8,0},{9,1},... | collective-permute-start | bytes 393224 | tf_op jit(solution)/shard_map/ppermute | solution.py:340
  9.1 11.2 %collective-permute-start.1 = (bf16[16,4096]{1,0:T(8,128)(2,1)S(1)}, bf16[16,4096]{1,0:T(8,128)(2,1)S(1)}, u32[]{:S(2)}, u32[]{:S(2)}) collective-permute-start(bf16[16,4096]{1,0:T(8,128)(2,1)S(1)} %get-tuple-element.39.refs_0_), channel_id=1, source_target_pairs={{0,2},{1,3},{2,0},{3,1},{4,6},{5,7},{6,4},{7,5},{8,10},{9,11},{10,... | collective-permute-start | bytes 393224 | tf_op jit(solution)/shard_map/ppermute | solution.py:340
  12.0 8.3 %collective-permute-start.2 = (bf16[16,4096]{1,0:T(8,128)(2,1)S(1)}, bf16[16,4096]{1,0:T(8,128)(2,1)S(1)}, u32[]{:S(2)}, u32[]{:S(2)}) collective-permute-start(bf16[16,4096]{1,0:T(8,128)(2,1)S(1)} %collective-permute-done.after_ref.refs_2_), channel_id=1, source_target_pairs={{0,2},{1,3},{2,0},{3,1},{4,6},{5,7},{6,4},{7,5},{8,10},{9,11},{10,... | collective-permute-start | bytes 393224 | tf_op jit(solution)/shard_map/ppermute | solution.py:340
  15.1 5.3 %collective-permute-start.7 = (bf16[16,4096]{1,0:T(8,128)(2,1)S(1)}, bf16[16,4096]{1,0:T(8,128)(2,1)S(1)}, u32[]{:S(2)}, u32[]{:S(2)}) collective-permute-start(bf16[16,4096]{1,0:T(8,128)(2,1)S(1)} %collective-permute-done.6.refs_2_), channel_id=1, source_target_pairs={{0,2},{1,3},{2,0},{3,1},{4,6},{5,7},{6,4},{7,5},{8,10},{9,11},{10,... | collective-permute-start | bytes 393224 | tf_op jit(solution)/shard_map/ppermute | solution.py:340
  18.7 5.0 %collective-permute-start.5 = (bf16[16,4096]{1,0:T(8,128)(2,1)S(1)}, bf16[16,4096]{1,0:T(8,128)(2,1)S(1)}, u32[]{:S(2)}, u32[]{:S(2)}) collective-permute-start(bf16[16,4096]{1,0:T(8,128)(2,1)S(1)} %join.10.refs_0_), channel_id=1, source_target_pairs={{0,2},{1,3},{2,0},{3,1},{4,6},{5,7},{6,4},{7,5},{8,10},{9,11},{10,... | collective-permute-start | bytes 393224 | tf_op jit(solution)/shard_map/ppermute | solution.py:340
  20.3 3.5 %collective-permute-start.3 = (bf16[64,4096]{1,0:T(8,128)(2,1)S(1)}, bf16[64,4096]{1,0:T(8,128)(2,1)S(1)}, u32[]{:S(2)}, u32[]{:S(2)}) collective-permute-start(bf16[64,4096]{1,0:T(8,128)(2,1)S(1)} %join.9.refs_0_), channel_id=1, source_target_pairs={{0,1},{1,0},{2,3},{3,2},{4,5},{5,4},{6,7},{7,6},{8,9},{9,8},{10,11... | collective-permute-start | bytes 1572872 | tf_op jit(solution)/shard_map/ppermute | solution.py:340
  23.7 2.0 %collective-permute-start.8 = (bf16[64,4096]{1,0:T(8,128)(2,1)S(1)}, bf16[64,4096]{1,0:T(8,128)(2,1)S(1)}, u32[]{:S(2)}, u32[]{:S(2)}) collective-permute-start(bf16[64,4096]{1,0:T(8,128)(2,1)S(1)} %join.12.refs_2_), channel_id=1, source_target_pairs={{0,1},{1,0},{2,3},{3,2},{4,5},{5,4},{6,7},{7,6},{8,9},{9,8},{10,11... | collective-permute-start | bytes 1572872 | tf_op jit(solution)/shard_map/ppermute | solution.py:340
  33.9 2.0 %collective-permute-start.9 = (bf16[64,4096]{1,0:T(8,128)(2,1)S(1)}, bf16[64,4096]{1,0:T(8,128)(2,1)S(1)}, u32[]{:S(2)}, u32[]{:S(2)}) collective-permute-start(bf16[64,4096]{1,0:T(8,128)(2,1)S(1)} %get-tuple-element.43), channel_id=1, source_target_pairs={{0,1},{1,0},{2,3},{3,2},{4,5},{5,4},{6,7},{7,6},{8,9},{9,8},{10,11... | collective-permute-start | bytes 1572872 | tf_op jit(solution)/shard_map/ppermute | solution.py:340
  36.0 6.4 %collective-permute-start.16 = (bf16[16,4096]{1,0:T(8,128)(2,1)S(1)}, bf16[16,4096]{1,0:T(8,128)(2,1)S(1)}, u32[]{:S(2)}, u32[]{:S(2)}) collective-permute-start(bf16[16,4096]{1,0:T(8,128)(2,1)S(1)} %get-tuple-element.54), channel_id=1, source_target_pairs={{0,2},{1,3},{2,0},{3,1},{4,6},{5,7},{6,4},{7,5},{8,10},{9,11},{10,... | collective-permute-start | bytes 393224 | tf_op jit(solution)/shard_map/ppermute | solution.py:340
  37.6 6.8 %collective-permute-start.14 = (bf16[16,4096]{1,0:T(8,128)(2,1)S(1)}, bf16[16,4096]{1,0:T(8,128)(2,1)S(1)}, u32[]{:S(2)}, u32[]{:S(2)}) collective-permute-start(bf16[16,4096]{1,0:T(8,128)(2,1)S(1)} %get-tuple-element.44.refs_0_), channel_id=1, source_target_pairs={{0,2},{1,3},{2,0},{3,1},{4,6},{5,7},{6,4},{7,5},{8,10},{9,11},{10,... | collective-permute-start | bytes 393224 | tf_op jit(solution)/shard_map/ppermute | solution.py:340
  41.0 5.9 %collective-permute-start.10 = (bf16[16,4096]{1,0:T(8,128)(2,1)S(1)}, bf16[16,4096]{1,0:T(8,128)(2,1)S(1)}, u32[]{:S(2)}, u32[]{:S(2)}) collective-permute-start(bf16[16,4096]{1,0:T(8,128)(2,1)S(1)} %get-tuple-element.46), channel_id=1, source_target_pairs={{0,1},{1,0},{2,3},{3,2},{4,5},{5,4},{6,7},{7,6},{8,9},{9,8},{10,11... | collective-permute-start | bytes 393224 | tf_op jit(solution)/shard_map/ppermute | solution.py:340
  41.1 5.9 %collective-permute-start.11 = (bf16[16,4096]{1,0:T(8,128)(2,1)S(1)}, bf16[16,4096]{1,0:T(8,128)(2,1)S(1)}, u32[]{:S(2)}, u32[]{:S(2)}) collective-permute-start(bf16[16,4096]{1,0:T(8,128)(2,1)S(1)} %get-tuple-element.47), channel_id=1, source_target_pairs={{0,1},{1,0},{2,3},{3,2},{4,5},{5,4},{6,7},{7,6},{8,9},{9,8},{10,11... | collective-permute-start | bytes 393224 | tf_op jit(solution)/shard_map/ppermute | solution.py:340
  41.6 5.4 %collective-permute-start.12 = (bf16[16,4096]{1,0:T(8,128)(2,1)S(1)}, bf16[16,4096]{1,0:T(8,128)(2,1)S(1)}, u32[]{:S(2)}, u32[]{:S(2)}) collective-permute-start(bf16[16,4096]{1,0:T(8,128)(2,1)S(1)} %get-tuple-element.48), channel_id=1, source_target_pairs={{0,1},{1,0},{2,3},{3,2},{4,5},{5,4},{6,7},{7,6},{8,9},{9,8},{10,11... | collective-permute-start | bytes 393224 | tf_op jit(solution)/shard_map/ppermute | solution.py:340
  42.4 4.6 %collective-permute-start.13 = (bf16[16,4096]{1,0:T(8,128)(2,1)S(1)}, bf16[16,4096]{1,0:T(8,128)(2,1)S(1)}, u32[]{:S(2)}, u32[]{:S(2)}) collective-permute-start(bf16[16,4096]{1,0:T(8,128)(2,1)S(1)} %get-tuple-element.49), channel_id=1, source_target_pairs={{0,1},{1,0},{2,3},{3,2},{4,5},{5,4},{6,7},{7,6},{8,9},{9,8},{10,11... | collective-permute-start | bytes 393224 | tf_op jit(solution)/shard_map/ppermute | solution.py:340
  44.4 12.3 %collective-permute-start.17 = (bf16[16,4096]{1,0:T(8,128)(2,1)S(1)}, bf16[16,4096]{1,0:T(8,128)(2,1)S(1)}, u32[]{:S(2)}, u32[]{:S(2)}) collective-permute-start(bf16[16,4096]{1,0:T(8,128)(2,1)S(1)} %add.13), channel_id=1, source_target_pairs={{0,12},{1,13},{2,14},{3,15},{4,8},{5,9},{6,10},{7,11},{8,4},{9,5},... | collective-permute-start | bytes 393224 | tf_op jit(solution)/shard_map/ppermute | solution.py:340
  46.9 11.1 %collective-permute-start.18 = (bf16[16,4096]{1,0:T(8,128)(2,1)S(1)}, bf16[16,4096]{1,0:T(8,128)(2,1)S(1)}, u32[]{:S(2)}, u32[]{:S(2)}) collective-permute-start(bf16[16,4096]{1,0:T(8,128)(2,1)S(1)} %add.12.refs_1_), channel_id=1, source_target_pairs={{0,8},{1,9},{2,10},{3,11},{4,12},{5,13},{6,14},{7,15},{8,0},{9,1},... | collective-permute-start | bytes 393224 | tf_op jit(solution)/shard_map/ppermute | solution.py:340
  47.1 5.0 %collective-permute-start.19 = (bf16[16,2048]{1,0:T(8,128)(2,1)S(1)}, bf16[16,2048]{1,0:T(8,128)(2,1)S(1)}, u32[]{:S(2)}, u32[]{:S(2)}) collective-permute-start(bf16[16,2048]{1,0:T(8,128)(2,1)S(1)} %get-tuple-element.56), channel_id=1, source_target_pairs={{0,2},{1,3},{2,0},{3,1},{4,6},{5,7},{6,4},{7,5},{8,10},{9,11},{10,... | collective-permute-start | bytes 196616 | tf_op jit(solution)/shard_map/ppermute | solution.py:340
  48.7 9.4 %collective-permute-start.15 = (bf16[16,4096]{1,0:T(8,128)(2,1)S(1)}, bf16[16,4096]{1,0:T(8,128)(2,1)S(1)}, u32[]{:S(2)}, u32[]{:S(2)}) collective-permute-start(bf16[16,4096]{1,0:T(8,128)(2,1)S(1)} %join.13), channel_id=1, source_target_pairs={{0,2},{1,3},{2,0},{3,1},{4,6},{5,7},{6,4},{7,5},{8,10},{9,11},{10,... | collective-permute-start | bytes 393224 | tf_op jit(solution)/shard_map/ppermute | solution.py:340
  49.3 5.7 %collective-permute-start.21 = (bf16[16,2048]{1,0:T(8,128)(2,1)S(1)}, bf16[16,2048]{1,0:T(8,128)(2,1)S(1)}, u32[]{:S(2)}, u32[]{:S(2)}) collective-permute-start(bf16[16,2048]{1,0:T(8,128)(2,1)S(1)} %get-tuple-element.58), channel_id=1, source_target_pairs={{0,2},{1,3},{2,0},{3,1},{4,6},{5,7},{6,4},{7,5},{8,10},{9,11},{10,... | collective-permute-start | bytes 196616 | tf_op jit(solution)/shard_map/ppermute | solution.py:340
  52.1 6.6 %collective-permute-start.20 = (bf16[16,2048]{1,0:T(8,128)(2,1)S(1)}, bf16[16,2048]{1,0:T(8,128)(2,1)S(1)}, u32[]{:S(2)}, u32[]{:S(2)}) collective-permute-start(bf16[16,2048]{1,0:T(8,128)(2,1)S(1)} %add.14), channel_id=1, source_target_pairs={{0,4},{1,5},{2,6},{3,7},{4,0},{5,1},{6,2},{7,3},{8,12},{9,13},{10,... | collective-permute-start | bytes 196616 | tf_op jit(solution)/shard_map/ppermute | solution.py:340
  55.1 4.7 %collective-permute-start.22 = (bf16[16,2048]{1,0:T(8,128)(2,1)S(1)}, bf16[16,2048]{1,0:T(8,128)(2,1)S(1)}, u32[]{:S(2)}, u32[]{:S(2)}) collective-permute-start(bf16[16,2048]{1,0:T(8,128)(2,1)S(1)} %add.15), channel_id=1, source_target_pairs={{0,4},{1,5},{2,6},{3,7},{4,0},{5,1},{6,2},{7,3},{8,12},{9,13},{10,... | collective-permute-start | bytes 196616 | tf_op jit(solution)/shard_map/ppermute | solution.py:340
  (4 other events, 88.4 us)

commit v17 on v13

--- a/solution.py
+++ b/solution.py
@@ -175,7 +175,7 @@
         rows_ref[to:to + high - low, :] = refs[source][low:high, :]
         to += high - low
     hidden = w_ref.shape[0]
-    tile = min(512, hidden)
+    tile = min(1024, hidden)
 
     @pl.loop(0, hidden // tile)
     def _(i):
@@ -201,30 +201,35 @@
     )(*parts, w, *after)
 
 
-def down_kernel(h_ref, w_ref, keep_ref, send_ref, *, columns):
-    half = keep_ref.shape[0]
+def down_kernel(h_ref, w_ref, *outs, columns, low):
     first, last, tile = columns
+    groups = len(outs) // 2
+    half = outs[0].shape[0]
 
     @pl.loop(0, (last - first) // tile)
     def _(i):
-        cut = pl.ds(pl.multiple_of(i * tile, tile), tile)
-        from_ = pl.ds(pl.multiple_of(first + i * tile, tile), tile)
-        out = jnp.dot(h_ref[...], w_ref[:, from_], preferred_element_type=F32)
-        keep_ref[:, cut] = out[:half]
-        send_ref[:, cut] = out[half:].astype(BF16)
-
-
-def down(hid, w, columns):
-    half = hid.shape[0] // 2
+        to = pl.ds(pl.multiple_of(i * tile, tile), tile)
+        cut = pl.ds(pl.multiple_of(first + i * tile, tile), tile)
+        rows = slice(low, low + 2 * half * groups)
+        out = jnp.dot(h_ref[rows, :], w_ref[:, cut], preferred_element_type=F32)
+        for g in range(groups):
+            at = 2 * half * g
+            outs[2 * g][:, to] = out[at:at + half]
+            outs[2 * g + 1][:, to] = out[at + half:at + 2 * half].astype(BF16)
+
+
+def down(hid, low, groups, w, columns):
+    half = hid.shape[0] // 4
     step = columns[1] - columns[0]
     return pl.pallas_call(
-        functools.partial(down_kernel, columns=columns),
+        functools.partial(down_kernel, columns=columns, low=low),
         in_specs=[VMEM] * 2,
-        out_specs=[VMEM] * 2,
+        out_specs=[VMEM] * (2 * groups),
         out_shape=[
             jax.ShapeDtypeStruct((half, step), F32),
             jax.ShapeDtypeStruct((half, step), BF16),
-        ],
+        ]
+        * groups,
         compiler_params=params(8),
         cost_estimate=FREE,
         name="down",
@@ -345,54 +350,61 @@
     beside[-1] = join([beside[-1]], [])
     early, late = list(range(experts // 2)), list(range(experts // 2, experts))
     parts = []
-    sources = []
+    segments = {}
     for members in (early, late):
         pieces = [join([x for i in members for x in (blocks[i], beside[i])], [])]
         height = pieces[0].shape[0]
         for mask in near[1:]:
             block = pieces[0] if len(pieces) == 1 else join(pieces, [])
             pieces = [block, swap(block, mask)]
-        cuts = []
-        for piece in pieces:
-            cuts += [(len(parts), at, at + height) for at in range(0, piece.shape[0], height)]
-            parts.append(piece)
-        sources.append(cuts)
-    sources = [cut for pair in zip(*sources) for cut in pair]
-
+        for at, i in enumerate(members):
+            segments[i] = []
+            for k, piece in enumerate(pieces):
+                for base in range(2 * at * slots, piece.shape[0], height):
+                    segments[i].append((len(parts) + k, base, base + 2 * slots))
+        parts += pieces
+    groups = [[1, 2], list(range(3, experts)) + [0]]
+    sources = [
+        cut for members in groups for cuts in zip(*[segments[i] for i in members]) for cut in cuts
+    ]
     hid = up(parts, sources, w_up, [])
 
-    step = 5 * width // 8
-    keep_a, send_a = down(hid, w_down, (0, step, step // 2))
-    keep_b, send_b = down(hid, w_down, (step, width, width - step))
-    pairs = []
-    for keep, send in ((keep_a, send_a), (keep_b, send_b)):
+    def gather(keep, send):
         for i, mask in enumerate(reversed(near[1:])):
             if i:
                 middle = keep.shape[0] // 2
                 keep, send = add(
                     [(keep, got)], [[(0, 0, middle)], [(0, middle, 2 * middle)]], [F32, BF16]
                 )
-            if pairs:
-                send = join([send], [pairs[0][1]])
             got = swap(send, mask)
-        pairs.append((keep, got))
-
-    def outs(side):
-        rows = [(2 * i + side) * slots for i in range(experts)]
-        return [[(piece, at, at + slots) for piece in range(len(pairs))] for at in rows]
-
-    sums = add(pairs, outs(1) + outs(0), [BF16] * experts + [F32] * experts)
-    sends, keeps = sums[:experts], sums[experts:]
-    back = {}
-    for i in range(1, experts):
-        got = swap(sends[i], near[0])
-        (part,) = add([(keeps[i], got)], [[(0, 0, slots)]], [BF16])
-        back[i] = swap(part, far[i - 1])
-        if i == 1:
-            own_send = join(sends[:1], [part])
-    got = swap(own_send, near[0])
-    acc = own_part(mixes[0], keeps[0], got, back[1])
-    return post(mixes[1], table, acc, [back[i] for i in range(2, experts)])
+        return keep, got
+
+    half = hid.shape[0] // 2
+    step = 5 * width // 8
+    keep, send, *others = down(hid, 0, 2, w_down, (0, step, step // 2))
+    heads = [gather(keep, send), gather(*others)]
+    tails = []
+    for g in range(2):
+        keep, send = down(hid, g * half, 1, w_down, (step, width, width - step))
+        tails.append(gather(keep, send))
+    block = {}
+    for members, head, tail in zip(groups, heads, tails):
+        outs = []
+        for at in range(len(members)):
+            for side in (1, 0):
+                low = (2 * at + side) * slots
+                outs.append([(piece, low, low + slots) for piece in range(2)])
+        sums = add([head, tail], outs, [BF16, F32] * len(members))
+        block.update((i, sums[2 * at:2 * at + 2]) for at, i in enumerate(members))
+
+    def total(send, keep):
+        return add([(keep, swap(send, near[0]))], [[(0, 0, slots)]], [BF16])[0]
+
+    sums = [total(*block[i]) for i in range(1, experts)]
+    back = [swap(part, mask) for part, mask in zip(sums, far)]
+    send, keep = block[0]
+    acc = own_part(mixes[0], keep, swap(join([send], [sums[0]]), near[0]), back[0])
+    return post(mixes[1], table, acc, back[1:])
 
 
 def solution(mesh):

time: 59.8 us -> 58.6 us (0.980)
  waiting for transfers between devices: 21.6 us -> 19.5 us
  starting transfers between devices: 21.8 us -> 23 us
    ppermute x18 -> x20, waiting for transfers between devices: 21.6 us -> 19.5 us  [swap(): return lax.ppermute(x, 'expert', [(i, i ^ mask) for i in range(devices)])]
    ppermute x18 -> x20, starting transfers between devices: 21.8 us -> 23 us  [swap(): return lax.ppermute(x, 'expert', [(i, i ^ mask) for i in range(devices)])]
    pallas_call x2 -> x3, Pallas kernels: 4.92 us -> 5.11 us  [down(): pl.pallas_call(functools.partial(down_kernel, columns=columns, low=low),...]
  transfers between devices with their start and end apart: 18 -> 20, of which waited for: 13 -> 10; matrix products, arithmetic and copies ran while one was open for 0% -> 0% of each run, Pallas kernels for 6% -> 6%
where the time goes in v17:
time: 58.6 us; the launch traced here: 58.4 us
  starting transfers between devices  23 us (39%)
  waiting for transfers between devices  19.5 us (33%)
  Pallas kernels  15.7 us (27%)
    ppermute x20, starting transfers between devices, swap(): return lax.ppermute(x, 'expert', [(i, i ^ mask) for i in range(devices)])  23 us
    ppermute x20, waiting for transfers between devices, swap(): return lax.ppermute(x, 'expert', [(i, i ^ mask) for i in range(devices)])  19.5 us
    pallas_call x1, Pallas kernels, up(): pl.pallas_call(functools.partial(up_kernel, sources=sources, count=len(pa...  5.27 us
    pallas_call x3, Pallas kernels, down(): pl.pallas_call(functools.partial(down_kernel, columns=columns, low=low),...  5.11 us
    pallas_call x1, Pallas kernels, first(): pl.pallas_call(first_kernel, in_specs=[SMEM] + [HBM] * 7, out_specs=[VMEM...  2.39 us
    pallas_call x1, Pallas kernels, post(): pl.pallas_call(post_kernel, in_specs=[VMEM] * (3 + len(blocks)), out_spec...  1.21 us
  transfers between devices with their start and end apart: 20, of which 10 were waited for; matrix products, arithmetic and copies ran while one was open for 0% of the time, Pallas kernels for 6%

profile of v17, /device:TPU:0, one launch (start us, length us, event | category | flops | bytes accessed | tf_op | source)
XLA Modules:
  0.0 58.4 jit_solution(10508206724802073586)
XLA Ops:
  0.1 2.4 %first.1 = (bf16[16,4096]{1,0:T(8,128)(2,1)S(1)}, bf16[128,4096]{1,0:T(8,128)(2,1)S(1)}, f32[3,4096]{1,0:T(4,128)S(1)}, s32[4,16]{1,0:T(4,128)S(1)}, f32[4,16]{1,0:T(4,128)S(1)}) custom-call(s32[2]{0:T(128)S(1)} %pad_add_fusion.info_ref, bf16[128,4096]{1,0:T(8,128)(2,1)} %refs_0_.1, s32[4,16]{1,0:T(4,128)} %bitcast.6, f32[2,4096]{1,0:T(2,128)} %refs_2_.1, ...), custom_call_target="tpu_custom_call" | custom-call | flops 1 | bytes 1 | tf_op jit(solution)/shard_map/first/pallas_call | solution.py:78
  2.5 5.1 %collective-permute-start = (bf16[16,4096]{1,0:T(8,128)(2,1)S(1)}, bf16[16,4096]{1,0:T(8,128)(2,1)S(1)}, u32[]{:S(2)}, u32[]{:S(2)}) collective-permute-start(bf16[16,4096]{1,0:T(8,128)(2,1)S(1)} %get-tuple-element.33), channel_id=1, source_target_pairs={{0,12},{1,13},{2,14},{3,15},{4,8},{5,9},{6,10},{7,11},{8,4},{9,5},... | collective-permute-start | bytes 393224 | tf_op jit(solution)/shard_map/ppermute | solution.py:336
  9.1 1.7 %collective-permute-start.1 = (bf16[16,4096]{1,0:T(8,128)(2,1)S(1)}, bf16[16,4096]{1,0:T(8,128)(2,1)S(1)}, u32[]{:S(2)}, u32[]{:S(2)}) collective-permute-start(bf16[16,4096]{1,0:T(8,128)(2,1)S(1)} %get-tuple-element.38.refs_0_), channel_id=1, source_target_pairs={{0,2},{1,3},{2,0},{3,1},{4,6},{5,7},{6,4},{7,5},{8,10},{9,11},{10,... | collective-permute-start | bytes 393224 | tf_op jit(solution)/shard_map/ppermute | solution.py:336
  10.8 1.2 %collective-permute-done.after_ref.refs_2_ = bf16[16,4096]{1,0:T(8,128)(2,1)S(1)} collective-permute-done((bf16[16,4096]{1,0:T(8,128)(2,1)S(1)}, bf16[16,4096]{1,0:T(8,128)(2,1)S(1)}, u32[]{:S(2)}, u32[]{:S(2)}) %collective-permute-start) | collective-permute-done | bytes 131104 | tf_op jit(solution)/shard_map/ppermute | solution.py:336
  12.0 1.8 %collective-permute-start.2 = (bf16[16,4096]{1,0:T(8,128)(2,1)S(1)}, bf16[16,4096]{1,0:T(8,128)(2,1)S(1)}, u32[]{:S(2)}, u32[]{:S(2)}) collective-permute-start(bf16[16,4096]{1,0:T(8,128)(2,1)S(1)} %collective-permute-done.after_ref.refs_2_), channel_id=1, source_target_pairs={{0,2},{1,3},{2,0},{3,1},{4,6},{5,7},{6,4},{7,5},{8,10},{9,11},{10,... | collective-permute-start | bytes 393224 | tf_op jit(solution)/shard_map/ppermute | solution.py:336
  13.9 1.2 %collective-permute-done.6.refs_2_ = bf16[16,4096]{1,0:T(8,128)(2,1)S(1)} collective-permute-done((bf16[16,4096]{1,0:T(8,128)(2,1)S(1)}, bf16[16,4096]{1,0:T(8,128)(2,1)S(1)}, u32[]{:S(2)}, u32[]{:S(2)}) %collective-permute-start.6) | collective-permute-done | bytes 131104 | tf_op jit(solution)/shard_map/ppermute | solution.py:336
  15.1 1.6 %collective-permute-start.7 = (bf16[16,4096]{1,0:T(8,128)(2,1)S(1)}, bf16[16,4096]{1,0:T(8,128)(2,1)S(1)}, u32[]{:S(2)}, u32[]{:S(2)}) collective-permute-start(bf16[16,4096]{1,0:T(8,128)(2,1)S(1)} %collective-permute-done.6.refs_2_), channel_id=1, source_target_pairs={{0,2},{1,3},{2,0},{3,1},{4,6},{5,7},{6,4},{7,5},{8,10},{9,11},{10,... | collective-permute-start | bytes 393224 | tf_op jit(solution)/shard_map/ppermute | solution.py:336
  16.7 2.0 %collective-permute-done.4.refs_0_ = bf16[16,4096]{1,0:T(8,128)(2,1)S(1)} collective-permute-done((bf16[16,4096]{1,0:T(8,128)(2,1)S(1)}, bf16[16,4096]{1,0:T(8,128)(2,1)S(1)}, u32[]{:S(2)}, u32[]{:S(2)}) %collective-permute-start.4) | collective-permute-done | bytes 131104 | tf_op jit(solution)/shard_map/ppermute | solution.py:336
  18.7 1.6 %collective-permute-start.5 = (bf16[16,4096]{1,0:T(8,128)(2,1)S(1)}, bf16[16,4096]{1,0:T(8,128)(2,1)S(1)}, u32[]{:S(2)}, u32[]{:S(2)}) collective-permute-start(bf16[16,4096]{1,0:T(8,128)(2,1)S(1)} %join.6.refs_0_), channel_id=1, source_target_pairs={{0,2},{1,3},{2,0},{3,1},{4,6},{5,7},{6,4},{7,5},{8,10},{9,11},{10,... | collective-permute-start | bytes 393224 | tf_op jit(solution)/shard_map/ppermute | solution.py:336
  20.4 3.3 %collective-permute-done.5.refs_1_ = bf16[16,4096]{1,0:T(8,128)(2,1)S(1)} collective-permute-done((bf16[16,4096]{1,0:T(8,128)(2,1)S(1)}, bf16[16,4096]{1,0:T(8,128)(2,1)S(1)}, u32[]{:S(2)}, u32[]{:S(2)}) %collective-permute-start.5) | collective-permute-done | bytes 131104 | tf_op jit(solution)/shard_map/ppermute | solution.py:336
  23.8 1.9 %collective-permute-done.8.refs_3_ = bf16[64,4096]{1,0:T(8,128)(2,1)S(1)} collective-permute-done((bf16[64,4096]{1,0:T(8,128)(2,1)S(1)}, bf16[64,4096]{1,0:T(8,128)(2,1)S(1)}, u32[]{:S(2)}, u32[]{:S(2)}) %collective-permute-start.8) | collective-permute-done | bytes 524320 | tf_op jit(solution)/shard_map/ppermute | solution.py:336
  25.7 5.3 %up.1.h_ref = bf16[256,2048]{1,0:T(8,128)(2,1)S(1)} custom-call(bf16[64,4096]{1,0:T(8,128)(2,1)S(1)} %join.5.refs_0_, bf16[64,4096]{1,0:T(8,128)(2,1)S(1)} %collective-permute-done.3.refs_1_, bf16[64,4096]{1,0:T(8,128)(2,1)S(1)} %join.8.refs_2_, bf16[64,4096]{1,0:T(8,128)(2,1)S(1)} %collective-permute-done.8.refs_3_, bf16[2048,4096]{1,0:T(8,128)(2,1)S(1)} %copy-done), custom_call_target="tpu_custom_call" | custom-call | flops 1 | bytes 1 | tf_op jit(solution)/shard_map/up/pallas_call | solution.py:192
  31.0 3.1 %down.3 = (f32[64,2560]{1,0:T(8,128)S(1)}, bf16[64,2560]{1,0:T(8,128)(2,1)S(1)}, f32[64,2560]{1,0:T(8,128)S(1)}, bf16[64,2560]{1,0:T(8,128)(2,1)S(1)}) custom-call(bf16[256,2048]{1,0:T(8,128)(2,1)S(1)} %up.1.h_ref, bf16[2048,4096]{1,0:T(8,128)(2,1)S(1)} %bitcast.5), custom_call_target="tpu_custom_call" | custom-call | flops 1 | bytes 1 | tf_op jit(solution)/shard_map/down/pallas_call | solution.py:224
  34.8 1.0 %down.5 = (f32[64,1536]{1,0:T(8,128)S(1)}, bf16[64,1536]{1,0:T(8,128)(2,1)S(1)}) custom-call(bf16[256,2048]{1,0:T(8,128)(2,1)S(1)} %up.1.h_ref, bf16[2048,4096]{1,0:T(8,128)(2,1)S(1)} %bitcast.5), custom_call_target="tpu_custom_call" | custom-call | flops 1 | bytes 1 | tf_op jit(solution)/shard_map/down/pallas_call | solution.py:224
  37.5 1.6 %collective-permute-start.13 = (bf16[16,4096]{1,0:T(8,128)(2,1)S(1)}, bf16[16,4096]{1,0:T(8,128)(2,1)S(1)}, u32[]{:S(2)}, u32[]{:S(2)}) collective-permute-start(bf16[16,4096]{1,0:T(8,128)(2,1)S(1)} %get-tuple-element.52), channel_id=1, source_target_pairs={{0,2},{1,3},{2,0},{3,1},{4,6},{5,7},{6,4},{7,5},{8,10},{9,11},{10,... | collective-permute-start | bytes 393224 | tf_op jit(solution)/shard_map/ppermute | solution.py:336
  40.2 1.1 %collective-permute-start.16 = (bf16[16,4096]{1,0:T(8,128)(2,1)S(1)}, bf16[16,4096]{1,0:T(8,128)(2,1)S(1)}, u32[]{:S(2)}, u32[]{:S(2)}) collective-permute-start(bf16[16,4096]{1,0:T(8,128)(2,1)S(1)} %get-tuple-element.54), channel_id=1, source_target_pairs={{0,2},{1,3},{2,0},{3,1},{4,6},{5,7},{6,4},{7,5},{8,10},{9,11},{10,... | collective-permute-start | bytes 393224 | tf_op jit(solution)/shard_map/ppermute | solution.py:336
  41.3 2.6 %collective-permute-done.13.refs_1_ = bf16[16,4096]{1,0:T(8,128)(2,1)S(1)} collective-permute-done((bf16[16,4096]{1,0:T(8,128)(2,1)S(1)}, bf16[16,4096]{1,0:T(8,128)(2,1)S(1)}, u32[]{:S(2)}, u32[]{:S(2)}) %collective-permute-start.13) | collective-permute-done | bytes 131104 | tf_op jit(solution)/shard_map/ppermute | solution.py:336
  43.9 2.5 %collective-permute-start.15 = (bf16[16,4096]{1,0:T(8,128)(2,1)S(1)}, bf16[16,4096]{1,0:T(8,128)(2,1)S(1)}, u32[]{:S(2)}, u32[]{:S(2)}) collective-permute-start(bf16[16,4096]{1,0:T(8,128)(2,1)S(1)} %add.11.refs_1_), channel_id=1, source_target_pairs={{0,12},{1,13},{2,14},{3,15},{4,8},{5,9},{6,10},{7,11},{8,4},{9,5},... | collective-permute-start | bytes 393224 | tf_op jit(solution)/shard_map/ppermute | solution.py:336
  46.5 1.6 %collective-permute-start.14 = (bf16[16,4096]{1,0:T(8,128)(2,1)S(1)}, bf16[16,4096]{1,0:T(8,128)(2,1)S(1)}, u32[]{:S(2)}, u32[]{:S(2)}) collective-permute-start(bf16[16,4096]{1,0:T(8,128)(2,1)S(1)} %join.9), channel_id=1, source_target_pairs={{0,2},{1,3},{2,0},{3,1},{4,6},{5,7},{6,4},{7,5},{8,10},{9,11},{10,... | collective-permute-start | bytes 393224 | tf_op jit(solution)/shard_map/ppermute | solution.py:336
  48.2 1.3 %collective-permute-done.16.refs_1_ = bf16[16,4096]{1,0:T(8,128)(2,1)S(1)} collective-permute-done((bf16[16,4096]{1,0:T(8,128)(2,1)S(1)}, bf16[16,4096]{1,0:T(8,128)(2,1)S(1)}, u32[]{:S(2)}, u32[]{:S(2)}) %collective-permute-start.16) | collective-permute-done | bytes 131104 | tf_op jit(solution)/shard_map/ppermute | solution.py:336
  49.5 1.3 %collective-permute-start.17 = (bf16[16,4096]{1,0:T(8,128)(2,1)S(1)}, bf16[16,4096]{1,0:T(8,128)(2,1)S(1)}, u32[]{:S(2)}, u32[]{:S(2)}) collective-permute-start(bf16[16,4096]{1,0:T(8,128)(2,1)S(1)} %add.12), channel_id=1, source_target_pairs={{0,8},{1,9},{2,10},{3,11},{4,12},{5,13},{6,14},{7,15},{8,0},{9,1},... | collective-permute-start | bytes 393224 | tf_op jit(solution)/shard_map/ppermute | solution.py:336
  51.9 2.4 %collective-permute-done.19.refs_1_ = bf16[16,4096]{1,0:T(8,128)(2,1)S(1)} collective-permute-done((bf16[16,4096]{1,0:T(8,128)(2,1)S(1)}, bf16[16,4096]{1,0:T(8,128)(2,1)S(1)}, u32[]{:S(2)}, u32[]{:S(2)}) %collective-permute-start.19) | collective-permute-done | bytes 131104 | tf_op jit(solution)/shard_map/ppermute | solution.py:336
  54.4 2.9 %collective-permute-done.17.refs_0_ = bf16[16,4096]{1,0:T(8,128)(2,1)S(1)} collective-permute-done((bf16[16,4096]{1,0:T(8,128)(2,1)S(1)}, bf16[16,4096]{1,0:T(8,128)(2,1)S(1)}, u32[]{:S(2)}, u32[]{:S(2)}) %collective-permute-start.17) | collective-permute-done | bytes 131104 | tf_op jit(solution)/shard_map/ppermute | solution.py:336
  57.2 1.2 %post.1 = bf16[128,4096]{1,0:T(8,128)(2,1)} custom-call(bf16[128,64]{1,0:T(8,128)(2,1)S(1)} %get-tuple-element.34.mix_ref, f32[3,4096]{1,0:T(4,128)S(1)} %get-tuple-element.35.table_ref, f32[128,4096]{1,0:T(8,128)S(1)} %own_part.1.acc_ref, bf16[16,4096]{1,0:T(8,128)(2,1)S(1)} %collective-permute-done.17.refs_0_, ...), custom_call_target="tpu_custom_call" | custom-call | flops 1 | bytes 1 | tf_op jit(solution)/shard_map/post/pallas_call | solution.py:304
  (47 shorter events, 6.6 us)
Async XLA Ops:
  2.5 9.5 %collective-permute-start = (bf16[16,4096]{1,0:T(8,128)(2,1)S(1)}, bf16[16,4096]{1,0:T(8,128)(2,1)S(1)}, u32[]{:S(2)}, u32[]{:S(2)}) collective-permute-start(bf16[16,4096]{1,0:T(8,128)(2,1)S(1)} %get-tuple-element.33), channel_id=1, source_target_pairs={{0,12},{1,13},{2,14},{3,15},{4,8},{5,9},{6,10},{7,11},{8,4},{9,5},... | collective-permute-start | bytes 393224 | tf_op jit(solution)/shard_map/ppermute | solution.py:336
  7.6 23.4 %slice-start = ((s8[16777216]{0:T(1024)(128)(4,1)}), s8[4194304]{0:T(1024)(128)(4,1)S(1)}, s32[]{:S(2)}) async-start(s8[16777216]{0:T(1024)(128)(4,1)} %bitcast.4), calls=%async_computation | async-start | bytes 8388608
  7.6 23.4 %slice-start.1 = ((s8[16777216]{0:T(1024)(128)(4,1)}), s8[4194304]{0:T(1024)(128)(4,1)S(1)}, s32[]{:S(2)}) async-start(s8[16777216]{0:T(1024)(128)(4,1)} %bitcast.4), calls=%async_computation.1 | async-start | bytes 8388608
  7.6 23.4 %slice-start.2 = ((s8[16777216]{0:T(1024)(128)(4,1)}), s8[4194304]{0:T(1024)(128)(4,1)S(1)}, s32[]{:S(2)}) async-start(s8[16777216]{0:T(1024)(128)(4,1)} %bitcast.4), calls=%async_computation.2 | async-start | bytes 8388608
  7.6 23.4 %slice-start.3 = ((s8[16777216]{0:T(1024)(128)(4,1)}), s8[4194304]{0:T(1024)(128)(4,1)S(1)}, s32[]{:S(2)}) async-start(s8[16777216]{0:T(1024)(128)(4,1)} %bitcast.4), calls=%async_computation.3 | async-start | bytes 8388608
  8.4 6.7 %collective-permute-start.6 = (bf16[16,4096]{1,0:T(8,128)(2,1)S(1)}, bf16[16,4096]{1,0:T(8,128)(2,1)S(1)}, u32[]{:S(2)}, u32[]{:S(2)}) collective-permute-start(bf16[16,4096]{1,0:T(8,128)(2,1)S(1)} %get-tuple-element.40), channel_id=1, source_target_pairs={{0,4},{1,5},{2,6},{3,7},{4,0},{5,1},{6,2},{7,3},{8,12},{9,13},{10,... | collective-permute-start | bytes 393224 | tf_op jit(solution)/shard_map/ppermute | solution.py:336
  8.5 10.2 %collective-permute-start.4 = (bf16[16,4096]{1,0:T(8,128)(2,1)S(1)}, bf16[16,4096]{1,0:T(8,128)(2,1)S(1)}, u32[]{:S(2)}, u32[]{:S(2)}) collective-permute-start(bf16[16,4096]{1,0:T(8,128)(2,1)S(1)} %get-tuple-element.39), channel_id=1, source_target_pairs={{0,8},{1,9},{2,10},{3,11},{4,12},{5,13},{6,14},{7,15},{8,0},{9,1},... | collective-permute-start | bytes 393224 | tf_op jit(solution)/shard_map/ppermute | solution.py:336
  9.1 11.2 %collective-permute-start.1 = (bf16[16,4096]{1,0:T(8,128)(2,1)S(1)}, bf16[16,4096]{1,0:T(8,128)(2,1)S(1)}, u32[]{:S(2)}, u32[]{:S(2)}) collective-permute-start(bf16[16,4096]{1,0:T(8,128)(2,1)S(1)} %get-tuple-element.38.refs_0_), channel_id=1, source_target_pairs={{0,2},{1,3},{2,0},{3,1},{4,6},{5,7},{6,4},{7,5},{8,10},{9,11},{10,... | collective-permute-start | bytes 393224 | tf_op jit(solution)/shard_map/ppermute | solution.py:336
  12.0 8.3 %collective-permute-start.2 = (bf16[16,4096]{1,0:T(8,128)(2,1)S(1)}, bf16[16,4096]{1,0:T(8,128)(2,1)S(1)}, u32[]{:S(2)}, u32[]{:S(2)}) collective-permute-start(bf16[16,4096]{1,0:T(8,128)(2,1)S(1)} %collective-permute-done.after_ref.refs_2_), channel_id=1, source_target_pairs={{0,2},{1,3},{2,0},{3,1},{4,6},{5,7},{6,4},{7,5},{8,10},{9,11},{10,... | collective-permute-start | bytes 393224 | tf_op jit(solution)/shard_map/ppermute | solution.py:336
  15.1 5.3 %collective-permute-start.7 = (bf16[16,4096]{1,0:T(8,128)(2,1)S(1)}, bf16[16,4096]{1,0:T(8,128)(2,1)S(1)}, u32[]{:S(2)}, u32[]{:S(2)}) collective-permute-start(bf16[16,4096]{1,0:T(8,128)(2,1)S(1)} %collective-permute-done.6.refs_2_), channel_id=1, source_target_pairs={{0,2},{1,3},{2,0},{3,1},{4,6},{5,7},{6,4},{7,5},{8,10},{9,11},{10,... | collective-permute-start | bytes 393224 | tf_op jit(solution)/shard_map/ppermute | solution.py:336
  18.7 5.0 %collective-permute-start.5 = (bf16[16,4096]{1,0:T(8,128)(2,1)S(1)}, bf16[16,4096]{1,0:T(8,128)(2,1)S(1)}, u32[]{:S(2)}, u32[]{:S(2)}) collective-permute-start(bf16[16,4096]{1,0:T(8,128)(2,1)S(1)} %join.6.refs_0_), channel_id=1, source_target_pairs={{0,2},{1,3},{2,0},{3,1},{4,6},{5,7},{6,4},{7,5},{8,10},{9,11},{10,... | collective-permute-start | bytes 393224 | tf_op jit(solution)/shard_map/ppermute | solution.py:336
  20.3 3.5 %collective-permute-start.3 = (bf16[64,4096]{1,0:T(8,128)(2,1)S(1)}, bf16[64,4096]{1,0:T(8,128)(2,1)S(1)}, u32[]{:S(2)}, u32[]{:S(2)}) collective-permute-start(bf16[64,4096]{1,0:T(8,128)(2,1)S(1)} %join.5.refs_0_), channel_id=1, source_target_pairs={{0,1},{1,0},{2,3},{3,2},{4,5},{5,4},{6,7},{7,6},{8,9},{9,8},{10,11... | collective-permute-start | bytes 1572872 | tf_op jit(solution)/shard_map/ppermute | solution.py:336
  23.7 2.0 %collective-permute-start.8 = (bf16[64,4096]{1,0:T(8,128)(2,1)S(1)}, bf16[64,4096]{1,0:T(8,128)(2,1)S(1)}, u32[]{:S(2)}, u32[]{:S(2)}) collective-permute-start(bf16[64,4096]{1,0:T(8,128)(2,1)S(1)} %join.8.refs_2_), channel_id=1, source_target_pairs={{0,1},{1,0},{2,3},{3,2},{4,5},{5,4},{6,7},{7,6},{8,9},{9,8},{10,11... | collective-permute-start | bytes 1572872 | tf_op jit(solution)/shard_map/ppermute | solution.py:336
  34.2 3.2 %collective-permute-start.11 = (bf16[64,2560]{1,0:T(8,128)(2,1)S(1)}, bf16[64,2560]{1,0:T(8,128)(2,1)S(1)}, u32[]{:S(2)}, u32[]{:S(2)}) collective-permute-start(bf16[64,2560]{1,0:T(8,128)(2,1)S(1)} %get-tuple-element.48), channel_id=1, source_target_pairs={{0,1},{1,0},{2,3},{3,2},{4,5},{5,4},{6,7},{7,6},{8,9},{9,8},{10,11... | collective-permute-start | bytes 983048 | tf_op jit(solution)/shard_map/ppermute | solution.py:336
  34.4 4.7 %collective-permute-start.9 = (bf16[64,2560]{1,0:T(8,128)(2,1)S(1)}, bf16[64,2560]{1,0:T(8,128)(2,1)S(1)}, u32[]{:S(2)}, u32[]{:S(2)}) collective-permute-start(bf16[64,2560]{1,0:T(8,128)(2,1)S(1)} %get-tuple-element.42), channel_id=1, source_target_pairs={{0,1},{1,0},{2,3},{3,2},{4,5},{5,4},{6,7},{7,6},{8,9},{9,8},{10,11... | collective-permute-start | bytes 983048 | tf_op jit(solution)/shard_map/ppermute | solution.py:336
  35.8 1.6 %collective-permute-start.12 = (bf16[64,1536]{1,0:T(8,128)(2,1)S(1)}, bf16[64,1536]{1,0:T(8,128)(2,1)S(1)}, u32[]{:S(2)}, u32[]{:S(2)}) collective-permute-start(bf16[64,1536]{1,0:T(8,128)(2,1)S(1)} %get-tuple-element.50), channel_id=1, source_target_pairs={{0,1},{1,0},{2,3},{3,2},{4,5},{5,4},{6,7},{7,6},{8,9},{9,8},{10,11... | collective-permute-start | bytes 589832 | tf_op jit(solution)/shard_map/ppermute | solution.py:336
  37.0 2.1 %collective-permute-start.10 = (bf16[64,1536]{1,0:T(8,128)(2,1)S(1)}, bf16[64,1536]{1,0:T(8,128)(2,1)S(1)}, u32[]{:S(2)}, u32[]{:S(2)}) collective-permute-start(bf16[64,1536]{1,0:T(8,128)(2,1)S(1)} %get-tuple-element.44), channel_id=1, source_target_pairs={{0,1},{1,0},{2,3},{3,2},{4,5},{5,4},{6,7},{7,6},{8,9},{9,8},{10,11... | collective-permute-start | bytes 589832 | tf_op jit(solution)/shard_map/ppermute | solution.py:336
  37.5 6.4 %collective-permute-start.13 = (bf16[16,4096]{1,0:T(8,128)(2,1)S(1)}, bf16[16,4096]{1,0:T(8,128)(2,1)S(1)}, u32[]{:S(2)}, u32[]{:S(2)}) collective-permute-start(bf16[16,4096]{1,0:T(8,128)(2,1)S(1)} %get-tuple-element.52), channel_id=1, source_target_pairs={{0,2},{1,3},{2,0},{3,1},{4,6},{5,7},{6,4},{7,5},{8,10},{9,11},{10,... | collective-permute-start | bytes 393224 | tf_op jit(solution)/shard_map/ppermute | solution.py:336
  39.2 8.9 %collective-permute-start.18 = (bf16[16,4096]{1,0:T(8,128)(2,1)S(1)}, bf16[16,4096]{1,0:T(8,128)(2,1)S(1)}, u32[]{:S(2)}, u32[]{:S(2)}) collective-permute-start(bf16[16,4096]{1,0:T(8,128)(2,1)S(1)} %get-tuple-element.56), channel_id=1, source_target_pairs={{0,2},{1,3},{2,0},{3,1},{4,6},{5,7},{6,4},{7,5},{8,10},{9,11},{10,... | collective-permute-start | bytes 393224 | tf_op jit(solution)/shard_map/ppermute | solution.py:336
  40.2 9.4 %collective-permute-start.16 = (bf16[16,4096]{1,0:T(8,128)(2,1)S(1)}, bf16[16,4096]{1,0:T(8,128)(2,1)S(1)}, u32[]{:S(2)}, u32[]{:S(2)}) collective-permute-start(bf16[16,4096]{1,0:T(8,128)(2,1)S(1)} %get-tuple-element.54), channel_id=1, source_target_pairs={{0,2},{1,3},{2,0},{3,1},{4,6},{5,7},{6,4},{7,5},{8,10},{9,11},{10,... | collective-permute-start | bytes 393224 | tf_op jit(solution)/shard_map/ppermute | solution.py:336
  43.9 7.6 %collective-permute-start.15 = (bf16[16,4096]{1,0:T(8,128)(2,1)S(1)}, bf16[16,4096]{1,0:T(8,128)(2,1)S(1)}, u32[]{:S(2)}, u32[]{:S(2)}) collective-permute-start(bf16[16,4096]{1,0:T(8,128)(2,1)S(1)} %add.11.refs_1_), channel_id=1, source_target_pairs={{0,12},{1,13},{2,14},{3,15},{4,8},{5,9},{6,10},{7,11},{8,4},{9,5},... | collective-permute-start | bytes 393224 | tf_op jit(solution)/shard_map/ppermute | solution.py:336
  46.5 5.0 %collective-permute-start.14 = (bf16[16,4096]{1,0:T(8,128)(2,1)S(1)}, bf16[16,4096]{1,0:T(8,128)(2,1)S(1)}, u32[]{:S(2)}, u32[]{:S(2)}) collective-permute-start(bf16[16,4096]{1,0:T(8,128)(2,1)S(1)} %join.9), channel_id=1, source_target_pairs={{0,2},{1,3},{2,0},{3,1},{4,6},{5,7},{6,4},{7,5},{8,10},{9,11},{10,... | collective-permute-start | bytes 393224 | tf_op jit(solution)/shard_map/ppermute | solution.py:336
  48.1 6.2 %collective-permute-start.19 = (bf16[16,4096]{1,0:T(8,128)(2,1)S(1)}, bf16[16,4096]{1,0:T(8,128)(2,1)S(1)}, u32[]{:S(2)}, u32[]{:S(2)}) collective-permute-start(bf16[16,4096]{1,0:T(8,128)(2,1)S(1)} %add.13), channel_id=1, source_target_pairs={{0,4},{1,5},{2,6},{3,7},{4,0},{5,1},{6,2},{7,3},{8,12},{9,13},{10,... | collective-permute-start | bytes 393224 | tf_op jit(solution)/shard_map/ppermute | solution.py:336
  49.5 7.7 %collective-permute-start.17 = (bf16[16,4096]{1,0:T(8,128)(2,1)S(1)}, bf16[16,4096]{1,0:T(8,128)(2,1)S(1)}, u32[]{:S(2)}, u32[]{:S(2)}) collective-permute-start(bf16[16,4096]{1,0:T(8,128)(2,1)S(1)} %add.12), channel_id=1, source_target_pairs={{0,8},{1,9},{2,10},{3,11},{4,12},{5,13},{6,14},{7,15},{8,0},{9,1},... | collective-permute-start | bytes 393224 | tf_op jit(solution)/shard_map/ppermute | solution.py:336
  (1 other events, 18.1 us)

commit v18 on v17

--- a/solution.py
+++ b/solution.py
@@ -201,9 +201,9 @@
     )(*parts, w, *after)
 
 
-def down_kernel(h_ref, w_ref, *outs, columns, low):
+def down_kernel(h_ref, w_ref, *refs, columns, low, groups):
     first, last, tile = columns
-    groups = len(outs) // 2
+    outs = refs[len(refs) - 2 * groups:]
     half = outs[0].shape[0]
 
     @pl.loop(0, (last - first) // tile)
@@ -218,12 +218,12 @@
             outs[2 * g + 1][:, to] = out[at + half:at + 2 * half].astype(BF16)
 
 
-def down(hid, low, groups, w, columns):
+def down(hid, low, groups, w, columns, after):
     half = hid.shape[0] // 4
     step = columns[1] - columns[0]
     return pl.pallas_call(
-        functools.partial(down_kernel, columns=columns, low=low),
-        in_specs=[VMEM] * 2,
+        functools.partial(down_kernel, columns=columns, low=low, groups=groups),
+        in_specs=[VMEM] * 2 + [ANY] * len(after),
         out_specs=[VMEM] * (2 * groups),
         out_shape=[
             jax.ShapeDtypeStruct((half, step), F32),
@@ -233,7 +233,7 @@
         compiler_params=params(8),
         cost_estimate=FREE,
         name="down",
-    )(hid, w)
+    )(hid, w, *after)
 
 
 def add_kernel(*refs, count, outs):
@@ -381,29 +381,36 @@
 
     half = hid.shape[0] // 2
     step = 5 * width // 8
-    keep, send, *others = down(hid, 0, 2, w_down, (0, step, step // 2))
+    keep, send, *others = down(hid, 0, 2, w_down, (0, step, step // 2), [])
     heads = [gather(keep, send), gather(*others)]
-    tails = []
-    for g in range(2):
-        keep, send = down(hid, g * half, 1, w_down, (step, width, width - step))
-        tails.append(gather(keep, send))
-    block = {}
-    for members, head, tail in zip(groups, heads, tails):
+    def sums_of(members, pairs):
         outs = []
         for at in range(len(members)):
             for side in (1, 0):
                 low = (2 * at + side) * slots
-                outs.append([(piece, low, low + slots) for piece in range(2)])
-        sums = add([head, tail], outs, [BF16, F32] * len(members))
-        block.update((i, sums[2 * at:2 * at + 2]) for at, i in enumerate(members))
+                outs.append([(piece, low, low + slots) for piece in range(len(pairs))])
+        sums = add(pairs, outs, [BF16, F32] * len(members))
+        return {i: sums[2 * at:2 * at + 2] for at, i in enumerate(members)}
+
+    tail = gather(*down(hid, 0, 1, w_down, (step, width, width - step), []))
+    block = sums_of(groups[0], [heads[0], tail])
+    tails = []
+    after = []
+    part = (width - step) // 2
+    for low in range(step, width, part):
+        tails.append(gather(*down(hid, half, 1, w_down, (low, low + part, part), after)))
+    block.update(sums_of(groups[1], [heads[1]] + tails))
 
     def total(send, keep):
         return add([(keep, swap(send, near[0]))], [[(0, 0, slots)]], [BF16])[0]
 
     sums = [total(*block[i]) for i in range(1, experts)]
-    back = [swap(part, mask) for part, mask in zip(sums, far)]
+    back = [swap(sums[0], far[0])]
+    for k in range(1, experts - 1):
+        part = sums[k] if k == 1 else join([sums[k]], back[:1])
+        back.append(swap(part, far[k]))
     send, keep = block[0]
-    acc = own_part(mixes[0], keep, swap(join([send], [sums[0]]), near[0]), back[0])
+    acc = own_part(mixes[0], keep, swap(join([send], [sums[1]]), near[0]), back[0])
     return post(mixes[1], table, acc, back[1:])
 
 

time: 58.6 us -> 60.5 us (1.032)
  starting transfers between devices: 23 us -> 26.9 us
  waiting for transfers between devices: 19.5 us -> 17.3 us
    ppermute x20 -> x21, starting transfers between devices: 23 us -> 26.9 us  [swap(): return lax.ppermute(x, 'expert', [(i, i ^ mask) for i in range(devices)])]
    ppermute x20 -> x21, waiting for transfers between devices: 19.5 us -> 17.3 us  [swap(): return lax.ppermute(x, 'expert', [(i, i ^ mask) for i in range(devices)])]
    pallas_call x3 -> x4, Pallas kernels: 5.11 us -> 5.31 us  [down(): pl.pallas_call(functools.partial(down_kernel, columns=columns, low=low, g...]
  transfers between devices with their start and end apart: 20 -> 21, of which waited for: 10 -> 14; matrix products, arithmetic and copies ran while one was open for 0% -> 0% of each run, Pallas kernels for 6% -> 6%
where the time goes in v18:
time: 60.5 us; the launch traced here: 60.3 us
  starting transfers between devices  26.9 us (44%)
  waiting for transfers between devices  17.3 us (29%)
  Pallas kernels  15.8 us (26%)
    ppermute x21, starting transfers between devices, swap(): return lax.ppermute(x, 'expert', [(i, i ^ mask) for i in range(devices)])  26.9 us
    ppermute x21, waiting for transfers between devices, swap(): return lax.ppermute(x, 'expert', [(i, i ^ mask) for i in range(devices)])  17.3 us
    pallas_call x4, Pallas kernels, down(): pl.pallas_call(functools.partial(down_kernel, columns=columns, low=low, g...  5.31 us
    pallas_call x1, Pallas kernels, up(): pl.pallas_call(functools.partial(up_kernel, sources=sources, count=len(pa...  5.27 us
    pallas_call x1, Pallas kernels, first(): pl.pallas_call(first_kernel, in_specs=[SMEM] + [HBM] * 7, out_specs=[VMEM...  2.39 us
  transfers between devices with their start and end apart: 21, of which 14 were waited for; matrix products, arithmetic and copies ran while one was open for 0% of the time, Pallas kernels for 6%

profile of v18, /device:TPU:0, one launch (start us, length us, event | category | flops | bytes accessed | tf_op | source)
XLA Modules:
  0.0 60.3 jit_solution(3655899773798617656)
XLA Ops:
  0.1 2.4 %first.1 = (bf16[16,4096]{1,0:T(8,128)(2,1)S(1)}, bf16[128,4096]{1,0:T(8,128)(2,1)S(1)}, f32[3,4096]{1,0:T(4,128)S(1)}, s32[4,16]{1,0:T(4,128)S(1)}, f32[4,16]{1,0:T(4,128)S(1)}) custom-call(s32[2]{0:T(128)S(1)} %pad_add_fusion.info_ref, bf16[128,4096]{1,0:T(8,128)(2,1)} %refs_0_.1, s32[4,16]{1,0:T(4,128)} %bitcast.6, f32[2,4096]{1,0:T(2,128)} %refs_2_.1, ...), custom_call_target="tpu_custom_call" | custom-call | flops 1 | bytes 1 | tf_op jit(solution)/shard_map/first/pallas_call | solution.py:78
  2.5 5.1 %collective-permute-start = (bf16[16,4096]{1,0:T(8,128)(2,1)S(1)}, bf16[16,4096]{1,0:T(8,128)(2,1)S(1)}, u32[]{:S(2)}, u32[]{:S(2)}) collective-permute-start(bf16[16,4096]{1,0:T(8,128)(2,1)S(1)} %get-tuple-element.35), channel_id=1, source_target_pairs={{0,12},{1,13},{2,14},{3,15},{4,8},{5,9},{6,10},{7,11},{8,4},{9,5},... | collective-permute-start | bytes 393224 | tf_op jit(solution)/shard_map/ppermute | solution.py:336
  9.1 1.7 %collective-permute-start.1 = (bf16[16,4096]{1,0:T(8,128)(2,1)S(1)}, bf16[16,4096]{1,0:T(8,128)(2,1)S(1)}, u32[]{:S(2)}, u32[]{:S(2)}) collective-permute-start(bf16[16,4096]{1,0:T(8,128)(2,1)S(1)} %get-tuple-element.40.refs_0_), channel_id=1, source_target_pairs={{0,2},{1,3},{2,0},{3,1},{4,6},{5,7},{6,4},{7,5},{8,10},{9,11},{10,... | collective-permute-start | bytes 393224 | tf_op jit(solution)/shard_map/ppermute | solution.py:336
  10.8 1.2 %collective-permute-done.after_ref.refs_2_ = bf16[16,4096]{1,0:T(8,128)(2,1)S(1)} collective-permute-done((bf16[16,4096]{1,0:T(8,128)(2,1)S(1)}, bf16[16,4096]{1,0:T(8,128)(2,1)S(1)}, u32[]{:S(2)}, u32[]{:S(2)}) %collective-permute-start) | collective-permute-done | bytes 131104 | tf_op jit(solution)/shard_map/ppermute | solution.py:336
  12.0 1.8 %collective-permute-start.2 = (bf16[16,4096]{1,0:T(8,128)(2,1)S(1)}, bf16[16,4096]{1,0:T(8,128)(2,1)S(1)}, u32[]{:S(2)}, u32[]{:S(2)}) collective-permute-start(bf16[16,4096]{1,0:T(8,128)(2,1)S(1)} %collective-permute-done.after_ref.refs_2_), channel_id=1, source_target_pairs={{0,2},{1,3},{2,0},{3,1},{4,6},{5,7},{6,4},{7,5},{8,10},{9,11},{10,... | collective-permute-start | bytes 393224 | tf_op jit(solution)/shard_map/ppermute | solution.py:336
  13.9 1.2 %collective-permute-done.6.refs_2_ = bf16[16,4096]{1,0:T(8,128)(2,1)S(1)} collective-permute-done((bf16[16,4096]{1,0:T(8,128)(2,1)S(1)}, bf16[16,4096]{1,0:T(8,128)(2,1)S(1)}, u32[]{:S(2)}, u32[]{:S(2)}) %collective-permute-start.6) | collective-permute-done | bytes 131104 | tf_op jit(solution)/shard_map/ppermute | solution.py:336
  15.1 1.6 %collective-permute-start.7 = (bf16[16,4096]{1,0:T(8,128)(2,1)S(1)}, bf16[16,4096]{1,0:T(8,128)(2,1)S(1)}, u32[]{:S(2)}, u32[]{:S(2)}) collective-permute-start(bf16[16,4096]{1,0:T(8,128)(2,1)S(1)} %collective-permute-done.6.refs_2_), channel_id=1, source_target_pairs={{0,2},{1,3},{2,0},{3,1},{4,6},{5,7},{6,4},{7,5},{8,10},{9,11},{10,... | collective-permute-start | bytes 393224 | tf_op jit(solution)/shard_map/ppermute | solution.py:336
  16.7 2.0 %collective-permute-done.4.refs_0_ = bf16[16,4096]{1,0:T(8,128)(2,1)S(1)} collective-permute-done((bf16[16,4096]{1,0:T(8,128)(2,1)S(1)}, bf16[16,4096]{1,0:T(8,128)(2,1)S(1)}, u32[]{:S(2)}, u32[]{:S(2)}) %collective-permute-start.4) | collective-permute-done | bytes 131104 | tf_op jit(solution)/shard_map/ppermute | solution.py:336
  18.7 1.6 %collective-permute-start.5 = (bf16[16,4096]{1,0:T(8,128)(2,1)S(1)}, bf16[16,4096]{1,0:T(8,128)(2,1)S(1)}, u32[]{:S(2)}, u32[]{:S(2)}) collective-permute-start(bf16[16,4096]{1,0:T(8,128)(2,1)S(1)} %join.7.refs_0_), channel_id=1, source_target_pairs={{0,2},{1,3},{2,0},{3,1},{4,6},{5,7},{6,4},{7,5},{8,10},{9,11},{10,... | collective-permute-start | bytes 393224 | tf_op jit(solution)/shard_map/ppermute | solution.py:336
  20.4 3.3 %collective-permute-done.5.refs_1_ = bf16[16,4096]{1,0:T(8,128)(2,1)S(1)} collective-permute-done((bf16[16,4096]{1,0:T(8,128)(2,1)S(1)}, bf16[16,4096]{1,0:T(8,128)(2,1)S(1)}, u32[]{:S(2)}, u32[]{:S(2)}) %collective-permute-start.5) | collective-permute-done | bytes 131104 | tf_op jit(solution)/shard_map/ppermute | solution.py:336
  23.8 1.9 %collective-permute-done.8.refs_3_ = bf16[64,4096]{1,0:T(8,128)(2,1)S(1)} collective-permute-done((bf16[64,4096]{1,0:T(8,128)(2,1)S(1)}, bf16[64,4096]{1,0:T(8,128)(2,1)S(1)}, u32[]{:S(2)}, u32[]{:S(2)}) %collective-permute-start.8) | collective-permute-done | bytes 524320 | tf_op jit(solution)/shard_map/ppermute | solution.py:336
  25.7 5.3 %up.1.h_ref = bf16[256,2048]{1,0:T(8,128)(2,1)S(1)} custom-call(bf16[64,4096]{1,0:T(8,128)(2,1)S(1)} %join.6.refs_0_, bf16[64,4096]{1,0:T(8,128)(2,1)S(1)} %collective-permute-done.3.refs_1_, bf16[64,4096]{1,0:T(8,128)(2,1)S(1)} %join.9.refs_2_, bf16[64,4096]{1,0:T(8,128)(2,1)S(1)} %collective-permute-done.8.refs_3_, bf16[2048,4096]{1,0:T(8,128)(2,1)S(1)} %copy-done), custom_call_target="tpu_custom_call" | custom-call | flops 1 | bytes 1 | tf_op jit(solution)/shard_map/up/pallas_call | solution.py:192
  31.0 3.1 %down.4 = (f32[64,2560]{1,0:T(8,128)S(1)}, bf16[64,2560]{1,0:T(8,128)(2,1)S(1)}, f32[64,2560]{1,0:T(8,128)S(1)}, bf16[64,2560]{1,0:T(8,128)(2,1)S(1)}) custom-call(bf16[256,2048]{1,0:T(8,128)(2,1)S(1)} %up.1.h_ref, bf16[2048,4096]{1,0:T(8,128)(2,1)S(1)} %bitcast.5), custom_call_target="tpu_custom_call" | custom-call | flops 1 | bytes 1 | tf_op jit(solution)/shard_map/down/pallas_call | solution.py:224
  34.4 1.0 %down.7 = (f32[64,1536]{1,0:T(8,128)S(1)}, bf16[64,1536]{1,0:T(8,128)(2,1)S(1)}) custom-call(bf16[256,2048]{1,0:T(8,128)(2,1)S(1)} %up.1.h_ref, bf16[2048,4096]{1,0:T(8,128)(2,1)S(1)} %bitcast.5), custom_call_target="tpu_custom_call" | custom-call | flops 1 | bytes 1 | tf_op jit(solution)/shard_map/down/pallas_call | solution.py:224
  36.0 1.4 %collective-permute-done.13.refs_3_ = bf16[64,1536]{1,0:T(8,128)(2,1)S(1)} collective-permute-done((bf16[64,1536]{1,0:T(8,128)(2,1)S(1)}, bf16[64,1536]{1,0:T(8,128)(2,1)S(1)}, u32[]{:S(2)}, u32[]{:S(2)}) %collective-permute-start.13) | collective-permute-done | bytes 196640 | tf_op jit(solution)/shard_map/ppermute | solution.py:336
  37.5 1.6 %collective-permute-start.16 = (bf16[16,4096]{1,0:T(8,128)(2,1)S(1)}, bf16[16,4096]{1,0:T(8,128)(2,1)S(1)}, u32[]{:S(2)}, u32[]{:S(2)}) collective-permute-start(bf16[16,4096]{1,0:T(8,128)(2,1)S(1)} %get-tuple-element.58), channel_id=1, source_target_pairs={{0,2},{1,3},{2,0},{3,1},{4,6},{5,7},{6,4},{7,5},{8,10},{9,11},{10,... | collective-permute-start | bytes 393224 | tf_op jit(solution)/shard_map/ppermute | solution.py:336
  41.9 1.2 %collective-permute-start.19 = (bf16[16,4096]{1,0:T(8,128)(2,1)S(1)}, bf16[16,4096]{1,0:T(8,128)(2,1)S(1)}, u32[]{:S(2)}, u32[]{:S(2)}) collective-permute-start(bf16[16,4096]{1,0:T(8,128)(2,1)S(1)} %get-tuple-element.60), channel_id=1, source_target_pairs={{0,2},{1,3},{2,0},{3,1},{4,6},{5,7},{6,4},{7,5},{8,10},{9,11},{10,... | collective-permute-start | bytes 393224 | tf_op jit(solution)/shard_map/ppermute | solution.py:336
  43.3 2.5 %collective-permute-start.17 = (bf16[16,4096]{1,0:T(8,128)(2,1)S(1)}, bf16[16,4096]{1,0:T(8,128)(2,1)S(1)}, u32[]{:S(2)}, u32[]{:S(2)}) collective-permute-start(bf16[16,4096]{1,0:T(8,128)(2,1)S(1)} %add.12), channel_id=1, source_target_pairs={{0,12},{1,13},{2,14},{3,15},{4,8},{5,9},{6,10},{7,11},{8,4},{9,5},... | collective-permute-start | bytes 393224 | tf_op jit(solution)/shard_map/ppermute | solution.py:336
  45.9 1.3 %collective-permute-done.14.refs_1_ = bf16[16,4096]{1,0:T(8,128)(2,1)S(1)} collective-permute-done((bf16[16,4096]{1,0:T(8,128)(2,1)S(1)}, bf16[16,4096]{1,0:T(8,128)(2,1)S(1)}, u32[]{:S(2)}, u32[]{:S(2)}) %collective-permute-start.14) | collective-permute-done | bytes 131104 | tf_op jit(solution)/shard_map/ppermute | solution.py:336
  48.1 0.9 %collective-permute-start.15 = (bf16[16,4096]{1,0:T(8,128)(2,1)S(1)}, bf16[16,4096]{1,0:T(8,128)(2,1)S(1)}, u32[]{:S(2)}, u32[]{:S(2)}) collective-permute-start(bf16[16,4096]{1,0:T(8,128)(2,1)S(1)} %join.10), channel_id=1, source_target_pairs={{0,2},{1,3},{2,0},{3,1},{4,6},{5,7},{6,4},{7,5},{8,10},{9,11},{10,... | collective-permute-start | bytes 393224 | tf_op jit(solution)/shard_map/ppermute | solution.py:336
  49.2 1.8 %collective-permute-done.17.got_ref.refs_1_ = bf16[16,4096]{1,0:T(8,128)(2,1)S(1)} collective-permute-done((bf16[16,4096]{1,0:T(8,128)(2,1)S(1)}, bf16[16,4096]{1,0:T(8,128)(2,1)S(1)}, u32[]{:S(2)}, u32[]{:S(2)}) %collective-permute-start.17) | collective-permute-done | bytes 131104 | tf_op jit(solution)/shard_map/ppermute | solution.py:336
  50.9 5.2 %collective-permute-start.20 = (bf16[16,4096]{1,0:T(8,128)(2,1)S(1)}, bf16[16,4096]{1,0:T(8,128)(2,1)S(1)}, u32[]{:S(2)}, u32[]{:S(2)}) collective-permute-start(bf16[16,4096]{1,0:T(8,128)(2,1)S(1)} %join.11), channel_id=1, source_target_pairs={{0,4},{1,5},{2,6},{3,7},{4,0},{5,1},{6,2},{7,3},{8,12},{9,13},{10,... | collective-permute-start | bytes 393224 | tf_op jit(solution)/shard_map/ppermute | solution.py:336
  57.1 2.0 %collective-permute-done.20.refs_1_ = bf16[16,4096]{1,0:T(8,128)(2,1)S(1)} collective-permute-done((bf16[16,4096]{1,0:T(8,128)(2,1)S(1)}, bf16[16,4096]{1,0:T(8,128)(2,1)S(1)}, u32[]{:S(2)}, u32[]{:S(2)}) %collective-permute-start.20) | collective-permute-done | bytes 131104 | tf_op jit(solution)/shard_map/ppermute | solution.py:336
  59.1 1.2 %post.1 = bf16[128,4096]{1,0:T(8,128)(2,1)} custom-call(bf16[128,64]{1,0:T(8,128)(2,1)S(1)} %get-tuple-element.36.mix_ref, f32[3,4096]{1,0:T(4,128)S(1)} %get-tuple-element.37.table_ref, f32[128,4096]{1,0:T(8,128)S(1)} %own_part.1.acc_ref, bf16[16,4096]{1,0:T(8,128)(2,1)S(1)} %collective-permute-done.18.refs_0_, ...), custom_call_target="tpu_custom_call" | custom-call | flops 1 | bytes 1 | tf_op jit(solution)/shard_map/post/pallas_call | solution.py:304
  (51 shorter events, 7.9 us)
Async XLA Ops:
  2.5 9.5 %collective-permute-start = (bf16[16,4096]{1,0:T(8,128)(2,1)S(1)}, bf16[16,4096]{1,0:T(8,128)(2,1)S(1)}, u32[]{:S(2)}, u32[]{:S(2)}) collective-permute-start(bf16[16,4096]{1,0:T(8,128)(2,1)S(1)} %get-tuple-element.35), channel_id=1, source_target_pairs={{0,12},{1,13},{2,14},{3,15},{4,8},{5,9},{6,10},{7,11},{8,4},{9,5},... | collective-permute-start | bytes 393224 | tf_op jit(solution)/shard_map/ppermute | solution.py:336
  7.6 23.4 %slice-start.1 = ((s8[16777216]{0:T(1024)(128)(4,1)}), s8[4194304]{0:T(1024)(128)(4,1)S(1)}, s32[]{:S(2)}) async-start(s8[16777216]{0:T(1024)(128)(4,1)} %bitcast.4), calls=%async_computation.1 | async-start | bytes 8388608
  7.6 23.4 %slice-start.2 = ((s8[16777216]{0:T(1024)(128)(4,1)}), s8[4194304]{0:T(1024)(128)(4,1)S(1)}, s32[]{:S(2)}) async-start(s8[16777216]{0:T(1024)(128)(4,1)} %bitcast.4), calls=%async_computation.2 | async-start | bytes 8388608
  7.6 23.4 %slice-start.3 = ((s8[16777216]{0:T(1024)(128)(4,1)}), s8[4194304]{0:T(1024)(128)(4,1)S(1)}, s32[]{:S(2)}) async-start(s8[16777216]{0:T(1024)(128)(4,1)} %bitcast.4), calls=%async_computation.3 | async-start | bytes 8388608
  8.4 6.7 %collective-permute-start.6 = (bf16[16,4096]{1,0:T(8,128)(2,1)S(1)}, bf16[16,4096]{1,0:T(8,128)(2,1)S(1)}, u32[]{:S(2)}, u32[]{:S(2)}) collective-permute-start(bf16[16,4096]{1,0:T(8,128)(2,1)S(1)} %get-tuple-element.42), channel_id=1, source_target_pairs={{0,4},{1,5},{2,6},{3,7},{4,0},{5,1},{6,2},{7,3},{8,12},{9,13},{10,... | collective-permute-start | bytes 393224 | tf_op jit(solution)/shard_map/ppermute | solution.py:336
  8.5 10.2 %collective-permute-start.4 = (bf16[16,4096]{1,0:T(8,128)(2,1)S(1)}, bf16[16,4096]{1,0:T(8,128)(2,1)S(1)}, u32[]{:S(2)}, u32[]{:S(2)}) collective-permute-start(bf16[16,4096]{1,0:T(8,128)(2,1)S(1)} %get-tuple-element.41), channel_id=1, source_target_pairs={{0,8},{1,9},{2,10},{3,11},{4,12},{5,13},{6,14},{7,15},{8,0},{9,1},... | collective-permute-start | bytes 393224 | tf_op jit(solution)/shard_map/ppermute | solution.py:336
  9.1 11.2 %collective-permute-start.1 = (bf16[16,4096]{1,0:T(8,128)(2,1)S(1)}, bf16[16,4096]{1,0:T(8,128)(2,1)S(1)}, u32[]{:S(2)}, u32[]{:S(2)}) collective-permute-start(bf16[16,4096]{1,0:T(8,128)(2,1)S(1)} %get-tuple-element.40.refs_0_), channel_id=1, source_target_pairs={{0,2},{1,3},{2,0},{3,1},{4,6},{5,7},{6,4},{7,5},{8,10},{9,11},{10,... | collective-permute-start | bytes 393224 | tf_op jit(solution)/shard_map/ppermute | solution.py:336
  12.0 8.3 %collective-permute-start.2 = (bf16[16,4096]{1,0:T(8,128)(2,1)S(1)}, bf16[16,4096]{1,0:T(8,128)(2,1)S(1)}, u32[]{:S(2)}, u32[]{:S(2)}) collective-permute-start(bf16[16,4096]{1,0:T(8,128)(2,1)S(1)} %collective-permute-done.after_ref.refs_2_), channel_id=1, source_target_pairs={{0,2},{1,3},{2,0},{3,1},{4,6},{5,7},{6,4},{7,5},{8,10},{9,11},{10,... | collective-permute-start | bytes 393224 | tf_op jit(solution)/shard_map/ppermute | solution.py:336
  15.1 5.3 %collective-permute-start.7 = (bf16[16,4096]{1,0:T(8,128)(2,1)S(1)}, bf16[16,4096]{1,0:T(8,128)(2,1)S(1)}, u32[]{:S(2)}, u32[]{:S(2)}) collective-permute-start(bf16[16,4096]{1,0:T(8,128)(2,1)S(1)} %collective-permute-done.6.refs_2_), channel_id=1, source_target_pairs={{0,2},{1,3},{2,0},{3,1},{4,6},{5,7},{6,4},{7,5},{8,10},{9,11},{10,... | collective-permute-start | bytes 393224 | tf_op jit(solution)/shard_map/ppermute | solution.py:336
  18.7 5.0 %collective-permute-start.5 = (bf16[16,4096]{1,0:T(8,128)(2,1)S(1)}, bf16[16,4096]{1,0:T(8,128)(2,1)S(1)}, u32[]{:S(2)}, u32[]{:S(2)}) collective-permute-start(bf16[16,4096]{1,0:T(8,128)(2,1)S(1)} %join.7.refs_0_), channel_id=1, source_target_pairs={{0,2},{1,3},{2,0},{3,1},{4,6},{5,7},{6,4},{7,5},{8,10},{9,11},{10,... | collective-permute-start | bytes 393224 | tf_op jit(solution)/shard_map/ppermute | solution.py:336
  20.3 3.5 %collective-permute-start.3 = (bf16[64,4096]{1,0:T(8,128)(2,1)S(1)}, bf16[64,4096]{1,0:T(8,128)(2,1)S(1)}, u32[]{:S(2)}, u32[]{:S(2)}) collective-permute-start(bf16[64,4096]{1,0:T(8,128)(2,1)S(1)} %join.6.refs_0_), channel_id=1, source_target_pairs={{0,1},{1,0},{2,3},{3,2},{4,5},{5,4},{6,7},{7,6},{8,9},{9,8},{10,11... | collective-permute-start | bytes 1572872 | tf_op jit(solution)/shard_map/ppermute | solution.py:336
  23.7 2.0 %collective-permute-start.8 = (bf16[64,4096]{1,0:T(8,128)(2,1)S(1)}, bf16[64,4096]{1,0:T(8,128)(2,1)S(1)}, u32[]{:S(2)}, u32[]{:S(2)}) collective-permute-start(bf16[64,4096]{1,0:T(8,128)(2,1)S(1)} %join.9.refs_2_), channel_id=1, source_target_pairs={{0,1},{1,0},{2,3},{3,2},{4,5},{5,4},{6,7},{7,6},{8,9},{9,8},{10,11... | collective-permute-start | bytes 1572872 | tf_op jit(solution)/shard_map/ppermute | solution.py:336
  34.2 3.2 %collective-permute-start.12 = (bf16[64,2560]{1,0:T(8,128)(2,1)S(1)}, bf16[64,2560]{1,0:T(8,128)(2,1)S(1)}, u32[]{:S(2)}, u32[]{:S(2)}) collective-permute-start(bf16[64,2560]{1,0:T(8,128)(2,1)S(1)} %get-tuple-element.52), channel_id=1, source_target_pairs={{0,1},{1,0},{2,3},{3,2},{4,5},{5,4},{6,7},{7,6},{8,9},{9,8},{10,11... | collective-permute-start | bytes 983048 | tf_op jit(solution)/shard_map/ppermute | solution.py:336
  35.4 6.4 %collective-permute-start.9 = (bf16[64,2560]{1,0:T(8,128)(2,1)S(1)}, bf16[64,2560]{1,0:T(8,128)(2,1)S(1)}, u32[]{:S(2)}, u32[]{:S(2)}) collective-permute-start(bf16[64,2560]{1,0:T(8,128)(2,1)S(1)} %get-tuple-element.44), channel_id=1, source_target_pairs={{0,1},{1,0},{2,3},{3,2},{4,5},{5,4},{6,7},{7,6},{8,9},{9,8},{10,11... | collective-permute-start | bytes 983048 | tf_op jit(solution)/shard_map/ppermute | solution.py:336
  35.8 1.5 %collective-permute-start.13 = (bf16[64,1536]{1,0:T(8,128)(2,1)S(1)}, bf16[64,1536]{1,0:T(8,128)(2,1)S(1)}, u32[]{:S(2)}, u32[]{:S(2)}) collective-permute-start(bf16[64,1536]{1,0:T(8,128)(2,1)S(1)} %get-tuple-element.54), channel_id=1, source_target_pairs={{0,1},{1,0},{2,3},{3,2},{4,5},{5,4},{6,7},{7,6},{8,9},{9,8},{10,11... | collective-permute-start | bytes 589832 | tf_op jit(solution)/shard_map/ppermute | solution.py:336
  37.5 5.8 %collective-permute-start.16 = (bf16[16,4096]{1,0:T(8,128)(2,1)S(1)}, bf16[16,4096]{1,0:T(8,128)(2,1)S(1)}, u32[]{:S(2)}, u32[]{:S(2)}) collective-permute-start(bf16[16,4096]{1,0:T(8,128)(2,1)S(1)} %get-tuple-element.58), channel_id=1, source_target_pairs={{0,2},{1,3},{2,0},{3,1},{4,6},{5,7},{6,4},{7,5},{8,10},{9,11},{10,... | collective-permute-start | bytes 393224 | tf_op jit(solution)/shard_map/ppermute | solution.py:336
  40.3 1.4 %collective-permute-start.11 = (bf16[64,768]{1,0:T(8,128)(2,1)S(1)}, bf16[64,768]{1,0:T(8,128)(2,1)S(1)}, u32[]{:S(2)}, u32[]{:S(2)}) collective-permute-start(bf16[64,768]{1,0:T(8,128)(2,1)S(1)} %get-tuple-element.48), channel_id=1, source_target_pairs={{0,1},{1,0},{2,3},{3,2},{4,5},{5,4},{6,7},{7,6},{8,9},{9,8},{10,11... | collective-permute-start | bytes 294920 | tf_op jit(solution)/shard_map/ppermute | solution.py:336
  40.4 1.4 %collective-permute-start.10 = (bf16[64,768]{1,0:T(8,128)(2,1)S(1)}, bf16[64,768]{1,0:T(8,128)(2,1)S(1)}, u32[]{:S(2)}, u32[]{:S(2)}) collective-permute-start(bf16[64,768]{1,0:T(8,128)(2,1)S(1)} %get-tuple-element.46), channel_id=1, source_target_pairs={{0,1},{1,0},{2,3},{3,2},{4,5},{5,4},{6,7},{7,6},{8,9},{9,8},{10,11... | collective-permute-start | bytes 294920 | tf_op jit(solution)/shard_map/ppermute | solution.py:336
  40.8 6.4 %collective-permute-start.14 = (bf16[16,4096]{1,0:T(8,128)(2,1)S(1)}, bf16[16,4096]{1,0:T(8,128)(2,1)S(1)}, u32[]{:S(2)}, u32[]{:S(2)}) collective-permute-start(bf16[16,4096]{1,0:T(8,128)(2,1)S(1)} %get-tuple-element.56), channel_id=1, source_target_pairs={{0,2},{1,3},{2,0},{3,1},{4,6},{5,7},{6,4},{7,5},{8,10},{9,11},{10,... | collective-permute-start | bytes 393224 | tf_op jit(solution)/shard_map/ppermute | solution.py:336
  41.9 7.3 %collective-permute-start.19 = (bf16[16,4096]{1,0:T(8,128)(2,1)S(1)}, bf16[16,4096]{1,0:T(8,128)(2,1)S(1)}, u32[]{:S(2)}, u32[]{:S(2)}) collective-permute-start(bf16[16,4096]{1,0:T(8,128)(2,1)S(1)} %get-tuple-element.60), channel_id=1, source_target_pairs={{0,2},{1,3},{2,0},{3,1},{4,6},{5,7},{6,4},{7,5},{8,10},{9,11},{10,... | collective-permute-start | bytes 393224 | tf_op jit(solution)/shard_map/ppermute | solution.py:336
  43.3 7.6 %collective-permute-start.17 = (bf16[16,4096]{1,0:T(8,128)(2,1)S(1)}, bf16[16,4096]{1,0:T(8,128)(2,1)S(1)}, u32[]{:S(2)}, u32[]{:S(2)}) collective-permute-start(bf16[16,4096]{1,0:T(8,128)(2,1)S(1)} %add.12), channel_id=1, source_target_pairs={{0,12},{1,13},{2,14},{3,15},{4,8},{5,9},{6,10},{7,11},{8,4},{9,5},... | collective-permute-start | bytes 393224 | tf_op jit(solution)/shard_map/ppermute | solution.py:336
  47.2 9.9 %collective-permute-start.18 = (bf16[16,4096]{1,0:T(8,128)(2,1)S(1)}, bf16[16,4096]{1,0:T(8,128)(2,1)S(1)}, u32[]{:S(2)}, u32[]{:S(2)}) collective-permute-start(bf16[16,4096]{1,0:T(8,128)(2,1)S(1)} %add.11.refs_1_), channel_id=1, source_target_pairs={{0,8},{1,9},{2,10},{3,11},{4,12},{5,13},{6,14},{7,15},{8,0},{9,1},... | collective-permute-start | bytes 393224 | tf_op jit(solution)/shard_map/ppermute | solution.py:336
  48.1 8.0 %collective-permute-start.15 = (bf16[16,4096]{1,0:T(8,128)(2,1)S(1)}, bf16[16,4096]{1,0:T(8,128)(2,1)S(1)}, u32[]{:S(2)}, u32[]{:S(2)}) collective-permute-start(bf16[16,4096]{1,0:T(8,128)(2,1)S(1)} %join.10), channel_id=1, source_target_pairs={{0,2},{1,3},{2,0},{3,1},{4,6},{5,7},{6,4},{7,5},{8,10},{9,11},{10,... | collective-permute-start | bytes 393224 | tf_op jit(solution)/shard_map/ppermute | solution.py:336
  50.9 8.2 %collective-permute-start.20 = (bf16[16,4096]{1,0:T(8,128)(2,1)S(1)}, bf16[16,4096]{1,0:T(8,128)(2,1)S(1)}, u32[]{:S(2)}, u32[]{:S(2)}) collective-permute-start(bf16[16,4096]{1,0:T(8,128)(2,1)S(1)} %join.11), channel_id=1, source_target_pairs={{0,4},{1,5},{2,6},{3,7},{4,0},{5,1},{6,2},{7,3},{8,12},{9,13},{10,... | collective-permute-start | bytes 393224 | tf_op jit(solution)/shard_map/ppermute | solution.py:336
  (2 other events, 41.6 us)

commit v19 on v18

--- a/solution.py
+++ b/solution.py
@@ -264,32 +264,46 @@
     )(*args)
 
 
-def own_kernel(mix_ref, keep_ref, near_ref, got_ref, acc_ref):
-    own = (keep_ref[...] + near_ref[...].astype(F32)).astype(BF16)
+def own_kernel(mix_ref, got_ref, *refs):
+    acc_ref = refs[-1]
+    own = [ref[...] for ref in refs[:-1]]
+    own = own[0] if len(own) == 1 else jnp.concatenate(own, axis=1)
     values = jnp.concatenate([own, got_ref[...]] * 2, axis=0)
     acc_ref[...] = jnp.dot(mix_ref[...], values, preferred_element_type=F32)
 
 
-def own_part(mix, keep, near, got):
+def own_part(mix, got, own):
     return pl.pallas_call(
         own_kernel,
-        in_specs=[VMEM] * 4,
+        in_specs=[VMEM] * (2 + len(own)),
         out_specs=VMEM,
-        out_shape=jax.ShapeDtypeStruct((mix.shape[0], keep.shape[1]), F32),
+        out_shape=jax.ShapeDtypeStruct((mix.shape[0], got.shape[1]), F32),
         compiler_params=params(12),
         cost_estimate=FREE,
         name="own_part",
-    )(mix, keep, near, got)
-
-
-def post_kernel(mix_ref, table_ref, acc_ref, *refs):
-    blocks = refs[:-3]
+    )(mix, got, *own)
+
+
+def post_kernel(mix_ref, table_ref, acc_ref, *refs, counts):
     out_hbm, out_ref, sems = refs[-3:]
     step = out_ref.shape[1] // sems.shape[0]
     copies = []
     for i in range(sems.shape[0]):
+        values = []
+        at = 0
+        for count in counts:
+            pieces = []
+            base = 0
+            for ref in refs[at:at + count]:
+                low = max(i * step - base, 0)
+                high = min((i + 1) * step - base, ref.shape[1])
+                if low < high:
+                    pieces.append(ref[:, low:high])
+                base += ref.shape[1]
+            values.append(pieces[0] if len(pieces) == 1 else jnp.concatenate(pieces, axis=1))
+            at += count
+        values = jnp.concatenate(values * 2, axis=0)
         cut = pl.ds(i * step, step)
-        values = jnp.concatenate([ref[:, cut] for ref in blocks] * 2, axis=0)
         mixed = acc_ref[:, cut] + jnp.dot(mix_ref[...], values, preferred_element_type=F32)
         out_ref[:, cut] = (table_ref[2:3, cut] * mixed).astype(BF16)
         copy = pltpu.make_async_copy(out_ref.at[:, cut], out_hbm.at[:, cut], sems.at[i])
@@ -301,16 +315,17 @@
 
 def post(mix, table, acc, blocks):
     tok_rows, width = acc.shape
-    return pl.pallas_call(
-        post_kernel,
-        in_specs=[VMEM] * (3 + len(blocks)),
+    args = [x for block in blocks for x in block]
+    return pl.pallas_call(
+        functools.partial(post_kernel, counts=[len(block) for block in blocks]),
+        in_specs=[VMEM] * (3 + len(args)),
         out_specs=HBM,
         out_shape=jax.ShapeDtypeStruct((tok_rows, width), BF16),
         scratch_shapes=[pltpu.VMEM((tok_rows, width), BF16), pltpu.SemaphoreType.DMA((4,))],
         compiler_params=params(8),
         cost_estimate=FREE,
         name="post",
-    )(mix, table, acc, *blocks)
+    )(mix, table, acc, *args)
 
 
 def shards(tokens, shift, scale, gate, w_up, w_down, pick, count, combine):
@@ -365,8 +380,11 @@
         parts += pieces
     groups = [[1, 2], list(range(3, experts)) + [0]]
     sources = [
-        cut for members in groups for cuts in zip(*[segments[i] for i in members]) for cut in cuts
+        cut for cuts in zip(*[segments[i] for i in groups[0]]) for cut in cuts
     ]
+    for cuts in zip(*[segments[i] for i in groups[1]]):
+        sources += [(k, low, low + slots) for k, low, _ in cuts]
+        sources += [(k, low + slots, high) for k, low, high in cuts]
     hid = up(parts, sources, w_up, [])
 
     def gather(keep, send):
@@ -383,34 +401,33 @@
     step = 5 * width // 8
     keep, send, *others = down(hid, 0, 2, w_down, (0, step, step // 2), [])
     heads = [gather(keep, send), gather(*others)]
-    def sums_of(members, pairs):
-        outs = []
-        for at in range(len(members)):
-            for side in (1, 0):
-                low = (2 * at + side) * slots
-                outs.append([(piece, low, low + slots) for piece in range(len(pairs))])
-        sums = add(pairs, outs, [BF16, F32] * len(members))
-        return {i: sums[2 * at:2 * at + 2] for at, i in enumerate(members)}
+    def both(low, height, pieces):
+        return [[(piece, at, at + height) for piece in pieces] for at in (low + height, low)]
+
+    def total(send, keep, cuts):
+        return add([(keep, swap(send, near[0]))], [[(0, *cut)] for cut in cuts], [BF16] * len(cuts))
 
     tail = gather(*down(hid, 0, 1, w_down, (step, width, width - step), []))
-    block = sums_of(groups[0], [heads[0], tail])
+    outs = both(0, slots, [0, 1]) + both(2 * slots, slots, [0, 1])
+    sums = add([heads[0], tail], outs, [BF16, F32] * 2)
+    part = (width - step) // 1
     tails = []
-    after = []
-    part = (width - step) // 2
     for low in range(step, width, part):
-        tails.append(gather(*down(hid, half, 1, w_down, (low, low + part, part), after)))
-    block.update(sums_of(groups[1], [heads[1]] + tails))
-
-    def total(send, keep):
-        return add([(keep, swap(send, near[0]))], [[(0, 0, slots)]], [BF16])[0]
-
-    sums = [total(*block[i]) for i in range(1, experts)]
-    back = [swap(sums[0], far[0])]
-    for k in range(1, experts - 1):
-        part = sums[k] if k == 1 else join([sums[k]], back[:1])
-        back.append(swap(part, far[k]))
-    send, keep = block[0]
-    acc = own_part(mixes[0], keep, swap(join([send], [sums[1]]), near[0]), back[0])
+        tails.append(gather(*down(hid, half, 1, w_down, (low, low + part, part), [])))
+    height = len(groups[1]) * slots
+    every = list(range(1 + 1))
+    outs = both(0, height, every[:1]) + both(0, height, every[1:])
+    near_sums = add([heads[1]] + tails, outs, [BF16, F32] * 2)
+
+    back = []
+    for k in range(2):
+        (summed,) = total(*sums[2 * k:2 * k + 2], [(0, slots)])
+        back.append([swap(summed, far[k])])
+    cuts = [(at, at + slots) for at in range(0, height, slots)]
+    columns = [total(*near_sums[2 * k:2 * k + 2], cuts) for k in range(2)]
+    for k, mask in enumerate(far[2:]):
+        back.append([swap(rows[k], mask) for rows in columns])
+    acc = own_part(mixes[0], back[0][0], [rows[-1] for rows in columns])
     return post(mixes[1], table, acc, back[1:])
 
 

time: 60.5 us -> 59.1 us (0.977)
  starting transfers between devices: 26.9 us -> 23.7 us
  waiting for transfers between devices: 17.3 us -> 19.3 us
    ppermute x21, starting transfers between devices: 26.9 us -> 23.7 us  [swap(): return lax.ppermute(x, 'expert', [(i, i ^ mask) for i in range(devices)])]
    ppermute x21, waiting for transfers between devices: 17.3 us -> 19.3 us  [swap(): return lax.ppermute(x, 'expert', [(i, i ^ mask) for i in range(devices)])]
    pallas_call x4 -> x3, Pallas kernels: 5.31 us -> 5.11 us  [down(): pl.pallas_call(functools.partial(down_kernel, columns=columns, low=low, g...]
  transfers between devices with their start and end apart: 21 -> 21, of which waited for: 14 -> 10; matrix products, arithmetic and copies ran while one was open for 0% -> 0% of each run, Pallas kernels for 6% -> 6%
where the time goes in v19:
time: 59.1 us; the launch traced here: 59 us
  starting transfers between devices  23.7 us (40%)
  waiting for transfers between devices  19.3 us (33%)
  Pallas kernels  15.7 us (27%)
    ppermute x21, starting transfers between devices, swap(): return lax.ppermute(x, 'expert', [(i, i ^ mask) for i in range(devices)])  23.7 us
    ppermute x21, waiting for transfers between devices, swap(): return lax.ppermute(x, 'expert', [(i, i ^ mask) for i in range(devices)])  19.3 us
    pallas_call x1, Pallas kernels, up(): pl.pallas_call(functools.partial(up_kernel, sources=sources, count=len(pa...  5.27 us
    pallas_call x3, Pallas kernels, down(): pl.pallas_call(functools.partial(down_kernel, columns=columns, low=low, g...  5.11 us
    pallas_call x1, Pallas kernels, first(): pl.pallas_call(first_kernel, in_specs=[SMEM] + [HBM] * 7, out_specs=[VMEM...  2.39 us
    pallas_call x1, Pallas kernels, post(): pl.pallas_call(functools.partial(post_kernel, counts=[len(block) for bloc...  1.21 us
  transfers between devices with their start and end apart: 21, of which 10 were waited for; matrix products, arithmetic and copies ran while one was open for 0% of the time, Pallas kernels for 6%

profile of v19, /device:TPU:0, one launch (start us, length us, event | category | flops | bytes accessed | tf_op | source)
XLA Modules:
  0.0 59.0 jit_solution(5309441002725807160)
XLA Ops:
  0.1 2.4 %first.1 = (bf16[16,4096]{1,0:T(8,128)(2,1)S(1)}, bf16[128,4096]{1,0:T(8,128)(2,1)S(1)}, f32[3,4096]{1,0:T(4,128)S(1)}, s32[4,16]{1,0:T(4,128)S(1)}, f32[4,16]{1,0:T(4,128)S(1)}) custom-call(s32[2]{0:T(128)S(1)} %pad_add_fusion.info_ref, bf16[128,4096]{1,0:T(8,128)(2,1)} %refs_0_.1, s32[4,16]{1,0:T(4,128)} %bitcast.6, f32[2,4096]{1,0:T(2,128)} %refs_2_.1, ...), custom_call_target="tpu_custom_call" | custom-call | flops 1 | bytes 1 | tf_op jit(solution)/shard_map/first/pallas_call | solution.py:78
  2.5 5.1 %collective-permute-start = (bf16[16,4096]{1,0:T(8,128)(2,1)S(1)}, bf16[16,4096]{1,0:T(8,128)(2,1)S(1)}, u32[]{:S(2)}, u32[]{:S(2)}) collective-permute-start(bf16[16,4096]{1,0:T(8,128)(2,1)S(1)} %get-tuple-element.37), channel_id=1, source_target_pairs={{0,12},{1,13},{2,14},{3,15},{4,8},{5,9},{6,10},{7,11},{8,4},{9,5},... | collective-permute-start | bytes 393224 | tf_op jit(solution)/shard_map/ppermute | solution.py:351
  9.1 1.7 %collective-permute-start.1 = (bf16[16,4096]{1,0:T(8,128)(2,1)S(1)}, bf16[16,4096]{1,0:T(8,128)(2,1)S(1)}, u32[]{:S(2)}, u32[]{:S(2)}) collective-permute-start(bf16[16,4096]{1,0:T(8,128)(2,1)S(1)} %get-tuple-element.42.refs_0_), channel_id=1, source_target_pairs={{0,2},{1,3},{2,0},{3,1},{4,6},{5,7},{6,4},{7,5},{8,10},{9,11},{10,... | collective-permute-start | bytes 393224 | tf_op jit(solution)/shard_map/ppermute | solution.py:351
  10.8 1.2 %collective-permute-done.after_ref.refs_2_ = bf16[16,4096]{1,0:T(8,128)(2,1)S(1)} collective-permute-done((bf16[16,4096]{1,0:T(8,128)(2,1)S(1)}, bf16[16,4096]{1,0:T(8,128)(2,1)S(1)}, u32[]{:S(2)}, u32[]{:S(2)}) %collective-permute-start) | collective-permute-done | bytes 131104 | tf_op jit(solution)/shard_map/ppermute | solution.py:351
  12.0 1.8 %collective-permute-start.2 = (bf16[16,4096]{1,0:T(8,128)(2,1)S(1)}, bf16[16,4096]{1,0:T(8,128)(2,1)S(1)}, u32[]{:S(2)}, u32[]{:S(2)}) collective-permute-start(bf16[16,4096]{1,0:T(8,128)(2,1)S(1)} %collective-permute-done.after_ref.refs_2_), channel_id=1, source_target_pairs={{0,2},{1,3},{2,0},{3,1},{4,6},{5,7},{6,4},{7,5},{8,10},{9,11},{10,... | collective-permute-start | bytes 393224 | tf_op jit(solution)/shard_map/ppermute | solution.py:351
  13.9 1.2 %collective-permute-done.6.refs_2_ = bf16[16,4096]{1,0:T(8,128)(2,1)S(1)} collective-permute-done((bf16[16,4096]{1,0:T(8,128)(2,1)S(1)}, bf16[16,4096]{1,0:T(8,128)(2,1)S(1)}, u32[]{:S(2)}, u32[]{:S(2)}) %collective-permute-start.6) | collective-permute-done | bytes 131104 | tf_op jit(solution)/shard_map/ppermute | solution.py:351
  15.1 1.6 %collective-permute-start.7 = (bf16[16,4096]{1,0:T(8,128)(2,1)S(1)}, bf16[16,4096]{1,0:T(8,128)(2,1)S(1)}, u32[]{:S(2)}, u32[]{:S(2)}) collective-permute-start(bf16[16,4096]{1,0:T(8,128)(2,1)S(1)} %collective-permute-done.6.refs_2_), channel_id=1, source_target_pairs={{0,2},{1,3},{2,0},{3,1},{4,6},{5,7},{6,4},{7,5},{8,10},{9,11},{10,... | collective-permute-start | bytes 393224 | tf_op jit(solution)/shard_map/ppermute | solution.py:351
  16.7 2.0 %collective-permute-done.4.refs_0_ = bf16[16,4096]{1,0:T(8,128)(2,1)S(1)} collective-permute-done((bf16[16,4096]{1,0:T(8,128)(2,1)S(1)}, bf16[16,4096]{1,0:T(8,128)(2,1)S(1)}, u32[]{:S(2)}, u32[]{:S(2)}) %collective-permute-start.4) | collective-permute-done | bytes 131104 | tf_op jit(solution)/shard_map/ppermute | solution.py:351
  18.7 1.6 %collective-permute-start.5 = (bf16[16,4096]{1,0:T(8,128)(2,1)S(1)}, bf16[16,4096]{1,0:T(8,128)(2,1)S(1)}, u32[]{:S(2)}, u32[]{:S(2)}) collective-permute-start(bf16[16,4096]{1,0:T(8,128)(2,1)S(1)} %join.5.refs_0_), channel_id=1, source_target_pairs={{0,2},{1,3},{2,0},{3,1},{4,6},{5,7},{6,4},{7,5},{8,10},{9,11},{10,... | collective-permute-start | bytes 393224 | tf_op jit(solution)/shard_map/ppermute | solution.py:351
  20.4 3.3 %collective-permute-done.5.refs_1_ = bf16[16,4096]{1,0:T(8,128)(2,1)S(1)} collective-permute-done((bf16[16,4096]{1,0:T(8,128)(2,1)S(1)}, bf16[16,4096]{1,0:T(8,128)(2,1)S(1)}, u32[]{:S(2)}, u32[]{:S(2)}) %collective-permute-start.5) | collective-permute-done | bytes 131104 | tf_op jit(solution)/shard_map/ppermute | solution.py:351
  23.8 1.9 %collective-permute-done.8.refs_3_ = bf16[64,4096]{1,0:T(8,128)(2,1)S(1)} collective-permute-done((bf16[64,4096]{1,0:T(8,128)(2,1)S(1)}, bf16[64,4096]{1,0:T(8,128)(2,1)S(1)}, u32[]{:S(2)}, u32[]{:S(2)}) %collective-permute-start.8) | collective-permute-done | bytes 524320 | tf_op jit(solution)/shard_map/ppermute | solution.py:351
  25.7 5.3 %up.1.h_ref = bf16[256,2048]{1,0:T(8,128)(2,1)S(1)} custom-call(bf16[64,4096]{1,0:T(8,128)(2,1)S(1)} %join.4.refs_0_, bf16[64,4096]{1,0:T(8,128)(2,1)S(1)} %collective-permute-done.3.refs_1_, bf16[64,4096]{1,0:T(8,128)(2,1)S(1)} %join.7.refs_2_, bf16[64,4096]{1,0:T(8,128)(2,1)S(1)} %collective-permute-done.8.refs_3_, bf16[2048,4096]{1,0:T(8,128)(2,1)S(1)} %copy-done), custom_call_target="tpu_custom_call" | custom-call | flops 1 | bytes 1 | tf_op jit(solution)/shard_map/up/pallas_call | solution.py:192
  31.0 3.1 %down.3 = (f32[64,2560]{1,0:T(8,128)S(1)}, bf16[64,2560]{1,0:T(8,128)(2,1)S(1)}, f32[64,2560]{1,0:T(8,128)S(1)}, bf16[64,2560]{1,0:T(8,128)(2,1)S(1)}) custom-call(bf16[256,2048]{1,0:T(8,128)(2,1)S(1)} %up.1.h_ref, bf16[2048,4096]{1,0:T(8,128)(2,1)S(1)} %bitcast.5), custom_call_target="tpu_custom_call" | custom-call | flops 1 | bytes 1 | tf_op jit(solution)/shard_map/down/pallas_call | solution.py:224
  34.8 1.0 %down.4 = (f32[64,1536]{1,0:T(8,128)S(1)}, bf16[64,1536]{1,0:T(8,128)(2,1)S(1)}) custom-call(bf16[256,2048]{1,0:T(8,128)(2,1)S(1)} %up.1.h_ref, bf16[2048,4096]{1,0:T(8,128)(2,1)S(1)} %bitcast.5), custom_call_target="tpu_custom_call" | custom-call | flops 1 | bytes 1 | tf_op jit(solution)/shard_map/down/pallas_call | solution.py:224
  36.0 1.0 %down.5 = (f32[64,1536]{1,0:T(8,128)S(1)}, bf16[64,1536]{1,0:T(8,128)(2,1)S(1)}) custom-call(bf16[256,2048]{1,0:T(8,128)(2,1)S(1)} %up.1.h_ref, bf16[2048,4096]{1,0:T(8,128)(2,1)S(1)} %bitcast.5), custom_call_target="tpu_custom_call" | custom-call | flops 1 | bytes 1 | tf_op jit(solution)/shard_map/down/pallas_call | solution.py:224
  37.5 1.6 %collective-permute-start.11 = (bf16[16,4096]{1,0:T(8,128)(2,1)S(1)}, bf16[16,4096]{1,0:T(8,128)(2,1)S(1)}, u32[]{:S(2)}, u32[]{:S(2)}) collective-permute-start(bf16[16,4096]{1,0:T(8,128)(2,1)S(1)} %get-tuple-element.50), channel_id=1, source_target_pairs={{0,2},{1,3},{2,0},{3,1},{4,6},{5,7},{6,4},{7,5},{8,10},{9,11},{10,... | collective-permute-start | bytes 393224 | tf_op jit(solution)/shard_map/ppermute | solution.py:351
  39.7 1.6 %collective-permute-start.15 = (bf16[32,2560]{1,0:T(8,128)(2,1)S(1)}, bf16[32,2560]{1,0:T(8,128)(2,1)S(1)}, u32[]{:S(2)}, u32[]{:S(2)}) collective-permute-start(bf16[32,2560]{1,0:T(8,128)(2,1)S(1)} %get-tuple-element.56), channel_id=1, source_target_pairs={{0,2},{1,3},{2,0},{3,1},{4,6},{5,7},{6,4},{7,5},{8,10},{9,11},{10,... | collective-permute-start | bytes 491528 | tf_op jit(solution)/shard_map/ppermute | solution.py:351
  41.8 2.1 %collective-permute-done.11.refs_1_ = bf16[16,4096]{1,0:T(8,128)(2,1)S(1)} collective-permute-done((bf16[16,4096]{1,0:T(8,128)(2,1)S(1)}, bf16[16,4096]{1,0:T(8,128)(2,1)S(1)}, u32[]{:S(2)}, u32[]{:S(2)}) %collective-permute-start.11) | collective-permute-done | bytes 131104 | tf_op jit(solution)/shard_map/ppermute | solution.py:351
  43.9 2.5 %collective-permute-start.12 = (bf16[16,4096]{1,0:T(8,128)(2,1)S(1)}, bf16[16,4096]{1,0:T(8,128)(2,1)S(1)}, u32[]{:S(2)}, u32[]{:S(2)}) collective-permute-start(bf16[16,4096]{1,0:T(8,128)(2,1)S(1)} %add.11), channel_id=1, source_target_pairs={{0,12},{1,13},{2,14},{3,15},{4,8},{5,9},{6,10},{7,11},{8,4},{9,5},... | collective-permute-start | bytes 393224 | tf_op jit(solution)/shard_map/ppermute | solution.py:351
  46.7 1.3 %collective-permute-start.18 = (bf16[16,4096]{1,0:T(8,128)(2,1)S(1)}, bf16[16,4096]{1,0:T(8,128)(2,1)S(1)}, u32[]{:S(2)}, u32[]{:S(2)}) collective-permute-start(bf16[16,4096]{1,0:T(8,128)(2,1)S(1)} %add.15), channel_id=1, source_target_pairs={{0,8},{1,9},{2,10},{3,11},{4,12},{5,13},{6,14},{7,15},{8,0},{9,1},... | collective-permute-start | bytes 393224 | tf_op jit(solution)/shard_map/ppermute | solution.py:351
  48.0 2.2 %collective-permute-done.15.refs_1_ = bf16[32,2560]{1,0:T(8,128)(2,1)S(1)} collective-permute-done((bf16[32,2560]{1,0:T(8,128)(2,1)S(1)}, bf16[32,2560]{1,0:T(8,128)(2,1)S(1)}, u32[]{:S(2)}, u32[]{:S(2)}) %collective-permute-start.15) | collective-permute-done | bytes 163872 | tf_op jit(solution)/shard_map/ppermute | solution.py:351
  50.3 0.9 %collective-permute-start.19 = (bf16[16,2560]{1,0:T(8,128)(2,1)S(1)}, bf16[16,2560]{1,0:T(8,128)(2,1)S(1)}, u32[]{:S(2)}, u32[]{:S(2)}) collective-permute-start(bf16[16,2560]{1,0:T(8,128)(2,1)S(1)} %get-tuple-element.63), channel_id=1, source_target_pairs={{0,4},{1,5},{2,6},{3,7},{4,0},{5,1},{6,2},{7,3},{8,12},{9,13},{10,... | collective-permute-start | bytes 245768 | tf_op jit(solution)/shard_map/ppermute | solution.py:351
  52.9 4.8 %collective-permute-done.20.refs_2_ = bf16[16,1536]{1,0:T(8,128)(2,1)S(1)} collective-permute-done((bf16[16,1536]{1,0:T(8,128)(2,1)S(1)}, bf16[16,1536]{1,0:T(8,128)(2,1)S(1)}, u32[]{:S(2)}, u32[]{:S(2)}) %collective-permute-start.20) | collective-permute-done | bytes 49184 | tf_op jit(solution)/shard_map/ppermute | solution.py:351
  57.8 1.2 %post.1 = bf16[128,4096]{1,0:T(8,128)(2,1)} custom-call(bf16[128,64]{1,0:T(8,128)(2,1)S(1)} %get-tuple-element.38.mix_ref, f32[3,4096]{1,0:T(4,128)S(1)} %get-tuple-element.39.table_ref, f32[128,4096]{1,0:T(8,128)S(1)} %own_part.1.acc_ref, bf16[16,4096]{1,0:T(8,128)(2,1)S(1)} %collective-permute-done.18.refs_0_, ...), custom_call_target="tpu_custom_call" | custom-call | flops 1 | bytes 1 | tf_op jit(solution)/shard_map/post/pallas_call | solution.py:319
  (49 shorter events, 6.3 us)
Async XLA Ops:
  2.5 9.5 %collective-permute-start = (bf16[16,4096]{1,0:T(8,128)(2,1)S(1)}, bf16[16,4096]{1,0:T(8,128)(2,1)S(1)}, u32[]{:S(2)}, u32[]{:S(2)}) collective-permute-start(bf16[16,4096]{1,0:T(8,128)(2,1)S(1)} %get-tuple-element.37), channel_id=1, source_target_pairs={{0,12},{1,13},{2,14},{3,15},{4,8},{5,9},{6,10},{7,11},{8,4},{9,5},... | collective-permute-start | bytes 393224 | tf_op jit(solution)/shard_map/ppermute | solution.py:351
  7.6 23.4 %slice-start.1 = ((s8[16777216]{0:T(1024)(128)(4,1)}), s8[4194304]{0:T(1024)(128)(4,1)S(1)}, s32[]{:S(2)}) async-start(s8[16777216]{0:T(1024)(128)(4,1)} %bitcast.4), calls=%async_computation.1 | async-start | bytes 8388608
  7.6 23.4 %slice-start.2 = ((s8[16777216]{0:T(1024)(128)(4,1)}), s8[4194304]{0:T(1024)(128)(4,1)S(1)}, s32[]{:S(2)}) async-start(s8[16777216]{0:T(1024)(128)(4,1)} %bitcast.4), calls=%async_computation.2 | async-start | bytes 8388608
  7.6 23.4 %slice-start.3 = ((s8[16777216]{0:T(1024)(128)(4,1)}), s8[4194304]{0:T(1024)(128)(4,1)S(1)}, s32[]{:S(2)}) async-start(s8[16777216]{0:T(1024)(128)(4,1)} %bitcast.4), calls=%async_computation.3 | async-start | bytes 8388608
  8.4 6.7 %collective-permute-start.6 = (bf16[16,4096]{1,0:T(8,128)(2,1)S(1)}, bf16[16,4096]{1,0:T(8,128)(2,1)S(1)}, u32[]{:S(2)}, u32[]{:S(2)}) collective-permute-start(bf16[16,4096]{1,0:T(8,128)(2,1)S(1)} %get-tuple-element.44), channel_id=1, source_target_pairs={{0,4},{1,5},{2,6},{3,7},{4,0},{5,1},{6,2},{7,3},{8,12},{9,13},{10,... | collective-permute-start | bytes 393224 | tf_op jit(solution)/shard_map/ppermute | solution.py:351
  8.5 10.2 %collective-permute-start.4 = (bf16[16,4096]{1,0:T(8,128)(2,1)S(1)}, bf16[16,4096]{1,0:T(8,128)(2,1)S(1)}, u32[]{:S(2)}, u32[]{:S(2)}) collective-permute-start(bf16[16,4096]{1,0:T(8,128)(2,1)S(1)} %get-tuple-element.43), channel_id=1, source_target_pairs={{0,8},{1,9},{2,10},{3,11},{4,12},{5,13},{6,14},{7,15},{8,0},{9,1},... | collective-permute-start | bytes 393224 | tf_op jit(solution)/shard_map/ppermute | solution.py:351
  9.1 11.2 %collective-permute-start.1 = (bf16[16,4096]{1,0:T(8,128)(2,1)S(1)}, bf16[16,4096]{1,0:T(8,128)(2,1)S(1)}, u32[]{:S(2)}, u32[]{:S(2)}) collective-permute-start(bf16[16,4096]{1,0:T(8,128)(2,1)S(1)} %get-tuple-element.42.refs_0_), channel_id=1, source_target_pairs={{0,2},{1,3},{2,0},{3,1},{4,6},{5,7},{6,4},{7,5},{8,10},{9,11},{10,... | collective-permute-start | bytes 393224 | tf_op jit(solution)/shard_map/ppermute | solution.py:351
  12.0 8.3 %collective-permute-start.2 = (bf16[16,4096]{1,0:T(8,128)(2,1)S(1)}, bf16[16,4096]{1,0:T(8,128)(2,1)S(1)}, u32[]{:S(2)}, u32[]{:S(2)}) collective-permute-start(bf16[16,4096]{1,0:T(8,128)(2,1)S(1)} %collective-permute-done.after_ref.refs_2_), channel_id=1, source_target_pairs={{0,2},{1,3},{2,0},{3,1},{4,6},{5,7},{6,4},{7,5},{8,10},{9,11},{10,... | collective-permute-start | bytes 393224 | tf_op jit(solution)/shard_map/ppermute | solution.py:351
  15.1 5.3 %collective-permute-start.7 = (bf16[16,4096]{1,0:T(8,128)(2,1)S(1)}, bf16[16,4096]{1,0:T(8,128)(2,1)S(1)}, u32[]{:S(2)}, u32[]{:S(2)}) collective-permute-start(bf16[16,4096]{1,0:T(8,128)(2,1)S(1)} %collective-permute-done.6.refs_2_), channel_id=1, source_target_pairs={{0,2},{1,3},{2,0},{3,1},{4,6},{5,7},{6,4},{7,5},{8,10},{9,11},{10,... | collective-permute-start | bytes 393224 | tf_op jit(solution)/shard_map/ppermute | solution.py:351
  18.7 5.0 %collective-permute-start.5 = (bf16[16,4096]{1,0:T(8,128)(2,1)S(1)}, bf16[16,4096]{1,0:T(8,128)(2,1)S(1)}, u32[]{:S(2)}, u32[]{:S(2)}) collective-permute-start(bf16[16,4096]{1,0:T(8,128)(2,1)S(1)} %join.5.refs_0_), channel_id=1, source_target_pairs={{0,2},{1,3},{2,0},{3,1},{4,6},{5,7},{6,4},{7,5},{8,10},{9,11},{10,... | collective-permute-start | bytes 393224 | tf_op jit(solution)/shard_map/ppermute | solution.py:351
  20.3 3.5 %collective-permute-start.3 = (bf16[64,4096]{1,0:T(8,128)(2,1)S(1)}, bf16[64,4096]{1,0:T(8,128)(2,1)S(1)}, u32[]{:S(2)}, u32[]{:S(2)}) collective-permute-start(bf16[64,4096]{1,0:T(8,128)(2,1)S(1)} %join.4.refs_0_), channel_id=1, source_target_pairs={{0,1},{1,0},{2,3},{3,2},{4,5},{5,4},{6,7},{7,6},{8,9},{9,8},{10,11... | collective-permute-start | bytes 1572872 | tf_op jit(solution)/shard_map/ppermute | solution.py:351
  23.7 2.0 %collective-permute-start.8 = (bf16[64,4096]{1,0:T(8,128)(2,1)S(1)}, bf16[64,4096]{1,0:T(8,128)(2,1)S(1)}, u32[]{:S(2)}, u32[]{:S(2)}) collective-permute-start(bf16[64,4096]{1,0:T(8,128)(2,1)S(1)} %join.7.refs_2_), channel_id=1, source_target_pairs={{0,1},{1,0},{2,3},{3,2},{4,5},{5,4},{6,7},{7,6},{8,9},{9,8},{10,11... | collective-permute-start | bytes 1572872 | tf_op jit(solution)/shard_map/ppermute | solution.py:351
  34.2 3.2 %collective-permute-start.9 = (bf16[64,2560]{1,0:T(8,128)(2,1)S(1)}, bf16[64,2560]{1,0:T(8,128)(2,1)S(1)}, u32[]{:S(2)}, u32[]{:S(2)}) collective-permute-start(bf16[64,2560]{1,0:T(8,128)(2,1)S(1)} %get-tuple-element.46), channel_id=1, source_target_pairs={{0,1},{1,0},{2,3},{3,2},{4,5},{5,4},{6,7},{7,6},{8,9},{9,8},{10,11... | collective-permute-start | bytes 983048 | tf_op jit(solution)/shard_map/ppermute | solution.py:351
  34.4 5.2 %collective-permute-start.13 = (bf16[64,2560]{1,0:T(8,128)(2,1)S(1)}, bf16[64,2560]{1,0:T(8,128)(2,1)S(1)}, u32[]{:S(2)}, u32[]{:S(2)}) collective-permute-start(bf16[64,2560]{1,0:T(8,128)(2,1)S(1)} %get-tuple-element.52), channel_id=1, source_target_pairs={{0,1},{1,0},{2,3},{3,2},{4,5},{5,4},{6,7},{7,6},{8,9},{9,8},{10,11... | collective-permute-start | bytes 983048 | tf_op jit(solution)/shard_map/ppermute | solution.py:351
  35.8 1.6 %collective-permute-start.10 = (bf16[64,1536]{1,0:T(8,128)(2,1)S(1)}, bf16[64,1536]{1,0:T(8,128)(2,1)S(1)}, u32[]{:S(2)}, u32[]{:S(2)}) collective-permute-start(bf16[64,1536]{1,0:T(8,128)(2,1)S(1)} %get-tuple-element.48), channel_id=1, source_target_pairs={{0,1},{1,0},{2,3},{3,2},{4,5},{5,4},{6,7},{7,6},{8,9},{9,8},{10,11... | collective-permute-start | bytes 589832 | tf_op jit(solution)/shard_map/ppermute | solution.py:351
  37.0 2.6 %collective-permute-start.14 = (bf16[64,1536]{1,0:T(8,128)(2,1)S(1)}, bf16[64,1536]{1,0:T(8,128)(2,1)S(1)}, u32[]{:S(2)}, u32[]{:S(2)}) collective-permute-start(bf16[64,1536]{1,0:T(8,128)(2,1)S(1)} %get-tuple-element.54), channel_id=1, source_target_pairs={{0,1},{1,0},{2,3},{3,2},{4,5},{5,4},{6,7},{7,6},{8,9},{9,8},{10,11... | collective-permute-start | bytes 589832 | tf_op jit(solution)/shard_map/ppermute | solution.py:351
  37.5 6.4 %collective-permute-start.11 = (bf16[16,4096]{1,0:T(8,128)(2,1)S(1)}, bf16[16,4096]{1,0:T(8,128)(2,1)S(1)}, u32[]{:S(2)}, u32[]{:S(2)}) collective-permute-start(bf16[16,4096]{1,0:T(8,128)(2,1)S(1)} %get-tuple-element.50), channel_id=1, source_target_pairs={{0,2},{1,3},{2,0},{3,1},{4,6},{5,7},{6,4},{7,5},{8,10},{9,11},{10,... | collective-permute-start | bytes 393224 | tf_op jit(solution)/shard_map/ppermute | solution.py:351
  39.1 7.6 %collective-permute-start.17 = (bf16[16,4096]{1,0:T(8,128)(2,1)S(1)}, bf16[16,4096]{1,0:T(8,128)(2,1)S(1)}, u32[]{:S(2)}, u32[]{:S(2)}) collective-permute-start(bf16[16,4096]{1,0:T(8,128)(2,1)S(1)} %get-tuple-element.62), channel_id=1, source_target_pairs={{0,2},{1,3},{2,0},{3,1},{4,6},{5,7},{6,4},{7,5},{8,10},{9,11},{10,... | collective-permute-start | bytes 393224 | tf_op jit(solution)/shard_map/ppermute | solution.py:351
  39.7 10.5 %collective-permute-start.15 = (bf16[32,2560]{1,0:T(8,128)(2,1)S(1)}, bf16[32,2560]{1,0:T(8,128)(2,1)S(1)}, u32[]{:S(2)}, u32[]{:S(2)}) collective-permute-start(bf16[32,2560]{1,0:T(8,128)(2,1)S(1)} %get-tuple-element.56), channel_id=1, source_target_pairs={{0,2},{1,3},{2,0},{3,1},{4,6},{5,7},{6,4},{7,5},{8,10},{9,11},{10,... | collective-permute-start | bytes 491528 | tf_op jit(solution)/shard_map/ppermute | solution.py:351
  41.3 10.2 %collective-permute-start.16 = (bf16[32,1536]{1,0:T(8,128)(2,1)S(1)}, bf16[32,1536]{1,0:T(8,128)(2,1)S(1)}, u32[]{:S(2)}, u32[]{:S(2)}) collective-permute-start(bf16[32,1536]{1,0:T(8,128)(2,1)S(1)} %get-tuple-element.59), channel_id=1, source_target_pairs={{0,2},{1,3},{2,0},{3,1},{4,6},{5,7},{6,4},{7,5},{8,10},{9,11},{10,... | collective-permute-start | bytes 294920 | tf_op jit(solution)/shard_map/ppermute | solution.py:351
  43.9 8.6 %collective-permute-start.12 = (bf16[16,4096]{1,0:T(8,128)(2,1)S(1)}, bf16[16,4096]{1,0:T(8,128)(2,1)S(1)}, u32[]{:S(2)}, u32[]{:S(2)}) collective-permute-start(bf16[16,4096]{1,0:T(8,128)(2,1)S(1)} %add.11), channel_id=1, source_target_pairs={{0,12},{1,13},{2,14},{3,15},{4,8},{5,9},{6,10},{7,11},{8,4},{9,5},... | collective-permute-start | bytes 393224 | tf_op jit(solution)/shard_map/ppermute | solution.py:351
  46.7 11.0 %collective-permute-start.18 = (bf16[16,4096]{1,0:T(8,128)(2,1)S(1)}, bf16[16,4096]{1,0:T(8,128)(2,1)S(1)}, u32[]{:S(2)}, u32[]{:S(2)}) collective-permute-start(bf16[16,4096]{1,0:T(8,128)(2,1)S(1)} %add.15), channel_id=1, source_target_pairs={{0,8},{1,9},{2,10},{3,11},{4,12},{5,13},{6,14},{7,15},{8,0},{9,1},... | collective-permute-start | bytes 393224 | tf_op jit(solution)/shard_map/ppermute | solution.py:351
  50.3 7.5 %collective-permute-start.19 = (bf16[16,2560]{1,0:T(8,128)(2,1)S(1)}, bf16[16,2560]{1,0:T(8,128)(2,1)S(1)}, u32[]{:S(2)}, u32[]{:S(2)}) collective-permute-start(bf16[16,2560]{1,0:T(8,128)(2,1)S(1)} %get-tuple-element.63), channel_id=1, source_target_pairs={{0,4},{1,5},{2,6},{3,7},{4,0},{5,1},{6,2},{7,3},{8,12},{9,13},{10,... | collective-permute-start | bytes 245768 | tf_op jit(solution)/shard_map/ppermute | solution.py:351
  51.6 6.2 %collective-permute-start.20 = (bf16[16,1536]{1,0:T(8,128)(2,1)S(1)}, bf16[16,1536]{1,0:T(8,128)(2,1)S(1)}, u32[]{:S(2)}, u32[]{:S(2)}) collective-permute-start(bf16[16,1536]{1,0:T(8,128)(2,1)S(1)} %get-tuple-element.64), channel_id=1, source_target_pairs={{0,4},{1,5},{2,6},{3,7},{4,0},{5,1},{6,2},{7,3},{8,12},{9,13},{10,... | collective-permute-start | bytes 147464 | tf_op jit(solution)/shard_map/ppermute | solution.py:351
  (2 other events, 41.6 us)

commit v20 on v17

--- a/solution.py
+++ b/solution.py
@@ -347,11 +347,10 @@
     mixes = mixer(picks, weights, blocks[1], tok_rows)
     blocks[2] = join([blocks[2]], [mixes[0]])
     beside = [swap(block, near[0]) for block in blocks]
-    beside[-1] = join([beside[-1]], [])
     early, late = list(range(experts // 2)), list(range(experts // 2, experts))
     parts = []
     segments = {}
-    for members in (early, late):
+    for members in [[i] for i in early + late]:
         pieces = [join([x for i in members for x in (blocks[i], beside[i])], [])]
         height = pieces[0].shape[0]
         for mask in near[1:]:

time: 58.6 us -> 58.2 us (level)
  waiting for transfers between devices: 19.5 us -> 18.5 us
  starting transfers between devices: 23 us -> 23.6 us
    ppermute x20 -> x22, waiting for transfers between devices: 19.5 us -> 18.5 us  [swap(): return lax.ppermute(x, 'expert', [(i, i ^ mask) for i in range(devices)])]
    ppermute x20 -> x22, starting transfers between devices: 23 us -> 23.6 us  [swap(): return lax.ppermute(x, 'expert', [(i, i ^ mask) for i in range(devices)])]
  transfers between devices with their start and end apart: 20 -> 22, of which waited for: 10 -> 10; matrix products, arithmetic and copies ran while one was open for 0% -> 0% of each run, Pallas kernels for 6% -> 6%
where the time goes in v20:
time: 58.2 us; the launch traced here: 58 us
  starting transfers between devices  23.6 us (41%)
  waiting for transfers between devices  18.5 us (32%)
  Pallas kernels  15.6 us (27%)
    ppermute x22, starting transfers between devices, swap(): return lax.ppermute(x, 'expert', [(i, i ^ mask) for i in range(devices)])  23.6 us
    ppermute x22, waiting for transfers between devices, swap(): return lax.ppermute(x, 'expert', [(i, i ^ mask) for i in range(devices)])  18.5 us
    pallas_call x1, Pallas kernels, up(): pl.pallas_call(functools.partial(up_kernel, sources=sources, count=len(pa...  5.26 us
    pallas_call x3, Pallas kernels, down(): pl.pallas_call(functools.partial(down_kernel, columns=columns, low=low),...  5.11 us
    pallas_call x1, Pallas kernels, first(): pl.pallas_call(first_kernel, in_specs=[SMEM] + [HBM] * 7, out_specs=[VMEM...  2.39 us
    pallas_call x1, Pallas kernels, post(): pl.pallas_call(post_kernel, in_specs=[VMEM] * (3 + len(blocks)), out_spec...  1.21 us
  transfers between devices with their start and end apart: 22, of which 10 were waited for; matrix products, arithmetic and copies ran while one was open for 0% of the time, Pallas kernels for 6%

profile of v20, /device:TPU:0, one launch (start us, length us, event | category | flops | bytes accessed | tf_op | source)
XLA Modules:
  0.0 58.0 jit_solution(8210018302290868153)
XLA Ops:
  0.1 2.4 %first.1 = (bf16[16,4096]{1,0:T(8,128)(2,1)S(1)}, bf16[128,4096]{1,0:T(8,128)(2,1)S(1)}, f32[3,4096]{1,0:T(4,128)S(1)}, s32[4,16]{1,0:T(4,128)S(1)}, f32[4,16]{1,0:T(4,128)S(1)}) custom-call(s32[2]{0:T(128)S(1)} %pad_add_fusion.info_ref, bf16[128,4096]{1,0:T(8,128)(2,1)} %refs_0_.1, s32[4,16]{1,0:T(4,128)} %bitcast.6, f32[2,4096]{1,0:T(2,128)} %refs_2_.1, ...), custom_call_target="tpu_custom_call" | custom-call | flops 1 | bytes 1 | tf_op jit(solution)/shard_map/first/pallas_call | solution.py:78
  2.5 5.1 %collective-permute-start = (bf16[16,4096]{1,0:T(8,128)(2,1)S(1)}, bf16[16,4096]{1,0:T(8,128)(2,1)S(1)}, u32[]{:S(2)}, u32[]{:S(2)}) collective-permute-start(bf16[16,4096]{1,0:T(8,128)(2,1)S(1)} %get-tuple-element.33), channel_id=1, source_target_pairs={{0,12},{1,13},{2,14},{3,15},{4,8},{5,9},{6,10},{7,11},{8,4},{9,5},... | collective-permute-start | bytes 393224 | tf_op jit(solution)/shard_map/ppermute | solution.py:336
  9.1 1.7 %collective-permute-start.1 = (bf16[16,4096]{1,0:T(8,128)(2,1)S(1)}, bf16[16,4096]{1,0:T(8,128)(2,1)S(1)}, u32[]{:S(2)}, u32[]{:S(2)}) collective-permute-start(bf16[16,4096]{1,0:T(8,128)(2,1)S(1)} %get-tuple-element.38.refs_0_), channel_id=1, source_target_pairs={{0,2},{1,3},{2,0},{3,1},{4,6},{5,7},{6,4},{7,5},{8,10},{9,11},{10,... | collective-permute-start | bytes 393224 | tf_op jit(solution)/shard_map/ppermute | solution.py:336
  10.8 1.2 %collective-permute-done.after_ref.refs_0_ = bf16[16,4096]{1,0:T(8,128)(2,1)S(1)} collective-permute-done((bf16[16,4096]{1,0:T(8,128)(2,1)S(1)}, bf16[16,4096]{1,0:T(8,128)(2,1)S(1)}, u32[]{:S(2)}, u32[]{:S(2)}) %collective-permute-start) | collective-permute-done | bytes 131104 | tf_op jit(solution)/shard_map/ppermute | solution.py:336
  12.0 1.8 %collective-permute-start.3 = (bf16[16,4096]{1,0:T(8,128)(2,1)S(1)}, bf16[16,4096]{1,0:T(8,128)(2,1)S(1)}, u32[]{:S(2)}, u32[]{:S(2)}) collective-permute-start(bf16[16,4096]{1,0:T(8,128)(2,1)S(1)} %collective-permute-done.after_ref.refs_0_), channel_id=1, source_target_pairs={{0,2},{1,3},{2,0},{3,1},{4,6},{5,7},{6,4},{7,5},{8,10},{9,11},{10,... | collective-permute-start | bytes 393224 | tf_op jit(solution)/shard_map/ppermute | solution.py:336
  13.9 1.2 %collective-permute-done.8.refs_0_ = bf16[16,4096]{1,0:T(8,128)(2,1)S(1)} collective-permute-done((bf16[16,4096]{1,0:T(8,128)(2,1)S(1)}, bf16[16,4096]{1,0:T(8,128)(2,1)S(1)}, u32[]{:S(2)}, u32[]{:S(2)}) %collective-permute-start.8) | collective-permute-done | bytes 131104 | tf_op jit(solution)/shard_map/ppermute | solution.py:336
  15.1 1.6 %collective-permute-start.9 = (bf16[16,4096]{1,0:T(8,128)(2,1)S(1)}, bf16[16,4096]{1,0:T(8,128)(2,1)S(1)}, u32[]{:S(2)}, u32[]{:S(2)}) collective-permute-start(bf16[16,4096]{1,0:T(8,128)(2,1)S(1)} %collective-permute-done.8.refs_0_), channel_id=1, source_target_pairs={{0,2},{1,3},{2,0},{3,1},{4,6},{5,7},{6,4},{7,5},{8,10},{9,11},{10,... | collective-permute-start | bytes 393224 | tf_op jit(solution)/shard_map/ppermute | solution.py:336
  16.7 2.0 %collective-permute-done.5.refs_0_ = bf16[16,4096]{1,0:T(8,128)(2,1)S(1)} collective-permute-done((bf16[16,4096]{1,0:T(8,128)(2,1)S(1)}, bf16[16,4096]{1,0:T(8,128)(2,1)S(1)}, u32[]{:S(2)}, u32[]{:S(2)}) %collective-permute-start.5) | collective-permute-done | bytes 131104 | tf_op jit(solution)/shard_map/ppermute | solution.py:336
  18.7 1.6 %collective-permute-start.6 = (bf16[16,4096]{1,0:T(8,128)(2,1)S(1)}, bf16[16,4096]{1,0:T(8,128)(2,1)S(1)}, u32[]{:S(2)}, u32[]{:S(2)}) collective-permute-start(bf16[16,4096]{1,0:T(8,128)(2,1)S(1)} %join.8.refs_0_), channel_id=1, source_target_pairs={{0,2},{1,3},{2,0},{3,1},{4,6},{5,7},{6,4},{7,5},{8,10},{9,11},{10,... | collective-permute-start | bytes 393224 | tf_op jit(solution)/shard_map/ppermute | solution.py:336
  21.1 2.6 %collective-permute-done.6.refs_1_ = bf16[16,4096]{1,0:T(8,128)(2,1)S(1)} collective-permute-done((bf16[16,4096]{1,0:T(8,128)(2,1)S(1)}, bf16[16,4096]{1,0:T(8,128)(2,1)S(1)}, u32[]{:S(2)}, u32[]{:S(2)}) %collective-permute-start.6) | collective-permute-done | bytes 131104 | tf_op jit(solution)/shard_map/ppermute | solution.py:336
  23.8 1.5 %collective-permute-done.7.refs_5_ = bf16[32,4096]{1,0:T(8,128)(2,1)S(1)} collective-permute-done((bf16[32,4096]{1,0:T(8,128)(2,1)S(1)}, bf16[32,4096]{1,0:T(8,128)(2,1)S(1)}, u32[]{:S(2)}, u32[]{:S(2)}) %collective-permute-start.7) | collective-permute-done | bytes 262176 | tf_op jit(solution)/shard_map/ppermute | solution.py:336
  25.3 5.3 %up.1.h_ref = bf16[256,2048]{1,0:T(8,128)(2,1)S(1)} custom-call(bf16[32,4096]{1,0:T(8,128)(2,1)S(1)} %join.6.refs_0_, bf16[32,4096]{1,0:T(8,128)(2,1)S(1)} %collective-permute-done.2.refs_1_, bf16[32,4096]{1,0:T(8,128)(2,1)S(1)} %join.7.refs_2_, bf16[32,4096]{1,0:T(8,128)(2,1)S(1)} %collective-permute-done.4.refs_3_, bf16[32,4096]{1,0:T(8,128)(2,1)S(1)} %join.9.refs_4_, ...), custom_call_target="tpu_custom_call" | custom-call | flops 1 | bytes 1 | tf_op jit(solution)/shard_map/up/pallas_call | solution.py:192
  30.6 3.1 %down.3 = (f32[64,2560]{1,0:T(8,128)S(1)}, bf16[64,2560]{1,0:T(8,128)(2,1)S(1)}, f32[64,2560]{1,0:T(8,128)S(1)}, bf16[64,2560]{1,0:T(8,128)(2,1)S(1)}) custom-call(bf16[256,2048]{1,0:T(8,128)(2,1)S(1)} %up.1.h_ref, bf16[2048,4096]{1,0:T(8,128)(2,1)S(1)} %bitcast.5), custom_call_target="tpu_custom_call" | custom-call | flops 1 | bytes 1 | tf_op jit(solution)/shard_map/down/pallas_call | solution.py:224
  35.6 1.0 %down.4 = (f32[64,1536]{1,0:T(8,128)S(1)}, bf16[64,1536]{1,0:T(8,128)(2,1)S(1)}) custom-call(bf16[256,2048]{1,0:T(8,128)(2,1)S(1)} %up.1.h_ref, bf16[2048,4096]{1,0:T(8,128)(2,1)S(1)} %bitcast.5), custom_call_target="tpu_custom_call" | custom-call | flops 1 | bytes 1 | tf_op jit(solution)/shard_map/down/pallas_call | solution.py:224
  37.1 1.6 %collective-permute-start.15 = (bf16[16,4096]{1,0:T(8,128)(2,1)S(1)}, bf16[16,4096]{1,0:T(8,128)(2,1)S(1)}, u32[]{:S(2)}, u32[]{:S(2)}) collective-permute-start(bf16[16,4096]{1,0:T(8,128)(2,1)S(1)} %get-tuple-element.52), channel_id=1, source_target_pairs={{0,2},{1,3},{2,0},{3,1},{4,6},{5,7},{6,4},{7,5},{8,10},{9,11},{10,... | collective-permute-start | bytes 393224 | tf_op jit(solution)/shard_map/ppermute | solution.py:336
  39.8 1.1 %collective-permute-start.18 = (bf16[16,4096]{1,0:T(8,128)(2,1)S(1)}, bf16[16,4096]{1,0:T(8,128)(2,1)S(1)}, u32[]{:S(2)}, u32[]{:S(2)}) collective-permute-start(bf16[16,4096]{1,0:T(8,128)(2,1)S(1)} %get-tuple-element.54), channel_id=1, source_target_pairs={{0,2},{1,3},{2,0},{3,1},{4,6},{5,7},{6,4},{7,5},{8,10},{9,11},{10,... | collective-permute-start | bytes 393224 | tf_op jit(solution)/shard_map/ppermute | solution.py:336
  40.9 2.6 %collective-permute-done.15.refs_1_ = bf16[16,4096]{1,0:T(8,128)(2,1)S(1)} collective-permute-done((bf16[16,4096]{1,0:T(8,128)(2,1)S(1)}, bf16[16,4096]{1,0:T(8,128)(2,1)S(1)}, u32[]{:S(2)}, u32[]{:S(2)}) %collective-permute-start.15) | collective-permute-done | bytes 131104 | tf_op jit(solution)/shard_map/ppermute | solution.py:336
  43.5 2.5 %collective-permute-start.17 = (bf16[16,4096]{1,0:T(8,128)(2,1)S(1)}, bf16[16,4096]{1,0:T(8,128)(2,1)S(1)}, u32[]{:S(2)}, u32[]{:S(2)}) collective-permute-start(bf16[16,4096]{1,0:T(8,128)(2,1)S(1)} %add.11.refs_1_), channel_id=1, source_target_pairs={{0,12},{1,13},{2,14},{3,15},{4,8},{5,9},{6,10},{7,11},{8,4},{9,5},... | collective-permute-start | bytes 393224 | tf_op jit(solution)/shard_map/ppermute | solution.py:336
  46.1 1.6 %collective-permute-start.16 = (bf16[16,4096]{1,0:T(8,128)(2,1)S(1)}, bf16[16,4096]{1,0:T(8,128)(2,1)S(1)}, u32[]{:S(2)}, u32[]{:S(2)}) collective-permute-start(bf16[16,4096]{1,0:T(8,128)(2,1)S(1)} %join.11), channel_id=1, source_target_pairs={{0,2},{1,3},{2,0},{3,1},{4,6},{5,7},{6,4},{7,5},{8,10},{9,11},{10,... | collective-permute-start | bytes 393224 | tf_op jit(solution)/shard_map/ppermute | solution.py:336
  47.8 1.3 %collective-permute-done.18.refs_1_ = bf16[16,4096]{1,0:T(8,128)(2,1)S(1)} collective-permute-done((bf16[16,4096]{1,0:T(8,128)(2,1)S(1)}, bf16[16,4096]{1,0:T(8,128)(2,1)S(1)}, u32[]{:S(2)}, u32[]{:S(2)}) %collective-permute-start.18) | collective-permute-done | bytes 131104 | tf_op jit(solution)/shard_map/ppermute | solution.py:336
  49.2 1.2 %collective-permute-start.19 = (bf16[16,4096]{1,0:T(8,128)(2,1)S(1)}, bf16[16,4096]{1,0:T(8,128)(2,1)S(1)}, u32[]{:S(2)}, u32[]{:S(2)}) collective-permute-start(bf16[16,4096]{1,0:T(8,128)(2,1)S(1)} %add.12), channel_id=1, source_target_pairs={{0,8},{1,9},{2,10},{3,11},{4,12},{5,13},{6,14},{7,15},{8,0},{9,1},... | collective-permute-start | bytes 393224 | tf_op jit(solution)/shard_map/ppermute | solution.py:336
  51.5 2.4 %collective-permute-done.21.refs_1_ = bf16[16,4096]{1,0:T(8,128)(2,1)S(1)} collective-permute-done((bf16[16,4096]{1,0:T(8,128)(2,1)S(1)}, bf16[16,4096]{1,0:T(8,128)(2,1)S(1)}, u32[]{:S(2)}, u32[]{:S(2)}) %collective-permute-start.21) | collective-permute-done | bytes 131104 | tf_op jit(solution)/shard_map/ppermute | solution.py:336
  54.0 2.9 %collective-permute-done.19.refs_0_ = bf16[16,4096]{1,0:T(8,128)(2,1)S(1)} collective-permute-done((bf16[16,4096]{1,0:T(8,128)(2,1)S(1)}, bf16[16,4096]{1,0:T(8,128)(2,1)S(1)}, u32[]{:S(2)}, u32[]{:S(2)}) %collective-permute-start.19) | collective-permute-done | bytes 131104 | tf_op jit(solution)/shard_map/ppermute | solution.py:336
  56.8 1.2 %post.1 = bf16[128,4096]{1,0:T(8,128)(2,1)} custom-call(bf16[128,64]{1,0:T(8,128)(2,1)S(1)} %get-tuple-element.34.mix_ref, f32[3,4096]{1,0:T(4,128)S(1)} %get-tuple-element.35.table_ref, f32[128,4096]{1,0:T(8,128)S(1)} %own_part.1.acc_ref, bf16[16,4096]{1,0:T(8,128)(2,1)S(1)} %collective-permute-done.19.refs_0_, ...), custom_call_target="tpu_custom_call" | custom-call | flops 1 | bytes 1 | tf_op jit(solution)/shard_map/post/pallas_call | solution.py:304
  (52 shorter events, 7.2 us)
Async XLA Ops:
  2.5 9.5 %collective-permute-start = (bf16[16,4096]{1,0:T(8,128)(2,1)S(1)}, bf16[16,4096]{1,0:T(8,128)(2,1)S(1)}, u32[]{:S(2)}, u32[]{:S(2)}) collective-permute-start(bf16[16,4096]{1,0:T(8,128)(2,1)S(1)} %get-tuple-element.33), channel_id=1, source_target_pairs={{0,12},{1,13},{2,14},{3,15},{4,8},{5,9},{6,10},{7,11},{8,4},{9,5},... | collective-permute-start | bytes 393224 | tf_op jit(solution)/shard_map/ppermute | solution.py:336
  7.6 23.0 %slice-start.2 = ((s8[16777216]{0:T(1024)(128)(4,1)}), s8[4194304]{0:T(1024)(128)(4,1)S(1)}, s32[]{:S(2)}) async-start(s8[16777216]{0:T(1024)(128)(4,1)} %bitcast.4), calls=%async_computation.2 | async-start | bytes 8388608
  7.6 23.0 %slice-start.3 = ((s8[16777216]{0:T(1024)(128)(4,1)}), s8[4194304]{0:T(1024)(128)(4,1)S(1)}, s32[]{:S(2)}) async-start(s8[16777216]{0:T(1024)(128)(4,1)} %bitcast.4), calls=%async_computation.3 | async-start | bytes 8388608
  8.4 6.7 %collective-permute-start.8 = (bf16[16,4096]{1,0:T(8,128)(2,1)S(1)}, bf16[16,4096]{1,0:T(8,128)(2,1)S(1)}, u32[]{:S(2)}, u32[]{:S(2)}) collective-permute-start(bf16[16,4096]{1,0:T(8,128)(2,1)S(1)} %get-tuple-element.40), channel_id=1, source_target_pairs={{0,4},{1,5},{2,6},{3,7},{4,0},{5,1},{6,2},{7,3},{8,12},{9,13},{10,... | collective-permute-start | bytes 393224 | tf_op jit(solution)/shard_map/ppermute | solution.py:336
  8.5 10.2 %collective-permute-start.5 = (bf16[16,4096]{1,0:T(8,128)(2,1)S(1)}, bf16[16,4096]{1,0:T(8,128)(2,1)S(1)}, u32[]{:S(2)}, u32[]{:S(2)}) collective-permute-start(bf16[16,4096]{1,0:T(8,128)(2,1)S(1)} %get-tuple-element.39), channel_id=1, source_target_pairs={{0,8},{1,9},{2,10},{3,11},{4,12},{5,13},{6,14},{7,15},{8,0},{9,1},... | collective-permute-start | bytes 393224 | tf_op jit(solution)/shard_map/ppermute | solution.py:336
  9.1 11.2 %collective-permute-start.1 = (bf16[16,4096]{1,0:T(8,128)(2,1)S(1)}, bf16[16,4096]{1,0:T(8,128)(2,1)S(1)}, u32[]{:S(2)}, u32[]{:S(2)}) collective-permute-start(bf16[16,4096]{1,0:T(8,128)(2,1)S(1)} %get-tuple-element.38.refs_0_), channel_id=1, source_target_pairs={{0,2},{1,3},{2,0},{3,1},{4,6},{5,7},{6,4},{7,5},{8,10},{9,11},{10,... | collective-permute-start | bytes 393224 | tf_op jit(solution)/shard_map/ppermute | solution.py:336
  12.0 8.4 %collective-permute-start.3 = (bf16[16,4096]{1,0:T(8,128)(2,1)S(1)}, bf16[16,4096]{1,0:T(8,128)(2,1)S(1)}, u32[]{:S(2)}, u32[]{:S(2)}) collective-permute-start(bf16[16,4096]{1,0:T(8,128)(2,1)S(1)} %collective-permute-done.after_ref.refs_0_), channel_id=1, source_target_pairs={{0,2},{1,3},{2,0},{3,1},{4,6},{5,7},{6,4},{7,5},{8,10},{9,11},{10,... | collective-permute-start | bytes 393224 | tf_op jit(solution)/shard_map/ppermute | solution.py:336
  15.1 5.9 %collective-permute-start.9 = (bf16[16,4096]{1,0:T(8,128)(2,1)S(1)}, bf16[16,4096]{1,0:T(8,128)(2,1)S(1)}, u32[]{:S(2)}, u32[]{:S(2)}) collective-permute-start(bf16[16,4096]{1,0:T(8,128)(2,1)S(1)} %collective-permute-done.8.refs_0_), channel_id=1, source_target_pairs={{0,2},{1,3},{2,0},{3,1},{4,6},{5,7},{6,4},{7,5},{8,10},{9,11},{10,... | collective-permute-start | bytes 393224 | tf_op jit(solution)/shard_map/ppermute | solution.py:336
  18.7 5.0 %collective-permute-start.6 = (bf16[16,4096]{1,0:T(8,128)(2,1)S(1)}, bf16[16,4096]{1,0:T(8,128)(2,1)S(1)}, u32[]{:S(2)}, u32[]{:S(2)}) collective-permute-start(bf16[16,4096]{1,0:T(8,128)(2,1)S(1)} %join.8.refs_0_), channel_id=1, source_target_pairs={{0,2},{1,3},{2,0},{3,1},{4,6},{5,7},{6,4},{7,5},{8,10},{9,11},{10,... | collective-permute-start | bytes 393224 | tf_op jit(solution)/shard_map/ppermute | solution.py:336
  20.3 3.5 %collective-permute-start.2 = (bf16[32,4096]{1,0:T(8,128)(2,1)S(1)}, bf16[32,4096]{1,0:T(8,128)(2,1)S(1)}, u32[]{:S(2)}, u32[]{:S(2)}) collective-permute-start(bf16[32,4096]{1,0:T(8,128)(2,1)S(1)} %join.6.refs_0_), channel_id=1, source_target_pairs={{0,1},{1,0},{2,3},{3,2},{4,5},{5,4},{6,7},{7,6},{8,9},{9,8},{10,11... | collective-permute-start | bytes 786440 | tf_op jit(solution)/shard_map/ppermute | solution.py:336
  20.4 3.4 %collective-permute-start.4 = (bf16[32,4096]{1,0:T(8,128)(2,1)S(1)}, bf16[32,4096]{1,0:T(8,128)(2,1)S(1)}, u32[]{:S(2)}, u32[]{:S(2)}) collective-permute-start(bf16[32,4096]{1,0:T(8,128)(2,1)S(1)} %join.7.refs_2_), channel_id=1, source_target_pairs={{0,1},{1,0},{2,3},{3,2},{4,5},{5,4},{6,7},{7,6},{8,9},{9,8},{10,11... | collective-permute-start | bytes 786440 | tf_op jit(solution)/shard_map/ppermute | solution.py:336
  21.0 2.9 %collective-permute-start.10 = (bf16[32,4096]{1,0:T(8,128)(2,1)S(1)}, bf16[32,4096]{1,0:T(8,128)(2,1)S(1)}, u32[]{:S(2)}, u32[]{:S(2)}) collective-permute-start(bf16[32,4096]{1,0:T(8,128)(2,1)S(1)} %join.10.refs_6_), channel_id=1, source_target_pairs={{0,1},{1,0},{2,3},{3,2},{4,5},{5,4},{6,7},{7,6},{8,9},{9,8},{10,11... | collective-permute-start | bytes 786440 | tf_op jit(solution)/shard_map/ppermute | solution.py:336
  23.7 1.6 %collective-permute-start.7 = (bf16[32,4096]{1,0:T(8,128)(2,1)S(1)}, bf16[32,4096]{1,0:T(8,128)(2,1)S(1)}, u32[]{:S(2)}, u32[]{:S(2)}) collective-permute-start(bf16[32,4096]{1,0:T(8,128)(2,1)S(1)} %join.9.refs_4_), channel_id=1, source_target_pairs={{0,1},{1,0},{2,3},{3,2},{4,5},{5,4},{6,7},{7,6},{8,9},{9,8},{10,11... | collective-permute-start | bytes 786440 | tf_op jit(solution)/shard_map/ppermute | solution.py:336
  33.8 3.2 %collective-permute-start.13 = (bf16[64,2560]{1,0:T(8,128)(2,1)S(1)}, bf16[64,2560]{1,0:T(8,128)(2,1)S(1)}, u32[]{:S(2)}, u32[]{:S(2)}) collective-permute-start(bf16[64,2560]{1,0:T(8,128)(2,1)S(1)} %get-tuple-element.48), channel_id=1, source_target_pairs={{0,1},{1,0},{2,3},{3,2},{4,5},{5,4},{6,7},{7,6},{8,9},{9,8},{10,11... | collective-permute-start | bytes 983048 | tf_op jit(solution)/shard_map/ppermute | solution.py:336
  34.0 4.7 %collective-permute-start.11 = (bf16[64,2560]{1,0:T(8,128)(2,1)S(1)}, bf16[64,2560]{1,0:T(8,128)(2,1)S(1)}, u32[]{:S(2)}, u32[]{:S(2)}) collective-permute-start(bf16[64,2560]{1,0:T(8,128)(2,1)S(1)} %get-tuple-element.42), channel_id=1, source_target_pairs={{0,1},{1,0},{2,3},{3,2},{4,5},{5,4},{6,7},{7,6},{8,9},{9,8},{10,11... | collective-permute-start | bytes 983048 | tf_op jit(solution)/shard_map/ppermute | solution.py:336
  35.4 1.6 %collective-permute-start.14 = (bf16[64,1536]{1,0:T(8,128)(2,1)S(1)}, bf16[64,1536]{1,0:T(8,128)(2,1)S(1)}, u32[]{:S(2)}, u32[]{:S(2)}) collective-permute-start(bf16[64,1536]{1,0:T(8,128)(2,1)S(1)} %get-tuple-element.50), channel_id=1, source_target_pairs={{0,1},{1,0},{2,3},{3,2},{4,5},{5,4},{6,7},{7,6},{8,9},{9,8},{10,11... | collective-permute-start | bytes 589832 | tf_op jit(solution)/shard_map/ppermute | solution.py:336
  36.6 2.1 %collective-permute-start.12 = (bf16[64,1536]{1,0:T(8,128)(2,1)S(1)}, bf16[64,1536]{1,0:T(8,128)(2,1)S(1)}, u32[]{:S(2)}, u32[]{:S(2)}) collective-permute-start(bf16[64,1536]{1,0:T(8,128)(2,1)S(1)} %get-tuple-element.44), channel_id=1, source_target_pairs={{0,1},{1,0},{2,3},{3,2},{4,5},{5,4},{6,7},{7,6},{8,9},{9,8},{10,11... | collective-permute-start | bytes 589832 | tf_op jit(solution)/shard_map/ppermute | solution.py:336
  37.1 6.4 %collective-permute-start.15 = (bf16[16,4096]{1,0:T(8,128)(2,1)S(1)}, bf16[16,4096]{1,0:T(8,128)(2,1)S(1)}, u32[]{:S(2)}, u32[]{:S(2)}) collective-permute-start(bf16[16,4096]{1,0:T(8,128)(2,1)S(1)} %get-tuple-element.52), channel_id=1, source_target_pairs={{0,2},{1,3},{2,0},{3,1},{4,6},{5,7},{6,4},{7,5},{8,10},{9,11},{10,... | collective-permute-start | bytes 393224 | tf_op jit(solution)/shard_map/ppermute | solution.py:336
  38.8 8.9 %collective-permute-start.20 = (bf16[16,4096]{1,0:T(8,128)(2,1)S(1)}, bf16[16,4096]{1,0:T(8,128)(2,1)S(1)}, u32[]{:S(2)}, u32[]{:S(2)}) collective-permute-start(bf16[16,4096]{1,0:T(8,128)(2,1)S(1)} %get-tuple-element.56), channel_id=1, source_target_pairs={{0,2},{1,3},{2,0},{3,1},{4,6},{5,7},{6,4},{7,5},{8,10},{9,11},{10,... | collective-permute-start | bytes 393224 | tf_op jit(solution)/shard_map/ppermute | solution.py:336
  39.8 9.4 %collective-permute-start.18 = (bf16[16,4096]{1,0:T(8,128)(2,1)S(1)}, bf16[16,4096]{1,0:T(8,128)(2,1)S(1)}, u32[]{:S(2)}, u32[]{:S(2)}) collective-permute-start(bf16[16,4096]{1,0:T(8,128)(2,1)S(1)} %get-tuple-element.54), channel_id=1, source_target_pairs={{0,2},{1,3},{2,0},{3,1},{4,6},{5,7},{6,4},{7,5},{8,10},{9,11},{10,... | collective-permute-start | bytes 393224 | tf_op jit(solution)/shard_map/ppermute | solution.py:336
  43.5 7.6 %collective-permute-start.17 = (bf16[16,4096]{1,0:T(8,128)(2,1)S(1)}, bf16[16,4096]{1,0:T(8,128)(2,1)S(1)}, u32[]{:S(2)}, u32[]{:S(2)}) collective-permute-start(bf16[16,4096]{1,0:T(8,128)(2,1)S(1)} %add.11.refs_1_), channel_id=1, source_target_pairs={{0,12},{1,13},{2,14},{3,15},{4,8},{5,9},{6,10},{7,11},{8,4},{9,5},... | collective-permute-start | bytes 393224 | tf_op jit(solution)/shard_map/ppermute | solution.py:336
  46.1 5.0 %collective-permute-start.16 = (bf16[16,4096]{1,0:T(8,128)(2,1)S(1)}, bf16[16,4096]{1,0:T(8,128)(2,1)S(1)}, u32[]{:S(2)}, u32[]{:S(2)}) collective-permute-start(bf16[16,4096]{1,0:T(8,128)(2,1)S(1)} %join.11), channel_id=1, source_target_pairs={{0,2},{1,3},{2,0},{3,1},{4,6},{5,7},{6,4},{7,5},{8,10},{9,11},{10,... | collective-permute-start | bytes 393224 | tf_op jit(solution)/shard_map/ppermute | solution.py:336
  47.7 6.3 %collective-permute-start.21 = (bf16[16,4096]{1,0:T(8,128)(2,1)S(1)}, bf16[16,4096]{1,0:T(8,128)(2,1)S(1)}, u32[]{:S(2)}, u32[]{:S(2)}) collective-permute-start(bf16[16,4096]{1,0:T(8,128)(2,1)S(1)} %add.13), channel_id=1, source_target_pairs={{0,4},{1,5},{2,6},{3,7},{4,0},{5,1},{6,2},{7,3},{8,12},{9,13},{10,... | collective-permute-start | bytes 393224 | tf_op jit(solution)/shard_map/ppermute | solution.py:336
  49.2 7.7 %collective-permute-start.19 = (bf16[16,4096]{1,0:T(8,128)(2,1)S(1)}, bf16[16,4096]{1,0:T(8,128)(2,1)S(1)}, u32[]{:S(2)}, u32[]{:S(2)}) collective-permute-start(bf16[16,4096]{1,0:T(8,128)(2,1)S(1)} %add.12), channel_id=1, source_target_pairs={{0,8},{1,9},{2,10},{3,11},{4,12},{5,13},{6,14},{7,15},{8,0},{9,1},... | collective-permute-start | bytes 393224 | tf_op jit(solution)/shard_map/ppermute | solution.py:336
  (3 other events, 63.8 us)

commit v21 on v20

--- a/solution.py
+++ b/solution.py
@@ -26,14 +26,6 @@
     return pltpu.CompilerParams(vmem_limit_bytes=mib * MIB)
 
 
-def fetch(pairs, sems):
-    copies = [pltpu.make_async_copy(src, dst, sems.at[i]) for i, (src, dst) in enumerate(pairs)]
-    for copy in copies:
-        copy.start()
-    for copy in copies:
-        copy.wait()
-
-
 def turns(experts):
     return [0] + list(range(experts - 1, 0, -1))
 
@@ -42,8 +34,11 @@
     return lax.broadcasted_iota(jnp.int32, (tok_rows, picks.shape[1]), 0) == picks
 
 
-def modulate(picks, tok_ref, table_ref):
-    hot = hot_rows(picks, tok_ref.shape[0]).astype(F32).astype(BF16)
+def one_hot(picks, tok_rows):
+    return hot_rows(picks, tok_rows).astype(F32).astype(BF16)
+
+
+def modulate(hot, tok_ref, table_ref):
     values = lax.dot_general(hot, tok_ref[...], (((0,), (0,)), ((), ())), preferred_element_type=F32)
     center = values - jnp.mean(values, axis=1, keepdims=True)
     spread = jnp.mean(center * center, axis=1, keepdims=True)
@@ -55,10 +50,15 @@
     sources = refs[:7]
     far_ref, tok_ref, table_ref, picks_ref, weights_ref = refs[7:12]
     pick_ref, comb_ref, count_ref, shift_ref, scale_ref, gate_ref, sems = refs[12:]
-    fetch(
-        list(zip(sources, (tok_ref, pick_ref, shift_ref, scale_ref, gate_ref, comb_ref, count_ref))),
-        sems,
-    )
+    targets = (tok_ref, pick_ref, shift_ref, scale_ref, gate_ref, comb_ref, count_ref)
+    copies = [
+        pltpu.make_async_copy(src, dst, sems.at[i])
+        for i, (src, dst) in enumerate(zip(sources, targets))
+    ]
+    for copy in copies:
+        copy.start()
+    for copy in copies[1:]:
+        copy.wait()
     experts, slots = pick_ref.shape
     which = pl.ds(info_ref[0], 1)
     table_ref[0:1, :] = 1.0 + scale_ref[which, :]
@@ -69,7 +69,9 @@
         e = info_ref[1] ^ d
         picks_ref[i:i + 1, :] = pick_ref[pl.ds(e, 1), :]
         weights_ref[i:i + 1, :] = jnp.where(lanes < count_ref[0, e], comb_ref[pl.ds(e, 1), :], 0.0)
-    far_ref[...] = modulate(picks_ref[1:2, :], tok_ref, table_ref)
+    hot = one_hot(picks_ref[1:2, :], tok_ref.shape[0])
+    copies[0].wait()
+    far_ref[...] = modulate(hot, tok_ref, table_ref)
 
 
 def first(info, tokens, pick, shift, scale, gate, comb, count):
@@ -105,7 +107,7 @@
     experts, slots = picks_ref.shape
     order = [0] + list(range(2, experts))
     picks = jnp.concatenate([picks_ref[i:i + 1, :] for i in order], axis=1)
-    rows = modulate(picks, tok_ref, table_ref)
+    rows = modulate(one_hot(picks, tok_ref.shape[0]), tok_ref, table_ref)
     for i, out in enumerate(outs):
         out[...] = rows[i * slots:(i + 1) * slots]
 
@@ -177,7 +179,7 @@
     hidden = w_ref.shape[0]
     tile = min(1024, hidden)
 
-    @pl.loop(0, hidden // tile)
+    @pl.loop(0, hidden // tile, unroll=True)
     def _(i):
         cut = pl.ds(pl.multiple_of(i * tile, tile), tile)
         lifted = lax.dot_general(

time: 58.2 us -> 57.9 us (level)
  no operation moved by 1% of the time
where the time goes in v21:
time: 57.9 us; the launch traced here: 57.8 us
  starting transfers between devices  23.6 us (41%)
  waiting for transfers between devices  18.5 us (32%)
  Pallas kernels  15.4 us (27%)
    ppermute x22, starting transfers between devices, swap(): return lax.ppermute(x, 'expert', [(i, i ^ mask) for i in range(devices)])  23.6 us
    ppermute x22, waiting for transfers between devices, swap(): return lax.ppermute(x, 'expert', [(i, i ^ mask) for i in range(devices)])  18.5 us
    pallas_call x3, Pallas kernels, down(): pl.pallas_call(functools.partial(down_kernel, columns=columns, low=low),...  5.11 us
    pallas_call x1, Pallas kernels, up(): pl.pallas_call(functools.partial(up_kernel, sources=sources, count=len(pa...  5.03 us
    pallas_call x1, Pallas kernels, first(): pl.pallas_call(first_kernel, in_specs=[SMEM] + [HBM] * 7, out_specs=[VMEM...  2.35 us
    pallas_call x1, Pallas kernels, post(): pl.pallas_call(post_kernel, in_specs=[VMEM] * (3 + len(blocks)), out_spec...  1.21 us
  transfers between devices with their start and end apart: 22, of which 10 were waited for; matrix products, arithmetic and copies ran while one was open for 0% of the time, Pallas kernels for 6%

profile of v21, /device:TPU:0, one launch (start us, length us, event | category | flops | bytes accessed | tf_op | source)
XLA Modules:
  0.0 57.8 jit_solution(15055824063029145999)
XLA Ops:
  0.1 2.4 %first.1 = (bf16[16,4096]{1,0:T(8,128)(2,1)S(1)}, bf16[128,4096]{1,0:T(8,128)(2,1)S(1)}, f32[3,4096]{1,0:T(4,128)S(1)}, s32[4,16]{1,0:T(4,128)S(1)}, f32[4,16]{1,0:T(4,128)S(1)}) custom-call(s32[2]{0:T(128)S(1)} %pad_add_fusion.info_ref, bf16[128,4096]{1,0:T(8,128)(2,1)} %refs_0_.1, s32[4,16]{1,0:T(4,128)} %bitcast.6, f32[2,4096]{1,0:T(2,128)} %refs_2_.1, ...), custom_call_target="tpu_custom_call" | custom-call | flops 1 | bytes 1 | tf_op jit(solution)/shard_map/first/pallas_call | solution.py:80
  2.4 5.1 %collective-permute-start = (bf16[16,4096]{1,0:T(8,128)(2,1)S(1)}, bf16[16,4096]{1,0:T(8,128)(2,1)S(1)}, u32[]{:S(2)}, u32[]{:S(2)}) collective-permute-start(bf16[16,4096]{1,0:T(8,128)(2,1)S(1)} %get-tuple-element.33), channel_id=1, source_target_pairs={{0,12},{1,13},{2,14},{3,15},{4,8},{5,9},{6,10},{7,11},{8,4},{9,5},... | collective-permute-start | bytes 393224 | tf_op jit(solution)/shard_map/ppermute | solution.py:338
  9.0 1.7 %collective-permute-start.1 = (bf16[16,4096]{1,0:T(8,128)(2,1)S(1)}, bf16[16,4096]{1,0:T(8,128)(2,1)S(1)}, u32[]{:S(2)}, u32[]{:S(2)}) collective-permute-start(bf16[16,4096]{1,0:T(8,128)(2,1)S(1)} %get-tuple-element.38.refs_0_), channel_id=1, source_target_pairs={{0,2},{1,3},{2,0},{3,1},{4,6},{5,7},{6,4},{7,5},{8,10},{9,11},{10,... | collective-permute-start | bytes 393224 | tf_op jit(solution)/shard_map/ppermute | solution.py:338
  10.7 1.2 %collective-permute-done.after_ref.refs_0_ = bf16[16,4096]{1,0:T(8,128)(2,1)S(1)} collective-permute-done((bf16[16,4096]{1,0:T(8,128)(2,1)S(1)}, bf16[16,4096]{1,0:T(8,128)(2,1)S(1)}, u32[]{:S(2)}, u32[]{:S(2)}) %collective-permute-start) | collective-permute-done | bytes 131104 | tf_op jit(solution)/shard_map/ppermute | solution.py:338
  11.9 1.8 %collective-permute-start.3 = (bf16[16,4096]{1,0:T(8,128)(2,1)S(1)}, bf16[16,4096]{1,0:T(8,128)(2,1)S(1)}, u32[]{:S(2)}, u32[]{:S(2)}) collective-permute-start(bf16[16,4096]{1,0:T(8,128)(2,1)S(1)} %collective-permute-done.after_ref.refs_0_), channel_id=1, source_target_pairs={{0,2},{1,3},{2,0},{3,1},{4,6},{5,7},{6,4},{7,5},{8,10},{9,11},{10,... | collective-permute-start | bytes 393224 | tf_op jit(solution)/shard_map/ppermute | solution.py:338
  13.9 1.2 %collective-permute-done.8.refs_0_ = bf16[16,4096]{1,0:T(8,128)(2,1)S(1)} collective-permute-done((bf16[16,4096]{1,0:T(8,128)(2,1)S(1)}, bf16[16,4096]{1,0:T(8,128)(2,1)S(1)}, u32[]{:S(2)}, u32[]{:S(2)}) %collective-permute-start.8) | collective-permute-done | bytes 131104 | tf_op jit(solution)/shard_map/ppermute | solution.py:338
  15.0 1.6 %collective-permute-start.9 = (bf16[16,4096]{1,0:T(8,128)(2,1)S(1)}, bf16[16,4096]{1,0:T(8,128)(2,1)S(1)}, u32[]{:S(2)}, u32[]{:S(2)}) collective-permute-start(bf16[16,4096]{1,0:T(8,128)(2,1)S(1)} %collective-permute-done.8.refs_0_), channel_id=1, source_target_pairs={{0,2},{1,3},{2,0},{3,1},{4,6},{5,7},{6,4},{7,5},{8,10},{9,11},{10,... | collective-permute-start | bytes 393224 | tf_op jit(solution)/shard_map/ppermute | solution.py:338
  16.7 2.0 %collective-permute-done.5.refs_0_ = bf16[16,4096]{1,0:T(8,128)(2,1)S(1)} collective-permute-done((bf16[16,4096]{1,0:T(8,128)(2,1)S(1)}, bf16[16,4096]{1,0:T(8,128)(2,1)S(1)}, u32[]{:S(2)}, u32[]{:S(2)}) %collective-permute-start.5) | collective-permute-done | bytes 131104 | tf_op jit(solution)/shard_map/ppermute | solution.py:338
  18.6 1.6 %collective-permute-start.6 = (bf16[16,4096]{1,0:T(8,128)(2,1)S(1)}, bf16[16,4096]{1,0:T(8,128)(2,1)S(1)}, u32[]{:S(2)}, u32[]{:S(2)}) collective-permute-start(bf16[16,4096]{1,0:T(8,128)(2,1)S(1)} %join.8.refs_0_), channel_id=1, source_target_pairs={{0,2},{1,3},{2,0},{3,1},{4,6},{5,7},{6,4},{7,5},{8,10},{9,11},{10,... | collective-permute-start | bytes 393224 | tf_op jit(solution)/shard_map/ppermute | solution.py:338
  21.0 2.6 %collective-permute-done.6.refs_1_ = bf16[16,4096]{1,0:T(8,128)(2,1)S(1)} collective-permute-done((bf16[16,4096]{1,0:T(8,128)(2,1)S(1)}, bf16[16,4096]{1,0:T(8,128)(2,1)S(1)}, u32[]{:S(2)}, u32[]{:S(2)}) %collective-permute-start.6) | collective-permute-done | bytes 131104 | tf_op jit(solution)/shard_map/ppermute | solution.py:338
  23.8 1.5 %collective-permute-done.7.refs_5_ = bf16[32,4096]{1,0:T(8,128)(2,1)S(1)} collective-permute-done((bf16[32,4096]{1,0:T(8,128)(2,1)S(1)}, bf16[32,4096]{1,0:T(8,128)(2,1)S(1)}, u32[]{:S(2)}, u32[]{:S(2)}) %collective-permute-start.7) | collective-permute-done | bytes 262176 | tf_op jit(solution)/shard_map/ppermute | solution.py:338
  25.3 5.0 %up.1.h_ref = bf16[256,2048]{1,0:T(8,128)(2,1)S(1)} custom-call(bf16[32,4096]{1,0:T(8,128)(2,1)S(1)} %join.6.refs_0_, bf16[32,4096]{1,0:T(8,128)(2,1)S(1)} %collective-permute-done.2.refs_1_, bf16[32,4096]{1,0:T(8,128)(2,1)S(1)} %join.7.refs_2_, bf16[32,4096]{1,0:T(8,128)(2,1)S(1)} %collective-permute-done.4.refs_3_, bf16[32,4096]{1,0:T(8,128)(2,1)S(1)} %join.9.refs_4_, ...), custom_call_target="tpu_custom_call" | custom-call | flops 1 | bytes 1 | tf_op jit(solution)/shard_map/up/pallas_call | solution.py:194
  30.4 3.1 %down.3 = (f32[64,2560]{1,0:T(8,128)S(1)}, bf16[64,2560]{1,0:T(8,128)(2,1)S(1)}, f32[64,2560]{1,0:T(8,128)S(1)}, bf16[64,2560]{1,0:T(8,128)(2,1)S(1)}) custom-call(bf16[256,2048]{1,0:T(8,128)(2,1)S(1)} %up.1.h_ref, bf16[2048,4096]{1,0:T(8,128)(2,1)S(1)} %bitcast.5), custom_call_target="tpu_custom_call" | custom-call | flops 1 | bytes 1 | tf_op jit(solution)/shard_map/down/pallas_call | solution.py:226
  34.1 1.0 %down.5 = (f32[64,1536]{1,0:T(8,128)S(1)}, bf16[64,1536]{1,0:T(8,128)(2,1)S(1)}) custom-call(bf16[256,2048]{1,0:T(8,128)(2,1)S(1)} %up.1.h_ref, bf16[2048,4096]{1,0:T(8,128)(2,1)S(1)} %bitcast.5), custom_call_target="tpu_custom_call" | custom-call | flops 1 | bytes 1 | tf_op jit(solution)/shard_map/down/pallas_call | solution.py:226
  36.8 1.6 %collective-permute-start.15 = (bf16[16,4096]{1,0:T(8,128)(2,1)S(1)}, bf16[16,4096]{1,0:T(8,128)(2,1)S(1)}, u32[]{:S(2)}, u32[]{:S(2)}) collective-permute-start(bf16[16,4096]{1,0:T(8,128)(2,1)S(1)} %get-tuple-element.52), channel_id=1, source_target_pairs={{0,2},{1,3},{2,0},{3,1},{4,6},{5,7},{6,4},{7,5},{8,10},{9,11},{10,... | collective-permute-start | bytes 393224 | tf_op jit(solution)/shard_map/ppermute | solution.py:338
  39.5 1.1 %collective-permute-start.18 = (bf16[16,4096]{1,0:T(8,128)(2,1)S(1)}, bf16[16,4096]{1,0:T(8,128)(2,1)S(1)}, u32[]{:S(2)}, u32[]{:S(2)}) collective-permute-start(bf16[16,4096]{1,0:T(8,128)(2,1)S(1)} %get-tuple-element.54), channel_id=1, source_target_pairs={{0,2},{1,3},{2,0},{3,1},{4,6},{5,7},{6,4},{7,5},{8,10},{9,11},{10,... | collective-permute-start | bytes 393224 | tf_op jit(solution)/shard_map/ppermute | solution.py:338
  40.6 2.6 %collective-permute-done.15.refs_1_ = bf16[16,4096]{1,0:T(8,128)(2,1)S(1)} collective-permute-done((bf16[16,4096]{1,0:T(8,128)(2,1)S(1)}, bf16[16,4096]{1,0:T(8,128)(2,1)S(1)}, u32[]{:S(2)}, u32[]{:S(2)}) %collective-permute-start.15) | collective-permute-done | bytes 131104 | tf_op jit(solution)/shard_map/ppermute | solution.py:338
  43.3 2.5 %collective-permute-start.17 = (bf16[16,4096]{1,0:T(8,128)(2,1)S(1)}, bf16[16,4096]{1,0:T(8,128)(2,1)S(1)}, u32[]{:S(2)}, u32[]{:S(2)}) collective-permute-start(bf16[16,4096]{1,0:T(8,128)(2,1)S(1)} %add.11.refs_1_), channel_id=1, source_target_pairs={{0,12},{1,13},{2,14},{3,15},{4,8},{5,9},{6,10},{7,11},{8,4},{9,5},... | collective-permute-start | bytes 393224 | tf_op jit(solution)/shard_map/ppermute | solution.py:338
  45.8 1.6 %collective-permute-start.16 = (bf16[16,4096]{1,0:T(8,128)(2,1)S(1)}, bf16[16,4096]{1,0:T(8,128)(2,1)S(1)}, u32[]{:S(2)}, u32[]{:S(2)}) collective-permute-start(bf16[16,4096]{1,0:T(8,128)(2,1)S(1)} %join.11), channel_id=1, source_target_pairs={{0,2},{1,3},{2,0},{3,1},{4,6},{5,7},{6,4},{7,5},{8,10},{9,11},{10,... | collective-permute-start | bytes 393224 | tf_op jit(solution)/shard_map/ppermute | solution.py:338
  47.5 1.3 %collective-permute-done.18.refs_1_ = bf16[16,4096]{1,0:T(8,128)(2,1)S(1)} collective-permute-done((bf16[16,4096]{1,0:T(8,128)(2,1)S(1)}, bf16[16,4096]{1,0:T(8,128)(2,1)S(1)}, u32[]{:S(2)}, u32[]{:S(2)}) %collective-permute-start.18) | collective-permute-done | bytes 131104 | tf_op jit(solution)/shard_map/ppermute | solution.py:338
  48.9 1.3 %collective-permute-start.19 = (bf16[16,4096]{1,0:T(8,128)(2,1)S(1)}, bf16[16,4096]{1,0:T(8,128)(2,1)S(1)}, u32[]{:S(2)}, u32[]{:S(2)}) collective-permute-start(bf16[16,4096]{1,0:T(8,128)(2,1)S(1)} %add.12), channel_id=1, source_target_pairs={{0,8},{1,9},{2,10},{3,11},{4,12},{5,13},{6,14},{7,15},{8,0},{9,1},... | collective-permute-start | bytes 393224 | tf_op jit(solution)/shard_map/ppermute | solution.py:338
  51.3 2.4 %collective-permute-done.21.refs_1_ = bf16[16,4096]{1,0:T(8,128)(2,1)S(1)} collective-permute-done((bf16[16,4096]{1,0:T(8,128)(2,1)S(1)}, bf16[16,4096]{1,0:T(8,128)(2,1)S(1)}, u32[]{:S(2)}, u32[]{:S(2)}) %collective-permute-start.21) | collective-permute-done | bytes 131104 | tf_op jit(solution)/shard_map/ppermute | solution.py:338
  53.7 2.8 %collective-permute-done.19.refs_0_ = bf16[16,4096]{1,0:T(8,128)(2,1)S(1)} collective-permute-done((bf16[16,4096]{1,0:T(8,128)(2,1)S(1)}, bf16[16,4096]{1,0:T(8,128)(2,1)S(1)}, u32[]{:S(2)}, u32[]{:S(2)}) %collective-permute-start.19) | collective-permute-done | bytes 131104 | tf_op jit(solution)/shard_map/ppermute | solution.py:338
  56.6 1.2 %post.1 = bf16[128,4096]{1,0:T(8,128)(2,1)} custom-call(bf16[128,64]{1,0:T(8,128)(2,1)S(1)} %get-tuple-element.34.mix_ref, f32[3,4096]{1,0:T(4,128)S(1)} %get-tuple-element.35.table_ref, f32[128,4096]{1,0:T(8,128)S(1)} %own_part.1.acc_ref, bf16[16,4096]{1,0:T(8,128)(2,1)S(1)} %collective-permute-done.19.refs_0_, ...), custom_call_target="tpu_custom_call" | custom-call | flops 1 | bytes 1 | tf_op jit(solution)/shard_map/post/pallas_call | solution.py:306
  (52 shorter events, 7.2 us)
Async XLA Ops:
  2.4 9.5 %collective-permute-start = (bf16[16,4096]{1,0:T(8,128)(2,1)S(1)}, bf16[16,4096]{1,0:T(8,128)(2,1)S(1)}, u32[]{:S(2)}, u32[]{:S(2)}) collective-permute-start(bf16[16,4096]{1,0:T(8,128)(2,1)S(1)} %get-tuple-element.33), channel_id=1, source_target_pairs={{0,12},{1,13},{2,14},{3,15},{4,8},{5,9},{6,10},{7,11},{8,4},{9,5},... | collective-permute-start | bytes 393224 | tf_op jit(solution)/shard_map/ppermute | solution.py:338
  7.6 22.8 %slice-start.2 = ((s8[16777216]{0:T(1024)(128)(4,1)}), s8[4194304]{0:T(1024)(128)(4,1)S(1)}, s32[]{:S(2)}) async-start(s8[16777216]{0:T(1024)(128)(4,1)} %bitcast.4), calls=%async_computation.2 | async-start | bytes 8388608
  7.6 22.8 %slice-start.3 = ((s8[16777216]{0:T(1024)(128)(4,1)}), s8[4194304]{0:T(1024)(128)(4,1)S(1)}, s32[]{:S(2)}) async-start(s8[16777216]{0:T(1024)(128)(4,1)} %bitcast.4), calls=%async_computation.3 | async-start | bytes 8388608
  8.3 6.7 %collective-permute-start.8 = (bf16[16,4096]{1,0:T(8,128)(2,1)S(1)}, bf16[16,4096]{1,0:T(8,128)(2,1)S(1)}, u32[]{:S(2)}, u32[]{:S(2)}) collective-permute-start(bf16[16,4096]{1,0:T(8,128)(2,1)S(1)} %get-tuple-element.40), channel_id=1, source_target_pairs={{0,4},{1,5},{2,6},{3,7},{4,0},{5,1},{6,2},{7,3},{8,12},{9,13},{10,... | collective-permute-start | bytes 393224 | tf_op jit(solution)/shard_map/ppermute | solution.py:338
  8.4 10.2 %collective-permute-start.5 = (bf16[16,4096]{1,0:T(8,128)(2,1)S(1)}, bf16[16,4096]{1,0:T(8,128)(2,1)S(1)}, u32[]{:S(2)}, u32[]{:S(2)}) collective-permute-start(bf16[16,4096]{1,0:T(8,128)(2,1)S(1)} %get-tuple-element.39), channel_id=1, source_target_pairs={{0,8},{1,9},{2,10},{3,11},{4,12},{5,13},{6,14},{7,15},{8,0},{9,1},... | collective-permute-start | bytes 393224 | tf_op jit(solution)/shard_map/ppermute | solution.py:338
  9.0 11.2 %collective-permute-start.1 = (bf16[16,4096]{1,0:T(8,128)(2,1)S(1)}, bf16[16,4096]{1,0:T(8,128)(2,1)S(1)}, u32[]{:S(2)}, u32[]{:S(2)}) collective-permute-start(bf16[16,4096]{1,0:T(8,128)(2,1)S(1)} %get-tuple-element.38.refs_0_), channel_id=1, source_target_pairs={{0,2},{1,3},{2,0},{3,1},{4,6},{5,7},{6,4},{7,5},{8,10},{9,11},{10,... | collective-permute-start | bytes 393224 | tf_op jit(solution)/shard_map/ppermute | solution.py:338
  11.9 8.4 %collective-permute-start.3 = (bf16[16,4096]{1,0:T(8,128)(2,1)S(1)}, bf16[16,4096]{1,0:T(8,128)(2,1)S(1)}, u32[]{:S(2)}, u32[]{:S(2)}) collective-permute-start(bf16[16,4096]{1,0:T(8,128)(2,1)S(1)} %collective-permute-done.after_ref.refs_0_), channel_id=1, source_target_pairs={{0,2},{1,3},{2,0},{3,1},{4,6},{5,7},{6,4},{7,5},{8,10},{9,11},{10,... | collective-permute-start | bytes 393224 | tf_op jit(solution)/shard_map/ppermute | solution.py:338
  15.0 5.9 %collective-permute-start.9 = (bf16[16,4096]{1,0:T(8,128)(2,1)S(1)}, bf16[16,4096]{1,0:T(8,128)(2,1)S(1)}, u32[]{:S(2)}, u32[]{:S(2)}) collective-permute-start(bf16[16,4096]{1,0:T(8,128)(2,1)S(1)} %collective-permute-done.8.refs_0_), channel_id=1, source_target_pairs={{0,2},{1,3},{2,0},{3,1},{4,6},{5,7},{6,4},{7,5},{8,10},{9,11},{10,... | collective-permute-start | bytes 393224 | tf_op jit(solution)/shard_map/ppermute | solution.py:338
  18.6 5.0 %collective-permute-start.6 = (bf16[16,4096]{1,0:T(8,128)(2,1)S(1)}, bf16[16,4096]{1,0:T(8,128)(2,1)S(1)}, u32[]{:S(2)}, u32[]{:S(2)}) collective-permute-start(bf16[16,4096]{1,0:T(8,128)(2,1)S(1)} %join.8.refs_0_), channel_id=1, source_target_pairs={{0,2},{1,3},{2,0},{3,1},{4,6},{5,7},{6,4},{7,5},{8,10},{9,11},{10,... | collective-permute-start | bytes 393224 | tf_op jit(solution)/shard_map/ppermute | solution.py:338
  20.3 3.5 %collective-permute-start.2 = (bf16[32,4096]{1,0:T(8,128)(2,1)S(1)}, bf16[32,4096]{1,0:T(8,128)(2,1)S(1)}, u32[]{:S(2)}, u32[]{:S(2)}) collective-permute-start(bf16[32,4096]{1,0:T(8,128)(2,1)S(1)} %join.6.refs_0_), channel_id=1, source_target_pairs={{0,1},{1,0},{2,3},{3,2},{4,5},{5,4},{6,7},{7,6},{8,9},{9,8},{10,11... | collective-permute-start | bytes 786440 | tf_op jit(solution)/shard_map/ppermute | solution.py:338
  20.4 3.4 %collective-permute-start.4 = (bf16[32,4096]{1,0:T(8,128)(2,1)S(1)}, bf16[32,4096]{1,0:T(8,128)(2,1)S(1)}, u32[]{:S(2)}, u32[]{:S(2)}) collective-permute-start(bf16[32,4096]{1,0:T(8,128)(2,1)S(1)} %join.7.refs_2_), channel_id=1, source_target_pairs={{0,1},{1,0},{2,3},{3,2},{4,5},{5,4},{6,7},{7,6},{8,9},{9,8},{10,11... | collective-permute-start | bytes 786440 | tf_op jit(solution)/shard_map/ppermute | solution.py:338
  20.9 2.9 %collective-permute-start.10 = (bf16[32,4096]{1,0:T(8,128)(2,1)S(1)}, bf16[32,4096]{1,0:T(8,128)(2,1)S(1)}, u32[]{:S(2)}, u32[]{:S(2)}) collective-permute-start(bf16[32,4096]{1,0:T(8,128)(2,1)S(1)} %join.10.refs_6_), channel_id=1, source_target_pairs={{0,1},{1,0},{2,3},{3,2},{4,5},{5,4},{6,7},{7,6},{8,9},{9,8},{10,11... | collective-permute-start | bytes 786440 | tf_op jit(solution)/shard_map/ppermute | solution.py:338
  23.7 1.6 %collective-permute-start.7 = (bf16[32,4096]{1,0:T(8,128)(2,1)S(1)}, bf16[32,4096]{1,0:T(8,128)(2,1)S(1)}, u32[]{:S(2)}, u32[]{:S(2)}) collective-permute-start(bf16[32,4096]{1,0:T(8,128)(2,1)S(1)} %join.9.refs_4_), channel_id=1, source_target_pairs={{0,1},{1,0},{2,3},{3,2},{4,5},{5,4},{6,7},{7,6},{8,9},{9,8},{10,11... | collective-permute-start | bytes 786440 | tf_op jit(solution)/shard_map/ppermute | solution.py:338
  33.5 3.2 %collective-permute-start.13 = (bf16[64,2560]{1,0:T(8,128)(2,1)S(1)}, bf16[64,2560]{1,0:T(8,128)(2,1)S(1)}, u32[]{:S(2)}, u32[]{:S(2)}) collective-permute-start(bf16[64,2560]{1,0:T(8,128)(2,1)S(1)} %get-tuple-element.48), channel_id=1, source_target_pairs={{0,1},{1,0},{2,3},{3,2},{4,5},{5,4},{6,7},{7,6},{8,9},{9,8},{10,11... | collective-permute-start | bytes 983048 | tf_op jit(solution)/shard_map/ppermute | solution.py:338
  33.7 4.7 %collective-permute-start.11 = (bf16[64,2560]{1,0:T(8,128)(2,1)S(1)}, bf16[64,2560]{1,0:T(8,128)(2,1)S(1)}, u32[]{:S(2)}, u32[]{:S(2)}) collective-permute-start(bf16[64,2560]{1,0:T(8,128)(2,1)S(1)} %get-tuple-element.42), channel_id=1, source_target_pairs={{0,1},{1,0},{2,3},{3,2},{4,5},{5,4},{6,7},{7,6},{8,9},{9,8},{10,11... | collective-permute-start | bytes 983048 | tf_op jit(solution)/shard_map/ppermute | solution.py:338
  35.1 1.6 %collective-permute-start.14 = (bf16[64,1536]{1,0:T(8,128)(2,1)S(1)}, bf16[64,1536]{1,0:T(8,128)(2,1)S(1)}, u32[]{:S(2)}, u32[]{:S(2)}) collective-permute-start(bf16[64,1536]{1,0:T(8,128)(2,1)S(1)} %get-tuple-element.50), channel_id=1, source_target_pairs={{0,1},{1,0},{2,3},{3,2},{4,5},{5,4},{6,7},{7,6},{8,9},{9,8},{10,11... | collective-permute-start | bytes 589832 | tf_op jit(solution)/shard_map/ppermute | solution.py:338
  36.3 2.1 %collective-permute-start.12 = (bf16[64,1536]{1,0:T(8,128)(2,1)S(1)}, bf16[64,1536]{1,0:T(8,128)(2,1)S(1)}, u32[]{:S(2)}, u32[]{:S(2)}) collective-permute-start(bf16[64,1536]{1,0:T(8,128)(2,1)S(1)} %get-tuple-element.44), channel_id=1, source_target_pairs={{0,1},{1,0},{2,3},{3,2},{4,5},{5,4},{6,7},{7,6},{8,9},{9,8},{10,11... | collective-permute-start | bytes 589832 | tf_op jit(solution)/shard_map/ppermute | solution.py:338
  36.8 6.4 %collective-permute-start.15 = (bf16[16,4096]{1,0:T(8,128)(2,1)S(1)}, bf16[16,4096]{1,0:T(8,128)(2,1)S(1)}, u32[]{:S(2)}, u32[]{:S(2)}) collective-permute-start(bf16[16,4096]{1,0:T(8,128)(2,1)S(1)} %get-tuple-element.52), channel_id=1, source_target_pairs={{0,2},{1,3},{2,0},{3,1},{4,6},{5,7},{6,4},{7,5},{8,10},{9,11},{10,... | collective-permute-start | bytes 393224 | tf_op jit(solution)/shard_map/ppermute | solution.py:338
  38.5 8.9 %collective-permute-start.20 = (bf16[16,4096]{1,0:T(8,128)(2,1)S(1)}, bf16[16,4096]{1,0:T(8,128)(2,1)S(1)}, u32[]{:S(2)}, u32[]{:S(2)}) collective-permute-start(bf16[16,4096]{1,0:T(8,128)(2,1)S(1)} %get-tuple-element.56), channel_id=1, source_target_pairs={{0,2},{1,3},{2,0},{3,1},{4,6},{5,7},{6,4},{7,5},{8,10},{9,11},{10,... | collective-permute-start | bytes 393224 | tf_op jit(solution)/shard_map/ppermute | solution.py:338
  39.5 9.3 %collective-permute-start.18 = (bf16[16,4096]{1,0:T(8,128)(2,1)S(1)}, bf16[16,4096]{1,0:T(8,128)(2,1)S(1)}, u32[]{:S(2)}, u32[]{:S(2)}) collective-permute-start(bf16[16,4096]{1,0:T(8,128)(2,1)S(1)} %get-tuple-element.54), channel_id=1, source_target_pairs={{0,2},{1,3},{2,0},{3,1},{4,6},{5,7},{6,4},{7,5},{8,10},{9,11},{10,... | collective-permute-start | bytes 393224 | tf_op jit(solution)/shard_map/ppermute | solution.py:338
  43.3 7.6 %collective-permute-start.17 = (bf16[16,4096]{1,0:T(8,128)(2,1)S(1)}, bf16[16,4096]{1,0:T(8,128)(2,1)S(1)}, u32[]{:S(2)}, u32[]{:S(2)}) collective-permute-start(bf16[16,4096]{1,0:T(8,128)(2,1)S(1)} %add.11.refs_1_), channel_id=1, source_target_pairs={{0,12},{1,13},{2,14},{3,15},{4,8},{5,9},{6,10},{7,11},{8,4},{9,5},... | collective-permute-start | bytes 393224 | tf_op jit(solution)/shard_map/ppermute | solution.py:338
  45.8 5.0 %collective-permute-start.16 = (bf16[16,4096]{1,0:T(8,128)(2,1)S(1)}, bf16[16,4096]{1,0:T(8,128)(2,1)S(1)}, u32[]{:S(2)}, u32[]{:S(2)}) collective-permute-start(bf16[16,4096]{1,0:T(8,128)(2,1)S(1)} %join.11), channel_id=1, source_target_pairs={{0,2},{1,3},{2,0},{3,1},{4,6},{5,7},{6,4},{7,5},{8,10},{9,11},{10,... | collective-permute-start | bytes 393224 | tf_op jit(solution)/shard_map/ppermute | solution.py:338
  47.4 6.3 %collective-permute-start.21 = (bf16[16,4096]{1,0:T(8,128)(2,1)S(1)}, bf16[16,4096]{1,0:T(8,128)(2,1)S(1)}, u32[]{:S(2)}, u32[]{:S(2)}) collective-permute-start(bf16[16,4096]{1,0:T(8,128)(2,1)S(1)} %add.13), channel_id=1, source_target_pairs={{0,4},{1,5},{2,6},{3,7},{4,0},{5,1},{6,2},{7,3},{8,12},{9,13},{10,... | collective-permute-start | bytes 393224 | tf_op jit(solution)/shard_map/ppermute | solution.py:338
  48.9 7.7 %collective-permute-start.19 = (bf16[16,4096]{1,0:T(8,128)(2,1)S(1)}, bf16[16,4096]{1,0:T(8,128)(2,1)S(1)}, u32[]{:S(2)}, u32[]{:S(2)}) collective-permute-start(bf16[16,4096]{1,0:T(8,128)(2,1)S(1)} %add.12), channel_id=1, source_target_pairs={{0,8},{1,9},{2,10},{3,11},{4,12},{5,13},{6,14},{7,15},{8,0},{9,1},... | collective-permute-start | bytes 393224 | tf_op jit(solution)/shard_map/ppermute | solution.py:338
  (3 other events, 63.3 us)

commit v22 on v21

--- a/solution.py
+++ b/solution.py
@@ -8,6 +8,7 @@
 from jax.sharding import PartitionSpec as P
 
 MIB = 1024 * 1024
+PIECES = 4
 F32 = jnp.float32
 BF16 = jnp.bfloat16
 
@@ -51,13 +52,22 @@
     far_ref, tok_ref, table_ref, picks_ref, weights_ref = refs[7:12]
     pick_ref, comb_ref, count_ref, shift_ref, scale_ref, gate_ref, sems = refs[12:]
     targets = (tok_ref, pick_ref, shift_ref, scale_ref, gate_ref, comb_ref, count_ref)
+    part = tok_ref.shape[0] // PIECES
+    tokens = [
+        pltpu.make_async_copy(
+            sources[0].at[pl.ds(p * part, part), :],
+            tok_ref.at[pl.ds(p * part, part), :],
+            sems.at[len(sources) + p],
+        )
+        for p in range(PIECES)
+    ]
     copies = [
         pltpu.make_async_copy(src, dst, sems.at[i])
         for i, (src, dst) in enumerate(zip(sources, targets))
-    ]
+    ][1:]
+    for copy in tokens + copies:
+        copy.start()
     for copy in copies:
-        copy.start()
-    for copy in copies[1:]:
         copy.wait()
     experts, slots = pick_ref.shape
     which = pl.ds(info_ref[0], 1)
@@ -70,7 +80,8 @@
         picks_ref[i:i + 1, :] = pick_ref[pl.ds(e, 1), :]
         weights_ref[i:i + 1, :] = jnp.where(lanes < count_ref[0, e], comb_ref[pl.ds(e, 1), :], 0.0)
     hot = one_hot(picks_ref[1:2, :], tok_ref.shape[0])
-    copies[0].wait()
+    for copy in tokens:
+        copy.wait()
     far_ref[...] = modulate(hot, tok_ref, table_ref)
 
 
@@ -95,7 +106,7 @@
             pltpu.VMEM(shift.shape, F32),
             pltpu.VMEM(scale.shape, F32),
             pltpu.VMEM(gate.shape, F32),
-            pltpu.SemaphoreType.DMA((7,)),
+            pltpu.SemaphoreType.DMA((7 + PIECES,)),
         ],
         compiler_params=params(8),
         cost_estimate=FREE,

time: 57.9 us -> 57.9 us (level)
  no operation moved by 1% of the time
where the time goes in v22:
time: 57.9 us; the launch traced here: 57.8 us
  starting transfers between devices  23.6 us (41%)
  waiting for transfers between devices  18.5 us (32%)
  Pallas kernels  15.4 us (27%)
    ppermute x22, starting transfers between devices, swap(): return lax.ppermute(x, 'expert', [(i, i ^ mask) for i in range(devices)])  23.6 us
    ppermute x22, waiting for transfers between devices, swap(): return lax.ppermute(x, 'expert', [(i, i ^ mask) for i in range(devices)])  18.5 us
    pallas_call x3, Pallas kernels, down(): pl.pallas_call(functools.partial(down_kernel, columns=columns, low=low),...  5.11 us
    pallas_call x1, Pallas kernels, up(): pl.pallas_call(functools.partial(up_kernel, sources=sources, count=len(pa...  5.03 us
    pallas_call x1, Pallas kernels, first(): pl.pallas_call(first_kernel, in_specs=[SMEM] + [HBM] * 7, out_specs=[VMEM...  2.35 us
    pallas_call x1, Pallas kernels, post(): pl.pallas_call(post_kernel, in_specs=[VMEM] * (3 + len(blocks)), out_spec...  1.21 us
  transfers between devices with their start and end apart: 22, of which 10 were waited for; matrix products, arithmetic and copies ran while one was open for 0% of the time, Pallas kernels for 6%

profile of v22, /device:TPU:0, one launch (start us, length us, event | category | flops | bytes accessed | tf_op | source)
XLA Modules:
  0.0 57.8 jit_solution(15929429703340731924)
XLA Ops:
  0.1 2.4 %first.1 = (bf16[16,4096]{1,0:T(8,128)(2,1)S(1)}, bf16[128,4096]{1,0:T(8,128)(2,1)S(1)}, f32[3,4096]{1,0:T(4,128)S(1)}, s32[4,16]{1,0:T(4,128)S(1)}, f32[4,16]{1,0:T(4,128)S(1)}) custom-call(s32[2]{0:T(128)S(1)} %pad_add_fusion.info_ref, bf16[128,4096]{1,0:T(8,128)(2,1)} %refs_0_.1, s32[4,16]{1,0:T(4,128)} %bitcast.6, f32[2,4096]{1,0:T(2,128)} %refs_2_.1, ...), custom_call_target="tpu_custom_call" | custom-call | flops 1 | bytes 1 | tf_op jit(solution)/shard_map/first/pallas_call | solution.py:91
  2.4 5.1 %collective-permute-start = (bf16[16,4096]{1,0:T(8,128)(2,1)S(1)}, bf16[16,4096]{1,0:T(8,128)(2,1)S(1)}, u32[]{:S(2)}, u32[]{:S(2)}) collective-permute-start(bf16[16,4096]{1,0:T(8,128)(2,1)S(1)} %get-tuple-element.33), channel_id=1, source_target_pairs={{0,12},{1,13},{2,14},{3,15},{4,8},{5,9},{6,10},{7,11},{8,4},{9,5},... | collective-permute-start | bytes 393224 | tf_op jit(solution)/shard_map/ppermute | solution.py:349
  9.0 1.7 %collective-permute-start.1 = (bf16[16,4096]{1,0:T(8,128)(2,1)S(1)}, bf16[16,4096]{1,0:T(8,128)(2,1)S(1)}, u32[]{:S(2)}, u32[]{:S(2)}) collective-permute-start(bf16[16,4096]{1,0:T(8,128)(2,1)S(1)} %get-tuple-element.38.refs_0_), channel_id=1, source_target_pairs={{0,2},{1,3},{2,0},{3,1},{4,6},{5,7},{6,4},{7,5},{8,10},{9,11},{10,... | collective-permute-start | bytes 393224 | tf_op jit(solution)/shard_map/ppermute | solution.py:349
  10.7 1.2 %collective-permute-done.after_ref.refs_0_ = bf16[16,4096]{1,0:T(8,128)(2,1)S(1)} collective-permute-done((bf16[16,4096]{1,0:T(8,128)(2,1)S(1)}, bf16[16,4096]{1,0:T(8,128)(2,1)S(1)}, u32[]{:S(2)}, u32[]{:S(2)}) %collective-permute-start) | collective-permute-done | bytes 131104 | tf_op jit(solution)/shard_map/ppermute | solution.py:349
  11.9 1.8 %collective-permute-start.3 = (bf16[16,4096]{1,0:T(8,128)(2,1)S(1)}, bf16[16,4096]{1,0:T(8,128)(2,1)S(1)}, u32[]{:S(2)}, u32[]{:S(2)}) collective-permute-start(bf16[16,4096]{1,0:T(8,128)(2,1)S(1)} %collective-permute-done.after_ref.refs_0_), channel_id=1, source_target_pairs={{0,2},{1,3},{2,0},{3,1},{4,6},{5,7},{6,4},{7,5},{8,10},{9,11},{10,... | collective-permute-start | bytes 393224 | tf_op jit(solution)/shard_map/ppermute | solution.py:349
  13.9 1.2 %collective-permute-done.8.refs_0_ = bf16[16,4096]{1,0:T(8,128)(2,1)S(1)} collective-permute-done((bf16[16,4096]{1,0:T(8,128)(2,1)S(1)}, bf16[16,4096]{1,0:T(8,128)(2,1)S(1)}, u32[]{:S(2)}, u32[]{:S(2)}) %collective-permute-start.8) | collective-permute-done | bytes 131104 | tf_op jit(solution)/shard_map/ppermute | solution.py:349
  15.0 1.6 %collective-permute-start.9 = (bf16[16,4096]{1,0:T(8,128)(2,1)S(1)}, bf16[16,4096]{1,0:T(8,128)(2,1)S(1)}, u32[]{:S(2)}, u32[]{:S(2)}) collective-permute-start(bf16[16,4096]{1,0:T(8,128)(2,1)S(1)} %collective-permute-done.8.refs_0_), channel_id=1, source_target_pairs={{0,2},{1,3},{2,0},{3,1},{4,6},{5,7},{6,4},{7,5},{8,10},{9,11},{10,... | collective-permute-start | bytes 393224 | tf_op jit(solution)/shard_map/ppermute | solution.py:349
  16.7 2.0 %collective-permute-done.5.refs_0_ = bf16[16,4096]{1,0:T(8,128)(2,1)S(1)} collective-permute-done((bf16[16,4096]{1,0:T(8,128)(2,1)S(1)}, bf16[16,4096]{1,0:T(8,128)(2,1)S(1)}, u32[]{:S(2)}, u32[]{:S(2)}) %collective-permute-start.5) | collective-permute-done | bytes 131104 | tf_op jit(solution)/shard_map/ppermute | solution.py:349
  18.6 1.6 %collective-permute-start.6 = (bf16[16,4096]{1,0:T(8,128)(2,1)S(1)}, bf16[16,4096]{1,0:T(8,128)(2,1)S(1)}, u32[]{:S(2)}, u32[]{:S(2)}) collective-permute-start(bf16[16,4096]{1,0:T(8,128)(2,1)S(1)} %join.8.refs_0_), channel_id=1, source_target_pairs={{0,2},{1,3},{2,0},{3,1},{4,6},{5,7},{6,4},{7,5},{8,10},{9,11},{10,... | collective-permute-start | bytes 393224 | tf_op jit(solution)/shard_map/ppermute | solution.py:349
  21.0 2.6 %collective-permute-done.6.refs_1_ = bf16[16,4096]{1,0:T(8,128)(2,1)S(1)} collective-permute-done((bf16[16,4096]{1,0:T(8,128)(2,1)S(1)}, bf16[16,4096]{1,0:T(8,128)(2,1)S(1)}, u32[]{:S(2)}, u32[]{:S(2)}) %collective-permute-start.6) | collective-permute-done | bytes 131104 | tf_op jit(solution)/shard_map/ppermute | solution.py:349
  23.8 1.5 %collective-permute-done.7.refs_5_ = bf16[32,4096]{1,0:T(8,128)(2,1)S(1)} collective-permute-done((bf16[32,4096]{1,0:T(8,128)(2,1)S(1)}, bf16[32,4096]{1,0:T(8,128)(2,1)S(1)}, u32[]{:S(2)}, u32[]{:S(2)}) %collective-permute-start.7) | collective-permute-done | bytes 262176 | tf_op jit(solution)/shard_map/ppermute | solution.py:349
  25.3 5.0 %up.1.h_ref = bf16[256,2048]{1,0:T(8,128)(2,1)S(1)} custom-call(bf16[32,4096]{1,0:T(8,128)(2,1)S(1)} %join.6.refs_0_, bf16[32,4096]{1,0:T(8,128)(2,1)S(1)} %collective-permute-done.2.refs_1_, bf16[32,4096]{1,0:T(8,128)(2,1)S(1)} %join.7.refs_2_, bf16[32,4096]{1,0:T(8,128)(2,1)S(1)} %collective-permute-done.4.refs_3_, bf16[32,4096]{1,0:T(8,128)(2,1)S(1)} %join.9.refs_4_, ...), custom_call_target="tpu_custom_call" | custom-call | flops 1 | bytes 1 | tf_op jit(solution)/shard_map/up/pallas_call | solution.py:205
  30.4 3.1 %down.3 = (f32[64,2560]{1,0:T(8,128)S(1)}, bf16[64,2560]{1,0:T(8,128)(2,1)S(1)}, f32[64,2560]{1,0:T(8,128)S(1)}, bf16[64,2560]{1,0:T(8,128)(2,1)S(1)}) custom-call(bf16[256,2048]{1,0:T(8,128)(2,1)S(1)} %up.1.h_ref, bf16[2048,4096]{1,0:T(8,128)(2,1)S(1)} %bitcast.5), custom_call_target="tpu_custom_call" | custom-call | flops 1 | bytes 1 | tf_op jit(solution)/shard_map/down/pallas_call | solution.py:237
  36.8 1.6 %collective-permute-start.15 = (bf16[16,4096]{1,0:T(8,128)(2,1)S(1)}, bf16[16,4096]{1,0:T(8,128)(2,1)S(1)}, u32[]{:S(2)}, u32[]{:S(2)}) collective-permute-start(bf16[16,4096]{1,0:T(8,128)(2,1)S(1)} %get-tuple-element.52), channel_id=1, source_target_pairs={{0,2},{1,3},{2,0},{3,1},{4,6},{5,7},{6,4},{7,5},{8,10},{9,11},{10,... | collective-permute-start | bytes 393224 | tf_op jit(solution)/shard_map/ppermute | solution.py:349
  38.5 1.0 %collective-permute-start.20 = (bf16[16,4096]{1,0:T(8,128)(2,1)S(1)}, bf16[16,4096]{1,0:T(8,128)(2,1)S(1)}, u32[]{:S(2)}, u32[]{:S(2)}) collective-permute-start(bf16[16,4096]{1,0:T(8,128)(2,1)S(1)} %get-tuple-element.56), channel_id=1, source_target_pairs={{0,2},{1,3},{2,0},{3,1},{4,6},{5,7},{6,4},{7,5},{8,10},{9,11},{10,... | collective-permute-start | bytes 393224 | tf_op jit(solution)/shard_map/ppermute | solution.py:349
  39.5 1.1 %collective-permute-start.18 = (bf16[16,4096]{1,0:T(8,128)(2,1)S(1)}, bf16[16,4096]{1,0:T(8,128)(2,1)S(1)}, u32[]{:S(2)}, u32[]{:S(2)}) collective-permute-start(bf16[16,4096]{1,0:T(8,128)(2,1)S(1)} %get-tuple-element.54), channel_id=1, source_target_pairs={{0,2},{1,3},{2,0},{3,1},{4,6},{5,7},{6,4},{7,5},{8,10},{9,11},{10,... | collective-permute-start | bytes 393224 | tf_op jit(solution)/shard_map/ppermute | solution.py:349
  40.6 2.6 %collective-permute-done.15.refs_1_ = bf16[16,4096]{1,0:T(8,128)(2,1)S(1)} collective-permute-done((bf16[16,4096]{1,0:T(8,128)(2,1)S(1)}, bf16[16,4096]{1,0:T(8,128)(2,1)S(1)}, u32[]{:S(2)}, u32[]{:S(2)}) %collective-permute-start.15) | collective-permute-done | bytes 131104 | tf_op jit(solution)/shard_map/ppermute | solution.py:349
  43.3 2.6 %collective-permute-start.17 = (bf16[16,4096]{1,0:T(8,128)(2,1)S(1)}, bf16[16,4096]{1,0:T(8,128)(2,1)S(1)}, u32[]{:S(2)}, u32[]{:S(2)}) collective-permute-start(bf16[16,4096]{1,0:T(8,128)(2,1)S(1)} %add.11.refs_1_), channel_id=1, source_target_pairs={{0,12},{1,13},{2,14},{3,15},{4,8},{5,9},{6,10},{7,11},{8,4},{9,5},... | collective-permute-start | bytes 393224 | tf_op jit(solution)/shard_map/ppermute | solution.py:349
  45.8 1.6 %collective-permute-start.16 = (bf16[16,4096]{1,0:T(8,128)(2,1)S(1)}, bf16[16,4096]{1,0:T(8,128)(2,1)S(1)}, u32[]{:S(2)}, u32[]{:S(2)}) collective-permute-start(bf16[16,4096]{1,0:T(8,128)(2,1)S(1)} %join.11), channel_id=1, source_target_pairs={{0,2},{1,3},{2,0},{3,1},{4,6},{5,7},{6,4},{7,5},{8,10},{9,11},{10,... | collective-permute-start | bytes 393224 | tf_op jit(solution)/shard_map/ppermute | solution.py:349
  47.5 1.3 %collective-permute-done.18.refs_1_ = bf16[16,4096]{1,0:T(8,128)(2,1)S(1)} collective-permute-done((bf16[16,4096]{1,0:T(8,128)(2,1)S(1)}, bf16[16,4096]{1,0:T(8,128)(2,1)S(1)}, u32[]{:S(2)}, u32[]{:S(2)}) %collective-permute-start.18) | collective-permute-done | bytes 131104 | tf_op jit(solution)/shard_map/ppermute | solution.py:349
  48.9 1.3 %collective-permute-start.19 = (bf16[16,4096]{1,0:T(8,128)(2,1)S(1)}, bf16[16,4096]{1,0:T(8,128)(2,1)S(1)}, u32[]{:S(2)}, u32[]{:S(2)}) collective-permute-start(bf16[16,4096]{1,0:T(8,128)(2,1)S(1)} %add.12), channel_id=1, source_target_pairs={{0,8},{1,9},{2,10},{3,11},{4,12},{5,13},{6,14},{7,15},{8,0},{9,1},... | collective-permute-start | bytes 393224 | tf_op jit(solution)/shard_map/ppermute | solution.py:349
  51.3 2.4 %collective-permute-done.21.refs_1_ = bf16[16,4096]{1,0:T(8,128)(2,1)S(1)} collective-permute-done((bf16[16,4096]{1,0:T(8,128)(2,1)S(1)}, bf16[16,4096]{1,0:T(8,128)(2,1)S(1)}, u32[]{:S(2)}, u32[]{:S(2)}) %collective-permute-start.21) | collective-permute-done | bytes 131104 | tf_op jit(solution)/shard_map/ppermute | solution.py:349
  53.7 2.9 %collective-permute-done.19.refs_0_ = bf16[16,4096]{1,0:T(8,128)(2,1)S(1)} collective-permute-done((bf16[16,4096]{1,0:T(8,128)(2,1)S(1)}, bf16[16,4096]{1,0:T(8,128)(2,1)S(1)}, u32[]{:S(2)}, u32[]{:S(2)}) %collective-permute-start.19) | collective-permute-done | bytes 131104 | tf_op jit(solution)/shard_map/ppermute | solution.py:349
  56.6 1.2 %post.1 = bf16[128,4096]{1,0:T(8,128)(2,1)} custom-call(bf16[128,64]{1,0:T(8,128)(2,1)S(1)} %get-tuple-element.34.mix_ref, f32[3,4096]{1,0:T(4,128)S(1)} %get-tuple-element.35.table_ref, f32[128,4096]{1,0:T(8,128)S(1)} %own_part.1.acc_ref, bf16[16,4096]{1,0:T(8,128)(2,1)S(1)} %collective-permute-done.19.refs_0_, ...), custom_call_target="tpu_custom_call" | custom-call | flops 1 | bytes 1 | tf_op jit(solution)/shard_map/post/pallas_call | solution.py:317
  (52 shorter events, 7.2 us)
Async XLA Ops:
  2.4 9.5 %collective-permute-start = (bf16[16,4096]{1,0:T(8,128)(2,1)S(1)}, bf16[16,4096]{1,0:T(8,128)(2,1)S(1)}, u32[]{:S(2)}, u32[]{:S(2)}) collective-permute-start(bf16[16,4096]{1,0:T(8,128)(2,1)S(1)} %get-tuple-element.33), channel_id=1, source_target_pairs={{0,12},{1,13},{2,14},{3,15},{4,8},{5,9},{6,10},{7,11},{8,4},{9,5},... | collective-permute-start | bytes 393224 | tf_op jit(solution)/shard_map/ppermute | solution.py:349
  7.6 22.8 %slice-start.2 = ((s8[16777216]{0:T(1024)(128)(4,1)}), s8[4194304]{0:T(1024)(128)(4,1)S(1)}, s32[]{:S(2)}) async-start(s8[16777216]{0:T(1024)(128)(4,1)} %bitcast.4), calls=%async_computation.2 | async-start | bytes 8388608
  7.6 22.8 %slice-start.3 = ((s8[16777216]{0:T(1024)(128)(4,1)}), s8[4194304]{0:T(1024)(128)(4,1)S(1)}, s32[]{:S(2)}) async-start(s8[16777216]{0:T(1024)(128)(4,1)} %bitcast.4), calls=%async_computation.3 | async-start | bytes 8388608
  8.3 6.7 %collective-permute-start.8 = (bf16[16,4096]{1,0:T(8,128)(2,1)S(1)}, bf16[16,4096]{1,0:T(8,128)(2,1)S(1)}, u32[]{:S(2)}, u32[]{:S(2)}) collective-permute-start(bf16[16,4096]{1,0:T(8,128)(2,1)S(1)} %get-tuple-element.40), channel_id=1, source_target_pairs={{0,4},{1,5},{2,6},{3,7},{4,0},{5,1},{6,2},{7,3},{8,12},{9,13},{10,... | collective-permute-start | bytes 393224 | tf_op jit(solution)/shard_map/ppermute | solution.py:349
  8.4 10.2 %collective-permute-start.5 = (bf16[16,4096]{1,0:T(8,128)(2,1)S(1)}, bf16[16,4096]{1,0:T(8,128)(2,1)S(1)}, u32[]{:S(2)}, u32[]{:S(2)}) collective-permute-start(bf16[16,4096]{1,0:T(8,128)(2,1)S(1)} %get-tuple-element.39), channel_id=1, source_target_pairs={{0,8},{1,9},{2,10},{3,11},{4,12},{5,13},{6,14},{7,15},{8,0},{9,1},... | collective-permute-start | bytes 393224 | tf_op jit(solution)/shard_map/ppermute | solution.py:349
  9.0 11.2 %collective-permute-start.1 = (bf16[16,4096]{1,0:T(8,128)(2,1)S(1)}, bf16[16,4096]{1,0:T(8,128)(2,1)S(1)}, u32[]{:S(2)}, u32[]{:S(2)}) collective-permute-start(bf16[16,4096]{1,0:T(8,128)(2,1)S(1)} %get-tuple-element.38.refs_0_), channel_id=1, source_target_pairs={{0,2},{1,3},{2,0},{3,1},{4,6},{5,7},{6,4},{7,5},{8,10},{9,11},{10,... | collective-permute-start | bytes 393224 | tf_op jit(solution)/shard_map/ppermute | solution.py:349
  11.9 8.4 %collective-permute-start.3 = (bf16[16,4096]{1,0:T(8,128)(2,1)S(1)}, bf16[16,4096]{1,0:T(8,128)(2,1)S(1)}, u32[]{:S(2)}, u32[]{:S(2)}) collective-permute-start(bf16[16,4096]{1,0:T(8,128)(2,1)S(1)} %collective-permute-done.after_ref.refs_0_), channel_id=1, source_target_pairs={{0,2},{1,3},{2,0},{3,1},{4,6},{5,7},{6,4},{7,5},{8,10},{9,11},{10,... | collective-permute-start | bytes 393224 | tf_op jit(solution)/shard_map/ppermute | solution.py:349
  15.0 5.9 %collective-permute-start.9 = (bf16[16,4096]{1,0:T(8,128)(2,1)S(1)}, bf16[16,4096]{1,0:T(8,128)(2,1)S(1)}, u32[]{:S(2)}, u32[]{:S(2)}) collective-permute-start(bf16[16,4096]{1,0:T(8,128)(2,1)S(1)} %collective-permute-done.8.refs_0_), channel_id=1, source_target_pairs={{0,2},{1,3},{2,0},{3,1},{4,6},{5,7},{6,4},{7,5},{8,10},{9,11},{10,... | collective-permute-start | bytes 393224 | tf_op jit(solution)/shard_map/ppermute | solution.py:349
  18.6 5.0 %collective-permute-start.6 = (bf16[16,4096]{1,0:T(8,128)(2,1)S(1)}, bf16[16,4096]{1,0:T(8,128)(2,1)S(1)}, u32[]{:S(2)}, u32[]{:S(2)}) collective-permute-start(bf16[16,4096]{1,0:T(8,128)(2,1)S(1)} %join.8.refs_0_), channel_id=1, source_target_pairs={{0,2},{1,3},{2,0},{3,1},{4,6},{5,7},{6,4},{7,5},{8,10},{9,11},{10,... | collective-permute-start | bytes 393224 | tf_op jit(solution)/shard_map/ppermute | solution.py:349
  20.2 3.5 %collective-permute-start.2 = (bf16[32,4096]{1,0:T(8,128)(2,1)S(1)}, bf16[32,4096]{1,0:T(8,128)(2,1)S(1)}, u32[]{:S(2)}, u32[]{:S(2)}) collective-permute-start(bf16[32,4096]{1,0:T(8,128)(2,1)S(1)} %join.6.refs_0_), channel_id=1, source_target_pairs={{0,1},{1,0},{2,3},{3,2},{4,5},{5,4},{6,7},{7,6},{8,9},{9,8},{10,11... | collective-permute-start | bytes 786440 | tf_op jit(solution)/shard_map/ppermute | solution.py:349
  20.4 3.4 %collective-permute-start.4 = (bf16[32,4096]{1,0:T(8,128)(2,1)S(1)}, bf16[32,4096]{1,0:T(8,128)(2,1)S(1)}, u32[]{:S(2)}, u32[]{:S(2)}) collective-permute-start(bf16[32,4096]{1,0:T(8,128)(2,1)S(1)} %join.7.refs_2_), channel_id=1, source_target_pairs={{0,1},{1,0},{2,3},{3,2},{4,5},{5,4},{6,7},{7,6},{8,9},{9,8},{10,11... | collective-permute-start | bytes 786440 | tf_op jit(solution)/shard_map/ppermute | solution.py:349
  20.9 2.9 %collective-permute-start.10 = (bf16[32,4096]{1,0:T(8,128)(2,1)S(1)}, bf16[32,4096]{1,0:T(8,128)(2,1)S(1)}, u32[]{:S(2)}, u32[]{:S(2)}) collective-permute-start(bf16[32,4096]{1,0:T(8,128)(2,1)S(1)} %join.10.refs_6_), channel_id=1, source_target_pairs={{0,1},{1,0},{2,3},{3,2},{4,5},{5,4},{6,7},{7,6},{8,9},{9,8},{10,11... | collective-permute-start | bytes 786440 | tf_op jit(solution)/shard_map/ppermute | solution.py:349
  23.7 1.6 %collective-permute-start.7 = (bf16[32,4096]{1,0:T(8,128)(2,1)S(1)}, bf16[32,4096]{1,0:T(8,128)(2,1)S(1)}, u32[]{:S(2)}, u32[]{:S(2)}) collective-permute-start(bf16[32,4096]{1,0:T(8,128)(2,1)S(1)} %join.9.refs_4_), channel_id=1, source_target_pairs={{0,1},{1,0},{2,3},{3,2},{4,5},{5,4},{6,7},{7,6},{8,9},{9,8},{10,11... | collective-permute-start | bytes 786440 | tf_op jit(solution)/shard_map/ppermute | solution.py:349
  33.5 3.2 %collective-permute-start.13 = (bf16[64,2560]{1,0:T(8,128)(2,1)S(1)}, bf16[64,2560]{1,0:T(8,128)(2,1)S(1)}, u32[]{:S(2)}, u32[]{:S(2)}) collective-permute-start(bf16[64,2560]{1,0:T(8,128)(2,1)S(1)} %get-tuple-element.48), channel_id=1, source_target_pairs={{0,1},{1,0},{2,3},{3,2},{4,5},{5,4},{6,7},{7,6},{8,9},{9,8},{10,11... | collective-permute-start | bytes 983048 | tf_op jit(solution)/shard_map/ppermute | solution.py:349
  33.7 4.7 %collective-permute-start.11 = (bf16[64,2560]{1,0:T(8,128)(2,1)S(1)}, bf16[64,2560]{1,0:T(8,128)(2,1)S(1)}, u32[]{:S(2)}, u32[]{:S(2)}) collective-permute-start(bf16[64,2560]{1,0:T(8,128)(2,1)S(1)} %get-tuple-element.42), channel_id=1, source_target_pairs={{0,1},{1,0},{2,3},{3,2},{4,5},{5,4},{6,7},{7,6},{8,9},{9,8},{10,11... | collective-permute-start | bytes 983048 | tf_op jit(solution)/shard_map/ppermute | solution.py:349
  35.1 1.6 %collective-permute-start.14 = (bf16[64,1536]{1,0:T(8,128)(2,1)S(1)}, bf16[64,1536]{1,0:T(8,128)(2,1)S(1)}, u32[]{:S(2)}, u32[]{:S(2)}) collective-permute-start(bf16[64,1536]{1,0:T(8,128)(2,1)S(1)} %get-tuple-element.50), channel_id=1, source_target_pairs={{0,1},{1,0},{2,3},{3,2},{4,5},{5,4},{6,7},{7,6},{8,9},{9,8},{10,11... | collective-permute-start | bytes 589832 | tf_op jit(solution)/shard_map/ppermute | solution.py:349
  36.3 2.1 %collective-permute-start.12 = (bf16[64,1536]{1,0:T(8,128)(2,1)S(1)}, bf16[64,1536]{1,0:T(8,128)(2,1)S(1)}, u32[]{:S(2)}, u32[]{:S(2)}) collective-permute-start(bf16[64,1536]{1,0:T(8,128)(2,1)S(1)} %get-tuple-element.44), channel_id=1, source_target_pairs={{0,1},{1,0},{2,3},{3,2},{4,5},{5,4},{6,7},{7,6},{8,9},{9,8},{10,11... | collective-permute-start | bytes 589832 | tf_op jit(solution)/shard_map/ppermute | solution.py:349
  36.8 6.4 %collective-permute-start.15 = (bf16[16,4096]{1,0:T(8,128)(2,1)S(1)}, bf16[16,4096]{1,0:T(8,128)(2,1)S(1)}, u32[]{:S(2)}, u32[]{:S(2)}) collective-permute-start(bf16[16,4096]{1,0:T(8,128)(2,1)S(1)} %get-tuple-element.52), channel_id=1, source_target_pairs={{0,2},{1,3},{2,0},{3,1},{4,6},{5,7},{6,4},{7,5},{8,10},{9,11},{10,... | collective-permute-start | bytes 393224 | tf_op jit(solution)/shard_map/ppermute | solution.py:349
  38.5 8.9 %collective-permute-start.20 = (bf16[16,4096]{1,0:T(8,128)(2,1)S(1)}, bf16[16,4096]{1,0:T(8,128)(2,1)S(1)}, u32[]{:S(2)}, u32[]{:S(2)}) collective-permute-start(bf16[16,4096]{1,0:T(8,128)(2,1)S(1)} %get-tuple-element.56), channel_id=1, source_target_pairs={{0,2},{1,3},{2,0},{3,1},{4,6},{5,7},{6,4},{7,5},{8,10},{9,11},{10,... | collective-permute-start | bytes 393224 | tf_op jit(solution)/shard_map/ppermute | solution.py:349
  39.5 9.4 %collective-permute-start.18 = (bf16[16,4096]{1,0:T(8,128)(2,1)S(1)}, bf16[16,4096]{1,0:T(8,128)(2,1)S(1)}, u32[]{:S(2)}, u32[]{:S(2)}) collective-permute-start(bf16[16,4096]{1,0:T(8,128)(2,1)S(1)} %get-tuple-element.54), channel_id=1, source_target_pairs={{0,2},{1,3},{2,0},{3,1},{4,6},{5,7},{6,4},{7,5},{8,10},{9,11},{10,... | collective-permute-start | bytes 393224 | tf_op jit(solution)/shard_map/ppermute | solution.py:349
  43.3 7.6 %collective-permute-start.17 = (bf16[16,4096]{1,0:T(8,128)(2,1)S(1)}, bf16[16,4096]{1,0:T(8,128)(2,1)S(1)}, u32[]{:S(2)}, u32[]{:S(2)}) collective-permute-start(bf16[16,4096]{1,0:T(8,128)(2,1)S(1)} %add.11.refs_1_), channel_id=1, source_target_pairs={{0,12},{1,13},{2,14},{3,15},{4,8},{5,9},{6,10},{7,11},{8,4},{9,5},... | collective-permute-start | bytes 393224 | tf_op jit(solution)/shard_map/ppermute | solution.py:349
  45.8 5.0 %collective-permute-start.16 = (bf16[16,4096]{1,0:T(8,128)(2,1)S(1)}, bf16[16,4096]{1,0:T(8,128)(2,1)S(1)}, u32[]{:S(2)}, u32[]{:S(2)}) collective-permute-start(bf16[16,4096]{1,0:T(8,128)(2,1)S(1)} %join.11), channel_id=1, source_target_pairs={{0,2},{1,3},{2,0},{3,1},{4,6},{5,7},{6,4},{7,5},{8,10},{9,11},{10,... | collective-permute-start | bytes 393224 | tf_op jit(solution)/shard_map/ppermute | solution.py:349
  47.4 6.3 %collective-permute-start.21 = (bf16[16,4096]{1,0:T(8,128)(2,1)S(1)}, bf16[16,4096]{1,0:T(8,128)(2,1)S(1)}, u32[]{:S(2)}, u32[]{:S(2)}) collective-permute-start(bf16[16,4096]{1,0:T(8,128)(2,1)S(1)} %add.13), channel_id=1, source_target_pairs={{0,4},{1,5},{2,6},{3,7},{4,0},{5,1},{6,2},{7,3},{8,12},{9,13},{10,... | collective-permute-start | bytes 393224 | tf_op jit(solution)/shard_map/ppermute | solution.py:349
  48.9 7.7 %collective-permute-start.19 = (bf16[16,4096]{1,0:T(8,128)(2,1)S(1)}, bf16[16,4096]{1,0:T(8,128)(2,1)S(1)}, u32[]{:S(2)}, u32[]{:S(2)}) collective-permute-start(bf16[16,4096]{1,0:T(8,128)(2,1)S(1)} %add.12), channel_id=1, source_target_pairs={{0,8},{1,9},{2,10},{3,11},{4,12},{5,13},{6,14},{7,15},{8,0},{9,1},... | collective-permute-start | bytes 393224 | tf_op jit(solution)/shard_map/ppermute | solution.py:349
  (3 other events, 63.3 us)

commit v23 on v22

--- a/solution.py
+++ b/solution.py
@@ -214,10 +214,10 @@
     )(*parts, w, *after)
 
 
-def down_kernel(h_ref, w_ref, *outs, columns, low):
+def down_kernel(h_ref, w_ref, *outs, columns, low, groups):
     first, last, tile = columns
-    groups = len(outs) // 2
-    half = outs[0].shape[0]
+    pairs = len(outs) // 2
+    half = outs[0].shape[0] * pairs // groups
 
     @pl.loop(0, (last - first) // tile)
     def _(i):
@@ -227,22 +227,25 @@
         out = jnp.dot(h_ref[rows, :], w_ref[:, cut], preferred_element_type=F32)
         for g in range(groups):
             at = 2 * half * g
-            outs[2 * g][:, to] = out[at:at + half]
-            outs[2 * g + 1][:, to] = out[at + half:at + 2 * half].astype(BF16)
-
-
-def down(hid, low, groups, w, columns):
-    half = hid.shape[0] // 4
+            keep_ref, send_ref = outs[2 * (g % pairs):2 * (g % pairs) + 2]
+            into = slice(g // pairs * half, (g // pairs + 1) * half)
+            keep_ref[into, to] = out[at:at + half]
+            send_ref[into, to] = out[at + half:at + 2 * half].astype(BF16)
+
+
+def down(hid, low, groups, w, columns, joint=False):
+    half = hid.shape[0] // 4 * (groups if joint else 1)
+    pairs = 1 if joint else groups
     step = columns[1] - columns[0]
     return pl.pallas_call(
-        functools.partial(down_kernel, columns=columns, low=low),
+        functools.partial(down_kernel, columns=columns, low=low, groups=groups),
         in_specs=[VMEM] * 2,
-        out_specs=[VMEM] * (2 * groups),
+        out_specs=[VMEM] * (2 * pairs),
         out_shape=[
             jax.ShapeDtypeStruct((half, step), F32),
             jax.ShapeDtypeStruct((half, step), BF16),
         ]
-        * groups,
+        * pairs,
         compiler_params=params(8),
         cost_estimate=FREE,
         name="down",
@@ -393,19 +396,21 @@
 
     half = hid.shape[0] // 2
     step = 5 * width // 8
-    keep, send, *others = down(hid, 0, 2, w_down, (0, step, step // 2))
-    heads = [gather(keep, send), gather(*others)]
+    joint = len(near) == 2
+    made = down(hid, 0, 2, w_down, (0, step, step // 2), joint)
+    heads = [gather(*made)] * 2 if joint else [gather(*made[:2]), gather(*made[2:])]
     tails = []
     for g in range(2):
         keep, send = down(hid, g * half, 1, w_down, (step, width, width - step))
         tails.append(gather(keep, send))
     block = {}
-    for members, head, tail in zip(groups, heads, tails):
+    for g, members, head, tail in zip(range(2), groups, heads, tails):
+        shift = g * half // 2 if joint else 0
         outs = []
         for at in range(len(members)):
             for side in (1, 0):
                 low = (2 * at + side) * slots
-                outs.append([(piece, low, low + slots) for piece in range(2)])
+                outs.append([(0, low + shift, low + shift + slots), (1, low, low + slots)])
         sums = add([head, tail], outs, [BF16, F32] * len(members))
         block.update((i, sums[2 * at:2 * at + 2]) for at, i in enumerate(members))
 

time: 57.9 us -> 57.6 us (level)
  starting transfers between devices: 23.6 us -> 22.9 us
    ppermute x22 -> x21, starting transfers between devices: 23.6 us -> 22.9 us  [swap(): return lax.ppermute(x, 'expert', [(i, i ^ mask) for i in range(devices)])]
    ppermute x22 -> x21, waiting for transfers between devices: 18.5 us -> 18.8 us  [swap(): return lax.ppermute(x, 'expert', [(i, i ^ mask) for i in range(devices)])]
  transfers between devices with their start and end apart: 22 -> 21, of which waited for: 10 -> 10; matrix products, arithmetic and copies ran while one was open for 0% -> 0% of each run, Pallas kernels for 6% -> 6%
where the time goes in v23:
time: 57.6 us; the launch traced here: 57.4 us
  starting transfers between devices  22.9 us (40%)
  waiting for transfers between devices  18.8 us (33%)
  Pallas kernels  15.4 us (27%)
    ppermute x21, starting transfers between devices, swap(): return lax.ppermute(x, 'expert', [(i, i ^ mask) for i in range(devices)])  22.9 us
    ppermute x21, waiting for transfers between devices, swap(): return lax.ppermute(x, 'expert', [(i, i ^ mask) for i in range(devices)])  18.8 us
    pallas_call x3, Pallas kernels, down(): pl.pallas_call(functools.partial(down_kernel, columns=columns, low=low, g...  5.12 us
    pallas_call x1, Pallas kernels, up(): pl.pallas_call(functools.partial(up_kernel, sources=sources, count=len(pa...  5.03 us
    pallas_call x1, Pallas kernels, first(): pl.pallas_call(first_kernel, in_specs=[SMEM] + [HBM] * 7, out_specs=[VMEM...  2.35 us
    pallas_call x1, Pallas kernels, post(): pl.pallas_call(post_kernel, in_specs=[VMEM] * (3 + len(blocks)), out_spec...  1.21 us
  transfers between devices with their start and end apart: 21, of which 10 were waited for; matrix products, arithmetic and copies ran while one was open for 0% of the time, Pallas kernels for 6%

profile of v23, /device:TPU:0, one launch (start us, length us, event | category | flops | bytes accessed | tf_op | source)
XLA Modules:
  0.0 57.4 jit_solution(4937510650505087510)
XLA Ops:
  0.1 2.4 %first.1 = (bf16[16,4096]{1,0:T(8,128)(2,1)S(1)}, bf16[128,4096]{1,0:T(8,128)(2,1)S(1)}, f32[3,4096]{1,0:T(4,128)S(1)}, s32[4,16]{1,0:T(4,128)S(1)}, f32[4,16]{1,0:T(4,128)S(1)}) custom-call(s32[2]{0:T(128)S(1)} %pad_add_fusion.info_ref, bf16[128,4096]{1,0:T(8,128)(2,1)} %refs_0_.1, s32[4,16]{1,0:T(4,128)} %bitcast.6, f32[2,4096]{1,0:T(2,128)} %refs_2_.1, ...), custom_call_target="tpu_custom_call" | custom-call | flops 1 | bytes 1 | tf_op jit(solution)/shard_map/first/pallas_call | solution.py:91
  2.4 5.1 %collective-permute-start = (bf16[16,4096]{1,0:T(8,128)(2,1)S(1)}, bf16[16,4096]{1,0:T(8,128)(2,1)S(1)}, u32[]{:S(2)}, u32[]{:S(2)}) collective-permute-start(bf16[16,4096]{1,0:T(8,128)(2,1)S(1)} %get-tuple-element.31), channel_id=1, source_target_pairs={{0,12},{1,13},{2,14},{3,15},{4,8},{5,9},{6,10},{7,11},{8,4},{9,5},... | collective-permute-start | bytes 393224 | tf_op jit(solution)/shard_map/ppermute | solution.py:352
  9.0 1.7 %collective-permute-start.1 = (bf16[16,4096]{1,0:T(8,128)(2,1)S(1)}, bf16[16,4096]{1,0:T(8,128)(2,1)S(1)}, u32[]{:S(2)}, u32[]{:S(2)}) collective-permute-start(bf16[16,4096]{1,0:T(8,128)(2,1)S(1)} %get-tuple-element.36.refs_0_), channel_id=1, source_target_pairs={{0,2},{1,3},{2,0},{3,1},{4,6},{5,7},{6,4},{7,5},{8,10},{9,11},{10,... | collective-permute-start | bytes 393224 | tf_op jit(solution)/shard_map/ppermute | solution.py:352
  10.7 1.2 %collective-permute-done.after_ref.refs_0_ = bf16[16,4096]{1,0:T(8,128)(2,1)S(1)} collective-permute-done((bf16[16,4096]{1,0:T(8,128)(2,1)S(1)}, bf16[16,4096]{1,0:T(8,128)(2,1)S(1)}, u32[]{:S(2)}, u32[]{:S(2)}) %collective-permute-start) | collective-permute-done | bytes 131104 | tf_op jit(solution)/shard_map/ppermute | solution.py:352
  11.9 1.8 %collective-permute-start.3 = (bf16[16,4096]{1,0:T(8,128)(2,1)S(1)}, bf16[16,4096]{1,0:T(8,128)(2,1)S(1)}, u32[]{:S(2)}, u32[]{:S(2)}) collective-permute-start(bf16[16,4096]{1,0:T(8,128)(2,1)S(1)} %collective-permute-done.after_ref.refs_0_), channel_id=1, source_target_pairs={{0,2},{1,3},{2,0},{3,1},{4,6},{5,7},{6,4},{7,5},{8,10},{9,11},{10,... | collective-permute-start | bytes 393224 | tf_op jit(solution)/shard_map/ppermute | solution.py:352
  13.9 1.2 %collective-permute-done.8.refs_0_ = bf16[16,4096]{1,0:T(8,128)(2,1)S(1)} collective-permute-done((bf16[16,4096]{1,0:T(8,128)(2,1)S(1)}, bf16[16,4096]{1,0:T(8,128)(2,1)S(1)}, u32[]{:S(2)}, u32[]{:S(2)}) %collective-permute-start.8) | collective-permute-done | bytes 131104 | tf_op jit(solution)/shard_map/ppermute | solution.py:352
  15.0 1.6 %collective-permute-start.9 = (bf16[16,4096]{1,0:T(8,128)(2,1)S(1)}, bf16[16,4096]{1,0:T(8,128)(2,1)S(1)}, u32[]{:S(2)}, u32[]{:S(2)}) collective-permute-start(bf16[16,4096]{1,0:T(8,128)(2,1)S(1)} %collective-permute-done.8.refs_0_), channel_id=1, source_target_pairs={{0,2},{1,3},{2,0},{3,1},{4,6},{5,7},{6,4},{7,5},{8,10},{9,11},{10,... | collective-permute-start | bytes 393224 | tf_op jit(solution)/shard_map/ppermute | solution.py:352
  16.7 2.0 %collective-permute-done.5.refs_0_ = bf16[16,4096]{1,0:T(8,128)(2,1)S(1)} collective-permute-done((bf16[16,4096]{1,0:T(8,128)(2,1)S(1)}, bf16[16,4096]{1,0:T(8,128)(2,1)S(1)}, u32[]{:S(2)}, u32[]{:S(2)}) %collective-permute-start.5) | collective-permute-done | bytes 131104 | tf_op jit(solution)/shard_map/ppermute | solution.py:352
  18.6 1.6 %collective-permute-start.6 = (bf16[16,4096]{1,0:T(8,128)(2,1)S(1)}, bf16[16,4096]{1,0:T(8,128)(2,1)S(1)}, u32[]{:S(2)}, u32[]{:S(2)}) collective-permute-start(bf16[16,4096]{1,0:T(8,128)(2,1)S(1)} %join.8.refs_0_), channel_id=1, source_target_pairs={{0,2},{1,3},{2,0},{3,1},{4,6},{5,7},{6,4},{7,5},{8,10},{9,11},{10,... | collective-permute-start | bytes 393224 | tf_op jit(solution)/shard_map/ppermute | solution.py:352
  21.0 2.6 %collective-permute-done.6.refs_1_ = bf16[16,4096]{1,0:T(8,128)(2,1)S(1)} collective-permute-done((bf16[16,4096]{1,0:T(8,128)(2,1)S(1)}, bf16[16,4096]{1,0:T(8,128)(2,1)S(1)}, u32[]{:S(2)}, u32[]{:S(2)}) %collective-permute-start.6) | collective-permute-done | bytes 131104 | tf_op jit(solution)/shard_map/ppermute | solution.py:352
  23.8 1.5 %collective-permute-done.7.refs_5_ = bf16[32,4096]{1,0:T(8,128)(2,1)S(1)} collective-permute-done((bf16[32,4096]{1,0:T(8,128)(2,1)S(1)}, bf16[32,4096]{1,0:T(8,128)(2,1)S(1)}, u32[]{:S(2)}, u32[]{:S(2)}) %collective-permute-start.7) | collective-permute-done | bytes 262176 | tf_op jit(solution)/shard_map/ppermute | solution.py:352
  25.3 5.0 %up.1.h_ref = bf16[256,2048]{1,0:T(8,128)(2,1)S(1)} custom-call(bf16[32,4096]{1,0:T(8,128)(2,1)S(1)} %join.6.refs_0_, bf16[32,4096]{1,0:T(8,128)(2,1)S(1)} %collective-permute-done.2.refs_1_, bf16[32,4096]{1,0:T(8,128)(2,1)S(1)} %join.7.refs_2_, bf16[32,4096]{1,0:T(8,128)(2,1)S(1)} %collective-permute-done.4.refs_3_, bf16[32,4096]{1,0:T(8,128)(2,1)S(1)} %join.9.refs_4_, ...), custom_call_target="tpu_custom_call" | custom-call | flops 1 | bytes 1 | tf_op jit(solution)/shard_map/up/pallas_call | solution.py:205
  30.4 3.1 %down.3 = (f32[128,2560]{1,0:T(8,128)S(1)}, bf16[128,2560]{1,0:T(8,128)(2,1)S(1)}) custom-call(bf16[256,2048]{1,0:T(8,128)(2,1)S(1)} %up.1.h_ref, bf16[2048,4096]{1,0:T(8,128)(2,1)S(1)} %bitcast.5), custom_call_target="tpu_custom_call" | custom-call | flops 1 | bytes 1 | tf_op jit(solution)/shard_map/down/pallas_call | solution.py:240
  33.7 1.0 %down.5 = (f32[64,1536]{1,0:T(8,128)S(1)}, bf16[64,1536]{1,0:T(8,128)(2,1)S(1)}) custom-call(bf16[256,2048]{1,0:T(8,128)(2,1)S(1)} %up.1.h_ref, bf16[2048,4096]{1,0:T(8,128)(2,1)S(1)} %bitcast.5), custom_call_target="tpu_custom_call" | custom-call | flops 1 | bytes 1 | tf_op jit(solution)/shard_map/down/pallas_call | solution.py:240
  35.2 1.0 %down.4 = (f32[64,1536]{1,0:T(8,128)S(1)}, bf16[64,1536]{1,0:T(8,128)(2,1)S(1)}) custom-call(bf16[256,2048]{1,0:T(8,128)(2,1)S(1)} %up.1.h_ref, bf16[2048,4096]{1,0:T(8,128)(2,1)S(1)} %bitcast.5), custom_call_target="tpu_custom_call" | custom-call | flops 1 | bytes 1 | tf_op jit(solution)/shard_map/down/pallas_call | solution.py:240
  36.5 1.6 %collective-permute-start.14 = (bf16[16,4096]{1,0:T(8,128)(2,1)S(1)}, bf16[16,4096]{1,0:T(8,128)(2,1)S(1)}, u32[]{:S(2)}, u32[]{:S(2)}) collective-permute-start(bf16[16,4096]{1,0:T(8,128)(2,1)S(1)} %get-tuple-element.48), channel_id=1, source_target_pairs={{0,2},{1,3},{2,0},{3,1},{4,6},{5,7},{6,4},{7,5},{8,10},{9,11},{10,... | collective-permute-start | bytes 393224 | tf_op jit(solution)/shard_map/ppermute | solution.py:352
  38.7 1.6 %collective-permute-start.19 = (bf16[16,4096]{1,0:T(8,128)(2,1)S(1)}, bf16[16,4096]{1,0:T(8,128)(2,1)S(1)}, u32[]{:S(2)}, u32[]{:S(2)}) collective-permute-start(bf16[16,4096]{1,0:T(8,128)(2,1)S(1)} %get-tuple-element.52), channel_id=1, source_target_pairs={{0,2},{1,3},{2,0},{3,1},{4,6},{5,7},{6,4},{7,5},{8,10},{9,11},{10,... | collective-permute-start | bytes 393224 | tf_op jit(solution)/shard_map/ppermute | solution.py:352
  40.2 2.6 %collective-permute-done.14.refs_1_ = bf16[16,4096]{1,0:T(8,128)(2,1)S(1)} collective-permute-done((bf16[16,4096]{1,0:T(8,128)(2,1)S(1)}, bf16[16,4096]{1,0:T(8,128)(2,1)S(1)}, u32[]{:S(2)}, u32[]{:S(2)}) %collective-permute-start.14) | collective-permute-done | bytes 131104 | tf_op jit(solution)/shard_map/ppermute | solution.py:352
  42.9 2.6 %collective-permute-start.16 = (bf16[16,4096]{1,0:T(8,128)(2,1)S(1)}, bf16[16,4096]{1,0:T(8,128)(2,1)S(1)}, u32[]{:S(2)}, u32[]{:S(2)}) collective-permute-start(bf16[16,4096]{1,0:T(8,128)(2,1)S(1)} %add.11.refs_1_), channel_id=1, source_target_pairs={{0,12},{1,13},{2,14},{3,15},{4,8},{5,9},{6,10},{7,11},{8,4},{9,5},... | collective-permute-start | bytes 393224 | tf_op jit(solution)/shard_map/ppermute | solution.py:352
  45.4 1.6 %collective-permute-start.15 = (bf16[16,4096]{1,0:T(8,128)(2,1)S(1)}, bf16[16,4096]{1,0:T(8,128)(2,1)S(1)}, u32[]{:S(2)}, u32[]{:S(2)}) collective-permute-start(bf16[16,4096]{1,0:T(8,128)(2,1)S(1)} %join.11), channel_id=1, source_target_pairs={{0,2},{1,3},{2,0},{3,1},{4,6},{5,7},{6,4},{7,5},{8,10},{9,11},{10,... | collective-permute-start | bytes 393224 | tf_op jit(solution)/shard_map/ppermute | solution.py:352
  47.1 1.3 %collective-permute-done.19.refs_1_ = bf16[16,4096]{1,0:T(8,128)(2,1)S(1)} collective-permute-done((bf16[16,4096]{1,0:T(8,128)(2,1)S(1)}, bf16[16,4096]{1,0:T(8,128)(2,1)S(1)}, u32[]{:S(2)}, u32[]{:S(2)}) %collective-permute-start.19) | collective-permute-done | bytes 131104 | tf_op jit(solution)/shard_map/ppermute | solution.py:352
  49.4 1.3 %collective-permute-done.15.near_ref = bf16[16,4096]{1,0:T(8,128)(2,1)S(1)} collective-permute-done((bf16[16,4096]{1,0:T(8,128)(2,1)S(1)}, bf16[16,4096]{1,0:T(8,128)(2,1)S(1)}, u32[]{:S(2)}, u32[]{:S(2)}) %collective-permute-start.15) | collective-permute-done | bytes 131104 | tf_op jit(solution)/shard_map/ppermute | solution.py:352
  51.4 4.9 %collective-permute-done.18.refs_0_ = bf16[16,4096]{1,0:T(8,128)(2,1)S(1)} collective-permute-done((bf16[16,4096]{1,0:T(8,128)(2,1)S(1)}, bf16[16,4096]{1,0:T(8,128)(2,1)S(1)}, u32[]{:S(2)}, u32[]{:S(2)}) %collective-permute-start.18) | collective-permute-done | bytes 131104 | tf_op jit(solution)/shard_map/ppermute | solution.py:352
  56.2 1.2 %post.1 = bf16[128,4096]{1,0:T(8,128)(2,1)} custom-call(bf16[128,64]{1,0:T(8,128)(2,1)S(1)} %get-tuple-element.32.mix_ref, f32[3,4096]{1,0:T(4,128)S(1)} %get-tuple-element.33.table_ref, f32[128,4096]{1,0:T(8,128)S(1)} %own_part.1.acc_ref, bf16[16,4096]{1,0:T(8,128)(2,1)S(1)} %collective-permute-done.18.refs_0_, ...), custom_call_target="tpu_custom_call" | custom-call | flops 1 | bytes 1 | tf_op jit(solution)/shard_map/post/pallas_call | solution.py:320
  (50 shorter events, 5.8 us)
Async XLA Ops:
  2.4 9.5 %collective-permute-start = (bf16[16,4096]{1,0:T(8,128)(2,1)S(1)}, bf16[16,4096]{1,0:T(8,128)(2,1)S(1)}, u32[]{:S(2)}, u32[]{:S(2)}) collective-permute-start(bf16[16,4096]{1,0:T(8,128)(2,1)S(1)} %get-tuple-element.31), channel_id=1, source_target_pairs={{0,12},{1,13},{2,14},{3,15},{4,8},{5,9},{6,10},{7,11},{8,4},{9,5},... | collective-permute-start | bytes 393224 | tf_op jit(solution)/shard_map/ppermute | solution.py:352
  7.6 22.8 %slice-start.1 = ((s8[16777216]{0:T(1024)(128)(4,1)}), s8[4194304]{0:T(1024)(128)(4,1)S(1)}, s32[]{:S(2)}) async-start(s8[16777216]{0:T(1024)(128)(4,1)} %bitcast.4), calls=%async_computation.1 | async-start | bytes 8388608
  7.6 22.8 %slice-start.2 = ((s8[16777216]{0:T(1024)(128)(4,1)}), s8[4194304]{0:T(1024)(128)(4,1)S(1)}, s32[]{:S(2)}) async-start(s8[16777216]{0:T(1024)(128)(4,1)} %bitcast.4), calls=%async_computation.2 | async-start | bytes 8388608
  7.6 22.8 %slice-start.3 = ((s8[16777216]{0:T(1024)(128)(4,1)}), s8[4194304]{0:T(1024)(128)(4,1)S(1)}, s32[]{:S(2)}) async-start(s8[16777216]{0:T(1024)(128)(4,1)} %bitcast.4), calls=%async_computation.3 | async-start | bytes 8388608
  8.3 6.7 %collective-permute-start.8 = (bf16[16,4096]{1,0:T(8,128)(2,1)S(1)}, bf16[16,4096]{1,0:T(8,128)(2,1)S(1)}, u32[]{:S(2)}, u32[]{:S(2)}) collective-permute-start(bf16[16,4096]{1,0:T(8,128)(2,1)S(1)} %get-tuple-element.38), channel_id=1, source_target_pairs={{0,4},{1,5},{2,6},{3,7},{4,0},{5,1},{6,2},{7,3},{8,12},{9,13},{10,... | collective-permute-start | bytes 393224 | tf_op jit(solution)/shard_map/ppermute | solution.py:352
  8.4 10.2 %collective-permute-start.5 = (bf16[16,4096]{1,0:T(8,128)(2,1)S(1)}, bf16[16,4096]{1,0:T(8,128)(2,1)S(1)}, u32[]{:S(2)}, u32[]{:S(2)}) collective-permute-start(bf16[16,4096]{1,0:T(8,128)(2,1)S(1)} %get-tuple-element.37), channel_id=1, source_target_pairs={{0,8},{1,9},{2,10},{3,11},{4,12},{5,13},{6,14},{7,15},{8,0},{9,1},... | collective-permute-start | bytes 393224 | tf_op jit(solution)/shard_map/ppermute | solution.py:352
  9.0 11.2 %collective-permute-start.1 = (bf16[16,4096]{1,0:T(8,128)(2,1)S(1)}, bf16[16,4096]{1,0:T(8,128)(2,1)S(1)}, u32[]{:S(2)}, u32[]{:S(2)}) collective-permute-start(bf16[16,4096]{1,0:T(8,128)(2,1)S(1)} %get-tuple-element.36.refs_0_), channel_id=1, source_target_pairs={{0,2},{1,3},{2,0},{3,1},{4,6},{5,7},{6,4},{7,5},{8,10},{9,11},{10,... | collective-permute-start | bytes 393224 | tf_op jit(solution)/shard_map/ppermute | solution.py:352
  11.9 8.4 %collective-permute-start.3 = (bf16[16,4096]{1,0:T(8,128)(2,1)S(1)}, bf16[16,4096]{1,0:T(8,128)(2,1)S(1)}, u32[]{:S(2)}, u32[]{:S(2)}) collective-permute-start(bf16[16,4096]{1,0:T(8,128)(2,1)S(1)} %collective-permute-done.after_ref.refs_0_), channel_id=1, source_target_pairs={{0,2},{1,3},{2,0},{3,1},{4,6},{5,7},{6,4},{7,5},{8,10},{9,11},{10,... | collective-permute-start | bytes 393224 | tf_op jit(solution)/shard_map/ppermute | solution.py:352
  15.0 5.9 %collective-permute-start.9 = (bf16[16,4096]{1,0:T(8,128)(2,1)S(1)}, bf16[16,4096]{1,0:T(8,128)(2,1)S(1)}, u32[]{:S(2)}, u32[]{:S(2)}) collective-permute-start(bf16[16,4096]{1,0:T(8,128)(2,1)S(1)} %collective-permute-done.8.refs_0_), channel_id=1, source_target_pairs={{0,2},{1,3},{2,0},{3,1},{4,6},{5,7},{6,4},{7,5},{8,10},{9,11},{10,... | collective-permute-start | bytes 393224 | tf_op jit(solution)/shard_map/ppermute | solution.py:352
  18.6 5.0 %collective-permute-start.6 = (bf16[16,4096]{1,0:T(8,128)(2,1)S(1)}, bf16[16,4096]{1,0:T(8,128)(2,1)S(1)}, u32[]{:S(2)}, u32[]{:S(2)}) collective-permute-start(bf16[16,4096]{1,0:T(8,128)(2,1)S(1)} %join.8.refs_0_), channel_id=1, source_target_pairs={{0,2},{1,3},{2,0},{3,1},{4,6},{5,7},{6,4},{7,5},{8,10},{9,11},{10,... | collective-permute-start | bytes 393224 | tf_op jit(solution)/shard_map/ppermute | solution.py:352
  20.2 3.5 %collective-permute-start.2 = (bf16[32,4096]{1,0:T(8,128)(2,1)S(1)}, bf16[32,4096]{1,0:T(8,128)(2,1)S(1)}, u32[]{:S(2)}, u32[]{:S(2)}) collective-permute-start(bf16[32,4096]{1,0:T(8,128)(2,1)S(1)} %join.6.refs_0_), channel_id=1, source_target_pairs={{0,1},{1,0},{2,3},{3,2},{4,5},{5,4},{6,7},{7,6},{8,9},{9,8},{10,11... | collective-permute-start | bytes 786440 | tf_op jit(solution)/shard_map/ppermute | solution.py:352
  20.4 3.4 %collective-permute-start.4 = (bf16[32,4096]{1,0:T(8,128)(2,1)S(1)}, bf16[32,4096]{1,0:T(8,128)(2,1)S(1)}, u32[]{:S(2)}, u32[]{:S(2)}) collective-permute-start(bf16[32,4096]{1,0:T(8,128)(2,1)S(1)} %join.7.refs_2_), channel_id=1, source_target_pairs={{0,1},{1,0},{2,3},{3,2},{4,5},{5,4},{6,7},{7,6},{8,9},{9,8},{10,11... | collective-permute-start | bytes 786440 | tf_op jit(solution)/shard_map/ppermute | solution.py:352
  20.9 2.9 %collective-permute-start.10 = (bf16[32,4096]{1,0:T(8,128)(2,1)S(1)}, bf16[32,4096]{1,0:T(8,128)(2,1)S(1)}, u32[]{:S(2)}, u32[]{:S(2)}) collective-permute-start(bf16[32,4096]{1,0:T(8,128)(2,1)S(1)} %join.10.refs_6_), channel_id=1, source_target_pairs={{0,1},{1,0},{2,3},{3,2},{4,5},{5,4},{6,7},{7,6},{8,9},{9,8},{10,11... | collective-permute-start | bytes 786440 | tf_op jit(solution)/shard_map/ppermute | solution.py:352
  23.7 1.6 %collective-permute-start.7 = (bf16[32,4096]{1,0:T(8,128)(2,1)S(1)}, bf16[32,4096]{1,0:T(8,128)(2,1)S(1)}, u32[]{:S(2)}, u32[]{:S(2)}) collective-permute-start(bf16[32,4096]{1,0:T(8,128)(2,1)S(1)} %join.9.refs_4_), channel_id=1, source_target_pairs={{0,1},{1,0},{2,3},{3,2},{4,5},{5,4},{6,7},{7,6},{8,9},{9,8},{10,11... | collective-permute-start | bytes 786440 | tf_op jit(solution)/shard_map/ppermute | solution.py:352
  33.5 2.8 %collective-permute-start.11 = (bf16[128,2560]{1,0:T(8,128)(2,1)S(1)}, bf16[128,2560]{1,0:T(8,128)(2,1)S(1)}, u32[]{:S(2)}, u32[]{:S(2)}) collective-permute-start(bf16[128,2560]{1,0:T(8,128)(2,1)S(1)} %get-tuple-element.40), channel_id=1, source_target_pairs={{0,1},{1,0},{2,3},{3,2},{4,5},{5,4},{6,7},{7,6},{8,9},{9,8},{10,11... | collective-permute-start | bytes 1966088 | tf_op jit(solution)/shard_map/ppermute | solution.py:352
  34.7 1.6 %collective-permute-start.13 = (bf16[64,1536]{1,0:T(8,128)(2,1)S(1)}, bf16[64,1536]{1,0:T(8,128)(2,1)S(1)}, u32[]{:S(2)}, u32[]{:S(2)}) collective-permute-start(bf16[64,1536]{1,0:T(8,128)(2,1)S(1)} %get-tuple-element.46), channel_id=1, source_target_pairs={{0,1},{1,0},{2,3},{3,2},{4,5},{5,4},{6,7},{7,6},{8,9},{9,8},{10,11... | collective-permute-start | bytes 589832 | tf_op jit(solution)/shard_map/ppermute | solution.py:352
  36.2 2.4 %collective-permute-start.12 = (bf16[64,1536]{1,0:T(8,128)(2,1)S(1)}, bf16[64,1536]{1,0:T(8,128)(2,1)S(1)}, u32[]{:S(2)}, u32[]{:S(2)}) collective-permute-start(bf16[64,1536]{1,0:T(8,128)(2,1)S(1)} %get-tuple-element.42), channel_id=1, source_target_pairs={{0,1},{1,0},{2,3},{3,2},{4,5},{5,4},{6,7},{7,6},{8,9},{9,8},{10,11... | collective-permute-start | bytes 589832 | tf_op jit(solution)/shard_map/ppermute | solution.py:352
  36.5 6.4 %collective-permute-start.14 = (bf16[16,4096]{1,0:T(8,128)(2,1)S(1)}, bf16[16,4096]{1,0:T(8,128)(2,1)S(1)}, u32[]{:S(2)}, u32[]{:S(2)}) collective-permute-start(bf16[16,4096]{1,0:T(8,128)(2,1)S(1)} %get-tuple-element.48), channel_id=1, source_target_pairs={{0,2},{1,3},{2,0},{3,1},{4,6},{5,7},{6,4},{7,5},{8,10},{9,11},{10,... | collective-permute-start | bytes 393224 | tf_op jit(solution)/shard_map/ppermute | solution.py:352
  38.1 9.0 %collective-permute-start.17 = (bf16[16,4096]{1,0:T(8,128)(2,1)S(1)}, bf16[16,4096]{1,0:T(8,128)(2,1)S(1)}, u32[]{:S(2)}, u32[]{:S(2)}) collective-permute-start(bf16[16,4096]{1,0:T(8,128)(2,1)S(1)} %get-tuple-element.50), channel_id=1, source_target_pairs={{0,2},{1,3},{2,0},{3,1},{4,6},{5,7},{6,4},{7,5},{8,10},{9,11},{10,... | collective-permute-start | bytes 393224 | tf_op jit(solution)/shard_map/ppermute | solution.py:352
  38.7 9.8 %collective-permute-start.19 = (bf16[16,4096]{1,0:T(8,128)(2,1)S(1)}, bf16[16,4096]{1,0:T(8,128)(2,1)S(1)}, u32[]{:S(2)}, u32[]{:S(2)}) collective-permute-start(bf16[16,4096]{1,0:T(8,128)(2,1)S(1)} %get-tuple-element.52), channel_id=1, source_target_pairs={{0,2},{1,3},{2,0},{3,1},{4,6},{5,7},{6,4},{7,5},{8,10},{9,11},{10,... | collective-permute-start | bytes 393224 | tf_op jit(solution)/shard_map/ppermute | solution.py:352
  42.9 8.1 %collective-permute-start.16 = (bf16[16,4096]{1,0:T(8,128)(2,1)S(1)}, bf16[16,4096]{1,0:T(8,128)(2,1)S(1)}, u32[]{:S(2)}, u32[]{:S(2)}) collective-permute-start(bf16[16,4096]{1,0:T(8,128)(2,1)S(1)} %add.11.refs_1_), channel_id=1, source_target_pairs={{0,12},{1,13},{2,14},{3,15},{4,8},{5,9},{6,10},{7,11},{8,4},{9,5},... | collective-permute-start | bytes 393224 | tf_op jit(solution)/shard_map/ppermute | solution.py:352
  45.4 5.3 %collective-permute-start.15 = (bf16[16,4096]{1,0:T(8,128)(2,1)S(1)}, bf16[16,4096]{1,0:T(8,128)(2,1)S(1)}, u32[]{:S(2)}, u32[]{:S(2)}) collective-permute-start(bf16[16,4096]{1,0:T(8,128)(2,1)S(1)} %join.11), channel_id=1, source_target_pairs={{0,2},{1,3},{2,0},{3,1},{4,6},{5,7},{6,4},{7,5},{8,10},{9,11},{10,... | collective-permute-start | bytes 393224 | tf_op jit(solution)/shard_map/ppermute | solution.py:352
  47.1 9.2 %collective-permute-start.18 = (bf16[16,4096]{1,0:T(8,128)(2,1)S(1)}, bf16[16,4096]{1,0:T(8,128)(2,1)S(1)}, u32[]{:S(2)}, u32[]{:S(2)}) collective-permute-start(bf16[16,4096]{1,0:T(8,128)(2,1)S(1)} %add.12), channel_id=1, source_target_pairs={{0,8},{1,9},{2,10},{3,11},{4,12},{5,13},{6,14},{7,15},{8,0},{9,1},... | collective-permute-start | bytes 393224 | tf_op jit(solution)/shard_map/ppermute | solution.py:352
  48.5 7.7 %collective-permute-start.20 = (bf16[16,4096]{1,0:T(8,128)(2,1)S(1)}, bf16[16,4096]{1,0:T(8,128)(2,1)S(1)}, u32[]{:S(2)}, u32[]{:S(2)}) collective-permute-start(bf16[16,4096]{1,0:T(8,128)(2,1)S(1)} %add.13), channel_id=1, source_target_pairs={{0,4},{1,5},{2,6},{3,7},{4,0},{5,1},{6,2},{7,3},{8,12},{9,13},{10,... | collective-permute-start | bytes 393224 | tf_op jit(solution)/shard_map/ppermute | solution.py:352
  (2 other events, 40.5 us)

commit v24 on v23

--- a/solution.py
+++ b/solution.py
@@ -219,7 +219,7 @@
     pairs = len(outs) // 2
     half = outs[0].shape[0] * pairs // groups
 
-    @pl.loop(0, (last - first) // tile)
+    @pl.loop(0, (last - first) // tile, unroll=True)
     def _(i):
         to = pl.ds(pl.multiple_of(i * tile, tile), tile)
         cut = pl.ds(pl.multiple_of(first + i * tile, tile), tile)

time: 57.6 us -> 57.3 us (level)
  no operation moved by 1% of the time
where the time goes in v24:
time: 57.3 us; the launch traced here: 57.2 us
  starting transfers between devices  22.9 us (40%)
  waiting for transfers between devices  18.8 us (33%)
  Pallas kernels  15.1 us (26%)
    ppermute x21, starting transfers between devices, swap(): return lax.ppermute(x, 'expert', [(i, i ^ mask) for i in range(devices)])  22.9 us
    ppermute x21, waiting for transfers between devices, swap(): return lax.ppermute(x, 'expert', [(i, i ^ mask) for i in range(devices)])  18.8 us
    pallas_call x1, Pallas kernels, up(): pl.pallas_call(functools.partial(up_kernel, sources=sources, count=len(pa...  5.03 us
    pallas_call x3, Pallas kernels, down(): pl.pallas_call(functools.partial(down_kernel, columns=columns, low=low, g...  4.84 us
    pallas_call x1, Pallas kernels, first(): pl.pallas_call(first_kernel, in_specs=[SMEM] + [HBM] * 7, out_specs=[VMEM...  2.35 us
    pallas_call x1, Pallas kernels, post(): pl.pallas_call(post_kernel, in_specs=[VMEM] * (3 + len(blocks)), out_spec...  1.21 us
  transfers between devices with their start and end apart: 21, of which 10 were waited for; matrix products, arithmetic and copies ran while one was open for 0% of the time, Pallas kernels for 6%

profile of v24, /device:TPU:0, one launch (start us, length us, event | category | flops | bytes accessed | tf_op | source)
XLA Modules:
  0.0 57.2 jit_solution(11190110243229608583)
XLA Ops:
  0.1 2.4 %first.1 = (bf16[16,4096]{1,0:T(8,128)(2,1)S(1)}, bf16[128,4096]{1,0:T(8,128)(2,1)S(1)}, f32[3,4096]{1,0:T(4,128)S(1)}, s32[4,16]{1,0:T(4,128)S(1)}, f32[4,16]{1,0:T(4,128)S(1)}) custom-call(s32[2]{0:T(128)S(1)} %pad_add_fusion.info_ref, bf16[128,4096]{1,0:T(8,128)(2,1)} %refs_0_.1, s32[4,16]{1,0:T(4,128)} %bitcast.6, f32[2,4096]{1,0:T(2,128)} %refs_2_.1, ...), custom_call_target="tpu_custom_call" | custom-call | flops 1 | bytes 1 | tf_op jit(solution)/shard_map/first/pallas_call | solution.py:91
  2.4 5.1 %collective-permute-start = (bf16[16,4096]{1,0:T(8,128)(2,1)S(1)}, bf16[16,4096]{1,0:T(8,128)(2,1)S(1)}, u32[]{:S(2)}, u32[]{:S(2)}) collective-permute-start(bf16[16,4096]{1,0:T(8,128)(2,1)S(1)} %get-tuple-element.31), channel_id=1, source_target_pairs={{0,12},{1,13},{2,14},{3,15},{4,8},{5,9},{6,10},{7,11},{8,4},{9,5},... | collective-permute-start | bytes 393224 | tf_op jit(solution)/shard_map/ppermute | solution.py:352
  9.0 1.7 %collective-permute-start.1 = (bf16[16,4096]{1,0:T(8,128)(2,1)S(1)}, bf16[16,4096]{1,0:T(8,128)(2,1)S(1)}, u32[]{:S(2)}, u32[]{:S(2)}) collective-permute-start(bf16[16,4096]{1,0:T(8,128)(2,1)S(1)} %get-tuple-element.36.refs_0_), channel_id=1, source_target_pairs={{0,2},{1,3},{2,0},{3,1},{4,6},{5,7},{6,4},{7,5},{8,10},{9,11},{10,... | collective-permute-start | bytes 393224 | tf_op jit(solution)/shard_map/ppermute | solution.py:352
  10.7 1.2 %collective-permute-done.after_ref.refs_0_ = bf16[16,4096]{1,0:T(8,128)(2,1)S(1)} collective-permute-done((bf16[16,4096]{1,0:T(8,128)(2,1)S(1)}, bf16[16,4096]{1,0:T(8,128)(2,1)S(1)}, u32[]{:S(2)}, u32[]{:S(2)}) %collective-permute-start) | collective-permute-done | bytes 131104 | tf_op jit(solution)/shard_map/ppermute | solution.py:352
  11.9 1.8 %collective-permute-start.3 = (bf16[16,4096]{1,0:T(8,128)(2,1)S(1)}, bf16[16,4096]{1,0:T(8,128)(2,1)S(1)}, u32[]{:S(2)}, u32[]{:S(2)}) collective-permute-start(bf16[16,4096]{1,0:T(8,128)(2,1)S(1)} %collective-permute-done.after_ref.refs_0_), channel_id=1, source_target_pairs={{0,2},{1,3},{2,0},{3,1},{4,6},{5,7},{6,4},{7,5},{8,10},{9,11},{10,... | collective-permute-start | bytes 393224 | tf_op jit(solution)/shard_map/ppermute | solution.py:352
  13.9 1.2 %collective-permute-done.8.refs_0_ = bf16[16,4096]{1,0:T(8,128)(2,1)S(1)} collective-permute-done((bf16[16,4096]{1,0:T(8,128)(2,1)S(1)}, bf16[16,4096]{1,0:T(8,128)(2,1)S(1)}, u32[]{:S(2)}, u32[]{:S(2)}) %collective-permute-start.8) | collective-permute-done | bytes 131104 | tf_op jit(solution)/shard_map/ppermute | solution.py:352
  15.0 1.6 %collective-permute-start.9 = (bf16[16,4096]{1,0:T(8,128)(2,1)S(1)}, bf16[16,4096]{1,0:T(8,128)(2,1)S(1)}, u32[]{:S(2)}, u32[]{:S(2)}) collective-permute-start(bf16[16,4096]{1,0:T(8,128)(2,1)S(1)} %collective-permute-done.8.refs_0_), channel_id=1, source_target_pairs={{0,2},{1,3},{2,0},{3,1},{4,6},{5,7},{6,4},{7,5},{8,10},{9,11},{10,... | collective-permute-start | bytes 393224 | tf_op jit(solution)/shard_map/ppermute | solution.py:352
  16.7 2.0 %collective-permute-done.5.refs_0_ = bf16[16,4096]{1,0:T(8,128)(2,1)S(1)} collective-permute-done((bf16[16,4096]{1,0:T(8,128)(2,1)S(1)}, bf16[16,4096]{1,0:T(8,128)(2,1)S(1)}, u32[]{:S(2)}, u32[]{:S(2)}) %collective-permute-start.5) | collective-permute-done | bytes 131104 | tf_op jit(solution)/shard_map/ppermute | solution.py:352
  18.6 1.6 %collective-permute-start.6 = (bf16[16,4096]{1,0:T(8,128)(2,1)S(1)}, bf16[16,4096]{1,0:T(8,128)(2,1)S(1)}, u32[]{:S(2)}, u32[]{:S(2)}) collective-permute-start(bf16[16,4096]{1,0:T(8,128)(2,1)S(1)} %join.8.refs_0_), channel_id=1, source_target_pairs={{0,2},{1,3},{2,0},{3,1},{4,6},{5,7},{6,4},{7,5},{8,10},{9,11},{10,... | collective-permute-start | bytes 393224 | tf_op jit(solution)/shard_map/ppermute | solution.py:352
  21.0 2.6 %collective-permute-done.6.refs_1_ = bf16[16,4096]{1,0:T(8,128)(2,1)S(1)} collective-permute-done((bf16[16,4096]{1,0:T(8,128)(2,1)S(1)}, bf16[16,4096]{1,0:T(8,128)(2,1)S(1)}, u32[]{:S(2)}, u32[]{:S(2)}) %collective-permute-start.6) | collective-permute-done | bytes 131104 | tf_op jit(solution)/shard_map/ppermute | solution.py:352
  23.8 1.5 %collective-permute-done.7.refs_5_ = bf16[32,4096]{1,0:T(8,128)(2,1)S(1)} collective-permute-done((bf16[32,4096]{1,0:T(8,128)(2,1)S(1)}, bf16[32,4096]{1,0:T(8,128)(2,1)S(1)}, u32[]{:S(2)}, u32[]{:S(2)}) %collective-permute-start.7) | collective-permute-done | bytes 262176 | tf_op jit(solution)/shard_map/ppermute | solution.py:352
  25.3 5.0 %up.1.h_ref = bf16[256,2048]{1,0:T(8,128)(2,1)S(1)} custom-call(bf16[32,4096]{1,0:T(8,128)(2,1)S(1)} %join.6.refs_0_, bf16[32,4096]{1,0:T(8,128)(2,1)S(1)} %collective-permute-done.2.refs_1_, bf16[32,4096]{1,0:T(8,128)(2,1)S(1)} %join.7.refs_2_, bf16[32,4096]{1,0:T(8,128)(2,1)S(1)} %collective-permute-done.4.refs_3_, bf16[32,4096]{1,0:T(8,128)(2,1)S(1)} %join.9.refs_4_, ...), custom_call_target="tpu_custom_call" | custom-call | flops 1 | bytes 1 | tf_op jit(solution)/shard_map/up/pallas_call | solution.py:205
  30.4 2.9 %down.3 = (f32[128,2560]{1,0:T(8,128)S(1)}, bf16[128,2560]{1,0:T(8,128)(2,1)S(1)}) custom-call(bf16[256,2048]{1,0:T(8,128)(2,1)S(1)} %up.1.h_ref, bf16[2048,4096]{1,0:T(8,128)(2,1)S(1)} %bitcast.5), custom_call_target="tpu_custom_call" | custom-call | flops 1 | bytes 1 | tf_op jit(solution)/shard_map/down/pallas_call | solution.py:240
  33.5 1.0 %down.5 = (f32[64,1536]{1,0:T(8,128)S(1)}, bf16[64,1536]{1,0:T(8,128)(2,1)S(1)}) custom-call(bf16[256,2048]{1,0:T(8,128)(2,1)S(1)} %up.1.h_ref, bf16[2048,4096]{1,0:T(8,128)(2,1)S(1)} %bitcast.5), custom_call_target="tpu_custom_call" | custom-call | flops 1 | bytes 1 | tf_op jit(solution)/shard_map/down/pallas_call | solution.py:240
  34.9 1.0 %down.4 = (f32[64,1536]{1,0:T(8,128)S(1)}, bf16[64,1536]{1,0:T(8,128)(2,1)S(1)}) custom-call(bf16[256,2048]{1,0:T(8,128)(2,1)S(1)} %up.1.h_ref, bf16[2048,4096]{1,0:T(8,128)(2,1)S(1)} %bitcast.5), custom_call_target="tpu_custom_call" | custom-call | flops 1 | bytes 1 | tf_op jit(solution)/shard_map/down/pallas_call | solution.py:240
  36.2 1.6 %collective-permute-start.14 = (bf16[16,4096]{1,0:T(8,128)(2,1)S(1)}, bf16[16,4096]{1,0:T(8,128)(2,1)S(1)}, u32[]{:S(2)}, u32[]{:S(2)}) collective-permute-start(bf16[16,4096]{1,0:T(8,128)(2,1)S(1)} %get-tuple-element.48), channel_id=1, source_target_pairs={{0,2},{1,3},{2,0},{3,1},{4,6},{5,7},{6,4},{7,5},{8,10},{9,11},{10,... | collective-permute-start | bytes 393224 | tf_op jit(solution)/shard_map/ppermute | solution.py:352
  38.4 1.6 %collective-permute-start.19 = (bf16[16,4096]{1,0:T(8,128)(2,1)S(1)}, bf16[16,4096]{1,0:T(8,128)(2,1)S(1)}, u32[]{:S(2)}, u32[]{:S(2)}) collective-permute-start(bf16[16,4096]{1,0:T(8,128)(2,1)S(1)} %get-tuple-element.52), channel_id=1, source_target_pairs={{0,2},{1,3},{2,0},{3,1},{4,6},{5,7},{6,4},{7,5},{8,10},{9,11},{10,... | collective-permute-start | bytes 393224 | tf_op jit(solution)/shard_map/ppermute | solution.py:352
  40.0 2.6 %collective-permute-done.14.refs_1_ = bf16[16,4096]{1,0:T(8,128)(2,1)S(1)} collective-permute-done((bf16[16,4096]{1,0:T(8,128)(2,1)S(1)}, bf16[16,4096]{1,0:T(8,128)(2,1)S(1)}, u32[]{:S(2)}, u32[]{:S(2)}) %collective-permute-start.14) | collective-permute-done | bytes 131104 | tf_op jit(solution)/shard_map/ppermute | solution.py:352
  42.6 2.6 %collective-permute-start.16 = (bf16[16,4096]{1,0:T(8,128)(2,1)S(1)}, bf16[16,4096]{1,0:T(8,128)(2,1)S(1)}, u32[]{:S(2)}, u32[]{:S(2)}) collective-permute-start(bf16[16,4096]{1,0:T(8,128)(2,1)S(1)} %add.11.refs_1_), channel_id=1, source_target_pairs={{0,12},{1,13},{2,14},{3,15},{4,8},{5,9},{6,10},{7,11},{8,4},{9,5},... | collective-permute-start | bytes 393224 | tf_op jit(solution)/shard_map/ppermute | solution.py:352
  45.2 1.6 %collective-permute-start.15 = (bf16[16,4096]{1,0:T(8,128)(2,1)S(1)}, bf16[16,4096]{1,0:T(8,128)(2,1)S(1)}, u32[]{:S(2)}, u32[]{:S(2)}) collective-permute-start(bf16[16,4096]{1,0:T(8,128)(2,1)S(1)} %join.11), channel_id=1, source_target_pairs={{0,2},{1,3},{2,0},{3,1},{4,6},{5,7},{6,4},{7,5},{8,10},{9,11},{10,... | collective-permute-start | bytes 393224 | tf_op jit(solution)/shard_map/ppermute | solution.py:352
  46.9 1.3 %collective-permute-done.19.refs_1_ = bf16[16,4096]{1,0:T(8,128)(2,1)S(1)} collective-permute-done((bf16[16,4096]{1,0:T(8,128)(2,1)S(1)}, bf16[16,4096]{1,0:T(8,128)(2,1)S(1)}, u32[]{:S(2)}, u32[]{:S(2)}) %collective-permute-start.19) | collective-permute-done | bytes 131104 | tf_op jit(solution)/shard_map/ppermute | solution.py:352
  49.2 1.3 %collective-permute-done.15.near_ref = bf16[16,4096]{1,0:T(8,128)(2,1)S(1)} collective-permute-done((bf16[16,4096]{1,0:T(8,128)(2,1)S(1)}, bf16[16,4096]{1,0:T(8,128)(2,1)S(1)}, u32[]{:S(2)}, u32[]{:S(2)}) %collective-permute-start.15) | collective-permute-done | bytes 131104 | tf_op jit(solution)/shard_map/ppermute | solution.py:352
  51.1 4.9 %collective-permute-done.18.refs_0_ = bf16[16,4096]{1,0:T(8,128)(2,1)S(1)} collective-permute-done((bf16[16,4096]{1,0:T(8,128)(2,1)S(1)}, bf16[16,4096]{1,0:T(8,128)(2,1)S(1)}, u32[]{:S(2)}, u32[]{:S(2)}) %collective-permute-start.18) | collective-permute-done | bytes 131104 | tf_op jit(solution)/shard_map/ppermute | solution.py:352
  56.0 1.2 %post.1 = bf16[128,4096]{1,0:T(8,128)(2,1)} custom-call(bf16[128,64]{1,0:T(8,128)(2,1)S(1)} %get-tuple-element.32.mix_ref, f32[3,4096]{1,0:T(4,128)S(1)} %get-tuple-element.33.table_ref, f32[128,4096]{1,0:T(8,128)S(1)} %own_part.1.acc_ref, bf16[16,4096]{1,0:T(8,128)(2,1)S(1)} %collective-permute-done.18.refs_0_, ...), custom_call_target="tpu_custom_call" | custom-call | flops 1 | bytes 1 | tf_op jit(solution)/shard_map/post/pallas_call | solution.py:320
  (50 shorter events, 5.8 us)
Async XLA Ops:
  2.4 9.5 %collective-permute-start = (bf16[16,4096]{1,0:T(8,128)(2,1)S(1)}, bf16[16,4096]{1,0:T(8,128)(2,1)S(1)}, u32[]{:S(2)}, u32[]{:S(2)}) collective-permute-start(bf16[16,4096]{1,0:T(8,128)(2,1)S(1)} %get-tuple-element.31), channel_id=1, source_target_pairs={{0,12},{1,13},{2,14},{3,15},{4,8},{5,9},{6,10},{7,11},{8,4},{9,5},... | collective-permute-start | bytes 393224 | tf_op jit(solution)/shard_map/ppermute | solution.py:352
  7.6 22.8 %slice-start.1 = ((s8[16777216]{0:T(1024)(128)(4,1)}), s8[4194304]{0:T(1024)(128)(4,1)S(1)}, s32[]{:S(2)}) async-start(s8[16777216]{0:T(1024)(128)(4,1)} %bitcast.4), calls=%async_computation.1 | async-start | bytes 8388608
  7.6 22.8 %slice-start.2 = ((s8[16777216]{0:T(1024)(128)(4,1)}), s8[4194304]{0:T(1024)(128)(4,1)S(1)}, s32[]{:S(2)}) async-start(s8[16777216]{0:T(1024)(128)(4,1)} %bitcast.4), calls=%async_computation.2 | async-start | bytes 8388608
  7.6 22.8 %slice-start.3 = ((s8[16777216]{0:T(1024)(128)(4,1)}), s8[4194304]{0:T(1024)(128)(4,1)S(1)}, s32[]{:S(2)}) async-start(s8[16777216]{0:T(1024)(128)(4,1)} %bitcast.4), calls=%async_computation.3 | async-start | bytes 8388608
  8.3 6.7 %collective-permute-start.8 = (bf16[16,4096]{1,0:T(8,128)(2,1)S(1)}, bf16[16,4096]{1,0:T(8,128)(2,1)S(1)}, u32[]{:S(2)}, u32[]{:S(2)}) collective-permute-start(bf16[16,4096]{1,0:T(8,128)(2,1)S(1)} %get-tuple-element.38), channel_id=1, source_target_pairs={{0,4},{1,5},{2,6},{3,7},{4,0},{5,1},{6,2},{7,3},{8,12},{9,13},{10,... | collective-permute-start | bytes 393224 | tf_op jit(solution)/shard_map/ppermute | solution.py:352
  8.4 10.2 %collective-permute-start.5 = (bf16[16,4096]{1,0:T(8,128)(2,1)S(1)}, bf16[16,4096]{1,0:T(8,128)(2,1)S(1)}, u32[]{:S(2)}, u32[]{:S(2)}) collective-permute-start(bf16[16,4096]{1,0:T(8,128)(2,1)S(1)} %get-tuple-element.37), channel_id=1, source_target_pairs={{0,8},{1,9},{2,10},{3,11},{4,12},{5,13},{6,14},{7,15},{8,0},{9,1},... | collective-permute-start | bytes 393224 | tf_op jit(solution)/shard_map/ppermute | solution.py:352
  9.0 11.2 %collective-permute-start.1 = (bf16[16,4096]{1,0:T(8,128)(2,1)S(1)}, bf16[16,4096]{1,0:T(8,128)(2,1)S(1)}, u32[]{:S(2)}, u32[]{:S(2)}) collective-permute-start(bf16[16,4096]{1,0:T(8,128)(2,1)S(1)} %get-tuple-element.36.refs_0_), channel_id=1, source_target_pairs={{0,2},{1,3},{2,0},{3,1},{4,6},{5,7},{6,4},{7,5},{8,10},{9,11},{10,... | collective-permute-start | bytes 393224 | tf_op jit(solution)/shard_map/ppermute | solution.py:352
  11.9 8.4 %collective-permute-start.3 = (bf16[16,4096]{1,0:T(8,128)(2,1)S(1)}, bf16[16,4096]{1,0:T(8,128)(2,1)S(1)}, u32[]{:S(2)}, u32[]{:S(2)}) collective-permute-start(bf16[16,4096]{1,0:T(8,128)(2,1)S(1)} %collective-permute-done.after_ref.refs_0_), channel_id=1, source_target_pairs={{0,2},{1,3},{2,0},{3,1},{4,6},{5,7},{6,4},{7,5},{8,10},{9,11},{10,... | collective-permute-start | bytes 393224 | tf_op jit(solution)/shard_map/ppermute | solution.py:352
  15.0 5.9 %collective-permute-start.9 = (bf16[16,4096]{1,0:T(8,128)(2,1)S(1)}, bf16[16,4096]{1,0:T(8,128)(2,1)S(1)}, u32[]{:S(2)}, u32[]{:S(2)}) collective-permute-start(bf16[16,4096]{1,0:T(8,128)(2,1)S(1)} %collective-permute-done.8.refs_0_), channel_id=1, source_target_pairs={{0,2},{1,3},{2,0},{3,1},{4,6},{5,7},{6,4},{7,5},{8,10},{9,11},{10,... | collective-permute-start | bytes 393224 | tf_op jit(solution)/shard_map/ppermute | solution.py:352
  18.6 5.0 %collective-permute-start.6 = (bf16[16,4096]{1,0:T(8,128)(2,1)S(1)}, bf16[16,4096]{1,0:T(8,128)(2,1)S(1)}, u32[]{:S(2)}, u32[]{:S(2)}) collective-permute-start(bf16[16,4096]{1,0:T(8,128)(2,1)S(1)} %join.8.refs_0_), channel_id=1, source_target_pairs={{0,2},{1,3},{2,0},{3,1},{4,6},{5,7},{6,4},{7,5},{8,10},{9,11},{10,... | collective-permute-start | bytes 393224 | tf_op jit(solution)/shard_map/ppermute | solution.py:352
  20.2 3.5 %collective-permute-start.2 = (bf16[32,4096]{1,0:T(8,128)(2,1)S(1)}, bf16[32,4096]{1,0:T(8,128)(2,1)S(1)}, u32[]{:S(2)}, u32[]{:S(2)}) collective-permute-start(bf16[32,4096]{1,0:T(8,128)(2,1)S(1)} %join.6.refs_0_), channel_id=1, source_target_pairs={{0,1},{1,0},{2,3},{3,2},{4,5},{5,4},{6,7},{7,6},{8,9},{9,8},{10,11... | collective-permute-start | bytes 786440 | tf_op jit(solution)/shard_map/ppermute | solution.py:352
  20.4 3.4 %collective-permute-start.4 = (bf16[32,4096]{1,0:T(8,128)(2,1)S(1)}, bf16[32,4096]{1,0:T(8,128)(2,1)S(1)}, u32[]{:S(2)}, u32[]{:S(2)}) collective-permute-start(bf16[32,4096]{1,0:T(8,128)(2,1)S(1)} %join.7.refs_2_), channel_id=1, source_target_pairs={{0,1},{1,0},{2,3},{3,2},{4,5},{5,4},{6,7},{7,6},{8,9},{9,8},{10,11... | collective-permute-start | bytes 786440 | tf_op jit(solution)/shard_map/ppermute | solution.py:352
  20.9 2.9 %collective-permute-start.10 = (bf16[32,4096]{1,0:T(8,128)(2,1)S(1)}, bf16[32,4096]{1,0:T(8,128)(2,1)S(1)}, u32[]{:S(2)}, u32[]{:S(2)}) collective-permute-start(bf16[32,4096]{1,0:T(8,128)(2,1)S(1)} %join.10.refs_6_), channel_id=1, source_target_pairs={{0,1},{1,0},{2,3},{3,2},{4,5},{5,4},{6,7},{7,6},{8,9},{9,8},{10,11... | collective-permute-start | bytes 786440 | tf_op jit(solution)/shard_map/ppermute | solution.py:352
  23.7 1.6 %collective-permute-start.7 = (bf16[32,4096]{1,0:T(8,128)(2,1)S(1)}, bf16[32,4096]{1,0:T(8,128)(2,1)S(1)}, u32[]{:S(2)}, u32[]{:S(2)}) collective-permute-start(bf16[32,4096]{1,0:T(8,128)(2,1)S(1)} %join.9.refs_4_), channel_id=1, source_target_pairs={{0,1},{1,0},{2,3},{3,2},{4,5},{5,4},{6,7},{7,6},{8,9},{9,8},{10,11... | collective-permute-start | bytes 786440 | tf_op jit(solution)/shard_map/ppermute | solution.py:352
  33.3 2.8 %collective-permute-start.11 = (bf16[128,2560]{1,0:T(8,128)(2,1)S(1)}, bf16[128,2560]{1,0:T(8,128)(2,1)S(1)}, u32[]{:S(2)}, u32[]{:S(2)}) collective-permute-start(bf16[128,2560]{1,0:T(8,128)(2,1)S(1)} %get-tuple-element.40), channel_id=1, source_target_pairs={{0,1},{1,0},{2,3},{3,2},{4,5},{5,4},{6,7},{7,6},{8,9},{9,8},{10,11... | collective-permute-start | bytes 1966088 | tf_op jit(solution)/shard_map/ppermute | solution.py:352
  34.5 1.6 %collective-permute-start.13 = (bf16[64,1536]{1,0:T(8,128)(2,1)S(1)}, bf16[64,1536]{1,0:T(8,128)(2,1)S(1)}, u32[]{:S(2)}, u32[]{:S(2)}) collective-permute-start(bf16[64,1536]{1,0:T(8,128)(2,1)S(1)} %get-tuple-element.46), channel_id=1, source_target_pairs={{0,1},{1,0},{2,3},{3,2},{4,5},{5,4},{6,7},{7,6},{8,9},{9,8},{10,11... | collective-permute-start | bytes 589832 | tf_op jit(solution)/shard_map/ppermute | solution.py:352
  35.9 2.4 %collective-permute-start.12 = (bf16[64,1536]{1,0:T(8,128)(2,1)S(1)}, bf16[64,1536]{1,0:T(8,128)(2,1)S(1)}, u32[]{:S(2)}, u32[]{:S(2)}) collective-permute-start(bf16[64,1536]{1,0:T(8,128)(2,1)S(1)} %get-tuple-element.42), channel_id=1, source_target_pairs={{0,1},{1,0},{2,3},{3,2},{4,5},{5,4},{6,7},{7,6},{8,9},{9,8},{10,11... | collective-permute-start | bytes 589832 | tf_op jit(solution)/shard_map/ppermute | solution.py:352
  36.2 6.4 %collective-permute-start.14 = (bf16[16,4096]{1,0:T(8,128)(2,1)S(1)}, bf16[16,4096]{1,0:T(8,128)(2,1)S(1)}, u32[]{:S(2)}, u32[]{:S(2)}) collective-permute-start(bf16[16,4096]{1,0:T(8,128)(2,1)S(1)} %get-tuple-element.48), channel_id=1, source_target_pairs={{0,2},{1,3},{2,0},{3,1},{4,6},{5,7},{6,4},{7,5},{8,10},{9,11},{10,... | collective-permute-start | bytes 393224 | tf_op jit(solution)/shard_map/ppermute | solution.py:352
  37.8 9.0 %collective-permute-start.17 = (bf16[16,4096]{1,0:T(8,128)(2,1)S(1)}, bf16[16,4096]{1,0:T(8,128)(2,1)S(1)}, u32[]{:S(2)}, u32[]{:S(2)}) collective-permute-start(bf16[16,4096]{1,0:T(8,128)(2,1)S(1)} %get-tuple-element.50), channel_id=1, source_target_pairs={{0,2},{1,3},{2,0},{3,1},{4,6},{5,7},{6,4},{7,5},{8,10},{9,11},{10,... | collective-permute-start | bytes 393224 | tf_op jit(solution)/shard_map/ppermute | solution.py:352
  38.4 9.8 %collective-permute-start.19 = (bf16[16,4096]{1,0:T(8,128)(2,1)S(1)}, bf16[16,4096]{1,0:T(8,128)(2,1)S(1)}, u32[]{:S(2)}, u32[]{:S(2)}) collective-permute-start(bf16[16,4096]{1,0:T(8,128)(2,1)S(1)} %get-tuple-element.52), channel_id=1, source_target_pairs={{0,2},{1,3},{2,0},{3,1},{4,6},{5,7},{6,4},{7,5},{8,10},{9,11},{10,... | collective-permute-start | bytes 393224 | tf_op jit(solution)/shard_map/ppermute | solution.py:352
  42.6 8.1 %collective-permute-start.16 = (bf16[16,4096]{1,0:T(8,128)(2,1)S(1)}, bf16[16,4096]{1,0:T(8,128)(2,1)S(1)}, u32[]{:S(2)}, u32[]{:S(2)}) collective-permute-start(bf16[16,4096]{1,0:T(8,128)(2,1)S(1)} %add.11.refs_1_), channel_id=1, source_target_pairs={{0,12},{1,13},{2,14},{3,15},{4,8},{5,9},{6,10},{7,11},{8,4},{9,5},... | collective-permute-start | bytes 393224 | tf_op jit(solution)/shard_map/ppermute | solution.py:352
  45.2 5.3 %collective-permute-start.15 = (bf16[16,4096]{1,0:T(8,128)(2,1)S(1)}, bf16[16,4096]{1,0:T(8,128)(2,1)S(1)}, u32[]{:S(2)}, u32[]{:S(2)}) collective-permute-start(bf16[16,4096]{1,0:T(8,128)(2,1)S(1)} %join.11), channel_id=1, source_target_pairs={{0,2},{1,3},{2,0},{3,1},{4,6},{5,7},{6,4},{7,5},{8,10},{9,11},{10,... | collective-permute-start | bytes 393224 | tf_op jit(solution)/shard_map/ppermute | solution.py:352
  46.8 9.2 %collective-permute-start.18 = (bf16[16,4096]{1,0:T(8,128)(2,1)S(1)}, bf16[16,4096]{1,0:T(8,128)(2,1)S(1)}, u32[]{:S(2)}, u32[]{:S(2)}) collective-permute-start(bf16[16,4096]{1,0:T(8,128)(2,1)S(1)} %add.12), channel_id=1, source_target_pairs={{0,8},{1,9},{2,10},{3,11},{4,12},{5,13},{6,14},{7,15},{8,0},{9,1},... | collective-permute-start | bytes 393224 | tf_op jit(solution)/shard_map/ppermute | solution.py:352
  48.2 7.7 %collective-permute-start.20 = (bf16[16,4096]{1,0:T(8,128)(2,1)S(1)}, bf16[16,4096]{1,0:T(8,128)(2,1)S(1)}, u32[]{:S(2)}, u32[]{:S(2)}) collective-permute-start(bf16[16,4096]{1,0:T(8,128)(2,1)S(1)} %add.13), channel_id=1, source_target_pairs={{0,4},{1,5},{2,6},{3,7},{4,0},{5,1},{6,2},{7,3},{8,12},{9,13},{10,... | collective-permute-start | bytes 393224 | tf_op jit(solution)/shard_map/ppermute | solution.py:352
  (2 other events, 40.5 us)

commit v25 on v24

--- a/solution.py
+++ b/solution.py
@@ -397,11 +397,11 @@
     half = hid.shape[0] // 2
     step = 5 * width // 8
     joint = len(near) == 2
-    made = down(hid, 0, 2, w_down, (0, step, step // 2), joint)
+    made = down(hid, 0, 2, w_down, (0, step, step // 5), joint)
     heads = [gather(*made)] * 2 if joint else [gather(*made[:2]), gather(*made[2:])]
     tails = []
     for g in range(2):
-        keep, send = down(hid, g * half, 1, w_down, (step, width, width - step))
+        keep, send = down(hid, g * half, 1, w_down, (step, width, (width - step) // 3))
         tails.append(gather(keep, send))
     block = {}
     for g, members, head, tail in zip(range(2), groups, heads, tails):

time: 57.3 us -> 57.3 us (level)
  no operation moved by 1% of the time
where the time goes in v25:
time: 57.3 us; the launch traced here: 57.2 us
  starting transfers between devices  22.9 us (40%)
  waiting for transfers between devices  18.8 us (33%)
  Pallas kernels  15.1 us (26%)
    ppermute x21, starting transfers between devices, swap(): return lax.ppermute(x, 'expert', [(i, i ^ mask) for i in range(devices)])  22.9 us
    ppermute x21, waiting for transfers between devices, swap(): return lax.ppermute(x, 'expert', [(i, i ^ mask) for i in range(devices)])  18.8 us
    pallas_call x1, Pallas kernels, up(): pl.pallas_call(functools.partial(up_kernel, sources=sources, count=len(pa...  5.03 us
    pallas_call x3, Pallas kernels, down(): pl.pallas_call(functools.partial(down_kernel, columns=columns, low=low, g...  4.85 us
    pallas_call x1, Pallas kernels, first(): pl.pallas_call(first_kernel, in_specs=[SMEM] + [HBM] * 7, out_specs=[VMEM...  2.35 us
    pallas_call x1, Pallas kernels, post(): pl.pallas_call(post_kernel, in_specs=[VMEM] * (3 + len(blocks)), out_spec...  1.2 us
  transfers between devices with their start and end apart: 21, of which 10 were waited for; matrix products, arithmetic and copies ran while one was open for 0% of the time, Pallas kernels for 6%

profile of v25, /device:TPU:0, one launch (start us, length us, event | category | flops | bytes accessed | tf_op | source)
XLA Modules:
  0.0 57.2 jit_solution(1922000449992849860)
XLA Ops:
  0.1 2.4 %first.1 = (bf16[16,4096]{1,0:T(8,128)(2,1)S(1)}, bf16[128,4096]{1,0:T(8,128)(2,1)S(1)}, f32[3,4096]{1,0:T(4,128)S(1)}, s32[4,16]{1,0:T(4,128)S(1)}, f32[4,16]{1,0:T(4,128)S(1)}) custom-call(s32[2]{0:T(128)S(1)} %pad_add_fusion.info_ref, bf16[128,4096]{1,0:T(8,128)(2,1)} %refs_0_.1, s32[4,16]{1,0:T(4,128)} %bitcast.6, f32[2,4096]{1,0:T(2,128)} %refs_2_.1, ...), custom_call_target="tpu_custom_call" | custom-call | flops 1 | bytes 1 | tf_op jit(solution)/shard_map/first/pallas_call | solution.py:91
  2.4 5.1 %collective-permute-start = (bf16[16,4096]{1,0:T(8,128)(2,1)S(1)}, bf16[16,4096]{1,0:T(8,128)(2,1)S(1)}, u32[]{:S(2)}, u32[]{:S(2)}) collective-permute-start(bf16[16,4096]{1,0:T(8,128)(2,1)S(1)} %get-tuple-element.31), channel_id=1, source_target_pairs={{0,12},{1,13},{2,14},{3,15},{4,8},{5,9},{6,10},{7,11},{8,4},{9,5},... | collective-permute-start | bytes 393224 | tf_op jit(solution)/shard_map/ppermute | solution.py:352
  9.0 1.7 %collective-permute-start.1 = (bf16[16,4096]{1,0:T(8,128)(2,1)S(1)}, bf16[16,4096]{1,0:T(8,128)(2,1)S(1)}, u32[]{:S(2)}, u32[]{:S(2)}) collective-permute-start(bf16[16,4096]{1,0:T(8,128)(2,1)S(1)} %get-tuple-element.36.refs_0_), channel_id=1, source_target_pairs={{0,2},{1,3},{2,0},{3,1},{4,6},{5,7},{6,4},{7,5},{8,10},{9,11},{10,... | collective-permute-start | bytes 393224 | tf_op jit(solution)/shard_map/ppermute | solution.py:352
  10.7 1.2 %collective-permute-done.after_ref.refs_0_ = bf16[16,4096]{1,0:T(8,128)(2,1)S(1)} collective-permute-done((bf16[16,4096]{1,0:T(8,128)(2,1)S(1)}, bf16[16,4096]{1,0:T(8,128)(2,1)S(1)}, u32[]{:S(2)}, u32[]{:S(2)}) %collective-permute-start) | collective-permute-done | bytes 131104 | tf_op jit(solution)/shard_map/ppermute | solution.py:352
  11.9 1.8 %collective-permute-start.3 = (bf16[16,4096]{1,0:T(8,128)(2,1)S(1)}, bf16[16,4096]{1,0:T(8,128)(2,1)S(1)}, u32[]{:S(2)}, u32[]{:S(2)}) collective-permute-start(bf16[16,4096]{1,0:T(8,128)(2,1)S(1)} %collective-permute-done.after_ref.refs_0_), channel_id=1, source_target_pairs={{0,2},{1,3},{2,0},{3,1},{4,6},{5,7},{6,4},{7,5},{8,10},{9,11},{10,... | collective-permute-start | bytes 393224 | tf_op jit(solution)/shard_map/ppermute | solution.py:352
  13.9 1.2 %collective-permute-done.8.refs_0_ = bf16[16,4096]{1,0:T(8,128)(2,1)S(1)} collective-permute-done((bf16[16,4096]{1,0:T(8,128)(2,1)S(1)}, bf16[16,4096]{1,0:T(8,128)(2,1)S(1)}, u32[]{:S(2)}, u32[]{:S(2)}) %collective-permute-start.8) | collective-permute-done | bytes 131104 | tf_op jit(solution)/shard_map/ppermute | solution.py:352
  15.0 1.6 %collective-permute-start.9 = (bf16[16,4096]{1,0:T(8,128)(2,1)S(1)}, bf16[16,4096]{1,0:T(8,128)(2,1)S(1)}, u32[]{:S(2)}, u32[]{:S(2)}) collective-permute-start(bf16[16,4096]{1,0:T(8,128)(2,1)S(1)} %collective-permute-done.8.refs_0_), channel_id=1, source_target_pairs={{0,2},{1,3},{2,0},{3,1},{4,6},{5,7},{6,4},{7,5},{8,10},{9,11},{10,... | collective-permute-start | bytes 393224 | tf_op jit(solution)/shard_map/ppermute | solution.py:352
  16.7 2.0 %collective-permute-done.5.refs_0_ = bf16[16,4096]{1,0:T(8,128)(2,1)S(1)} collective-permute-done((bf16[16,4096]{1,0:T(8,128)(2,1)S(1)}, bf16[16,4096]{1,0:T(8,128)(2,1)S(1)}, u32[]{:S(2)}, u32[]{:S(2)}) %collective-permute-start.5) | collective-permute-done | bytes 131104 | tf_op jit(solution)/shard_map/ppermute | solution.py:352
  18.6 1.6 %collective-permute-start.6 = (bf16[16,4096]{1,0:T(8,128)(2,1)S(1)}, bf16[16,4096]{1,0:T(8,128)(2,1)S(1)}, u32[]{:S(2)}, u32[]{:S(2)}) collective-permute-start(bf16[16,4096]{1,0:T(8,128)(2,1)S(1)} %join.8.refs_0_), channel_id=1, source_target_pairs={{0,2},{1,3},{2,0},{3,1},{4,6},{5,7},{6,4},{7,5},{8,10},{9,11},{10,... | collective-permute-start | bytes 393224 | tf_op jit(solution)/shard_map/ppermute | solution.py:352
  21.0 2.6 %collective-permute-done.6.refs_1_ = bf16[16,4096]{1,0:T(8,128)(2,1)S(1)} collective-permute-done((bf16[16,4096]{1,0:T(8,128)(2,1)S(1)}, bf16[16,4096]{1,0:T(8,128)(2,1)S(1)}, u32[]{:S(2)}, u32[]{:S(2)}) %collective-permute-start.6) | collective-permute-done | bytes 131104 | tf_op jit(solution)/shard_map/ppermute | solution.py:352
  23.8 1.5 %collective-permute-done.7.refs_5_ = bf16[32,4096]{1,0:T(8,128)(2,1)S(1)} collective-permute-done((bf16[32,4096]{1,0:T(8,128)(2,1)S(1)}, bf16[32,4096]{1,0:T(8,128)(2,1)S(1)}, u32[]{:S(2)}, u32[]{:S(2)}) %collective-permute-start.7) | collective-permute-done | bytes 262176 | tf_op jit(solution)/shard_map/ppermute | solution.py:352
  25.3 5.0 %up.1.h_ref = bf16[256,2048]{1,0:T(8,128)(2,1)S(1)} custom-call(bf16[32,4096]{1,0:T(8,128)(2,1)S(1)} %join.6.refs_0_, bf16[32,4096]{1,0:T(8,128)(2,1)S(1)} %collective-permute-done.2.refs_1_, bf16[32,4096]{1,0:T(8,128)(2,1)S(1)} %join.7.refs_2_, bf16[32,4096]{1,0:T(8,128)(2,1)S(1)} %collective-permute-done.4.refs_3_, bf16[32,4096]{1,0:T(8,128)(2,1)S(1)} %join.9.refs_4_, ...), custom_call_target="tpu_custom_call" | custom-call | flops 1 | bytes 1 | tf_op jit(solution)/shard_map/up/pallas_call | solution.py:205
  30.4 2.9 %down.3 = (f32[128,2560]{1,0:T(8,128)S(1)}, bf16[128,2560]{1,0:T(8,128)(2,1)S(1)}) custom-call(bf16[256,2048]{1,0:T(8,128)(2,1)S(1)} %up.1.h_ref, bf16[2048,4096]{1,0:T(8,128)(2,1)S(1)} %bitcast.5), custom_call_target="tpu_custom_call" | custom-call | flops 1 | bytes 1 | tf_op jit(solution)/shard_map/down/pallas_call | solution.py:240
  33.5 1.0 %down.5 = (f32[64,1536]{1,0:T(8,128)S(1)}, bf16[64,1536]{1,0:T(8,128)(2,1)S(1)}) custom-call(bf16[256,2048]{1,0:T(8,128)(2,1)S(1)} %up.1.h_ref, bf16[2048,4096]{1,0:T(8,128)(2,1)S(1)} %bitcast.5), custom_call_target="tpu_custom_call" | custom-call | flops 1 | bytes 1 | tf_op jit(solution)/shard_map/down/pallas_call | solution.py:240
  34.9 1.0 %down.4 = (f32[64,1536]{1,0:T(8,128)S(1)}, bf16[64,1536]{1,0:T(8,128)(2,1)S(1)}) custom-call(bf16[256,2048]{1,0:T(8,128)(2,1)S(1)} %up.1.h_ref, bf16[2048,4096]{1,0:T(8,128)(2,1)S(1)} %bitcast.5), custom_call_target="tpu_custom_call" | custom-call | flops 1 | bytes 1 | tf_op jit(solution)/shard_map/down/pallas_call | solution.py:240
  36.2 1.6 %collective-permute-start.14 = (bf16[16,4096]{1,0:T(8,128)(2,1)S(1)}, bf16[16,4096]{1,0:T(8,128)(2,1)S(1)}, u32[]{:S(2)}, u32[]{:S(2)}) collective-permute-start(bf16[16,4096]{1,0:T(8,128)(2,1)S(1)} %get-tuple-element.48), channel_id=1, source_target_pairs={{0,2},{1,3},{2,0},{3,1},{4,6},{5,7},{6,4},{7,5},{8,10},{9,11},{10,... | collective-permute-start | bytes 393224 | tf_op jit(solution)/shard_map/ppermute | solution.py:352
  38.4 1.6 %collective-permute-start.19 = (bf16[16,4096]{1,0:T(8,128)(2,1)S(1)}, bf16[16,4096]{1,0:T(8,128)(2,1)S(1)}, u32[]{:S(2)}, u32[]{:S(2)}) collective-permute-start(bf16[16,4096]{1,0:T(8,128)(2,1)S(1)} %get-tuple-element.52), channel_id=1, source_target_pairs={{0,2},{1,3},{2,0},{3,1},{4,6},{5,7},{6,4},{7,5},{8,10},{9,11},{10,... | collective-permute-start | bytes 393224 | tf_op jit(solution)/shard_map/ppermute | solution.py:352
  40.0 2.6 %collective-permute-done.14.refs_1_ = bf16[16,4096]{1,0:T(8,128)(2,1)S(1)} collective-permute-done((bf16[16,4096]{1,0:T(8,128)(2,1)S(1)}, bf16[16,4096]{1,0:T(8,128)(2,1)S(1)}, u32[]{:S(2)}, u32[]{:S(2)}) %collective-permute-start.14) | collective-permute-done | bytes 131104 | tf_op jit(solution)/shard_map/ppermute | solution.py:352
  42.6 2.5 %collective-permute-start.16 = (bf16[16,4096]{1,0:T(8,128)(2,1)S(1)}, bf16[16,4096]{1,0:T(8,128)(2,1)S(1)}, u32[]{:S(2)}, u32[]{:S(2)}) collective-permute-start(bf16[16,4096]{1,0:T(8,128)(2,1)S(1)} %add.11.refs_1_), channel_id=1, source_target_pairs={{0,12},{1,13},{2,14},{3,15},{4,8},{5,9},{6,10},{7,11},{8,4},{9,5},... | collective-permute-start | bytes 393224 | tf_op jit(solution)/shard_map/ppermute | solution.py:352
  45.2 1.6 %collective-permute-start.15 = (bf16[16,4096]{1,0:T(8,128)(2,1)S(1)}, bf16[16,4096]{1,0:T(8,128)(2,1)S(1)}, u32[]{:S(2)}, u32[]{:S(2)}) collective-permute-start(bf16[16,4096]{1,0:T(8,128)(2,1)S(1)} %join.11), channel_id=1, source_target_pairs={{0,2},{1,3},{2,0},{3,1},{4,6},{5,7},{6,4},{7,5},{8,10},{9,11},{10,... | collective-permute-start | bytes 393224 | tf_op jit(solution)/shard_map/ppermute | solution.py:352
  46.9 1.3 %collective-permute-done.19.refs_1_ = bf16[16,4096]{1,0:T(8,128)(2,1)S(1)} collective-permute-done((bf16[16,4096]{1,0:T(8,128)(2,1)S(1)}, bf16[16,4096]{1,0:T(8,128)(2,1)S(1)}, u32[]{:S(2)}, u32[]{:S(2)}) %collective-permute-start.19) | collective-permute-done | bytes 131104 | tf_op jit(solution)/shard_map/ppermute | solution.py:352
  49.2 1.3 %collective-permute-done.15.near_ref = bf16[16,4096]{1,0:T(8,128)(2,1)S(1)} collective-permute-done((bf16[16,4096]{1,0:T(8,128)(2,1)S(1)}, bf16[16,4096]{1,0:T(8,128)(2,1)S(1)}, u32[]{:S(2)}, u32[]{:S(2)}) %collective-permute-start.15) | collective-permute-done | bytes 131104 | tf_op jit(solution)/shard_map/ppermute | solution.py:352
  51.1 4.8 %collective-permute-done.18.refs_0_ = bf16[16,4096]{1,0:T(8,128)(2,1)S(1)} collective-permute-done((bf16[16,4096]{1,0:T(8,128)(2,1)S(1)}, bf16[16,4096]{1,0:T(8,128)(2,1)S(1)}, u32[]{:S(2)}, u32[]{:S(2)}) %collective-permute-start.18) | collective-permute-done | bytes 131104 | tf_op jit(solution)/shard_map/ppermute | solution.py:352
  56.0 1.2 %post.1 = bf16[128,4096]{1,0:T(8,128)(2,1)} custom-call(bf16[128,64]{1,0:T(8,128)(2,1)S(1)} %get-tuple-element.32.mix_ref, f32[3,4096]{1,0:T(4,128)S(1)} %get-tuple-element.33.table_ref, f32[128,4096]{1,0:T(8,128)S(1)} %own_part.1.acc_ref, bf16[16,4096]{1,0:T(8,128)(2,1)S(1)} %collective-permute-done.18.refs_0_, ...), custom_call_target="tpu_custom_call" | custom-call | flops 1 | bytes 1 | tf_op jit(solution)/shard_map/post/pallas_call | solution.py:320
  (50 shorter events, 5.9 us)
Async XLA Ops:
  2.4 9.5 %collective-permute-start = (bf16[16,4096]{1,0:T(8,128)(2,1)S(1)}, bf16[16,4096]{1,0:T(8,128)(2,1)S(1)}, u32[]{:S(2)}, u32[]{:S(2)}) collective-permute-start(bf16[16,4096]{1,0:T(8,128)(2,1)S(1)} %get-tuple-element.31), channel_id=1, source_target_pairs={{0,12},{1,13},{2,14},{3,15},{4,8},{5,9},{6,10},{7,11},{8,4},{9,5},... | collective-permute-start | bytes 393224 | tf_op jit(solution)/shard_map/ppermute | solution.py:352
  7.6 22.8 %slice-start.1 = ((s8[16777216]{0:T(1024)(128)(4,1)}), s8[4194304]{0:T(1024)(128)(4,1)S(1)}, s32[]{:S(2)}) async-start(s8[16777216]{0:T(1024)(128)(4,1)} %bitcast.4), calls=%async_computation.1 | async-start | bytes 8388608
  7.6 22.8 %slice-start.2 = ((s8[16777216]{0:T(1024)(128)(4,1)}), s8[4194304]{0:T(1024)(128)(4,1)S(1)}, s32[]{:S(2)}) async-start(s8[16777216]{0:T(1024)(128)(4,1)} %bitcast.4), calls=%async_computation.2 | async-start | bytes 8388608
  7.6 22.8 %slice-start.3 = ((s8[16777216]{0:T(1024)(128)(4,1)}), s8[4194304]{0:T(1024)(128)(4,1)S(1)}, s32[]{:S(2)}) async-start(s8[16777216]{0:T(1024)(128)(4,1)} %bitcast.4), calls=%async_computation.3 | async-start | bytes 8388608
  8.3 6.7 %collective-permute-start.8 = (bf16[16,4096]{1,0:T(8,128)(2,1)S(1)}, bf16[16,4096]{1,0:T(8,128)(2,1)S(1)}, u32[]{:S(2)}, u32[]{:S(2)}) collective-permute-start(bf16[16,4096]{1,0:T(8,128)(2,1)S(1)} %get-tuple-element.38), channel_id=1, source_target_pairs={{0,4},{1,5},{2,6},{3,7},{4,0},{5,1},{6,2},{7,3},{8,12},{9,13},{10,... | collective-permute-start | bytes 393224 | tf_op jit(solution)/shard_map/ppermute | solution.py:352
  8.4 10.2 %collective-permute-start.5 = (bf16[16,4096]{1,0:T(8,128)(2,1)S(1)}, bf16[16,4096]{1,0:T(8,128)(2,1)S(1)}, u32[]{:S(2)}, u32[]{:S(2)}) collective-permute-start(bf16[16,4096]{1,0:T(8,128)(2,1)S(1)} %get-tuple-element.37), channel_id=1, source_target_pairs={{0,8},{1,9},{2,10},{3,11},{4,12},{5,13},{6,14},{7,15},{8,0},{9,1},... | collective-permute-start | bytes 393224 | tf_op jit(solution)/shard_map/ppermute | solution.py:352
  9.0 11.2 %collective-permute-start.1 = (bf16[16,4096]{1,0:T(8,128)(2,1)S(1)}, bf16[16,4096]{1,0:T(8,128)(2,1)S(1)}, u32[]{:S(2)}, u32[]{:S(2)}) collective-permute-start(bf16[16,4096]{1,0:T(8,128)(2,1)S(1)} %get-tuple-element.36.refs_0_), channel_id=1, source_target_pairs={{0,2},{1,3},{2,0},{3,1},{4,6},{5,7},{6,4},{7,5},{8,10},{9,11},{10,... | collective-permute-start | bytes 393224 | tf_op jit(solution)/shard_map/ppermute | solution.py:352
  11.9 8.4 %collective-permute-start.3 = (bf16[16,4096]{1,0:T(8,128)(2,1)S(1)}, bf16[16,4096]{1,0:T(8,128)(2,1)S(1)}, u32[]{:S(2)}, u32[]{:S(2)}) collective-permute-start(bf16[16,4096]{1,0:T(8,128)(2,1)S(1)} %collective-permute-done.after_ref.refs_0_), channel_id=1, source_target_pairs={{0,2},{1,3},{2,0},{3,1},{4,6},{5,7},{6,4},{7,5},{8,10},{9,11},{10,... | collective-permute-start | bytes 393224 | tf_op jit(solution)/shard_map/ppermute | solution.py:352
  15.0 5.9 %collective-permute-start.9 = (bf16[16,4096]{1,0:T(8,128)(2,1)S(1)}, bf16[16,4096]{1,0:T(8,128)(2,1)S(1)}, u32[]{:S(2)}, u32[]{:S(2)}) collective-permute-start(bf16[16,4096]{1,0:T(8,128)(2,1)S(1)} %collective-permute-done.8.refs_0_), channel_id=1, source_target_pairs={{0,2},{1,3},{2,0},{3,1},{4,6},{5,7},{6,4},{7,5},{8,10},{9,11},{10,... | collective-permute-start | bytes 393224 | tf_op jit(solution)/shard_map/ppermute | solution.py:352
  18.6 5.0 %collective-permute-start.6 = (bf16[16,4096]{1,0:T(8,128)(2,1)S(1)}, bf16[16,4096]{1,0:T(8,128)(2,1)S(1)}, u32[]{:S(2)}, u32[]{:S(2)}) collective-permute-start(bf16[16,4096]{1,0:T(8,128)(2,1)S(1)} %join.8.refs_0_), channel_id=1, source_target_pairs={{0,2},{1,3},{2,0},{3,1},{4,6},{5,7},{6,4},{7,5},{8,10},{9,11},{10,... | collective-permute-start | bytes 393224 | tf_op jit(solution)/shard_map/ppermute | solution.py:352
  20.2 3.5 %collective-permute-start.2 = (bf16[32,4096]{1,0:T(8,128)(2,1)S(1)}, bf16[32,4096]{1,0:T(8,128)(2,1)S(1)}, u32[]{:S(2)}, u32[]{:S(2)}) collective-permute-start(bf16[32,4096]{1,0:T(8,128)(2,1)S(1)} %join.6.refs_0_), channel_id=1, source_target_pairs={{0,1},{1,0},{2,3},{3,2},{4,5},{5,4},{6,7},{7,6},{8,9},{9,8},{10,11... | collective-permute-start | bytes 786440 | tf_op jit(solution)/shard_map/ppermute | solution.py:352
  20.4 3.4 %collective-permute-start.4 = (bf16[32,4096]{1,0:T(8,128)(2,1)S(1)}, bf16[32,4096]{1,0:T(8,128)(2,1)S(1)}, u32[]{:S(2)}, u32[]{:S(2)}) collective-permute-start(bf16[32,4096]{1,0:T(8,128)(2,1)S(1)} %join.7.refs_2_), channel_id=1, source_target_pairs={{0,1},{1,0},{2,3},{3,2},{4,5},{5,4},{6,7},{7,6},{8,9},{9,8},{10,11... | collective-permute-start | bytes 786440 | tf_op jit(solution)/shard_map/ppermute | solution.py:352
  20.9 2.9 %collective-permute-start.10 = (bf16[32,4096]{1,0:T(8,128)(2,1)S(1)}, bf16[32,4096]{1,0:T(8,128)(2,1)S(1)}, u32[]{:S(2)}, u32[]{:S(2)}) collective-permute-start(bf16[32,4096]{1,0:T(8,128)(2,1)S(1)} %join.10.refs_6_), channel_id=1, source_target_pairs={{0,1},{1,0},{2,3},{3,2},{4,5},{5,4},{6,7},{7,6},{8,9},{9,8},{10,11... | collective-permute-start | bytes 786440 | tf_op jit(solution)/shard_map/ppermute | solution.py:352
  23.7 1.6 %collective-permute-start.7 = (bf16[32,4096]{1,0:T(8,128)(2,1)S(1)}, bf16[32,4096]{1,0:T(8,128)(2,1)S(1)}, u32[]{:S(2)}, u32[]{:S(2)}) collective-permute-start(bf16[32,4096]{1,0:T(8,128)(2,1)S(1)} %join.9.refs_4_), channel_id=1, source_target_pairs={{0,1},{1,0},{2,3},{3,2},{4,5},{5,4},{6,7},{7,6},{8,9},{9,8},{10,11... | collective-permute-start | bytes 786440 | tf_op jit(solution)/shard_map/ppermute | solution.py:352
  33.3 2.9 %collective-permute-start.11 = (bf16[128,2560]{1,0:T(8,128)(2,1)S(1)}, bf16[128,2560]{1,0:T(8,128)(2,1)S(1)}, u32[]{:S(2)}, u32[]{:S(2)}) collective-permute-start(bf16[128,2560]{1,0:T(8,128)(2,1)S(1)} %get-tuple-element.40), channel_id=1, source_target_pairs={{0,1},{1,0},{2,3},{3,2},{4,5},{5,4},{6,7},{7,6},{8,9},{9,8},{10,11... | collective-permute-start | bytes 1966088 | tf_op jit(solution)/shard_map/ppermute | solution.py:352
  34.5 1.6 %collective-permute-start.13 = (bf16[64,1536]{1,0:T(8,128)(2,1)S(1)}, bf16[64,1536]{1,0:T(8,128)(2,1)S(1)}, u32[]{:S(2)}, u32[]{:S(2)}) collective-permute-start(bf16[64,1536]{1,0:T(8,128)(2,1)S(1)} %get-tuple-element.46), channel_id=1, source_target_pairs={{0,1},{1,0},{2,3},{3,2},{4,5},{5,4},{6,7},{7,6},{8,9},{9,8},{10,11... | collective-permute-start | bytes 589832 | tf_op jit(solution)/shard_map/ppermute | solution.py:352
  35.9 2.4 %collective-permute-start.12 = (bf16[64,1536]{1,0:T(8,128)(2,1)S(1)}, bf16[64,1536]{1,0:T(8,128)(2,1)S(1)}, u32[]{:S(2)}, u32[]{:S(2)}) collective-permute-start(bf16[64,1536]{1,0:T(8,128)(2,1)S(1)} %get-tuple-element.42), channel_id=1, source_target_pairs={{0,1},{1,0},{2,3},{3,2},{4,5},{5,4},{6,7},{7,6},{8,9},{9,8},{10,11... | collective-permute-start | bytes 589832 | tf_op jit(solution)/shard_map/ppermute | solution.py:352
  36.2 6.4 %collective-permute-start.14 = (bf16[16,4096]{1,0:T(8,128)(2,1)S(1)}, bf16[16,4096]{1,0:T(8,128)(2,1)S(1)}, u32[]{:S(2)}, u32[]{:S(2)}) collective-permute-start(bf16[16,4096]{1,0:T(8,128)(2,1)S(1)} %get-tuple-element.48), channel_id=1, source_target_pairs={{0,2},{1,3},{2,0},{3,1},{4,6},{5,7},{6,4},{7,5},{8,10},{9,11},{10,... | collective-permute-start | bytes 393224 | tf_op jit(solution)/shard_map/ppermute | solution.py:352
  37.8 9.0 %collective-permute-start.17 = (bf16[16,4096]{1,0:T(8,128)(2,1)S(1)}, bf16[16,4096]{1,0:T(8,128)(2,1)S(1)}, u32[]{:S(2)}, u32[]{:S(2)}) collective-permute-start(bf16[16,4096]{1,0:T(8,128)(2,1)S(1)} %get-tuple-element.50), channel_id=1, source_target_pairs={{0,2},{1,3},{2,0},{3,1},{4,6},{5,7},{6,4},{7,5},{8,10},{9,11},{10,... | collective-permute-start | bytes 393224 | tf_op jit(solution)/shard_map/ppermute | solution.py:352
  38.4 9.8 %collective-permute-start.19 = (bf16[16,4096]{1,0:T(8,128)(2,1)S(1)}, bf16[16,4096]{1,0:T(8,128)(2,1)S(1)}, u32[]{:S(2)}, u32[]{:S(2)}) collective-permute-start(bf16[16,4096]{1,0:T(8,128)(2,1)S(1)} %get-tuple-element.52), channel_id=1, source_target_pairs={{0,2},{1,3},{2,0},{3,1},{4,6},{5,7},{6,4},{7,5},{8,10},{9,11},{10,... | collective-permute-start | bytes 393224 | tf_op jit(solution)/shard_map/ppermute | solution.py:352
  42.6 8.1 %collective-permute-start.16 = (bf16[16,4096]{1,0:T(8,128)(2,1)S(1)}, bf16[16,4096]{1,0:T(8,128)(2,1)S(1)}, u32[]{:S(2)}, u32[]{:S(2)}) collective-permute-start(bf16[16,4096]{1,0:T(8,128)(2,1)S(1)} %add.11.refs_1_), channel_id=1, source_target_pairs={{0,12},{1,13},{2,14},{3,15},{4,8},{5,9},{6,10},{7,11},{8,4},{9,5},... | collective-permute-start | bytes 393224 | tf_op jit(solution)/shard_map/ppermute | solution.py:352
  45.2 5.3 %collective-permute-start.15 = (bf16[16,4096]{1,0:T(8,128)(2,1)S(1)}, bf16[16,4096]{1,0:T(8,128)(2,1)S(1)}, u32[]{:S(2)}, u32[]{:S(2)}) collective-permute-start(bf16[16,4096]{1,0:T(8,128)(2,1)S(1)} %join.11), channel_id=1, source_target_pairs={{0,2},{1,3},{2,0},{3,1},{4,6},{5,7},{6,4},{7,5},{8,10},{9,11},{10,... | collective-permute-start | bytes 393224 | tf_op jit(solution)/shard_map/ppermute | solution.py:352
  46.8 9.2 %collective-permute-start.18 = (bf16[16,4096]{1,0:T(8,128)(2,1)S(1)}, bf16[16,4096]{1,0:T(8,128)(2,1)S(1)}, u32[]{:S(2)}, u32[]{:S(2)}) collective-permute-start(bf16[16,4096]{1,0:T(8,128)(2,1)S(1)} %add.12), channel_id=1, source_target_pairs={{0,8},{1,9},{2,10},{3,11},{4,12},{5,13},{6,14},{7,15},{8,0},{9,1},... | collective-permute-start | bytes 393224 | tf_op jit(solution)/shard_map/ppermute | solution.py:352
  48.2 7.7 %collective-permute-start.20 = (bf16[16,4096]{1,0:T(8,128)(2,1)S(1)}, bf16[16,4096]{1,0:T(8,128)(2,1)S(1)}, u32[]{:S(2)}, u32[]{:S(2)}) collective-permute-start(bf16[16,4096]{1,0:T(8,128)(2,1)S(1)} %add.13), channel_id=1, source_target_pairs={{0,4},{1,5},{2,6},{3,7},{4,0},{5,1},{6,2},{7,3},{8,12},{9,13},{10,... | collective-permute-start | bytes 393224 | tf_op jit(solution)/shard_map/ppermute | solution.py:352
  (2 other events, 40.5 us)
